TPU v7x, 32 devices: a whole 2x2x4 slice. The times are simulated.
32 devices in a mesh: tensor: 4 (over y, x), expert: 4 (over z), dp: 2 (over core).
Axes of the slice: x: 2, y: 2, z: 4, core: 2. Of those that a mesh axis runs over, the one named last changes fastest.
Arguments:
- tokens: bfloat16 [2048, 2048], P(('expert', 'dp')), may hold values from -6 to 6
- grad_output: bfloat16 [2048, 2048], P(('expert', 'dp')), may hold values from -4 to 4
- gate_prob: float32 [2048], P(('expert', 'dp')), may hold values from 0.3 to 1
- expert_index: int32 [2048, 1], P(('expert', 'dp')), may hold values from 0 to 3, as said below
- slot_index: int32 [2048, 1], P(('expert', 'dp')), may hold values from 0 to 127, as said below
- up_weight: bfloat16 [4, 2048, 4096], P('expert', 'dp', 'tensor'), may hold values from -0.125 to 0.125
- down_weight: bfloat16 [4, 2048, 4096], P('expert', 'dp', 'tensor'), may hold values from -0.09375 to 0.09375
Outputs:
- grad_tokens: bfloat16 [2048, 2048], P(('expert', 'dp'), 'tensor')
- grad_up: bfloat16 [4, 2048, 4096], P('expert', 'dp', 'tensor')
- grad_down: bfloat16 [4, 2048, 4096], P('expert', 'dp', 'tensor')
Inputs may be any that keep to these rules, and one draw needn't show every extreme that they name: `expert_index`: within each aligned block of 256 rows, at most 128 rows choose one expert; in every block one expert is chosen by exactly 128 rows, and other experts by varying numbers. `slot_index`: slots of rows that choose the same expert within an aligned block of 256 rows are distinct.
All inputs are finite; a program needn't handle non-finite values.
Results may differ from a plain program's by a relative error of at most 0.015.
Values may be sent and summed in bfloat16 or wider, within the bound.
No kernel may reach another device: no remote copies, remote signals or barrier semaphores. Data moves between devices by JAX's collectives and lax.ppermute only.
A program may use at most 128 MiB of HBM per device.

v0:
```python
import jax
import jax.numpy as jnp
from jax import lax
from jax.sharding import PartitionSpec as P


def expert_grads(token_rows, grad_rows, up_matrix, down_matrix):
    pre_act = jnp.dot(token_rows, up_matrix, preferred_element_type=jnp.float32)
    hidden = jax.nn.gelu(pre_act).astype(jnp.bfloat16)
    hidden_grad = jnp.dot(grad_rows, down_matrix, preferred_element_type=jnp.float32)
    slope_grad = jax.vjp(jax.nn.gelu, pre_act)[1](hidden_grad)[0].astype(jnp.bfloat16)
    input_part = lax.dot_general(
        slope_grad, up_matrix, (((1,), (1,)), ((), ())), preferred_element_type=jnp.float32
    )
    return (hidden, slope_grad, input_part)


def local(tokens, grad_output, gate_prob, expert_index, slot_index, up_weight, down_weight):
    experts = lax.axis_size("expert")
    tensor_size = lax.axis_size("tensor")
    tok_count = tokens.shape[0]
    model_width = tokens.shape[1]
    capacity = 2 * tok_count // experts
    feature_share = model_width // tensor_size
    position = expert_index[:, 0] * capacity + slot_index[:, 0]
    onehot = (
        lax.broadcasted_iota(jnp.int32, (experts * capacity, tok_count), 0) == position[None, :]
    ).astype(jnp.bfloat16)
    scaled = (grad_output.astype(jnp.float32) * gate_prob[:, None]).astype(jnp.bfloat16)
    up_full, down_full = (
        lax.all_gather(up_weight, "dp", axis=1, tiled=True),
        lax.all_gather(down_weight, "dp", axis=1, tiled=True),
    )
    up_full = up_full[0]
    down_full = down_full[0]

    def dispatch(columns):
        placed = jnp.dot(onehot, columns, preferred_element_type=jnp.float32).astype(jnp.bfloat16)
        return placed.reshape(experts, capacity, columns.shape[1])

    token_buf, grad_buf = (
        lax.all_to_all(dispatch(tokens), "expert", split_axis=0, concat_axis=0, tiled=True),
        lax.all_to_all(dispatch(scaled), "expert", split_axis=0, concat_axis=0, tiled=True),
    )
    rows_total = token_buf.shape[0] * capacity
    token_rows = token_buf.reshape(rows_total, model_width)
    grad_rows = grad_buf.reshape(rows_total, model_width)
    hidden, slope_grad, input_part = expert_grads(token_rows, grad_rows, up_full, down_full)
    columns = grad_rows
    grad_down = lax.psum_scatter(
        lax.dot_general(
            columns, hidden, (((0,), (0,)), ((), ())), preferred_element_type=jnp.float32
        ).astype(jnp.bfloat16),
        "dp",
        scatter_dimension=0,
        tiled=True,
    ).astype(jnp.float32)
    columns = token_rows
    grad_up = lax.psum_scatter(
        lax.dot_general(
            columns, slope_grad, (((0,), (0,)), ((), ())), preferred_element_type=jnp.float32
        ).astype(jnp.bfloat16),
        "dp",
        scatter_dimension=0,
        tiled=True,
    ).astype(jnp.float32)
    share_sums = lax.psum_scatter(
        input_part.reshape(experts, capacity, model_width).astype(jnp.bfloat16),
        "tensor",
        scatter_dimension=2,
        tiled=True,
    )
    returned = lax.all_to_all(share_sums, "expert", split_axis=0, concat_axis=0, tiled=True)
    grad_tokens = lax.dot_general(
        onehot,
        returned.reshape(experts * capacity, feature_share),
        (((0,), (0,)), ((), ())),
        preferred_element_type=jnp.float32,
    )
    return (
        grad_tokens.astype(jnp.bfloat16),
        grad_up[None].astype(jnp.bfloat16),
        grad_down[None].astype(jnp.bfloat16),
    )


def solution(mesh):
    placed = (
        P(("expert", "dp"), None),
        P(("expert", "dp"), None),
        P(("expert", "dp")),
        P(("expert", "dp"), None),
        P(("expert", "dp"), None),
        P("expert", "dp", "tensor"),
        P("expert", "dp", "tensor"),
    )
    return jax.shard_map(
        local,
        mesh=mesh,
        in_specs=placed,
        out_specs=(
            P(("expert", "dp"), "tensor"),
            P("expert", "dp", "tensor"),
            P("expert", "dp", "tensor"),
        ),
        check_vma=False,
    )
```

profile of v0, /device:TPU:0, one launch (start us, length us, event | category | flops | bytes accessed | tf_op | source)
XLA Modules:
  0.0 201.1 jit_solution(6632141049684848281)
XLA Ops:
  7.2 0.0 copy-start
  7.2 0.0 all-gather.5.cloned.1.call-start
  7.2 0.7 all-gather.5.cloned.1.call-update
  7.9 0.0 copy-done.2
  7.9 0.0 copy-done.3
  8.0 0.5 copy-done
  8.4 2.0 %convolution_convert_fusion.2 = bf16[512,2048]{1,0:T(8,128)(2,1)} fusion(bf16[256,2048]{1,0:T(8,128)(2,1)S(1)} %copy-done, s32[256]{0:T(256)S(1)} %bitcast.33), kind=kOutput, calls=%fused_computation.11 | convolution fusion | flops 538050560 | bytes 3146752 | tf_op jit(solution)/shard_map/dot_general | solution.py:38
  10.5 6.5 %all-to-all-start.1 = ((bf16[4,128,2048]{2,1,0:T(8,128)(2,1)}), bf16[4,128,2048]{2,1,0:T(8,128)(2,1)S(1)}, u32[]{:S(2)}, u32[]{:S(2)}) async-start(bf16[4,128,2048]{2,1,0:T(8,128)(2,1)} %bitcast.4), calls=%async_computation.1 | async-start | bytes 4194304 | tf_op jit(solution)/shard_map/all_to_all | solution.py:42
  16.9 0.7 all-gather.3.cloned.1.call-update
  17.7 3.5 %convolution_convert_fusion.3 = bf16[512,2048]{1,0:T(8,128)(2,1)} fusion(bf16[256,2048]{1,0:T(8,128)(2,1)} %param.8, f32[256]{0:T(256)S(1)} %copy-done.1, s32[256]{0:T(256)S(1)} %bitcast.34), kind=kOutput, calls=%fused_computation.12 | convolution fusion | flops 539623424 | bytes 3147776 | tf_op jit(solution)/shard_map/dot_general | solution.py:38
  21.2 43.9 %all-to-all-done.1 = bf16[4,128,2048]{2,1,0:T(8,128)(2,1)S(1)} async-done(((bf16[4,128,2048]{2,1,0:T(8,128)(2,1)}), bf16[4,128,2048]{2,1,0:T(8,128)(2,1)S(1)}, u32[]{:S(2)}, u32[]{:S(2)}) %all-to-all-start.1) | async-done | bytes 2097184 | tf_op jit(solution)/shard_map/all_to_all | solution.py:42
  65.1 4.5 %all-to-all-start = ((bf16[4,128,2048]{2,1,0:T(8,128)(2,1)}), bf16[4,128,2048]{2,1,0:T(8,128)(2,1)}, u32[]{:S(2)}, u32[]{:S(2)}) async-start(bf16[4,128,2048]{2,1,0:T(8,128)(2,1)} %bitcast.1), calls=%async_computation | async-start | bytes 4194304 | tf_op jit(solution)/shard_map/all_to_all | solution.py:43
  69.6 0.0 reduce-scatter.4.cloned.1.call-start
  69.7 0.0 all-gather.5.cloned.1.call-done
  69.7 5.9 %fusion.2 = f32[512,1024]{1,0:T(8,128)} fusion(bf16[512,2048]{1,0:T(8,128)(2,1)S(1)} %bitcast.30, bf16[1,2048,1024]{2,1,0:T(8,128)(2,1)} %all-gather.5.cloned.1.call-done), kind=kOutput, calls=%fused_computation.2 | convolution fusion | flops 2147483648 | bytes 8388608 | tf_op jit(solution)/shard_map/dot_general | solution.py:8
  75.6 41.8 %all-to-all-done = bf16[4,128,2048]{2,1,0:T(8,128)(2,1)} async-done(((bf16[4,128,2048]{2,1,0:T(8,128)(2,1)}), bf16[4,128,2048]{2,1,0:T(8,128)(2,1)}, u32[]{:S(2)}, u32[]{:S(2)}) %all-to-all-start) | async-done | bytes 2097184 | tf_op jit(solution)/shard_map/all_to_all | solution.py:43
  117.4 7.0 %fusion.15 = bf16[512,1024]{1,0:T(8,128)(2,1)S(1)} fusion(f32[512,1024]{1,0:T(8,128)} %fusion.2, bf16[512,2048]{1,0:T(8,128)(2,1)} %bitcast.2, bf16[1,2048,1024]{2,1,0:T(8,128)(2,1)} %all-gather.3.cloned.1.call-done), kind=kOutput, calls=%fused_computation.19 | convolution fusion | flops 2157969408 | bytes 9437184 | tf_op jit(solution)/shard_map/dot_general | solution.py:10
  124.4 0.0 copy-start.5
  124.4 1.0 copy-done.5
  125.3 3.7 %fusion.6 = bf16[4,128,2048]{2,1,0:T(8,128)(2,1)} fusion(bf16[4,128,1024]{2,1,0:T(8,128)(2,1)S(1)} %bitcast.38, bf16[1,2048,1024]{2,1,0:T(8,128)(2,1)S(1)} %copy-done.4), kind=kOutput, calls=%fused_computation.10 | convolution fusion | flops 2148532224 | bytes 7340032 | tf_op jit(solution)/shard_map/dot_general | solution.py:12
  129.0 0.0 reduce-scatter.4.cloned.1.call-update
  129.1 0.0 reduce-scatter.6.cloned.1.call-start
  129.1 5.6 %convolution_convert_fusion.1 = bf16[2048,1024]{1,0:T(8,128)(2,1)} fusion(bf16[512,2048]{1,0:T(8,128)(2,1)S(1)} %bitcast.31, bf16[512,1024]{1,0:T(8,128)(2,1)} %copy-done.5), kind=kOutput, calls=%fused_computation.7 | convolution fusion | flops 2149580800 | bytes 7340032 | tf_op jit(solution)/shard_map/dot_general | solution.py:60
  134.7 0.0 reduce-scatter.6.cloned.1.call-update
  134.7 0.2 reduce-scatter.8.cloned.1.call-start
  135.0 1.4 copy-done.6
  136.3 6.1 %convolution_convert_fusion = bf16[2048,1024]{1,0:T(8,128)(2,1)} fusion(bf16[512,2048]{1,0:T(8,128)(2,1)} %bitcast.2, f32[512,1024]{1,0:T(8,128)S(1)} %copy-done.6), kind=kOutput, calls=%fused_computation.6 | convolution fusion | flops 2154299392 | bytes 8388608 | tf_op jit(solution)/shard_map/dot_general | solution.py:51
  142.4 0.0 reduce-scatter.8.cloned.1.call-update
  142.4 21.1 %reduce-scatter.4.cloned.1.call-done = bf16[4,128,512]{2,1,0:T(8,128)(2,1)} async-done(((bf16[4,128,2048]{2,1,0:T(8,128)(2,1)}), bf16[4,128,512]{2,1,0:T(8,128)(2,1)}) %reduce-scatter.4.cloned.1.call-update) | async-done | bytes 524304 | tf_op jit(solution)/shard_map/reduce_scatter | solution.py:67
  163.6 19.1 %all_to_all.15 = bf16[4,128,512]{2,1,0:T(8,128)(2,1)S(1)} all-to-all(bf16[4,128,512]{2,1,0:T(8,128)(2,1)} %reduce-scatter.4.cloned.1.call-done), channel_id=1, replica_groups=mesh['tensor'=4,'expert'=4,'dp'=2] {'expert'}, dimensions={0} | all-to-all | bytes 1048576 | tf_op jit(solution)/shard_map/all_to_all | solution.py:73
  182.6 1.1 convolution_convert_fusion.4
  183.7 10.8 %reduce-scatter.8.cloned.1.call-done = bf16[1024,1024]{1,0:T(8,128)(2,1)} async-done(((bf16[2048,1024]{1,0:T(8,128)(2,1)}), bf16[1024,1024]{1,0:T(8,128)(2,1)}) %reduce-scatter.8.cloned.1.call-update) | async-done | bytes 2097168 | tf_op jit(solution)/shard_map/reduce_scatter | solution.py:50
  (11 shorter events, 0.0 us)
Async XLA Ops:
  7.2 1.3 copy-start
  7.2 0.8 copy-start.2
  7.2 0.8 copy-start.3
  7.2 62.5 %all-gather.5.cloned.1.call-start = ((), (), s32[]{:S(2)}) async-start(), calls=%async_computation.7 | async-start | bytes 6291456 | tf_op jit(solution)/shard_map/all_gather | solution.py:31
  10.5 7.2 %copy-start.1 = (f32[256]{0:T(256)S(1)}, f32[256]{0:T(256)}, u32[]{:S(2)}) copy-start(f32[256]{0:T(256)} %param.9) | copy-start | bytes 3076
  10.5 54.6 %all-to-all-start.1 = ((bf16[4,128,2048]{2,1,0:T(8,128)(2,1)}), bf16[4,128,2048]{2,1,0:T(8,128)(2,1)S(1)}, u32[]{:S(2)}, u32[]{:S(2)}) async-start(bf16[4,128,2048]{2,1,0:T(8,128)(2,1)} %bitcast.4), calls=%async_computation.1 | async-start | bytes 4194304 | tf_op jit(solution)/shard_map/all_to_all | solution.py:42
  16.9 100.5 %all-gather.3.cloned.1.call-start = ((), (), s32[]{:S(2)}) async-start(), calls=%async_computation.6 | async-start | bytes 6291456 | tf_op jit(solution)/shard_map/all_gather | solution.py:32
  65.1 52.3 %all-to-all-start = ((bf16[4,128,2048]{2,1,0:T(8,128)(2,1)}), bf16[4,128,2048]{2,1,0:T(8,128)(2,1)}, u32[]{:S(2)}, u32[]{:S(2)}) async-start(bf16[4,128,2048]{2,1,0:T(8,128)(2,1)} %bitcast.1), calls=%async_computation | async-start | bytes 4194304 | tf_op jit(solution)/shard_map/all_to_all | solution.py:43
  69.6 93.9 %reduce-scatter.4.cloned.1.call-start = ((), (), s32[]{:S(2)}) async-start(), calls=%async_computation.8 | async-start | bytes 2621440 | tf_op jit(solution)/shard_map/reduce_scatter | solution.py:67
  117.4 8.0 %copy-start.4 = (bf16[1,2048,1024]{2,1,0:T(8,128)(2,1)S(1)}, bf16[1,2048,1024]{2,1,0:T(8,128)(2,1)}, u32[]{:S(2)}) copy-start(bf16[1,2048,1024]{2,1,0:T(8,128)(2,1)} %all-gather.5.cloned.1.call-done) | copy-start | bytes 12582916
  124.4 1.0 copy-start.5
  129.1 54.6 %reduce-scatter.6.cloned.1.call-start = ((), (), s32[]{:S(2)}) async-start(), calls=%async_computation.9 | async-start | bytes 6291456 | tf_op jit(solution)/shard_map/reduce_scatter | solution.py:59
  134.7 1.6 copy-start.6
  134.7 59.8 %reduce-scatter.8.cloned.1.call-start = ((), (), s32[]{:S(2)}) async-start(), calls=%async_computation.10 | async-start | bytes 6291456 | tf_op jit(solution)/shard_map/reduce_scatter | solution.py:50
Sparse Core Ops, SparseCore 0:
  9.6 16.3 all-gather.4
  27.5 14.8 all-gather.2
  129.2 34.3 reduce-scatter.3
  166.4 12.0 reduce-scatter.5
  181.2 13.3 reduce-scatter.7
where the time goes:
time: 202 us; the launch traced here: 201 us
  waiting for transfers between devices  119 us (59%)
  matrix products  34.9 us (17%)
  blocking collectives  19.1 us (9%)
  between operations  13.8 us (7%)
  starting transfers between devices  11.3 us (6%)
  local copies, waits for them, and re-layouts  2.83 us (1%)
    all_to_all x1, waiting for transfers between devices, local(): lax.all_to_all(dispatch(tokens), 'expert', split_axis=0, concat_axis=0, t...  43.9 us
    all_to_all x1, waiting for transfers between devices, local(): lax.all_to_all(dispatch(scaled), 'expert', split_axis=0, concat_axis=0, t...  41.8 us
    reduce_scatter x1, waiting for transfers between devices, local(): lax.psum_scatter(input_part.reshape(experts, capacity, model_width).astyp...  21.1 us
    all_to_all x1, blocking collectives, local(): lax.all_to_all(share_sums, 'expert', split_axis=0, concat_axis=0, tiled=T...  19.1 us
    reduce_scatter x1, waiting for transfers between devices, local(): lax.psum_scatter(lax.dot_general(columns, hidden, (((0,), (0,)), ((), ())...  10.8 us
    dot_general x1, matrix products, expert_grads(): jnp.dot(grad_rows, down_matrix, preferred_element_type=jnp.float32)  6.98 us
    all_to_all x1, starting transfers between devices, local(): lax.all_to_all(dispatch(tokens), 'expert', split_axis=0, concat_axis=0, t...  6.46 us
    dot_general x1, matrix products, local(): lax.dot_general(columns, hidden, (((0,), (0,)), ((), ())), preferred_elem...  6.1 us
  transfers between devices with their start and end apart: 7, of which 4 were waited for; matrix products, arithmetic and copies ran while one was open for 12% of the time, Pallas kernels for 0%

commit v1 on v0

v1 whole, which is shorter than its diff:
```python
import jax
import jax.numpy as jnp
from jax import lax
from jax.sharding import PartitionSpec as P

F32 = jnp.float32
BF16 = jnp.bfloat16


def dot(lhs, rhs, contract):
    return lax.dot_general(lhs, rhs, ((contract[:1], contract[1:]), ((), ())), preferred_element_type=F32)


def xor_order(blocks, shift):
    low = (shift & 1) == 1
    high = (shift & 2) == 2
    once = [jnp.where(low, blocks[i ^ 1], blocks[i]) for i in range(4)]
    return [jnp.where(high, once[i ^ 2], once[i]) for i in range(4)]


def local(tokens, grad_output, gate_prob, expert_index, slot_index, up_weight, down_weight):
    experts = lax.axis_size("expert")
    tensor_size = lax.axis_size("tensor")
    e = lax.axis_index("expert")
    t = lax.axis_index("tensor")
    p = lax.axis_index("dp")
    tok_count, width = tokens.shape
    capacity = 2 * tok_count // experts
    share = width // tensor_size
    half = width // 2
    order = t ^ (2 * p)

    def swap(x):
        return lax.ppermute(x, "dp", [(0, 1), (1, 0)])

    def across(x, j):
        return lax.ppermute(x, "tensor", [(i, i ^ j) for i in range(tensor_size)])

    def shift(x, k):
        return lax.ppermute(x, "expert", [(i, (i + k) % experts) for i in range(experts)])

    up_own, down_own = up_weight[0], down_weight[0]
    up_other, down_other = swap(up_own), swap(down_own)

    position = expert_index[:, 0] * capacity + slot_index[:, 0]
    scaled = (grad_output.astype(F32) * gate_prob[:, None]).astype(BF16)

    def onehot(first, rows):
        ids = lax.broadcasted_iota(jnp.int32, (rows, tok_count), 0) + first
        return (ids == position[None, :]).astype(BF16)

    def place(hot, columns):
        return dot(hot, columns, (1, 0)).astype(BF16)

    def quarter(x):
        return lax.dynamic_slice_in_dim(x, t * share, share, 1)

    def halves(x):
        return (
            lax.dynamic_slice_in_dim(x, p * half, half, 1),
            lax.dynamic_slice_in_dim(x, (1 - p) * half, half, 1),
        )

    def spread(tok, grad):
        tok_x, tok_y = across(tok, 1), across(tok, 2)
        grad_x, grad_y = across(grad, 1), across(grad, 2)
        tok_d, grad_d = across(tok_y, 1), across(grad_x, 2)
        tok_all = xor_order([tok, tok_x, tok_y, tok_d], order)
        grad_all = xor_order([grad, grad_x, grad_y, grad_d], order)
        join = lambda a: (jnp.concatenate(a[:2], 1), jnp.concatenate(a[2:], 1))
        return join(tok_all), join(grad_all)

    def expert_rows(tok, grad):
        pre = dot(tok[0], up_own, (1, 0)) + dot(tok[1], up_other, (1, 0))
        hidden = jax.nn.gelu(pre).astype(BF16)
        hidden_grad = dot(grad[0], down_own, (1, 0)) + dot(grad[1], down_other, (1, 0))
        slope = jax.vjp(jax.nn.gelu, pre)[1](hidden_grad)[0].astype(BF16)
        own = dot(slope, up_own, (1, 1)).astype(BF16)
        other = dot(slope, up_other, (1, 1)).astype(BF16)
        parts = [own[:, :share], own[:, share:], other[:, :share], other[:, share:]]
        sends = xor_order(parts, order)
        total = sends[0].astype(F32)
        for j in (1, 2, 3):
            total = total + across(sends[j], j).astype(F32)
        return hidden, slope, total.astype(BF16)

    tok_q, grad_q = quarter(tokens), quarter(scaled)
    chunks = []
    if experts == 4:
        hots = [onehot(((e + k) % experts) * capacity, capacity) for k in range(experts)]
        rows = []
        for k in (1, 3, 2):
            rows.append((k, shift(place(hots[k], tok_q), k), shift(place(hots[k], grad_q), k)))
        chunks.append(
            (0, tuple(place(hots[0], x) for x in halves(tokens)), tuple(place(hots[0], x) for x in halves(scaled)))
        )
        for k, tok, grad in rows:
            chunks.append((k,) + spread(tok, grad))
    else:
        hots = [onehot(0, experts * capacity)]

        def exchange(x):
            placed = place(hots[0], x).reshape(experts, capacity, share)
            moved = lax.all_to_all(placed, "expert", split_axis=0, concat_axis=0, tiled=True)
            return moved.reshape(experts * capacity, share)

        chunks.append((0,) + spread(exchange(tok_q), exchange(grad_q)))

    grad_tokens = jnp.zeros((tok_count, share), F32)
    hiddens, slopes = [], []
    for k, tok, grad in chunks:
        hidden, slope, total = expert_rows(tok, grad)
        hiddens.append(hidden)
        slopes.append(slope)
        if experts == 4:
            back = shift(total, -k) if k else total
        else:
            back = lax.all_to_all(
                total.reshape(experts, capacity, share), "expert", split_axis=0, concat_axis=0, tiled=True
            ).reshape(experts * capacity, share)
        grad_tokens = grad_tokens + dot(hots[k], back, (0, 0))

    def weight_grad(index, outs):
        own = jnp.concatenate([c[index][0] for c in chunks], 0)
        other = jnp.concatenate([c[index][1] for c in chunks], 0)
        out = jnp.concatenate(outs, 0)
        got = swap(dot(other, out, (0, 0)).astype(BF16))
        mine = dot(own, out, (0, 0)).astype(BF16)
        return (mine.astype(F32) + got.astype(F32)).astype(BF16)[None]

    grad_down = weight_grad(2, hiddens)
    grad_up = weight_grad(1, slopes)
    return grad_tokens.astype(BF16), grad_up, grad_down


def solution(mesh):
    placed = (
        P(("expert", "dp"), None),
        P(("expert", "dp"), None),
        P(("expert", "dp")),
        P(("expert", "dp"), None),
        P(("expert", "dp"), None),
        P("expert", "dp", "tensor"),
        P("expert", "dp", "tensor"),
    )
    return jax.shard_map(
        local,
        mesh=mesh,
        in_specs=placed,
        out_specs=(
            P(("expert", "dp"), "tensor"),
            P("expert", "dp", "tensor"),
            P("expert", "dp", "tensor"),
        ),
        check_vma=False,
    )
```

time: 202 us -> 151 us (0.75)
  waiting for transfers between devices: 119 us -> 43.9 us
  starting transfers between devices: 11.3 us -> 48.6 us
  blocking collectives: 19.1 us -> 0 us
  matrix products: 34.9 us -> 49.3 us
  between operations: 13.8 us -> 1.13 us
  other arithmetic: 0.01 us -> 6.26 us
    all_to_all x2 -> x0, waiting for transfers between devices: 85.7 us -> none  [the longest x1 43.9 us: local(): lax.all_to_all(dispatch(tokens), 'expert', split_axis=0, concat_axis=0, t...]
    ppermute x0 -> x43, starting transfers between devices: none -> 48.6 us  [the longest x30 37.7 us: across(): return lax.ppermute(x, 'tensor', [(i, i ^ j) for i in range(tensor_size)])]
    ppermute x0 -> x43, waiting for transfers between devices: none -> 43.9 us  [the longest x9 22.1 us: shift(): lax.ppermute(x, 'expert', [(i, (i + k) % experts) for i in range(experts)])]
    reduce_scatter x3 -> x0, waiting for transfers between devices: 31.9 us -> none  [the longest x1 21.1 us: local(): lax.psum_scatter(input_part.reshape(experts, capacity, model_width).astyp...]
    all_to_all x1 -> x0, blocking collectives: 19.1 us -> none  [local(): lax.all_to_all(share_sums, 'expert', split_axis=0, concat_axis=0, tiled=T...]
    dot_general x8 -> x42, matrix products: 34.9 us -> 49.3 us  [dot(): lax.dot_general(lhs, rhs, ((contract[:1], contract[1:]), ((), ())), prefe...]
    all_to_all x2 -> x0, starting transfers between devices: 10.9 us -> none  [the longest x1 6.46 us: local(): lax.all_to_all(dispatch(tokens), 'expert', split_axis=0, concat_axis=0, t...]
    select_n x0 -> x10, other arithmetic: none -> 3.18 us  [xor_order(): return [jnp.where(high, once[i ^ 2], once[i]) for i in range(4)]]
  transfers between devices with their start and end apart: 7 -> 43, of which waited for: 4 -> 21; matrix products, arithmetic and copies ran while one was open for 12% -> 23% of each run, Pallas kernels for 0% -> 0%
where the time goes in v1:
time: 151 us; the launch traced here: 150 us
  matrix products  49.3 us (33%)
  starting transfers between devices  48.6 us (32%)
  waiting for transfers between devices  43.9 us (29%)
  other arithmetic  6.26 us (4%)
    dot_general x42, matrix products, dot(): lax.dot_general(lhs, rhs, ((contract[:1], contract[1:]), ((), ())), prefe...  49.3 us
    ppermute x30, starting transfers between devices, across(): return lax.ppermute(x, 'tensor', [(i, i ^ j) for i in range(tensor_size)])  37.7 us
    ppermute x9, waiting for transfers between devices, shift(): lax.ppermute(x, 'expert', [(i, (i + k) % experts) for i in range(experts)])  22.1 us
    ppermute x30, waiting for transfers between devices, across(): return lax.ppermute(x, 'tensor', [(i, i ^ j) for i in range(tensor_size)])  21.8 us
    ppermute x9, starting transfers between devices, shift(): lax.ppermute(x, 'expert', [(i, (i + k) % experts) for i in range(experts)])  10.4 us
    select_n x10, other arithmetic, xor_order(): return [jnp.where(high, once[i ^ 2], once[i]) for i in range(4)]  3.18 us
  transfers between devices with their start and end apart: 43, of which 21 were waited for; matrix products, arithmetic and copies ran while one was open for 23% of the time, Pallas kernels for 0%

profile of v1, /device:TPU:0, one launch (start us, length us, event | category | flops | bytes accessed | tf_op | source)
XLA Modules:
  0.0 150.4 jit_solution(7543802513132543075)
XLA Ops:
  2.8 4.1 %collective-permute-start.33 = (bf16[128,512]{1,0:T(8,128)(2,1)}, bf16[128,512]{1,0:T(8,128)(2,1)}, u32[]{:S(2)}, u32[]{:S(2)}) collective-permute-start(bf16[128,512]{1,0:T(8,128)(2,1)} %convolution_convert_fusion.14), channel_id=1, source_target_pairs={{0,4},{2,6},{4,0},{6,2},{1,5},{3,7},{5,1},{7,3},{8,12},{10,14},{12... | collective-permute-start | bytes 393224 | tf_op jit(solution)/shard_map/ppermute | solution.py:40
  11.2 3.8 %collective-permute-start.21 = (bf16[128,512]{1,0:T(8,128)(2,1)}, bf16[128,512]{1,0:T(8,128)(2,1)}, u32[]{:S(2)}, u32[]{:S(2)}) collective-permute-start(bf16[128,512]{1,0:T(8,128)(2,1)} %convolution_convert_fusion.16), channel_id=1, source_target_pairs={{0,6},{2,0},{4,2},{6,4},{1,7},{3,1},{5,3},{7,5},{8,14},{10,8},{12,... | collective-permute-start | bytes 393224 | tf_op jit(solution)/shard_map/ppermute | solution.py:40
  15.0 1.8 %convolution_convert_fusion.17 = bf16[128,512]{1,0:T(8,128)(2,1)} fusion(bf16[256,2048]{1,0:T(8,128)(2,1)} %copy-done.2, s32[]{:T(128)S(6)} %select_n.371, s32[256]{0:T(256)S(1)} %bitcast.69, s32[128]{0:T(128)S(1)} %iota_add_fusion.1), kind=kOutput, calls=%fused_computation.34 | convolution fusion | flops 33652736 | bytes 394756 | tf_op jit(solution)/shard_map/dot_general | solution.py:11
  20.1 2.2 %fusion.217 = f32[128,1024]{1,0:T(8,128)} fusion(bf16[128,1024]{1,0:T(8,128)(2,1)} %convolution_convert_fusion.11, bf16[1,1024,1024]{2,1,0:T(8,128)(2,1)S(1)} %copy-done.1), kind=kOutput, calls=%fused_computation.348 | convolution fusion | flops 268435456 | bytes 2883584 | tf_op jit(solution)/shard_map/dot_general | solution.py:11
  22.6 2.2 %fusion.222 = f32[128,1024]{1,0:T(8,128)S(1)} fusion(bf16[128,1024]{1,0:T(8,128)(2,1)S(1)} %convolution_convert_fusion.13, bf16[1,1024,1024]{2,1,0:T(8,128)(2,1)} %param.13), kind=kOutput, calls=%fused_computation.353 | convolution fusion | flops 268435456 | bytes 2883584 | tf_op jit(solution)/shard_map/dot_general | solution.py:11
  25.0 1.6 %collective-permute-start.9 = (bf16[128,512]{1,0:T(8,128)(2,1)S(1)}, bf16[128,512]{1,0:T(8,128)(2,1)S(1)}, u32[]{:S(2)}, u32[]{:S(2)}) collective-permute-start(bf16[128,512]{1,0:T(8,128)(2,1)S(1)} %convolution_convert_fusion.18), channel_id=1, source_target_pairs={{0,2},{2,4},{4,6},{6,0},{1,3},{3,5},{5,7},{7,1},{8,10},{10,12},{12... | collective-permute-start | bytes 393224 | tf_op jit(solution)/shard_map/ppermute | solution.py:40
  30.2 2.1 %collective-permute-done.9 = bf16[128,512]{1,0:T(8,128)(2,1)S(1)} collective-permute-done((bf16[128,512]{1,0:T(8,128)(2,1)S(1)}, bf16[128,512]{1,0:T(8,128)(2,1)S(1)}, u32[]{:S(2)}, u32[]{:S(2)}) %collective-permute-start.9) | collective-permute-done | bytes 131104 | tf_op jit(solution)/shard_map/ppermute | solution.py:40
  35.4 1.8 %collective-permute-start.32 = (bf16[128,512]{1,0:T(8,128)(2,1)}, bf16[128,512]{1,0:T(8,128)(2,1)S(1)}, u32[]{:S(2)}, u32[]{:S(2)}) collective-permute-start(bf16[128,512]{1,0:T(8,128)(2,1)} %collective-permute-done.29), channel_id=1, source_target_pairs={{0,16},{8,24},{16,0},{24,8},{1,17},{9,25},{17,1},{25,9},{2,18},{10... | collective-permute-start | bytes 393224 | tf_op jit(solution)/shard_map/ppermute | solution.py:37
  38.0 1.9 %collective-permute-start.22 = (bf16[128,512]{1,0:T(8,128)(2,1)}, bf16[128,512]{1,0:T(8,128)(2,1)S(1)}, u32[]{:S(2)}, u32[]{:S(2)}) collective-permute-start(bf16[128,512]{1,0:T(8,128)(2,1)} %collective-permute-done.21), channel_id=1, source_target_pairs={{0,16},{8,24},{16,0},{24,8},{1,17},{9,25},{17,1},{25,9},{2,18},{10... | collective-permute-start | bytes 393224 | tf_op jit(solution)/shard_map/ppermute | solution.py:37
  42.3 1.6 %collective-permute-start.24 = (bf16[128,512]{1,0:T(8,128)(2,1)}, bf16[128,512]{1,0:T(8,128)(2,1)S(1)}, u32[]{:S(2)}, u32[]{:S(2)}) collective-permute-start(bf16[128,512]{1,0:T(8,128)(2,1)} %collective-permute-done.21), channel_id=1, source_target_pairs={{0,8},{8,0},{16,24},{24,16},{1,9},{9,1},{17,25},{25,17},{2,10},{10... | collective-permute-start | bytes 393224 | tf_op jit(solution)/shard_map/ppermute | solution.py:37
  49.6 1.8 %collective-permute-start.20 = (bf16[128,512]{1,0:T(8,128)(2,1)S(1)}, bf16[128,512]{1,0:T(8,128)(2,1)S(1)}, u32[]{:S(2)}, u32[]{:S(2)}) collective-permute-start(bf16[128,512]{1,0:T(8,128)(2,1)S(1)} %collective-permute-done.17), channel_id=1, source_target_pairs={{0,16},{8,24},{16,0},{24,8},{1,17},{9,25},{17,1},{25,9},{2,18},{10... | collective-permute-start | bytes 393224 | tf_op jit(solution)/shard_map/ppermute | solution.py:37
  57.0 1.7 %collective-permute-done.10 = bf16[128,512]{1,0:T(8,128)(2,1)S(1)} collective-permute-done((bf16[128,512]{1,0:T(8,128)(2,1)S(1)}, bf16[128,512]{1,0:T(8,128)(2,1)S(1)}, u32[]{:S(2)}, u32[]{:S(2)}) %collective-permute-start.10) | collective-permute-done | bytes 131104 | tf_op jit(solution)/shard_map/ppermute | solution.py:37
  66.5 2.7 %collective-permute-done.7 = bf16[128,512]{1,0:T(8,128)(2,1)S(1)} collective-permute-done((bf16[128,512]{1,0:T(8,128)(2,1)S(1)}, bf16[128,512]{1,0:T(8,128)(2,1)S(1)}, u32[]{:S(2)}, u32[]{:S(2)}) %collective-permute-start.7) | collective-permute-done | bytes 131104 | tf_op jit(solution)/shard_map/ppermute | solution.py:37
  69.2 2.0 %fusion.132 = f32[128,1024]{1,0:T(8,128)S(1)} fusion(bf16[1024,1024]{1,0:T(8,128)(2,1)} %collective-permute-done.1, bf16[128,512]{1,0:T(8,128)(2,1)S(1)} %get-tuple-element.38, bf16[128,512]{1,0:T(8,128)(2,1)S(1)} %get-tuple-element.37), kind=kOutput, calls=%fused_computation.178 | convolution fusion | flops 268959744 | bytes 2883584 | tf_op jit(solution)/shard_map/dot_general | solution.py:11
  73.9 2.0 %fusion.118 = f32[128,1024]{1,0:T(8,128)S(1)} fusion(bf16[1024,1024]{1,0:T(8,128)(2,1)} %collective-permute-done.1, bf16[128,512]{1,0:T(8,128)(2,1)S(1)} %get-tuple-element.27, bf16[128,512]{1,0:T(8,128)(2,1)S(1)} %get-tuple-element.26), kind=kOutput, calls=%fused_computation.164 | convolution fusion | flops 268959744 | bytes 2883584 | tf_op jit(solution)/shard_map/dot_general | solution.py:11
  78.5 2.0 %fusion.104 = f32[128,1024]{1,0:T(8,128)S(1)} fusion(bf16[1024,1024]{1,0:T(8,128)(2,1)} %collective-permute-done.1, bf16[128,512]{1,0:T(8,128)(2,1)S(1)} %get-tuple-element.16, bf16[128,512]{1,0:T(8,128)(2,1)S(1)} %get-tuple-element.15), kind=kOutput, calls=%fused_computation.150 | convolution fusion | flops 268959744 | bytes 2883584 | tf_op jit(solution)/shard_map/dot_general | solution.py:11
  83.3 2.1 %multiply_convert_fusion.4 = (bf16[128,1024]{1,0:T(8,128)(2,1)S(1)}, f32[128,1024]{1,0:T(8,128)S(1)}) fusion(f32[128,1024]{1,0:T(8,128)S(1)} %copy-done.5, bf16[128,1024]{1,0:T(8,128)(2,1)S(1)} %convolution_convert_fusion.10, bf16[1024,1024]{1,0:T(8,128)(2,1)} %collective-permute-done.1), kind=kOutput, calls=%fused_computation.130 | convolution fusion | flops 269746176 | bytes 3670016 | tf_op jit(solution)/shard_map/dot_general | solution.py:11
  88.3 2.6 %convolution_convert_fusion.3 = bf16[128,1024]{1,0:T(8,128)(2,1)S(1)} fusion(bf16[128,1024]{1,0:T(8,128)(2,1)S(1)} %fusion.84, bf16[1024,1024]{1,0:T(8,128)(2,1)} %collective-permute-done.1), kind=kOutput, calls=%fused_computation.20 | convolution fusion | flops 268566528 | bytes 2621440 | tf_op jit(solution)/shard_map/dot_general | solution.py:11
  91.0 1.6 %collective-permute-start.39 = (bf16[128,512]{1,0:T(8,128)(2,1)S(1)}, bf16[128,512]{1,0:T(8,128)(2,1)S(1)}, u32[]{:S(2)}, u32[]{:S(2)}) collective-permute-start(bf16[128,512]{1,0:T(8,128)(2,1)S(1)} %get-tuple-element.30), channel_id=1, source_target_pairs={{0,24},{8,16},{16,8},{24,0},{1,25},{9,17},{17,9},{25,1},{2,26},{10... | collective-permute-start | bytes 393224 | tf_op jit(solution)/shard_map/ppermute | solution.py:37
  94.6 2.4 %convolution_convert_fusion.5 = bf16[128,1024]{1,0:T(8,128)(2,1)S(1)} fusion(bf16[128,1024]{1,0:T(8,128)(2,1)S(1)} %fusion.77, bf16[1024,1024]{1,0:T(8,128)(2,1)} %collective-permute-done.1), kind=kOutput, calls=%fused_computation.22 | convolution fusion | flops 268566528 | bytes 2621440 | tf_op jit(solution)/shard_map/dot_general | solution.py:11
  97.1 1.6 %collective-permute-start.27 = (bf16[128,512]{1,0:T(8,128)(2,1)S(1)}, bf16[128,512]{1,0:T(8,128)(2,1)S(1)}, u32[]{:S(2)}, u32[]{:S(2)}) collective-permute-start(bf16[128,512]{1,0:T(8,128)(2,1)S(1)} %get-tuple-element.19), channel_id=1, source_target_pairs={{0,24},{8,16},{16,8},{24,0},{1,25},{9,17},{17,9},{25,1},{2,26},{10... | collective-permute-start | bytes 393224 | tf_op jit(solution)/shard_map/ppermute | solution.py:37
  100.0 2.4 %convolution_convert_fusion.7 = bf16[128,1024]{1,0:T(8,128)(2,1)S(1)} fusion(bf16[128,1024]{1,0:T(8,128)(2,1)S(1)} %fusion.70, bf16[1024,1024]{1,0:T(8,128)(2,1)} %collective-permute-done.1), kind=kOutput, calls=%fused_computation.24 | convolution fusion | flops 268566528 | bytes 2621440 | tf_op jit(solution)/shard_map/dot_general | solution.py:11
  102.4 2.4 %convolution_convert_fusion.9 = bf16[128,1024]{1,0:T(8,128)(2,1)S(1)} fusion(bf16[128,1024]{1,0:T(8,128)(2,1)S(1)} %fusion.63, bf16[1024,1024]{1,0:T(8,128)(2,1)} %collective-permute-done.1), kind=kOutput, calls=%fused_computation.26 | convolution fusion | flops 268566528 | bytes 2621440 | tf_op jit(solution)/shard_map/dot_general | solution.py:11
  107.1 1.6 %collective-permute-start.15 = (bf16[128,512]{1,0:T(8,128)(2,1)S(1)}, bf16[128,512]{1,0:T(8,128)(2,1)S(1)}, u32[]{:S(2)}, u32[]{:S(2)}) collective-permute-start(bf16[128,512]{1,0:T(8,128)(2,1)S(1)} %get-tuple-element.8), channel_id=1, source_target_pairs={{0,24},{8,16},{16,8},{24,0},{1,25},{9,17},{17,9},{25,1},{2,26},{10... | collective-permute-start | bytes 393224 | tf_op jit(solution)/shard_map/ppermute | solution.py:37
  108.7 2.2 %collective-permute-done.26 = bf16[128,512]{1,0:T(8,128)(2,1)S(1)} collective-permute-done((bf16[128,512]{1,0:T(8,128)(2,1)S(1)}, bf16[128,512]{1,0:T(8,128)(2,1)S(1)}, u32[]{:S(2)}, u32[]{:S(2)}) %collective-permute-start.26) | collective-permute-done | bytes 131104 | tf_op jit(solution)/shard_map/ppermute | solution.py:37
  113.4 1.9 %collective-permute-done.15 = bf16[128,512]{1,0:T(8,128)(2,1)S(1)} collective-permute-done((bf16[128,512]{1,0:T(8,128)(2,1)S(1)}, bf16[128,512]{1,0:T(8,128)(2,1)S(1)}, u32[]{:S(2)}, u32[]{:S(2)}) %collective-permute-start.15) | collective-permute-done | bytes 131104 | tf_op jit(solution)/shard_map/ppermute | solution.py:37
  119.3 7.3 %collective-permute-done.40 = bf16[128,512]{1,0:T(8,128)(2,1)S(1)} collective-permute-done((bf16[128,512]{1,0:T(8,128)(2,1)S(1)}, bf16[128,512]{1,0:T(8,128)(2,1)S(1)}, u32[]{:S(2)}, u32[]{:S(2)}) %collective-permute-start.40) | collective-permute-done | bytes 131104 | tf_op jit(solution)/shard_map/ppermute | solution.py:40
  126.9 7.3 %collective-permute-done.28 = bf16[128,512]{1,0:T(8,128)(2,1)S(1)} collective-permute-done((bf16[128,512]{1,0:T(8,128)(2,1)S(1)}, bf16[128,512]{1,0:T(8,128)(2,1)S(1)}, u32[]{:S(2)}, u32[]{:S(2)}) %collective-permute-start.28) | collective-permute-done | bytes 131104 | tf_op jit(solution)/shard_map/ppermute | solution.py:40
  134.5 4.6 %collective-permute-done.16 = bf16[128,512]{1,0:T(8,128)(2,1)S(1)} collective-permute-done((bf16[128,512]{1,0:T(8,128)(2,1)S(1)}, bf16[128,512]{1,0:T(8,128)(2,1)S(1)}, u32[]{:S(2)}, u32[]{:S(2)}) %collective-permute-start.16) | collective-permute-done | bytes 131104 | tf_op jit(solution)/shard_map/ppermute | solution.py:40
  140.3 3.8 %collective-permute-done.2 = bf16[128,512]{1,0:T(8,128)(2,1)S(1)} collective-permute-done((bf16[128,512]{1,0:T(8,128)(2,1)S(1)}, bf16[128,512]{1,0:T(8,128)(2,1)S(1)}, u32[]{:S(2)}, u32[]{:S(2)}) %collective-permute-start.2) | collective-permute-done | bytes 131104 | tf_op jit(solution)/shard_map/ppermute | solution.py:37
  145.2 2.6 %fusion = bf16[1,1024,1024]{2,1,0:T(8,128)(2,1)} fusion(bf16[1024,1024]{1,0:T(8,128)(2,1)S(1)} %collective-permute-done.41, bf16[128,512]{1,0:T(8,128)(2,1)S(1)} %get-tuple-element.36, bf16[128,512]{1,0:T(8,128)(2,1)S(1)} %get-tuple-element.35, bf16[128,512]{1,0:T(8,128)(2,1)S(1)} %get-tuple-element.25, bf16[128,512]{1,0:T(8,128)(2,1)S(1)} %get-tuple-element.24, ...), kind=kOutput, calls=%fused_computation.2 | convolution fusion | flops 1090519040 | bytes 6291456 | tf_op jit(solution)/shard_map/dot_general | solution.py:11
  147.8 2.6 %fusion.1 = bf16[1,1024,1024]{2,1,0:T(8,128)(2,1)} fusion(bf16[1024,1024]{1,0:T(8,128)(2,1)S(1)} %collective-permute-done.42, bf16[128,512]{1,0:T(8,128)(2,1)S(1)} %get-tuple-element.32, bf16[128,512]{1,0:T(8,128)(2,1)S(1)} %get-tuple-element.31, bf16[128,512]{1,0:T(8,128)(2,1)S(1)} %get-tuple-element.21, bf16[128,512]{1,0:T(8,128)(2,1)S(1)} %get-tuple-element.20, ...), kind=kOutput, calls=%fused_computation.3 | convolution fusion | flops 1090519040 | bytes 6291456 | tf_op jit(solution)/shard_map/dot_general | solution.py:11
  (131 shorter events, 64.9 us)
Async XLA Ops:
  0.6 68.6 %collective-permute-start.1 = (bf16[1024,1024]{1,0:T(8,128)(2,1)}, bf16[1024,1024]{1,0:T(8,128)(2,1)}, u32[]{:S(2)}, u32[]{:S(2)}) collective-permute-start(bf16[1024,1024]{1,0:T(8,128)(2,1)} %bitcast.64), channel_id=1, source_target_pairs={{0,1},{1,0},{2,3},{3,2},{4,5},{5,4},{6,7},{7,6},{8,9},{9,8},{10,11... | collective-permute-start | bytes 6291464 | tf_op jit(solution)/shard_map/ppermute | solution.py:34
  2.8 22.3 %collective-permute-start.33 = (bf16[128,512]{1,0:T(8,128)(2,1)}, bf16[128,512]{1,0:T(8,128)(2,1)}, u32[]{:S(2)}, u32[]{:S(2)}) collective-permute-start(bf16[128,512]{1,0:T(8,128)(2,1)} %convolution_convert_fusion.14), channel_id=1, source_target_pairs={{0,4},{2,6},{4,0},{6,2},{1,5},{3,7},{5,1},{7,3},{8,12},{10,14},{12... | collective-permute-start | bytes 393224 | tf_op jit(solution)/shard_map/ppermute | solution.py:40
  10.1 16.5 %collective-permute-start.29 = (bf16[128,512]{1,0:T(8,128)(2,1)}, bf16[128,512]{1,0:T(8,128)(2,1)}, u32[]{:S(2)}, u32[]{:S(2)}) collective-permute-start(bf16[128,512]{1,0:T(8,128)(2,1)} %convolution_convert_fusion.15), channel_id=1, source_target_pairs={{0,4},{2,6},{4,0},{6,2},{1,5},{3,7},{5,1},{7,3},{8,12},{10,14},{12... | collective-permute-start | bytes 393224 | tf_op jit(solution)/shard_map/ppermute | solution.py:40
  11.2 17.2 %collective-permute-start.21 = (bf16[128,512]{1,0:T(8,128)(2,1)}, bf16[128,512]{1,0:T(8,128)(2,1)}, u32[]{:S(2)}, u32[]{:S(2)}) collective-permute-start(bf16[128,512]{1,0:T(8,128)(2,1)} %convolution_convert_fusion.16), channel_id=1, source_target_pairs={{0,6},{2,0},{4,2},{6,4},{1,7},{3,1},{5,3},{7,5},{8,14},{10,8},{12,... | collective-permute-start | bytes 393224 | tf_op jit(solution)/shard_map/ppermute | solution.py:40
  16.8 12.0 %collective-permute-start.17 = (bf16[128,512]{1,0:T(8,128)(2,1)}, bf16[128,512]{1,0:T(8,128)(2,1)S(1)}, u32[]{:S(2)}, u32[]{:S(2)}) collective-permute-start(bf16[128,512]{1,0:T(8,128)(2,1)} %convolution_convert_fusion.17), channel_id=1, source_target_pairs={{0,6},{2,0},{4,2},{6,4},{1,7},{3,1},{5,3},{7,5},{8,14},{10,8},{12,... | collective-permute-start | bytes 393224 | tf_op jit(solution)/shard_map/ppermute | solution.py:40
  25.0 7.3 %collective-permute-start.9 = (bf16[128,512]{1,0:T(8,128)(2,1)S(1)}, bf16[128,512]{1,0:T(8,128)(2,1)S(1)}, u32[]{:S(2)}, u32[]{:S(2)}) collective-permute-start(bf16[128,512]{1,0:T(8,128)(2,1)S(1)} %convolution_convert_fusion.18), channel_id=1, source_target_pairs={{0,2},{2,4},{4,6},{6,0},{1,3},{3,5},{5,7},{7,1},{8,10},{10,12},{12... | collective-permute-start | bytes 393224 | tf_op jit(solution)/shard_map/ppermute | solution.py:40
  26.7 7.1 %collective-permute-start.34 = (bf16[128,512]{1,0:T(8,128)(2,1)}, bf16[128,512]{1,0:T(8,128)(2,1)S(1)}, u32[]{:S(2)}, u32[]{:S(2)}) collective-permute-start(bf16[128,512]{1,0:T(8,128)(2,1)} %collective-permute-done.33), channel_id=1, source_target_pairs={{0,16},{8,24},{16,0},{24,8},{1,17},{9,25},{17,1},{25,9},{2,18},{10... | collective-permute-start | bytes 393224 | tf_op jit(solution)/shard_map/ppermute | solution.py:37
  28.4 7.0 %collective-permute-start.5 = (bf16[128,512]{1,0:T(8,128)(2,1)S(1)}, bf16[128,512]{1,0:T(8,128)(2,1)S(1)}, u32[]{:S(2)}, u32[]{:S(2)}) collective-permute-start(bf16[128,512]{1,0:T(8,128)(2,1)S(1)} %convolution_convert_fusion.19), channel_id=1, source_target_pairs={{0,2},{2,4},{4,6},{6,0},{1,3},{3,5},{5,7},{7,1},{8,10},{10,12},{12... | collective-permute-start | bytes 393224 | tf_op jit(solution)/shard_map/ppermute | solution.py:40
  28.7 6.7 %collective-permute-start.36 = (bf16[128,512]{1,0:T(8,128)(2,1)}, bf16[128,512]{1,0:T(8,128)(2,1)S(1)}, u32[]{:S(2)}, u32[]{:S(2)}) collective-permute-start(bf16[128,512]{1,0:T(8,128)(2,1)} %collective-permute-done.33), channel_id=1, source_target_pairs={{0,8},{8,0},{16,24},{24,16},{1,9},{9,1},{17,25},{25,17},{2,10},{10... | collective-permute-start | bytes 393224 | tf_op jit(solution)/shard_map/ppermute | solution.py:37
  35.4 36.4 %collective-permute-start = (bf16[1024,1024]{1,0:T(8,128)(2,1)S(1)}, bf16[1024,1024]{1,0:T(8,128)(2,1)S(1)}, u32[]{:S(2)}, u32[]{:S(2)}) collective-permute-start(bf16[1024,1024]{1,0:T(8,128)(2,1)S(1)} %bitcast.65), channel_id=1, source_target_pairs={{0,1},{1,0},{2,3},{3,2},{4,5},{5,4},{6,7},{7,6},{8,9},{9,8},{10,11... | collective-permute-start | bytes 6291464 | tf_op jit(solution)/shard_map/ppermute | solution.py:34
  35.4 6.8 %collective-permute-start.32 = (bf16[128,512]{1,0:T(8,128)(2,1)}, bf16[128,512]{1,0:T(8,128)(2,1)S(1)}, u32[]{:S(2)}, u32[]{:S(2)}) collective-permute-start(bf16[128,512]{1,0:T(8,128)(2,1)} %collective-permute-done.29), channel_id=1, source_target_pairs={{0,16},{8,24},{16,0},{24,8},{1,17},{9,25},{17,1},{25,9},{2,18},{10... | collective-permute-start | bytes 393224 | tf_op jit(solution)/shard_map/ppermute | solution.py:37
  38.0 6.8 %collective-permute-start.22 = (bf16[128,512]{1,0:T(8,128)(2,1)}, bf16[128,512]{1,0:T(8,128)(2,1)S(1)}, u32[]{:S(2)}, u32[]{:S(2)}) collective-permute-start(bf16[128,512]{1,0:T(8,128)(2,1)} %collective-permute-done.21), channel_id=1, source_target_pairs={{0,16},{8,24},{16,0},{24,8},{1,17},{9,25},{17,1},{25,9},{2,18},{10... | collective-permute-start | bytes 393224 | tf_op jit(solution)/shard_map/ppermute | solution.py:37
  39.9 7.3 %collective-permute-start.31 = (bf16[128,512]{1,0:T(8,128)(2,1)S(1)}, bf16[128,512]{1,0:T(8,128)(2,1)S(1)}, u32[]{:S(2)}, u32[]{:S(2)}) collective-permute-start(bf16[128,512]{1,0:T(8,128)(2,1)S(1)} %collective-permute-done.30), channel_id=1, source_target_pairs={{0,16},{8,24},{16,0},{24,8},{1,17},{9,25},{17,1},{25,9},{2,18},{10... | collective-permute-start | bytes 393224 | tf_op jit(solution)/shard_map/ppermute | solution.py:37
  42.3 7.4 %collective-permute-start.24 = (bf16[128,512]{1,0:T(8,128)(2,1)}, bf16[128,512]{1,0:T(8,128)(2,1)S(1)}, u32[]{:S(2)}, u32[]{:S(2)}) collective-permute-start(bf16[128,512]{1,0:T(8,128)(2,1)} %collective-permute-done.21), channel_id=1, source_target_pairs={{0,8},{8,0},{16,24},{24,16},{1,9},{9,1},{17,25},{25,17},{2,10},{10... | collective-permute-start | bytes 393224 | tf_op jit(solution)/shard_map/ppermute | solution.py:37
  44.8 6.6 %collective-permute-start.18 = (bf16[128,512]{1,0:T(8,128)(2,1)S(1)}, bf16[128,512]{1,0:T(8,128)(2,1)S(1)}, u32[]{:S(2)}, u32[]{:S(2)}) collective-permute-start(bf16[128,512]{1,0:T(8,128)(2,1)S(1)} %collective-permute-done.17), channel_id=1, source_target_pairs={{0,8},{8,0},{16,24},{24,16},{1,9},{9,1},{17,25},{25,17},{2,10},{10... | collective-permute-start | bytes 393224 | tf_op jit(solution)/shard_map/ppermute | solution.py:37
  49.6 6.4 %collective-permute-start.20 = (bf16[128,512]{1,0:T(8,128)(2,1)S(1)}, bf16[128,512]{1,0:T(8,128)(2,1)S(1)}, u32[]{:S(2)}, u32[]{:S(2)}) collective-permute-start(bf16[128,512]{1,0:T(8,128)(2,1)S(1)} %collective-permute-done.17), channel_id=1, source_target_pairs={{0,16},{8,24},{16,0},{24,8},{1,17},{9,25},{17,1},{25,9},{2,18},{10... | collective-permute-start | bytes 393224 | tf_op jit(solution)/shard_map/ppermute | solution.py:37
  51.4 7.3 %collective-permute-start.10 = (bf16[128,512]{1,0:T(8,128)(2,1)S(1)}, bf16[128,512]{1,0:T(8,128)(2,1)S(1)}, u32[]{:S(2)}, u32[]{:S(2)}) collective-permute-start(bf16[128,512]{1,0:T(8,128)(2,1)S(1)} %collective-permute-done.9), channel_id=1, source_target_pairs={{0,16},{8,24},{16,0},{24,8},{1,17},{9,25},{17,1},{25,9},{2,18},{10... | collective-permute-start | bytes 393224 | tf_op jit(solution)/shard_map/ppermute | solution.py:37
  53.1 7.0 %collective-permute-start.19 = (bf16[128,512]{1,0:T(8,128)(2,1)S(1)}, bf16[128,512]{1,0:T(8,128)(2,1)S(1)}, u32[]{:S(2)}, u32[]{:S(2)}) collective-permute-start(bf16[128,512]{1,0:T(8,128)(2,1)S(1)} %collective-permute-done.18), channel_id=1, source_target_pairs={{0,16},{8,24},{16,0},{24,8},{1,17},{9,25},{17,1},{25,9},{2,18},{10... | collective-permute-start | bytes 393224 | tf_op jit(solution)/shard_map/ppermute | solution.py:37
  91.0 13.9 %collective-permute-start.39 = (bf16[128,512]{1,0:T(8,128)(2,1)S(1)}, bf16[128,512]{1,0:T(8,128)(2,1)S(1)}, u32[]{:S(2)}, u32[]{:S(2)}) collective-permute-start(bf16[128,512]{1,0:T(8,128)(2,1)S(1)} %get-tuple-element.30), channel_id=1, source_target_pairs={{0,24},{8,16},{16,8},{24,0},{1,25},{9,17},{17,9},{25,1},{2,26},{10... | collective-permute-start | bytes 393224 | tf_op jit(solution)/shard_map/ppermute | solution.py:37
  92.6 13.8 %collective-permute-start.38 = (bf16[128,512]{1,0:T(8,128)(2,1)S(1)}, bf16[128,512]{1,0:T(8,128)(2,1)S(1)}, u32[]{:S(2)}, u32[]{:S(2)}) collective-permute-start(bf16[128,512]{1,0:T(8,128)(2,1)S(1)} %get-tuple-element.29), channel_id=1, source_target_pairs={{0,16},{8,24},{16,0},{24,8},{1,17},{9,25},{17,1},{25,9},{2,18},{10... | collective-permute-start | bytes 393224 | tf_op jit(solution)/shard_map/ppermute | solution.py:37
  94.0 12.9 %collective-permute-start.37 = (bf16[128,512]{1,0:T(8,128)(2,1)S(1)}, bf16[128,512]{1,0:T(8,128)(2,1)S(1)}, u32[]{:S(2)}, u32[]{:S(2)}) collective-permute-start(bf16[128,512]{1,0:T(8,128)(2,1)S(1)} %get-tuple-element.28), channel_id=1, source_target_pairs={{0,8},{8,0},{16,24},{24,16},{1,9},{9,1},{17,25},{25,17},{2,10},{10... | collective-permute-start | bytes 393224 | tf_op jit(solution)/shard_map/ppermute | solution.py:37
  97.1 10.0 %collective-permute-start.27 = (bf16[128,512]{1,0:T(8,128)(2,1)S(1)}, bf16[128,512]{1,0:T(8,128)(2,1)S(1)}, u32[]{:S(2)}, u32[]{:S(2)}) collective-permute-start(bf16[128,512]{1,0:T(8,128)(2,1)S(1)} %get-tuple-element.19), channel_id=1, source_target_pairs={{0,24},{8,16},{16,8},{24,0},{1,25},{9,17},{17,9},{25,1},{2,26},{10... | collective-permute-start | bytes 393224 | tf_op jit(solution)/shard_map/ppermute | solution.py:37
  98.7 46.5 %collective-permute-start.41 = (bf16[1024,1024]{1,0:T(8,128)(2,1)S(1)}, bf16[1024,1024]{1,0:T(8,128)(2,1)S(1)}, u32[]{:S(2)}, u32[]{:S(2)}) collective-permute-start(bf16[1024,1024]{1,0:T(8,128)(2,1)S(1)} %convolution_convert_fusion.1), channel_id=1, source_target_pairs={{0,1},{1,0},{2,3},{3,2},{4,5},{5,4},{6,7},{7,6},{8,9},{9,8},{10,11... | collective-permute-start | bytes 6291464 | tf_op jit(solution)/shard_map/ppermute | solution.py:34
  106.4 6.3 %collective-permute-start.25 = (bf16[128,512]{1,0:T(8,128)(2,1)S(1)}, bf16[128,512]{1,0:T(8,128)(2,1)S(1)}, u32[]{:S(2)}, u32[]{:S(2)}) collective-permute-start(bf16[128,512]{1,0:T(8,128)(2,1)S(1)} %get-tuple-element.17), channel_id=1, source_target_pairs={{0,8},{8,0},{16,24},{24,16},{1,9},{9,1},{17,25},{25,17},{2,10},{10... | collective-permute-start | bytes 393224 | tf_op jit(solution)/shard_map/ppermute | solution.py:37
  106.9 40.9 %collective-permute-start.42 = (bf16[1024,1024]{1,0:T(8,128)(2,1)S(1)}, bf16[1024,1024]{1,0:T(8,128)(2,1)S(1)}, u32[]{:S(2)}, u32[]{:S(2)}) collective-permute-start(bf16[1024,1024]{1,0:T(8,128)(2,1)S(1)} %convolution_convert_fusion), channel_id=1, source_target_pairs={{0,1},{1,0},{2,3},{3,2},{4,5},{5,4},{6,7},{7,6},{8,9},{9,8},{10,11... | collective-permute-start | bytes 6291464 | tf_op jit(solution)/shard_map/ppermute | solution.py:34
  107.1 8.2 %collective-permute-start.15 = (bf16[128,512]{1,0:T(8,128)(2,1)S(1)}, bf16[128,512]{1,0:T(8,128)(2,1)S(1)}, u32[]{:S(2)}, u32[]{:S(2)}) collective-permute-start(bf16[128,512]{1,0:T(8,128)(2,1)S(1)} %get-tuple-element.8), channel_id=1, source_target_pairs={{0,24},{8,16},{16,8},{24,0},{1,25},{9,17},{17,9},{25,1},{2,26},{10... | collective-permute-start | bytes 393224 | tf_op jit(solution)/shard_map/ppermute | solution.py:37
  110.9 6.8 %collective-permute-start.14 = (bf16[128,512]{1,0:T(8,128)(2,1)S(1)}, bf16[128,512]{1,0:T(8,128)(2,1)S(1)}, u32[]{:S(2)}, u32[]{:S(2)}) collective-permute-start(bf16[128,512]{1,0:T(8,128)(2,1)S(1)} %get-tuple-element.7), channel_id=1, source_target_pairs={{0,16},{8,24},{16,0},{24,8},{1,17},{9,25},{17,1},{25,9},{2,18},{10... | collective-permute-start | bytes 393224 | tf_op jit(solution)/shard_map/ppermute | solution.py:37
  112.7 6.4 %collective-permute-start.13 = (bf16[128,512]{1,0:T(8,128)(2,1)S(1)}, bf16[128,512]{1,0:T(8,128)(2,1)S(1)}, u32[]{:S(2)}, u32[]{:S(2)}) collective-permute-start(bf16[128,512]{1,0:T(8,128)(2,1)S(1)} %get-tuple-element.6), channel_id=1, source_target_pairs={{0,8},{8,0},{16,24},{24,16},{1,9},{9,1},{17,25},{25,17},{2,10},{10... | collective-permute-start | bytes 393224 | tf_op jit(solution)/shard_map/ppermute | solution.py:37
  115.3 24.9 %collective-permute-start.4 = (bf16[128,512]{1,0:T(8,128)(2,1)S(1)}, bf16[128,512]{1,0:T(8,128)(2,1)S(1)}, u32[]{:S(2)}, u32[]{:S(2)}) collective-permute-start(bf16[128,512]{1,0:T(8,128)(2,1)S(1)} %get-tuple-element.5), channel_id=1, source_target_pairs={{0,24},{8,16},{16,8},{24,0},{1,25},{9,17},{17,9},{25,1},{2,26},{10... | collective-permute-start | bytes 393224 | tf_op jit(solution)/shard_map/ppermute | solution.py:37
  117.7 22.6 %collective-permute-start.3 = (bf16[128,512]{1,0:T(8,128)(2,1)S(1)}, bf16[128,512]{1,0:T(8,128)(2,1)S(1)}, u32[]{:S(2)}, u32[]{:S(2)}) collective-permute-start(bf16[128,512]{1,0:T(8,128)(2,1)S(1)} %get-tuple-element.4), channel_id=1, source_target_pairs={{0,16},{8,24},{16,0},{24,8},{1,17},{9,25},{17,1},{25,9},{2,18},{10... | collective-permute-start | bytes 393224 | tf_op jit(solution)/shard_map/ppermute | solution.py:37
  119.1 7.5 %collective-permute-start.40 = (bf16[128,512]{1,0:T(8,128)(2,1)S(1)}, bf16[128,512]{1,0:T(8,128)(2,1)S(1)}, u32[]{:S(2)}, u32[]{:S(2)}) collective-permute-start(bf16[128,512]{1,0:T(8,128)(2,1)S(1)} %add_convert_fusion.2), channel_id=1, source_target_pairs={{0,4},{2,6},{4,0},{6,2},{1,5},{3,7},{5,1},{7,3},{8,12},{10,14},{12... | collective-permute-start | bytes 393224 | tf_op jit(solution)/shard_map/ppermute | solution.py:40
  126.6 7.6 %collective-permute-start.28 = (bf16[128,512]{1,0:T(8,128)(2,1)S(1)}, bf16[128,512]{1,0:T(8,128)(2,1)S(1)}, u32[]{:S(2)}, u32[]{:S(2)}) collective-permute-start(bf16[128,512]{1,0:T(8,128)(2,1)S(1)} %add_convert_fusion.3), channel_id=1, source_target_pairs={{0,2},{2,4},{4,6},{6,0},{1,3},{3,5},{5,7},{7,1},{8,10},{10,12},{12... | collective-permute-start | bytes 393224 | tf_op jit(solution)/shard_map/ppermute | solution.py:40
  (19 other events, 127.9 us)

commit v2 on v1

v2 whole, which is shorter than its diff:
```python
import functools

import jax
import jax.numpy as jnp
from jax import lax
from jax.experimental import pallas as pl
from jax.experimental.pallas import tpu as pltpu
from jax.sharding import PartitionSpec as P

F32 = jnp.float32
BF16 = jnp.bfloat16
I32 = jnp.int32
ANY = pl.BlockSpec(memory_space=pl.ANY)
VMEM = pl.BlockSpec(memory_space=pltpu.VMEM)
SMEM = pl.BlockSpec(memory_space=pltpu.SMEM)
LIMIT = 44 * 2**20


def dot(lhs, rhs, left=1, right=0):
    return lax.dot_general(lhs, rhs, (((left,), (right,)), ((), ())), preferred_element_type=F32)


def hits(position, first, rows):
    ids = lax.broadcasted_iota(I32, (rows, position.shape[1]), 0) + first
    return ids == position


def gate_of(hit, gate):
    return jnp.sum(jnp.where(hit, gate, 0.0), axis=1, keepdims=True)


def place_kernel(spans, where, position, gate, tok, grad, *outs):
    share = tok.shape[1]
    for k, (rows, out) in enumerate(zip(spans, outs)):
        hit = hits(position[...], where[k], rows)
        hot = hit.astype(BF16)
        out[:, :share] = dot(hot, tok[...]).astype(BF16)
        out[:, share:] = (dot(hot, grad[...]) * gate_of(hit, gate[...])).astype(BF16)


def place(spans, firsts, quarter, position, gate, tokens, grad_output, share):
    count = tokens.shape[0]
    where = jnp.stack(list(firsts) + [quarter]).astype(I32)
    column = lambda i, w: (0, w[len(spans)])
    full = lambda shape: pl.BlockSpec(shape, lambda i, w: (0, 0))
    return pl.pallas_call(
        functools.partial(place_kernel, spans),
        out_shape=[jax.ShapeDtypeStruct((rows, 2 * share), BF16) for rows in spans],
        grid_spec=pltpu.PrefetchScalarGridSpec(
            num_scalar_prefetch=1,
            grid=(1,),
            in_specs=[
                full((1, count)),
                full((1, count)),
                pl.BlockSpec((count, share), column),
                pl.BlockSpec((count, share), column),
            ],
            out_specs=[full((rows, 2 * share)) for rows in spans],
        ),
        compiler_params=pltpu.CompilerParams(vmem_limit_bytes=LIMIT),
        cost_estimate=pl.CostEstimate(
            flops=4 * sum(spans) * count * share, bytes_accessed=4 * (count + sum(spans)) * share, transcendentals=0
        ),
        name="place_rows",
    )(where, position, gate, tokens, grad_output)


def gelu_parts(pre):
    c = 0.7978845608028654
    square = pre * pre
    th = jnp.tanh(c * (pre + 0.044715 * (pre * square)))
    half = 0.5 * (1.0 + th)
    return pre * half, half + 0.5 * pre * (1.0 - th * th) * (c + (3 * 0.044715 * c) * square)


def expert_kernel(own_rows, chunk_rows, base, aliased, where, *refs):
    refs = list(refs)
    take = lambda n: [refs.pop(0) for _ in range(n)]
    if own_rows:
        position, gate, tokens, grad_output = take(4)
    chunks = [take(5) for _ in chunk_rows]
    weights = take(4)
    if aliased:
        take(4)
    tok_out, grad_out, hidden_out, slope_out = take(4)
    blocks = take(4)
    tok, grad, up, down, hidden, slope, back = take(7)
    if own_rows:
        tokens_in, grad_in = take(2)
    (sem,) = take(1)
    rows, width = tok.shape
    half, share = width // 2, width // 4
    order, first, half_start = where[0], where[1], where[2]
    count = [0]

    def copy(src, dst):
        c = pltpu.make_async_copy(src, dst, sem.at[count[0]])
        count[0] += 1
        c.start()
        return c

    waits = []
    if own_rows:
        other_start = half - half_start
        for src, dst in ((tokens, tokens_in), (grad_output, grad_in)):
            for start, place_at in ((half_start, 0), (other_start, half)):
                start = pl.multiple_of(start, half)
                waits.append(copy(src.at[:, pl.ds(start, half)], dst.at[:, pl.ds(place_at, half)]))
    at = own_rows
    for (z, x, y, tok_d, grad_d), n in zip(chunks, chunk_rows):
        tok_slots = [r.at[:, pl.ds(0, share)] for r in (z, x, y)] + [tok_d]
        grad_slots = [r.at[:, pl.ds(share, share)] for r in (z, x, y)] + [grad_d]
        for j in range(4):
            columns = pl.ds(pl.multiple_of((order ^ j) * share, share), share)
            waits.append(copy(tok_slots[j], tok.at[pl.ds(at, n), columns]))
            waits.append(copy(grad_slots[j], grad.at[pl.ds(at, n), columns]))
        at += n
    up_own, up_other, down_own, down_other = weights
    up_waits = [copy(up_own, up.at[pl.ds(0, half), :]), copy(up_other, up.at[pl.ds(half, half), :])]
    down_waits = [copy(down_own, down.at[pl.ds(0, half), :]), copy(down_other, down.at[pl.ds(half, half), :])]
    for w in waits:
        w.wait()
    if own_rows:
        hit = hits(position[...], first, own_rows)
        hot = hit.astype(BF16)
        tok[:own_rows, :] = dot(hot, tokens_in[...]).astype(BF16)
        grad[:own_rows, :] = (dot(hot, grad_in[...]) * gate_of(hit, gate[...])).astype(BF16)
    outs = [copy(tok, tok_out.at[pl.ds(base, rows), :]), copy(grad, grad_out.at[pl.ds(base, rows), :])]
    for w in up_waits + down_waits:
        w.wait()
    hid = hidden.shape[1]
    step = 256
    for n in range(0, hid, step):
        pre = dot(tok[...], up[:, n : n + step])
        hidden_grad = dot(grad[...], down[:, n : n + step])
        act, deriv = gelu_parts(pre)
        hidden[:, n : n + step] = act.astype(BF16)
        slope[:, n : n + step] = (hidden_grad * deriv).astype(BF16)
    outs.append(copy(hidden, hidden_out.at[pl.ds(base, rows), :]))
    outs.append(copy(slope, slope_out.at[pl.ds(base, rows), :]))
    for n in range(4):
        back[n] = dot(slope[...], up[pl.ds(n * share, share), :], 1, 1).astype(BF16)
    for j in range(4):
        outs.append(copy(back.at[order ^ j], blocks[j]))
    for w in outs:
        w.wait()


def expert_rows(where, own, chunks, weights, total_rows, base, previous):
    own_rows = own[0] if own else 0
    chunk_rows = [c[0].shape[0] for c in chunks]
    rows = own_rows + sum(chunk_rows)
    half, hid = weights[0].shape
    width, share = 2 * half, half // 2
    operands = [where]
    specs = [SMEM]
    if own:
        operands += own[1:]
        specs += [VMEM, VMEM, ANY, ANY]
    for c in chunks:
        operands += c
        specs += [ANY] * 5
    operands += weights
    specs += [ANY] * 4
    aliases = {}
    if previous:
        aliases = {len(operands) + i: i for i in range(4)}
        operands += previous
        specs += [ANY] * 4
    shape = lambda *s: jax.ShapeDtypeStruct(s, BF16)
    buf = lambda *s: pltpu.VMEM(s, BF16)
    scratch = [
        buf(rows, width), buf(rows, width), buf(width, hid), buf(width, hid),
        buf(rows, hid), buf(rows, hid), buf(4, rows, share),
    ]
    copies = 4 + 8 * len(chunks) + 8
    if own:
        count = own[3].shape[0]
        scratch += [buf(count, width), buf(count, width)]
        copies += 4
    scratch.append(pltpu.SemaphoreType.DMA((copies,)))
    out = pl.pallas_call(
        functools.partial(expert_kernel, own_rows, chunk_rows, base, bool(previous)),
        out_shape=[shape(total_rows, width)] * 2 + [shape(total_rows, hid)] * 2 + [shape(rows, share)] * 4,
        in_specs=specs,
        out_specs=[ANY] * 8,
        scratch_shapes=scratch,
        input_output_aliases=aliases,
        compiler_params=pltpu.CompilerParams(vmem_limit_bytes=LIMIT),
        cost_estimate=pl.CostEstimate(
            flops=6 * rows * width * hid, bytes_accessed=4 * width * hid + 8 * rows * width, transcendentals=rows * hid
        ),
        name="expert_rows",
    )(*operands)
    return list(out[:4]), list(out[4:])


def unplace_kernel(spans, where, position, *refs):
    out = refs[-1]
    total = None
    for k, (rows, back) in enumerate(zip(spans, refs[:-1])):
        hot = hits(position[...], where[k], rows).astype(BF16)
        part = dot(hot, back[...], 0, 0)
        total = part if total is None else total + part
    out[...] = total.astype(BF16)


def unplace(firsts, position, backs):
    spans = [b.shape[0] for b in backs]
    count, share = position.shape[1], backs[0].shape[1]
    return pl.pallas_call(
        functools.partial(unplace_kernel, spans),
        out_shape=jax.ShapeDtypeStruct((count, share), BF16),
        in_specs=[SMEM] + [VMEM] * (1 + len(backs)),
        out_specs=VMEM,
        compiler_params=pltpu.CompilerParams(vmem_limit_bytes=LIMIT),
        cost_estimate=pl.CostEstimate(
            flops=2 * sum(spans) * count * share, bytes_accessed=2 * (count + sum(spans)) * share, transcendentals=0
        ),
        name="unplace_rows",
    )(jnp.stack(firsts).astype(I32), position, *backs)


def local(tokens, grad_output, gate_prob, expert_index, slot_index, up_weight, down_weight):
    experts = lax.axis_size("expert")
    tensor_size = lax.axis_size("tensor")
    e = lax.axis_index("expert")
    t = lax.axis_index("tensor")
    p = lax.axis_index("dp")
    tok_count, width = tokens.shape
    capacity = 2 * tok_count // experts
    share = width // tensor_size
    half = width // 2
    where = jnp.stack([t ^ (2 * p), e * capacity, p * half]).astype(I32)

    def swap(x):
        return lax.ppermute(x, "dp", [(0, 1), (1, 0)])

    def across(x, j):
        return lax.ppermute(x, "tensor", [(i, i ^ j) for i in range(tensor_size)])

    def shift(x, k):
        return lax.ppermute(x, "expert", [(i, (i + k) % experts) for i in range(experts)])

    def spread(rows):
        x, y = across(rows, 1), across(rows, 2)
        return [rows, x, y, across(y[:, :share], 1), across(x[:, share:], 2)]

    def collect(blocks):
        got = [across(blocks[j], j) for j in (1, 2, 3)]

        def total(lo, hi):
            terms = [b[lo:hi].astype(F32) for b in [blocks[0]] + got]
            return (terms[0] + terms[1] + (terms[2] + terms[3])).astype(BF16)

        return total

    up_own, down_own = up_weight[0], down_weight[0]
    weights = [up_own, swap(up_own), down_own, swap(down_own)]
    position = (expert_index * capacity + slot_index).reshape(1, tok_count)
    gate = gate_prob.reshape(1, tok_count)

    if experts == 4:
        shifts = (1, 3, 2)
        firsts = [((e + k) % experts) * capacity for k in shifts]
        sends = place([capacity] * 3, firsts, t, position, gate, tokens, grad_output, share)
        chunks = [spread(shift(rows, k)) for rows, k in zip(sends, shifts)]
        own = [capacity, position, gate, tokens, grad_output]
        kept, blocks = expert_rows(where, own, chunks[:2], weights, 4 * capacity, 0, None)
        total = collect(blocks)
        backs = [total(0, capacity)]
        backs += [shift(total(i * capacity, (i + 1) * capacity), -k) for i, k in ((1, 1), (2, 3))]
        kept, blocks = expert_rows(where, None, chunks[2:], weights, 4 * capacity, 3 * capacity, kept)
        backs.append(shift(collect(blocks)(0, capacity), -2))
        places = [e * capacity] + firsts
    else:
        rows = experts * capacity

        def exchange(x):
            moved = lax.all_to_all(
                x.reshape(experts, capacity, x.shape[1]), "expert", split_axis=0, concat_axis=0, tiled=True
            )
            return moved.reshape(rows, x.shape[1])

        (send,) = place([rows], [jnp.int32(0)], t, position, gate, tokens, grad_output, share)
        kept, blocks = expert_rows(where, None, [spread(exchange(send))], weights, rows, 0, None)
        backs = [exchange(collect(blocks)(0, rows))]
        places = [jnp.int32(0)]

    grad_tokens = unplace(places, position, backs)
    tok_rows, grad_rows, hidden, slope = kept

    def weight_grad(rows, out):
        got = swap(dot(rows[:, half:], out, 0, 0).astype(BF16))
        mine = dot(rows[:, :half], out, 0, 0).astype(BF16)
        return (mine.astype(F32) + got.astype(F32)).astype(BF16)[None]

    return grad_tokens, weight_grad(tok_rows, slope), weight_grad(grad_rows, hidden)


def solution(mesh):
    placed = (
        P(("expert", "dp"), None),
        P(("expert", "dp"), None),
        P(("expert", "dp")),
        P(("expert", "dp"), None),
        P(("expert", "dp"), None),
        P("expert", "dp", "tensor"),
        P("expert", "dp", "tensor"),
    )
    return jax.shard_map(
        local,
        mesh=mesh,
        in_specs=placed,
        out_specs=(
            P(("expert", "dp"), "tensor"),
            P("expert", "dp", "tensor"),
            P("expert", "dp", "tensor"),
        ),
        check_vma=False,
    )
```

time: 151 us -> 130 us (0.86)
  matrix products: 49.3 us -> 5.19 us
  Pallas kernels: 0 us -> 23 us
  starting transfers between devices: 48.6 us -> 36 us
  local copies, waits for them, and re-layouts: 1.2 us -> 11.9 us
  waiting for transfers between devices: 43.9 us -> 46.4 us
    dot_general x42 -> x4, matrix products: 49.3 us -> 5.19 us  [dot(): lax.dot_general(lhs, rhs, (((left,), (right,)), ((), ())), preferred_elem...]
    pallas_call x0 -> x4, Pallas kernels: none -> 23 us  [the longest x2 20.4 us: expert_rows(): pl.pallas_call(functools.partial(expert_kernel, own_rows, chunk_rows, bas...]
    ppermute x30 -> x18, starting transfers between devices: 37.7 us -> 24.8 us  [across(): return lax.ppermute(x, 'tensor', [(i, i ^ j) for i in range(tensor_size)])]
    unnamed x16 -> x32, local copies, waits for them, and re-layouts: 1.2 us -> 9.94 us
    broadcast_in_dim x0 -> x2, other arithmetic: none -> 4.63 us  [weight_grad(): return (mine.astype(F32) + got.astype(F32)).astype(BF16)[None]]
    ppermute x30 -> x18, waiting for transfers between devices: 21.8 us -> 25.9 us  [across(): return lax.ppermute(x, 'tensor', [(i, i ^ j) for i in range(tensor_size)])]
    select_n x10 -> x0, other arithmetic: 3.18 us -> none  [xor_order(): return [jnp.where(high, once[i ^ 2], once[i]) for i in range(4)]]
    slice x0 -> x6, local copies, waits for them, and re-layouts: none -> 2.01 us  [spread(): return [rows, x, y, across(y[:, :share], 1), across(x[:, share:], 2)]]
  transfers between devices with their start and end apart: 43 -> 28, of which waited for: 21 -> 13; matrix products, arithmetic and copies ran while one was open for 23% -> 7% of each run, Pallas kernels for 0% -> 12%
where the time goes in v2:
time: 130 us; the launch traced here: 129 us
  waiting for transfers between devices  46.4 us (36%)
  starting transfers between devices  36 us (28%)
  Pallas kernels  23 us (18%)
  local copies, waits for them, and re-layouts  11.9 us (9%)
  other arithmetic  5.84 us (4%)
  matrix products  5.19 us (4%)
    ppermute x18, waiting for transfers between devices, across(): return lax.ppermute(x, 'tensor', [(i, i ^ j) for i in range(tensor_size)])  25.9 us
    ppermute x18, starting transfers between devices, across(): return lax.ppermute(x, 'tensor', [(i, i ^ j) for i in range(tensor_size)])  24.8 us
    ppermute x6, waiting for transfers between devices, shift(): lax.ppermute(x, 'expert', [(i, (i + k) % experts) for i in range(experts)])  20.5 us
    pallas_call x2, Pallas kernels, expert_rows(): pl.pallas_call(functools.partial(expert_kernel, own_rows, chunk_rows, bas...  20.4 us
    ppermute x6, starting transfers between devices, shift(): lax.ppermute(x, 'expert', [(i, (i + k) % experts) for i in range(experts)])  9.96 us
    unnamed x32, local copies, waits for them, and re-layouts  9.94 us
    dot_general x4, matrix products, dot(): lax.dot_general(lhs, rhs, (((left,), (right,)), ((), ())), preferred_elem...  5.19 us
    broadcast_in_dim x2, other arithmetic, weight_grad(): return (mine.astype(F32) + got.astype(F32)).astype(BF16)[None]  4.63 us
  transfers between devices with their start and end apart: 28, of which 13 were waited for; matrix products, arithmetic and copies ran while one was open for 7% of the time, Pallas kernels for 12%

profile of v2, /device:TPU:0, one launch (start us, length us, event | category | flops | bytes accessed | tf_op | source)
XLA Modules:
  0.0 129.3 jit_solution(12296159843340789158)
XLA Ops:
  6.1 3.1 %collective-permute-start = (bf16[128,1024]{1,0:T(8,128)(2,1)S(1)}, bf16[128,1024]{1,0:T(8,128)(2,1)S(1)}, u32[]{:S(2)}, u32[]{:S(2)}) collective-permute-start(bf16[128,1024]{1,0:T(8,128)(2,1)S(1)} %get-tuple-element.22), channel_id=1, source_target_pairs={{0,2},{2,4},{4,6},{6,0},{1,3},{3,5},{5,7},{7,1},{8,10},{10,12},{12... | collective-permute-start | bytes 786440 | tf_op jit(solution)/shard_map/ppermute | solution.py:243
  9.1 2.1 %collective-permute-start.5 = (bf16[128,1024]{1,0:T(8,128)(2,1)S(1)}, bf16[128,1024]{1,0:T(8,128)(2,1)S(1)}, u32[]{:S(2)}, u32[]{:S(2)}) collective-permute-start(bf16[128,1024]{1,0:T(8,128)(2,1)S(1)} %get-tuple-element.23), channel_id=1, source_target_pairs={{0,6},{2,0},{4,2},{6,4},{1,7},{3,1},{5,3},{7,5},{8,14},{10,8},{12,... | collective-permute-start | bytes 786440 | tf_op jit(solution)/shard_map/ppermute | solution.py:243
  12.2 6.1 %collective-permute-done.refs_4_ = bf16[128,1024]{1,0:T(8,128)(2,1)S(1)} collective-permute-done((bf16[128,1024]{1,0:T(8,128)(2,1)S(1)}, bf16[128,1024]{1,0:T(8,128)(2,1)S(1)}, u32[]{:S(2)}, u32[]{:S(2)}) %collective-permute-start) | collective-permute-done | bytes 262176 | tf_op jit(solution)/shard_map/ppermute | solution.py:243
  18.3 1.8 %collective-permute-start.2 = (bf16[128,1024]{1,0:T(8,128)(2,1)S(1)}, bf16[128,1024]{1,0:T(8,128)(2,1)S(1)}, u32[]{:S(2)}, u32[]{:S(2)}) collective-permute-start(bf16[128,1024]{1,0:T(8,128)(2,1)S(1)} %collective-permute-done.refs_4_), channel_id=1, source_target_pairs={{0,16},{8,24},{16,0},{24,8},{1,17},{9,25},{17,1},{25,9},{2,18},{10... | collective-permute-start | bytes 786440 | tf_op jit(solution)/shard_map/ppermute | solution.py:240
  20.1 2.7 %collective-permute-done.5.refs_9_ = bf16[128,1024]{1,0:T(8,128)(2,1)S(1)} collective-permute-done((bf16[128,1024]{1,0:T(8,128)(2,1)S(1)}, bf16[128,1024]{1,0:T(8,128)(2,1)S(1)}, u32[]{:S(2)}, u32[]{:S(2)}) %collective-permute-start.5) | collective-permute-done | bytes 262176 | tf_op jit(solution)/shard_map/ppermute | solution.py:243
  22.8 1.5 %collective-permute-start.1 = (bf16[128,1024]{1,0:T(8,128)(2,1)S(1)}, bf16[128,1024]{1,0:T(8,128)(2,1)S(1)}, u32[]{:S(2)}, u32[]{:S(2)}) collective-permute-start(bf16[128,1024]{1,0:T(8,128)(2,1)S(1)} %collective-permute-done.refs_4_), channel_id=1, source_target_pairs={{0,8},{8,0},{16,24},{24,16},{1,9},{9,1},{17,25},{25,17},{2,10},{10... | collective-permute-start | bytes 786440 | tf_op jit(solution)/shard_map/ppermute | solution.py:240
  25.0 9.6 %collective-permute-done.17.refs_0_ = bf16[128,1024]{1,0:T(8,128)(2,1)S(1)} collective-permute-done((bf16[128,1024]{1,0:T(8,128)(2,1)S(1)}, bf16[128,1024]{1,0:T(8,128)(2,1)S(1)}, u32[]{:S(2)}, u32[]{:S(2)}) %collective-permute-start.17) | collective-permute-done | bytes 262176 | tf_op jit(solution)/shard_map/ppermute | solution.py:243
  34.6 1.5 %collective-permute-start.7 = (bf16[128,1024]{1,0:T(8,128)(2,1)S(1)}, bf16[128,1024]{1,0:T(8,128)(2,1)S(1)}, u32[]{:S(2)}, u32[]{:S(2)}) collective-permute-start(bf16[128,1024]{1,0:T(8,128)(2,1)S(1)} %collective-permute-done.5.refs_9_), channel_id=1, source_target_pairs={{0,16},{8,24},{16,0},{24,8},{1,17},{9,25},{17,1},{25,9},{2,18},{10... | collective-permute-start | bytes 786440 | tf_op jit(solution)/shard_map/ppermute | solution.py:240
  36.1 1.5 %collective-permute-start.6 = (bf16[128,1024]{1,0:T(8,128)(2,1)S(1)}, bf16[128,1024]{1,0:T(8,128)(2,1)S(1)}, u32[]{:S(2)}, u32[]{:S(2)}) collective-permute-start(bf16[128,1024]{1,0:T(8,128)(2,1)S(1)} %collective-permute-done.5.refs_9_), channel_id=1, source_target_pairs={{0,8},{8,0},{16,24},{24,16},{1,9},{9,1},{17,25},{25,17},{2,10},{10... | collective-permute-start | bytes 786440 | tf_op jit(solution)/shard_map/ppermute | solution.py:240
  38.8 4.9 %collective-permute-done.7.refs_11_ = bf16[128,1024]{1,0:T(8,128)(2,1)S(1)} collective-permute-done((bf16[128,1024]{1,0:T(8,128)(2,1)S(1)}, bf16[128,1024]{1,0:T(8,128)(2,1)S(1)}, u32[]{:S(2)}, u32[]{:S(2)}) %collective-permute-start.7) | collective-permute-done | bytes 262176 | tf_op jit(solution)/shard_map/ppermute | solution.py:240
  43.7 1.5 %collective-permute-start.18 = (bf16[128,1024]{1,0:T(8,128)(2,1)S(1)}, bf16[128,1024]{1,0:T(8,128)(2,1)S(1)}, u32[]{:S(2)}, u32[]{:S(2)}) collective-permute-start(bf16[128,1024]{1,0:T(8,128)(2,1)S(1)} %collective-permute-done.17.refs_0_), channel_id=1, source_target_pairs={{0,8},{8,0},{16,24},{24,16},{1,9},{9,1},{17,25},{25,17},{2,10},{10... | collective-permute-start | bytes 786440 | tf_op jit(solution)/shard_map/ppermute | solution.py:240
  48.4 1.5 %collective-permute-start.4 = (bf16[128,512]{1,0:T(8,128)(2,1)}, bf16[128,512]{1,0:T(8,128)(2,1)}, u32[]{:S(2)}, u32[]{:S(2)}) collective-permute-start(bf16[128,512]{1,0:T(8,128)(2,1)} %slice.89), channel_id=1, source_target_pairs={{0,16},{8,24},{16,0},{24,8},{1,17},{9,25},{17,1},{25,9},{2,18},{10... | collective-permute-start | bytes 393224 | tf_op jit(solution)/shard_map/ppermute | solution.py:240
  49.9 1.7 %collective-permute-done.18.refs_1_ = bf16[128,1024]{1,0:T(8,128)(2,1)S(1)} collective-permute-done((bf16[128,1024]{1,0:T(8,128)(2,1)S(1)}, bf16[128,1024]{1,0:T(8,128)(2,1)S(1)}, u32[]{:S(2)}, u32[]{:S(2)}) %collective-permute-start.18) | collective-permute-done | bytes 262176 | tf_op jit(solution)/shard_map/ppermute | solution.py:240
  51.6 1.5 %collective-permute-start.8 = (bf16[128,512]{1,0:T(8,128)(2,1)}, bf16[128,512]{1,0:T(8,128)(2,1)}, u32[]{:S(2)}, u32[]{:S(2)}) collective-permute-start(bf16[128,512]{1,0:T(8,128)(2,1)} %slice.90), channel_id=1, source_target_pairs={{0,8},{8,0},{16,24},{24,16},{1,9},{9,1},{17,25},{25,17},{2,10},{10... | collective-permute-start | bytes 393224 | tf_op jit(solution)/shard_map/ppermute | solution.py:240
  54.3 1.6 %collective-permute-start.9 = (bf16[128,512]{1,0:T(8,128)(2,1)}, bf16[128,512]{1,0:T(8,128)(2,1)}, u32[]{:S(2)}, u32[]{:S(2)}) collective-permute-start(bf16[128,512]{1,0:T(8,128)(2,1)} %slice.91), channel_id=1, source_target_pairs={{0,16},{8,24},{16,0},{24,8},{1,17},{9,25},{17,1},{25,9},{2,18},{10... | collective-permute-start | bytes 393224 | tf_op jit(solution)/shard_map/ppermute | solution.py:240
  56.0 1.6 %collective-permute-start.20 = (bf16[128,512]{1,0:T(8,128)(2,1)S(1)}, bf16[128,512]{1,0:T(8,128)(2,1)S(1)}, u32[]{:S(2)}, u32[]{:S(2)}) collective-permute-start(bf16[128,512]{1,0:T(8,128)(2,1)S(1)} %slice.101), channel_id=1, source_target_pairs={{0,8},{8,0},{16,24},{24,16},{1,9},{9,1},{17,25},{25,17},{2,10},{10... | collective-permute-start | bytes 393224 | tf_op jit(solution)/shard_map/ppermute | solution.py:240
  57.6 1.7 %collective-permute-start.21 = (bf16[128,512]{1,0:T(8,128)(2,1)S(1)}, bf16[128,512]{1,0:T(8,128)(2,1)S(1)}, u32[]{:S(2)}, u32[]{:S(2)}) collective-permute-start(bf16[128,512]{1,0:T(8,128)(2,1)S(1)} %slice.102), channel_id=1, source_target_pairs={{0,16},{8,24},{16,0},{24,8},{1,17},{9,25},{17,1},{25,9},{2,18},{10... | collective-permute-start | bytes 393224 | tf_op jit(solution)/shard_map/ppermute | solution.py:240
  63.7 12.3 %expert_rows.2 = (bf16[512,2048]{1,0:T(8,128)(2,1)S(1)}, bf16[512,2048]{1,0:T(8,128)(2,1)}, bf16[512,1024]{1,0:T(8,128)(2,1)S(1)}, bf16[512,1024]{1,0:T(8,128)(2...) custom-call(s32[3]{0:T(128)S(1)} %pad_add_fusion.1.where, ...), custom_call_target="tpu_custom_call" | custom-call | flops 4831838208 | bytes 14680064 | tf_op jit(solution)/shard_map/expert_rows/pallas_call | solution.py:182
  76.1 1.6 %copy-done.1 = bf16[512,2048]{1,0:T(8,128)(2,1)S(1)} copy-done((bf16[512,2048]{1,0:T(8,128)(2,1)S(1)}, bf16[512,2048]{1,0:T(8,128)(2,1)}, u32[]{:S(2)}) %copy-start.1) | copy-done | bytes 2097176
  77.7 8.0 %expert_rows.3 = (bf16[512,2048]{1,0:T(8,128)(2,1)S(1)}, bf16[512,2048]{1,0:T(8,128)(2,1)S(1)}, bf16[512,1024]{1,0:T(8,128)(2,1)S(1)}, bf16[512,1024]{1,0:T(8,12...) custom-call(s32[3]{0:T(128)S(1)} %pad_add_fusion.1.where, ...), custom_call_target="tpu_custom_call", output_to_operand_aliasing={{0}: (10, {}), {1}: (11, {}), {2}: (12, {}), {3}: (13, {})} | custom-call | flops 1610612736 | bytes 10485760 | tf_op jit(solution)/shard_map/expert_rows/pallas_call | solution.py:182
  85.7 1.3 %convolution_convert_fusion = bf16[1024,1024]{1,0:T(8,128)(2,1)S(1)} fusion(bf16[512,1024]{1,0:T(8,128)(2,1)S(1)} %get-tuple-element.40, bf16[512,2048]{1,0:T(8,128)(2,1)S(1)} %get-tuple-element.39), kind=kOutput, calls=%fused_computation.4 | convolution fusion | flops 1074790400 | bytes 4194304 | tf_op jit(solution)/shard_map/dot_general | solution.py:20
  89.0 1.5 %collective-permute-start.22 = (bf16[128,512]{1,0:T(8,128)(2,1)S(1)}, bf16[128,512]{1,0:T(8,128)(2,1)S(1)}, u32[]{:S(2)}, u32[]{:S(2)}) collective-permute-start(bf16[128,512]{1,0:T(8,128)(2,1)S(1)} %get-tuple-element.34), channel_id=1, source_target_pairs={{0,8},{8,0},{16,24},{24,16},{1,9},{9,1},{17,25},{25,17},{2,10},{10... | collective-permute-start | bytes 393224 | tf_op jit(solution)/shard_map/ppermute | solution.py:240
  92.6 2.2 %collective-permute-done.22 = bf16[128,512]{1,0:T(8,128)(2,1)S(1)} collective-permute-done((bf16[128,512]{1,0:T(8,128)(2,1)S(1)}, bf16[128,512]{1,0:T(8,128)(2,1)S(1)}, u32[]{:S(2)}, u32[]{:S(2)}) %collective-permute-start.22) | collective-permute-done | bytes 131104 | tf_op jit(solution)/shard_map/ppermute | solution.py:240
  94.8 2.1 %collective-permute-start.12 = (bf16[384,512]{1,0:T(8,128)(2,1)S(1)}, bf16[384,512]{1,0:T(8,128)(2,1)S(1)}, u32[]{:S(2)}, u32[]{:S(2)}) collective-permute-start(bf16[384,512]{1,0:T(8,128)(2,1)S(1)} %get-tuple-element.25), channel_id=1, source_target_pairs={{0,8},{8,0},{16,24},{24,16},{1,9},{9,1},{17,25},{25,17},{2,10},{10... | collective-permute-start | bytes 1179656 | tf_op jit(solution)/shard_map/ppermute | solution.py:240
  98.1 2.0 %collective-permute-start.13 = (bf16[384,512]{1,0:T(8,128)(2,1)S(1)}, bf16[384,512]{1,0:T(8,128)(2,1)S(1)}, u32[]{:S(2)}, u32[]{:S(2)}) collective-permute-start(bf16[384,512]{1,0:T(8,128)(2,1)S(1)} %get-tuple-element.26), channel_id=1, source_target_pairs={{0,16},{8,24},{16,0},{24,8},{1,17},{9,25},{17,1},{25,9},{2,18},{10... | collective-permute-start | bytes 1179656 | tf_op jit(solution)/shard_map/ppermute | solution.py:240
  102.0 4.9 %collective-permute-done.12 = bf16[384,512]{1,0:T(8,128)(2,1)S(1)} collective-permute-done((bf16[384,512]{1,0:T(8,128)(2,1)S(1)}, bf16[384,512]{1,0:T(8,128)(2,1)S(1)}, u32[]{:S(2)}, u32[]{:S(2)}) %collective-permute-start.12) | collective-permute-done | bytes 393248 | tf_op jit(solution)/shard_map/ppermute | solution.py:240
  106.9 8.5 %collective-permute-done.13 = bf16[384,512]{1,0:T(8,128)(2,1)S(1)} collective-permute-done((bf16[384,512]{1,0:T(8,128)(2,1)S(1)}, bf16[384,512]{1,0:T(8,128)(2,1)S(1)}, u32[]{:S(2)}, u32[]{:S(2)}) %collective-permute-start.13) | collective-permute-done | bytes 393248 | tf_op jit(solution)/shard_map/ppermute | solution.py:240
  115.7 3.8 %collective-permute-start.15 = (bf16[128,512]{1,0:T(8,128)(2,1)S(1)}, bf16[128,512]{1,0:T(8,128)(2,1)S(1)}, u32[]{:S(2)}, u32[]{:S(2)}) collective-permute-start(bf16[128,512]{1,0:T(8,128)(2,1)S(1)} %get-tuple-element.42), channel_id=1, source_target_pairs={{0,6},{2,0},{4,2},{6,4},{1,7},{3,1},{5,3},{7,5},{8,14},{10,8},{12,... | collective-permute-start | bytes 393224 | tf_op jit(solution)/shard_map/ppermute | solution.py:243
  120.8 2.1 %collective-permute-done.16.refs_2_ = bf16[128,512]{1,0:T(8,128)(2,1)S(1)} collective-permute-done((bf16[128,512]{1,0:T(8,128)(2,1)S(1)}, bf16[128,512]{1,0:T(8,128)(2,1)S(1)}, u32[]{:S(2)}, u32[]{:S(2)}) %collective-permute-start.16) | collective-permute-done | bytes 131104 | tf_op jit(solution)/shard_map/ppermute | solution.py:243
  122.9 1.7 %unplace_rows.1 = bf16[256,512]{1,0:T(8,128)(2,1)} custom-call(s32[4]{0:T(128)S(1)} %pad_add_fusion.where, s32[1,256]{1,0:T(1,128)S(1)} %add_bitcast_fusion.position.refs_0_, bf16[128,512]{1,0:T(8,128)(2,1)S(1)} %get-tuple-element.43.refs_0_, bf16[128,512]{1,0:T(8,128)(2,1)S(1)} %collective-permute-done.15.refs_1_, ...), custom_call_target="tpu_custom_call" | custom-call | flops 134217728 | bytes 786432 | tf_op jit(solution)/shard_map/unplace_rows/pallas_call | solution.py:211
  124.6 2.3 %fusion.1 = bf16[1,1024,1024]{2,1,0:T(8,128)(2,1)} fusion(bf16[1024,1024]{1,0:T(8,128)(2,1)S(1)} %collective-permute-done.27, bf16[1024,1024]{1,0:T(8,128)(2,1)S(1)} %fusion.3), kind=kLoop, calls=%fused_computation.3 | loop fusion | flops 4194304 | bytes 6291456 | tf_op jit(solution)/shard_map/broadcast_in_dim | solution.py:296
  126.9 2.3 %fusion = bf16[1,1024,1024]{2,1,0:T(8,128)(2,1)} fusion(bf16[1024,1024]{1,0:T(8,128)(2,1)S(1)} %collective-permute-done.26, bf16[1024,1024]{1,0:T(8,128)(2,1)S(1)} %fusion.6), kind=kLoop, calls=%fused_computation.2 | loop fusion | flops 4194304 | bytes 6291456 | tf_op jit(solution)/shard_map/broadcast_in_dim | solution.py:296
  (78 shorter events, 25.7 us)
Async XLA Ops:
  0.6 59.3 %copy-start.11 = (f32[256]{0:T(256)S(1)}, f32[256]{0:T(256)}, u32[]{:S(2)}) copy-start(f32[256]{0:T(256)} %param.9) | copy-start | bytes 3076
  0.6 59.2 %collective-permute-start.10 = (bf16[1024,1024]{1,0:T(8,128)(2,1)}, bf16[1024,1024]{1,0:T(8,128)(2,1)}, u32[]{:S(2)}, u32[]{:S(2)}) collective-permute-start(bf16[1024,1024]{1,0:T(8,128)(2,1)} %bitcast.20), channel_id=1, source_target_pairs={{0,1},{1,0},{2,3},{3,2},{4,5},{5,4},{6,7},{7,6},{8,9},{9,8},{10,11... | collective-permute-start | bytes 6291464 | tf_op jit(solution)/shard_map/ppermute | solution.py:237
  1.2 58.7 %collective-permute-start.11 = (bf16[1024,1024]{1,0:T(8,128)(2,1)}, bf16[1024,1024]{1,0:T(8,128)(2,1)}, u32[]{:S(2)}, u32[]{:S(2)}) collective-permute-start(bf16[1024,1024]{1,0:T(8,128)(2,1)} %bitcast.25), channel_id=1, source_target_pairs={{0,1},{1,0},{2,3},{3,2},{4,5},{5,4},{6,7},{7,6},{8,9},{9,8},{10,11... | collective-permute-start | bytes 6291464 | tf_op jit(solution)/shard_map/ppermute | solution.py:237
  5.1 54.8 %copy-start.3 = (bf16[256,2048]{1,0:T(8,128)(2,1)S(1)}, bf16[256,2048]{1,0:T(8,128)(2,1)}, u32[]{:S(2)}) copy-start(bf16[256,2048]{1,0:T(8,128)(2,1)} %refs_2_.1) | copy-start | bytes 3145732
  5.2 54.8 %copy-start.5 = (bf16[256,2048]{1,0:T(8,128)(2,1)S(1)}, bf16[256,2048]{1,0:T(8,128)(2,1)}, u32[]{:S(2)}) copy-start(bf16[256,2048]{1,0:T(8,128)(2,1)} %refs_3_.1) | copy-start | bytes 3145732
  6.1 12.2 %collective-permute-start = (bf16[128,1024]{1,0:T(8,128)(2,1)S(1)}, bf16[128,1024]{1,0:T(8,128)(2,1)S(1)}, u32[]{:S(2)}, u32[]{:S(2)}) collective-permute-start(bf16[128,1024]{1,0:T(8,128)(2,1)S(1)} %get-tuple-element.22), channel_id=1, source_target_pairs={{0,2},{2,4},{4,6},{6,0},{1,3},{3,5},{5,7},{7,1},{8,10},{10,12},{12... | collective-permute-start | bytes 786440 | tf_op jit(solution)/shard_map/ppermute | solution.py:243
  9.1 13.6 %collective-permute-start.5 = (bf16[128,1024]{1,0:T(8,128)(2,1)S(1)}, bf16[128,1024]{1,0:T(8,128)(2,1)S(1)}, u32[]{:S(2)}, u32[]{:S(2)}) collective-permute-start(bf16[128,1024]{1,0:T(8,128)(2,1)S(1)} %get-tuple-element.23), channel_id=1, source_target_pairs={{0,6},{2,0},{4,2},{6,4},{1,7},{3,1},{5,3},{7,5},{8,14},{10,8},{12,... | collective-permute-start | bytes 786440 | tf_op jit(solution)/shard_map/ppermute | solution.py:243
  11.2 23.3 %collective-permute-start.17 = (bf16[128,1024]{1,0:T(8,128)(2,1)S(1)}, bf16[128,1024]{1,0:T(8,128)(2,1)S(1)}, u32[]{:S(2)}, u32[]{:S(2)}) collective-permute-start(bf16[128,1024]{1,0:T(8,128)(2,1)S(1)} %get-tuple-element.28), channel_id=1, source_target_pairs={{0,4},{2,6},{4,0},{6,2},{1,5},{3,7},{5,1},{7,3},{8,12},{10,14},{12... | collective-permute-start | bytes 786440 | tf_op jit(solution)/shard_map/ppermute | solution.py:243
  18.3 17.8 %collective-permute-start.2 = (bf16[128,1024]{1,0:T(8,128)(2,1)S(1)}, bf16[128,1024]{1,0:T(8,128)(2,1)S(1)}, u32[]{:S(2)}, u32[]{:S(2)}) collective-permute-start(bf16[128,1024]{1,0:T(8,128)(2,1)S(1)} %collective-permute-done.refs_4_), channel_id=1, source_target_pairs={{0,16},{8,24},{16,0},{24,8},{1,17},{9,25},{17,1},{25,9},{2,18},{10... | collective-permute-start | bytes 786440 | tf_op jit(solution)/shard_map/ppermute | solution.py:240
  22.8 15.5 %collective-permute-start.1 = (bf16[128,1024]{1,0:T(8,128)(2,1)S(1)}, bf16[128,1024]{1,0:T(8,128)(2,1)S(1)}, u32[]{:S(2)}, u32[]{:S(2)}) collective-permute-start(bf16[128,1024]{1,0:T(8,128)(2,1)S(1)} %collective-permute-done.refs_4_), channel_id=1, source_target_pairs={{0,8},{8,0},{16,24},{24,16},{1,9},{9,1},{17,25},{25,17},{2,10},{10... | collective-permute-start | bytes 786440 | tf_op jit(solution)/shard_map/ppermute | solution.py:240
  34.6 9.2 %collective-permute-start.7 = (bf16[128,1024]{1,0:T(8,128)(2,1)S(1)}, bf16[128,1024]{1,0:T(8,128)(2,1)S(1)}, u32[]{:S(2)}, u32[]{:S(2)}) collective-permute-start(bf16[128,1024]{1,0:T(8,128)(2,1)S(1)} %collective-permute-done.5.refs_9_), channel_id=1, source_target_pairs={{0,16},{8,24},{16,0},{24,8},{1,17},{9,25},{17,1},{25,9},{2,18},{10... | collective-permute-start | bytes 786440 | tf_op jit(solution)/shard_map/ppermute | solution.py:240
  36.1 9.2 %collective-permute-start.6 = (bf16[128,1024]{1,0:T(8,128)(2,1)S(1)}, bf16[128,1024]{1,0:T(8,128)(2,1)S(1)}, u32[]{:S(2)}, u32[]{:S(2)}) collective-permute-start(bf16[128,1024]{1,0:T(8,128)(2,1)S(1)} %collective-permute-done.5.refs_9_), channel_id=1, source_target_pairs={{0,8},{8,0},{16,24},{24,16},{1,9},{9,1},{17,25},{25,17},{2,10},{10... | collective-permute-start | bytes 786440 | tf_op jit(solution)/shard_map/ppermute | solution.py:240
  38.3 10.1 %collective-permute-start.19 = (bf16[128,1024]{1,0:T(8,128)(2,1)S(1)}, bf16[128,1024]{1,0:T(8,128)(2,1)S(1)}, u32[]{:S(2)}, u32[]{:S(2)}) collective-permute-start(bf16[128,1024]{1,0:T(8,128)(2,1)S(1)} %collective-permute-done.17.refs_0_), channel_id=1, source_target_pairs={{0,16},{8,24},{16,0},{24,8},{1,17},{9,25},{17,1},{25,9},{2,18},{10... | collective-permute-start | bytes 786440 | tf_op jit(solution)/shard_map/ppermute | solution.py:240
  43.7 7.8 %collective-permute-start.18 = (bf16[128,1024]{1,0:T(8,128)(2,1)S(1)}, bf16[128,1024]{1,0:T(8,128)(2,1)S(1)}, u32[]{:S(2)}, u32[]{:S(2)}) collective-permute-start(bf16[128,1024]{1,0:T(8,128)(2,1)S(1)} %collective-permute-done.17.refs_0_), channel_id=1, source_target_pairs={{0,8},{8,0},{16,24},{24,16},{1,9},{9,1},{17,25},{25,17},{2,10},{10... | collective-permute-start | bytes 786440 | tf_op jit(solution)/shard_map/ppermute | solution.py:240
  45.3 9.0 %collective-permute-start.3 = (bf16[128,512]{1,0:T(8,128)(2,1)S(1)}, bf16[128,512]{1,0:T(8,128)(2,1)S(1)}, u32[]{:S(2)}, u32[]{:S(2)}) collective-permute-start(bf16[128,512]{1,0:T(8,128)(2,1)S(1)} %slice.88), channel_id=1, source_target_pairs={{0,8},{8,0},{16,24},{24,16},{1,9},{9,1},{17,25},{25,17},{2,10},{10... | collective-permute-start | bytes 393224 | tf_op jit(solution)/shard_map/ppermute | solution.py:240
  48.4 7.6 %collective-permute-start.4 = (bf16[128,512]{1,0:T(8,128)(2,1)}, bf16[128,512]{1,0:T(8,128)(2,1)}, u32[]{:S(2)}, u32[]{:S(2)}) collective-permute-start(bf16[128,512]{1,0:T(8,128)(2,1)} %slice.89), channel_id=1, source_target_pairs={{0,16},{8,24},{16,0},{24,8},{1,17},{9,25},{17,1},{25,9},{2,18},{10... | collective-permute-start | bytes 393224 | tf_op jit(solution)/shard_map/ppermute | solution.py:240
  51.6 6.0 %collective-permute-start.8 = (bf16[128,512]{1,0:T(8,128)(2,1)}, bf16[128,512]{1,0:T(8,128)(2,1)}, u32[]{:S(2)}, u32[]{:S(2)}) collective-permute-start(bf16[128,512]{1,0:T(8,128)(2,1)} %slice.90), channel_id=1, source_target_pairs={{0,8},{8,0},{16,24},{24,16},{1,9},{9,1},{17,25},{25,17},{2,10},{10... | collective-permute-start | bytes 393224 | tf_op jit(solution)/shard_map/ppermute | solution.py:240
  54.3 5.6 %collective-permute-start.9 = (bf16[128,512]{1,0:T(8,128)(2,1)}, bf16[128,512]{1,0:T(8,128)(2,1)}, u32[]{:S(2)}, u32[]{:S(2)}) collective-permute-start(bf16[128,512]{1,0:T(8,128)(2,1)} %slice.91), channel_id=1, source_target_pairs={{0,16},{8,24},{16,0},{24,8},{1,17},{9,25},{17,1},{25,9},{2,18},{10... | collective-permute-start | bytes 393224 | tf_op jit(solution)/shard_map/ppermute | solution.py:240
  56.0 20.1 %copy-start = (bf16[1,1024,1024]{2,1,0:T(8,128)(2,1)S(1)}, bf16[1,1024,1024]{2,1,0:T(8,128)(2,1)}, u32[]{:S(2)}) copy-start(bf16[1,1024,1024]{2,1,0:T(8,128)(2,1)} %param.12) | copy-start | bytes 6291460
  56.0 20.0 %collective-permute-start.20 = (bf16[128,512]{1,0:T(8,128)(2,1)S(1)}, bf16[128,512]{1,0:T(8,128)(2,1)S(1)}, u32[]{:S(2)}, u32[]{:S(2)}) collective-permute-start(bf16[128,512]{1,0:T(8,128)(2,1)S(1)} %slice.101), channel_id=1, source_target_pairs={{0,8},{8,0},{16,24},{24,16},{1,9},{9,1},{17,25},{25,17},{2,10},{10... | collective-permute-start | bytes 393224 | tf_op jit(solution)/shard_map/ppermute | solution.py:240
  57.6 18.5 %collective-permute-start.21 = (bf16[128,512]{1,0:T(8,128)(2,1)S(1)}, bf16[128,512]{1,0:T(8,128)(2,1)S(1)}, u32[]{:S(2)}, u32[]{:S(2)}) collective-permute-start(bf16[128,512]{1,0:T(8,128)(2,1)S(1)} %slice.102), channel_id=1, source_target_pairs={{0,16},{8,24},{16,0},{24,8},{1,17},{9,25},{17,1},{25,9},{2,18},{10... | collective-permute-start | bytes 393224 | tf_op jit(solution)/shard_map/ppermute | solution.py:240
  87.0 37.6 %collective-permute-start.27 = (bf16[1024,1024]{1,0:T(8,128)(2,1)S(1)}, bf16[1024,1024]{1,0:T(8,128)(2,1)S(1)}, u32[]{:S(2)}, u32[]{:S(2)}) collective-permute-start(bf16[1024,1024]{1,0:T(8,128)(2,1)S(1)} %convolution_convert_fusion), channel_id=1, source_target_pairs={{0,1},{1,0},{2,3},{3,2},{4,5},{5,4},{6,7},{7,6},{8,9},{9,8},{10,11... | collective-permute-start | bytes 6291464 | tf_op jit(solution)/shard_map/ppermute | solution.py:237
  88.4 38.5 %collective-permute-start.26 = (bf16[1024,1024]{1,0:T(8,128)(2,1)S(1)}, bf16[1024,1024]{1,0:T(8,128)(2,1)S(1)}, u32[]{:S(2)}, u32[]{:S(2)}) collective-permute-start(bf16[1024,1024]{1,0:T(8,128)(2,1)S(1)} %convolution_convert_fusion.1), channel_id=1, source_target_pairs={{0,1},{1,0},{2,3},{3,2},{4,5},{5,4},{6,7},{7,6},{8,9},{9,8},{10,11... | collective-permute-start | bytes 6291464 | tf_op jit(solution)/shard_map/ppermute | solution.py:237
  89.0 5.8 %collective-permute-start.22 = (bf16[128,512]{1,0:T(8,128)(2,1)S(1)}, bf16[128,512]{1,0:T(8,128)(2,1)S(1)}, u32[]{:S(2)}, u32[]{:S(2)}) collective-permute-start(bf16[128,512]{1,0:T(8,128)(2,1)S(1)} %get-tuple-element.34), channel_id=1, source_target_pairs={{0,8},{8,0},{16,24},{24,16},{1,9},{9,1},{17,25},{25,17},{2,10},{10... | collective-permute-start | bytes 393224 | tf_op jit(solution)/shard_map/ppermute | solution.py:240
  90.5 7.6 %collective-permute-start.23 = (bf16[128,512]{1,0:T(8,128)(2,1)S(1)}, bf16[128,512]{1,0:T(8,128)(2,1)S(1)}, u32[]{:S(2)}, u32[]{:S(2)}) collective-permute-start(bf16[128,512]{1,0:T(8,128)(2,1)S(1)} %get-tuple-element.35), channel_id=1, source_target_pairs={{0,16},{8,24},{16,0},{24,8},{1,17},{9,25},{17,1},{25,9},{2,18},{10... | collective-permute-start | bytes 393224 | tf_op jit(solution)/shard_map/ppermute | solution.py:240
  91.8 8.4 %collective-permute-start.24 = (bf16[128,512]{1,0:T(8,128)(2,1)S(1)}, bf16[128,512]{1,0:T(8,128)(2,1)S(1)}, u32[]{:S(2)}, u32[]{:S(2)}) collective-permute-start(bf16[128,512]{1,0:T(8,128)(2,1)S(1)} %get-tuple-element.36), channel_id=1, source_target_pairs={{0,24},{8,16},{16,8},{24,0},{1,25},{9,17},{17,9},{25,1},{2,26},{10... | collective-permute-start | bytes 393224 | tf_op jit(solution)/shard_map/ppermute | solution.py:240
  94.8 12.1 %collective-permute-start.12 = (bf16[384,512]{1,0:T(8,128)(2,1)S(1)}, bf16[384,512]{1,0:T(8,128)(2,1)S(1)}, u32[]{:S(2)}, u32[]{:S(2)}) collective-permute-start(bf16[384,512]{1,0:T(8,128)(2,1)S(1)} %get-tuple-element.25), channel_id=1, source_target_pairs={{0,8},{8,0},{16,24},{24,16},{1,9},{9,1},{17,25},{25,17},{2,10},{10... | collective-permute-start | bytes 1179656 | tf_op jit(solution)/shard_map/ppermute | solution.py:240
  98.1 17.2 %collective-permute-start.13 = (bf16[384,512]{1,0:T(8,128)(2,1)S(1)}, bf16[384,512]{1,0:T(8,128)(2,1)S(1)}, u32[]{:S(2)}, u32[]{:S(2)}) collective-permute-start(bf16[384,512]{1,0:T(8,128)(2,1)S(1)} %get-tuple-element.26), channel_id=1, source_target_pairs={{0,16},{8,24},{16,0},{24,8},{1,17},{9,25},{17,1},{25,9},{2,18},{10... | collective-permute-start | bytes 1179656 | tf_op jit(solution)/shard_map/ppermute | solution.py:240
  100.2 15.2 %collective-permute-start.14 = (bf16[384,512]{1,0:T(8,128)(2,1)S(1)}, bf16[384,512]{1,0:T(8,128)(2,1)S(1)}, u32[]{:S(2)}, u32[]{:S(2)}) collective-permute-start(bf16[384,512]{1,0:T(8,128)(2,1)S(1)} %get-tuple-element.27), channel_id=1, source_target_pairs={{0,24},{8,16},{16,8},{24,0},{1,25},{9,17},{17,9},{25,1},{2,26},{10... | collective-permute-start | bytes 1179656 | tf_op jit(solution)/shard_map/ppermute | solution.py:240
  106.9 13.9 %collective-permute-start.25 = (bf16[128,512]{1,0:T(8,128)(2,1)S(1)}, bf16[128,512]{1,0:T(8,128)(2,1)S(1)}, u32[]{:S(2)}, u32[]{:S(2)}) collective-permute-start(bf16[128,512]{1,0:T(8,128)(2,1)S(1)} %add_convert_fusion.2), channel_id=1, source_target_pairs={{0,4},{2,6},{4,0},{6,2},{1,5},{3,7},{5,1},{7,3},{8,12},{10,14},{12... | collective-permute-start | bytes 393224 | tf_op jit(solution)/shard_map/ppermute | solution.py:243
  115.6 7.3 %collective-permute-start.16 = (bf16[128,512]{1,0:T(8,128)(2,1)S(1)}, bf16[128,512]{1,0:T(8,128)(2,1)S(1)}, u32[]{:S(2)}, u32[]{:S(2)}) collective-permute-start(bf16[128,512]{1,0:T(8,128)(2,1)S(1)} %get-tuple-element.41), channel_id=1, source_target_pairs={{0,2},{2,4},{4,6},{6,0},{1,3},{3,5},{5,7},{7,1},{8,10},{10,12},{12... | collective-permute-start | bytes 393224 | tf_op jit(solution)/shard_map/ppermute | solution.py:243
  115.7 7.3 %collective-permute-start.15 = (bf16[128,512]{1,0:T(8,128)(2,1)S(1)}, bf16[128,512]{1,0:T(8,128)(2,1)S(1)}, u32[]{:S(2)}, u32[]{:S(2)}) collective-permute-start(bf16[128,512]{1,0:T(8,128)(2,1)S(1)} %get-tuple-element.42), channel_id=1, source_target_pairs={{0,6},{2,0},{4,2},{6,4},{1,7},{3,1},{5,3},{7,5},{8,14},{10,8},{12,... | collective-permute-start | bytes 393224 | tf_op jit(solution)/shard_map/ppermute | solution.py:243
  (12 other events, 25.6 us)

commit v3 on v2

v3 whole, which is shorter than its diff:
```python
import functools

import jax
import jax.numpy as jnp
from jax import lax
from jax.experimental import pallas as pl
from jax.experimental.pallas import tpu as pltpu
from jax.sharding import PartitionSpec as P

F32 = jnp.float32
BF16 = jnp.bfloat16
I32 = jnp.int32
ANY = pl.BlockSpec(memory_space=pl.ANY)
VMEM = pl.BlockSpec(memory_space=pltpu.VMEM)
SMEM = pl.BlockSpec(memory_space=pltpu.SMEM)
HBM = pl.BlockSpec(memory_space=pltpu.HBM)
LIMIT = 22 * 2**20


def dot(lhs, rhs, left=1, right=0):
    return lax.dot_general(lhs, rhs, (((left,), (right,)), ((), ())), preferred_element_type=F32)


def hits(position, first, rows):
    ids = lax.broadcasted_iota(I32, (rows, position.shape[1]), 0) + first
    return ids == position


def gate_of(hit, gate):
    return jnp.sum(jnp.where(hit, gate, 0.0), axis=1, keepdims=True)


def place_kernel(spans, where, position, gate, tokens, grad_output, *refs):
    outs, (tok, grad, sem) = refs[: len(spans)], refs[len(spans) :]
    share = tok.shape[1]
    columns = pl.ds(pl.multiple_of(where[len(spans)] * share, share), share)
    first = pltpu.make_async_copy(tokens.at[:, columns], tok, sem.at[0])
    second = pltpu.make_async_copy(grad_output.at[:, columns], grad, sem.at[1])
    first.start()
    second.start()
    found = [hits(position[...], where[k], rows) for k, rows in enumerate(spans)]
    first.wait()
    second.wait()
    for hit, out in zip(found, outs):
        hot = hit.astype(BF16)
        out[:, :share] = dot(hot, tok[...]).astype(BF16)
        out[:, share:] = (dot(hot, grad[...]) * gate_of(hit, gate[...])).astype(BF16)


def place(spans, firsts, quarter, position, gate, tokens, grad_output, share):
    count = tokens.shape[0]
    where = jnp.stack(list(firsts) + [quarter]).astype(I32)
    return pl.pallas_call(
        functools.partial(place_kernel, spans),
        out_shape=[jax.ShapeDtypeStruct((rows, 2 * share), BF16) for rows in spans],
        in_specs=[SMEM, VMEM, VMEM, HBM, HBM],
        out_specs=[VMEM] * len(spans),
        scratch_shapes=[
            pltpu.VMEM((count, share), BF16), pltpu.VMEM((count, share), BF16), pltpu.SemaphoreType.DMA((2,))
        ],
        compiler_params=pltpu.CompilerParams(vmem_limit_bytes=54 * 2**20),
        cost_estimate=pl.CostEstimate(
            flops=4 * sum(spans) * count * share, bytes_accessed=4 * (count + sum(spans)) * share, transcendentals=0
        ),
        name="place_rows",
    )(where, position, gate, tokens, grad_output)


def gelu_parts(pre):
    c = 0.7978845608028654
    square = pre * pre
    th = jnp.tanh(c * (pre + 0.044715 * (pre * square)))
    half = 0.5 * (1.0 + th)
    return pre * half, half + 0.5 * pre * (1.0 - th * th) * (c + (3 * 0.044715 * c) * square)


def expert_kernel(own_rows, chunk_rows, base, block_base, aliased, where, *refs):
    refs = list(refs)
    take = lambda n: [refs.pop(0) for _ in range(n)]
    if own_rows:
        position, gate, tokens, grad_output = take(4)
    chunks = [take(5) for _ in chunk_rows]
    up_own, up_other, down_own, down_other = take(4)
    take(aliased)
    tok_out, grad_out, hidden_out, slope_out = take(4)
    blocks = take(4)
    tok, grad, hidden, slope, back = take(5)
    if own_rows:
        tokens_in, grad_in = take(2)
    (sem,) = take(1)
    rows, width = tok.shape
    half, share = width // 2, width // 4
    order, first, half_start = where[0], where[1], where[2]
    count = [0]

    def copy(src, dst):
        c = pltpu.make_async_copy(src, dst, sem.at[count[0]])
        count[0] += 1
        c.start()
        return c

    if own_rows:
        waits = []
        other_start = half - half_start
        for src, dst in ((tokens, tokens_in), (grad_output, grad_in)):
            for start, place_at in ((half_start, 0), (other_start, half)):
                start = pl.multiple_of(start, half)
                waits.append(copy(src.at[:, pl.ds(start, half)], dst.at[:, pl.ds(place_at, half)]))
        hit = hits(position[...], first, own_rows)
        hot = hit.astype(BF16)
        for w in waits:
            w.wait()
        tok[:own_rows, :] = dot(hot, tokens_in[...]).astype(BF16)
        grad[:own_rows, :] = (dot(hot, grad_in[...]) * gate_of(hit, gate[...])).astype(BF16)
    at = own_rows
    for (z, x, y, tok_d, grad_d), n in zip(chunks, chunk_rows):
        for j in range(4):
            columns = pl.ds(pl.multiple_of((order ^ j) * share, share), share)
            tok[at : at + n, columns] = (z, x, y)[j][:, :share] if j < 3 else tok_d[...]
            grad[at : at + n, columns] = (z, x, y)[j][:, share:] if j < 3 else grad_d[...]
        at += n
    outs = [copy(tok, tok_out.at[pl.ds(base, rows), :]), copy(grad, grad_out.at[pl.ds(base, rows), :])]
    hid = hidden.shape[1]
    step = 256
    for n in range(0, hid, step):
        cols = slice(n, n + step)
        pre = dot(tok[:, :half], up_own[:, cols]) + dot(tok[:, half:], up_other[:, cols])
        hidden_grad = dot(grad[:, :half], down_own[:, cols]) + dot(grad[:, half:], down_other[:, cols])
        act, deriv = gelu_parts(pre)
        hidden[:, cols] = act.astype(BF16)
        slope[:, cols] = (hidden_grad * deriv).astype(BF16)
    outs.append(copy(hidden, hidden_out.at[pl.ds(base, rows), :]))
    outs.append(copy(slope, slope_out.at[pl.ds(base, rows), :]))
    for n in range(4):
        source = (up_own, up_other)[n // 2]
        lo = (n % 2) * share
        back[n] = dot(slope[...], source[lo : lo + share, :], 1, 1).astype(BF16)
    for j in range(4):
        outs.append(copy(back.at[order ^ j], blocks[j].at[pl.ds(block_base, rows), :]))
    for w in outs:
        w.wait()


def expert_rows(where, own, chunks, weights, total_rows, base, block_rows, block_base, kept, blocks):
    own_rows = own[0] if own else 0
    chunk_rows = [c[0].shape[0] for c in chunks]
    rows = own_rows + sum(chunk_rows)
    half, hid = weights[0].shape
    width, share = 2 * half, half // 2
    operands = [where]
    specs = [SMEM]
    if own:
        operands += own[1:]
        specs += [VMEM, VMEM, HBM, HBM]
    for c in chunks:
        operands += c
        specs += [VMEM] * 5
    operands += weights
    specs += [VMEM] * 4
    aliases = {}
    for first, previous in ((0, kept), (4, blocks)):
        if previous:
            aliases.update({len(operands) + i: first + i for i in range(4)})
            operands += previous
            specs += [ANY] * 4
    shape = lambda *s: jax.ShapeDtypeStruct(s, BF16)
    buf = lambda *s: pltpu.VMEM(s, BF16)
    scratch = [buf(rows, width), buf(rows, width), buf(rows, hid), buf(rows, hid), buf(4, rows, share)]
    copies = 8
    if own:
        count = own[3].shape[0]
        scratch += [buf(count, width), buf(count, width)]
        copies += 4
    scratch.append(pltpu.SemaphoreType.DMA((copies,)))
    out = pl.pallas_call(
        functools.partial(expert_kernel, own_rows, chunk_rows, base, block_base, len(aliases)),
        out_shape=[shape(total_rows, width)] * 2 + [shape(total_rows, hid)] * 2 + [shape(block_rows, share)] * 4,
        in_specs=specs,
        out_specs=[ANY] * 8,
        scratch_shapes=scratch,
        input_output_aliases=aliases,
        compiler_params=pltpu.CompilerParams(vmem_limit_bytes=LIMIT + rows * 2**15),
        cost_estimate=pl.CostEstimate(
            flops=6 * rows * width * hid, bytes_accessed=4 * width * hid + 8 * rows * width, transcendentals=rows * hid
        ),
        name="expert_rows",
    )(*operands)
    return list(out[:4]), list(out[4:])


def unplace_kernel(spans, where, position, *refs):
    out = refs[-1]
    total = None
    for k, (rows, back) in enumerate(zip(spans, refs[:-1])):
        hot = hits(position[...], where[k], rows).astype(BF16)
        part = dot(hot, back[...], 0, 0)
        total = part if total is None else total + part
    out[...] = total.astype(BF16)


def unplace(firsts, position, backs):
    spans = [b.shape[0] for b in backs]
    count, share = position.shape[1], backs[0].shape[1]
    return pl.pallas_call(
        functools.partial(unplace_kernel, spans),
        out_shape=jax.ShapeDtypeStruct((count, share), BF16),
        in_specs=[SMEM] + [VMEM] * (1 + len(backs)),
        out_specs=VMEM,
        compiler_params=pltpu.CompilerParams(vmem_limit_bytes=LIMIT),
        cost_estimate=pl.CostEstimate(
            flops=2 * sum(spans) * count * share, bytes_accessed=2 * (count + sum(spans)) * share, transcendentals=0
        ),
        name="unplace_rows",
    )(jnp.stack(firsts).astype(I32), position, *backs)


def outer_kernel(rows, out, *refs):
    total = dot(rows[...], out[...], 0, 0).astype(BF16)
    if len(refs) > 1:
        total = (total.astype(F32) + refs[0][...].astype(F32)).astype(BF16)
    refs[-1][...] = total


def outer(rows, out, which, got):
    count, width = rows.shape
    hid = out.shape[1]
    half, block = width // 2, width // 8
    steps = half // block
    tile = pl.BlockSpec((block, hid), lambda i: (i, 0))
    operands = [rows, out] + ([] if got is None else [got])
    return pl.pallas_call(
        outer_kernel,
        out_shape=jax.ShapeDtypeStruct((half, hid), BF16),
        grid=(steps,),
        in_specs=[
            pl.BlockSpec((count, block), lambda i: (0, which * steps + i)),
            pl.BlockSpec((count, hid), lambda i: (0, 0)),
        ]
        + [tile] * (len(operands) - 2),
        out_specs=tile,
        compiler_params=pltpu.CompilerParams(vmem_limit_bytes=LIMIT),
        cost_estimate=pl.CostEstimate(
            flops=2 * count * half * hid, bytes_accessed=2 * (count * (half + hid) + half * hid), transcendentals=0
        ),
        name="weight_grad",
    )(*operands)


def local(tokens, grad_output, gate_prob, expert_index, slot_index, up_weight, down_weight):
    experts = lax.axis_size("expert")
    tensor_size = lax.axis_size("tensor")
    e = lax.axis_index("expert")
    t = lax.axis_index("tensor")
    p = lax.axis_index("dp")
    tok_count, width = tokens.shape
    capacity = 2 * tok_count // experts
    share = width // tensor_size
    half = width // 2
    where = jnp.stack([t ^ (2 * p), e * capacity, p * half]).astype(I32)

    def swap(x):
        return lax.ppermute(x, "dp", [(0, 1), (1, 0)])

    def across(x, j):
        return lax.ppermute(x, "tensor", [(i, i ^ j) for i in range(tensor_size)])

    def shift(x, k):
        return lax.ppermute(x, "expert", [(i, (i + k) % experts) for i in range(experts)])

    def after(x, *others):
        return lax.optimization_barrier((x,) + others)[0]

    def spread(rows, *before):
        x, y = across(rows, 1), across(rows, 2)
        if before:
            x, y = after(x, *before), after(y, *before)
        return [rows, x, y, across(y[:, :share], 1), across(x[:, share:], 2)]

    def collect(blocks):
        got = [across(blocks[j], j) for j in (1, 2, 3)]

        def total(lo, hi):
            terms = [b[lo:hi].astype(F32) for b in [blocks[0]] + got]
            return (terms[0] + terms[1] + (terms[2] + terms[3])).astype(BF16)

        return total, got

    position = (expert_index * capacity + slot_index).reshape(1, tok_count)
    gate = gate_prob.reshape(1, tok_count)
    up_own, down_own = up_weight[0], down_weight[0]

    weights = [up_own, swap(up_own), down_own, swap(down_own)]

    if experts == 4:
        shifts = (1, 3, 2)
        firsts = [((e + k) % experts) * capacity for k in shifts]
        sends = place([capacity] * 3, firsts, t, position, gate, tokens, grad_output, share)
        one, three = shift(sends[0], 1), shift(sends[1], 3)
        own = [capacity, position, gate, tokens, grad_output]
        kept, blocks = expert_rows(where, own, [], weights, 4 * capacity, 0, capacity, 0, None, None)
        two = shift(after(sends[2], blocks[0]), 2)
        backs = [collect(blocks)[0](0, capacity)]
        near = spread(jnp.concatenate([after(one, blocks[0]), three], 0), backs[0])
        far = spread(two)
        kept, blocks = expert_rows(
            where, None, [near], weights, 4 * capacity, capacity, 2 * capacity, 0, kept, None
        )
        total, got = collect(blocks)
        backs += [shift(total(i * capacity, (i + 1) * capacity), -k) for i, k in ((0, 1), (1, 3))]
        kept, blocks = expert_rows(where, None, [far], weights, 4 * capacity, 3 * capacity, capacity, 0, kept, None)
        last, got_last = collect(blocks)
        got += got_last
        backs.append(shift(last(0, capacity), -2))
        places = [e * capacity] + firsts
    else:
        rows = experts * capacity

        def exchange(x):
            moved = lax.all_to_all(
                x.reshape(experts, capacity, x.shape[1]), "expert", split_axis=0, concat_axis=0, tiled=True
            )
            return moved.reshape(rows, x.shape[1])

        (send,) = place([rows], [jnp.int32(0)], t, position, gate, tokens, grad_output, share)
        kept, blocks = expert_rows(where, None, [spread(exchange(send))], weights, rows, 0, rows, 0, None, None)
        total, got = collect(blocks)
        backs = [exchange(total(0, rows))]
        places = [jnp.int32(0)]

    grad_tokens = unplace(places, position, backs)
    tok_rows, grad_rows, hidden, slope = kept

    hidden, slope = after(hidden, *got), after(slope, *got)
    got_up = swap(outer(tok_rows, slope, 1, None))
    got_down = swap(outer(grad_rows, hidden, 1, None))
    return grad_tokens, outer(tok_rows, slope, 0, got_up)[None], outer(grad_rows, hidden, 0, got_down)[None]


def solution(mesh):
    placed = (
        P(("expert", "dp"), None),
        P(("expert", "dp"), None),
        P(("expert", "dp")),
        P(("expert", "dp"), None),
        P(("expert", "dp"), None),
        P("expert", "dp", "tensor"),
        P("expert", "dp", "tensor"),
    )
    return jax.shard_map(
        local,
        mesh=mesh,
        in_specs=placed,
        out_specs=(
            P(("expert", "dp"), "tensor"),
            P("expert", "dp", "tensor"),
            P("expert", "dp", "tensor"),
        ),
        check_vma=False,
    )
```

time: 130 us -> 123 us (0.946)
  Pallas kernels: 23 us -> 35.5 us
  local copies, waits for them, and re-layouts: 11.9 us -> 4.15 us
  starting transfers between devices: 36 us -> 30 us
  matrix products: 5.19 us -> 0 us
  other arithmetic: 5.84 us -> 2.26 us
  waiting for transfers between devices: 46.4 us -> 49.5 us
    pallas_call x0 -> x4, Pallas kernels: none -> 10.4 us  [outer(): pl.pallas_call(outer_kernel, out_shape=jax.ShapeDtypeStruct((half, hid),...]
    ppermute x18 -> x17, starting transfers between devices: 24.8 us -> 18 us  [across(): return lax.ppermute(x, 'tensor', [(i, i ^ j) for i in range(tensor_size)])]
    unnamed x32 -> x17, local copies, waits for them, and re-layouts: 9.94 us -> 4.08 us
    dot_general x4 -> x0, matrix products: 5.19 us -> none  [dot(): lax.dot_general(lhs, rhs, (((left,), (right,)), ((), ())), preferred_elem...]
    ppermute x18 -> x17, waiting for transfers between devices: 25.9 us -> 30.6 us  [across(): return lax.ppermute(x, 'tensor', [(i, i ^ j) for i in range(tensor_size)])]
    broadcast_in_dim x2 -> x0, other arithmetic: 4.63 us -> none  [weight_grad(): return (mine.astype(F32) + got.astype(F32)).astype(BF16)[None]]
    pallas_call x1, Pallas kernels: 0.92 us -> 2.92 us  [place(): pl.pallas_call(functools.partial(place_kernel, spans), out_shape=[jax.Sha...]
    slice x6 -> x4, local copies, waits for them, and re-layouts: 2.01 us -> 0.05 us  [spread(): return [rows, x, y, across(y[:, :share], 1), across(x[:, share:], 2)]]
  transfers between devices with their start and end apart: 28 -> 27, of which waited for: 13 -> 11; matrix products, arithmetic and copies ran while one was open for 7% -> 2% of each run, Pallas kernels for 12% -> 19%
where the time goes in v3:
time: 123 us; the launch traced here: 122 us
  waiting for transfers between devices  49.5 us (40%)
  Pallas kernels  35.5 us (29%)
  starting transfers between devices  30 us (24%)
  local copies, waits for them, and re-layouts  4.15 us (3%)
  other arithmetic  2.26 us (2%)
    ppermute x17, waiting for transfers between devices, across(): return lax.ppermute(x, 'tensor', [(i, i ^ j) for i in range(tensor_size)])  30.6 us
    pallas_call x3, Pallas kernels, expert_rows(): pl.pallas_call(functools.partial(expert_kernel, own_rows, chunk_rows, bas...  20.5 us
    ppermute x6, waiting for transfers between devices, shift(): lax.ppermute(x, 'expert', [(i, (i + k) % experts) for i in range(experts)])  18.8 us
    ppermute x17, starting transfers between devices, across(): return lax.ppermute(x, 'tensor', [(i, i ^ j) for i in range(tensor_size)])  18 us
    ppermute x6, starting transfers between devices, shift(): lax.ppermute(x, 'expert', [(i, (i + k) % experts) for i in range(experts)])  10.8 us
    pallas_call x4, Pallas kernels, outer(): pl.pallas_call(outer_kernel, out_shape=jax.ShapeDtypeStruct((half, hid),...  10.4 us
    unnamed x17, local copies, waits for them, and re-layouts  4.08 us
    pallas_call x1, Pallas kernels, place(): pl.pallas_call(functools.partial(place_kernel, spans), out_shape=[jax.Sha...  2.92 us
  transfers between devices with their start and end apart: 27, of which 11 were waited for; matrix products, arithmetic and copies ran while one was open for 2% of the time, Pallas kernels for 19%

profile of v3, /device:TPU:0, one launch (start us, length us, event | category | flops | bytes accessed | tf_op | source)
XLA Modules:
  0.0 122.3 jit_solution(17895339060109267305)
XLA Ops:
  1.8 1.3 %add_bitcast_fusion.refs_0_.position = s32[1,256]{1,0:T(1,128)} fusion(s32[256,1]{0,1:T(1,128)} %param.11, s32[256,1]{0,1:T(1,128)} %param.10), kind=kLoop, calls=%fused_computation.6 | loop fusion | flops 512 | bytes 3072 | tf_op jit(solution)/shard_map/reshape | solution.py:288
  3.1 2.9 %place_rows.1 = (bf16[128,1024]{1,0:T(8,128)(2,1)}, bf16[128,1024]{1,0:T(8,128)(2,1)}, bf16[128,1024]{1,0:T(8,128)(2,1)}) custom-call(s32[4]{0:T(128)} %pad_add_fusion.2.where, s32[1,256]{1,0:T(1,128)} %add_bitcast_fusion.refs_0_.position, f32[1,256]{1,0:T(1,128)} %bitcast.22, bf16[256,2048]{1,0:T(8,128)(2,1)} %tokens.1, bf16[256,2048]{1,0:T(8,128)(2,1)} %grad_output.1), custom_call_target="tpu_custom_call" | custom-call | flops 201326592 | bytes 1310720 | tf_op jit(solution)/shard_map/place_rows/pallas_call | solution.py:53
  6.0 3.1 %collective-permute-start.5 = (bf16[128,1024]{1,0:T(8,128)(2,1)}, bf16[128,1024]{1,0:T(8,128)(2,1)S(1)}, u32[]{:S(2)}, u32[]{:S(2)}) collective-permute-start(bf16[128,1024]{1,0:T(8,128)(2,1)} %get-tuple-element.40), channel_id=1, source_target_pairs={{0,2},{2,4},{4,6},{6,0},{1,3},{3,5},{5,7},{7,1},{8,10},{10,12},{12... | collective-permute-start | bytes 786440 | tf_op jit(solution)/shard_map/ppermute | solution.py:268
  9.1 2.1 %collective-permute-start.6 = (bf16[128,1024]{1,0:T(8,128)(2,1)}, bf16[128,1024]{1,0:T(8,128)(2,1)S(1)}, u32[]{:S(2)}, u32[]{:S(2)}) collective-permute-start(bf16[128,1024]{1,0:T(8,128)(2,1)} %get-tuple-element.42), channel_id=1, source_target_pairs={{0,6},{2,0},{4,2},{6,4},{1,7},{3,1},{5,3},{7,5},{8,14},{10,8},{12,... | collective-permute-start | bytes 786440 | tf_op jit(solution)/shard_map/ppermute | solution.py:268
  11.3 1.6 %copy-done.1 = bf16[1,1024,1024]{2,1,0:T(8,128)(2,1)S(1)} copy-done((bf16[1,1024,1024]{2,1,0:T(8,128)(2,1)S(1)}, bf16[1,1024,1024]{2,1,0:T(8,128)(2,1)}, u32[]{:S(2)}) %copy-start.1) | copy-done | bytes 2097176
  12.9 1.2 %copy-done.3 = bf16[256,2048]{1,0:T(8,128)(2,1)S(1)} copy-done((bf16[256,2048]{1,0:T(8,128)(2,1)S(1)}, bf16[256,2048]{1,0:T(8,128)(2,1)}, u32[]{:S(2)}) %copy-start.3) | copy-done | bytes 1048600
  14.1 1.2 %copy-done.4 = bf16[256,2048]{1,0:T(8,128)(2,1)S(1)} copy-done((bf16[256,2048]{1,0:T(8,128)(2,1)S(1)}, bf16[256,2048]{1,0:T(8,128)(2,1)}, u32[]{:S(2)}) %copy-start.4) | copy-done | bytes 1048600
  15.3 7.1 %expert_rows.3 = (bf16[512,2048]{1,0:T(8,128)(2,1)S(1)}, bf16[512,2048]{1,0:T(8,128)(2,1)S(1)}, bf16[512,1024]{1,0:T(8,128)(2,1)S(1)}, bf16[512,1024]{1,0:T(8,12...) custom-call(s32[3]{0:T(128)S(1)} %pad_add_fusion.1.where, ...), custom_call_target="tpu_custom_call" | custom-call | flops 1610612736 | bytes 10485760 | tf_op jit(solution)/shard_map/expert_rows/pallas_call | solution.py:175
  22.9 1.6 %collective-permute-start.7 = (bf16[256,1024]{1,0:T(8,128)(2,1)S(1)}, bf16[256,1024]{1,0:T(8,128)(2,1)S(1)}, u32[]{:S(2)}, u32[]{:S(2)}) collective-permute-start(bf16[256,1024]{1,0:T(8,128)(2,1)S(1)} %constant_dynamic-update-slice_fusion.refs_0_), channel_id=1, source_target_pairs={{0,8},{8,0},{16,24},{24,16},{1,9},{9,1},{17,25},{25,17},{2,10},{10... | collective-permute-start | bytes 1572872 | tf_op jit(solution)/shard_map/ppermute | solution.py:265
  24.5 1.5 %collective-permute-start.8 = (bf16[256,1024]{1,0:T(8,128)(2,1)S(1)}, bf16[256,1024]{1,0:T(8,128)(2,1)S(1)}, u32[]{:S(2)}, u32[]{:S(2)}) collective-permute-start(bf16[256,1024]{1,0:T(8,128)(2,1)S(1)} %constant_dynamic-update-slice_fusion.refs_0_), channel_id=1, source_target_pairs={{0,16},{8,24},{16,0},{24,8},{1,17},{9,25},{17,1},{25,9},{2,18},{10... | collective-permute-start | bytes 1572872 | tf_op jit(solution)/shard_map/ppermute | solution.py:265
  26.5 1.5 %collective-permute-start.3 = (bf16[128,512]{1,0:T(8,128)(2,1)S(1)}, bf16[128,512]{1,0:T(8,128)(2,1)S(1)}, u32[]{:S(2)}, u32[]{:S(2)}) collective-permute-start(bf16[128,512]{1,0:T(8,128)(2,1)S(1)} %get-tuple-element.38), channel_id=1, source_target_pairs={{0,16},{8,24},{16,0},{24,8},{1,17},{9,25},{17,1},{25,9},{2,18},{10... | collective-permute-start | bytes 393224 | tf_op jit(solution)/shard_map/ppermute | solution.py:265
  28.0 1.5 %collective-permute-start.2 = (bf16[128,512]{1,0:T(8,128)(2,1)S(1)}, bf16[128,512]{1,0:T(8,128)(2,1)S(1)}, u32[]{:S(2)}, u32[]{:S(2)}) collective-permute-start(bf16[128,512]{1,0:T(8,128)(2,1)S(1)} %get-tuple-element.37), channel_id=1, source_target_pairs={{0,8},{8,0},{16,24},{24,16},{1,9},{9,1},{17,25},{25,17},{2,10},{10... | collective-permute-start | bytes 393224 | tf_op jit(solution)/shard_map/ppermute | solution.py:265
  29.5 12.0 %collective-permute-done.4 = bf16[128,512]{1,0:T(8,128)(2,1)S(1)} collective-permute-done((bf16[128,512]{1,0:T(8,128)(2,1)S(1)}, bf16[128,512]{1,0:T(8,128)(2,1)S(1)}, u32[]{:S(2)}, u32[]{:S(2)}) %collective-permute-start.4) | collective-permute-done | bytes 131104 | tf_op jit(solution)/shard_map/ppermute | solution.py:265
  41.5 1.3 %collective-permute-start.16 = (bf16[128,1024]{1,0:T(8,128)(2,1)S(1)}, bf16[128,1024]{1,0:T(8,128)(2,1)S(1)}, u32[]{:S(2)}, u32[]{:S(2)}) collective-permute-start(bf16[128,1024]{1,0:T(8,128)(2,1)S(1)} %copy-done.7), channel_id=1, source_target_pairs={{0,4},{2,6},{4,0},{6,2},{1,5},{3,7},{5,1},{7,3},{8,12},{10,14},{12... | collective-permute-start | bytes 786440 | tf_op jit(solution)/shard_map/ppermute | solution.py:268
  43.1 9.8 %collective-permute-done.16.refs_0_ = bf16[128,1024]{1,0:T(8,128)(2,1)S(1)} collective-permute-done((bf16[128,1024]{1,0:T(8,128)(2,1)S(1)}, bf16[128,1024]{1,0:T(8,128)(2,1)S(1)}, u32[]{:S(2)}, u32[]{:S(2)}) %collective-permute-start.16) | collective-permute-done | bytes 262176 | tf_op jit(solution)/shard_map/ppermute | solution.py:268
  52.9 1.5 %collective-permute-start.17 = (bf16[128,1024]{1,0:T(8,128)(2,1)S(1)}, bf16[128,1024]{1,0:T(8,128)(2,1)S(1)}, u32[]{:S(2)}, u32[]{:S(2)}) collective-permute-start(bf16[128,1024]{1,0:T(8,128)(2,1)S(1)} %collective-permute-done.16.refs_0_), channel_id=1, source_target_pairs={{0,8},{8,0},{16,24},{24,16},{1,9},{9,1},{17,25},{25,17},{2,10},{10... | collective-permute-start | bytes 786440 | tf_op jit(solution)/shard_map/ppermute | solution.py:265
  55.6 1.6 %collective-permute-start.10 = (bf16[256,512]{1,0:T(8,128)(2,1)S(1)}, bf16[256,512]{1,0:T(8,128)(2,1)S(1)}, u32[]{:S(2)}, u32[]{:S(2)}) collective-permute-start(bf16[256,512]{1,0:T(8,128)(2,1)S(1)} %slice.37), channel_id=1, source_target_pairs={{0,16},{8,24},{16,0},{24,8},{1,17},{9,25},{17,1},{25,9},{2,18},{10... | collective-permute-start | bytes 786440 | tf_op jit(solution)/shard_map/ppermute | solution.py:265
  57.2 6.5 %collective-permute-done.18.refs_2_ = bf16[128,1024]{1,0:T(8,128)(2,1)S(1)} collective-permute-done((bf16[128,1024]{1,0:T(8,128)(2,1)S(1)}, bf16[128,1024]{1,0:T(8,128)(2,1)S(1)}, u32[]{:S(2)}, u32[]{:S(2)}) %collective-permute-start.18) | collective-permute-done | bytes 262176 | tf_op jit(solution)/shard_map/ppermute | solution.py:265
  67.2 6.9 %expert_rows.4 = (bf16[512,2048]{1,0:T(8,128)(2,1)S(1)}, bf16[512,2048]{1,0:T(8,128)(2,1)S(1)}, bf16[512,1024]{1,0:T(8,128)(2,1)S(1)}, bf16[512,1024]{1,0:T(8,12...) custom-call(s32[3]{0:T(128)S(1)} %pad_add_fusion.1.where, ...), custom_call_target="tpu_custom_call", output_to_operand_aliasing={{0}: (10, {}), {1}: (11, {}), {2}: (12, {}), {3}: (13, {})} | custom-call | flops 3221225472 | bytes 12582912 | tf_op jit(solution)/shard_map/expert_rows/pallas_call | solution.py:175
  74.2 6.5 %expert_rows.5 = (bf16[512,2048]{1,0:T(8,128)(2,1)S(1)}, bf16[512,2048]{1,0:T(8,128)(2,1)S(1)}, bf16[512,1024]{1,0:T(8,128)(2,1)S(1)}, bf16[512,1024]{1,0:T(8,12...) custom-call(s32[3]{0:T(128)S(1)} %pad_add_fusion.1.where, ...), custom_call_target="tpu_custom_call", output_to_operand_aliasing={{0}: (10, {}), {1}: (11, {}), {2}: (12, {}), {3}: (13, {})} | custom-call | flops 1610612736 | bytes 10485760 | tf_op jit(solution)/shard_map/expert_rows/pallas_call | solution.py:175
  81.2 2.4 %collective-permute-start.13 = (bf16[256,512]{1,0:T(8,128)(2,1)S(1)}, bf16[256,512]{1,0:T(8,128)(2,1)S(1)}, u32[]{:S(2)}, u32[]{:S(2)}) collective-permute-start(bf16[256,512]{1,0:T(8,128)(2,1)S(1)} %get-tuple-element.52), channel_id=1, source_target_pairs={{0,24},{8,16},{16,8},{24,0},{1,25},{9,17},{17,9},{25,1},{2,26},{10... | collective-permute-start | bytes 786440 | tf_op jit(solution)/shard_map/ppermute | solution.py:265
  84.7 1.5 %collective-permute-start.22 = (bf16[128,512]{1,0:T(8,128)(2,1)S(1)}, bf16[128,512]{1,0:T(8,128)(2,1)S(1)}, u32[]{:S(2)}, u32[]{:S(2)}) collective-permute-start(bf16[128,512]{1,0:T(8,128)(2,1)S(1)} %get-tuple-element.61), channel_id=1, source_target_pairs={{0,16},{8,24},{16,0},{24,8},{1,17},{9,25},{17,1},{25,9},{2,18},{10... | collective-permute-start | bytes 393224 | tf_op jit(solution)/shard_map/ppermute | solution.py:265
  86.2 1.8 %collective-permute-done.23 = bf16[128,512]{1,0:T(8,128)(2,1)S(1)} collective-permute-done((bf16[128,512]{1,0:T(8,128)(2,1)S(1)}, bf16[128,512]{1,0:T(8,128)(2,1)S(1)}, u32[]{:S(2)}, u32[]{:S(2)}) %collective-permute-start.23) | collective-permute-done | bytes 131104 | tf_op jit(solution)/shard_map/ppermute | solution.py:265
  88.6 7.7 %collective-permute-done.22 = bf16[128,512]{1,0:T(8,128)(2,1)S(1)} collective-permute-done((bf16[128,512]{1,0:T(8,128)(2,1)S(1)}, bf16[128,512]{1,0:T(8,128)(2,1)S(1)}, u32[]{:S(2)}, u32[]{:S(2)}) %collective-permute-start.22) | collective-permute-done | bytes 131104 | tf_op jit(solution)/shard_map/ppermute | solution.py:265
  96.3 2.1 %weight_grad.4 = bf16[1024,1024]{1,0:T(8,128)(2,1)S(1)} custom-call(bf16[512,2048]{1,0:T(8,128)(2,1)S(1)} %get-tuple-element.63.rows, bf16[512,1024]{1,0:T(8,128)(2,1)S(1)} %get-tuple-element.65.out), custom_call_target="tpu_custom_call" | custom-call | flops 1073741824 | bytes 4194304 | tf_op jit(solution)/shard_map/weight_grad/pallas_call | solution.py:231
  98.5 2.1 %weight_grad.6 = bf16[1024,1024]{1,0:T(8,128)(2,1)S(1)} custom-call(bf16[512,2048]{1,0:T(8,128)(2,1)S(1)} %get-tuple-element.66.rows, bf16[512,1024]{1,0:T(8,128)(2,1)S(1)} %get-tuple-element.68.out), custom_call_target="tpu_custom_call" | custom-call | flops 1073741824 | bytes 4194304 | tf_op jit(solution)/shard_map/weight_grad/pallas_call | solution.py:231
  101.4 3.6 %collective-permute-start.14 = (bf16[128,512]{1,0:T(8,128)(2,1)S(1)}, bf16[128,512]{1,0:T(8,128)(2,1)S(1)}, u32[]{:S(2)}, u32[]{:S(2)}) collective-permute-start(bf16[128,512]{1,0:T(8,128)(2,1)S(1)} %get-tuple-element.70), channel_id=1, source_target_pairs={{0,6},{2,0},{4,2},{6,4},{1,7},{3,1},{5,3},{7,5},{8,14},{10,8},{12,... | collective-permute-start | bytes 393224 | tf_op jit(solution)/shard_map/ppermute | solution.py:268
  105.7 6.1 %collective-permute-done.24.refs_3_ = bf16[128,512]{1,0:T(8,128)(2,1)S(1)} collective-permute-done((bf16[128,512]{1,0:T(8,128)(2,1)S(1)}, bf16[128,512]{1,0:T(8,128)(2,1)S(1)}, u32[]{:S(2)}, u32[]{:S(2)}) %collective-permute-start.24) | collective-permute-done | bytes 131104 | tf_op jit(solution)/shard_map/ppermute | solution.py:268
  111.8 2.4 %collective-permute-done.15.refs_2_ = bf16[128,512]{1,0:T(8,128)(2,1)S(1)} collective-permute-done((bf16[128,512]{1,0:T(8,128)(2,1)S(1)}, bf16[128,512]{1,0:T(8,128)(2,1)S(1)}, u32[]{:S(2)}, u32[]{:S(2)}) %collective-permute-start.15) | collective-permute-done | bytes 131104 | tf_op jit(solution)/shard_map/ppermute | solution.py:268
  114.3 1.7 %unplace_rows.1 = bf16[256,512]{1,0:T(8,128)(2,1)} custom-call(s32[4]{0:T(128)S(1)} %pad_add_fusion.where, s32[1,256]{1,0:T(1,128)S(1)} %copy-done.5, bf16[128,512]{1,0:T(8,128)(2,1)S(1)} %add_convert_fusion.3.refs_0_, bf16[128,512]{1,0:T(8,128)(2,1)S(1)} %collective-permute-done.14.refs_1_, bf16[128,512]{1,0:T(8,128)(2,1)S(1)} %collective-permute-done.15.refs_2_, ...), custom_call_target="tpu_custom_call" | custom-call | flops 134217728 | bytes 786432 | tf_op jit(solution)/shard_map/unplace_rows/pallas_call | solution.py:204
  116.0 3.1 %weight_grad.5 = bf16[1024,1024]{1,0:T(8,128)(2,1)} custom-call(bf16[512,2048]{1,0:T(8,128)(2,1)S(1)} %get-tuple-element.63.rows, bf16[512,1024]{1,0:T(8,128)(2,1)S(1)} %get-tuple-element.65.out, bf16[1024,1024]{1,0:T(8,128)(2,1)S(1)} %collective-permute-done.25.refs_0_), custom_call_target="tpu_custom_call" | custom-call | flops 1073741824 | bytes 4194304 | tf_op jit(solution)/shard_map/weight_grad/pallas_call | solution.py:231
  119.1 3.1 %weight_grad.7 = bf16[1024,1024]{1,0:T(8,128)(2,1)} custom-call(bf16[512,2048]{1,0:T(8,128)(2,1)S(1)} %get-tuple-element.66.rows, bf16[512,1024]{1,0:T(8,128)(2,1)S(1)} %get-tuple-element.68.out, bf16[1024,1024]{1,0:T(8,128)(2,1)S(1)} %collective-permute-done.26.refs_0_), custom_call_target="tpu_custom_call" | custom-call | flops 1073741824 | bytes 4194304 | tf_op jit(solution)/shard_map/weight_grad/pallas_call | solution.py:231
  (60 shorter events, 11.0 us)
Async XLA Ops:
  0.6 10.6 %copy-start = (bf16[1,1024,1024]{2,1,0:T(8,128)(2,1)S(1)}, bf16[1,1024,1024]{2,1,0:T(8,128)(2,1)}, u32[]{:S(2)}) copy-start(bf16[1,1024,1024]{2,1,0:T(8,128)(2,1)} %param.12) | copy-start | bytes 6291460
  0.6 10.6 %copy-start.6 = (f32[256]{0:T(256)S(1)}, f32[256]{0:T(256)}, u32[]{:S(2)}) copy-start(f32[256]{0:T(256)} %param.9) | copy-start | bytes 3076
  0.7 10.6 %collective-permute-start = (bf16[1024,1024]{1,0:T(8,128)(2,1)}, bf16[1024,1024]{1,0:T(8,128)(2,1)}, u32[]{:S(2)}, u32[]{:S(2)}) collective-permute-start(bf16[1024,1024]{1,0:T(8,128)(2,1)} %bitcast.14), channel_id=1, source_target_pairs={{0,1},{1,0},{2,3},{3,2},{4,5},{5,4},{6,7},{7,6},{8,9},{9,8},{10,11... | collective-permute-start | bytes 6291464 | tf_op jit(solution)/shard_map/ppermute | solution.py:262
  1.2 10.1 %collective-permute-start.1 = (bf16[1024,1024]{1,0:T(8,128)(2,1)}, bf16[1024,1024]{1,0:T(8,128)(2,1)}, u32[]{:S(2)}, u32[]{:S(2)}) collective-permute-start(bf16[1024,1024]{1,0:T(8,128)(2,1)} %bitcast.18), channel_id=1, source_target_pairs={{0,1},{1,0},{2,3},{3,2},{4,5},{5,4},{6,7},{7,6},{8,9},{9,8},{10,11... | collective-permute-start | bytes 6291464 | tf_op jit(solution)/shard_map/ppermute | solution.py:262
  3.1 8.2 %copy-start.5 = (s32[1,256]{1,0:T(1,128)S(1)}, s32[1,256]{1,0:T(1,128)}, u32[]{:S(2)}) copy-start(s32[1,256]{1,0:T(1,128)} %add_bitcast_fusion.refs_0_.position) | copy-start | bytes 3076
  6.0 16.4 %collective-permute-start.5 = (bf16[128,1024]{1,0:T(8,128)(2,1)}, bf16[128,1024]{1,0:T(8,128)(2,1)S(1)}, u32[]{:S(2)}, u32[]{:S(2)}) collective-permute-start(bf16[128,1024]{1,0:T(8,128)(2,1)} %get-tuple-element.40), channel_id=1, source_target_pairs={{0,2},{2,4},{4,6},{6,0},{1,3},{3,5},{5,7},{7,1},{8,10},{10,12},{12... | collective-permute-start | bytes 786440 | tf_op jit(solution)/shard_map/ppermute | solution.py:268
  9.1 13.8 %collective-permute-start.6 = (bf16[128,1024]{1,0:T(8,128)(2,1)}, bf16[128,1024]{1,0:T(8,128)(2,1)S(1)}, u32[]{:S(2)}, u32[]{:S(2)}) collective-permute-start(bf16[128,1024]{1,0:T(8,128)(2,1)} %get-tuple-element.42), channel_id=1, source_target_pairs={{0,6},{2,0},{4,2},{6,4},{1,7},{3,1},{5,3},{7,5},{8,14},{10,8},{12,... | collective-permute-start | bytes 786440 | tf_op jit(solution)/shard_map/ppermute | solution.py:268
  15.3 26.2 %copy-start.7 = (bf16[128,1024]{1,0:T(8,128)(2,1)S(1)}, bf16[128,1024]{1,0:T(8,128)(2,1)}, u32[]{:S(2)}) copy-start(bf16[128,1024]{1,0:T(8,128)(2,1)} %get-tuple-element.54) | copy-start | bytes 786436
  22.4 44.8 %copy-start.2 = (bf16[1,1024,1024]{2,1,0:T(8,128)(2,1)S(1)}, bf16[1,1024,1024]{2,1,0:T(8,128)(2,1)}, u32[]{:S(2)}) copy-start(bf16[1,1024,1024]{2,1,0:T(8,128)(2,1)} %param.13) | copy-start | bytes 6291460
  22.9 32.0 %collective-permute-start.7 = (bf16[256,1024]{1,0:T(8,128)(2,1)S(1)}, bf16[256,1024]{1,0:T(8,128)(2,1)S(1)}, u32[]{:S(2)}, u32[]{:S(2)}) collective-permute-start(bf16[256,1024]{1,0:T(8,128)(2,1)S(1)} %constant_dynamic-update-slice_fusion.refs_0_), channel_id=1, source_target_pairs={{0,8},{8,0},{16,24},{24,16},{1,9},{9,1},{17,25},{25,17},{2,10},{10... | collective-permute-start | bytes 1572872 | tf_op jit(solution)/shard_map/ppermute | solution.py:265
  24.5 30.5 %collective-permute-start.8 = (bf16[256,1024]{1,0:T(8,128)(2,1)S(1)}, bf16[256,1024]{1,0:T(8,128)(2,1)S(1)}, u32[]{:S(2)}, u32[]{:S(2)}) collective-permute-start(bf16[256,1024]{1,0:T(8,128)(2,1)S(1)} %constant_dynamic-update-slice_fusion.refs_0_), channel_id=1, source_target_pairs={{0,16},{8,24},{16,0},{24,8},{1,17},{9,25},{17,1},{25,9},{2,18},{10... | collective-permute-start | bytes 1572872 | tf_op jit(solution)/shard_map/ppermute | solution.py:265
  26.0 15.5 %collective-permute-start.4 = (bf16[128,512]{1,0:T(8,128)(2,1)S(1)}, bf16[128,512]{1,0:T(8,128)(2,1)S(1)}, u32[]{:S(2)}, u32[]{:S(2)}) collective-permute-start(bf16[128,512]{1,0:T(8,128)(2,1)S(1)} %get-tuple-element.39), channel_id=1, source_target_pairs={{0,24},{8,16},{16,8},{24,0},{1,25},{9,17},{17,9},{25,1},{2,26},{10... | collective-permute-start | bytes 393224 | tf_op jit(solution)/shard_map/ppermute | solution.py:265
  26.5 16.6 %collective-permute-start.3 = (bf16[128,512]{1,0:T(8,128)(2,1)S(1)}, bf16[128,512]{1,0:T(8,128)(2,1)S(1)}, u32[]{:S(2)}, u32[]{:S(2)}) collective-permute-start(bf16[128,512]{1,0:T(8,128)(2,1)S(1)} %get-tuple-element.38), channel_id=1, source_target_pairs={{0,16},{8,24},{16,0},{24,8},{1,17},{9,25},{17,1},{25,9},{2,18},{10... | collective-permute-start | bytes 393224 | tf_op jit(solution)/shard_map/ppermute | solution.py:265
  28.0 15.1 %collective-permute-start.2 = (bf16[128,512]{1,0:T(8,128)(2,1)S(1)}, bf16[128,512]{1,0:T(8,128)(2,1)S(1)}, u32[]{:S(2)}, u32[]{:S(2)}) collective-permute-start(bf16[128,512]{1,0:T(8,128)(2,1)S(1)} %get-tuple-element.37), channel_id=1, source_target_pairs={{0,8},{8,0},{16,24},{24,16},{1,9},{9,1},{17,25},{25,17},{2,10},{10... | collective-permute-start | bytes 393224 | tf_op jit(solution)/shard_map/ppermute | solution.py:265
  41.5 11.4 %collective-permute-start.16 = (bf16[128,1024]{1,0:T(8,128)(2,1)S(1)}, bf16[128,1024]{1,0:T(8,128)(2,1)S(1)}, u32[]{:S(2)}, u32[]{:S(2)}) collective-permute-start(bf16[128,1024]{1,0:T(8,128)(2,1)S(1)} %copy-done.7), channel_id=1, source_target_pairs={{0,4},{2,6},{4,0},{6,2},{1,5},{3,7},{5,1},{7,3},{8,12},{10,14},{12... | collective-permute-start | bytes 786440 | tf_op jit(solution)/shard_map/ppermute | solution.py:268
  52.9 11.4 %collective-permute-start.17 = (bf16[128,1024]{1,0:T(8,128)(2,1)S(1)}, bf16[128,1024]{1,0:T(8,128)(2,1)S(1)}, u32[]{:S(2)}, u32[]{:S(2)}) collective-permute-start(bf16[128,1024]{1,0:T(8,128)(2,1)S(1)} %collective-permute-done.16.refs_0_), channel_id=1, source_target_pairs={{0,8},{8,0},{16,24},{24,16},{1,9},{9,1},{17,25},{25,17},{2,10},{10... | collective-permute-start | bytes 786440 | tf_op jit(solution)/shard_map/ppermute | solution.py:265
  54.4 9.2 %collective-permute-start.18 = (bf16[128,1024]{1,0:T(8,128)(2,1)S(1)}, bf16[128,1024]{1,0:T(8,128)(2,1)S(1)}, u32[]{:S(2)}, u32[]{:S(2)}) collective-permute-start(bf16[128,1024]{1,0:T(8,128)(2,1)S(1)} %collective-permute-done.16.refs_0_), channel_id=1, source_target_pairs={{0,16},{8,24},{16,0},{24,8},{1,17},{9,25},{17,1},{25,9},{2,18},{10... | collective-permute-start | bytes 786440 | tf_op jit(solution)/shard_map/ppermute | solution.py:265
  55.0 11.0 %collective-permute-start.9 = (bf16[256,512]{1,0:T(8,128)(2,1)S(1)}, bf16[256,512]{1,0:T(8,128)(2,1)S(1)}, u32[]{:S(2)}, u32[]{:S(2)}) collective-permute-start(bf16[256,512]{1,0:T(8,128)(2,1)S(1)} %slice.36), channel_id=1, source_target_pairs={{0,8},{8,0},{16,24},{24,16},{1,9},{9,1},{17,25},{25,17},{2,10},{10... | collective-permute-start | bytes 786440 | tf_op jit(solution)/shard_map/ppermute | solution.py:265
  55.6 11.6 %collective-permute-start.10 = (bf16[256,512]{1,0:T(8,128)(2,1)S(1)}, bf16[256,512]{1,0:T(8,128)(2,1)S(1)}, u32[]{:S(2)}, u32[]{:S(2)}) collective-permute-start(bf16[256,512]{1,0:T(8,128)(2,1)S(1)} %slice.37), channel_id=1, source_target_pairs={{0,16},{8,24},{16,0},{24,8},{1,17},{9,25},{17,1},{25,9},{2,18},{10... | collective-permute-start | bytes 786440 | tf_op jit(solution)/shard_map/ppermute | solution.py:265
  63.7 10.4 %collective-permute-start.19 = (bf16[128,512]{1,0:T(8,128)(2,1)S(1)}, bf16[128,512]{1,0:T(8,128)(2,1)S(1)}, u32[]{:S(2)}, u32[]{:S(2)}) collective-permute-start(bf16[128,512]{1,0:T(8,128)(2,1)S(1)} %slice.54), channel_id=1, source_target_pairs={{0,8},{8,0},{16,24},{24,16},{1,9},{9,1},{17,25},{25,17},{2,10},{10... | collective-permute-start | bytes 393224 | tf_op jit(solution)/shard_map/ppermute | solution.py:265
  64.3 9.8 %collective-permute-start.20 = (bf16[128,512]{1,0:T(8,128)(2,1)S(1)}, bf16[128,512]{1,0:T(8,128)(2,1)S(1)}, u32[]{:S(2)}, u32[]{:S(2)}) collective-permute-start(bf16[128,512]{1,0:T(8,128)(2,1)S(1)} %slice.55), channel_id=1, source_target_pairs={{0,16},{8,24},{16,0},{24,8},{1,17},{9,25},{17,1},{25,9},{2,18},{10... | collective-permute-start | bytes 393224 | tf_op jit(solution)/shard_map/ppermute | solution.py:265
  80.6 7.4 %collective-permute-start.23 = (bf16[128,512]{1,0:T(8,128)(2,1)S(1)}, bf16[128,512]{1,0:T(8,128)(2,1)S(1)}, u32[]{:S(2)}, u32[]{:S(2)}) collective-permute-start(bf16[128,512]{1,0:T(8,128)(2,1)S(1)} %get-tuple-element.62), channel_id=1, source_target_pairs={{0,24},{8,16},{16,8},{24,0},{1,25},{9,17},{17,9},{25,1},{2,26},{10... | collective-permute-start | bytes 393224 | tf_op jit(solution)/shard_map/ppermute | solution.py:265
  81.2 15.0 %collective-permute-start.13 = (bf16[256,512]{1,0:T(8,128)(2,1)S(1)}, bf16[256,512]{1,0:T(8,128)(2,1)S(1)}, u32[]{:S(2)}, u32[]{:S(2)}) collective-permute-start(bf16[256,512]{1,0:T(8,128)(2,1)S(1)} %get-tuple-element.52), channel_id=1, source_target_pairs={{0,24},{8,16},{16,8},{24,0},{1,25},{9,17},{17,9},{25,1},{2,26},{10... | collective-permute-start | bytes 786440 | tf_op jit(solution)/shard_map/ppermute | solution.py:265
  83.6 12.6 %collective-permute-start.12 = (bf16[256,512]{1,0:T(8,128)(2,1)S(1)}, bf16[256,512]{1,0:T(8,128)(2,1)S(1)}, u32[]{:S(2)}, u32[]{:S(2)}) collective-permute-start(bf16[256,512]{1,0:T(8,128)(2,1)S(1)} %get-tuple-element.51), channel_id=1, source_target_pairs={{0,16},{8,24},{16,0},{24,8},{1,17},{9,25},{17,1},{25,9},{2,18},{10... | collective-permute-start | bytes 786440 | tf_op jit(solution)/shard_map/ppermute | solution.py:265
  84.1 12.1 %collective-permute-start.11 = (bf16[256,512]{1,0:T(8,128)(2,1)S(1)}, bf16[256,512]{1,0:T(8,128)(2,1)S(1)}, u32[]{:S(2)}, u32[]{:S(2)}) collective-permute-start(bf16[256,512]{1,0:T(8,128)(2,1)S(1)} %get-tuple-element.50), channel_id=1, source_target_pairs={{0,8},{8,0},{16,24},{24,16},{1,9},{9,1},{17,25},{25,17},{2,10},{10... | collective-permute-start | bytes 786440 | tf_op jit(solution)/shard_map/ppermute | solution.py:265
  84.7 11.6 %collective-permute-start.22 = (bf16[128,512]{1,0:T(8,128)(2,1)S(1)}, bf16[128,512]{1,0:T(8,128)(2,1)S(1)}, u32[]{:S(2)}, u32[]{:S(2)}) collective-permute-start(bf16[128,512]{1,0:T(8,128)(2,1)S(1)} %get-tuple-element.61), channel_id=1, source_target_pairs={{0,16},{8,24},{16,0},{24,8},{1,17},{9,25},{17,1},{25,9},{2,18},{10... | collective-permute-start | bytes 393224 | tf_op jit(solution)/shard_map/ppermute | solution.py:265
  88.0 8.2 %collective-permute-start.21 = (bf16[128,512]{1,0:T(8,128)(2,1)S(1)}, bf16[128,512]{1,0:T(8,128)(2,1)S(1)}, u32[]{:S(2)}, u32[]{:S(2)}) collective-permute-start(bf16[128,512]{1,0:T(8,128)(2,1)S(1)} %get-tuple-element.60), channel_id=1, source_target_pairs={{0,8},{8,0},{16,24},{24,16},{1,9},{9,1},{17,25},{25,17},{2,10},{10... | collective-permute-start | bytes 393224 | tf_op jit(solution)/shard_map/ppermute | solution.py:265
  98.4 17.6 %collective-permute-start.25 = (bf16[1024,1024]{1,0:T(8,128)(2,1)S(1)}, bf16[1024,1024]{1,0:T(8,128)(2,1)S(1)}, u32[]{:S(2)}, u32[]{:S(2)}) collective-permute-start(bf16[1024,1024]{1,0:T(8,128)(2,1)S(1)} %weight_grad.4), channel_id=1, source_target_pairs={{0,1},{1,0},{2,3},{3,2},{4,5},{5,4},{6,7},{7,6},{8,9},{9,8},{10,11... | collective-permute-start | bytes 6291464 | tf_op jit(solution)/shard_map/ppermute | solution.py:262
  100.5 18.6 %collective-permute-start.26 = (bf16[1024,1024]{1,0:T(8,128)(2,1)S(1)}, bf16[1024,1024]{1,0:T(8,128)(2,1)S(1)}, u32[]{:S(2)}, u32[]{:S(2)}) collective-permute-start(bf16[1024,1024]{1,0:T(8,128)(2,1)S(1)} %weight_grad.6), channel_id=1, source_target_pairs={{0,1},{1,0},{2,3},{3,2},{4,5},{5,4},{6,7},{7,6},{8,9},{9,8},{10,11... | collective-permute-start | bytes 6291464 | tf_op jit(solution)/shard_map/ppermute | solution.py:262
  101.2 10.7 %collective-permute-start.24 = (bf16[128,512]{1,0:T(8,128)(2,1)S(1)}, bf16[128,512]{1,0:T(8,128)(2,1)S(1)}, u32[]{:S(2)}, u32[]{:S(2)}) collective-permute-start(bf16[128,512]{1,0:T(8,128)(2,1)S(1)} %add_convert_fusion), channel_id=1, source_target_pairs={{0,4},{2,6},{4,0},{6,2},{1,5},{3,7},{5,1},{7,3},{8,12},{10,14},{12... | collective-permute-start | bytes 393224 | tf_op jit(solution)/shard_map/ppermute | solution.py:268
  101.4 10.5 %collective-permute-start.14 = (bf16[128,512]{1,0:T(8,128)(2,1)S(1)}, bf16[128,512]{1,0:T(8,128)(2,1)S(1)}, u32[]{:S(2)}, u32[]{:S(2)}) collective-permute-start(bf16[128,512]{1,0:T(8,128)(2,1)S(1)} %get-tuple-element.70), channel_id=1, source_target_pairs={{0,6},{2,0},{4,2},{6,4},{1,7},{3,1},{5,3},{7,5},{8,14},{10,8},{12,... | collective-permute-start | bytes 393224 | tf_op jit(solution)/shard_map/ppermute | solution.py:268
  105.0 9.2 %collective-permute-start.15 = (bf16[128,512]{1,0:T(8,128)(2,1)S(1)}, bf16[128,512]{1,0:T(8,128)(2,1)S(1)}, u32[]{:S(2)}, u32[]{:S(2)}) collective-permute-start(bf16[128,512]{1,0:T(8,128)(2,1)S(1)} %get-tuple-element.69), channel_id=1, source_target_pairs={{0,2},{2,4},{4,6},{6,0},{1,3},{3,5},{5,7},{7,1},{8,10},{10,12},{12... | collective-permute-start | bytes 393224 | tf_op jit(solution)/shard_map/ppermute | solution.py:268
  (3 other events, 4.0 us)

commit v4 on v3

v4 whole, which is shorter than its diff:
```python
import functools

import jax
import jax.numpy as jnp
from jax import lax
from jax.experimental import pallas as pl
from jax.experimental.pallas import tpu as pltpu
from jax.sharding import PartitionSpec as P

F32 = jnp.float32
BF16 = jnp.bfloat16
I32 = jnp.int32
ANY = pl.BlockSpec(memory_space=pl.ANY)
VMEM = pl.BlockSpec(memory_space=pltpu.VMEM)
SMEM = pl.BlockSpec(memory_space=pltpu.SMEM)
HBM = pl.BlockSpec(memory_space=pltpu.HBM)
LIMIT = 22 * 2**20


def dot(lhs, rhs, left=1, right=0):
    return lax.dot_general(lhs, rhs, (((left,), (right,)), ((), ())), preferred_element_type=F32)


def hits(position, first, rows):
    ids = lax.broadcasted_iota(I32, (rows, position.shape[1]), 0) + first
    return ids == position


def places(index, slot, capacity):
    return index[...] * capacity + slot[...]


def expert_first(k, capacity):
    experts = lax.axis_size("expert")
    return 0 if k is None else lax.rem(lax.axis_index("expert") + k, experts) * capacity


def gate_of(hit, gate):
    return jnp.sum(jnp.where(hit, gate, 0.0), axis=1, keepdims=True)


def place_kernel(spans, shifts, capacity, index, slot, gate, tokens, grad_output, *refs):
    outs, (tok, grad, sem) = refs[: len(spans)], refs[len(spans) :]
    share = tok.shape[1]
    columns = pl.ds(pl.multiple_of(lax.axis_index("tensor") * share, share), share)
    first = pltpu.make_async_copy(tokens.at[:, columns], tok, sem.at[0])
    second = pltpu.make_async_copy(grad_output.at[:, columns], grad, sem.at[1])
    first.start()
    second.start()
    position = places(index, slot, capacity)
    found = [hits(position, expert_first(k, capacity), rows) for k, rows in zip(shifts, spans)]
    first.wait()
    second.wait()
    for hit, out in zip(found, outs):
        hot = hit.astype(BF16)
        out[:, :share] = dot(hot, tok[...]).astype(BF16)
        out[:, share:] = (dot(hot, grad[...]) * gate_of(hit, gate[...])).astype(BF16)


def place(spans, shifts, capacity, index, slot, gate, tokens, grad_output, share):
    count = tokens.shape[0]
    return pl.pallas_call(
        functools.partial(place_kernel, spans, shifts, capacity),
        out_shape=[jax.ShapeDtypeStruct((rows, 2 * share), BF16) for rows in spans],
        in_specs=[VMEM, VMEM, VMEM, HBM, HBM],
        out_specs=[VMEM] * len(spans),
        scratch_shapes=[
            pltpu.VMEM((count, share), BF16), pltpu.VMEM((count, share), BF16), pltpu.SemaphoreType.DMA((2,))
        ],
        compiler_params=pltpu.CompilerParams(vmem_limit_bytes=LIMIT),
        cost_estimate=pl.CostEstimate(
            flops=4 * sum(spans) * count * share, bytes_accessed=4 * (count + sum(spans)) * share, transcendentals=0
        ),
        name="place_rows",
    )(index, slot, gate, tokens, grad_output)


def gelu_parts(pre):
    c = 0.7978845608028654
    square = pre * pre
    th = jnp.tanh(c * (pre + 0.044715 * (pre * square)))
    half = 0.5 * (1.0 + th)
    return pre * half, half + 0.5 * pre * (1.0 - th * th) * (c + (3 * 0.044715 * c) * square)


def expert_kernel(own_rows, chunk_rows, base, block_base, aliased, *refs):
    refs = list(refs)
    take = lambda n: [refs.pop(0) for _ in range(n)]
    if own_rows:
        index, slot, gate, tokens, grad_output = take(5)
    chunks = [take(5) for _ in chunk_rows]
    up_halves, down_halves = take(2), take(2)
    take(aliased)
    tok_out, grad_out, hidden_out, slope_out = take(4)
    blocks = take(4)
    tok, grad, up, down, hidden, slope, back = take(7)
    if own_rows:
        tokens_in, grad_in = take(2)
    (sem,) = take(1)
    rows, width = tok.shape
    half, share = width // 2, width // 4
    mine = lax.axis_index("dp")
    order = lax.axis_index("tensor") ^ (2 * mine)
    count = [0]

    def copy(src, dst):
        c = pltpu.make_async_copy(src, dst, sem.at[count[0]])
        count[0] += 1
        c.start()
        return c

    waits = []
    if own_rows:
        for src, dst in ((tokens, tokens_in), (grad_output, grad_in)):
            for start, place_at in ((mine * half, 0), ((1 - mine) * half, half)):
                start = pl.multiple_of(start, half)
                waits.append(copy(src.at[:, pl.ds(start, half)], dst.at[:, pl.ds(place_at, half)]))
    at = own_rows
    for (z, x, y, tok_d, grad_d), n in zip(chunks, chunk_rows):
        tok_slots = [r.at[:, pl.ds(0, share)] for r in (z, x, y)] + [tok_d]
        grad_slots = [r.at[:, pl.ds(share, share)] for r in (z, x, y)] + [grad_d]
        for j in range(4):
            columns = pl.ds(pl.multiple_of((order ^ j) * share, share), share)
            waits.append(copy(tok_slots[j], tok.at[pl.ds(at, n), columns]))
            waits.append(copy(grad_slots[j], grad.at[pl.ds(at, n), columns]))
        at += n
    hid = hidden.shape[1]
    step = 256
    tiles = []
    for n in range(0, hid, step):
        cols = pl.ds(n, step)
        tiles.append([])
        for halves, dst in ((up_halves, up), (down_halves, down)):
            for i in range(2):
                tiles[-1].append(copy(halves[i].at[:, cols], dst.at[pl.ds(i * half, half), cols]))
    if own_rows:
        hit = hits(places(index, slot, own_rows), expert_first(0, own_rows), own_rows)
        hot = hit.astype(BF16)
        scale = gate_of(hit, gate[...])
    for w in waits:
        w.wait()
    if own_rows:
        tok[:own_rows, :] = dot(hot, tokens_in[...]).astype(BF16)
        grad[:own_rows, :] = (dot(hot, grad_in[...]) * scale).astype(BF16)
    outs = [copy(tok, tok_out.at[pl.ds(base, rows), :]), copy(grad, grad_out.at[pl.ds(base, rows), :])]
    for n, arrived in zip(range(0, hid, step), tiles):
        cols = slice(n, n + step)
        for w in arrived:
            w.wait()
        pre = dot(tok[...], up[:, cols])
        hidden_grad = dot(grad[...], down[:, cols])
        act, deriv = gelu_parts(pre)
        hidden[:, cols] = act.astype(BF16)
        slope[:, cols] = (hidden_grad * deriv).astype(BF16)
    outs.append(copy(hidden, hidden_out.at[pl.ds(base, rows), :]))
    outs.append(copy(slope, slope_out.at[pl.ds(base, rows), :]))
    for j in range(4):
        quarter = pl.ds(pl.multiple_of((order ^ j) * share, share), share)
        back[j] = dot(slope[...], up[quarter, :], 1, 1).astype(BF16)
        outs.append(copy(back.at[j], blocks[j].at[pl.ds(block_base, rows), :]))
    for w in outs:
        w.wait()


def expert_rows(own, chunks, weights, total_rows, base, block_rows, block_base, kept, blocks):
    own_rows = own[0] if own else 0
    chunk_rows = [c[0].shape[0] for c in chunks]
    rows = own_rows + sum(chunk_rows)
    half, hid = weights[0].shape
    width, share = 2 * half, half // 2
    operands = []
    specs = []
    if own:
        operands += own[1:]
        specs += [VMEM, VMEM, VMEM, HBM, HBM]
    for c in chunks:
        operands += c
        specs += [ANY] * 5
    operands += weights
    specs += [HBM] * 4
    aliases = {}
    for first, previous in ((0, kept), (4, blocks)):
        if previous:
            aliases.update({len(operands) + i: first + i for i in range(4)})
            operands += previous
            specs += [ANY] * 4
    shape = lambda *s: jax.ShapeDtypeStruct(s, BF16)
    buf = lambda *s: pltpu.VMEM(s, BF16)
    scratch = [
        buf(rows, width), buf(rows, width), buf(width, hid), buf(width, hid),
        buf(rows, hid), buf(rows, hid), buf(4, rows, share),
    ]
    copies = 8 + 8 * len(chunks) + 4 * (hid // 256)
    if own:
        count = own[4].shape[0]
        scratch += [buf(count, width), buf(count, width)]
        copies += 4
    scratch.append(pltpu.SemaphoreType.DMA((copies,)))
    out = pl.pallas_call(
        functools.partial(expert_kernel, own_rows, chunk_rows, base, block_base, len(aliases)),
        out_shape=[shape(total_rows, width)] * 2 + [shape(total_rows, hid)] * 2 + [shape(block_rows, share)] * 4,
        in_specs=specs,
        out_specs=[ANY] * 8,
        scratch_shapes=scratch,
        input_output_aliases=aliases,
        compiler_params=pltpu.CompilerParams(vmem_limit_bytes=LIMIT + rows * 2**15),
        cost_estimate=pl.CostEstimate(
            flops=6 * rows * width * hid, bytes_accessed=4 * width * hid + 8 * rows * width, transcendentals=rows * hid
        ),
        name="expert_rows",
    )(*operands)
    return list(out[:4]), list(out[4:])


def unplace_kernel(spans, shifts, capacity, index, slot, *refs):
    out = refs[-1]
    position = places(index, slot, capacity)
    total = None
    for k, rows, back in zip(shifts, spans, refs[:-1]):
        hot = hits(position, expert_first(k, capacity), rows).astype(BF16)
        part = dot(hot, back[...], 0, 0)
        total = part if total is None else total + part
    out[...] = total.astype(BF16)


def unplace(shifts, capacity, index, slot, backs):
    spans = [b.shape[0] for b in backs]
    count, share = index.shape[1], backs[0].shape[1]
    return pl.pallas_call(
        functools.partial(unplace_kernel, spans, shifts, capacity),
        out_shape=jax.ShapeDtypeStruct((count, share), BF16),
        in_specs=[VMEM] * (2 + len(backs)),
        out_specs=VMEM,
        compiler_params=pltpu.CompilerParams(vmem_limit_bytes=LIMIT),
        cost_estimate=pl.CostEstimate(
            flops=2 * sum(spans) * count * share, bytes_accessed=2 * (count + sum(spans)) * share, transcendentals=0
        ),
        name="unplace_rows",
    )(index, slot, *backs)


def outer_kernel(rows, out, *refs):
    total = dot(rows[...], out[...], 0, 0).astype(BF16)
    if len(refs) > 1:
        total = (total.astype(F32) + refs[0][...].astype(F32)).astype(BF16)
    refs[-1][...] = total


def outer(rows, out, which, got):
    count, width = rows.shape
    hid = out.shape[1]
    half, block = width // 2, width // 8
    steps = half // block
    tile = pl.BlockSpec((block, hid), lambda i: (i, 0))
    operands = [rows, out] + ([] if got is None else [got])
    return pl.pallas_call(
        outer_kernel,
        out_shape=jax.ShapeDtypeStruct((half, hid), BF16),
        grid=(steps,),
        in_specs=[
            pl.BlockSpec((count, block), lambda i: (0, which * steps + i)),
            pl.BlockSpec((count, hid), lambda i: (0, 0)),
        ]
        + [tile] * (len(operands) - 2),
        out_specs=tile,
        compiler_params=pltpu.CompilerParams(vmem_limit_bytes=LIMIT),
        cost_estimate=pl.CostEstimate(
            flops=2 * count * half * hid, bytes_accessed=2 * (count * (half + hid) + half * hid), transcendentals=0
        ),
        name="weight_grad",
    )(*operands)


def local(tokens, grad_output, gate_prob, expert_index, slot_index, up_weight, down_weight):
    experts = lax.axis_size("expert")
    tensor_size = lax.axis_size("tensor")
    tok_count, width = tokens.shape
    capacity = 2 * tok_count // experts
    share = width // tensor_size

    def swap(x):
        return lax.ppermute(x, "dp", [(0, 1), (1, 0)])

    def across(x, j):
        return lax.ppermute(x, "tensor", [(i, i ^ j) for i in range(tensor_size)])

    def shift(x, k):
        return lax.ppermute(x, "expert", [(i, (i + k) % experts) for i in range(experts)])

    def after(x, *others):
        return lax.optimization_barrier((x,) + others)[0]

    def spread(rows, *before):
        x, y = across(rows, 1), across(rows, 2)
        half_y, half_x = y[:, :share], x[:, share:]
        if before:
            half_y, half_x = after(half_y, *before), after(half_x, *before)
        return [rows, x, y, across(half_y, 1), across(half_x, 2)]

    def collect(blocks):
        got = [across(blocks[j], j) for j in (1, 2, 3)]

        def total(lo, hi):
            terms = [b[lo:hi].astype(F32) for b in [blocks[0]] + got]
            return (terms[0] + terms[1] + (terms[2] + terms[3])).astype(BF16)

        return total, got

    index, slot = expert_index.reshape(1, tok_count), slot_index.reshape(1, tok_count)
    gate = gate_prob.reshape(1, tok_count)
    up_own, down_own = up_weight[0], down_weight[0]
    weights = [up_own, swap(up_own), down_own, swap(down_own)]

    if experts == 4:
        shifts = [1, 3, 2]
        sends = place([capacity] * 3, shifts, capacity, index, slot, gate, tokens, grad_output, share)
        one, three = shift(sends[0], 1), shift(sends[1], 3)
        own = [capacity, index, slot, gate, tokens, grad_output]
        most = 3 * capacity
        kept, blocks = expert_rows(own, [], weights, 4 * capacity, 0, most, 0, None, None)
        two = shift(after(sends[2], blocks[0]), 2)
        near = spread(jnp.concatenate([after(one, blocks[0]), three], 0))
        kept, blocks = expert_rows(None, [near], weights, 4 * capacity, capacity, most, capacity, kept, blocks)
        far = spread(after(two, *near[3:]), blocks[0])
        total, got = collect(blocks)
        sums = [total(i * capacity, (i + 1) * capacity) for i in range(3)]
        kept, blocks = expert_rows(None, [far], weights, 4 * capacity, most, capacity, 0, kept, None)
        total, _ = collect([blocks[0]] + [after(b, got[0]) for b in blocks[1:]])
        sums.append(total(0, capacity))
        backs = sums[:1] + [shift(x, -k) for x, k in zip(sums[1:], shifts)]
        shifts = [0] + shifts
    else:
        rows = experts * capacity
        shifts = [None]

        def exchange(x):
            moved = lax.all_to_all(
                x.reshape(experts, capacity, x.shape[1]), "expert", split_axis=0, concat_axis=0, tiled=True
            )
            return moved.reshape(rows, x.shape[1])

        (send,) = place([rows], shifts, capacity, index, slot, gate, tokens, grad_output, share)
        kept, blocks = expert_rows(None, [spread(exchange(send))], weights, rows, 0, rows, 0, None, None)
        total, _ = collect(blocks)
        sums = [total(0, rows)]
        backs = [exchange(sums[0])]

    tok_rows, grad_rows, hidden, slope = kept
    hidden, slope = after(hidden, *sums), after(slope, *sums)
    got_up = swap(outer(tok_rows, slope, 1, None))
    got_down = swap(outer(grad_rows, hidden, 1, None))
    grad_up, grad_down = outer(tok_rows, slope, 0, got_up), outer(grad_rows, hidden, 0, got_down)
    backs[-1] = after(backs[-1], grad_up, grad_down)
    return unplace(shifts, capacity, index, slot, backs), grad_up[None], grad_down[None]


def solution(mesh):
    placed = (
        P(("expert", "dp"), None),
        P(("expert", "dp"), None),
        P(("expert", "dp")),
        P(("expert", "dp"), None),
        P(("expert", "dp"), None),
        P("expert", "dp", "tensor"),
        P("expert", "dp", "tensor"),
    )
    return jax.shard_map(
        local,
        mesh=mesh,
        in_specs=placed,
        out_specs=(
            P(("expert", "dp"), "tensor"),
            P("expert", "dp", "tensor"),
            P("expert", "dp", "tensor"),
        ),
        check_vma=False,
    )
```

time: 123 us -> 111 us (0.902)
  waiting for transfers between devices: 49.5 us -> 38.3 us
  local copies, waits for them, and re-layouts: 4.15 us -> 8.67 us
  Pallas kernels: 35.5 us -> 32.7 us
  other arithmetic: 2.26 us -> 0.27 us
    ppermute x6, waiting for transfers between devices: 18.8 us -> 5.68 us  [shift(): lax.ppermute(x, 'expert', [(i, (i + k) % experts) for i in range(experts)])]
    unnamed x17 -> x27, local copies, waits for them, and re-layouts: 4.08 us -> 8.59 us
    pallas_call x2, Pallas kernels: 4.63 us -> 1.64 us  [the longest x1 1.18 us: unplace(): pl.pallas_call(functools.partial(unplace_kernel, spans, shifts, capacity)...]
    ppermute x17 -> x14, waiting for transfers between devices: 30.6 us -> 32.6 us  [across(): return lax.ppermute(x, 'tensor', [(i, i ^ j) for i in range(tensor_size)])]
    reshape x1 -> x0, other arithmetic: 1.28 us -> none  [local(): position = (expert_index * capacity + slot_index).reshape(1, tok_count)]
    ppermute x17 -> x14, starting transfers between devices: 18 us -> 17.5 us  [across(): return lax.ppermute(x, 'tensor', [(i, i ^ j) for i in range(tensor_size)])]
  transfers between devices with their start and end apart: 27 -> 24, of which waited for: 11 -> 11; matrix products, arithmetic and copies ran while one was open for 2% -> 0% of each run, Pallas kernels for 19% -> 27%
where the time goes in v4:
time: 111 us; the launch traced here: 110 us
  waiting for transfers between devices  38.3 us (35%)
  Pallas kernels  32.7 us (29%)
  starting transfers between devices  29.5 us (27%)
  local copies, waits for them, and re-layouts  8.67 us (8%)
    ppermute x14, waiting for transfers between devices, across(): return lax.ppermute(x, 'tensor', [(i, i ^ j) for i in range(tensor_size)])  32.6 us
    pallas_call x3, Pallas kernels, expert_rows(): pl.pallas_call(functools.partial(expert_kernel, own_rows, chunk_rows, bas...  20.7 us
    ppermute x14, starting transfers between devices, across(): return lax.ppermute(x, 'tensor', [(i, i ^ j) for i in range(tensor_size)])  17.5 us
    ppermute x6, starting transfers between devices, shift(): lax.ppermute(x, 'expert', [(i, (i + k) % experts) for i in range(experts)])  10.8 us
    pallas_call x4, Pallas kernels, outer(): pl.pallas_call(outer_kernel, out_shape=jax.ShapeDtypeStruct((half, hid),...  10.3 us
    unnamed x27, local copies, waits for them, and re-layouts  8.59 us
    ppermute x6, waiting for transfers between devices, shift(): lax.ppermute(x, 'expert', [(i, (i + k) % experts) for i in range(experts)])  5.68 us
  transfers between devices with their start and end apart: 24, of which 11 were waited for; matrix products, arithmetic and copies ran while one was open for 0% of the time, Pallas kernels for 27%

profile of v4, /device:TPU:0, one launch (start us, length us, event | category | flops | bytes accessed | tf_op | source)
XLA Modules:
  0.0 110.2 jit_solution(14892726926017771456)
XLA Ops:
  1.2 1.3 %copy-done.3 = bf16[256,2048]{1,0:T(8,128)(2,1)S(1)} copy-done((bf16[256,2048]{1,0:T(8,128)(2,1)S(1)}, bf16[256,2048]{1,0:T(8,128)(2,1)}, u32[]{:S(2)}) %copy-start.3) | copy-done | bytes 1048600
  2.5 1.2 %copy-done.5 = bf16[256,2048]{1,0:T(8,128)(2,1)S(1)} copy-done((bf16[256,2048]{1,0:T(8,128)(2,1)S(1)}, bf16[256,2048]{1,0:T(8,128)(2,1)}, u32[]{:S(2)}) %copy-start.5) | copy-done | bytes 1048600
  6.2 3.1 %collective-permute-start = (bf16[128,1024]{1,0:T(8,128)(2,1)S(1)}, bf16[128,1024]{1,0:T(8,128)(2,1)S(1)}, u32[]{:S(2)}, u32[]{:S(2)}) collective-permute-start(bf16[128,1024]{1,0:T(8,128)(2,1)S(1)} %get-tuple-element.41), channel_id=1, source_target_pairs={{0,2},{2,4},{4,6},{6,0},{1,3},{3,5},{5,7},{7,1},{8,10},{10,12},{12... | collective-permute-start | bytes 786440 | tf_op jit(solution)/shard_map/ppermute | solution.py:288
  9.3 2.1 %collective-permute-start.3 = (bf16[128,1024]{1,0:T(8,128)(2,1)S(1)}, bf16[128,1024]{1,0:T(8,128)(2,1)S(1)}, u32[]{:S(2)}, u32[]{:S(2)}) collective-permute-start(bf16[128,1024]{1,0:T(8,128)(2,1)S(1)} %get-tuple-element.44), channel_id=1, source_target_pairs={{0,6},{2,0},{4,2},{6,4},{1,7},{3,1},{5,3},{7,5},{8,14},{10,8},{12,... | collective-permute-start | bytes 786440 | tf_op jit(solution)/shard_map/ppermute | solution.py:288
  11.4 1.6 %copy-done.1 = bf16[1,1024,1024]{2,1,0:T(8,128)(2,1)S(1)} copy-done((bf16[1,1024,1024]{2,1,0:T(8,128)(2,1)S(1)}, bf16[1,1024,1024]{2,1,0:T(8,128)(2,1)}, u32[]{:S(2)}) %copy-start.1) | copy-done | bytes 2097176
  15.5 7.0 %expert_rows.3 = (bf16[512,2048]{1,0:T(8,128)(2,1)S(1)}, bf16[512,2048]{1,0:T(8,128)(2,1)S(1)}, bf16[512,1024]{1,0:T(8,128)(2,1)S(1)}, bf16[512,1024]{1,0:T(8,12...) custom-call(s32[1,256]{1,0:T(1,128)S(1)} %bitcast.16, ...), custom_call_target="tpu_custom_call" | custom-call | flops 1610612736 | bytes 10485760 | tf_op jit(solution)/shard_map/expert_rows/pallas_call | solution.py:199
  22.9 1.6 %collective-permute-start.5 = (bf16[256,1024]{1,0:T(8,128)(2,1)S(1)}, bf16[256,1024]{1,0:T(8,128)(2,1)S(1)}, u32[]{:S(2)}, u32[]{:S(2)}) collective-permute-start(bf16[256,1024]{1,0:T(8,128)(2,1)S(1)} %constant_dynamic-update-slice_fusion.refs_0_), channel_id=1, source_target_pairs={{0,16},{8,24},{16,0},{24,8},{1,17},{9,25},{17,1},{25,9},{2,18},{10... | collective-permute-start | bytes 1572872 | tf_op jit(solution)/shard_map/ppermute | solution.py:285
  24.5 1.5 %collective-permute-start.4 = (bf16[256,1024]{1,0:T(8,128)(2,1)S(1)}, bf16[256,1024]{1,0:T(8,128)(2,1)S(1)}, u32[]{:S(2)}, u32[]{:S(2)}) collective-permute-start(bf16[256,1024]{1,0:T(8,128)(2,1)S(1)} %constant_dynamic-update-slice_fusion.refs_0_), channel_id=1, source_target_pairs={{0,8},{8,0},{16,24},{24,16},{1,9},{9,1},{17,25},{25,17},{2,10},{10... | collective-permute-start | bytes 1572872 | tf_op jit(solution)/shard_map/ppermute | solution.py:285
  26.0 1.3 %collective-permute-start.13 = (bf16[128,1024]{1,0:T(8,128)(2,1)S(1)}, bf16[128,1024]{1,0:T(8,128)(2,1)S(1)}, u32[]{:S(2)}, u32[]{:S(2)}) collective-permute-start(bf16[128,1024]{1,0:T(8,128)(2,1)S(1)} %get-tuple-element.57), channel_id=1, source_target_pairs={{0,4},{2,6},{4,0},{6,2},{1,5},{3,7},{5,1},{7,3},{8,12},{10,14},{12... | collective-permute-start | bytes 786440 | tf_op jit(solution)/shard_map/ppermute | solution.py:288
  27.3 9.0 %collective-permute-done.5.refs_2_ = bf16[256,1024]{1,0:T(8,128)(2,1)S(1)} collective-permute-done((bf16[256,1024]{1,0:T(8,128)(2,1)S(1)}, bf16[256,1024]{1,0:T(8,128)(2,1)S(1)}, u32[]{:S(2)}, u32[]{:S(2)}) %collective-permute-start.5) | collective-permute-done | bytes 524320 | tf_op jit(solution)/shard_map/ppermute | solution.py:285
  36.3 1.6 %collective-permute-start.6 = (bf16[256,512]{1,0:T(8,128)(2,1)S(1)}, bf16[256,512]{1,0:T(8,128)(2,1)S(1)}, u32[]{:S(2)}, u32[]{:S(2)}) collective-permute-start(bf16[256,512]{1,0:T(8,128)(2,1)S(1)} %slice.64), channel_id=1, source_target_pairs={{0,8},{8,0},{16,24},{24,16},{1,9},{9,1},{17,25},{25,17},{2,10},{10... | collective-permute-start | bytes 786440 | tf_op jit(solution)/shard_map/ppermute | solution.py:285
  37.9 1.6 %collective-permute-start.7 = (bf16[256,512]{1,0:T(8,128)(2,1)S(1)}, bf16[256,512]{1,0:T(8,128)(2,1)S(1)}, u32[]{:S(2)}, u32[]{:S(2)}) collective-permute-start(bf16[256,512]{1,0:T(8,128)(2,1)S(1)} %slice.65), channel_id=1, source_target_pairs={{0,16},{8,24},{16,0},{24,8},{1,17},{9,25},{17,1},{25,9},{2,18},{10... | collective-permute-start | bytes 786440 | tf_op jit(solution)/shard_map/ppermute | solution.py:285
  39.7 3.5 %collective-permute-done.6.refs_3_ = bf16[256,512]{1,0:T(8,128)(2,1)S(1)} collective-permute-done((bf16[256,512]{1,0:T(8,128)(2,1)S(1)}, bf16[256,512]{1,0:T(8,128)(2,1)S(1)}, u32[]{:S(2)}, u32[]{:S(2)}) %collective-permute-start.6) | collective-permute-done | bytes 262176 | tf_op jit(solution)/shard_map/ppermute | solution.py:285
  43.2 1.3 %collective-permute-done.7.refs_4_ = bf16[256,512]{1,0:T(8,128)(2,1)S(1)} collective-permute-done((bf16[256,512]{1,0:T(8,128)(2,1)S(1)}, bf16[256,512]{1,0:T(8,128)(2,1)S(1)}, u32[]{:S(2)}, u32[]{:S(2)}) %collective-permute-start.7) | collective-permute-done | bytes 262176 | tf_op jit(solution)/shard_map/ppermute | solution.py:285
  44.5 1.5 %collective-permute-start.15 = (bf16[128,1024]{1,0:T(8,128)(2,1)S(1)}, bf16[128,1024]{1,0:T(8,128)(2,1)S(1)}, u32[]{:S(2)}, u32[]{:S(2)}) collective-permute-start(bf16[128,1024]{1,0:T(8,128)(2,1)S(1)} %collective-permute-done.13.refs_0_), channel_id=1, source_target_pairs={{0,16},{8,24},{16,0},{24,8},{1,17},{9,25},{17,1},{25,9},{2,18},{10... | collective-permute-start | bytes 786440 | tf_op jit(solution)/shard_map/ppermute | solution.py:285
  46.5 7.1 %expert_rows.4 = (bf16[512,2048]{1,0:T(8,128)(2,1)S(1)}, bf16[512,2048]{1,0:T(8,128)(2,1)S(1)}, bf16[512,1024]{1,0:T(8,128)(2,1)S(1)}, bf16[512,1024]{1,0:T(8,12...) custom-call(bf16[256,1024]{1,0:T(8,128)(2,1)S(1)} %constant_dynamic-, ...), custom_call_target="tpu_custom_call", output_to_operand_aliasing={{0}: (9, {}), {1}: (10, {}), {2}: (11, {}), {3}: (12, {}), ... | custom-call | flops 3221225472 | bytes 12582912 | tf_op jit(solution)/shard_map/expert_rows/pallas_call | solution.py:199
  53.7 1.5 %collective-permute-start.8 = (bf16[384,512]{1,0:T(8,128)(2,1)S(1)}, bf16[384,512]{1,0:T(8,128)(2,1)S(1)}, u32[]{:S(2)}, u32[]{:S(2)}) collective-permute-start(bf16[384,512]{1,0:T(8,128)(2,1)S(1)} %get-tuple-element.53), channel_id=1, source_target_pairs={{0,8},{8,0},{16,24},{24,16},{1,9},{9,1},{17,25},{25,17},{2,10},{10... | collective-permute-start | bytes 1179656 | tf_op jit(solution)/shard_map/ppermute | solution.py:285
  55.7 1.5 %collective-permute-start.10 = (bf16[384,512]{1,0:T(8,128)(2,1)S(1)}, bf16[384,512]{1,0:T(8,128)(2,1)S(1)}, u32[]{:S(2)}, u32[]{:S(2)}) collective-permute-start(bf16[384,512]{1,0:T(8,128)(2,1)S(1)} %get-tuple-element.55), channel_id=1, source_target_pairs={{0,24},{8,16},{16,8},{24,0},{1,25},{9,17},{17,9},{25,1},{2,26},{10... | collective-permute-start | bytes 1179656 | tf_op jit(solution)/shard_map/ppermute | solution.py:285
  57.2 1.5 %collective-permute-start.16 = (bf16[128,512]{1,0:T(8,128)(2,1)S(1)}, bf16[128,512]{1,0:T(8,128)(2,1)S(1)}, u32[]{:S(2)}, u32[]{:S(2)}) collective-permute-start(bf16[128,512]{1,0:T(8,128)(2,1)S(1)} %slice.75), channel_id=1, source_target_pairs={{0,8},{8,0},{16,24},{24,16},{1,9},{9,1},{17,25},{25,17},{2,10},{10... | collective-permute-start | bytes 393224 | tf_op jit(solution)/shard_map/ppermute | solution.py:285
  59.3 13.5 %collective-permute-done.16.refs_3_ = bf16[128,512]{1,0:T(8,128)(2,1)S(1)} collective-permute-done((bf16[128,512]{1,0:T(8,128)(2,1)S(1)}, bf16[128,512]{1,0:T(8,128)(2,1)S(1)}, u32[]{:S(2)}, u32[]{:S(2)}) %collective-permute-start.16) | collective-permute-done | bytes 131104 | tf_op jit(solution)/shard_map/ppermute | solution.py:285
  74.0 6.6 %expert_rows.5 = (bf16[512,2048]{1,0:T(8,128)(2,1)S(1)}, bf16[512,2048]{1,0:T(8,128)(2,1)S(1)}, bf16[512,1024]{1,0:T(8,128)(2,1)S(1)}, bf16[512,1024]{1,0:T(8,12...) custom-call(bf16[128,1024]{1,0:T(8,128)(2,1)S(1)} %collective-permut, ...), custom_call_target="tpu_custom_call", output_to_operand_aliasing={{0}: (9, {}), {1}: (10, {}), {2}: (11, {}), {3}: (12, {})} | custom-call | flops 1610612736 | bytes 10485760 | tf_op jit(solution)/shard_map/expert_rows/pallas_call | solution.py:199
  81.2 1.5 %collective-permute-start.20 = (bf16[128,512]{1,0:T(8,128)(2,1)S(1)}, bf16[128,512]{1,0:T(8,128)(2,1)S(1)}, u32[]{:S(2)}, u32[]{:S(2)}) collective-permute-start(bf16[128,512]{1,0:T(8,128)(2,1)S(1)} %get-tuple-element.71), channel_id=1, source_target_pairs={{0,24},{8,16},{16,8},{24,0},{1,25},{9,17},{17,9},{25,1},{2,26},{10... | collective-permute-start | bytes 393224 | tf_op jit(solution)/shard_map/ppermute | solution.py:285
  82.7 1.5 %collective-permute-start.18 = (bf16[128,512]{1,0:T(8,128)(2,1)S(1)}, bf16[128,512]{1,0:T(8,128)(2,1)S(1)}, u32[]{:S(2)}, u32[]{:S(2)}) collective-permute-start(bf16[128,512]{1,0:T(8,128)(2,1)S(1)} %get-tuple-element.67), channel_id=1, source_target_pairs={{0,8},{8,0},{16,24},{24,16},{1,9},{9,1},{17,25},{25,17},{2,10},{10... | collective-permute-start | bytes 393224 | tf_op jit(solution)/shard_map/ppermute | solution.py:285
  84.4 1.3 %collective-permute-done.19 = bf16[128,512]{1,0:T(8,128)(2,1)S(1)} collective-permute-done((bf16[128,512]{1,0:T(8,128)(2,1)S(1)}, bf16[128,512]{1,0:T(8,128)(2,1)S(1)}, u32[]{:S(2)}, u32[]{:S(2)}) %collective-permute-start.19) | collective-permute-done | bytes 131104 | tf_op jit(solution)/shard_map/ppermute | solution.py:285
  85.7 1.4 %collective-permute-done.20 = bf16[128,512]{1,0:T(8,128)(2,1)S(1)} collective-permute-done((bf16[128,512]{1,0:T(8,128)(2,1)S(1)}, bf16[128,512]{1,0:T(8,128)(2,1)S(1)}, u32[]{:S(2)}, u32[]{:S(2)}) %collective-permute-start.20) | collective-permute-done | bytes 131104 | tf_op jit(solution)/shard_map/ppermute | solution.py:285
  87.1 1.5 %collective-permute-done.18 = bf16[128,512]{1,0:T(8,128)(2,1)S(1)} collective-permute-done((bf16[128,512]{1,0:T(8,128)(2,1)S(1)}, bf16[128,512]{1,0:T(8,128)(2,1)S(1)}, u32[]{:S(2)}, u32[]{:S(2)}) %collective-permute-start.18) | collective-permute-done | bytes 131104 | tf_op jit(solution)/shard_map/ppermute | solution.py:285
  88.6 2.0 %weight_grad.6 = bf16[1024,1024]{1,0:T(8,128)(2,1)S(1)} custom-call(bf16[512,2048]{1,0:T(8,128)(2,1)S(1)} %get-tuple-element.75.rows, bf16[512,1024]{1,0:T(8,128)(2,1)S(1)} %get-tuple-element.77.out), custom_call_target="tpu_custom_call" | custom-call | flops 1073741824 | bytes 4194304 | tf_op jit(solution)/shard_map/weight_grad/pallas_call | solution.py:256
  90.7 2.0 %weight_grad.4 = bf16[1024,1024]{1,0:T(8,128)(2,1)S(1)} custom-call(bf16[512,2048]{1,0:T(8,128)(2,1)S(1)} %get-tuple-element.72.rows, bf16[512,1024]{1,0:T(8,128)(2,1)S(1)} %get-tuple-element.74.out), custom_call_target="tpu_custom_call" | custom-call | flops 1073741824 | bytes 4194304 | tf_op jit(solution)/shard_map/weight_grad/pallas_call | solution.py:256
  93.3 2.8 %collective-permute-start.12 = (bf16[128,512]{1,0:T(8,128)(2,1)S(1)}, bf16[128,512]{1,0:T(8,128)(2,1)S(1)}, u32[]{:S(2)}, u32[]{:S(2)}) collective-permute-start(bf16[128,512]{1,0:T(8,128)(2,1)S(1)} %get-tuple-element.79), channel_id=1, source_target_pairs={{0,2},{2,4},{4,6},{6,0},{1,3},{3,5},{5,7},{7,1},{8,10},{10,12},{12... | collective-permute-start | bytes 393224 | tf_op jit(solution)/shard_map/ppermute | solution.py:288
  97.6 3.1 %weight_grad.7 = bf16[1024,1024]{1,0:T(8,128)(2,1)} custom-call(bf16[512,2048]{1,0:T(8,128)(2,1)S(1)} %get-tuple-element.75.rows, bf16[512,1024]{1,0:T(8,128)(2,1)S(1)} %get-tuple-element.77.out, bf16[1024,1024]{1,0:T(8,128)(2,1)S(1)} %collective-permute-done.23.refs_0_), custom_call_target="tpu_custom_call" | custom-call | flops 1073741824 | bytes 4194304 | tf_op jit(solution)/shard_map/weight_grad/pallas_call | solution.py:256
  100.8 3.1 %weight_grad.5 = bf16[1024,1024]{1,0:T(8,128)(2,1)} custom-call(bf16[512,2048]{1,0:T(8,128)(2,1)S(1)} %get-tuple-element.72.rows, bf16[512,1024]{1,0:T(8,128)(2,1)S(1)} %get-tuple-element.74.out, bf16[1024,1024]{1,0:T(8,128)(2,1)S(1)} %collective-permute-done.22.refs_0_), custom_call_target="tpu_custom_call" | custom-call | flops 1073741824 | bytes 4194304 | tf_op jit(solution)/shard_map/weight_grad/pallas_call | solution.py:256
  103.9 5.2 %collective-permute-done.21.refs_3_ = bf16[128,512]{1,0:T(8,128)(2,1)S(1)} collective-permute-done((bf16[128,512]{1,0:T(8,128)(2,1)S(1)}, bf16[128,512]{1,0:T(8,128)(2,1)S(1)}, u32[]{:S(2)}, u32[]{:S(2)}) %collective-permute-start.21) | collective-permute-done | bytes 131104 | tf_op jit(solution)/shard_map/ppermute | solution.py:288
  (59 shorter events, 13.0 us)
Async XLA Ops:
  0.6 10.8 %copy-start = (bf16[1,1024,1024]{2,1,0:T(8,128)(2,1)S(1)}, bf16[1,1024,1024]{2,1,0:T(8,128)(2,1)}, u32[]{:S(2)}) copy-start(bf16[1,1024,1024]{2,1,0:T(8,128)(2,1)} %param.12) | copy-start | bytes 6291460
  0.6 10.8 %collective-permute-start.1 = (bf16[1024,1024]{1,0:T(8,128)(2,1)}, bf16[1024,1024]{1,0:T(8,128)(2,1)S(1)}, u32[]{:S(2)}, u32[]{:S(2)}) collective-permute-start(bf16[1024,1024]{1,0:T(8,128)(2,1)} %bitcast.7), channel_id=1, source_target_pairs={{0,1},{1,0},{2,3},{3,2},{4,5},{5,4},{6,7},{7,6},{8,9},{9,8},{10,11... | collective-permute-start | bytes 6291464 | tf_op jit(solution)/shard_map/ppermute | solution.py:282
  1.2 10.2 %collective-permute-start.2 = (bf16[1024,1024]{1,0:T(8,128)(2,1)}, bf16[1024,1024]{1,0:T(8,128)(2,1)S(1)}, u32[]{:S(2)}, u32[]{:S(2)}) collective-permute-start(bf16[1024,1024]{1,0:T(8,128)(2,1)} %bitcast.11), channel_id=1, source_target_pairs={{0,1},{1,0},{2,3},{3,2},{4,5},{5,4},{6,7},{7,6},{8,9},{9,8},{10,11... | collective-permute-start | bytes 6291464 | tf_op jit(solution)/shard_map/ppermute | solution.py:282
  1.2 1.3 %copy-start.3 = (bf16[256,2048]{1,0:T(8,128)(2,1)S(1)}, bf16[256,2048]{1,0:T(8,128)(2,1)}, u32[]{:S(2)}) copy-start(bf16[256,2048]{1,0:T(8,128)(2,1)} %refs_3_.1) | copy-start | bytes 3145732
  2.5 1.2 %copy-start.5 = (bf16[256,2048]{1,0:T(8,128)(2,1)S(1)}, bf16[256,2048]{1,0:T(8,128)(2,1)}, u32[]{:S(2)}) copy-start(bf16[256,2048]{1,0:T(8,128)(2,1)} %refs_4_.1) | copy-start | bytes 3145732
  5.8 5.6 %copy-start.8 = (s32[256,1]{0,1:T(1,128)S(1)}, s32[256,1]{0,1:T(1,128)}, u32[]{:S(2)}) copy-start(s32[256,1]{0,1:T(1,128)} %param.10) | copy-start | bytes 3076
  5.8 5.7 %copy-start.10 = (s32[256,1]{0,1:T(1,128)S(1)}, s32[256,1]{0,1:T(1,128)}, u32[]{:S(2)}) copy-start(s32[256,1]{0,1:T(1,128)} %param.11) | copy-start | bytes 3076
  5.8 5.7 %copy-start.12 = (f32[256]{0:T(256)S(1)}, f32[256]{0:T(256)}, u32[]{:S(2)}) copy-start(f32[256]{0:T(256)} %param.9) | copy-start | bytes 3076
  6.2 16.3 %collective-permute-start = (bf16[128,1024]{1,0:T(8,128)(2,1)S(1)}, bf16[128,1024]{1,0:T(8,128)(2,1)S(1)}, u32[]{:S(2)}, u32[]{:S(2)}) collective-permute-start(bf16[128,1024]{1,0:T(8,128)(2,1)S(1)} %get-tuple-element.41), channel_id=1, source_target_pairs={{0,2},{2,4},{4,6},{6,0},{1,3},{3,5},{5,7},{7,1},{8,10},{10,12},{12... | collective-permute-start | bytes 786440 | tf_op jit(solution)/shard_map/ppermute | solution.py:288
  9.3 13.6 %collective-permute-start.3 = (bf16[128,1024]{1,0:T(8,128)(2,1)S(1)}, bf16[128,1024]{1,0:T(8,128)(2,1)S(1)}, u32[]{:S(2)}, u32[]{:S(2)}) collective-permute-start(bf16[128,1024]{1,0:T(8,128)(2,1)S(1)} %get-tuple-element.44), channel_id=1, source_target_pairs={{0,6},{2,0},{4,2},{6,4},{1,7},{3,1},{5,3},{7,5},{8,14},{10,8},{12,... | collective-permute-start | bytes 786440 | tf_op jit(solution)/shard_map/ppermute | solution.py:288
  11.4 1.6 %copy-start.1 = (bf16[1,1024,1024]{2,1,0:T(8,128)(2,1)S(1)}, bf16[1,1024,1024]{2,1,0:T(8,128)(2,1)}, u32[]{:S(2)}) copy-start(bf16[1,1024,1024]{2,1,0:T(8,128)(2,1)} %param.13) | copy-start | bytes 6291460
  22.5 24.1 %copy-start.2 = (bf16[1,1024,1024]{2,1,0:T(8,128)(2,1)S(1)}, bf16[1,1024,1024]{2,1,0:T(8,128)(2,1)}, u32[]{:S(2)}) copy-start(bf16[1,1024,1024]{2,1,0:T(8,128)(2,1)} %param.13) | copy-start | bytes 6291460
  22.9 13.4 %collective-permute-start.5 = (bf16[256,1024]{1,0:T(8,128)(2,1)S(1)}, bf16[256,1024]{1,0:T(8,128)(2,1)S(1)}, u32[]{:S(2)}, u32[]{:S(2)}) collective-permute-start(bf16[256,1024]{1,0:T(8,128)(2,1)S(1)} %constant_dynamic-update-slice_fusion.refs_0_), channel_id=1, source_target_pairs={{0,16},{8,24},{16,0},{24,8},{1,17},{9,25},{17,1},{25,9},{2,18},{10... | collective-permute-start | bytes 1572872 | tf_op jit(solution)/shard_map/ppermute | solution.py:285
  24.5 13.4 %collective-permute-start.4 = (bf16[256,1024]{1,0:T(8,128)(2,1)S(1)}, bf16[256,1024]{1,0:T(8,128)(2,1)S(1)}, u32[]{:S(2)}, u32[]{:S(2)}) collective-permute-start(bf16[256,1024]{1,0:T(8,128)(2,1)S(1)} %constant_dynamic-update-slice_fusion.refs_0_), channel_id=1, source_target_pairs={{0,8},{8,0},{16,24},{24,16},{1,9},{9,1},{17,25},{25,17},{2,10},{10... | collective-permute-start | bytes 1572872 | tf_op jit(solution)/shard_map/ppermute | solution.py:285
  26.0 13.7 %collective-permute-start.13 = (bf16[128,1024]{1,0:T(8,128)(2,1)S(1)}, bf16[128,1024]{1,0:T(8,128)(2,1)S(1)}, u32[]{:S(2)}, u32[]{:S(2)}) collective-permute-start(bf16[128,1024]{1,0:T(8,128)(2,1)S(1)} %get-tuple-element.57), channel_id=1, source_target_pairs={{0,4},{2,6},{4,0},{6,2},{1,5},{3,7},{5,1},{7,3},{8,12},{10,14},{12... | collective-permute-start | bytes 786440 | tf_op jit(solution)/shard_map/ppermute | solution.py:288
  36.3 6.8 %collective-permute-start.6 = (bf16[256,512]{1,0:T(8,128)(2,1)S(1)}, bf16[256,512]{1,0:T(8,128)(2,1)S(1)}, u32[]{:S(2)}, u32[]{:S(2)}) collective-permute-start(bf16[256,512]{1,0:T(8,128)(2,1)S(1)} %slice.64), channel_id=1, source_target_pairs={{0,8},{8,0},{16,24},{24,16},{1,9},{9,1},{17,25},{25,17},{2,10},{10... | collective-permute-start | bytes 786440 | tf_op jit(solution)/shard_map/ppermute | solution.py:285
  37.9 6.6 %collective-permute-start.7 = (bf16[256,512]{1,0:T(8,128)(2,1)S(1)}, bf16[256,512]{1,0:T(8,128)(2,1)S(1)}, u32[]{:S(2)}, u32[]{:S(2)}) collective-permute-start(bf16[256,512]{1,0:T(8,128)(2,1)S(1)} %slice.65), channel_id=1, source_target_pairs={{0,16},{8,24},{16,0},{24,8},{1,17},{9,25},{17,1},{25,9},{2,18},{10... | collective-permute-start | bytes 786440 | tf_op jit(solution)/shard_map/ppermute | solution.py:285
  44.5 12.7 %collective-permute-start.15 = (bf16[128,1024]{1,0:T(8,128)(2,1)S(1)}, bf16[128,1024]{1,0:T(8,128)(2,1)S(1)}, u32[]{:S(2)}, u32[]{:S(2)}) collective-permute-start(bf16[128,1024]{1,0:T(8,128)(2,1)S(1)} %collective-permute-done.13.refs_0_), channel_id=1, source_target_pairs={{0,16},{8,24},{16,0},{24,8},{1,17},{9,25},{17,1},{25,9},{2,18},{10... | collective-permute-start | bytes 786440 | tf_op jit(solution)/shard_map/ppermute | solution.py:285
  46.0 12.8 %collective-permute-start.14 = (bf16[128,1024]{1,0:T(8,128)(2,1)S(1)}, bf16[128,1024]{1,0:T(8,128)(2,1)S(1)}, u32[]{:S(2)}, u32[]{:S(2)}) collective-permute-start(bf16[128,1024]{1,0:T(8,128)(2,1)S(1)} %collective-permute-done.13.refs_0_), channel_id=1, source_target_pairs={{0,8},{8,0},{16,24},{24,16},{1,9},{9,1},{17,25},{25,17},{2,10},{10... | collective-permute-start | bytes 786440 | tf_op jit(solution)/shard_map/ppermute | solution.py:285
  53.7 27.0 %collective-permute-start.8 = (bf16[384,512]{1,0:T(8,128)(2,1)S(1)}, bf16[384,512]{1,0:T(8,128)(2,1)S(1)}, u32[]{:S(2)}, u32[]{:S(2)}) collective-permute-start(bf16[384,512]{1,0:T(8,128)(2,1)S(1)} %get-tuple-element.53), channel_id=1, source_target_pairs={{0,8},{8,0},{16,24},{24,16},{1,9},{9,1},{17,25},{25,17},{2,10},{10... | collective-permute-start | bytes 1179656 | tf_op jit(solution)/shard_map/ppermute | solution.py:285
  55.2 29.0 %collective-permute-start.9 = (bf16[384,512]{1,0:T(8,128)(2,1)S(1)}, bf16[384,512]{1,0:T(8,128)(2,1)S(1)}, u32[]{:S(2)}, u32[]{:S(2)}) collective-permute-start(bf16[384,512]{1,0:T(8,128)(2,1)S(1)} %get-tuple-element.54), channel_id=1, source_target_pairs={{0,16},{8,24},{16,0},{24,8},{1,17},{9,25},{17,1},{25,9},{2,18},{10... | collective-permute-start | bytes 1179656 | tf_op jit(solution)/shard_map/ppermute | solution.py:285
  55.7 28.5 %collective-permute-start.10 = (bf16[384,512]{1,0:T(8,128)(2,1)S(1)}, bf16[384,512]{1,0:T(8,128)(2,1)S(1)}, u32[]{:S(2)}, u32[]{:S(2)}) collective-permute-start(bf16[384,512]{1,0:T(8,128)(2,1)S(1)} %get-tuple-element.55), channel_id=1, source_target_pairs={{0,24},{8,16},{16,8},{24,0},{1,25},{9,17},{17,9},{25,1},{2,26},{10... | collective-permute-start | bytes 1179656 | tf_op jit(solution)/shard_map/ppermute | solution.py:285
  57.2 15.6 %collective-permute-start.16 = (bf16[128,512]{1,0:T(8,128)(2,1)S(1)}, bf16[128,512]{1,0:T(8,128)(2,1)S(1)}, u32[]{:S(2)}, u32[]{:S(2)}) collective-permute-start(bf16[128,512]{1,0:T(8,128)(2,1)S(1)} %slice.75), channel_id=1, source_target_pairs={{0,8},{8,0},{16,24},{24,16},{1,9},{9,1},{17,25},{25,17},{2,10},{10... | collective-permute-start | bytes 393224 | tf_op jit(solution)/shard_map/ppermute | solution.py:285
  58.8 15.2 %collective-permute-start.17 = (bf16[128,512]{1,0:T(8,128)(2,1)S(1)}, bf16[128,512]{1,0:T(8,128)(2,1)S(1)}, u32[]{:S(2)}, u32[]{:S(2)}) collective-permute-start(bf16[128,512]{1,0:T(8,128)(2,1)S(1)} %slice.76), channel_id=1, source_target_pairs={{0,16},{8,24},{16,0},{24,8},{1,17},{9,25},{17,1},{25,9},{2,18},{10... | collective-permute-start | bytes 393224 | tf_op jit(solution)/shard_map/ppermute | solution.py:285
  80.6 5.0 %collective-permute-start.19 = (bf16[128,512]{1,0:T(8,128)(2,1)S(1)}, bf16[128,512]{1,0:T(8,128)(2,1)S(1)}, u32[]{:S(2)}, u32[]{:S(2)}) collective-permute-start(bf16[128,512]{1,0:T(8,128)(2,1)S(1)} %get-tuple-element.69), channel_id=1, source_target_pairs={{0,16},{8,24},{16,0},{24,8},{1,17},{9,25},{17,1},{25,9},{2,18},{10... | collective-permute-start | bytes 393224 | tf_op jit(solution)/shard_map/ppermute | solution.py:285
  81.2 5.9 %collective-permute-start.20 = (bf16[128,512]{1,0:T(8,128)(2,1)S(1)}, bf16[128,512]{1,0:T(8,128)(2,1)S(1)}, u32[]{:S(2)}, u32[]{:S(2)}) collective-permute-start(bf16[128,512]{1,0:T(8,128)(2,1)S(1)} %get-tuple-element.71), channel_id=1, source_target_pairs={{0,24},{8,16},{16,8},{24,0},{1,25},{9,17},{17,9},{25,1},{2,26},{10... | collective-permute-start | bytes 393224 | tf_op jit(solution)/shard_map/ppermute | solution.py:285
  82.7 5.8 %collective-permute-start.18 = (bf16[128,512]{1,0:T(8,128)(2,1)S(1)}, bf16[128,512]{1,0:T(8,128)(2,1)S(1)}, u32[]{:S(2)}, u32[]{:S(2)}) collective-permute-start(bf16[128,512]{1,0:T(8,128)(2,1)S(1)} %get-tuple-element.67), channel_id=1, source_target_pairs={{0,8},{8,0},{16,24},{24,16},{1,9},{9,1},{17,25},{25,17},{2,10},{10... | collective-permute-start | bytes 393224 | tf_op jit(solution)/shard_map/ppermute | solution.py:285
  90.7 7.0 %collective-permute-start.23 = (bf16[1024,1024]{1,0:T(8,128)(2,1)S(1)}, bf16[1024,1024]{1,0:T(8,128)(2,1)S(1)}, u32[]{:S(2)}, u32[]{:S(2)}) collective-permute-start(bf16[1024,1024]{1,0:T(8,128)(2,1)S(1)} %weight_grad.6), channel_id=1, source_target_pairs={{0,1},{1,0},{2,3},{3,2},{4,5},{5,4},{6,7},{7,6},{8,9},{9,8},{10,11... | collective-permute-start | bytes 6291464 | tf_op jit(solution)/shard_map/ppermute | solution.py:282
  92.8 8.0 %collective-permute-start.22 = (bf16[1024,1024]{1,0:T(8,128)(2,1)S(1)}, bf16[1024,1024]{1,0:T(8,128)(2,1)S(1)}, u32[]{:S(2)}, u32[]{:S(2)}) collective-permute-start(bf16[1024,1024]{1,0:T(8,128)(2,1)S(1)} %weight_grad.4), channel_id=1, source_target_pairs={{0,1},{1,0},{2,3},{3,2},{4,5},{5,4},{6,7},{7,6},{8,9},{9,8},{10,11... | collective-permute-start | bytes 6291464 | tf_op jit(solution)/shard_map/ppermute | solution.py:282
  93.3 15.7 %collective-permute-start.12 = (bf16[128,512]{1,0:T(8,128)(2,1)S(1)}, bf16[128,512]{1,0:T(8,128)(2,1)S(1)}, u32[]{:S(2)}, u32[]{:S(2)}) collective-permute-start(bf16[128,512]{1,0:T(8,128)(2,1)S(1)} %get-tuple-element.79), channel_id=1, source_target_pairs={{0,2},{2,4},{4,6},{6,0},{1,3},{3,5},{5,7},{7,1},{8,10},{10,12},{12... | collective-permute-start | bytes 393224 | tf_op jit(solution)/shard_map/ppermute | solution.py:288
  96.2 12.9 %collective-permute-start.11 = (bf16[128,512]{1,0:T(8,128)(2,1)S(1)}, bf16[128,512]{1,0:T(8,128)(2,1)S(1)}, u32[]{:S(2)}, u32[]{:S(2)}) collective-permute-start(bf16[128,512]{1,0:T(8,128)(2,1)S(1)} %get-tuple-element.80), channel_id=1, source_target_pairs={{0,6},{2,0},{4,2},{6,4},{1,7},{3,1},{5,3},{7,5},{8,14},{10,8},{12,... | collective-permute-start | bytes 393224 | tf_op jit(solution)/shard_map/ppermute | solution.py:288
  97.2 11.9 %collective-permute-start.21 = (bf16[128,512]{1,0:T(8,128)(2,1)S(1)}, bf16[128,512]{1,0:T(8,128)(2,1)S(1)}, u32[]{:S(2)}, u32[]{:S(2)}) collective-permute-start(bf16[128,512]{1,0:T(8,128)(2,1)S(1)} %add_convert_fusion), channel_id=1, source_target_pairs={{0,4},{2,6},{4,0},{6,2},{1,5},{3,7},{5,1},{7,3},{8,12},{10,14},{12... | collective-permute-start | bytes 393224 | tf_op jit(solution)/shard_map/ppermute | solution.py:288
  (5 other events, 4.5 us)

commit v5 on v4

--- a/solution.py
+++ b/solution.py
@@ -15,6 +15,7 @@
 SMEM = pl.BlockSpec(memory_space=pltpu.SMEM)
 HBM = pl.BlockSpec(memory_space=pltpu.HBM)
 LIMIT = 22 * 2**20
+SMALL = pl.CostEstimate(flops=1000, bytes_accessed=1000, transcendentals=0)
 
 
 def dot(lhs, rhs, left=1, right=0):
@@ -67,10 +68,8 @@
         scratch_shapes=[
             pltpu.VMEM((count, share), BF16), pltpu.VMEM((count, share), BF16), pltpu.SemaphoreType.DMA((2,))
         ],
-        compiler_params=pltpu.CompilerParams(vmem_limit_bytes=LIMIT),
-        cost_estimate=pl.CostEstimate(
-            flops=4 * sum(spans) * count * share, bytes_accessed=4 * (count + sum(spans)) * share, transcendentals=0
-        ),
+        compiler_params=pltpu.CompilerParams(vmem_limit_bytes=54 * 2**20),
+        cost_estimate=SMALL,
         name="place_rows",
     )(index, slot, gate, tokens, grad_output)
 
@@ -177,7 +176,7 @@
         operands += c
         specs += [ANY] * 5
     operands += weights
-    specs += [HBM] * 4
+    specs += [ANY] * 4
     aliases = {}
     for first, previous in ((0, kept), (4, blocks)):
         if previous:
@@ -232,9 +231,7 @@
         in_specs=[VMEM] * (2 + len(backs)),
         out_specs=VMEM,
         compiler_params=pltpu.CompilerParams(vmem_limit_bytes=LIMIT),
-        cost_estimate=pl.CostEstimate(
-            flops=2 * sum(spans) * count * share, bytes_accessed=2 * (count + sum(spans)) * share, transcendentals=0
-        ),
+        cost_estimate=SMALL,
         name="unplace_rows",
     )(index, slot, *backs)
 
@@ -264,9 +261,7 @@
         + [tile] * (len(operands) - 2),
         out_specs=tile,
         compiler_params=pltpu.CompilerParams(vmem_limit_bytes=LIMIT),
-        cost_estimate=pl.CostEstimate(
-            flops=2 * count * half * hid, bytes_accessed=2 * (count * (half + hid) + half * hid), transcendentals=0
-        ),
+        cost_estimate=SMALL,
         name="weight_grad",
     )(*operands)
 
@@ -305,6 +300,11 @@
             return (terms[0] + terms[1] + (terms[2] + terms[3])).astype(BF16)
 
         return total, got
+
+    def other_halves(kept):
+        tok_rows, grad_rows, hidden, slope = kept
+        pairs = ((tok_rows, slope), (grad_rows, hidden))
+        return [dot(rows[:, width // 2 :], out, 0, 0).astype(BF16) for rows, out in pairs]
 
     index, slot = expert_index.reshape(1, tok_count), slot_index.reshape(1, tok_count)
     gate = gate_prob.reshape(1, tok_count)
@@ -320,14 +320,16 @@
         kept, blocks = expert_rows(own, [], weights, 4 * capacity, 0, most, 0, None, None)
         two = shift(after(sends[2], blocks[0]), 2)
         near = spread(jnp.concatenate([after(one, blocks[0]), three], 0))
+        far = spread(after(two, *near[1:3]))
+        near[0] = after(near[0], *far[3:])
         kept, blocks = expert_rows(None, [near], weights, 4 * capacity, capacity, most, capacity, kept, blocks)
-        far = spread(after(two, *near[3:]), blocks[0])
         total, got = collect(blocks)
-        sums = [total(i * capacity, (i + 1) * capacity) for i in range(3)]
+        backs = [total(0, capacity)]
+        backs += [shift(total(i * capacity, (i + 1) * capacity), -k) for i, k in ((1, 1), (2, 3))]
         kept, blocks = expert_rows(None, [far], weights, 4 * capacity, most, capacity, 0, kept, None)
-        total, _ = collect([blocks[0]] + [after(b, got[0]) for b in blocks[1:]])
-        sums.append(total(0, capacity))
-        backs = sums[:1] + [shift(x, -k) for x, k in zip(sums[1:], shifts)]
+        others = other_halves(kept)
+        total, _ = collect([blocks[0]] + [after(b, *got, *others) for b in blocks[1:]])
+        backs.append(shift(after(total(0, capacity), *backs[1:]), -2))
         shifts = [0] + shifts
     else:
         rows = experts * capacity
@@ -341,14 +343,12 @@
 
         (send,) = place([rows], shifts, capacity, index, slot, gate, tokens, grad_output, share)
         kept, blocks = expert_rows(None, [spread(exchange(send))], weights, rows, 0, rows, 0, None, None)
-        total, _ = collect(blocks)
-        sums = [total(0, rows)]
-        backs = [exchange(sums[0])]
+        others = other_halves(kept)
+        total, got = collect(blocks)
+        backs = [exchange(total(0, rows))]
 
     tok_rows, grad_rows, hidden, slope = kept
-    hidden, slope = after(hidden, *sums), after(slope, *sums)
-    got_up = swap(outer(tok_rows, slope, 1, None))
-    got_down = swap(outer(grad_rows, hidden, 1, None))
+    got_up, got_down = [swap(after(x, *got)) for x in others]
     grad_up, grad_down = outer(tok_rows, slope, 0, got_up), outer(grad_rows, hidden, 0, got_down)
     backs[-1] = after(backs[-1], grad_up, grad_down)
     return unplace(shifts, capacity, index, slot, backs), grad_up[None], grad_down[None]

time: 111 us -> 107 us (0.964)
  waiting for transfers between devices: 38.3 us -> 33.5 us
  local copies, waits for them, and re-layouts: 8.67 us -> 4.15 us
  starting transfers between devices: 29.5 us -> 32.8 us
  matrix products: 0 us -> 2.58 us
  Pallas kernels: 32.7 us -> 31.1 us
    ppermute x14, waiting for transfers between devices: 32.6 us -> 17.8 us  [across(): return lax.ppermute(x, 'tensor', [(i, i ^ j) for i in range(tensor_size)])]
    ppermute x6, waiting for transfers between devices: 5.68 us -> 15.7 us  [shift(): lax.ppermute(x, 'expert', [(i, (i + k) % experts) for i in range(experts)])]
    ppermute x6, starting transfers between devices: 10.8 us -> 15.3 us  [shift(): lax.ppermute(x, 'expert', [(i, (i + k) % experts) for i in range(experts)])]
    unnamed x27 -> x19, local copies, waits for them, and re-layouts: 8.59 us -> 4.08 us
    pallas_call x4 -> x2, Pallas kernels: 10.3 us -> 6.24 us  [outer(): pl.pallas_call(outer_kernel, out_shape=jax.ShapeDtypeStruct((half, hid),...]
    dot_general x0 -> x2, matrix products: none -> 2.58 us  [dot(): lax.dot_general(lhs, rhs, (((left,), (right,)), ((), ())), preferred_elem...]
    pallas_call x1, Pallas kernels: 0.46 us -> 2.93 us  [place(): pl.pallas_call(functools.partial(place_kernel, spans, shifts, capacity),...]
    ppermute x14, starting transfers between devices: 17.5 us -> 16.4 us  [across(): return lax.ppermute(x, 'tensor', [(i, i ^ j) for i in range(tensor_size)])]
  transfers between devices with their start and end apart: 24 -> 24, of which waited for: 11 -> 8; matrix products, arithmetic and copies ran while one was open for 0% -> 3% of each run, Pallas kernels for 27% -> 22%
where the time goes in v5:
time: 107 us; the launch traced here: 105 us
  waiting for transfers between devices  33.5 us (31%)
  starting transfers between devices  32.8 us (31%)
  Pallas kernels  31.1 us (29%)
  local copies, waits for them, and re-layouts  4.15 us (4%)
  matrix products  2.58 us (2%)
    pallas_call x3, Pallas kernels, expert_rows(): pl.pallas_call(functools.partial(expert_kernel, own_rows, chunk_rows, bas...  20.8 us
    ppermute x14, waiting for transfers between devices, across(): return lax.ppermute(x, 'tensor', [(i, i ^ j) for i in range(tensor_size)])  17.8 us
    ppermute x14, starting transfers between devices, across(): return lax.ppermute(x, 'tensor', [(i, i ^ j) for i in range(tensor_size)])  16.4 us
    ppermute x6, waiting for transfers between devices, shift(): lax.ppermute(x, 'expert', [(i, (i + k) % experts) for i in range(experts)])  15.7 us
    ppermute x6, starting transfers between devices, shift(): lax.ppermute(x, 'expert', [(i, (i + k) % experts) for i in range(experts)])  15.3 us
    pallas_call x2, Pallas kernels, outer(): pl.pallas_call(outer_kernel, out_shape=jax.ShapeDtypeStruct((half, hid),...  6.24 us
    unnamed x19, local copies, waits for them, and re-layouts  4.08 us
    pallas_call x1, Pallas kernels, place(): pl.pallas_call(functools.partial(place_kernel, spans, shifts, capacity),...  2.93 us
  transfers between devices with their start and end apart: 24, of which 8 were waited for; matrix products, arithmetic and copies ran while one was open for 3% of the time, Pallas kernels for 22%

profile of v5, /device:TPU:0, one launch (start us, length us, event | category | flops | bytes accessed | tf_op | source)
XLA Modules:
  0.0 105.3 jit_solution(6535574473901081784)
XLA Ops:
  1.3 2.9 %place_rows.1 = (bf16[128,1024]{1,0:T(8,128)(2,1)}, bf16[128,1024]{1,0:T(8,128)(2,1)}, bf16[128,1024]{1,0:T(8,128)(2,1)}) custom-call(s32[1,256]{1,0:T(1,128)} %bitcast.17, s32[1,256]{1,0:T(1,128)} %bitcast.20, f32[1,256]{1,0:T(1,128)} %bitcast.23, bf16[256,2048]{1,0:T(8,128)(2,1)} %refs_3_.1, bf16[256,2048]{1,0:T(8,128)(2,1)} %refs_4_.1), custom_call_target="tpu_custom_call" | custom-call | flops 1000 | bytes 1000 | tf_op jit(solution)/shard_map/place_rows/pallas_call | solution.py:63
  4.2 3.1 %collective-permute-start = (bf16[128,1024]{1,0:T(8,128)(2,1)}, bf16[128,1024]{1,0:T(8,128)(2,1)S(1)}, u32[]{:S(2)}, u32[]{:S(2)}) collective-permute-start(bf16[128,1024]{1,0:T(8,128)(2,1)} %get-tuple-element.41), channel_id=1, source_target_pairs={{0,2},{2,4},{4,6},{6,0},{1,3},{3,5},{5,7},{7,1},{8,10},{10,12},{12... | collective-permute-start | bytes 786440 | tf_op jit(solution)/shard_map/ppermute | solution.py:283
  7.3 2.1 %collective-permute-start.3 = (bf16[128,1024]{1,0:T(8,128)(2,1)}, bf16[128,1024]{1,0:T(8,128)(2,1)S(1)}, u32[]{:S(2)}, u32[]{:S(2)}) collective-permute-start(bf16[128,1024]{1,0:T(8,128)(2,1)} %get-tuple-element.44), channel_id=1, source_target_pairs={{0,6},{2,0},{4,2},{6,4},{1,7},{3,1},{5,3},{7,5},{8,14},{10,8},{12,... | collective-permute-start | bytes 786440 | tf_op jit(solution)/shard_map/ppermute | solution.py:283
  9.4 1.6 %copy-done.1 = bf16[1,1024,1024]{2,1,0:T(8,128)(2,1)S(1)} copy-done((bf16[1,1024,1024]{2,1,0:T(8,128)(2,1)S(1)}, bf16[1,1024,1024]{2,1,0:T(8,128)(2,1)}, u32[]{:S(2)}) %copy-start.1) | copy-done | bytes 2097176
  11.0 1.2 %copy-done.3 = bf16[256,2048]{1,0:T(8,128)(2,1)S(1)} copy-done((bf16[256,2048]{1,0:T(8,128)(2,1)S(1)}, bf16[256,2048]{1,0:T(8,128)(2,1)}, u32[]{:S(2)}) %copy-start.3) | copy-done | bytes 1048600
  12.2 1.2 %copy-done.4 = bf16[256,2048]{1,0:T(8,128)(2,1)S(1)} copy-done((bf16[256,2048]{1,0:T(8,128)(2,1)S(1)}, bf16[256,2048]{1,0:T(8,128)(2,1)}, u32[]{:S(2)}) %copy-start.4) | copy-done | bytes 1048600
  13.5 7.0 %expert_rows.3 = (bf16[512,2048]{1,0:T(8,128)(2,1)S(1)}, bf16[512,2048]{1,0:T(8,128)(2,1)S(1)}, bf16[512,1024]{1,0:T(8,128)(2,1)S(1)}, bf16[512,1024]{1,0:T(8,12...) custom-call(s32[1,256]{1,0:T(1,128)S(1)} %bitcast.18, ...), custom_call_target="tpu_custom_call" | custom-call | flops 1610612736 | bytes 10485760 | tf_op jit(solution)/shard_map/expert_rows/pallas_call | solution.py:198
  21.1 1.6 %collective-permute-start.6 = (bf16[256,1024]{1,0:T(8,128)(2,1)S(1)}, bf16[256,1024]{1,0:T(8,128)(2,1)S(1)}, u32[]{:S(2)}, u32[]{:S(2)}) collective-permute-start(bf16[256,1024]{1,0:T(8,128)(2,1)S(1)} %constant_dynamic-update-slice_fusion.refs_0_), channel_id=1, source_target_pairs={{0,16},{8,24},{16,0},{24,8},{1,17},{9,25},{17,1},{25,9},{2,18},{10... | collective-permute-start | bytes 1572872 | tf_op jit(solution)/shard_map/ppermute | solution.py:280
  22.7 1.5 %collective-permute-start.5 = (bf16[256,1024]{1,0:T(8,128)(2,1)S(1)}, bf16[256,1024]{1,0:T(8,128)(2,1)S(1)}, u32[]{:S(2)}, u32[]{:S(2)}) collective-permute-start(bf16[256,1024]{1,0:T(8,128)(2,1)S(1)} %constant_dynamic-update-slice_fusion.refs_0_), channel_id=1, source_target_pairs={{0,8},{8,0},{16,24},{24,16},{1,9},{9,1},{17,25},{25,17},{2,10},{10... | collective-permute-start | bytes 1572872 | tf_op jit(solution)/shard_map/ppermute | solution.py:280
  24.2 2.2 %collective-permute-start.4 = (bf16[128,1024]{1,0:T(8,128)(2,1)S(1)}, bf16[128,1024]{1,0:T(8,128)(2,1)S(1)}, u32[]{:S(2)}, u32[]{:S(2)}) collective-permute-start(bf16[128,1024]{1,0:T(8,128)(2,1)S(1)} %copy-done.8), channel_id=1, source_target_pairs={{0,4},{2,6},{4,0},{6,2},{1,5},{3,7},{5,1},{7,3},{8,12},{10,14},{12... | collective-permute-start | bytes 786440 | tf_op jit(solution)/shard_map/ppermute | solution.py:283
  26.4 11.8 %collective-permute-done.4.refs_0_ = bf16[128,1024]{1,0:T(8,128)(2,1)S(1)} collective-permute-done((bf16[128,1024]{1,0:T(8,128)(2,1)S(1)}, bf16[128,1024]{1,0:T(8,128)(2,1)S(1)}, u32[]{:S(2)}, u32[]{:S(2)}) %collective-permute-start.4) | collective-permute-done | bytes 262176 | tf_op jit(solution)/shard_map/ppermute | solution.py:283
  39.2 1.6 %collective-permute-start.11 = (bf16[256,512]{1,0:T(8,128)(2,1)S(1)}, bf16[256,512]{1,0:T(8,128)(2,1)S(1)}, u32[]{:S(2)}, u32[]{:S(2)}) collective-permute-start(bf16[256,512]{1,0:T(8,128)(2,1)S(1)} %slice.74), channel_id=1, source_target_pairs={{0,8},{8,0},{16,24},{24,16},{1,9},{9,1},{17,25},{25,17},{2,10},{10... | collective-permute-start | bytes 786440 | tf_op jit(solution)/shard_map/ppermute | solution.py:280
  40.8 1.6 %collective-permute-start.12 = (bf16[256,512]{1,0:T(8,128)(2,1)S(1)}, bf16[256,512]{1,0:T(8,128)(2,1)S(1)}, u32[]{:S(2)}, u32[]{:S(2)}) collective-permute-start(bf16[256,512]{1,0:T(8,128)(2,1)S(1)} %slice.75), channel_id=1, source_target_pairs={{0,16},{8,24},{16,0},{24,8},{1,17},{9,25},{17,1},{25,9},{2,18},{10... | collective-permute-start | bytes 786440 | tf_op jit(solution)/shard_map/ppermute | solution.py:280
  42.4 5.0 %collective-permute-done.9.refs_1_ = bf16[128,1024]{1,0:T(8,128)(2,1)S(1)} collective-permute-done((bf16[128,1024]{1,0:T(8,128)(2,1)S(1)}, bf16[128,1024]{1,0:T(8,128)(2,1)S(1)}, u32[]{:S(2)}, u32[]{:S(2)}) %collective-permute-start.9) | collective-permute-done | bytes 262176 | tf_op jit(solution)/shard_map/ppermute | solution.py:280
  48.0 1.5 %collective-permute-start.8 = (bf16[128,512]{1,0:T(8,128)(2,1)S(1)}, bf16[128,512]{1,0:T(8,128)(2,1)S(1)}, u32[]{:S(2)}, u32[]{:S(2)}) collective-permute-start(bf16[128,512]{1,0:T(8,128)(2,1)S(1)} %slice.72), channel_id=1, source_target_pairs={{0,8},{8,0},{16,24},{24,16},{1,9},{9,1},{17,25},{25,17},{2,10},{10... | collective-permute-start | bytes 393224 | tf_op jit(solution)/shard_map/ppermute | solution.py:280
  49.5 4.5 %collective-permute-done.10.refs_4_ = bf16[128,512]{1,0:T(8,128)(2,1)S(1)} collective-permute-done((bf16[128,512]{1,0:T(8,128)(2,1)S(1)}, bf16[128,512]{1,0:T(8,128)(2,1)S(1)}, u32[]{:S(2)}, u32[]{:S(2)}) %collective-permute-start.10) | collective-permute-done | bytes 131104 | tf_op jit(solution)/shard_map/ppermute | solution.py:280
  54.0 7.1 %expert_rows.4 = (bf16[512,2048]{1,0:T(8,128)(2,1)S(1)}, bf16[512,2048]{1,0:T(8,128)(2,1)S(1)}, bf16[512,1024]{1,0:T(8,128)(2,1)S(1)}, bf16[512,1024]{1,0:T(8,12...) custom-call(bf16[256,1024]{1,0:T(8,128)(2,1)S(1)} %constant_dynamic-, ...), custom_call_target="tpu_custom_call", output_to_operand_aliasing={{0}: (9, {}), {1}: (10, {}), {2}: (11, {}), {3}: (12, {}), ... | custom-call | flops 3221225472 | bytes 12582912 | tf_op jit(solution)/shard_map/expert_rows/pallas_call | solution.py:198
  61.1 1.6 %collective-permute-start.13 = (bf16[384,512]{1,0:T(8,128)(2,1)S(1)}, bf16[384,512]{1,0:T(8,128)(2,1)S(1)}, u32[]{:S(2)}, u32[]{:S(2)}) collective-permute-start(bf16[384,512]{1,0:T(8,128)(2,1)S(1)} %get-tuple-element.57), channel_id=1, source_target_pairs={{0,8},{8,0},{16,24},{24,16},{1,9},{9,1},{17,25},{25,17},{2,10},{10... | collective-permute-start | bytes 1179656 | tf_op jit(solution)/shard_map/ppermute | solution.py:280
  63.2 1.5 %collective-permute-start.15 = (bf16[384,512]{1,0:T(8,128)(2,1)S(1)}, bf16[384,512]{1,0:T(8,128)(2,1)S(1)}, u32[]{:S(2)}, u32[]{:S(2)}) collective-permute-start(bf16[384,512]{1,0:T(8,128)(2,1)S(1)} %get-tuple-element.59), channel_id=1, source_target_pairs={{0,24},{8,16},{16,8},{24,0},{1,25},{9,17},{17,9},{25,1},{2,26},{10... | collective-permute-start | bytes 1179656 | tf_op jit(solution)/shard_map/ppermute | solution.py:280
  64.7 6.7 %expert_rows.5 = (bf16[512,2048]{1,0:T(8,128)(2,1)S(1)}, bf16[512,2048]{1,0:T(8,128)(2,1)S(1)}, bf16[512,1024]{1,0:T(8,128)(2,1)S(1)}, bf16[512,1024]{1,0:T(8,12...) custom-call(bf16[128,1024]{1,0:T(8,128)(2,1)S(1)} %collective-permut, ...), custom_call_target="tpu_custom_call", output_to_operand_aliasing={{0}: (9, {}), {1}: (10, {}), {2}: (11, {}), {3}: (12, {})} | custom-call | flops 1610612736 | bytes 10485760 | tf_op jit(solution)/shard_map/expert_rows/pallas_call | solution.py:198
  71.4 1.3 %convolution_convert_fusion.1 = bf16[1024,1024]{1,0:T(8,128)(2,1)S(1)} fusion(bf16[512,1024]{1,0:T(8,128)(2,1)S(1)} %get-tuple-element.67.out, bf16[512,2048]{1,0:T(8,128)(2,1)S(1)} %get-tuple-element.66.rows), kind=kOutput, calls=%fused_computation.1 | convolution fusion | flops 1074790400 | bytes 4194304 | tf_op jit(solution)/shard_map/dot_general | solution.py:22
  72.7 1.3 %convolution_convert_fusion = bf16[1024,1024]{1,0:T(8,128)(2,1)S(1)} fusion(bf16[512,1024]{1,0:T(8,128)(2,1)S(1)} %get-tuple-element.69.out, bf16[512,2048]{1,0:T(8,128)(2,1)S(1)} %get-tuple-element.68.rows), kind=kOutput, calls=%fused_computation | convolution fusion | flops 1074790400 | bytes 4194304 | tf_op jit(solution)/shard_map/dot_general | solution.py:22
  74.0 5.6 %collective-permute-done.14 = bf16[384,512]{1,0:T(8,128)(2,1)S(1)} collective-permute-done((bf16[384,512]{1,0:T(8,128)(2,1)S(1)}, bf16[384,512]{1,0:T(8,128)(2,1)S(1)}, u32[]{:S(2)}, u32[]{:S(2)}) %collective-permute-start.14) | collective-permute-done | bytes 393248 | tf_op jit(solution)/shard_map/ppermute | solution.py:280
  80.7 1.2 %collective-permute-start.19 = (bf16[128,512]{1,0:T(8,128)(2,1)S(1)}, bf16[128,512]{1,0:T(8,128)(2,1)S(1)}, u32[]{:S(2)}, u32[]{:S(2)}) collective-permute-start(bf16[128,512]{1,0:T(8,128)(2,1)S(1)} %get-tuple-element.72), channel_id=1, source_target_pairs={{0,16},{8,24},{16,0},{24,8},{1,17},{9,25},{17,1},{25,9},{2,18},{10... | collective-permute-start | bytes 393224 | tf_op jit(solution)/shard_map/ppermute | solution.py:280
  81.9 1.8 %collective-permute-start.20 = (bf16[128,512]{1,0:T(8,128)(2,1)S(1)}, bf16[128,512]{1,0:T(8,128)(2,1)S(1)}, u32[]{:S(2)}, u32[]{:S(2)}) collective-permute-start(bf16[128,512]{1,0:T(8,128)(2,1)S(1)} %get-tuple-element.74), channel_id=1, source_target_pairs={{0,24},{8,16},{16,8},{24,0},{1,25},{9,17},{17,9},{25,1},{2,26},{10... | collective-permute-start | bytes 393224 | tf_op jit(solution)/shard_map/ppermute | solution.py:280
  83.8 2.7 %collective-permute-done.18 = bf16[128,512]{1,0:T(8,128)(2,1)S(1)} collective-permute-done((bf16[128,512]{1,0:T(8,128)(2,1)S(1)}, bf16[128,512]{1,0:T(8,128)(2,1)S(1)}, u32[]{:S(2)}, u32[]{:S(2)}) %collective-permute-start.18) | collective-permute-done | bytes 131104 | tf_op jit(solution)/shard_map/ppermute | solution.py:280
  86.5 2.9 %collective-permute-start.17 = (bf16[128,512]{1,0:T(8,128)(2,1)S(1)}, bf16[128,512]{1,0:T(8,128)(2,1)S(1)}, u32[]{:S(2)}, u32[]{:S(2)}) collective-permute-start(bf16[128,512]{1,0:T(8,128)(2,1)S(1)} %get-tuple-element.79), channel_id=1, source_target_pairs={{0,2},{2,4},{4,6},{6,0},{1,3},{3,5},{5,7},{7,1},{8,10},{10,12},{12... | collective-permute-start | bytes 393224 | tf_op jit(solution)/shard_map/ppermute | solution.py:283
  89.4 5.0 %collective-permute-start.16 = (bf16[128,512]{1,0:T(8,128)(2,1)S(1)}, bf16[128,512]{1,0:T(8,128)(2,1)S(1)}, u32[]{:S(2)}, u32[]{:S(2)}) collective-permute-start(bf16[128,512]{1,0:T(8,128)(2,1)S(1)} %get-tuple-element.80), channel_id=1, source_target_pairs={{0,6},{2,0},{4,2},{6,4},{1,7},{3,1},{5,3},{7,5},{8,14},{10,8},{12,... | collective-permute-start | bytes 393224 | tf_op jit(solution)/shard_map/ppermute | solution.py:283
  94.4 1.2 %collective-permute-done.17.refs_2_ = bf16[128,512]{1,0:T(8,128)(2,1)S(1)} collective-permute-done((bf16[128,512]{1,0:T(8,128)(2,1)S(1)}, bf16[128,512]{1,0:T(8,128)(2,1)S(1)}, u32[]{:S(2)}, u32[]{:S(2)}) %collective-permute-start.17) | collective-permute-done | bytes 131104 | tf_op jit(solution)/shard_map/ppermute | solution.py:283
  95.6 2.1 %collective-permute-done.16.refs_1_ = bf16[128,512]{1,0:T(8,128)(2,1)S(1)} collective-permute-done((bf16[128,512]{1,0:T(8,128)(2,1)S(1)}, bf16[128,512]{1,0:T(8,128)(2,1)S(1)}, u32[]{:S(2)}, u32[]{:S(2)}) %collective-permute-start.16) | collective-permute-done | bytes 131104 | tf_op jit(solution)/shard_map/ppermute | solution.py:283
  97.8 3.1 %weight_grad.3 = bf16[1024,1024]{1,0:T(8,128)(2,1)} custom-call(bf16[512,2048]{1,0:T(8,128)(2,1)S(1)} %get-tuple-element.68.rows, bf16[512,1024]{1,0:T(8,128)(2,1)S(1)} %get-tuple-element.69.out, bf16[1024,1024]{1,0:T(8,128)(2,1)S(1)} %collective-permute-done.23.refs_0_), custom_call_target="tpu_custom_call" | custom-call | flops 1000 | bytes 1000 | tf_op jit(solution)/shard_map/weight_grad/pallas_call | solution.py:253
  101.0 3.1 %weight_grad.2 = bf16[1024,1024]{1,0:T(8,128)(2,1)} custom-call(bf16[512,2048]{1,0:T(8,128)(2,1)S(1)} %get-tuple-element.66.rows, bf16[512,1024]{1,0:T(8,128)(2,1)S(1)} %get-tuple-element.67.out, bf16[1024,1024]{1,0:T(8,128)(2,1)S(1)} %collective-permute-done.22.refs_0_), custom_call_target="tpu_custom_call" | custom-call | flops 1000 | bytes 1000 | tf_op jit(solution)/shard_map/weight_grad/pallas_call | solution.py:253
  (51 shorter events, 6.0 us)
Async XLA Ops:
  0.6 8.7 %copy-start = (bf16[1,1024,1024]{2,1,0:T(8,128)(2,1)S(1)}, bf16[1,1024,1024]{2,1,0:T(8,128)(2,1)}, u32[]{:S(2)}) copy-start(bf16[1,1024,1024]{2,1,0:T(8,128)(2,1)} %param.12) | copy-start | bytes 6291460
  0.6 8.7 %copy-start.6 = (s32[256,1]{0,1:T(1,128)S(1)}, s32[256,1]{0,1:T(1,128)}, u32[]{:S(2)}) copy-start(s32[256,1]{0,1:T(1,128)} %param.11) | copy-start | bytes 3076
  0.7 8.7 %copy-start.5 = (s32[256,1]{0,1:T(1,128)S(1)}, s32[256,1]{0,1:T(1,128)}, u32[]{:S(2)}) copy-start(s32[256,1]{0,1:T(1,128)} %param.10) | copy-start | bytes 3076
  0.7 8.7 %copy-start.7 = (f32[256]{0:T(256)S(1)}, f32[256]{0:T(256)}, u32[]{:S(2)}) copy-start(f32[256]{0:T(256)} %param.9) | copy-start | bytes 3076
  0.7 8.7 %collective-permute-start.1 = (bf16[1024,1024]{1,0:T(8,128)(2,1)}, bf16[1024,1024]{1,0:T(8,128)(2,1)S(1)}, u32[]{:S(2)}, u32[]{:S(2)}) collective-permute-start(bf16[1024,1024]{1,0:T(8,128)(2,1)} %bitcast.9), channel_id=1, source_target_pairs={{0,1},{1,0},{2,3},{3,2},{4,5},{5,4},{6,7},{7,6},{8,9},{9,8},{10,11... | collective-permute-start | bytes 6291464 | tf_op jit(solution)/shard_map/ppermute | solution.py:277
  1.2 8.2 %collective-permute-start.2 = (bf16[1024,1024]{1,0:T(8,128)(2,1)}, bf16[1024,1024]{1,0:T(8,128)(2,1)S(1)}, u32[]{:S(2)}, u32[]{:S(2)}) collective-permute-start(bf16[1024,1024]{1,0:T(8,128)(2,1)} %bitcast.13), channel_id=1, source_target_pairs={{0,1},{1,0},{2,3},{3,2},{4,5},{5,4},{6,7},{7,6},{8,9},{9,8},{10,11... | collective-permute-start | bytes 6291464 | tf_op jit(solution)/shard_map/ppermute | solution.py:277
  4.2 16.3 %collective-permute-start = (bf16[128,1024]{1,0:T(8,128)(2,1)}, bf16[128,1024]{1,0:T(8,128)(2,1)S(1)}, u32[]{:S(2)}, u32[]{:S(2)}) collective-permute-start(bf16[128,1024]{1,0:T(8,128)(2,1)} %get-tuple-element.41), channel_id=1, source_target_pairs={{0,2},{2,4},{4,6},{6,0},{1,3},{3,5},{5,7},{7,1},{8,10},{10,12},{12... | collective-permute-start | bytes 786440 | tf_op jit(solution)/shard_map/ppermute | solution.py:283
  7.3 13.8 %collective-permute-start.3 = (bf16[128,1024]{1,0:T(8,128)(2,1)}, bf16[128,1024]{1,0:T(8,128)(2,1)S(1)}, u32[]{:S(2)}, u32[]{:S(2)}) collective-permute-start(bf16[128,1024]{1,0:T(8,128)(2,1)} %get-tuple-element.44), channel_id=1, source_target_pairs={{0,6},{2,0},{4,2},{6,4},{1,7},{3,1},{5,3},{7,5},{8,14},{10,8},{12,... | collective-permute-start | bytes 786440 | tf_op jit(solution)/shard_map/ppermute | solution.py:283
  9.4 1.6 %copy-start.1 = (bf16[1,1024,1024]{2,1,0:T(8,128)(2,1)S(1)}, bf16[1,1024,1024]{2,1,0:T(8,128)(2,1)}, u32[]{:S(2)}) copy-start(bf16[1,1024,1024]{2,1,0:T(8,128)(2,1)} %param.13) | copy-start | bytes 6291460
  11.0 1.2 %copy-start.3 = (bf16[256,2048]{1,0:T(8,128)(2,1)S(1)}, bf16[256,2048]{1,0:T(8,128)(2,1)}, u32[]{:S(2)}) copy-start(bf16[256,2048]{1,0:T(8,128)(2,1)} %refs_3_.1) | copy-start | bytes 3145732
  13.5 10.7 %copy-start.8 = (bf16[128,1024]{1,0:T(8,128)(2,1)S(1)}, bf16[128,1024]{1,0:T(8,128)(2,1)}, u32[]{:S(2)}) copy-start(bf16[128,1024]{1,0:T(8,128)(2,1)} %get-tuple-element.46) | copy-start | bytes 786436
  20.5 33.6 %copy-start.2 = (bf16[1,1024,1024]{2,1,0:T(8,128)(2,1)S(1)}, bf16[1,1024,1024]{2,1,0:T(8,128)(2,1)}, u32[]{:S(2)}) copy-start(bf16[1,1024,1024]{2,1,0:T(8,128)(2,1)} %param.13) | copy-start | bytes 6291460
  21.1 17.1 %collective-permute-start.6 = (bf16[256,1024]{1,0:T(8,128)(2,1)S(1)}, bf16[256,1024]{1,0:T(8,128)(2,1)S(1)}, u32[]{:S(2)}, u32[]{:S(2)}) collective-permute-start(bf16[256,1024]{1,0:T(8,128)(2,1)S(1)} %constant_dynamic-update-slice_fusion.refs_0_), channel_id=1, source_target_pairs={{0,16},{8,24},{16,0},{24,8},{1,17},{9,25},{17,1},{25,9},{2,18},{10... | collective-permute-start | bytes 1572872 | tf_op jit(solution)/shard_map/ppermute | solution.py:280
  22.7 15.5 %collective-permute-start.5 = (bf16[256,1024]{1,0:T(8,128)(2,1)S(1)}, bf16[256,1024]{1,0:T(8,128)(2,1)S(1)}, u32[]{:S(2)}, u32[]{:S(2)}) collective-permute-start(bf16[256,1024]{1,0:T(8,128)(2,1)S(1)} %constant_dynamic-update-slice_fusion.refs_0_), channel_id=1, source_target_pairs={{0,8},{8,0},{16,24},{24,16},{1,9},{9,1},{17,25},{25,17},{2,10},{10... | collective-permute-start | bytes 1572872 | tf_op jit(solution)/shard_map/ppermute | solution.py:280
  24.2 14.0 %collective-permute-start.4 = (bf16[128,1024]{1,0:T(8,128)(2,1)S(1)}, bf16[128,1024]{1,0:T(8,128)(2,1)S(1)}, u32[]{:S(2)}, u32[]{:S(2)}) collective-permute-start(bf16[128,1024]{1,0:T(8,128)(2,1)S(1)} %copy-done.8), channel_id=1, source_target_pairs={{0,4},{2,6},{4,0},{6,2},{1,5},{3,7},{5,1},{7,3},{8,12},{10,14},{12... | collective-permute-start | bytes 786440 | tf_op jit(solution)/shard_map/ppermute | solution.py:283
  38.2 9.2 %collective-permute-start.9 = (bf16[128,1024]{1,0:T(8,128)(2,1)S(1)}, bf16[128,1024]{1,0:T(8,128)(2,1)S(1)}, u32[]{:S(2)}, u32[]{:S(2)}) collective-permute-start(bf16[128,1024]{1,0:T(8,128)(2,1)S(1)} %collective-permute-done.4.refs_0_), channel_id=1, source_target_pairs={{0,8},{8,0},{16,24},{24,16},{1,9},{9,1},{17,25},{25,17},{2,10},{10... | collective-permute-start | bytes 786440 | tf_op jit(solution)/shard_map/ppermute | solution.py:280
  38.7 9.3 %collective-permute-start.7 = (bf16[128,1024]{1,0:T(8,128)(2,1)S(1)}, bf16[128,1024]{1,0:T(8,128)(2,1)S(1)}, u32[]{:S(2)}, u32[]{:S(2)}) collective-permute-start(bf16[128,1024]{1,0:T(8,128)(2,1)S(1)} %collective-permute-done.4.refs_0_), channel_id=1, source_target_pairs={{0,16},{8,24},{16,0},{24,8},{1,17},{9,25},{17,1},{25,9},{2,18},{10... | collective-permute-start | bytes 786440 | tf_op jit(solution)/shard_map/ppermute | solution.py:280
  39.2 14.8 %collective-permute-start.11 = (bf16[256,512]{1,0:T(8,128)(2,1)S(1)}, bf16[256,512]{1,0:T(8,128)(2,1)S(1)}, u32[]{:S(2)}, u32[]{:S(2)}) collective-permute-start(bf16[256,512]{1,0:T(8,128)(2,1)S(1)} %slice.74), channel_id=1, source_target_pairs={{0,8},{8,0},{16,24},{24,16},{1,9},{9,1},{17,25},{25,17},{2,10},{10... | collective-permute-start | bytes 786440 | tf_op jit(solution)/shard_map/ppermute | solution.py:280
  40.8 13.2 %collective-permute-start.12 = (bf16[256,512]{1,0:T(8,128)(2,1)S(1)}, bf16[256,512]{1,0:T(8,128)(2,1)S(1)}, u32[]{:S(2)}, u32[]{:S(2)}) collective-permute-start(bf16[256,512]{1,0:T(8,128)(2,1)S(1)} %slice.75), channel_id=1, source_target_pairs={{0,16},{8,24},{16,0},{24,8},{1,17},{9,25},{17,1},{25,9},{2,18},{10... | collective-permute-start | bytes 786440 | tf_op jit(solution)/shard_map/ppermute | solution.py:280
  47.4 6.6 %collective-permute-start.10 = (bf16[128,512]{1,0:T(8,128)(2,1)S(1)}, bf16[128,512]{1,0:T(8,128)(2,1)S(1)}, u32[]{:S(2)}, u32[]{:S(2)}) collective-permute-start(bf16[128,512]{1,0:T(8,128)(2,1)S(1)} %slice.73), channel_id=1, source_target_pairs={{0,16},{8,24},{16,0},{24,8},{1,17},{9,25},{17,1},{25,9},{2,18},{10... | collective-permute-start | bytes 393224 | tf_op jit(solution)/shard_map/ppermute | solution.py:280
  48.0 6.0 %collective-permute-start.8 = (bf16[128,512]{1,0:T(8,128)(2,1)S(1)}, bf16[128,512]{1,0:T(8,128)(2,1)S(1)}, u32[]{:S(2)}, u32[]{:S(2)}) collective-permute-start(bf16[128,512]{1,0:T(8,128)(2,1)S(1)} %slice.72), channel_id=1, source_target_pairs={{0,8},{8,0},{16,24},{24,16},{1,9},{9,1},{17,25},{25,17},{2,10},{10... | collective-permute-start | bytes 393224 | tf_op jit(solution)/shard_map/ppermute | solution.py:280
  61.1 12.8 %collective-permute-start.13 = (bf16[384,512]{1,0:T(8,128)(2,1)S(1)}, bf16[384,512]{1,0:T(8,128)(2,1)S(1)}, u32[]{:S(2)}, u32[]{:S(2)}) collective-permute-start(bf16[384,512]{1,0:T(8,128)(2,1)S(1)} %get-tuple-element.57), channel_id=1, source_target_pairs={{0,8},{8,0},{16,24},{24,16},{1,9},{9,1},{17,25},{25,17},{2,10},{10... | collective-permute-start | bytes 1179656 | tf_op jit(solution)/shard_map/ppermute | solution.py:280
  62.7 16.9 %collective-permute-start.14 = (bf16[384,512]{1,0:T(8,128)(2,1)S(1)}, bf16[384,512]{1,0:T(8,128)(2,1)S(1)}, u32[]{:S(2)}, u32[]{:S(2)}) collective-permute-start(bf16[384,512]{1,0:T(8,128)(2,1)S(1)} %get-tuple-element.58), channel_id=1, source_target_pairs={{0,16},{8,24},{16,0},{24,8},{1,17},{9,25},{17,1},{25,9},{2,18},{10... | collective-permute-start | bytes 1179656 | tf_op jit(solution)/shard_map/ppermute | solution.py:280
  63.2 16.4 %collective-permute-start.15 = (bf16[384,512]{1,0:T(8,128)(2,1)S(1)}, bf16[384,512]{1,0:T(8,128)(2,1)S(1)}, u32[]{:S(2)}, u32[]{:S(2)}) collective-permute-start(bf16[384,512]{1,0:T(8,128)(2,1)S(1)} %get-tuple-element.59), channel_id=1, source_target_pairs={{0,24},{8,16},{16,8},{24,0},{1,25},{9,17},{17,9},{25,1},{2,26},{10... | collective-permute-start | bytes 1179656 | tf_op jit(solution)/shard_map/ppermute | solution.py:280
  79.6 18.2 %collective-permute-start.23 = (bf16[1024,1024]{1,0:T(8,128)(2,1)S(1)}, bf16[1024,1024]{1,0:T(8,128)(2,1)S(1)}, u32[]{:S(2)}, u32[]{:S(2)}) collective-permute-start(bf16[1024,1024]{1,0:T(8,128)(2,1)S(1)} %convolution_convert_fusion), channel_id=1, source_target_pairs={{0,1},{1,0},{2,3},{3,2},{4,5},{5,4},{6,7},{7,6},{8,9},{9,8},{10,11... | collective-permute-start | bytes 6291464 | tf_op jit(solution)/shard_map/ppermute | solution.py:277
  79.6 21.4 %collective-permute-start.22 = (bf16[1024,1024]{1,0:T(8,128)(2,1)S(1)}, bf16[1024,1024]{1,0:T(8,128)(2,1)S(1)}, u32[]{:S(2)}, u32[]{:S(2)}) collective-permute-start(bf16[1024,1024]{1,0:T(8,128)(2,1)S(1)} %convolution_convert_fusion.1), channel_id=1, source_target_pairs={{0,1},{1,0},{2,3},{3,2},{4,5},{5,4},{6,7},{7,6},{8,9},{9,8},{10,11... | collective-permute-start | bytes 6291464 | tf_op jit(solution)/shard_map/ppermute | solution.py:277
  80.1 6.4 %collective-permute-start.18 = (bf16[128,512]{1,0:T(8,128)(2,1)S(1)}, bf16[128,512]{1,0:T(8,128)(2,1)S(1)}, u32[]{:S(2)}, u32[]{:S(2)}) collective-permute-start(bf16[128,512]{1,0:T(8,128)(2,1)S(1)} %get-tuple-element.70), channel_id=1, source_target_pairs={{0,8},{8,0},{16,24},{24,16},{1,9},{9,1},{17,25},{25,17},{2,10},{10... | collective-permute-start | bytes 393224 | tf_op jit(solution)/shard_map/ppermute | solution.py:280
  80.7 8.7 %collective-permute-start.19 = (bf16[128,512]{1,0:T(8,128)(2,1)S(1)}, bf16[128,512]{1,0:T(8,128)(2,1)S(1)}, u32[]{:S(2)}, u32[]{:S(2)}) collective-permute-start(bf16[128,512]{1,0:T(8,128)(2,1)S(1)} %get-tuple-element.72), channel_id=1, source_target_pairs={{0,16},{8,24},{16,0},{24,8},{1,17},{9,25},{17,1},{25,9},{2,18},{10... | collective-permute-start | bytes 393224 | tf_op jit(solution)/shard_map/ppermute | solution.py:280
  81.9 12.5 %collective-permute-start.20 = (bf16[128,512]{1,0:T(8,128)(2,1)S(1)}, bf16[128,512]{1,0:T(8,128)(2,1)S(1)}, u32[]{:S(2)}, u32[]{:S(2)}) collective-permute-start(bf16[128,512]{1,0:T(8,128)(2,1)S(1)} %get-tuple-element.74), channel_id=1, source_target_pairs={{0,24},{8,16},{16,8},{24,0},{1,25},{9,17},{17,9},{25,1},{2,26},{10... | collective-permute-start | bytes 393224 | tf_op jit(solution)/shard_map/ppermute | solution.py:280
  86.5 9.1 %collective-permute-start.17 = (bf16[128,512]{1,0:T(8,128)(2,1)S(1)}, bf16[128,512]{1,0:T(8,128)(2,1)S(1)}, u32[]{:S(2)}, u32[]{:S(2)}) collective-permute-start(bf16[128,512]{1,0:T(8,128)(2,1)S(1)} %get-tuple-element.79), channel_id=1, source_target_pairs={{0,2},{2,4},{4,6},{6,0},{1,3},{3,5},{5,7},{7,1},{8,10},{10,12},{12... | collective-permute-start | bytes 393224 | tf_op jit(solution)/shard_map/ppermute | solution.py:283
  89.4 8.4 %collective-permute-start.16 = (bf16[128,512]{1,0:T(8,128)(2,1)S(1)}, bf16[128,512]{1,0:T(8,128)(2,1)S(1)}, u32[]{:S(2)}, u32[]{:S(2)}) collective-permute-start(bf16[128,512]{1,0:T(8,128)(2,1)S(1)} %get-tuple-element.80), channel_id=1, source_target_pairs={{0,6},{2,0},{4,2},{6,4},{1,7},{3,1},{5,3},{7,5},{8,14},{10,8},{12,... | collective-permute-start | bytes 393224 | tf_op jit(solution)/shard_map/ppermute | solution.py:283
  97.7 6.4 %collective-permute-start.21 = (bf16[128,512]{1,0:T(8,128)(2,1)S(1)}, bf16[128,512]{1,0:T(8,128)(2,1)S(1)}, u32[]{:S(2)}, u32[]{:S(2)}) collective-permute-start(bf16[128,512]{1,0:T(8,128)(2,1)S(1)} %add_convert_fusion), channel_id=1, source_target_pairs={{0,4},{2,6},{4,0},{6,2},{1,5},{3,7},{5,1},{7,3},{8,12},{10,14},{12... | collective-permute-start | bytes 393224 | tf_op jit(solution)/shard_map/ppermute | solution.py:283
  (1 other events, 1.2 us)

commit v6 on v5

--- a/solution.py
+++ b/solution.py
@@ -74,6 +74,40 @@
     )(index, slot, gate, tokens, grad_output)
 
 
+def place_own_kernel(capacity, index, slot, gate, tokens, grad_output, tok, grad, tok_in, grad_in, sem):
+    half = tok.shape[1] // 2
+    mine = lax.axis_index("dp")
+    waits = []
+    for k, (src, dst) in enumerate(((tokens, tok_in), (grad_output, grad_in))):
+        for i, start in enumerate((mine * half, (1 - mine) * half)):
+            source = src.at[:, pl.ds(pl.multiple_of(start, half), half)]
+            waits.append(pltpu.make_async_copy(source, dst.at[:, pl.ds(i * half, half)], sem.at[2 * k + i]))
+            waits[-1].start()
+    hit = hits(places(index, slot, capacity), expert_first(0, capacity), capacity)
+    hot = hit.astype(BF16)
+    scale = gate_of(hit, gate[...])
+    for w in waits:
+        w.wait()
+    tok[...] = dot(hot, tok_in[...]).astype(BF16)
+    grad[...] = (dot(hot, grad_in[...]) * scale).astype(BF16)
+
+
+def place_own(capacity, index, slot, gate, tokens, grad_output):
+    count, width = tokens.shape
+    return pl.pallas_call(
+        functools.partial(place_own_kernel, capacity),
+        out_shape=[jax.ShapeDtypeStruct((capacity, width), BF16)] * 2,
+        in_specs=[VMEM, VMEM, VMEM, HBM, HBM],
+        out_specs=[VMEM] * 2,
+        scratch_shapes=[
+            pltpu.VMEM((count, width), BF16), pltpu.VMEM((count, width), BF16), pltpu.SemaphoreType.DMA((4,))
+        ],
+        compiler_params=pltpu.CompilerParams(vmem_limit_bytes=54 * 2**20),
+        cost_estimate=SMALL,
+        name="place_own_rows",
+    )(index, slot, gate, tokens, grad_output)
+
+
 def gelu_parts(pre):
     c = 0.7978845608028654
     square = pre * pre
@@ -86,15 +120,13 @@
     refs = list(refs)
     take = lambda n: [refs.pop(0) for _ in range(n)]
     if own_rows:
-        index, slot, gate, tokens, grad_output = take(5)
+        tok_own, grad_own = take(2)
     chunks = [take(5) for _ in chunk_rows]
     up_halves, down_halves = take(2), take(2)
     take(aliased)
     tok_out, grad_out, hidden_out, slope_out = take(4)
     blocks = take(4)
     tok, grad, up, down, hidden, slope, back = take(7)
-    if own_rows:
-        tokens_in, grad_in = take(2)
     (sem,) = take(1)
     rows, width = tok.shape
     half, share = width // 2, width // 4
@@ -110,10 +142,8 @@
 
     waits = []
     if own_rows:
-        for src, dst in ((tokens, tokens_in), (grad_output, grad_in)):
-            for start, place_at in ((mine * half, 0), ((1 - mine) * half, half)):
-                start = pl.multiple_of(start, half)
-                waits.append(copy(src.at[:, pl.ds(start, half)], dst.at[:, pl.ds(place_at, half)]))
+        waits.append(copy(tok_own, tok.at[pl.ds(0, own_rows), :]))
+        waits.append(copy(grad_own, grad.at[pl.ds(0, own_rows), :]))
     at = own_rows
     for (z, x, y, tok_d, grad_d), n in zip(chunks, chunk_rows):
         tok_slots = [r.at[:, pl.ds(0, share)] for r in (z, x, y)] + [tok_d]
@@ -132,15 +162,8 @@
         for halves, dst in ((up_halves, up), (down_halves, down)):
             for i in range(2):
                 tiles[-1].append(copy(halves[i].at[:, cols], dst.at[pl.ds(i * half, half), cols]))
-    if own_rows:
-        hit = hits(places(index, slot, own_rows), expert_first(0, own_rows), own_rows)
-        hot = hit.astype(BF16)
-        scale = gate_of(hit, gate[...])
     for w in waits:
         w.wait()
-    if own_rows:
-        tok[:own_rows, :] = dot(hot, tokens_in[...]).astype(BF16)
-        grad[:own_rows, :] = (dot(hot, grad_in[...]) * scale).astype(BF16)
     outs = [copy(tok, tok_out.at[pl.ds(base, rows), :]), copy(grad, grad_out.at[pl.ds(base, rows), :])]
     for n, arrived in zip(range(0, hid, step), tiles):
         cols = slice(n, n + step)
@@ -162,7 +185,7 @@
 
 
 def expert_rows(own, chunks, weights, total_rows, base, block_rows, block_base, kept, blocks):
-    own_rows = own[0] if own else 0
+    own_rows = own[0].shape[0] if own else 0
     chunk_rows = [c[0].shape[0] for c in chunks]
     rows = own_rows + sum(chunk_rows)
     half, hid = weights[0].shape
@@ -170,8 +193,8 @@
     operands = []
     specs = []
     if own:
-        operands += own[1:]
-        specs += [VMEM, VMEM, VMEM, HBM, HBM]
+        operands += own
+        specs += [ANY] * 2
     for c in chunks:
         operands += c
         specs += [ANY] * 5
@@ -191,9 +214,7 @@
     ]
     copies = 8 + 8 * len(chunks) + 4 * (hid // 256)
     if own:
-        count = own[4].shape[0]
-        scratch += [buf(count, width), buf(count, width)]
-        copies += 4
+        copies += 2
     scratch.append(pltpu.SemaphoreType.DMA((copies,)))
     out = pl.pallas_call(
         functools.partial(expert_kernel, own_rows, chunk_rows, base, block_base, len(aliases)),
@@ -315,21 +336,21 @@
         shifts = [1, 3, 2]
         sends = place([capacity] * 3, shifts, capacity, index, slot, gate, tokens, grad_output, share)
         one, three = shift(sends[0], 1), shift(sends[1], 3)
-        own = [capacity, index, slot, gate, tokens, grad_output]
-        most = 3 * capacity
-        kept, blocks = expert_rows(own, [], weights, 4 * capacity, 0, most, 0, None, None)
-        two = shift(after(sends[2], blocks[0]), 2)
-        near = spread(jnp.concatenate([after(one, blocks[0]), three], 0))
-        far = spread(after(two, *near[1:3]))
-        near[0] = after(near[0], *far[3:])
-        kept, blocks = expert_rows(None, [near], weights, 4 * capacity, capacity, most, capacity, kept, blocks)
+        own = place_own(capacity, index, slot, gate, after(tokens, sends[0]), grad_output)
+        kept, blocks = expert_rows(own, [], weights, 4 * capacity, 0, capacity, 0, None, None)
         total, got = collect(blocks)
         backs = [total(0, capacity)]
-        backs += [shift(total(i * capacity, (i + 1) * capacity), -k) for i, k in ((1, 1), (2, 3))]
-        kept, blocks = expert_rows(None, [far], weights, 4 * capacity, most, capacity, 0, kept, None)
+        two = shift(after(sends[2], blocks[0]), 2)
+        near = spread(jnp.concatenate([after(one, *got), three], 0))
+        far = spread(after(two, *near[1:3]))
+        near[0] = after(near[0], *far[1:3])
+        kept, blocks = expert_rows(None, [near], weights, 4 * capacity, capacity, 2 * capacity, 0, kept, None)
+        total, got = collect(blocks)
+        backs += [shift(total(i * capacity, (i + 1) * capacity), -k) for i, k in ((0, 1), (1, 3))]
+        kept, blocks = expert_rows(None, [far], weights, 4 * capacity, 3 * capacity, capacity, 0, kept, None)
         others = other_halves(kept)
         total, _ = collect([blocks[0]] + [after(b, *got, *others) for b in blocks[1:]])
-        backs.append(shift(after(total(0, capacity), *backs[1:]), -2))
+        backs.append(shift(total(0, capacity), -2))
         shifts = [0] + shifts
     else:
         rows = experts * capacity

time: 107 us -> 106 us (level); the launches traced: 105 us -> 105 us
  Pallas kernels: 31.1 us -> 34.4 us
  local copies, waits for them, and re-layouts: 4.15 us -> 2.19 us
  starting transfers between devices: 32.8 us -> 31.2 us
    ppermute x6, starting transfers between devices: 15.3 us -> 10.8 us  [shift(): lax.ppermute(x, 'expert', [(i, (i + k) % experts) for i in range(experts)])]
    pallas_call x0 -> x1, Pallas kernels: none -> 3.54 us  [place_own(): pl.pallas_call(functools.partial(place_own_kernel, capacity), out_shape=[...]
    ppermute x14 -> x17, starting transfers between devices: 16.4 us -> 19.2 us  [across(): return lax.ppermute(x, 'tensor', [(i, i ^ j) for i in range(tensor_size)])]
    unnamed x19 -> x15, local copies, waits for them, and re-layouts: 4.08 us -> 2.11 us
    ppermute x14 -> x17, waiting for transfers between devices: 17.8 us -> 19.2 us  [across(): return lax.ppermute(x, 'tensor', [(i, i ^ j) for i in range(tensor_size)])]
  transfers between devices with their start and end apart: 24 -> 27, of which waited for: 8 -> 10; matrix products, arithmetic and copies ran while one was open for 3% -> 3% of each run, Pallas kernels for 22% -> 32%
where the time goes in v6:
time: 106 us; the launch traced here: 105 us
  Pallas kernels  34.4 us (32%)
  waiting for transfers between devices  33.9 us (32%)
  starting transfers between devices  31.2 us (29%)
  matrix products  2.58 us (2%)
  local copies, waits for them, and re-layouts  2.19 us (2%)
    pallas_call x3, Pallas kernels, expert_rows(): pl.pallas_call(functools.partial(expert_kernel, own_rows, chunk_rows, bas...  20 us
    ppermute x17, starting transfers between devices, across(): return lax.ppermute(x, 'tensor', [(i, i ^ j) for i in range(tensor_size)])  19.2 us
    ppermute x17, waiting for transfers between devices, across(): return lax.ppermute(x, 'tensor', [(i, i ^ j) for i in range(tensor_size)])  19.2 us
    ppermute x6, waiting for transfers between devices, shift(): lax.ppermute(x, 'expert', [(i, (i + k) % experts) for i in range(experts)])  14.6 us
    ppermute x6, starting transfers between devices, shift(): lax.ppermute(x, 'expert', [(i, (i + k) % experts) for i in range(experts)])  10.8 us
    pallas_call x2, Pallas kernels, outer(): pl.pallas_call(outer_kernel, out_shape=jax.ShapeDtypeStruct((half, hid),...  6.26 us
    pallas_call x1, Pallas kernels, place_own(): pl.pallas_call(functools.partial(place_own_kernel, capacity), out_shape=[...  3.54 us
    pallas_call x1, Pallas kernels, place(): pl.pallas_call(functools.partial(place_kernel, spans, shifts, capacity),...  3.46 us
  transfers between devices with their start and end apart: 27, of which 10 were waited for; matrix products, arithmetic and copies ran while one was open for 3% of the time, Pallas kernels for 32%

profile of v6, /device:TPU:0, one launch (start us, length us, event | category | flops | bytes accessed | tf_op | source)
XLA Modules:
  0.0 105.4 jit_solution(16561352230795331667)
XLA Ops:
  1.2 3.5 %place_rows.1 = (bf16[128,1024]{1,0:T(8,128)(2,1)}, bf16[128,1024]{1,0:T(8,128)(2,1)}, bf16[128,1024]{1,0:T(8,128)(2,1)}) custom-call(s32[1,256]{1,0:T(1,128)} %bitcast.17, s32[1,256]{1,0:T(1,128)} %bitcast.20, f32[1,256]{1,0:T(1,128)} %bitcast.25, bf16[256,2048]{1,0:T(8,128)(2,1)} %tokens.2, bf16[256,2048]{1,0:T(8,128)(2,1)} %grad_output.3), custom_call_target="tpu_custom_call" | custom-call | flops 1000 | bytes 1000 | tf_op jit(solution)/shard_map/place_rows/pallas_call | solution.py:63
  4.7 3.1 %collective-permute-start.5 = (bf16[128,1024]{1,0:T(8,128)(2,1)}, bf16[128,1024]{1,0:T(8,128)(2,1)S(1)}, u32[]{:S(2)}, u32[]{:S(2)}) collective-permute-start(bf16[128,1024]{1,0:T(8,128)(2,1)} %get-tuple-element.43), channel_id=1, source_target_pairs={{0,2},{2,4},{4,6},{6,0},{1,3},{3,5},{5,7},{7,1},{8,10},{10,12},{12... | collective-permute-start | bytes 786440 | tf_op jit(solution)/shard_map/ppermute | solution.py:304
  7.8 2.1 %collective-permute-start.6 = (bf16[128,1024]{1,0:T(8,128)(2,1)}, bf16[128,1024]{1,0:T(8,128)(2,1)S(1)}, u32[]{:S(2)}, u32[]{:S(2)}) collective-permute-start(bf16[128,1024]{1,0:T(8,128)(2,1)} %get-tuple-element.52), channel_id=1, source_target_pairs={{0,6},{2,0},{4,2},{6,4},{1,7},{3,1},{5,3},{7,5},{8,14},{10,8},{12,... | collective-permute-start | bytes 786440 | tf_op jit(solution)/shard_map/ppermute | solution.py:304
  9.8 3.5 %place_own_rows.1 = (bf16[128,2048]{1,0:T(8,128)(2,1)}, bf16[128,2048]{1,0:T(8,128)(2,1)}) custom-call(s32[1,256]{1,0:T(1,128)} %bitcast.18, s32[1,256]{1,0:T(1,128)} %bitcast.21, f32[1,256]{1,0:T(1,128)} %bitcast.26, bf16[256,2048]{1,0:T(8,128)(2,1)} %tokens.2, bf16[256,2048]{1,0:T(8,128)(2,1)} %grad_output.3), custom_call_target="tpu_custom_call" | custom-call | flops 1000 | bytes 1000 | tf_op jit(solution)/shard_map/place_own_rows/pallas_call | solution.py:97
  15.5 6.3 %expert_rows.3 = (bf16[512,2048]{1,0:T(8,128)(2,1)S(1)}, bf16[512,2048]{1,0:T(8,128)(2,1)S(1)}, bf16[512,1024]{1,0:T(8,128)(2,1)S(1)}, bf16[512,1024]{1,0:T(8,12...) custom-call(bf16[128,2048]{1,0:T(8,128)(2,1)S(1)} %copy-done.2, ...), custom_call_target="tpu_custom_call" | custom-call | flops 1610612736 | bytes 10485760 | tf_op jit(solution)/shard_map/expert_rows/pallas_call | solution.py:219
  21.8 2.7 %collective-permute-start.4 = (bf16[128,512]{1,0:T(8,128)(2,1)S(1)}, bf16[128,512]{1,0:T(8,128)(2,1)S(1)}, u32[]{:S(2)}, u32[]{:S(2)}) collective-permute-start(bf16[128,512]{1,0:T(8,128)(2,1)S(1)} %get-tuple-element.50), channel_id=1, source_target_pairs={{0,24},{8,16},{16,8},{24,0},{1,25},{9,17},{17,9},{25,1},{2,26},{10... | collective-permute-start | bytes 393224 | tf_op jit(solution)/shard_map/ppermute | solution.py:301
  25.4 3.0 %collective-permute-done.4 = bf16[128,512]{1,0:T(8,128)(2,1)S(1)} collective-permute-done((bf16[128,512]{1,0:T(8,128)(2,1)S(1)}, bf16[128,512]{1,0:T(8,128)(2,1)S(1)}, u32[]{:S(2)}, u32[]{:S(2)}) %collective-permute-start.4) | collective-permute-done | bytes 131104 | tf_op jit(solution)/shard_map/ppermute | solution.py:301
  28.4 2.4 %collective-permute-done.3 = bf16[128,512]{1,0:T(8,128)(2,1)S(1)} collective-permute-done((bf16[128,512]{1,0:T(8,128)(2,1)S(1)}, bf16[128,512]{1,0:T(8,128)(2,1)S(1)}, u32[]{:S(2)}, u32[]{:S(2)}) %collective-permute-start.3) | collective-permute-done | bytes 131104 | tf_op jit(solution)/shard_map/ppermute | solution.py:301
  30.9 1.6 %collective-permute-start.8 = (bf16[256,1024]{1,0:T(8,128)(2,1)S(1)}, bf16[256,1024]{1,0:T(8,128)(2,1)S(1)}, u32[]{:S(2)}, u32[]{:S(2)}) collective-permute-start(bf16[256,1024]{1,0:T(8,128)(2,1)S(1)} %constant_dynamic-update-slice_fusion.refs_0_), channel_id=1, source_target_pairs={{0,8},{8,0},{16,24},{24,16},{1,9},{9,1},{17,25},{25,17},{2,10},{10... | collective-permute-start | bytes 1572872 | tf_op jit(solution)/shard_map/ppermute | solution.py:301
  33.9 12.0 %collective-permute-done.7.refs_0_ = bf16[128,1024]{1,0:T(8,128)(2,1)S(1)} collective-permute-done((bf16[128,1024]{1,0:T(8,128)(2,1)S(1)}, bf16[128,1024]{1,0:T(8,128)(2,1)S(1)}, u32[]{:S(2)}, u32[]{:S(2)}) %collective-permute-start.7) | collective-permute-done | bytes 262176 | tf_op jit(solution)/shard_map/ppermute | solution.py:304
  45.9 1.7 %collective-permute-start.10 = (bf16[128,1024]{1,0:T(8,128)(2,1)S(1)}, bf16[128,1024]{1,0:T(8,128)(2,1)S(1)}, u32[]{:S(2)}, u32[]{:S(2)}) collective-permute-start(bf16[128,1024]{1,0:T(8,128)(2,1)S(1)} %collective-permute-done.7.refs_0_), channel_id=1, source_target_pairs={{0,8},{8,0},{16,24},{24,16},{1,9},{9,1},{17,25},{25,17},{2,10},{10... | collective-permute-start | bytes 786440 | tf_op jit(solution)/shard_map/ppermute | solution.py:301
  48.0 1.6 %collective-permute-start.12 = (bf16[256,512]{1,0:T(8,128)(2,1)S(1)}, bf16[256,512]{1,0:T(8,128)(2,1)S(1)}, u32[]{:S(2)}, u32[]{:S(2)}) collective-permute-start(bf16[256,512]{1,0:T(8,128)(2,1)S(1)} %slice.56), channel_id=1, source_target_pairs={{0,8},{8,0},{16,24},{24,16},{1,9},{9,1},{17,25},{25,17},{2,10},{10... | collective-permute-start | bytes 786440 | tf_op jit(solution)/shard_map/ppermute | solution.py:301
  50.1 4.9 %collective-permute-done.10.refs_1_ = bf16[128,1024]{1,0:T(8,128)(2,1)S(1)} collective-permute-done((bf16[128,1024]{1,0:T(8,128)(2,1)S(1)}, bf16[128,1024]{1,0:T(8,128)(2,1)S(1)}, u32[]{:S(2)}, u32[]{:S(2)}) %collective-permute-start.10) | collective-permute-done | bytes 262176 | tf_op jit(solution)/shard_map/ppermute | solution.py:301
  55.0 1.7 %collective-permute-done.11.refs_2_ = bf16[128,1024]{1,0:T(8,128)(2,1)S(1)} collective-permute-done((bf16[128,1024]{1,0:T(8,128)(2,1)S(1)}, bf16[128,1024]{1,0:T(8,128)(2,1)S(1)}, u32[]{:S(2)}, u32[]{:S(2)}) %collective-permute-start.11) | collective-permute-done | bytes 262176 | tf_op jit(solution)/shard_map/ppermute | solution.py:301
  57.2 1.7 %collective-permute-start.20 = (bf16[128,512]{1,0:T(8,128)(2,1)S(1)}, bf16[128,512]{1,0:T(8,128)(2,1)S(1)}, u32[]{:S(2)}, u32[]{:S(2)}) collective-permute-start(bf16[128,512]{1,0:T(8,128)(2,1)S(1)} %slice.65), channel_id=1, source_target_pairs={{0,16},{8,24},{16,0},{24,8},{1,17},{9,25},{17,1},{25,9},{2,18},{10... | collective-permute-start | bytes 393224 | tf_op jit(solution)/shard_map/ppermute | solution.py:301
  58.9 1.7 %collective-permute-done.12.refs_3_ = bf16[256,512]{1,0:T(8,128)(2,1)S(1)} collective-permute-done((bf16[256,512]{1,0:T(8,128)(2,1)S(1)}, bf16[256,512]{1,0:T(8,128)(2,1)S(1)}, u32[]{:S(2)}, u32[]{:S(2)}) %collective-permute-start.12) | collective-permute-done | bytes 262176 | tf_op jit(solution)/shard_map/ppermute | solution.py:301
  60.7 1.7 %collective-permute-done.13.refs_4_ = bf16[256,512]{1,0:T(8,128)(2,1)S(1)} collective-permute-done((bf16[256,512]{1,0:T(8,128)(2,1)S(1)}, bf16[256,512]{1,0:T(8,128)(2,1)S(1)}, u32[]{:S(2)}, u32[]{:S(2)}) %collective-permute-start.13) | collective-permute-done | bytes 262176 | tf_op jit(solution)/shard_map/ppermute | solution.py:301
  62.4 7.1 %expert_rows.4 = (bf16[512,2048]{1,0:T(8,128)(2,1)S(1)}, bf16[512,2048]{1,0:T(8,128)(2,1)S(1)}, bf16[512,1024]{1,0:T(8,128)(2,1)S(1)}, bf16[512,1024]{1,0:T(8,12...) custom-call(bf16[256,1024]{1,0:T(8,128)(2,1)S(1)} %constant_dynamic-, ...), custom_call_target="tpu_custom_call", output_to_operand_aliasing={{0}: (9, {}), {1}: (10, {}), {2}: (11, {}), {3}: (12, {})} | custom-call | flops 3221225472 | bytes 12582912 | tf_op jit(solution)/shard_map/expert_rows/pallas_call | solution.py:219
  69.4 1.5 %collective-permute-start.16 = (bf16[256,512]{1,0:T(8,128)(2,1)S(1)}, bf16[256,512]{1,0:T(8,128)(2,1)S(1)}, u32[]{:S(2)}, u32[]{:S(2)}) collective-permute-start(bf16[256,512]{1,0:T(8,128)(2,1)S(1)} %get-tuple-element.64), channel_id=1, source_target_pairs={{0,24},{8,16},{16,8},{24,0},{1,25},{9,17},{17,9},{25,1},{2,26},{10... | collective-permute-start | bytes 786440 | tf_op jit(solution)/shard_map/ppermute | solution.py:301
  71.3 1.7 %collective-permute-start.14 = (bf16[256,512]{1,0:T(8,128)(2,1)S(1)}, bf16[256,512]{1,0:T(8,128)(2,1)S(1)}, u32[]{:S(2)}, u32[]{:S(2)}) collective-permute-start(bf16[256,512]{1,0:T(8,128)(2,1)S(1)} %get-tuple-element.62), channel_id=1, source_target_pairs={{0,8},{8,0},{16,24},{24,16},{1,9},{9,1},{17,25},{25,17},{2,10},{10... | collective-permute-start | bytes 786440 | tf_op jit(solution)/shard_map/ppermute | solution.py:301
  73.0 6.6 %expert_rows.5 = (bf16[512,2048]{1,0:T(8,128)(2,1)S(1)}, bf16[512,2048]{1,0:T(8,128)(2,1)S(1)}, bf16[512,1024]{1,0:T(8,128)(2,1)S(1)}, bf16[512,1024]{1,0:T(8,12...) custom-call(bf16[128,1024]{1,0:T(8,128)(2,1)S(1)} %collective-permut, ...), custom_call_target="tpu_custom_call", output_to_operand_aliasing={{0}: (9, {}), {1}: (10, {}), {2}: (11, {}), {3}: (12, {})} | custom-call | flops 1610612736 | bytes 10485760 | tf_op jit(solution)/shard_map/expert_rows/pallas_call | solution.py:219
  79.6 1.3 %convolution_convert_fusion.1 = bf16[1024,1024]{1,0:T(8,128)(2,1)S(1)} fusion(bf16[512,1024]{1,0:T(8,128)(2,1)S(1)} %get-tuple-element.72.out, bf16[512,2048]{1,0:T(8,128)(2,1)S(1)} %get-tuple-element.71.rows), kind=kOutput, calls=%fused_computation.1 | convolution fusion | flops 1074790400 | bytes 4194304 | tf_op jit(solution)/shard_map/dot_general | solution.py:22
  80.9 1.3 %convolution_convert_fusion = bf16[1024,1024]{1,0:T(8,128)(2,1)S(1)} fusion(bf16[512,1024]{1,0:T(8,128)(2,1)S(1)} %get-tuple-element.74.out, bf16[512,2048]{1,0:T(8,128)(2,1)S(1)} %get-tuple-element.73.rows), kind=kOutput, calls=%fused_computation | convolution fusion | flops 1074790400 | bytes 4194304 | tf_op jit(solution)/shard_map/dot_general | solution.py:22
  82.8 1.5 %collective-permute-start.23 = (bf16[128,512]{1,0:T(8,128)(2,1)S(1)}, bf16[128,512]{1,0:T(8,128)(2,1)S(1)}, u32[]{:S(2)}, u32[]{:S(2)}) collective-permute-start(bf16[128,512]{1,0:T(8,128)(2,1)S(1)} %get-tuple-element.79), channel_id=1, source_target_pairs={{0,24},{8,16},{16,8},{24,0},{1,25},{9,17},{17,9},{25,1},{2,26},{10... | collective-permute-start | bytes 393224 | tf_op jit(solution)/shard_map/ppermute | solution.py:301
  84.7 1.7 %collective-permute-start.21 = (bf16[128,512]{1,0:T(8,128)(2,1)S(1)}, bf16[128,512]{1,0:T(8,128)(2,1)S(1)}, u32[]{:S(2)}, u32[]{:S(2)}) collective-permute-start(bf16[128,512]{1,0:T(8,128)(2,1)S(1)} %get-tuple-element.75), channel_id=1, source_target_pairs={{0,8},{8,0},{16,24},{24,16},{1,9},{9,1},{17,25},{25,17},{2,10},{10... | collective-permute-start | bytes 393224 | tf_op jit(solution)/shard_map/ppermute | solution.py:301
  86.5 3.6 %collective-permute-done.23 = bf16[128,512]{1,0:T(8,128)(2,1)S(1)} collective-permute-done((bf16[128,512]{1,0:T(8,128)(2,1)S(1)}, bf16[128,512]{1,0:T(8,128)(2,1)S(1)}, u32[]{:S(2)}, u32[]{:S(2)}) %collective-permute-start.23) | collective-permute-done | bytes 131104 | tf_op jit(solution)/shard_map/ppermute | solution.py:301
  90.1 2.5 %collective-permute-start.17 = (bf16[128,512]{1,0:T(8,128)(2,1)S(1)}, bf16[128,512]{1,0:T(8,128)(2,1)S(1)}, u32[]{:S(2)}, u32[]{:S(2)}) collective-permute-start(bf16[128,512]{1,0:T(8,128)(2,1)S(1)} %get-tuple-element.84), channel_id=1, source_target_pairs={{0,6},{2,0},{4,2},{6,4},{1,7},{3,1},{5,3},{7,5},{8,14},{10,8},{12,... | collective-permute-start | bytes 393224 | tf_op jit(solution)/shard_map/ppermute | solution.py:304
  92.7 2.5 %collective-permute-start.24 = (bf16[128,512]{1,0:T(8,128)(2,1)S(1)}, bf16[128,512]{1,0:T(8,128)(2,1)S(1)}, u32[]{:S(2)}, u32[]{:S(2)}) collective-permute-start(bf16[128,512]{1,0:T(8,128)(2,1)S(1)} %add_convert_fusion), channel_id=1, source_target_pairs={{0,4},{2,6},{4,0},{6,2},{1,5},{3,7},{5,1},{7,3},{8,12},{10,14},{12... | collective-permute-start | bytes 393224 | tf_op jit(solution)/shard_map/ppermute | solution.py:304
  95.3 3.1 %weight_grad.2 = bf16[1024,1024]{1,0:T(8,128)(2,1)} custom-call(bf16[512,2048]{1,0:T(8,128)(2,1)S(1)} %get-tuple-element.71.rows, bf16[512,1024]{1,0:T(8,128)(2,1)S(1)} %get-tuple-element.72.out, bf16[1024,1024]{1,0:T(8,128)(2,1)S(1)} %collective-permute-done.25.refs_0_), custom_call_target="tpu_custom_call" | custom-call | flops 1000 | bytes 1000 | tf_op jit(solution)/shard_map/weight_grad/pallas_call | solution.py:274
  98.4 3.1 %weight_grad.3 = bf16[1024,1024]{1,0:T(8,128)(2,1)} custom-call(bf16[512,2048]{1,0:T(8,128)(2,1)S(1)} %get-tuple-element.73.rows, bf16[512,1024]{1,0:T(8,128)(2,1)S(1)} %get-tuple-element.74.out, bf16[1024,1024]{1,0:T(8,128)(2,1)S(1)} %collective-permute-done.26.refs_0_), custom_call_target="tpu_custom_call" | custom-call | flops 1000 | bytes 1000 | tf_op jit(solution)/shard_map/weight_grad/pallas_call | solution.py:274
  101.5 2.7 %collective-permute-done.24.refs_3_ = bf16[128,512]{1,0:T(8,128)(2,1)S(1)} collective-permute-done((bf16[128,512]{1,0:T(8,128)(2,1)S(1)}, bf16[128,512]{1,0:T(8,128)(2,1)S(1)}, u32[]{:S(2)}, u32[]{:S(2)}) %collective-permute-start.24) | collective-permute-done | bytes 131104 | tf_op jit(solution)/shard_map/ppermute | solution.py:304
  104.2 1.2 %unplace_rows.1 = bf16[256,512]{1,0:T(8,128)(2,1)} custom-call(s32[1,256]{1,0:T(1,128)S(1)} %bitcast.19, s32[1,256]{1,0:T(1,128)S(1)} %bitcast.22, bf16[128,512]{1,0:T(8,128)(2,1)S(1)} %add_convert_fusion.3.refs_0_, bf16[128,512]{1,0:T(8,128)(2,1)S(1)} %collective-permute-done.17.refs_1_, bf16[128,512]{1,0:T(8,128)(2,1)S(1)} %collective-permute-done.18.refs_2_, ...), custom_call_target="tpu_custom_call" | custom-call | flops 1000 | bytes 1000 | tf_op jit(solution)/shard_map/unplace_rows/pallas_call | solution.py:249
  (55 shorter events, 8.1 us)
Async XLA Ops:
  0.6 12.8 %collective-permute-start = (bf16[1024,1024]{1,0:T(8,128)(2,1)}, bf16[1024,1024]{1,0:T(8,128)(2,1)S(1)}, u32[]{:S(2)}, u32[]{:S(2)}) collective-permute-start(bf16[1024,1024]{1,0:T(8,128)(2,1)} %bitcast.9), channel_id=1, source_target_pairs={{0,1},{1,0},{2,3},{3,2},{4,5},{5,4},{6,7},{7,6},{8,9},{9,8},{10,11... | collective-permute-start | bytes 6291464 | tf_op jit(solution)/shard_map/ppermute | solution.py:298
  1.1 12.3 %collective-permute-start.1 = (bf16[1024,1024]{1,0:T(8,128)(2,1)}, bf16[1024,1024]{1,0:T(8,128)(2,1)S(1)}, u32[]{:S(2)}, u32[]{:S(2)}) collective-permute-start(bf16[1024,1024]{1,0:T(8,128)(2,1)} %bitcast.13), channel_id=1, source_target_pairs={{0,1},{1,0},{2,3},{3,2},{4,5},{5,4},{6,7},{7,6},{8,9},{9,8},{10,11... | collective-permute-start | bytes 6291464 | tf_op jit(solution)/shard_map/ppermute | solution.py:298
  1.2 12.2 %copy-start = (bf16[1,1024,1024]{2,1,0:T(8,128)(2,1)S(1)}, bf16[1,1024,1024]{2,1,0:T(8,128)(2,1)}, u32[]{:S(2)}) copy-start(bf16[1,1024,1024]{2,1,0:T(8,128)(2,1)} %param.12) | copy-start | bytes 6291460
  1.2 12.2 %copy-start.1 = (bf16[1,1024,1024]{2,1,0:T(8,128)(2,1)S(1)}, bf16[1,1024,1024]{2,1,0:T(8,128)(2,1)}, u32[]{:S(2)}) copy-start(bf16[1,1024,1024]{2,1,0:T(8,128)(2,1)} %param.13) | copy-start | bytes 6291460
  4.7 20.7 %collective-permute-start.5 = (bf16[128,1024]{1,0:T(8,128)(2,1)}, bf16[128,1024]{1,0:T(8,128)(2,1)S(1)}, u32[]{:S(2)}, u32[]{:S(2)}) collective-permute-start(bf16[128,1024]{1,0:T(8,128)(2,1)} %get-tuple-element.43), channel_id=1, source_target_pairs={{0,2},{2,4},{4,6},{6,0},{1,3},{3,5},{5,7},{7,1},{8,10},{10,12},{12... | collective-permute-start | bytes 786440 | tf_op jit(solution)/shard_map/ppermute | solution.py:304
  7.8 23.1 %collective-permute-start.6 = (bf16[128,1024]{1,0:T(8,128)(2,1)}, bf16[128,1024]{1,0:T(8,128)(2,1)S(1)}, u32[]{:S(2)}, u32[]{:S(2)}) collective-permute-start(bf16[128,1024]{1,0:T(8,128)(2,1)} %get-tuple-element.52), channel_id=1, source_target_pairs={{0,6},{2,0},{4,2},{6,4},{1,7},{3,1},{5,3},{7,5},{8,14},{10,8},{12,... | collective-permute-start | bytes 786440 | tf_op jit(solution)/shard_map/ppermute | solution.py:304
  15.5 17.7 %copy-start.6 = (bf16[128,1024]{1,0:T(8,128)(2,1)S(1)}, bf16[128,1024]{1,0:T(8,128)(2,1)}, u32[]{:S(2)}) copy-start(bf16[128,1024]{1,0:T(8,128)(2,1)} %get-tuple-element.54) | copy-start | bytes 786436
  21.8 6.6 %collective-permute-start.4 = (bf16[128,512]{1,0:T(8,128)(2,1)S(1)}, bf16[128,512]{1,0:T(8,128)(2,1)S(1)}, u32[]{:S(2)}, u32[]{:S(2)}) collective-permute-start(bf16[128,512]{1,0:T(8,128)(2,1)S(1)} %get-tuple-element.50), channel_id=1, source_target_pairs={{0,24},{8,16},{16,8},{24,0},{1,25},{9,17},{17,9},{25,1},{2,26},{10... | collective-permute-start | bytes 393224 | tf_op jit(solution)/shard_map/ppermute | solution.py:301
  24.5 6.3 %collective-permute-start.3 = (bf16[128,512]{1,0:T(8,128)(2,1)S(1)}, bf16[128,512]{1,0:T(8,128)(2,1)S(1)}, u32[]{:S(2)}, u32[]{:S(2)}) collective-permute-start(bf16[128,512]{1,0:T(8,128)(2,1)S(1)} %get-tuple-element.49), channel_id=1, source_target_pairs={{0,16},{8,24},{16,0},{24,8},{1,17},{9,25},{17,1},{25,9},{2,18},{10... | collective-permute-start | bytes 393224 | tf_op jit(solution)/shard_map/ppermute | solution.py:301
  25.0 5.9 %collective-permute-start.2 = (bf16[128,512]{1,0:T(8,128)(2,1)S(1)}, bf16[128,512]{1,0:T(8,128)(2,1)S(1)}, u32[]{:S(2)}, u32[]{:S(2)}) collective-permute-start(bf16[128,512]{1,0:T(8,128)(2,1)S(1)} %get-tuple-element.48), channel_id=1, source_target_pairs={{0,8},{8,0},{16,24},{24,16},{1,9},{9,1},{17,25},{25,17},{2,10},{10... | collective-permute-start | bytes 393224 | tf_op jit(solution)/shard_map/ppermute | solution.py:301
  30.9 14.9 %collective-permute-start.8 = (bf16[256,1024]{1,0:T(8,128)(2,1)S(1)}, bf16[256,1024]{1,0:T(8,128)(2,1)S(1)}, u32[]{:S(2)}, u32[]{:S(2)}) collective-permute-start(bf16[256,1024]{1,0:T(8,128)(2,1)S(1)} %constant_dynamic-update-slice_fusion.refs_0_), channel_id=1, source_target_pairs={{0,8},{8,0},{16,24},{24,16},{1,9},{9,1},{17,25},{25,17},{2,10},{10... | collective-permute-start | bytes 1572872 | tf_op jit(solution)/shard_map/ppermute | solution.py:301
  32.5 13.3 %collective-permute-start.9 = (bf16[256,1024]{1,0:T(8,128)(2,1)S(1)}, bf16[256,1024]{1,0:T(8,128)(2,1)S(1)}, u32[]{:S(2)}, u32[]{:S(2)}) collective-permute-start(bf16[256,1024]{1,0:T(8,128)(2,1)S(1)} %constant_dynamic-update-slice_fusion.refs_0_), channel_id=1, source_target_pairs={{0,16},{8,24},{16,0},{24,8},{1,17},{9,25},{17,1},{25,9},{2,18},{10... | collective-permute-start | bytes 1572872 | tf_op jit(solution)/shard_map/ppermute | solution.py:301
  33.2 12.6 %collective-permute-start.7 = (bf16[128,1024]{1,0:T(8,128)(2,1)S(1)}, bf16[128,1024]{1,0:T(8,128)(2,1)S(1)}, u32[]{:S(2)}, u32[]{:S(2)}) collective-permute-start(bf16[128,1024]{1,0:T(8,128)(2,1)S(1)} %copy-done.6), channel_id=1, source_target_pairs={{0,4},{2,6},{4,0},{6,2},{1,5},{3,7},{5,1},{7,3},{8,12},{10,14},{12... | collective-permute-start | bytes 786440 | tf_op jit(solution)/shard_map/ppermute | solution.py:304
  45.9 9.2 %collective-permute-start.10 = (bf16[128,1024]{1,0:T(8,128)(2,1)S(1)}, bf16[128,1024]{1,0:T(8,128)(2,1)S(1)}, u32[]{:S(2)}, u32[]{:S(2)}) collective-permute-start(bf16[128,1024]{1,0:T(8,128)(2,1)S(1)} %collective-permute-done.7.refs_0_), channel_id=1, source_target_pairs={{0,8},{8,0},{16,24},{24,16},{1,9},{9,1},{17,25},{25,17},{2,10},{10... | collective-permute-start | bytes 786440 | tf_op jit(solution)/shard_map/ppermute | solution.py:301
  47.5 9.2 %collective-permute-start.11 = (bf16[128,1024]{1,0:T(8,128)(2,1)S(1)}, bf16[128,1024]{1,0:T(8,128)(2,1)S(1)}, u32[]{:S(2)}, u32[]{:S(2)}) collective-permute-start(bf16[128,1024]{1,0:T(8,128)(2,1)S(1)} %collective-permute-done.7.refs_0_), channel_id=1, source_target_pairs={{0,16},{8,24},{16,0},{24,8},{1,17},{9,25},{17,1},{25,9},{2,18},{10... | collective-permute-start | bytes 786440 | tf_op jit(solution)/shard_map/ppermute | solution.py:301
  48.0 12.6 %collective-permute-start.12 = (bf16[256,512]{1,0:T(8,128)(2,1)S(1)}, bf16[256,512]{1,0:T(8,128)(2,1)S(1)}, u32[]{:S(2)}, u32[]{:S(2)}) collective-permute-start(bf16[256,512]{1,0:T(8,128)(2,1)S(1)} %slice.56), channel_id=1, source_target_pairs={{0,8},{8,0},{16,24},{24,16},{1,9},{9,1},{17,25},{25,17},{2,10},{10... | collective-permute-start | bytes 786440 | tf_op jit(solution)/shard_map/ppermute | solution.py:301
  49.7 12.7 %collective-permute-start.13 = (bf16[256,512]{1,0:T(8,128)(2,1)S(1)}, bf16[256,512]{1,0:T(8,128)(2,1)S(1)}, u32[]{:S(2)}, u32[]{:S(2)}) collective-permute-start(bf16[256,512]{1,0:T(8,128)(2,1)S(1)} %slice.57), channel_id=1, source_target_pairs={{0,16},{8,24},{16,0},{24,8},{1,17},{9,25},{17,1},{25,9},{2,18},{10... | collective-permute-start | bytes 786440 | tf_op jit(solution)/shard_map/ppermute | solution.py:301
  56.8 16.2 %collective-permute-start.19 = (bf16[128,512]{1,0:T(8,128)(2,1)S(1)}, bf16[128,512]{1,0:T(8,128)(2,1)S(1)}, u32[]{:S(2)}, u32[]{:S(2)}) collective-permute-start(bf16[128,512]{1,0:T(8,128)(2,1)S(1)} %slice.64), channel_id=1, source_target_pairs={{0,8},{8,0},{16,24},{24,16},{1,9},{9,1},{17,25},{25,17},{2,10},{10... | collective-permute-start | bytes 393224 | tf_op jit(solution)/shard_map/ppermute | solution.py:301
  57.2 15.8 %collective-permute-start.20 = (bf16[128,512]{1,0:T(8,128)(2,1)S(1)}, bf16[128,512]{1,0:T(8,128)(2,1)S(1)}, u32[]{:S(2)}, u32[]{:S(2)}) collective-permute-start(bf16[128,512]{1,0:T(8,128)(2,1)S(1)} %slice.65), channel_id=1, source_target_pairs={{0,16},{8,24},{16,0},{24,8},{1,17},{9,25},{17,1},{25,9},{2,18},{10... | collective-permute-start | bytes 393224 | tf_op jit(solution)/shard_map/ppermute | solution.py:301
  69.4 12.8 %collective-permute-start.16 = (bf16[256,512]{1,0:T(8,128)(2,1)S(1)}, bf16[256,512]{1,0:T(8,128)(2,1)S(1)}, u32[]{:S(2)}, u32[]{:S(2)}) collective-permute-start(bf16[256,512]{1,0:T(8,128)(2,1)S(1)} %get-tuple-element.64), channel_id=1, source_target_pairs={{0,24},{8,16},{16,8},{24,0},{1,25},{9,17},{17,9},{25,1},{2,26},{10... | collective-permute-start | bytes 786440 | tf_op jit(solution)/shard_map/ppermute | solution.py:301
  70.9 11.3 %collective-permute-start.15 = (bf16[256,512]{1,0:T(8,128)(2,1)S(1)}, bf16[256,512]{1,0:T(8,128)(2,1)S(1)}, u32[]{:S(2)}, u32[]{:S(2)}) collective-permute-start(bf16[256,512]{1,0:T(8,128)(2,1)S(1)} %get-tuple-element.63), channel_id=1, source_target_pairs={{0,16},{8,24},{16,0},{24,8},{1,17},{9,25},{17,1},{25,9},{2,18},{10... | collective-permute-start | bytes 786440 | tf_op jit(solution)/shard_map/ppermute | solution.py:301
  71.3 10.9 %collective-permute-start.14 = (bf16[256,512]{1,0:T(8,128)(2,1)S(1)}, bf16[256,512]{1,0:T(8,128)(2,1)S(1)}, u32[]{:S(2)}, u32[]{:S(2)}) collective-permute-start(bf16[256,512]{1,0:T(8,128)(2,1)S(1)} %get-tuple-element.62), channel_id=1, source_target_pairs={{0,8},{8,0},{16,24},{24,16},{1,9},{9,1},{17,25},{25,17},{2,10},{10... | collective-permute-start | bytes 786440 | tf_op jit(solution)/shard_map/ppermute | solution.py:301
  82.3 13.0 %collective-permute-start.25 = (bf16[1024,1024]{1,0:T(8,128)(2,1)S(1)}, bf16[1024,1024]{1,0:T(8,128)(2,1)S(1)}, u32[]{:S(2)}, u32[]{:S(2)}) collective-permute-start(bf16[1024,1024]{1,0:T(8,128)(2,1)S(1)} %convolution_convert_fusion.1), channel_id=1, source_target_pairs={{0,1},{1,0},{2,3},{3,2},{4,5},{5,4},{6,7},{7,6},{8,9},{9,8},{10,11... | collective-permute-start | bytes 6291464 | tf_op jit(solution)/shard_map/ppermute | solution.py:298
  82.3 16.1 %collective-permute-start.26 = (bf16[1024,1024]{1,0:T(8,128)(2,1)S(1)}, bf16[1024,1024]{1,0:T(8,128)(2,1)S(1)}, u32[]{:S(2)}, u32[]{:S(2)}) collective-permute-start(bf16[1024,1024]{1,0:T(8,128)(2,1)S(1)} %convolution_convert_fusion), channel_id=1, source_target_pairs={{0,1},{1,0},{2,3},{3,2},{4,5},{5,4},{6,7},{7,6},{8,9},{9,8},{10,11... | collective-permute-start | bytes 6291464 | tf_op jit(solution)/shard_map/ppermute | solution.py:298
  82.8 7.3 %collective-permute-start.23 = (bf16[128,512]{1,0:T(8,128)(2,1)S(1)}, bf16[128,512]{1,0:T(8,128)(2,1)S(1)}, u32[]{:S(2)}, u32[]{:S(2)}) collective-permute-start(bf16[128,512]{1,0:T(8,128)(2,1)S(1)} %get-tuple-element.79), channel_id=1, source_target_pairs={{0,24},{8,16},{16,8},{24,0},{1,25},{9,17},{17,9},{25,1},{2,26},{10... | collective-permute-start | bytes 393224 | tf_op jit(solution)/shard_map/ppermute | solution.py:301
  84.3 8.3 %collective-permute-start.22 = (bf16[128,512]{1,0:T(8,128)(2,1)S(1)}, bf16[128,512]{1,0:T(8,128)(2,1)S(1)}, u32[]{:S(2)}, u32[]{:S(2)}) collective-permute-start(bf16[128,512]{1,0:T(8,128)(2,1)S(1)} %get-tuple-element.77), channel_id=1, source_target_pairs={{0,16},{8,24},{16,0},{24,8},{1,17},{9,25},{17,1},{25,9},{2,18},{10... | collective-permute-start | bytes 393224 | tf_op jit(solution)/shard_map/ppermute | solution.py:301
  84.7 7.9 %collective-permute-start.21 = (bf16[128,512]{1,0:T(8,128)(2,1)S(1)}, bf16[128,512]{1,0:T(8,128)(2,1)S(1)}, u32[]{:S(2)}, u32[]{:S(2)}) collective-permute-start(bf16[128,512]{1,0:T(8,128)(2,1)S(1)} %get-tuple-element.75), channel_id=1, source_target_pairs={{0,8},{8,0},{16,24},{24,16},{1,9},{9,1},{17,25},{25,17},{2,10},{10... | collective-permute-start | bytes 393224 | tf_op jit(solution)/shard_map/ppermute | solution.py:301
  90.1 14.1 %collective-permute-start.17 = (bf16[128,512]{1,0:T(8,128)(2,1)S(1)}, bf16[128,512]{1,0:T(8,128)(2,1)S(1)}, u32[]{:S(2)}, u32[]{:S(2)}) collective-permute-start(bf16[128,512]{1,0:T(8,128)(2,1)S(1)} %get-tuple-element.84), channel_id=1, source_target_pairs={{0,6},{2,0},{4,2},{6,4},{1,7},{3,1},{5,3},{7,5},{8,14},{10,8},{12,... | collective-permute-start | bytes 393224 | tf_op jit(solution)/shard_map/ppermute | solution.py:304
  92.6 11.6 %collective-permute-start.18 = (bf16[128,512]{1,0:T(8,128)(2,1)S(1)}, bf16[128,512]{1,0:T(8,128)(2,1)S(1)}, u32[]{:S(2)}, u32[]{:S(2)}) collective-permute-start(bf16[128,512]{1,0:T(8,128)(2,1)S(1)} %get-tuple-element.83), channel_id=1, source_target_pairs={{0,2},{2,4},{4,6},{6,0},{1,3},{3,5},{5,7},{7,1},{8,10},{10,12},{12... | collective-permute-start | bytes 393224 | tf_op jit(solution)/shard_map/ppermute | solution.py:304
  92.7 11.5 %collective-permute-start.24 = (bf16[128,512]{1,0:T(8,128)(2,1)S(1)}, bf16[128,512]{1,0:T(8,128)(2,1)S(1)}, u32[]{:S(2)}, u32[]{:S(2)}) collective-permute-start(bf16[128,512]{1,0:T(8,128)(2,1)S(1)} %add_convert_fusion), channel_id=1, source_target_pairs={{0,4},{2,6},{4,0},{6,2},{1,5},{3,7},{5,1},{7,3},{8,12},{10,14},{12... | collective-permute-start | bytes 393224 | tf_op jit(solution)/shard_map/ppermute | solution.py:304
  98.4 5.8 %copy-start.4 = (s32[256,1]{0,1:T(1,128)S(1)}, s32[256,1]{0,1:T(1,128)}, u32[]{:S(2)}) copy-start(s32[256,1]{0,1:T(1,128)} %param.10) | copy-start | bytes 3076
  98.4 5.8 %copy-start.5 = (s32[256,1]{0,1:T(1,128)S(1)}, s32[256,1]{0,1:T(1,128)}, u32[]{:S(2)}) copy-start(s32[256,1]{0,1:T(1,128)} %param.11) | copy-start | bytes 3076
  (2 other events, 2.1 us)

commit v7 on v5

v7 whole, which is shorter than its diff:
```python
import functools

import jax
import jax.numpy as jnp
from jax import lax
from jax.experimental import pallas as pl
from jax.experimental.pallas import tpu as pltpu
from jax.sharding import PartitionSpec as P

F32 = jnp.float32
BF16 = jnp.bfloat16
I32 = jnp.int32
ANY = pl.BlockSpec(memory_space=pl.ANY)
VMEM = pl.BlockSpec(memory_space=pltpu.VMEM)
SMEM = pl.BlockSpec(memory_space=pltpu.SMEM)
HBM = pl.BlockSpec(memory_space=pltpu.HBM)
LIMIT = 22 * 2**20
SMALL = pl.CostEstimate(flops=1000, bytes_accessed=1000, transcendentals=0)


def dot(lhs, rhs, left=1, right=0):
    return lax.dot_general(lhs, rhs, (((left,), (right,)), ((), ())), preferred_element_type=F32)


def hits(position, first, rows):
    ids = lax.broadcasted_iota(I32, (rows, position.shape[1]), 0) + first
    return ids == position


def places(index, slot, capacity):
    return index[...] * capacity + slot[...]


def expert_first(k, capacity):
    experts = lax.axis_size("expert")
    return 0 if k is None else lax.rem(lax.axis_index("expert") + k, experts) * capacity


def gate_of(hit, gate):
    return jnp.sum(jnp.where(hit, gate, 0.0), axis=1, keepdims=True)


class Copies:
    def __init__(self, sem):
        self.sem, self.count = sem, 0

    def start(self, src, dst):
        copy = pltpu.make_async_copy(src, dst, self.sem.at[self.count])
        self.count += 1
        copy.start()
        return copy

    def rows(self, src, dst, count, pieces):
        step = count // pieces
        return [self.start(src.at[pl.ds(i * step, step), :], dst.at[pl.ds(i * step, step), :]) for i in range(pieces)]


def wait(copies):
    for copy in copies:
        copy.wait()


def place_kernel(spans, shifts, capacity, own, index, slot, gate, tokens, grad_output, *refs):
    sends, refs = refs[: len(spans)], refs[len(spans) :]
    if own:
        owns, refs = refs[:2], refs[2:]
    tok, grad, packed = refs[:3]
    copies = Copies(refs[-1])
    count, width = tok.shape
    half, share = width // 2, width // 4
    arrive = copies.rows(tokens, tok, count, 8) + copies.rows(grad_output, grad, count, 8)
    position = places(index, slot, capacity)
    found = [hits(position, expert_first(k, capacity), rows) for k, rows in zip(shifts, spans)]
    scales = [gate_of(hit, gate[...]) for hit in found]
    hots = [hit.astype(BF16) for hit in found]
    columns = pl.ds(pl.multiple_of(lax.axis_index("tensor") * share, share), share)
    wait(arrive)
    leave = []
    at = 0
    for hot, scale, rows, out in zip(hots, scales, spans, sends):
        packed[at : at + rows, :share] = dot(hot, tok[:, columns]).astype(BF16)
        packed[at : at + rows, share:] = (dot(hot, grad[:, columns]) * scale).astype(BF16)
        leave += copies.rows(packed.at[pl.ds(at, rows), :], out, rows, 2)
        at += rows
    if own:
        mine = lax.axis_index("dp")
        hit = hits(position, expert_first(0, capacity), capacity)
        hot, scale = hit.astype(BF16), gate_of(hit, gate[...])
        placed = refs[3:5]
        for i, start in enumerate((mine * half, (1 - mine) * half)):
            source = pl.ds(pl.multiple_of(start, half), half)
            target = slice(i * half, (i + 1) * half)
            placed[0][:, target] = dot(hot, tok[:, source]).astype(BF16)
            placed[1][:, target] = (dot(hot, grad[:, source]) * scale).astype(BF16)
        for src, dst in zip(placed, owns):
            leave += copies.rows(src, dst, capacity, 2)
    wait(leave)


def place(spans, shifts, capacity, own, index, slot, gate, tokens, grad_output):
    count, width = tokens.shape
    shapes = [(rows, width // 2) for rows in spans] + [(capacity, width)] * (2 if own else 0)
    buf = lambda *shape: pltpu.VMEM(shape, BF16)
    scratch = [buf(count, width), buf(count, width), buf(sum(spans), width // 2)]
    scratch += [buf(capacity, width)] * (2 if own else 0)
    return pl.pallas_call(
        functools.partial(place_kernel, spans, shifts, capacity, own),
        out_shape=[jax.ShapeDtypeStruct(shape, BF16) for shape in shapes],
        in_specs=[VMEM, VMEM, VMEM, HBM, HBM],
        out_specs=[ANY] * len(shapes),
        scratch_shapes=scratch + [pltpu.SemaphoreType.DMA((16 + 2 * len(shapes),))],
        compiler_params=pltpu.CompilerParams(vmem_limit_bytes=54 * 2**20),
        cost_estimate=SMALL,
        name="place_rows",
    )(index, slot, gate, tokens, grad_output)


def gelu_parts(pre):
    c = 0.7978845608028654
    square = pre * pre
    th = jnp.tanh(c * (pre + 0.044715 * (pre * square)))
    half = 0.5 * (1.0 + th)
    return pre * half, half + 0.5 * pre * (1.0 - th * th) * (c + (3 * 0.044715 * c) * square)


def expert_kernel(first, base, groups, aliased, *refs):
    refs = list(refs)
    take = lambda n: [refs.pop(0) for _ in range(n)]
    slots = take(2 if first is None else 5)
    up_halves, down_halves = take(2), take(2)
    take(aliased)
    kept_rows, kept_acts = take(2)
    targets = [take(4 if step is None else 2) for _, step in groups]
    tok, grad, up, down, hidden, slope, back = take(7)
    copies = Copies(take(1)[0])
    rows, width = tok.shape
    half, share = width // 2, width // 4
    order = lax.axis_index("tensor") ^ (2 * lax.axis_index("dp"))
    arrive = []
    if first is None:
        arrive += copies.rows(slots[0], tok, rows, 2) + copies.rows(slots[1], grad, rows, 2)
    else:
        span = pl.ds(first, rows)
        for j in range(4):
            columns = pl.ds(pl.multiple_of((order ^ j) * share, share), share)
            if j < 3:
                sources = [slots[j].at[span, pl.ds(0, share)], slots[j].at[span, pl.ds(share, share)]]
            else:
                sources = [slots[3].at[span, :], slots[4].at[span, :]]
            arrive += [copies.start(src, dst.at[:, columns]) for src, dst in zip(sources, (tok, grad))]
    hid = hidden.shape[1]
    step = 256
    tiles = []
    for n in range(0, hid, step):
        cols = pl.ds(n, step)
        tiles.append([])
        for halves, dst in ((up_halves, up), (down_halves, down)):
            for i in range(2):
                tiles[-1].append(copies.start(halves[i].at[:, cols], dst.at[pl.ds(i * half, half), cols]))
    wait(arrive)
    mine = pl.ds(base, rows)
    leave = [copies.start(src, kept_rows.at[i, mine, :]) for i, src in enumerate((tok, grad))]
    for n, arrived in zip(range(0, hid, step), tiles):
        cols = slice(n, n + step)
        wait(arrived)
        pre = dot(tok[...], up[:, cols])
        hidden_grad = dot(grad[...], down[:, cols])
        act, deriv = gelu_parts(pre)
        hidden[:, cols] = act.astype(BF16)
        slope[:, cols] = (hidden_grad * deriv).astype(BF16)
    leave += [copies.start(src, kept_acts.at[i, mine, :]) for i, src in enumerate((slope, hidden))]
    for j in range(4):
        quarter = pl.ds(pl.multiple_of((order ^ j) * share, share), share)
        back[j] = dot(slope[...], up[quarter, :], 1, 1).astype(BF16)
        at = 0
        for (n, step), outs in zip(groups, targets):
            out = outs[j] if step is None else outs[(j & step) // step].at[(j & (3 - step)) // (3 - step)]
            leave.append(copies.start(back.at[j, pl.ds(at, n), :], out))
            at += n
    wait(leave)


def expert_rows(slots, first, groups, weights, total_rows, base, kept):
    rows = sum(n for n, _ in groups)
    half, hid = weights[0].shape
    width, share = 2 * half, half // 2
    operands = list(slots) + list(weights) + list(kept or [])
    aliases = {len(slots) + 4 + i: i for i in range(2)} if kept else {}
    shape = lambda *s: jax.ShapeDtypeStruct(s, BF16)
    buf = lambda *s: pltpu.VMEM(s, BF16)
    quarters = [[shape(n, share)] * 4 if step is None else [shape(2, n, share)] * 2 for n, step in groups]
    counts = [len(q) for q in quarters]
    out = pl.pallas_call(
        functools.partial(expert_kernel, first, base, groups, len(aliases)),
        out_shape=[shape(2, total_rows, width), shape(2, total_rows, hid)] + sum(quarters, []),
        in_specs=[ANY] * len(operands),
        out_specs=[ANY] * (2 + sum(counts)),
        scratch_shapes=[
            buf(rows, width), buf(rows, width), buf(width, hid), buf(width, hid),
            buf(rows, hid), buf(rows, hid), buf(4, rows, share),
            pltpu.SemaphoreType.DMA((12 + 4 * (hid // 256) + 4 * len(groups),)),
        ],
        input_output_aliases=aliases,
        compiler_params=pltpu.CompilerParams(vmem_limit_bytes=LIMIT + rows * 2**15),
        cost_estimate=pl.CostEstimate(
            flops=6 * rows * width * hid, bytes_accessed=4 * width * hid + 8 * rows * width, transcendentals=rows * hid
        ),
        name="expert_rows",
    )(*operands)
    starts = [2 + sum(counts[:i]) for i in range(len(counts))]
    return list(out[:2]), [list(out[i : i + n]) for i, n in zip(starts, counts)]


def unplace_kernel(spans, shifts, capacity, index, slot, *refs):
    out = refs[-1]
    position = places(index, slot, capacity)
    total = None
    for k, rows, back in zip(shifts, spans, refs[:-1]):
        hot = hits(position, expert_first(k, capacity), rows).astype(BF16)
        part = dot(hot, back[...], 0, 0)
        total = part if total is None else total + part
    out[...] = total.astype(BF16)


def unplace(shifts, capacity, index, slot, backs):
    spans = [b.shape[0] for b in backs]
    count, share = index.shape[1], backs[0].shape[1]
    return pl.pallas_call(
        functools.partial(unplace_kernel, spans, shifts, capacity),
        out_shape=jax.ShapeDtypeStruct((count, share), BF16),
        in_specs=[VMEM] * (2 + len(backs)),
        out_specs=VMEM,
        compiler_params=pltpu.CompilerParams(vmem_limit_bytes=LIMIT),
        cost_estimate=SMALL,
        name="unplace_rows",
    )(index, slot, *backs)


def weight_grad_kernel(rows, acts, got, up_out, down_out, total, sem):
    copies = Copies(sem)
    half = total.shape[1]
    step = 128
    leave = []
    for i, out in enumerate((up_out, down_out)):
        for n in range(0, half, step):
            mine = dot(rows[i, :, n : n + step], acts[i], 0, 0).astype(BF16).astype(F32)
            total[i, n : n + step, :] = (mine + got[i, n : n + step, :].astype(F32)).astype(BF16)
            leave.append(copies.start(total.at[i, pl.ds(n, step), :], out.at[pl.ds(n, step), :]))
    wait(leave)


def weight_grads(kept_rows, kept_acts, got):
    _, count, width = kept_rows.shape
    hid = kept_acts.shape[2]
    half = width // 2
    return pl.pallas_call(
        weight_grad_kernel,
        out_shape=[jax.ShapeDtypeStruct((half, hid), BF16)] * 2,
        grid=(1,),
        in_specs=[
            pl.BlockSpec((2, count, half), lambda i: (0, 0, 0)),
            pl.BlockSpec((2, count, hid), lambda i: (0, 0, 0)),
            pl.BlockSpec((2, half, hid), lambda i: (0, 0, 0)),
        ],
        out_specs=[ANY] * 2,
        scratch_shapes=[pltpu.VMEM((2, half, hid), BF16), pltpu.SemaphoreType.DMA((2 * (half // 128),))],
        compiler_params=pltpu.CompilerParams(vmem_limit_bytes=40 * 2**20),
        cost_estimate=SMALL,
        name="weight_grads",
    )(kept_rows, kept_acts, got)


def local(tokens, grad_output, gate_prob, expert_index, slot_index, up_weight, down_weight):
    experts = lax.axis_size("expert")
    tensor_size = lax.axis_size("tensor")
    tok_count, width = tokens.shape
    capacity = 2 * tok_count // experts
    share = width // tensor_size

    def swap(x):
        return lax.ppermute(x, "dp", [(0, 1), (1, 0)])

    def across(x, j):
        return lax.ppermute(x, "tensor", [(i, i ^ j) for i in range(tensor_size)])

    def shift(x, k):
        return lax.ppermute(x, "expert", [(i, (i + k) % experts) for i in range(experts)])

    def after(x, *others):
        return lax.optimization_barrier((x,) + others)[0]

    def spread(rows, *before):
        x, y = across(rows, 1), across(rows, 2)
        half_y, half_x = y[:, :share], x[:, share:]
        if before:
            half_y, half_x = after(half_y, *before), after(half_x, *before)
        return [rows, x, y, across(half_y, 1), across(half_x, 2)]

    def collect(blocks):
        got = [across(blocks[j], j) for j in (1, 2, 3)]
        terms = [b.astype(F32) for b in [blocks[0]] + got]
        return (terms[0] + terms[1] + (terms[2] + terms[3])).astype(BF16), got

    def collect_pair(pair, step):
        keep, send = pair
        got = across(send, step)
        last = across((keep[1].astype(F32) + got[1].astype(F32)).astype(BF16), 3 - step)
        return (keep[0].astype(F32) + got[0].astype(F32) + last.astype(F32)).astype(BF16), got

    def other_halves(kept):
        rows, acts = kept
        dims = (((1,), (1,)), ((0,), (0,)))
        return lax.dot_general(rows[:, :, width // 2 :], acts, dims, preferred_element_type=F32).astype(BF16)

    index, slot = expert_index.reshape(1, tok_count), slot_index.reshape(1, tok_count)
    gate = gate_prob.reshape(1, tok_count)
    up_own, down_own = up_weight[0], down_weight[0]
    weights = [up_own, swap(up_own), down_own, swap(down_own)]

    if experts == 4:
        shifts = [1, 3, 2]
        placed = place([capacity] * 3, shifts, capacity, True, index, slot, gate, tokens, grad_output)
        moved = [shift(rows, k) for rows, k in zip(placed, shifts)]
        everything = 4 * capacity
        slots = spread(jnp.concatenate(moved, 0))
        own = [after(placed[3], *moved), placed[4]]
        kept, (pair,) = expert_rows(own, None, [(capacity, 1)], weights, everything, 0, None)
        back, got_own = collect_pair([pair[0], after(pair[1], *slots[3:])], 1)
        backs = [back]
        kept, pairs = expert_rows(slots, 0, [(capacity, 1), (capacity, 2)], weights, everything, capacity, kept)
        (one, got_one), (three, got_three) = collect_pair(pairs[0], 1), collect_pair(pairs[1], 2)
        backs += [shift(one, -1), shift(three, -3)]
        kept, (blocks,) = expert_rows(
            [after(slots[0], got_own)] + slots[1:], 2 * capacity, [(capacity, None)], weights, everything, 3 * capacity, kept
        )
        others = other_halves([kept[0], after(kept[1], got_one, got_three)])
        grads = weight_grads(*kept, swap(others))
        two, _ = collect([blocks[0]] + [after(b, got_one, got_three) for b in blocks[1:]])
        backs.append(after(shift(two, -2), *grads))
        shifts = [0] + shifts
    else:
        rows = experts * capacity
        shifts = [None]

        def exchange(x):
            moved = lax.all_to_all(
                x.reshape(experts, capacity, x.shape[1]), "expert", split_axis=0, concat_axis=0, tiled=True
            )
            return moved.reshape(rows, x.shape[1])

        (send,) = place([rows], shifts, capacity, False, index, slot, gate, tokens, grad_output)
        kept, (blocks,) = expert_rows(spread(exchange(send)), 0, [(rows, None)], weights, rows, 0, None)
        others = other_halves(kept)
        grads = weight_grads(*kept, swap(others))
        total, _ = collect(blocks)
        backs = [exchange(total)]

    return unplace(shifts, capacity, index, slot, backs), grads[0][None], grads[1][None]


def solution(mesh):
    placed = (
        P(("expert", "dp"), None),
        P(("expert", "dp"), None),
        P(("expert", "dp")),
        P(("expert", "dp"), None),
        P(("expert", "dp"), None),
        P("expert", "dp", "tensor"),
        P("expert", "dp", "tensor"),
    )
    return jax.shard_map(
        local,
        mesh=mesh,
        in_specs=placed,
        out_specs=(
            P(("expert", "dp"), "tensor"),
            P("expert", "dp", "tensor"),
            P("expert", "dp", "tensor"),
        ),
        check_vma=False,
    )
```

time: 107 us -> 116 us (1.084)
  waiting for transfers between devices: 33.5 us -> 58.2 us
  starting transfers between devices: 32.8 us -> 22.7 us
  local copies, waits for them, and re-layouts: 4.15 us -> 0.14 us
    ppermute x6, waiting for transfers between devices: 15.7 us -> 28.8 us  [shift(): lax.ppermute(x, 'expert', [(i, (i + k) % experts) for i in range(experts)])]
    ppermute x14 -> x13, waiting for transfers between devices: 17.8 us -> 29.4 us  [across(): return lax.ppermute(x, 'tensor', [(i, i ^ j) for i in range(tensor_size)])]
    ppermute x6, starting transfers between devices: 15.3 us -> 6.3 us  [shift(): lax.ppermute(x, 'expert', [(i, (i + k) % experts) for i in range(experts)])]
    unnamed x19 -> x14, local copies, waits for them, and re-layouts: 4.08 us -> 0.07 us
    ppermute x14 -> x13, starting transfers between devices: 16.4 us -> 15.7 us  [across(): return lax.ppermute(x, 'tensor', [(i, i ^ j) for i in range(tensor_size)])]
    pallas_call x6 -> x5, Pallas kernels: 29.9 us -> 29.6 us  [the longest x3 21.5 us: expert_rows(): pl.pallas_call(functools.partial(expert_kernel, first, base, groups, len(...]
    dot_general x2 -> x1, matrix products: 2.58 us -> 2.38 us  [other_halves(): lax.dot_general(rows[:, :, width // 2:], acts, dims, preferred_element_ty...]
  transfers between devices with their start and end apart: 24 -> 22, of which waited for: 8 -> 10; matrix products, arithmetic and copies ran while one was open for 3% -> 0% of each run, Pallas kernels for 22% -> 26%
where the time goes in v7:
time: 116 us; the launch traced here: 115 us
  waiting for transfers between devices  58.2 us (50%)
  Pallas kernels  30.8 us (27%)
  starting transfers between devices  22.7 us (20%)
  matrix products  2.38 us (2%)
    ppermute x13, waiting for transfers between devices, across(): return lax.ppermute(x, 'tensor', [(i, i ^ j) for i in range(tensor_size)])  29.4 us
    ppermute x6, waiting for transfers between devices, shift(): lax.ppermute(x, 'expert', [(i, (i + k) % experts) for i in range(experts)])  28.8 us
    pallas_call x3, Pallas kernels, expert_rows(): pl.pallas_call(functools.partial(expert_kernel, first, base, groups, len(...  21.5 us
    ppermute x13, starting transfers between devices, across(): return lax.ppermute(x, 'tensor', [(i, i ^ j) for i in range(tensor_size)])  15.7 us
    ppermute x6, starting transfers between devices, shift(): lax.ppermute(x, 'expert', [(i, (i + k) % experts) for i in range(experts)])  6.3 us
    pallas_call x1, Pallas kernels, place(): pl.pallas_call(functools.partial(place_kernel, spans, shifts, capacity, o...  4.24 us
    pallas_call x1, Pallas kernels, weight_grads(): pl.pallas_call(weight_grad_kernel, out_shape=[jax.ShapeDtypeStruct((half,...  3.87 us
    dot_general x1, matrix products, other_halves(): lax.dot_general(rows[:, :, width // 2:], acts, dims, preferred_element_ty...  2.38 us
  transfers between devices with their start and end apart: 22, of which 10 were waited for; matrix products, arithmetic and copies ran while one was open for 0% of the time, Pallas kernels for 26%

profile of v7, /device:TPU:0, one launch (start us, length us, event | category | flops | bytes accessed | tf_op | source)
XLA Modules:
  0.0 115.4 jit_solution(10597106406084177138)
XLA Ops:
  1.2 4.2 %place_rows.1 = (bf16[128,1024]{1,0:T(8,128)(2,1)}, bf16[128,1024]{1,0:T(8,128)(2,1)}, bf16[128,1024]{1,0:T(8,128)(2,1)}, bf16[128,2048]{1,0:T(8,128)(2,1)}, bf16[128,2048]{1,0:T(8,128)(2,1)}) custom-call(s32[1,256]{1,0:T(1,128)} %bitcast.34, s32[1,256]{1,0:T(1,128)} %bitcast.36, f32[1,256]{1,0:T(1,128)} %bitcast.38, bf16[256,2048]{1,0:T(8,128)(2,1)} %tokens.1, ...), custom_call_target="tpu_custom_call" | custom-call | flops 1000 | bytes 1000 | tf_op jit(solution)/shard_map/place_rows/pallas_call | solution.py:106
  5.5 3.1 %collective-permute-start = (bf16[128,1024]{1,0:T(8,128)(2,1)}, bf16[128,1024]{1,0:T(8,128)(2,1)S(1)}, u32[]{:S(2)}, u32[]{:S(2)}) collective-permute-start(bf16[128,1024]{1,0:T(8,128)(2,1)} %get-tuple-element.35), channel_id=1, source_target_pairs={{0,2},{2,4},{4,6},{6,0},{1,3},{3,5},{5,7},{7,1},{8,10},{10,12},{12... | collective-permute-start | bytes 786440 | tf_op jit(solution)/shard_map/ppermute | solution.py:287
  8.6 2.1 %collective-permute-start.1 = (bf16[128,1024]{1,0:T(8,128)(2,1)}, bf16[128,1024]{1,0:T(8,128)(2,1)S(1)}, u32[]{:S(2)}, u32[]{:S(2)}) collective-permute-start(bf16[128,1024]{1,0:T(8,128)(2,1)} %get-tuple-element.36), channel_id=1, source_target_pairs={{0,6},{2,0},{4,2},{6,4},{1,7},{3,1},{5,3},{7,5},{8,14},{10,8},{12,... | collective-permute-start | bytes 786440 | tf_op jit(solution)/shard_map/ppermute | solution.py:287
  10.7 0.9 collective-permute-start.2
  11.6 6.3 %collective-permute-done = bf16[128,1024]{1,0:T(8,128)(2,1)S(1)} collective-permute-done((bf16[128,1024]{1,0:T(8,128)(2,1)}, bf16[128,1024]{1,0:T(8,128)(2,1)S(1)}, u32[]{:S(2)}, u32[]{:S(2)}) %collective-permute-start) | collective-permute-done | bytes 262176 | tf_op jit(solution)/shard_map/ppermute | solution.py:287
  18.0 4.4 %collective-permute-done.1 = bf16[128,1024]{1,0:T(8,128)(2,1)S(1)} collective-permute-done((bf16[128,1024]{1,0:T(8,128)(2,1)}, bf16[128,1024]{1,0:T(8,128)(2,1)S(1)}, u32[]{:S(2)}, u32[]{:S(2)}) %collective-permute-start.1) | collective-permute-done | bytes 262176 | tf_op jit(solution)/shard_map/ppermute | solution.py:287
  22.4 11.8 %collective-permute-done.2 = bf16[128,1024]{1,0:T(8,128)(2,1)S(1)} collective-permute-done((bf16[128,1024]{1,0:T(8,128)(2,1)}, bf16[128,1024]{1,0:T(8,128)(2,1)S(1)}, u32[]{:S(2)}, u32[]{:S(2)}) %collective-permute-start.2) | collective-permute-done | bytes 262176 | tf_op jit(solution)/shard_map/ppermute | solution.py:287
  34.2 1.6 %collective-permute-start.5 = (bf16[384,1024]{1,0:T(8,128)(2,1)S(1)}, bf16[384,1024]{1,0:T(8,128)(2,1)S(1)}, u32[]{:S(2)}, u32[]{:S(2)}) collective-permute-start(bf16[384,1024]{1,0:T(8,128)(2,1)S(1)} %constant_dynamic-update-slice_fusion.refs_0_), channel_id=1, source_target_pairs={{0,16},{8,24},{16,0},{24,8},{1,17},{9,25},{17,1},{25,9},{2,18},{10... | collective-permute-start | bytes 2359304 | tf_op jit(solution)/shard_map/ppermute | solution.py:284
  35.8 1.5 %collective-permute-start.7 = (bf16[384,1024]{1,0:T(8,128)(2,1)S(1)}, bf16[384,1024]{1,0:T(8,128)(2,1)S(1)}, u32[]{:S(2)}, u32[]{:S(2)}) collective-permute-start(bf16[384,1024]{1,0:T(8,128)(2,1)S(1)} %constant_dynamic-update-slice_fusion.refs_0_), channel_id=1, source_target_pairs={{0,8},{8,0},{16,24},{24,16},{1,9},{9,1},{17,25},{25,17},{2,10},{10... | collective-permute-start | bytes 2359304 | tf_op jit(solution)/shard_map/ppermute | solution.py:284
  37.3 16.5 %collective-permute-done.5.refs_2_ = bf16[384,1024]{1,0:T(8,128)(2,1)S(1)} collective-permute-done((bf16[384,1024]{1,0:T(8,128)(2,1)S(1)}, bf16[384,1024]{1,0:T(8,128)(2,1)S(1)}, u32[]{:S(2)}, u32[]{:S(2)}) %collective-permute-start.5) | collective-permute-done | bytes 786464 | tf_op jit(solution)/shard_map/ppermute | solution.py:284
  53.8 1.6 %collective-permute-start.6 = (bf16[384,512]{1,0:T(8,128)(2,1)S(1)}, bf16[384,512]{1,0:T(8,128)(2,1)S(1)}, u32[]{:S(2)}, u32[]{:S(2)}) collective-permute-start(bf16[384,512]{1,0:T(8,128)(2,1)S(1)} %slice.60), channel_id=1, source_target_pairs={{0,8},{8,0},{16,24},{24,16},{1,9},{9,1},{17,25},{25,17},{2,10},{10... | collective-permute-start | bytes 1179656 | tf_op jit(solution)/shard_map/ppermute | solution.py:284
  55.4 1.6 %collective-permute-start.8 = (bf16[384,512]{1,0:T(8,128)(2,1)S(1)}, bf16[384,512]{1,0:T(8,128)(2,1)S(1)}, u32[]{:S(2)}, u32[]{:S(2)}) collective-permute-start(bf16[384,512]{1,0:T(8,128)(2,1)S(1)} %slice.61), channel_id=1, source_target_pairs={{0,16},{8,24},{16,0},{24,8},{1,17},{9,25},{17,1},{25,9},{2,18},{10... | collective-permute-start | bytes 1179656 | tf_op jit(solution)/shard_map/ppermute | solution.py:284
  57.0 6.4 %expert_rows.3 = (bf16[2,512,2048]{2,1,0:T(8,128)(2,1)S(1)}, bf16[2,512,1024]{2,1,0:T(8,128)(2,1)S(1)}, bf16[2,128,512]{2,1,0:T(8,128)(2,1)S(1)}, bf16[2,128,512]{2,1,0:T(8,128)(2,1)S(1)}) custom-call(bf16[128,2048]{1,0:T(8,128)(2,1)S(1)} %copy-done.2, bf16[128,2048]{1,0:T(8,128)(2,1)S(1)} %copy-done.3, bf16[1024,1024]{1,0:T(8,128)(2,1)S(1)} %bitcast.27, ...), custom_call_target="tpu_custom_call" | custom-call | flops 1610612736 | bytes 10485760 | tf_op jit(solution)/shard_map/expert_rows/pallas_call | solution.py:193
  63.4 0.6 collective-permute-done.6.refs_3_
  64.1 1.3 %collective-permute-done.8.refs_4_ = bf16[384,512]{1,0:T(8,128)(2,1)S(1)} collective-permute-done((bf16[384,512]{1,0:T(8,128)(2,1)S(1)}, bf16[384,512]{1,0:T(8,128)(2,1)S(1)}, u32[]{:S(2)}, u32[]{:S(2)}) %collective-permute-start.8) | collective-permute-done | bytes 393248 | tf_op jit(solution)/shard_map/ppermute | solution.py:284
  65.4 1.1 collective-permute-start.9
  66.5 8.4 %expert_rows.4 = (bf16[2,512,2048]{2,1,0:T(8,128)(2,1)S(1)}, bf16[2,512,1024]{2,1,0:T(8,128)(2,1)S(1)}, bf16[2,128,512]{2,1,0:T(8,128)(2,1)S(1)}, bf16[2,128,512...) custom-call(bf16[384,1024]{1,0:T(8,128)(2,1)S(1)} %constant_dynamic-, ...), custom_call_target="tpu_custom_call", output_to_operand_aliasing={{0}: (9, {}), {1}: (10, {})} | custom-call | flops 3221225472 | bytes 12582912 | tf_op jit(solution)/shard_map/expert_rows/pallas_call | solution.py:193
  74.8 1.0 collective-permute-start.11
  75.8 1.5 %collective-permute-start.14 = (bf16[2,128,512]{2,1,0:T(8,128)(2,1)S(1)}, bf16[2,128,512]{2,1,0:T(8,128)(2,1)S(1)}, u32[]{:S(2)}, u32[]{:S(2)}) collective-permute-start(bf16[2,128,512]{2,1,0:T(8,128)(2,1)S(1)} %get-tuple-element.48), channel_id=1, source_target_pairs={{0,16},{8,24},{16,0},{24,8},{1,17},{9,25},{17,1},{25,9},{2,18},{10... | collective-permute-start | bytes 786440 | tf_op jit(solution)/shard_map/ppermute | solution.py:284
  77.4 6.7 %expert_rows.5 = (bf16[2,512,2048]{2,1,0:T(8,128)(2,1)S(1)}, bf16[2,512,1024]{2,1,0:T(8,128)(2,1)S(1)}, bf16[128,512]{1,0:T(8,128)(2,1)S(1)}, bf16[128,512]{1,0:...) custom-call(bf16[384,1024]{1,0:T(8,128)(2,1)S(1)} %constant_dynamic-, ...), custom_call_target="tpu_custom_call", output_to_operand_aliasing={{0}: (9, {}), {1}: (10, {})} | custom-call | flops 1610612736 | bytes 10485760 | tf_op jit(solution)/shard_map/expert_rows/pallas_call | solution.py:193
  84.1 2.4 %convolution_convert_fusion = bf16[2,1024,1024]{2,1,0:T(8,128)(2,1)S(1)} fusion(bf16[2,512,1024]{2,1,0:T(8,128)(2,1)S(1)} %get-tuple-element.61.acts, bf16[2,512,2048]{2,1,0:T(8,128)(2,1)S(1)} %get-tuple-element.59.rows), kind=kOutput, calls=%fused_computation | convolution fusion | flops 2149580800 | bytes 8388608 | tf_op jit(solution)/shard_map/dot_general | solution.py:313
  86.6 0.6 collective-permute-start.10
  87.2 1.6 %collective-permute-start.12 = (bf16[128,512]{1,0:T(8,128)(2,1)S(1)}, bf16[128,512]{1,0:T(8,128)(2,1)S(1)}, u32[]{:S(2)}, u32[]{:S(2)}) collective-permute-start(bf16[128,512]{1,0:T(8,128)(2,1)S(1)} %fusion.5), channel_id=1, source_target_pairs={{0,16},{8,24},{16,0},{24,8},{1,17},{9,25},{17,1},{25,9},{2,18},{10... | collective-permute-start | bytes 393224 | tf_op jit(solution)/shard_map/ppermute | solution.py:284
  88.8 0.6 collective-permute-start.15
  89.4 1.4 %collective-permute-start.19 = (bf16[128,512]{1,0:T(8,128)(2,1)S(1)}, bf16[128,512]{1,0:T(8,128)(2,1)S(1)}, u32[]{:S(2)}, u32[]{:S(2)}) collective-permute-start(bf16[128,512]{1,0:T(8,128)(2,1)S(1)} %get-tuple-element.58), channel_id=1, source_target_pairs={{0,24},{8,16},{16,8},{24,0},{1,25},{9,17},{17,9},{25,1},{2,26},{10... | collective-permute-start | bytes 393224 | tf_op jit(solution)/shard_map/ppermute | solution.py:284
  90.9 7.3 %collective-permute-done.12 = bf16[128,512]{1,0:T(8,128)(2,1)S(1)} collective-permute-done((bf16[128,512]{1,0:T(8,128)(2,1)S(1)}, bf16[128,512]{1,0:T(8,128)(2,1)S(1)}, u32[]{:S(2)}, u32[]{:S(2)}) %collective-permute-start.12) | collective-permute-done | bytes 131104 | tf_op jit(solution)/shard_map/ppermute | solution.py:284
  98.2 0.5 collective-permute-start.18
  98.7 1.2 %collective-permute-start.17 = (bf16[128,512]{1,0:T(8,128)(2,1)S(1)}, bf16[128,512]{1,0:T(8,128)(2,1)S(1)}, u32[]{:S(2)}, u32[]{:S(2)}) collective-permute-start(bf16[128,512]{1,0:T(8,128)(2,1)S(1)} %get-tuple-element.54), channel_id=1, source_target_pairs={{0,8},{8,0},{16,24},{24,16},{1,9},{9,1},{17,25},{25,17},{2,10},{10... | collective-permute-start | bytes 393224 | tf_op jit(solution)/shard_map/ppermute | solution.py:284
  100.0 3.2 %collective-permute-done.18 = bf16[128,512]{1,0:T(8,128)(2,1)S(1)} collective-permute-done((bf16[128,512]{1,0:T(8,128)(2,1)S(1)}, bf16[128,512]{1,0:T(8,128)(2,1)S(1)}, u32[]{:S(2)}, u32[]{:S(2)}) %collective-permute-start.18) | collective-permute-done | bytes 131104 | tf_op jit(solution)/shard_map/ppermute | solution.py:284
  104.1 3.9 %weight_grads.1 = (bf16[1024,1024]{1,0:T(8,128)(2,1)}, bf16[1024,1024]{1,0:T(8,128)(2,1)}) custom-call(bf16[2,512,2048]{2,1,0:T(8,128)(2,1)S(1)} %get-tuple-element.59.rows, bf16[2,512,1024]{2,1,0:T(8,128)(2,1)S(1)} %get-tuple-element.61.acts, bf16[2,1024,1024]{2,1,0:T(8,128)(2,1)S(1)} %collective-permute-done.21.got), custom_call_target="tpu_custom_call" | custom-call | flops 1000 | bytes 1000 | tf_op jit(solution)/shard_map/weight_grads/pallas_call | solution.py:256
  107.9 6.2 %collective-permute-done.20.refs_3_ = bf16[128,512]{1,0:T(8,128)(2,1)S(1)} collective-permute-done((bf16[128,512]{1,0:T(8,128)(2,1)S(1)}, bf16[128,512]{1,0:T(8,128)(2,1)S(1)}, u32[]{:S(2)}, u32[]{:S(2)}) %collective-permute-start.20) | collective-permute-done | bytes 131104 | tf_op jit(solution)/shard_map/ppermute | solution.py:287
  114.2 1.2 %unplace_rows.1 = bf16[256,512]{1,0:T(8,128)(2,1)} custom-call(s32[1,256]{1,0:T(1,128)S(1)} %bitcast.35, s32[1,256]{1,0:T(1,128)S(1)} %bitcast.37, bf16[128,512]{1,0:T(8,128)(2,1)S(1)} %fusion.3.refs_0_, bf16[128,512]{1,0:T(8,128)(2,1)S(1)} %collective-permute-done.13.refs_1_, bf16[128,512]{1,0:T(8,128)(2,1)S(1)} %collective-permute-done.16.refs_2_, ...), custom_call_target="tpu_custom_call" | custom-call | flops 1000 | bytes 1000 | tf_op jit(solution)/shard_map/unplace_rows/pallas_call | solution.py:228
  (43 shorter events, 1.9 us)
Async XLA Ops:
  0.6 56.3 %collective-permute-start.3 = (bf16[1024,1024]{1,0:T(8,128)(2,1)}, bf16[1024,1024]{1,0:T(8,128)(2,1)S(1)}, u32[]{:S(2)}, u32[]{:S(2)}) collective-permute-start(bf16[1024,1024]{1,0:T(8,128)(2,1)} %bitcast.26), channel_id=1, source_target_pairs={{0,1},{1,0},{2,3},{3,2},{4,5},{5,4},{6,7},{7,6},{8,9},{9,8},{10,11... | collective-permute-start | bytes 6291464 | tf_op jit(solution)/shard_map/ppermute | solution.py:281
  1.1 55.8 %collective-permute-start.4 = (bf16[1024,1024]{1,0:T(8,128)(2,1)}, bf16[1024,1024]{1,0:T(8,128)(2,1)S(1)}, u32[]{:S(2)}, u32[]{:S(2)}) collective-permute-start(bf16[1024,1024]{1,0:T(8,128)(2,1)} %bitcast.30), channel_id=1, source_target_pairs={{0,1},{1,0},{2,3},{3,2},{4,5},{5,4},{6,7},{7,6},{8,9},{9,8},{10,11... | collective-permute-start | bytes 6291464 | tf_op jit(solution)/shard_map/ppermute | solution.py:281
  1.2 55.7 %copy-start.1 = (bf16[1,1024,1024]{2,1,0:T(8,128)(2,1)S(1)}, bf16[1,1024,1024]{2,1,0:T(8,128)(2,1)}, u32[]{:S(2)}) copy-start(bf16[1,1024,1024]{2,1,0:T(8,128)(2,1)} %param.13) | copy-start | bytes 6291460
  5.5 51.5 %copy-start = (bf16[1,1024,1024]{2,1,0:T(8,128)(2,1)S(1)}, bf16[1,1024,1024]{2,1,0:T(8,128)(2,1)}, u32[]{:S(2)}) copy-start(bf16[1,1024,1024]{2,1,0:T(8,128)(2,1)} %param.12) | copy-start | bytes 6291460
  5.5 51.5 %copy-start.2 = (bf16[128,2048]{1,0:T(8,128)(2,1)S(1)}, bf16[128,2048]{1,0:T(8,128)(2,1)}, u32[]{:S(2)}) copy-start(bf16[128,2048]{1,0:T(8,128)(2,1)} %get-tuple-element.38.refs_0_) | copy-start | bytes 1572868
  5.5 51.5 %copy-start.3 = (bf16[128,2048]{1,0:T(8,128)(2,1)S(1)}, bf16[128,2048]{1,0:T(8,128)(2,1)}, u32[]{:S(2)}) copy-start(bf16[128,2048]{1,0:T(8,128)(2,1)} %get-tuple-element.39.refs_1_) | copy-start | bytes 1572868
  5.5 12.4 %collective-permute-start = (bf16[128,1024]{1,0:T(8,128)(2,1)}, bf16[128,1024]{1,0:T(8,128)(2,1)S(1)}, u32[]{:S(2)}, u32[]{:S(2)}) collective-permute-start(bf16[128,1024]{1,0:T(8,128)(2,1)} %get-tuple-element.35), channel_id=1, source_target_pairs={{0,2},{2,4},{4,6},{6,0},{1,3},{3,5},{5,7},{7,1},{8,10},{10,12},{12... | collective-permute-start | bytes 786440 | tf_op jit(solution)/shard_map/ppermute | solution.py:287
  8.6 13.8 %collective-permute-start.1 = (bf16[128,1024]{1,0:T(8,128)(2,1)}, bf16[128,1024]{1,0:T(8,128)(2,1)S(1)}, u32[]{:S(2)}, u32[]{:S(2)}) collective-permute-start(bf16[128,1024]{1,0:T(8,128)(2,1)} %get-tuple-element.36), channel_id=1, source_target_pairs={{0,6},{2,0},{4,2},{6,4},{1,7},{3,1},{5,3},{7,5},{8,14},{10,8},{12,... | collective-permute-start | bytes 786440 | tf_op jit(solution)/shard_map/ppermute | solution.py:287
  10.7 23.5 %collective-permute-start.2 = (bf16[128,1024]{1,0:T(8,128)(2,1)}, bf16[128,1024]{1,0:T(8,128)(2,1)S(1)}, u32[]{:S(2)}, u32[]{:S(2)}) collective-permute-start(bf16[128,1024]{1,0:T(8,128)(2,1)} %get-tuple-element.37), channel_id=1, source_target_pairs={{0,4},{2,6},{4,0},{6,2},{1,5},{3,7},{5,1},{7,3},{8,12},{10,14},{12... | collective-permute-start | bytes 786440 | tf_op jit(solution)/shard_map/ppermute | solution.py:287
  34.2 19.5 %collective-permute-start.5 = (bf16[384,1024]{1,0:T(8,128)(2,1)S(1)}, bf16[384,1024]{1,0:T(8,128)(2,1)S(1)}, u32[]{:S(2)}, u32[]{:S(2)}) collective-permute-start(bf16[384,1024]{1,0:T(8,128)(2,1)S(1)} %constant_dynamic-update-slice_fusion.refs_0_), channel_id=1, source_target_pairs={{0,16},{8,24},{16,0},{24,8},{1,17},{9,25},{17,1},{25,9},{2,18},{10... | collective-permute-start | bytes 2359304 | tf_op jit(solution)/shard_map/ppermute | solution.py:284
  35.8 19.5 %collective-permute-start.7 = (bf16[384,1024]{1,0:T(8,128)(2,1)S(1)}, bf16[384,1024]{1,0:T(8,128)(2,1)S(1)}, u32[]{:S(2)}, u32[]{:S(2)}) collective-permute-start(bf16[384,1024]{1,0:T(8,128)(2,1)S(1)} %constant_dynamic-update-slice_fusion.refs_0_), channel_id=1, source_target_pairs={{0,8},{8,0},{16,24},{24,16},{1,9},{9,1},{17,25},{25,17},{2,10},{10... | collective-permute-start | bytes 2359304 | tf_op jit(solution)/shard_map/ppermute | solution.py:284
  53.8 10.3 %collective-permute-start.6 = (bf16[384,512]{1,0:T(8,128)(2,1)S(1)}, bf16[384,512]{1,0:T(8,128)(2,1)S(1)}, u32[]{:S(2)}, u32[]{:S(2)}) collective-permute-start(bf16[384,512]{1,0:T(8,128)(2,1)S(1)} %slice.60), channel_id=1, source_target_pairs={{0,8},{8,0},{16,24},{24,16},{1,9},{9,1},{17,25},{25,17},{2,10},{10... | collective-permute-start | bytes 1179656 | tf_op jit(solution)/shard_map/ppermute | solution.py:284
  55.4 10.0 %collective-permute-start.8 = (bf16[384,512]{1,0:T(8,128)(2,1)S(1)}, bf16[384,512]{1,0:T(8,128)(2,1)S(1)}, u32[]{:S(2)}, u32[]{:S(2)}) collective-permute-start(bf16[384,512]{1,0:T(8,128)(2,1)S(1)} %slice.61), channel_id=1, source_target_pairs={{0,16},{8,24},{16,0},{24,8},{1,17},{9,25},{17,1},{25,9},{2,18},{10... | collective-permute-start | bytes 1179656 | tf_op jit(solution)/shard_map/ppermute | solution.py:284
  65.4 12.0 %collective-permute-start.9 = (bf16[2,128,512]{2,1,0:T(8,128)(2,1)S(1)}, bf16[2,128,512]{2,1,0:T(8,128)(2,1)S(1)}, u32[]{:S(2)}, u32[]{:S(2)}) collective-permute-start(bf16[2,128,512]{2,1,0:T(8,128)(2,1)S(1)} %get-tuple-element.42), channel_id=1, source_target_pairs={{0,8},{8,0},{16,24},{24,16},{1,9},{9,1},{17,25},{25,17},{2,10},{10... | collective-permute-start | bytes 786440 | tf_op jit(solution)/shard_map/ppermute | solution.py:284
  74.8 9.2 %collective-permute-start.11 = (bf16[2,128,512]{2,1,0:T(8,128)(2,1)S(1)}, bf16[2,128,512]{2,1,0:T(8,128)(2,1)S(1)}, u32[]{:S(2)}, u32[]{:S(2)}) collective-permute-start(bf16[2,128,512]{2,1,0:T(8,128)(2,1)S(1)} %get-tuple-element.46), channel_id=1, source_target_pairs={{0,8},{8,0},{16,24},{24,16},{1,9},{9,1},{17,25},{25,17},{2,10},{10... | collective-permute-start | bytes 786440 | tf_op jit(solution)/shard_map/ppermute | solution.py:284
  75.8 8.2 %collective-permute-start.14 = (bf16[2,128,512]{2,1,0:T(8,128)(2,1)S(1)}, bf16[2,128,512]{2,1,0:T(8,128)(2,1)S(1)}, u32[]{:S(2)}, u32[]{:S(2)}) collective-permute-start(bf16[2,128,512]{2,1,0:T(8,128)(2,1)S(1)} %get-tuple-element.48), channel_id=1, source_target_pairs={{0,16},{8,24},{16,0},{24,8},{1,17},{9,25},{17,1},{25,9},{2,18},{10... | collective-permute-start | bytes 786440 | tf_op jit(solution)/shard_map/ppermute | solution.py:284
  86.5 17.6 %collective-permute-start.21 = (bf16[2,1024,1024]{2,1,0:T(8,128)(2,1)S(1)}, bf16[2,1024,1024]{2,1,0:T(8,128)(2,1)S(1)}, u32[]{:S(2)}, u32[]{:S(2)}) collective-permute-start(bf16[2,1024,1024]{2,1,0:T(8,128)(2,1)S(1)} %convolution_convert_fusion), channel_id=1, source_target_pairs={{0,1},{1,0},{2,3},{3,2},{4,5},{5,4},{6,7},{7,6},{8,9},{9,8},{10,11... | collective-permute-start | bytes 12582920 | tf_op jit(solution)/shard_map/ppermute | solution.py:281
  86.6 17.4 %collective-permute-start.10 = (bf16[128,512]{1,0:T(8,128)(2,1)S(1)}, bf16[128,512]{1,0:T(8,128)(2,1)S(1)}, u32[]{:S(2)}, u32[]{:S(2)}) collective-permute-start(bf16[128,512]{1,0:T(8,128)(2,1)S(1)} %fusion.4), channel_id=1, source_target_pairs={{0,16},{8,24},{16,0},{24,8},{1,17},{9,25},{17,1},{25,9},{2,18},{10... | collective-permute-start | bytes 393224 | tf_op jit(solution)/shard_map/ppermute | solution.py:284
  87.2 11.0 %collective-permute-start.12 = (bf16[128,512]{1,0:T(8,128)(2,1)S(1)}, bf16[128,512]{1,0:T(8,128)(2,1)S(1)}, u32[]{:S(2)}, u32[]{:S(2)}) collective-permute-start(bf16[128,512]{1,0:T(8,128)(2,1)S(1)} %fusion.5), channel_id=1, source_target_pairs={{0,16},{8,24},{16,0},{24,8},{1,17},{9,25},{17,1},{25,9},{2,18},{10... | collective-permute-start | bytes 393224 | tf_op jit(solution)/shard_map/ppermute | solution.py:284
  88.8 9.9 %collective-permute-start.15 = (bf16[128,512]{1,0:T(8,128)(2,1)S(1)}, bf16[128,512]{1,0:T(8,128)(2,1)S(1)}, u32[]{:S(2)}, u32[]{:S(2)}) collective-permute-start(bf16[128,512]{1,0:T(8,128)(2,1)S(1)} %fusion.6), channel_id=1, source_target_pairs={{0,8},{8,0},{16,24},{24,16},{1,9},{9,1},{17,25},{25,17},{2,10},{10... | collective-permute-start | bytes 393224 | tf_op jit(solution)/shard_map/ppermute | solution.py:284
  89.4 10.5 %collective-permute-start.19 = (bf16[128,512]{1,0:T(8,128)(2,1)S(1)}, bf16[128,512]{1,0:T(8,128)(2,1)S(1)}, u32[]{:S(2)}, u32[]{:S(2)}) collective-permute-start(bf16[128,512]{1,0:T(8,128)(2,1)S(1)} %get-tuple-element.58), channel_id=1, source_target_pairs={{0,24},{8,16},{16,8},{24,0},{1,25},{9,17},{17,9},{25,1},{2,26},{10... | collective-permute-start | bytes 393224 | tf_op jit(solution)/shard_map/ppermute | solution.py:284
  98.2 5.1 %collective-permute-start.18 = (bf16[128,512]{1,0:T(8,128)(2,1)S(1)}, bf16[128,512]{1,0:T(8,128)(2,1)S(1)}, u32[]{:S(2)}, u32[]{:S(2)}) collective-permute-start(bf16[128,512]{1,0:T(8,128)(2,1)S(1)} %get-tuple-element.56), channel_id=1, source_target_pairs={{0,16},{8,24},{16,0},{24,8},{1,17},{9,25},{17,1},{25,9},{2,18},{10... | collective-permute-start | bytes 393224 | tf_op jit(solution)/shard_map/ppermute | solution.py:284
  98.7 5.0 %collective-permute-start.17 = (bf16[128,512]{1,0:T(8,128)(2,1)S(1)}, bf16[128,512]{1,0:T(8,128)(2,1)S(1)}, u32[]{:S(2)}, u32[]{:S(2)}) collective-permute-start(bf16[128,512]{1,0:T(8,128)(2,1)S(1)} %get-tuple-element.54), channel_id=1, source_target_pairs={{0,8},{8,0},{16,24},{24,16},{1,9},{9,1},{17,25},{25,17},{2,10},{10... | collective-permute-start | bytes 393224 | tf_op jit(solution)/shard_map/ppermute | solution.py:284
  100.0 14.2 %collective-permute-start.13 = (bf16[128,512]{1,0:T(8,128)(2,1)S(1)}, bf16[128,512]{1,0:T(8,128)(2,1)S(1)}, u32[]{:S(2)}, u32[]{:S(2)}) collective-permute-start(bf16[128,512]{1,0:T(8,128)(2,1)S(1)} %fusion.2), channel_id=1, source_target_pairs={{0,6},{2,0},{4,2},{6,4},{1,7},{3,1},{5,3},{7,5},{8,14},{10,8},{12,... | collective-permute-start | bytes 393224 | tf_op jit(solution)/shard_map/ppermute | solution.py:287
  103.3 10.9 %collective-permute-start.16 = (bf16[128,512]{1,0:T(8,128)(2,1)S(1)}, bf16[128,512]{1,0:T(8,128)(2,1)S(1)}, u32[]{:S(2)}, u32[]{:S(2)}) collective-permute-start(bf16[128,512]{1,0:T(8,128)(2,1)S(1)} %fusion.1), channel_id=1, source_target_pairs={{0,2},{2,4},{4,6},{6,0},{1,3},{3,5},{5,7},{7,1},{8,10},{10,12},{12... | collective-permute-start | bytes 393224 | tf_op jit(solution)/shard_map/ppermute | solution.py:287
  103.8 10.3 %collective-permute-start.20 = (bf16[128,512]{1,0:T(8,128)(2,1)S(1)}, bf16[128,512]{1,0:T(8,128)(2,1)S(1)}, u32[]{:S(2)}, u32[]{:S(2)}) collective-permute-start(bf16[128,512]{1,0:T(8,128)(2,1)S(1)} %add_convert_fusion), channel_id=1, source_target_pairs={{0,4},{2,6},{4,0},{6,2},{1,5},{3,7},{5,1},{7,3},{8,12},{10,14},{12... | collective-permute-start | bytes 393224 | tf_op jit(solution)/shard_map/ppermute | solution.py:287
  104.0 10.1 %copy-start.4 = (s32[256,1]{0,1:T(1,128)S(1)}, s32[256,1]{0,1:T(1,128)}, u32[]{:S(2)}) copy-start(s32[256,1]{0,1:T(1,128)} %param.10) | copy-start | bytes 3076
  104.0 10.1 %copy-start.5 = (s32[256,1]{0,1:T(1,128)S(1)}, s32[256,1]{0,1:T(1,128)}, u32[]{:S(2)}) copy-start(s32[256,1]{0,1:T(1,128)} %param.11) | copy-start | bytes 3076

commit v8 on v7

--- a/solution.py
+++ b/solution.py
@@ -322,16 +322,17 @@
         placed = place([capacity] * 3, shifts, capacity, True, index, slot, gate, tokens, grad_output)
         moved = [shift(rows, k) for rows, k in zip(placed, shifts)]
         everything = 4 * capacity
-        slots = spread(jnp.concatenate(moved, 0))
-        own = [after(placed[3], *moved), placed[4]]
-        kept, (pair,) = expert_rows(own, None, [(capacity, 1)], weights, everything, 0, None)
-        back, got_own = collect_pair([pair[0], after(pair[1], *slots[3:])], 1)
+        kept, (pair,) = expert_rows(placed[3:], None, [(capacity, 1)], weights, everything, 0, None)
+        near = spread(jnp.concatenate([after(moved[0], pair[0]), moved[1]], 0))
+        far = spread(after(moved[2], *near[1:3]))
+        near[0] = after(near[0], *far[1:3])
+        back, got_own = collect_pair([pair[0], after(pair[1], *near[3:])], 1)
         backs = [back]
-        kept, pairs = expert_rows(slots, 0, [(capacity, 1), (capacity, 2)], weights, everything, capacity, kept)
+        kept, pairs = expert_rows(near, 0, [(capacity, 1), (capacity, 2)], weights, everything, capacity, kept)
         (one, got_one), (three, got_three) = collect_pair(pairs[0], 1), collect_pair(pairs[1], 2)
         backs += [shift(one, -1), shift(three, -3)]
         kept, (blocks,) = expert_rows(
-            [after(slots[0], got_own)] + slots[1:], 2 * capacity, [(capacity, None)], weights, everything, 3 * capacity, kept
+            [after(far[0], got_own)] + far[1:], 0, [(capacity, None)], weights, everything, 3 * capacity, kept
         )
         others = other_halves([kept[0], after(kept[1], got_one, got_three)])
         grads = weight_grads(*kept, swap(others))

time: 116 us -> 103 us (0.89)
  waiting for transfers between devices: 58.2 us -> 33.3 us
  starting transfers between devices: 22.7 us -> 31.7 us
  local copies, waits for them, and re-layouts: 0.14 us -> 3.79 us
    ppermute x6, waiting for transfers between devices: 28.8 us -> 6.96 us  [shift(): lax.ppermute(x, 'expert', [(i, (i + k) % experts) for i in range(experts)])]
    ppermute x13 -> x17, starting transfers between devices: 15.7 us -> 20.7 us  [across(): return lax.ppermute(x, 'tensor', [(i, i ^ j) for i in range(tensor_size)])]
    ppermute x6, starting transfers between devices: 6.3 us -> 10.3 us  [shift(): lax.ppermute(x, 'expert', [(i, (i + k) % experts) for i in range(experts)])]
    unnamed x14 -> x17, local copies, waits for them, and re-layouts: 0.07 us -> 3.71 us
    ppermute x13 -> x17, waiting for transfers between devices: 29.4 us -> 26.4 us  [across(): return lax.ppermute(x, 'tensor', [(i, i ^ j) for i in range(tensor_size)])]
  transfers between devices with their start and end apart: 22 -> 26, of which waited for: 10 -> 9; matrix products, arithmetic and copies ran while one was open for 0% -> 0% of each run, Pallas kernels for 26% -> 29%
where the time goes in v8:
time: 103 us
  waiting for transfers between devices  33.3 us (32%)
  starting transfers between devices  31.7 us (31%)
  Pallas kernels  30.5 us (30%)
  local copies, waits for them, and re-layouts  3.79 us (4%)
  matrix products  2.38 us (2%)
    ppermute x17, waiting for transfers between devices, across(): return lax.ppermute(x, 'tensor', [(i, i ^ j) for i in range(tensor_size)])  26.4 us
    pallas_call x3, Pallas kernels, expert_rows(): pl.pallas_call(functools.partial(expert_kernel, first, base, groups, len(...  21.4 us
    ppermute x17, starting transfers between devices, across(): return lax.ppermute(x, 'tensor', [(i, i ^ j) for i in range(tensor_size)])  20.7 us
    ppermute x6, starting transfers between devices, shift(): lax.ppermute(x, 'expert', [(i, (i + k) % experts) for i in range(experts)])  10.3 us
    ppermute x6, waiting for transfers between devices, shift(): lax.ppermute(x, 'expert', [(i, (i + k) % experts) for i in range(experts)])  6.96 us
    pallas_call x1, Pallas kernels, place(): pl.pallas_call(functools.partial(place_kernel, spans, shifts, capacity, o...  4.13 us
    pallas_call x1, Pallas kernels, weight_grads(): pl.pallas_call(weight_grad_kernel, out_shape=[jax.ShapeDtypeStruct((half,...  3.87 us
    unnamed x17, local copies, waits for them, and re-layouts  3.71 us
  transfers between devices with their start and end apart: 26, of which 9 were waited for; matrix products, arithmetic and copies ran while one was open for 0% of the time, Pallas kernels for 29%

profile of v8, /device:TPU:0, one launch (start us, length us, event | category | flops | bytes accessed | tf_op | source)
XLA Modules:
  0.0 102.9 jit_solution(1317195530475008221)
XLA Ops:
  1.2 4.1 %place_rows.1 = (bf16[128,1024]{1,0:T(8,128)(2,1)}, bf16[128,1024]{1,0:T(8,128)(2,1)}, bf16[128,1024]{1,0:T(8,128)(2,1)}, bf16[128,2048]{1,0:T(8,128)(2,1)}, bf16[128,2048]{1,0:T(8,128)(2,1)}) custom-call(s32[1,256]{1,0:T(1,128)} %bitcast.34, s32[1,256]{1,0:T(1,128)} %bitcast.36, f32[1,256]{1,0:T(1,128)} %bitcast.38, bf16[256,2048]{1,0:T(8,128)(2,1)} %tokens.1, ...), custom_call_target="tpu_custom_call" | custom-call | flops 1000 | bytes 1000 | tf_op jit(solution)/shard_map/place_rows/pallas_call | solution.py:106
  5.4 3.1 %collective-permute-start.2 = (bf16[128,1024]{1,0:T(8,128)(2,1)}, bf16[128,1024]{1,0:T(8,128)(2,1)S(1)}, u32[]{:S(2)}, u32[]{:S(2)}) collective-permute-start(bf16[128,1024]{1,0:T(8,128)(2,1)} %get-tuple-element.40), channel_id=1, source_target_pairs={{0,2},{2,4},{4,6},{6,0},{1,3},{3,5},{5,7},{7,1},{8,10},{10,12},{12... | collective-permute-start | bytes 786440 | tf_op jit(solution)/shard_map/ppermute | solution.py:287
  8.4 2.1 %collective-permute-start.3 = (bf16[128,1024]{1,0:T(8,128)(2,1)}, bf16[128,1024]{1,0:T(8,128)(2,1)S(1)}, u32[]{:S(2)}, u32[]{:S(2)}) collective-permute-start(bf16[128,1024]{1,0:T(8,128)(2,1)} %get-tuple-element.42), channel_id=1, source_target_pairs={{0,6},{2,0},{4,2},{6,4},{1,7},{3,1},{5,3},{7,5},{8,14},{10,8},{12,... | collective-permute-start | bytes 786440 | tf_op jit(solution)/shard_map/ppermute | solution.py:287
  10.6 1.6 %copy-done.1 = bf16[1,1024,1024]{2,1,0:T(8,128)(2,1)S(1)} copy-done((bf16[1,1024,1024]{2,1,0:T(8,128)(2,1)S(1)}, bf16[1,1024,1024]{2,1,0:T(8,128)(2,1)}, u32[]{:S(2)}) %copy-start.1) | copy-done | bytes 2097176
  14.2 6.3 %expert_rows.3 = (bf16[2,512,2048]{2,1,0:T(8,128)(2,1)S(1)}, bf16[2,512,1024]{2,1,0:T(8,128)(2,1)S(1)}, bf16[2,128,512]{2,1,0:T(8,128)(2,1)S(1)}, bf16[2,128,512]{2,1,0:T(8,128)(2,1)S(1)}) custom-call(bf16[128,2048]{1,0:T(8,128)(2,1)S(1)} %copy-done.3, bf16[128,2048]{1,0:T(8,128)(2,1)S(1)} %copy-done.4, bf16[1024,1024]{1,0:T(8,128)(2,1)S(1)} %bitcast.27, ...), custom_call_target="tpu_custom_call" | custom-call | flops 1610612736 | bytes 10485760 | tf_op jit(solution)/shard_map/expert_rows/pallas_call | solution.py:193
  20.6 1.6 %collective-permute-done.3 = bf16[128,1024]{1,0:T(8,128)(2,1)S(1)} collective-permute-done((bf16[128,1024]{1,0:T(8,128)(2,1)}, bf16[128,1024]{1,0:T(8,128)(2,1)S(1)}, u32[]{:S(2)}, u32[]{:S(2)}) %collective-permute-start.3) | collective-permute-done | bytes 262176 | tf_op jit(solution)/shard_map/ppermute | solution.py:287
  22.3 1.6 %collective-permute-start.6 = (bf16[256,1024]{1,0:T(8,128)(2,1)S(1)}, bf16[256,1024]{1,0:T(8,128)(2,1)S(1)}, u32[]{:S(2)}, u32[]{:S(2)}) collective-permute-start(bf16[256,1024]{1,0:T(8,128)(2,1)S(1)} %constant_dynamic-update-slice_fusion.refs_0_), channel_id=1, source_target_pairs={{0,8},{8,0},{16,24},{24,16},{1,9},{9,1},{17,25},{25,17},{2,10},{10... | collective-permute-start | bytes 1572872 | tf_op jit(solution)/shard_map/ppermute | solution.py:284
  23.8 1.5 %collective-permute-start.4 = (bf16[256,1024]{1,0:T(8,128)(2,1)S(1)}, bf16[256,1024]{1,0:T(8,128)(2,1)S(1)}, u32[]{:S(2)}, u32[]{:S(2)}) collective-permute-start(bf16[256,1024]{1,0:T(8,128)(2,1)S(1)} %constant_dynamic-update-slice_fusion.refs_0_), channel_id=1, source_target_pairs={{0,16},{8,24},{16,0},{24,8},{1,17},{9,25},{17,1},{25,9},{2,18},{10... | collective-permute-start | bytes 1572872 | tf_op jit(solution)/shard_map/ppermute | solution.py:284
  25.3 1.3 %collective-permute-start.10 = (bf16[128,1024]{1,0:T(8,128)(2,1)S(1)}, bf16[128,1024]{1,0:T(8,128)(2,1)S(1)}, u32[]{:S(2)}, u32[]{:S(2)}) collective-permute-start(bf16[128,1024]{1,0:T(8,128)(2,1)S(1)} %copy-done.7), channel_id=1, source_target_pairs={{0,4},{2,6},{4,0},{6,2},{1,5},{3,7},{5,1},{7,3},{8,12},{10,14},{12... | collective-permute-start | bytes 786440 | tf_op jit(solution)/shard_map/ppermute | solution.py:287
  26.7 8.9 %collective-permute-done.6.refs_1_ = bf16[256,1024]{1,0:T(8,128)(2,1)S(1)} collective-permute-done((bf16[256,1024]{1,0:T(8,128)(2,1)S(1)}, bf16[256,1024]{1,0:T(8,128)(2,1)S(1)}, u32[]{:S(2)}, u32[]{:S(2)}) %collective-permute-start.6) | collective-permute-done | bytes 524320 | tf_op jit(solution)/shard_map/ppermute | solution.py:284
  35.6 1.6 %collective-permute-start.7 = (bf16[256,512]{1,0:T(8,128)(2,1)S(1)}, bf16[256,512]{1,0:T(8,128)(2,1)S(1)}, u32[]{:S(2)}, u32[]{:S(2)}) collective-permute-start(bf16[256,512]{1,0:T(8,128)(2,1)S(1)} %slice.69), channel_id=1, source_target_pairs={{0,16},{8,24},{16,0},{24,8},{1,17},{9,25},{17,1},{25,9},{2,18},{10... | collective-permute-start | bytes 786440 | tf_op jit(solution)/shard_map/ppermute | solution.py:284
  37.2 1.6 %collective-permute-start.5 = (bf16[256,512]{1,0:T(8,128)(2,1)S(1)}, bf16[256,512]{1,0:T(8,128)(2,1)S(1)}, u32[]{:S(2)}, u32[]{:S(2)}) collective-permute-start(bf16[256,512]{1,0:T(8,128)(2,1)S(1)} %slice.68), channel_id=1, source_target_pairs={{0,8},{8,0},{16,24},{24,16},{1,9},{9,1},{17,25},{25,17},{2,10},{10... | collective-permute-start | bytes 786440 | tf_op jit(solution)/shard_map/ppermute | solution.py:284
  40.4 4.1 %collective-permute-done.7.refs_4_ = bf16[256,512]{1,0:T(8,128)(2,1)S(1)} collective-permute-done((bf16[256,512]{1,0:T(8,128)(2,1)S(1)}, bf16[256,512]{1,0:T(8,128)(2,1)S(1)}, u32[]{:S(2)}, u32[]{:S(2)}) %collective-permute-start.7) | collective-permute-done | bytes 262176 | tf_op jit(solution)/shard_map/ppermute | solution.py:284
  44.5 2.0 %collective-permute-done.5.refs_3_ = bf16[256,512]{1,0:T(8,128)(2,1)S(1)} collective-permute-done((bf16[256,512]{1,0:T(8,128)(2,1)S(1)}, bf16[256,512]{1,0:T(8,128)(2,1)S(1)}, u32[]{:S(2)}, u32[]{:S(2)}) %collective-permute-start.5) | collective-permute-done | bytes 262176 | tf_op jit(solution)/shard_map/ppermute | solution.py:284
  46.5 1.5 %collective-permute-start.8 = (bf16[2,128,512]{2,1,0:T(8,128)(2,1)S(1)}, bf16[2,128,512]{2,1,0:T(8,128)(2,1)S(1)}, u32[]{:S(2)}, u32[]{:S(2)}) collective-permute-start(bf16[2,128,512]{2,1,0:T(8,128)(2,1)S(1)} %get-tuple-element.43), channel_id=1, source_target_pairs={{0,8},{8,0},{16,24},{24,16},{1,9},{9,1},{17,25},{25,17},{2,10},{10... | collective-permute-start | bytes 786440 | tf_op jit(solution)/shard_map/ppermute | solution.py:284
  48.0 1.5 %collective-permute-start.19 = (bf16[128,512]{1,0:T(8,128)(2,1)S(1)}, bf16[128,512]{1,0:T(8,128)(2,1)S(1)}, u32[]{:S(2)}, u32[]{:S(2)}) collective-permute-start(bf16[128,512]{1,0:T(8,128)(2,1)S(1)} %slice.76), channel_id=1, source_target_pairs={{0,8},{8,0},{16,24},{24,16},{1,9},{9,1},{17,25},{25,17},{2,10},{10... | collective-permute-start | bytes 393224 | tf_op jit(solution)/shard_map/ppermute | solution.py:284
  49.6 2.6 %collective-permute-done.11.refs_1_ = bf16[128,1024]{1,0:T(8,128)(2,1)S(1)} collective-permute-done((bf16[128,1024]{1,0:T(8,128)(2,1)S(1)}, bf16[128,1024]{1,0:T(8,128)(2,1)S(1)}, u32[]{:S(2)}, u32[]{:S(2)}) %collective-permute-start.11) | collective-permute-done | bytes 262176 | tf_op jit(solution)/shard_map/ppermute | solution.py:284
  52.1 1.1 %collective-permute-start.20 = (bf16[128,512]{1,0:T(8,128)(2,1)S(1)}, bf16[128,512]{1,0:T(8,128)(2,1)S(1)}, u32[]{:S(2)}, u32[]{:S(2)}) collective-permute-start(bf16[128,512]{1,0:T(8,128)(2,1)S(1)} %slice.77), channel_id=1, source_target_pairs={{0,16},{8,24},{16,0},{24,8},{1,17},{9,25},{17,1},{25,9},{2,18},{10... | collective-permute-start | bytes 393224 | tf_op jit(solution)/shard_map/ppermute | solution.py:284
  53.3 8.4 %expert_rows.4 = (bf16[2,512,2048]{2,1,0:T(8,128)(2,1)S(1)}, bf16[2,512,1024]{2,1,0:T(8,128)(2,1)S(1)}, bf16[2,128,512]{2,1,0:T(8,128)(2,1)S(1)}, bf16[2,128,512...) custom-call(bf16[256,1024]{1,0:T(8,128)(2,1)S(1)} %constant_dynamic-, ...), custom_call_target="tpu_custom_call", output_to_operand_aliasing={{0}: (9, {}), {1}: (10, {})} | custom-call | flops 3221225472 | bytes 12582912 | tf_op jit(solution)/shard_map/expert_rows/pallas_call | solution.py:193
  62.6 1.5 %collective-permute-start.16 = (bf16[2,128,512]{2,1,0:T(8,128)(2,1)S(1)}, bf16[2,128,512]{2,1,0:T(8,128)(2,1)S(1)}, u32[]{:S(2)}, u32[]{:S(2)}) collective-permute-start(bf16[2,128,512]{2,1,0:T(8,128)(2,1)S(1)} %get-tuple-element.52), channel_id=1, source_target_pairs={{0,16},{8,24},{16,0},{24,8},{1,17},{9,25},{17,1},{25,9},{2,18},{10... | collective-permute-start | bytes 786440 | tf_op jit(solution)/shard_map/ppermute | solution.py:284
  64.2 6.6 %expert_rows.5 = (bf16[2,512,2048]{2,1,0:T(8,128)(2,1)S(1)}, bf16[2,512,1024]{2,1,0:T(8,128)(2,1)S(1)}, bf16[128,512]{1,0:T(8,128)(2,1)S(1)}, bf16[128,512]{1,0:...) custom-call(bf16[128,1024]{1,0:T(8,128)(2,1)S(1)} %collective-permut, ...), custom_call_target="tpu_custom_call", output_to_operand_aliasing={{0}: (9, {}), {1}: (10, {})} | custom-call | flops 1610612736 | bytes 10485760 | tf_op jit(solution)/shard_map/expert_rows/pallas_call | solution.py:193
  70.8 2.4 %convolution_convert_fusion = bf16[2,1024,1024]{2,1,0:T(8,128)(2,1)S(1)} fusion(bf16[2,512,1024]{2,1,0:T(8,128)(2,1)S(1)} %get-tuple-element.65.acts, bf16[2,512,2048]{2,1,0:T(8,128)(2,1)S(1)} %get-tuple-element.63.rows), kind=kOutput, calls=%fused_computation | convolution fusion | flops 2149580800 | bytes 8388608 | tf_op jit(solution)/shard_map/dot_general | solution.py:313
  73.9 1.6 %collective-permute-start.14 = (bf16[128,512]{1,0:T(8,128)(2,1)S(1)}, bf16[128,512]{1,0:T(8,128)(2,1)S(1)}, u32[]{:S(2)}, u32[]{:S(2)}) collective-permute-start(bf16[128,512]{1,0:T(8,128)(2,1)S(1)} %fusion.5), channel_id=1, source_target_pairs={{0,16},{8,24},{16,0},{24,8},{1,17},{9,25},{17,1},{25,9},{2,18},{10... | collective-permute-start | bytes 393224 | tf_op jit(solution)/shard_map/ppermute | solution.py:284
  76.2 1.5 %collective-permute-start.21 = (bf16[128,512]{1,0:T(8,128)(2,1)S(1)}, bf16[128,512]{1,0:T(8,128)(2,1)S(1)}, u32[]{:S(2)}, u32[]{:S(2)}) collective-permute-start(bf16[128,512]{1,0:T(8,128)(2,1)S(1)} %get-tuple-element.58), channel_id=1, source_target_pairs={{0,8},{8,0},{16,24},{24,16},{1,9},{9,1},{17,25},{25,17},{2,10},{10... | collective-permute-start | bytes 393224 | tf_op jit(solution)/shard_map/ppermute | solution.py:284
  77.7 4.4 %collective-permute-done.14 = bf16[128,512]{1,0:T(8,128)(2,1)S(1)} collective-permute-done((bf16[128,512]{1,0:T(8,128)(2,1)S(1)}, bf16[128,512]{1,0:T(8,128)(2,1)S(1)}, u32[]{:S(2)}, u32[]{:S(2)}) %collective-permute-start.14) | collective-permute-done | bytes 131104 | tf_op jit(solution)/shard_map/ppermute | solution.py:284
  82.7 1.6 %collective-permute-start.23 = (bf16[128,512]{1,0:T(8,128)(2,1)S(1)}, bf16[128,512]{1,0:T(8,128)(2,1)S(1)}, u32[]{:S(2)}, u32[]{:S(2)}) collective-permute-start(bf16[128,512]{1,0:T(8,128)(2,1)S(1)} %get-tuple-element.62), channel_id=1, source_target_pairs={{0,24},{8,16},{16,8},{24,0},{1,25},{9,17},{17,9},{25,1},{2,26},{10... | collective-permute-start | bytes 393224 | tf_op jit(solution)/shard_map/ppermute | solution.py:284
  84.3 1.4 %collective-permute-start.15 = (bf16[128,512]{1,0:T(8,128)(2,1)S(1)}, bf16[128,512]{1,0:T(8,128)(2,1)S(1)}, u32[]{:S(2)}, u32[]{:S(2)}) collective-permute-start(bf16[128,512]{1,0:T(8,128)(2,1)S(1)} %fusion.2), channel_id=1, source_target_pairs={{0,6},{2,0},{4,2},{6,4},{1,7},{3,1},{5,3},{7,5},{8,14},{10,8},{12,... | collective-permute-start | bytes 393224 | tf_op jit(solution)/shard_map/ppermute | solution.py:287
  85.8 4.3 %collective-permute-done.22 = bf16[128,512]{1,0:T(8,128)(2,1)S(1)} collective-permute-done((bf16[128,512]{1,0:T(8,128)(2,1)S(1)}, bf16[128,512]{1,0:T(8,128)(2,1)S(1)}, u32[]{:S(2)}, u32[]{:S(2)}) %collective-permute-start.22) | collective-permute-done | bytes 131104 | tf_op jit(solution)/shard_map/ppermute | solution.py:284
  90.0 1.7 %collective-permute-start.18 = (bf16[128,512]{1,0:T(8,128)(2,1)S(1)}, bf16[128,512]{1,0:T(8,128)(2,1)S(1)}, u32[]{:S(2)}, u32[]{:S(2)}) collective-permute-start(bf16[128,512]{1,0:T(8,128)(2,1)S(1)} %fusion.1), channel_id=1, source_target_pairs={{0,2},{2,4},{4,6},{6,0},{1,3},{3,5},{5,7},{7,1},{8,10},{10,12},{12... | collective-permute-start | bytes 393224 | tf_op jit(solution)/shard_map/ppermute | solution.py:287
  92.7 3.9 %weight_grads.1 = (bf16[1024,1024]{1,0:T(8,128)(2,1)}, bf16[1024,1024]{1,0:T(8,128)(2,1)}) custom-call(bf16[2,512,2048]{2,1,0:T(8,128)(2,1)S(1)} %get-tuple-element.63.rows, bf16[2,512,1024]{2,1,0:T(8,128)(2,1)S(1)} %get-tuple-element.65.acts, bf16[2,1024,1024]{2,1,0:T(8,128)(2,1)S(1)} %collective-permute-done.25.got), custom_call_target="tpu_custom_call" | custom-call | flops 1000 | bytes 1000 | tf_op jit(solution)/shard_map/weight_grads/pallas_call | solution.py:256
  96.5 5.2 %collective-permute-done.24.refs_3_ = bf16[128,512]{1,0:T(8,128)(2,1)S(1)} collective-permute-done((bf16[128,512]{1,0:T(8,128)(2,1)S(1)}, bf16[128,512]{1,0:T(8,128)(2,1)S(1)}, u32[]{:S(2)}, u32[]{:S(2)}) %collective-permute-start.24) | collective-permute-done | bytes 131104 | tf_op jit(solution)/shard_map/ppermute | solution.py:287
  101.7 1.2 %unplace_rows.1 = bf16[256,512]{1,0:T(8,128)(2,1)} custom-call(s32[1,256]{1,0:T(1,128)S(1)} %bitcast.35, s32[1,256]{1,0:T(1,128)S(1)} %bitcast.37, bf16[128,512]{1,0:T(8,128)(2,1)S(1)} %fusion.3.refs_0_, bf16[128,512]{1,0:T(8,128)(2,1)S(1)} %collective-permute-done.15.refs_1_, bf16[128,512]{1,0:T(8,128)(2,1)S(1)} %collective-permute-done.18.refs_2_, ...), custom_call_target="tpu_custom_call" | custom-call | flops 1000 | bytes 1000 | tf_op jit(solution)/shard_map/unplace_rows/pallas_call | solution.py:228
  (56 shorter events, 8.3 us)
Async XLA Ops:
  0.6 9.9 %copy-start = (bf16[1,1024,1024]{2,1,0:T(8,128)(2,1)S(1)}, bf16[1,1024,1024]{2,1,0:T(8,128)(2,1)}, u32[]{:S(2)}) copy-start(bf16[1,1024,1024]{2,1,0:T(8,128)(2,1)} %param.12) | copy-start | bytes 6291460
  0.6 9.9 %collective-permute-start = (bf16[1024,1024]{1,0:T(8,128)(2,1)}, bf16[1024,1024]{1,0:T(8,128)(2,1)S(1)}, u32[]{:S(2)}, u32[]{:S(2)}) collective-permute-start(bf16[1024,1024]{1,0:T(8,128)(2,1)} %bitcast.26), channel_id=1, source_target_pairs={{0,1},{1,0},{2,3},{3,2},{4,5},{5,4},{6,7},{7,6},{8,9},{9,8},{10,11... | collective-permute-start | bytes 6291464 | tf_op jit(solution)/shard_map/ppermute | solution.py:281
  1.2 9.4 %collective-permute-start.1 = (bf16[1024,1024]{1,0:T(8,128)(2,1)}, bf16[1024,1024]{1,0:T(8,128)(2,1)S(1)}, u32[]{:S(2)}, u32[]{:S(2)}) collective-permute-start(bf16[1024,1024]{1,0:T(8,128)(2,1)} %bitcast.30), channel_id=1, source_target_pairs={{0,1},{1,0},{2,3},{3,2},{4,5},{5,4},{6,7},{7,6},{8,9},{9,8},{10,11... | collective-permute-start | bytes 6291464 | tf_op jit(solution)/shard_map/ppermute | solution.py:281
  5.4 15.2 %collective-permute-start.2 = (bf16[128,1024]{1,0:T(8,128)(2,1)}, bf16[128,1024]{1,0:T(8,128)(2,1)S(1)}, u32[]{:S(2)}, u32[]{:S(2)}) collective-permute-start(bf16[128,1024]{1,0:T(8,128)(2,1)} %get-tuple-element.40), channel_id=1, source_target_pairs={{0,2},{2,4},{4,6},{6,0},{1,3},{3,5},{5,7},{7,1},{8,10},{10,12},{12... | collective-permute-start | bytes 786440 | tf_op jit(solution)/shard_map/ppermute | solution.py:287
  8.4 13.8 %collective-permute-start.3 = (bf16[128,1024]{1,0:T(8,128)(2,1)}, bf16[128,1024]{1,0:T(8,128)(2,1)S(1)}, u32[]{:S(2)}, u32[]{:S(2)}) collective-permute-start(bf16[128,1024]{1,0:T(8,128)(2,1)} %get-tuple-element.42), channel_id=1, source_target_pairs={{0,6},{2,0},{4,2},{6,4},{1,7},{3,1},{5,3},{7,5},{8,14},{10,8},{12,... | collective-permute-start | bytes 786440 | tf_op jit(solution)/shard_map/ppermute | solution.py:287
  10.5 1.6 %copy-start.1 = (bf16[1,1024,1024]{2,1,0:T(8,128)(2,1)S(1)}, bf16[1,1024,1024]{2,1,0:T(8,128)(2,1)}, u32[]{:S(2)}) copy-start(bf16[1,1024,1024]{2,1,0:T(8,128)(2,1)} %param.13) | copy-start | bytes 6291460
  14.2 11.1 %copy-start.7 = (bf16[128,1024]{1,0:T(8,128)(2,1)S(1)}, bf16[128,1024]{1,0:T(8,128)(2,1)}, u32[]{:S(2)}) copy-start(bf16[128,1024]{1,0:T(8,128)(2,1)} %get-tuple-element.44) | copy-start | bytes 786436
  20.6 32.7 %copy-start.2 = (bf16[1,1024,1024]{2,1,0:T(8,128)(2,1)S(1)}, bf16[1,1024,1024]{2,1,0:T(8,128)(2,1)}, u32[]{:S(2)}) copy-start(bf16[1,1024,1024]{2,1,0:T(8,128)(2,1)} %param.13) | copy-start | bytes 6291460
  22.3 13.3 %collective-permute-start.6 = (bf16[256,1024]{1,0:T(8,128)(2,1)S(1)}, bf16[256,1024]{1,0:T(8,128)(2,1)S(1)}, u32[]{:S(2)}, u32[]{:S(2)}) collective-permute-start(bf16[256,1024]{1,0:T(8,128)(2,1)S(1)} %constant_dynamic-update-slice_fusion.refs_0_), channel_id=1, source_target_pairs={{0,8},{8,0},{16,24},{24,16},{1,9},{9,1},{17,25},{25,17},{2,10},{10... | collective-permute-start | bytes 1572872 | tf_op jit(solution)/shard_map/ppermute | solution.py:284
  23.8 13.4 %collective-permute-start.4 = (bf16[256,1024]{1,0:T(8,128)(2,1)S(1)}, bf16[256,1024]{1,0:T(8,128)(2,1)S(1)}, u32[]{:S(2)}, u32[]{:S(2)}) collective-permute-start(bf16[256,1024]{1,0:T(8,128)(2,1)S(1)} %constant_dynamic-update-slice_fusion.refs_0_), channel_id=1, source_target_pairs={{0,16},{8,24},{16,0},{24,8},{1,17},{9,25},{17,1},{25,9},{2,18},{10... | collective-permute-start | bytes 1572872 | tf_op jit(solution)/shard_map/ppermute | solution.py:284
  25.3 13.6 %collective-permute-start.10 = (bf16[128,1024]{1,0:T(8,128)(2,1)S(1)}, bf16[128,1024]{1,0:T(8,128)(2,1)S(1)}, u32[]{:S(2)}, u32[]{:S(2)}) collective-permute-start(bf16[128,1024]{1,0:T(8,128)(2,1)S(1)} %copy-done.7), channel_id=1, source_target_pairs={{0,4},{2,6},{4,0},{6,2},{1,5},{3,7},{5,1},{7,3},{8,12},{10,14},{12... | collective-permute-start | bytes 786440 | tf_op jit(solution)/shard_map/ppermute | solution.py:287
  35.6 8.9 %collective-permute-start.7 = (bf16[256,512]{1,0:T(8,128)(2,1)S(1)}, bf16[256,512]{1,0:T(8,128)(2,1)S(1)}, u32[]{:S(2)}, u32[]{:S(2)}) collective-permute-start(bf16[256,512]{1,0:T(8,128)(2,1)S(1)} %slice.69), channel_id=1, source_target_pairs={{0,16},{8,24},{16,0},{24,8},{1,17},{9,25},{17,1},{25,9},{2,18},{10... | collective-permute-start | bytes 786440 | tf_op jit(solution)/shard_map/ppermute | solution.py:284
  37.2 9.3 %collective-permute-start.5 = (bf16[256,512]{1,0:T(8,128)(2,1)S(1)}, bf16[256,512]{1,0:T(8,128)(2,1)S(1)}, u32[]{:S(2)}, u32[]{:S(2)}) collective-permute-start(bf16[256,512]{1,0:T(8,128)(2,1)S(1)} %slice.68), channel_id=1, source_target_pairs={{0,8},{8,0},{16,24},{24,16},{1,9},{9,1},{17,25},{25,17},{2,10},{10... | collective-permute-start | bytes 786440 | tf_op jit(solution)/shard_map/ppermute | solution.py:284
  38.9 9.1 %collective-permute-start.12 = (bf16[128,1024]{1,0:T(8,128)(2,1)S(1)}, bf16[128,1024]{1,0:T(8,128)(2,1)S(1)}, u32[]{:S(2)}, u32[]{:S(2)}) collective-permute-start(bf16[128,1024]{1,0:T(8,128)(2,1)S(1)} %collective-permute-done.10.refs_0_), channel_id=1, source_target_pairs={{0,16},{8,24},{16,0},{24,8},{1,17},{9,25},{17,1},{25,9},{2,18},{10... | collective-permute-start | bytes 786440 | tf_op jit(solution)/shard_map/ppermute | solution.py:284
  39.4 12.7 %collective-permute-start.11 = (bf16[128,1024]{1,0:T(8,128)(2,1)S(1)}, bf16[128,1024]{1,0:T(8,128)(2,1)S(1)}, u32[]{:S(2)}, u32[]{:S(2)}) collective-permute-start(bf16[128,1024]{1,0:T(8,128)(2,1)S(1)} %collective-permute-done.10.refs_0_), channel_id=1, source_target_pairs={{0,8},{8,0},{16,24},{24,16},{1,9},{9,1},{17,25},{25,17},{2,10},{10... | collective-permute-start | bytes 786440 | tf_op jit(solution)/shard_map/ppermute | solution.py:284
  46.5 17.6 %collective-permute-start.8 = (bf16[2,128,512]{2,1,0:T(8,128)(2,1)S(1)}, bf16[2,128,512]{2,1,0:T(8,128)(2,1)S(1)}, u32[]{:S(2)}, u32[]{:S(2)}) collective-permute-start(bf16[2,128,512]{2,1,0:T(8,128)(2,1)S(1)} %get-tuple-element.43), channel_id=1, source_target_pairs={{0,8},{8,0},{16,24},{24,16},{1,9},{9,1},{17,25},{25,17},{2,10},{10... | collective-permute-start | bytes 786440 | tf_op jit(solution)/shard_map/ppermute | solution.py:284
  48.0 16.1 %collective-permute-start.19 = (bf16[128,512]{1,0:T(8,128)(2,1)S(1)}, bf16[128,512]{1,0:T(8,128)(2,1)S(1)}, u32[]{:S(2)}, u32[]{:S(2)}) collective-permute-start(bf16[128,512]{1,0:T(8,128)(2,1)S(1)} %slice.76), channel_id=1, source_target_pairs={{0,8},{8,0},{16,24},{24,16},{1,9},{9,1},{17,25},{25,17},{2,10},{10... | collective-permute-start | bytes 393224 | tf_op jit(solution)/shard_map/ppermute | solution.py:284
  52.1 12.0 %collective-permute-start.20 = (bf16[128,512]{1,0:T(8,128)(2,1)S(1)}, bf16[128,512]{1,0:T(8,128)(2,1)S(1)}, u32[]{:S(2)}, u32[]{:S(2)}) collective-permute-start(bf16[128,512]{1,0:T(8,128)(2,1)S(1)} %slice.77), channel_id=1, source_target_pairs={{0,16},{8,24},{16,0},{24,8},{1,17},{9,25},{17,1},{25,9},{2,18},{10... | collective-permute-start | bytes 393224 | tf_op jit(solution)/shard_map/ppermute | solution.py:284
  61.7 9.2 %collective-permute-start.13 = (bf16[2,128,512]{2,1,0:T(8,128)(2,1)S(1)}, bf16[2,128,512]{2,1,0:T(8,128)(2,1)S(1)}, u32[]{:S(2)}, u32[]{:S(2)}) collective-permute-start(bf16[2,128,512]{2,1,0:T(8,128)(2,1)S(1)} %get-tuple-element.50), channel_id=1, source_target_pairs={{0,8},{8,0},{16,24},{24,16},{1,9},{9,1},{17,25},{25,17},{2,10},{10... | collective-permute-start | bytes 786440 | tf_op jit(solution)/shard_map/ppermute | solution.py:284
  62.6 8.2 %collective-permute-start.16 = (bf16[2,128,512]{2,1,0:T(8,128)(2,1)S(1)}, bf16[2,128,512]{2,1,0:T(8,128)(2,1)S(1)}, u32[]{:S(2)}, u32[]{:S(2)}) collective-permute-start(bf16[2,128,512]{2,1,0:T(8,128)(2,1)S(1)} %get-tuple-element.52), channel_id=1, source_target_pairs={{0,16},{8,24},{16,0},{24,8},{1,17},{9,25},{17,1},{25,9},{2,18},{10... | collective-permute-start | bytes 786440 | tf_op jit(solution)/shard_map/ppermute | solution.py:284
  73.2 19.4 %collective-permute-start.25 = (bf16[2,1024,1024]{2,1,0:T(8,128)(2,1)S(1)}, bf16[2,1024,1024]{2,1,0:T(8,128)(2,1)S(1)}, u32[]{:S(2)}, u32[]{:S(2)}) collective-permute-start(bf16[2,1024,1024]{2,1,0:T(8,128)(2,1)S(1)} %convolution_convert_fusion), channel_id=1, source_target_pairs={{0,1},{1,0},{2,3},{3,2},{4,5},{5,4},{6,7},{7,6},{8,9},{9,8},{10,11... | collective-permute-start | bytes 12582920 | tf_op jit(solution)/shard_map/ppermute | solution.py:281
  73.3 19.2 %collective-permute-start.9 = (bf16[128,512]{1,0:T(8,128)(2,1)S(1)}, bf16[128,512]{1,0:T(8,128)(2,1)S(1)}, u32[]{:S(2)}, u32[]{:S(2)}) collective-permute-start(bf16[128,512]{1,0:T(8,128)(2,1)S(1)} %fusion.4), channel_id=1, source_target_pairs={{0,16},{8,24},{16,0},{24,8},{1,17},{9,25},{17,1},{25,9},{2,18},{10... | collective-permute-start | bytes 393224 | tf_op jit(solution)/shard_map/ppermute | solution.py:284
  73.9 8.2 %collective-permute-start.14 = (bf16[128,512]{1,0:T(8,128)(2,1)S(1)}, bf16[128,512]{1,0:T(8,128)(2,1)S(1)}, u32[]{:S(2)}, u32[]{:S(2)}) collective-permute-start(bf16[128,512]{1,0:T(8,128)(2,1)S(1)} %fusion.5), channel_id=1, source_target_pairs={{0,16},{8,24},{16,0},{24,8},{1,17},{9,25},{17,1},{25,9},{2,18},{10... | collective-permute-start | bytes 393224 | tf_op jit(solution)/shard_map/ppermute | solution.py:284
  75.6 7.1 %collective-permute-start.17 = (bf16[128,512]{1,0:T(8,128)(2,1)S(1)}, bf16[128,512]{1,0:T(8,128)(2,1)S(1)}, u32[]{:S(2)}, u32[]{:S(2)}) collective-permute-start(bf16[128,512]{1,0:T(8,128)(2,1)S(1)} %fusion.6), channel_id=1, source_target_pairs={{0,8},{8,0},{16,24},{24,16},{1,9},{9,1},{17,25},{25,17},{2,10},{10... | collective-permute-start | bytes 393224 | tf_op jit(solution)/shard_map/ppermute | solution.py:284
  76.2 8.1 %collective-permute-start.21 = (bf16[128,512]{1,0:T(8,128)(2,1)S(1)}, bf16[128,512]{1,0:T(8,128)(2,1)S(1)}, u32[]{:S(2)}, u32[]{:S(2)}) collective-permute-start(bf16[128,512]{1,0:T(8,128)(2,1)S(1)} %get-tuple-element.58), channel_id=1, source_target_pairs={{0,8},{8,0},{16,24},{24,16},{1,9},{9,1},{17,25},{25,17},{2,10},{10... | collective-permute-start | bytes 393224 | tf_op jit(solution)/shard_map/ppermute | solution.py:284
  82.1 7.9 %collective-permute-start.22 = (bf16[128,512]{1,0:T(8,128)(2,1)S(1)}, bf16[128,512]{1,0:T(8,128)(2,1)S(1)}, u32[]{:S(2)}, u32[]{:S(2)}) collective-permute-start(bf16[128,512]{1,0:T(8,128)(2,1)S(1)} %get-tuple-element.60), channel_id=1, source_target_pairs={{0,16},{8,24},{16,0},{24,8},{1,17},{9,25},{17,1},{25,9},{2,18},{10... | collective-permute-start | bytes 393224 | tf_op jit(solution)/shard_map/ppermute | solution.py:284
  82.7 9.1 %collective-permute-start.23 = (bf16[128,512]{1,0:T(8,128)(2,1)S(1)}, bf16[128,512]{1,0:T(8,128)(2,1)S(1)}, u32[]{:S(2)}, u32[]{:S(2)}) collective-permute-start(bf16[128,512]{1,0:T(8,128)(2,1)S(1)} %get-tuple-element.62), channel_id=1, source_target_pairs={{0,24},{8,16},{16,8},{24,0},{1,25},{9,17},{17,9},{25,1},{2,26},{10... | collective-permute-start | bytes 393224 | tf_op jit(solution)/shard_map/ppermute | solution.py:284
  84.3 17.4 %collective-permute-start.15 = (bf16[128,512]{1,0:T(8,128)(2,1)S(1)}, bf16[128,512]{1,0:T(8,128)(2,1)S(1)}, u32[]{:S(2)}, u32[]{:S(2)}) collective-permute-start(bf16[128,512]{1,0:T(8,128)(2,1)S(1)} %fusion.2), channel_id=1, source_target_pairs={{0,6},{2,0},{4,2},{6,4},{1,7},{3,1},{5,3},{7,5},{8,14},{10,8},{12,... | collective-permute-start | bytes 393224 | tf_op jit(solution)/shard_map/ppermute | solution.py:287
  90.0 11.7 %collective-permute-start.18 = (bf16[128,512]{1,0:T(8,128)(2,1)S(1)}, bf16[128,512]{1,0:T(8,128)(2,1)S(1)}, u32[]{:S(2)}, u32[]{:S(2)}) collective-permute-start(bf16[128,512]{1,0:T(8,128)(2,1)S(1)} %fusion.1), channel_id=1, source_target_pairs={{0,2},{2,4},{4,6},{6,0},{1,3},{3,5},{5,7},{7,1},{8,10},{10,12},{12... | collective-permute-start | bytes 393224 | tf_op jit(solution)/shard_map/ppermute | solution.py:287
  91.9 9.8 %collective-permute-start.24 = (bf16[128,512]{1,0:T(8,128)(2,1)S(1)}, bf16[128,512]{1,0:T(8,128)(2,1)S(1)}, u32[]{:S(2)}, u32[]{:S(2)}) collective-permute-start(bf16[128,512]{1,0:T(8,128)(2,1)S(1)} %add_convert_fusion), channel_id=1, source_target_pairs={{0,4},{2,6},{4,0},{6,2},{1,5},{3,7},{5,1},{7,3},{8,12},{10,14},{12... | collective-permute-start | bytes 393224 | tf_op jit(solution)/shard_map/ppermute | solution.py:287
  92.6 9.1 %copy-start.5 = (s32[256,1]{0,1:T(1,128)S(1)}, s32[256,1]{0,1:T(1,128)}, u32[]{:S(2)}) copy-start(s32[256,1]{0,1:T(1,128)} %param.10) | copy-start | bytes 3076
  92.6 9.1 %copy-start.6 = (s32[256,1]{0,1:T(1,128)S(1)}, s32[256,1]{0,1:T(1,128)}, u32[]{:S(2)}) copy-start(s32[256,1]{0,1:T(1,128)} %param.11) | copy-start | bytes 3076
  (2 other events, 2.1 us)

commit v9 on v8

--- a/solution.py
+++ b/solution.py
@@ -60,55 +60,43 @@
         copy.wait()
 
 
-def place_kernel(spans, shifts, capacity, own, index, slot, gate, tokens, grad_output, *refs):
-    sends, refs = refs[: len(spans)], refs[len(spans) :]
-    if own:
-        owns, refs = refs[:2], refs[2:]
-    tok, grad, packed = refs[:3]
-    copies = Copies(refs[-1])
-    count, width = tok.shape
-    half, share = width // 2, width // 4
-    arrive = copies.rows(tokens, tok, count, 8) + copies.rows(grad_output, grad, count, 8)
-    position = places(index, slot, capacity)
+def place_kernel(spans, shifts, capacity, index, slot, gate, tokens, grad_output, *refs):
+    sends, (index_in, slot_in, gate_in, tok, grad, packed, sem) = refs[: len(spans)], refs[len(spans) :]
+    copies = Copies(sem)
+    count, share = tok.shape
+    columns = pl.ds(pl.multiple_of(lax.axis_index("tensor") * share, share), share)
+    small = [copies.start(src, dst) for src, dst in ((index, index_in), (slot, slot_in), (gate, gate_in))]
+    arrive = copies.rows(tokens.at[:, columns], tok, count, 4) + copies.rows(grad_output.at[:, columns], grad, count, 4)
+    wait(small)
+    position = places(index_in, slot_in, capacity)
     found = [hits(position, expert_first(k, capacity), rows) for k, rows in zip(shifts, spans)]
-    scales = [gate_of(hit, gate[...]) for hit in found]
+    scales = [gate_of(hit, gate_in[...]) for hit in found]
     hots = [hit.astype(BF16) for hit in found]
-    columns = pl.ds(pl.multiple_of(lax.axis_index("tensor") * share, share), share)
     wait(arrive)
     leave = []
     at = 0
     for hot, scale, rows, out in zip(hots, scales, spans, sends):
-        packed[at : at + rows, :share] = dot(hot, tok[:, columns]).astype(BF16)
-        packed[at : at + rows, share:] = (dot(hot, grad[:, columns]) * scale).astype(BF16)
+        packed[at : at + rows, :share] = dot(hot, tok[...]).astype(BF16)
+        packed[at : at + rows, share:] = (dot(hot, grad[...]) * scale).astype(BF16)
         leave += copies.rows(packed.at[pl.ds(at, rows), :], out, rows, 2)
         at += rows
-    if own:
-        mine = lax.axis_index("dp")
-        hit = hits(position, expert_first(0, capacity), capacity)
-        hot, scale = hit.astype(BF16), gate_of(hit, gate[...])
-        placed = refs[3:5]
-        for i, start in enumerate((mine * half, (1 - mine) * half)):
-            source = pl.ds(pl.multiple_of(start, half), half)
-            target = slice(i * half, (i + 1) * half)
-            placed[0][:, target] = dot(hot, tok[:, source]).astype(BF16)
-            placed[1][:, target] = (dot(hot, grad[:, source]) * scale).astype(BF16)
-        for src, dst in zip(placed, owns):
-            leave += copies.rows(src, dst, capacity, 2)
     wait(leave)
 
 
-def place(spans, shifts, capacity, own, index, slot, gate, tokens, grad_output):
+def place(spans, shifts, capacity, index, slot, gate, tokens, grad_output):
     count, width = tokens.shape
-    shapes = [(rows, width // 2) for rows in spans] + [(capacity, width)] * (2 if own else 0)
+    share = width // 4
     buf = lambda *shape: pltpu.VMEM(shape, BF16)
-    scratch = [buf(count, width), buf(count, width), buf(sum(spans), width // 2)]
-    scratch += [buf(capacity, width)] * (2 if own else 0)
     return pl.pallas_call(
-        functools.partial(place_kernel, spans, shifts, capacity, own),
-        out_shape=[jax.ShapeDtypeStruct(shape, BF16) for shape in shapes],
-        in_specs=[VMEM, VMEM, VMEM, HBM, HBM],
-        out_specs=[ANY] * len(shapes),
-        scratch_shapes=scratch + [pltpu.SemaphoreType.DMA((16 + 2 * len(shapes),))],
+        functools.partial(place_kernel, spans, shifts, capacity),
+        out_shape=[jax.ShapeDtypeStruct((rows, 2 * share), BF16) for rows in spans],
+        in_specs=[ANY] * 5,
+        out_specs=[ANY] * len(spans),
+        scratch_shapes=[
+            pltpu.VMEM((1, count), I32), pltpu.VMEM((1, count), I32), pltpu.VMEM((1, count), F32),
+            buf(count, share), buf(count, share), buf(sum(spans), 2 * share),
+            pltpu.SemaphoreType.DMA((11 + 2 * len(spans),)),
+        ],
         compiler_params=pltpu.CompilerParams(vmem_limit_bytes=54 * 2**20),
         cost_estimate=SMALL,
         name="place_rows",
@@ -126,19 +114,26 @@
 def expert_kernel(first, base, groups, aliased, *refs):
     refs = list(refs)
     take = lambda n: [refs.pop(0) for _ in range(n)]
-    slots = take(2 if first is None else 5)
+    slots = take(5)
     up_halves, down_halves = take(2), take(2)
     take(aliased)
     kept_rows, kept_acts = take(2)
     targets = [take(4 if step is None else 2) for _, step in groups]
     tok, grad, up, down, hidden, slope, back = take(7)
+    if first is None:
+        tok_in, grad_in = take(2)
     copies = Copies(take(1)[0])
     rows, width = tok.shape
     half, share = width // 2, width // 4
     order = lax.axis_index("tensor") ^ (2 * lax.axis_index("dp"))
     arrive = []
     if first is None:
-        arrive += copies.rows(slots[0], tok, rows, 2) + copies.rows(slots[1], grad, rows, 2)
+        mine = lax.axis_index("dp")
+        count = tok_in.shape[0]
+        for src, dst in zip(slots[3:], (tok_in, grad_in)):
+            for i, start in enumerate((mine * half, (1 - mine) * half)):
+                source = src.at[:, pl.ds(pl.multiple_of(start, half), half)]
+                arrive += copies.rows(source, dst.at[:, pl.ds(i * half, half)], count, 2)
     else:
         span = pl.ds(first, rows)
         for j in range(4):
@@ -157,7 +152,13 @@
         for halves, dst in ((up_halves, up), (down_halves, down)):
             for i in range(2):
                 tiles[-1].append(copies.start(halves[i].at[:, cols], dst.at[pl.ds(i * half, half), cols]))
+    if first is None:
+        hit = hits(places(slots[0], slots[1], rows), expert_first(0, rows), rows)
+        hot, scale = hit.astype(BF16), gate_of(hit, slots[2][...])
     wait(arrive)
+    if first is None:
+        tok[...] = dot(hot, tok_in[...]).astype(BF16)
+        grad[...] = (dot(hot, grad_in[...]) * scale).astype(BF16)
     mine = pl.ds(base, rows)
     leave = [copies.start(src, kept_rows.at[i, mine, :]) for i, src in enumerate((tok, grad))]
     for n, arrived in zip(range(0, hid, step), tiles):
@@ -193,13 +194,14 @@
     out = pl.pallas_call(
         functools.partial(expert_kernel, first, base, groups, len(aliases)),
         out_shape=[shape(2, total_rows, width), shape(2, total_rows, hid)] + sum(quarters, []),
-        in_specs=[ANY] * len(operands),
+        in_specs=([VMEM] * 3 if first is None else [ANY] * 3) + [ANY] * (len(operands) - 3),
         out_specs=[ANY] * (2 + sum(counts)),
         scratch_shapes=[
             buf(rows, width), buf(rows, width), buf(width, hid), buf(width, hid),
             buf(rows, hid), buf(rows, hid), buf(4, rows, share),
-            pltpu.SemaphoreType.DMA((12 + 4 * (hid // 256) + 4 * len(groups),)),
-        ],
+        ]
+        + ([buf(*slots[3].shape)] * 2 if first is None else [])
+        + [pltpu.SemaphoreType.DMA((12 + 4 * (hid // 256) + 4 * len(groups),))],
         input_output_aliases=aliases,
         compiler_params=pltpu.CompilerParams(vmem_limit_bytes=LIMIT + rows * 2**15),
         cost_estimate=pl.CostEstimate(
@@ -319,25 +321,24 @@
 
     if experts == 4:
         shifts = [1, 3, 2]
-        placed = place([capacity] * 3, shifts, capacity, True, index, slot, gate, tokens, grad_output)
-        moved = [shift(rows, k) for rows, k in zip(placed, shifts)]
+        sends = place([capacity] * 3, shifts, capacity, index, slot, gate, tokens, grad_output)
+        moved = [shift(rows, k) for rows, k in zip(sends, shifts)]
         everything = 4 * capacity
-        kept, (pair,) = expert_rows(placed[3:], None, [(capacity, 1)], weights, everything, 0, None)
+        own = [index, slot, gate, tokens, grad_output]
+        kept, (pair,) = expert_rows(own, None, [(capacity, 1)], weights, everything, 0, None)
         near = spread(jnp.concatenate([after(moved[0], pair[0]), moved[1]], 0))
         far = spread(after(moved[2], *near[1:3]))
         near[0] = after(near[0], *far[1:3])
         back, got_own = collect_pair([pair[0], after(pair[1], *near[3:])], 1)
-        backs = [back]
-        kept, pairs = expert_rows(near, 0, [(capacity, 1), (capacity, 2)], weights, everything, capacity, kept)
-        (one, got_one), (three, got_three) = collect_pair(pairs[0], 1), collect_pair(pairs[1], 2)
-        backs += [shift(one, -1), shift(three, -3)]
-        kept, (blocks,) = expert_rows(
-            [after(far[0], got_own)] + far[1:], 0, [(capacity, None)], weights, everything, 3 * capacity, kept
-        )
-        others = other_halves([kept[0], after(kept[1], got_one, got_three)])
-        grads = weight_grads(*kept, swap(others))
-        two, _ = collect([blocks[0]] + [after(b, got_one, got_three) for b in blocks[1:]])
-        backs.append(after(shift(two, -2), *grads))
+        kept, (blocks,) = expert_rows(near, 0, [(2 * capacity, None)], weights, everything, capacity, kept)
+        total, got = collect(blocks)
+        backs = [back, shift(total[:capacity], -1), shift(total[capacity:], -3)]
+        slots = [after(far[0], got_own)] + far[1:]
+        kept, (blocks,) = expert_rows(slots, 0, [(capacity, None)], weights, everything, 3 * capacity, kept)
+        others = other_halves(kept)
+        grads = weight_grads(*kept, swap(after(others, *got)))
+        total, _ = collect([blocks[0]] + [after(b, got[0], others) for b in blocks[1:]])
+        backs.append(after(shift(total, -2), *grads))
         shifts = [0] + shifts
     else:
         rows = experts * capacity
@@ -349,7 +350,7 @@
             )
             return moved.reshape(rows, x.shape[1])
 
-        (send,) = place([rows], shifts, capacity, False, index, slot, gate, tokens, grad_output)
+        (send,) = place([rows], shifts, capacity, index, slot, gate, tokens, grad_output)
         kept, (blocks,) = expert_rows(spread(exchange(send)), 0, [(rows, None)], weights, rows, 0, None)
         others = other_halves(kept)
         grads = weight_grads(*kept, swap(others))

time: 103 us -> 97.2 us (0.944)
  waiting for transfers between devices: 33.3 us -> 26.7 us
  starting transfers between devices: 31.7 us -> 34.4 us
  Pallas kernels: 30.5 us -> 28.2 us
    ppermute x17 -> x16, waiting for transfers between devices: 26.4 us -> 21.9 us  [across(): return lax.ppermute(x, 'tensor', [(i, i ^ j) for i in range(tensor_size)])]
    ppermute x6, starting transfers between devices: 10.3 us -> 13.1 us  [shift(): lax.ppermute(x, 'expert', [(i, (i + k) % experts) for i in range(experts)])]
    ppermute x6, waiting for transfers between devices: 6.96 us -> 4.82 us  [shift(): lax.ppermute(x, 'expert', [(i, (i + k) % experts) for i in range(experts)])]
    pallas_call x1, Pallas kernels: 4.13 us -> 2.41 us  [place(): pl.pallas_call(functools.partial(place_kernel, spans, shifts, capacity),...]
    unnamed x17 -> x19, local copies, waits for them, and re-layouts: 3.71 us -> 4.08 us
    ppermute x17 -> x16, starting transfers between devices: 20.7 us -> 20.6 us  [across(): return lax.ppermute(x, 'tensor', [(i, i ^ j) for i in range(tensor_size)])]
  transfers between devices with their start and end apart: 26 -> 25, of which waited for: 9 -> 10; matrix products, arithmetic and copies ran while one was open for 0% -> 3% of each run, Pallas kernels for 29% -> 28%
where the time goes in v9:
time: 97.2 us; the launch traced here: 97 us
  starting transfers between devices  34.4 us (35%)
  Pallas kernels  28.2 us (29%)
  waiting for transfers between devices  26.7 us (27%)
  local copies, waits for them, and re-layouts  4.17 us (4%)
  matrix products  2.39 us (2%)
    ppermute x16, waiting for transfers between devices, across(): return lax.ppermute(x, 'tensor', [(i, i ^ j) for i in range(tensor_size)])  21.9 us
    pallas_call x3, Pallas kernels, expert_rows(): pl.pallas_call(functools.partial(expert_kernel, first, base, groups, len(...  20.7 us
    ppermute x16, starting transfers between devices, across(): return lax.ppermute(x, 'tensor', [(i, i ^ j) for i in range(tensor_size)])  20.6 us
    ppermute x6, starting transfers between devices, shift(): lax.ppermute(x, 'expert', [(i, (i + k) % experts) for i in range(experts)])  13.1 us
    ppermute x6, waiting for transfers between devices, shift(): lax.ppermute(x, 'expert', [(i, (i + k) % experts) for i in range(experts)])  4.82 us
    unnamed x19, local copies, waits for them, and re-layouts  4.08 us
    pallas_call x1, Pallas kernels, weight_grads(): pl.pallas_call(weight_grad_kernel, out_shape=[jax.ShapeDtypeStruct((half,...  3.86 us
    pallas_call x1, Pallas kernels, place(): pl.pallas_call(functools.partial(place_kernel, spans, shifts, capacity),...  2.41 us
  transfers between devices with their start and end apart: 25, of which 10 were waited for; matrix products, arithmetic and copies ran while one was open for 3% of the time, Pallas kernels for 28%

profile of v9, /device:TPU:0, one launch (start us, length us, event | category | flops | bytes accessed | tf_op | source)
XLA Modules:
  0.0 97.0 jit_solution(3322906496420458061)
XLA Ops:
  1.3 2.4 %place_rows.1 = (bf16[128,1024]{1,0:T(8,128)(2,1)}, bf16[128,1024]{1,0:T(8,128)(2,1)}, bf16[128,1024]{1,0:T(8,128)(2,1)}) custom-call(s32[1,256]{1,0:T(1,128)} %bitcast.22, s32[1,256]{1,0:T(1,128)} %bitcast.25, f32[1,256]{1,0:T(1,128)} %bitcast.28, bf16[256,2048]{1,0:T(8,128)(2,1)} %tokens.1, bf16[256,2048]{1,0:T(8,128)(2,1)} %grad_output.1), custom_call_target="tpu_custom_call" | custom-call | flops 1000 | bytes 1000 | tf_op jit(solution)/shard_map/place_rows/pallas_call | solution.py:90
  3.7 3.1 %collective-permute-start.2 = (bf16[128,1024]{1,0:T(8,128)(2,1)}, bf16[128,1024]{1,0:T(8,128)(2,1)S(1)}, u32[]{:S(2)}, u32[]{:S(2)}) collective-permute-start(bf16[128,1024]{1,0:T(8,128)(2,1)} %get-tuple-element.36), channel_id=1, source_target_pairs={{0,2},{2,4},{4,6},{6,0},{1,3},{3,5},{5,7},{7,1},{8,10},{10,12},{12... | collective-permute-start | bytes 786440 | tf_op jit(solution)/shard_map/ppermute | solution.py:289
  6.8 2.1 %collective-permute-start.3 = (bf16[128,1024]{1,0:T(8,128)(2,1)}, bf16[128,1024]{1,0:T(8,128)(2,1)S(1)}, u32[]{:S(2)}, u32[]{:S(2)}) collective-permute-start(bf16[128,1024]{1,0:T(8,128)(2,1)} %get-tuple-element.38), channel_id=1, source_target_pairs={{0,6},{2,0},{4,2},{6,4},{1,7},{3,1},{5,3},{7,5},{8,14},{10,8},{12,... | collective-permute-start | bytes 786440 | tf_op jit(solution)/shard_map/ppermute | solution.py:289
  8.9 1.6 %copy-done.1 = bf16[1,1024,1024]{2,1,0:T(8,128)(2,1)S(1)} copy-done((bf16[1,1024,1024]{2,1,0:T(8,128)(2,1)S(1)}, bf16[1,1024,1024]{2,1,0:T(8,128)(2,1)}, u32[]{:S(2)}) %copy-start.1) | copy-done | bytes 2097176
  10.5 1.2 %copy-done.3 = bf16[256,2048]{1,0:T(8,128)(2,1)S(1)} copy-done((bf16[256,2048]{1,0:T(8,128)(2,1)S(1)}, bf16[256,2048]{1,0:T(8,128)(2,1)}, u32[]{:S(2)}) %copy-start.3) | copy-done | bytes 1048600
  11.7 1.2 %copy-done.4 = bf16[256,2048]{1,0:T(8,128)(2,1)S(1)} copy-done((bf16[256,2048]{1,0:T(8,128)(2,1)S(1)}, bf16[256,2048]{1,0:T(8,128)(2,1)}, u32[]{:S(2)}) %copy-start.4) | copy-done | bytes 1048600
  12.9 7.0 %expert_rows.3 = (bf16[2,512,2048]{2,1,0:T(8,128)(2,1)S(1)}, bf16[2,512,1024]{2,1,0:T(8,128)(2,1)S(1)}, bf16[2,128,512]{2,1,0:T(8,128)(2,1)S(1)}, bf16[2,128,512]{2,1,0:T(8,128)(2,1)S(1)}) custom-call(s32[1,256]{1,0:T(1,128)S(1)} %bitcast.23, s32[1,256]{1,0:T(1,128)S(1)} %bitcast.26, f32[1,256]{1,0:T(1,128)S(1)} %bitcast.29, ...), custom_call_target="tpu_custom_call" | custom-call | flops 1610612736 | bytes 10485760 | tf_op jit(solution)/shard_map/expert_rows/pallas_call | solution.py:194
  20.6 1.8 %collective-permute-start.6 = (bf16[256,1024]{1,0:T(8,128)(2,1)S(1)}, bf16[256,1024]{1,0:T(8,128)(2,1)S(1)}, u32[]{:S(2)}, u32[]{:S(2)}) collective-permute-start(bf16[256,1024]{1,0:T(8,128)(2,1)S(1)} %constant_dynamic-update-slice_fusion.refs_0_), channel_id=1, source_target_pairs={{0,8},{8,0},{16,24},{24,16},{1,9},{9,1},{17,25},{25,17},{2,10},{10... | collective-permute-start | bytes 1572872 | tf_op jit(solution)/shard_map/ppermute | solution.py:286
  22.3 1.5 %collective-permute-start.4 = (bf16[256,1024]{1,0:T(8,128)(2,1)S(1)}, bf16[256,1024]{1,0:T(8,128)(2,1)S(1)}, u32[]{:S(2)}, u32[]{:S(2)}) collective-permute-start(bf16[256,1024]{1,0:T(8,128)(2,1)S(1)} %constant_dynamic-update-slice_fusion.refs_0_), channel_id=1, source_target_pairs={{0,16},{8,24},{16,0},{24,8},{1,17},{9,25},{17,1},{25,9},{2,18},{10... | collective-permute-start | bytes 1572872 | tf_op jit(solution)/shard_map/ppermute | solution.py:286
  23.8 2.6 %collective-permute-start.10 = (bf16[128,1024]{1,0:T(8,128)(2,1)S(1)}, bf16[128,1024]{1,0:T(8,128)(2,1)S(1)}, u32[]{:S(2)}, u32[]{:S(2)}) collective-permute-start(bf16[128,1024]{1,0:T(8,128)(2,1)S(1)} %copy-done.8), channel_id=1, source_target_pairs={{0,4},{2,6},{4,0},{6,2},{1,5},{3,7},{5,1},{7,3},{8,12},{10,14},{12... | collective-permute-start | bytes 786440 | tf_op jit(solution)/shard_map/ppermute | solution.py:289
  26.4 8.1 %collective-permute-done.6.refs_1_ = bf16[256,1024]{1,0:T(8,128)(2,1)S(1)} collective-permute-done((bf16[256,1024]{1,0:T(8,128)(2,1)S(1)}, bf16[256,1024]{1,0:T(8,128)(2,1)S(1)}, u32[]{:S(2)}, u32[]{:S(2)}) %collective-permute-start.6) | collective-permute-done | bytes 524320 | tf_op jit(solution)/shard_map/ppermute | solution.py:286
  34.5 1.8 %collective-permute-start.7 = (bf16[256,512]{1,0:T(8,128)(2,1)S(1)}, bf16[256,512]{1,0:T(8,128)(2,1)S(1)}, u32[]{:S(2)}, u32[]{:S(2)}) collective-permute-start(bf16[256,512]{1,0:T(8,128)(2,1)S(1)} %slice.45), channel_id=1, source_target_pairs={{0,16},{8,24},{16,0},{24,8},{1,17},{9,25},{17,1},{25,9},{2,18},{10... | collective-permute-start | bytes 786440 | tf_op jit(solution)/shard_map/ppermute | solution.py:286
  36.4 1.6 %collective-permute-start.5 = (bf16[256,512]{1,0:T(8,128)(2,1)S(1)}, bf16[256,512]{1,0:T(8,128)(2,1)S(1)}, u32[]{:S(2)}, u32[]{:S(2)}) collective-permute-start(bf16[256,512]{1,0:T(8,128)(2,1)S(1)} %slice.44), channel_id=1, source_target_pairs={{0,8},{8,0},{16,24},{24,16},{1,9},{9,1},{17,25},{25,17},{2,10},{10... | collective-permute-start | bytes 786440 | tf_op jit(solution)/shard_map/ppermute | solution.py:286
  39.6 4.2 %collective-permute-done.7.refs_4_ = bf16[256,512]{1,0:T(8,128)(2,1)S(1)} collective-permute-done((bf16[256,512]{1,0:T(8,128)(2,1)S(1)}, bf16[256,512]{1,0:T(8,128)(2,1)S(1)}, u32[]{:S(2)}, u32[]{:S(2)}) %collective-permute-start.7) | collective-permute-done | bytes 262176 | tf_op jit(solution)/shard_map/ppermute | solution.py:286
  43.9 1.9 %collective-permute-done.5.refs_3_ = bf16[256,512]{1,0:T(8,128)(2,1)S(1)} collective-permute-done((bf16[256,512]{1,0:T(8,128)(2,1)S(1)}, bf16[256,512]{1,0:T(8,128)(2,1)S(1)}, u32[]{:S(2)}, u32[]{:S(2)}) %collective-permute-start.5) | collective-permute-done | bytes 262176 | tf_op jit(solution)/shard_map/ppermute | solution.py:286
  45.7 1.5 %collective-permute-start.8 = (bf16[2,128,512]{2,1,0:T(8,128)(2,1)S(1)}, bf16[2,128,512]{2,1,0:T(8,128)(2,1)S(1)}, u32[]{:S(2)}, u32[]{:S(2)}) collective-permute-start(bf16[2,128,512]{2,1,0:T(8,128)(2,1)S(1)} %get-tuple-element.39), channel_id=1, source_target_pairs={{0,8},{8,0},{16,24},{24,16},{1,9},{9,1},{17,25},{25,17},{2,10},{10... | collective-permute-start | bytes 786440 | tf_op jit(solution)/shard_map/ppermute | solution.py:286
  47.8 1.8 %collective-permute-start.18 = (bf16[128,512]{1,0:T(8,128)(2,1)S(1)}, bf16[128,512]{1,0:T(8,128)(2,1)S(1)}, u32[]{:S(2)}, u32[]{:S(2)}) collective-permute-start(bf16[128,512]{1,0:T(8,128)(2,1)S(1)} %slice.50), channel_id=1, source_target_pairs={{0,8},{8,0},{16,24},{24,16},{1,9},{9,1},{17,25},{25,17},{2,10},{10... | collective-permute-start | bytes 393224 | tf_op jit(solution)/shard_map/ppermute | solution.py:286
  49.5 1.8 %collective-permute-done.11.refs_1_ = bf16[128,1024]{1,0:T(8,128)(2,1)S(1)} collective-permute-done((bf16[128,1024]{1,0:T(8,128)(2,1)S(1)}, bf16[128,1024]{1,0:T(8,128)(2,1)S(1)}, u32[]{:S(2)}, u32[]{:S(2)}) %collective-permute-start.11) | collective-permute-done | bytes 262176 | tf_op jit(solution)/shard_map/ppermute | solution.py:286
  51.3 1.2 %collective-permute-start.19 = (bf16[128,512]{1,0:T(8,128)(2,1)S(1)}, bf16[128,512]{1,0:T(8,128)(2,1)S(1)}, u32[]{:S(2)}, u32[]{:S(2)}) collective-permute-start(bf16[128,512]{1,0:T(8,128)(2,1)S(1)} %slice.51), channel_id=1, source_target_pairs={{0,16},{8,24},{16,0},{24,8},{1,17},{9,25},{17,1},{25,9},{2,18},{10... | collective-permute-start | bytes 393224 | tf_op jit(solution)/shard_map/ppermute | solution.py:286
  52.5 7.0 %expert_rows.4 = (bf16[2,512,2048]{2,1,0:T(8,128)(2,1)S(1)}, bf16[2,512,1024]{2,1,0:T(8,128)(2,1)S(1)}, bf16[256,512]{1,0:T(8,128)(2,1)S(1)}, bf16[256,512]{1,0:...) custom-call(bf16[256,1024]{1,0:T(8,128)(2,1)S(1)} %constant_dynamic-, ...), custom_call_target="tpu_custom_call", output_to_operand_aliasing={{0}: (9, {}), {1}: (10, {})} | custom-call | flops 3221225472 | bytes 12582912 | tf_op jit(solution)/shard_map/expert_rows/pallas_call | solution.py:194
  60.5 1.5 %collective-permute-start.14 = (bf16[256,512]{1,0:T(8,128)(2,1)S(1)}, bf16[256,512]{1,0:T(8,128)(2,1)S(1)}, u32[]{:S(2)}, u32[]{:S(2)}) collective-permute-start(bf16[256,512]{1,0:T(8,128)(2,1)S(1)} %get-tuple-element.47), channel_id=1, source_target_pairs={{0,16},{8,24},{16,0},{24,8},{1,17},{9,25},{17,1},{25,9},{2,18},{10... | collective-permute-start | bytes 786440 | tf_op jit(solution)/shard_map/ppermute | solution.py:286
  63.1 6.6 %expert_rows.5 = (bf16[2,512,2048]{2,1,0:T(8,128)(2,1)S(1)}, bf16[2,512,1024]{2,1,0:T(8,128)(2,1)S(1)}, bf16[128,512]{1,0:T(8,128)(2,1)S(1)}, bf16[128,512]{1,0:...) custom-call(bf16[128,1024]{1,0:T(8,128)(2,1)S(1)} %collective-permut, ...), custom_call_target="tpu_custom_call", output_to_operand_aliasing={{0}: (9, {}), {1}: (10, {})} | custom-call | flops 1610612736 | bytes 10485760 | tf_op jit(solution)/shard_map/expert_rows/pallas_call | solution.py:194
  69.8 2.4 %convolution_convert_fusion = bf16[2,1024,1024]{2,1,0:T(8,128)(2,1)S(1)} fusion(bf16[2,512,1024]{2,1,0:T(8,128)(2,1)S(1)} %get-tuple-element.55.acts, bf16[2,512,2048]{2,1,0:T(8,128)(2,1)S(1)} %get-tuple-element.54.rows), kind=kOutput, calls=%fused_computation | convolution fusion | flops 2149580800 | bytes 8388608 | tf_op jit(solution)/shard_map/dot_general | solution.py:315
  73.3 1.5 %collective-permute-start.20 = (bf16[128,512]{1,0:T(8,128)(2,1)S(1)}, bf16[128,512]{1,0:T(8,128)(2,1)S(1)}, u32[]{:S(2)}, u32[]{:S(2)}) collective-permute-start(bf16[128,512]{1,0:T(8,128)(2,1)S(1)} %get-tuple-element.56), channel_id=1, source_target_pairs={{0,8},{8,0},{16,24},{24,16},{1,9},{9,1},{17,25},{25,17},{2,10},{10... | collective-permute-start | bytes 393224 | tf_op jit(solution)/shard_map/ppermute | solution.py:286
  75.3 1.5 %collective-permute-start.22 = (bf16[128,512]{1,0:T(8,128)(2,1)S(1)}, bf16[128,512]{1,0:T(8,128)(2,1)S(1)}, u32[]{:S(2)}, u32[]{:S(2)}) collective-permute-start(bf16[128,512]{1,0:T(8,128)(2,1)S(1)} %get-tuple-element.60), channel_id=1, source_target_pairs={{0,24},{8,16},{16,8},{24,0},{1,25},{9,17},{17,9},{25,1},{2,26},{10... | collective-permute-start | bytes 393224 | tf_op jit(solution)/shard_map/ppermute | solution.py:286
  77.0 2.3 %collective-permute-done.20 = bf16[128,512]{1,0:T(8,128)(2,1)S(1)} collective-permute-done((bf16[128,512]{1,0:T(8,128)(2,1)S(1)}, bf16[128,512]{1,0:T(8,128)(2,1)S(1)}, u32[]{:S(2)}, u32[]{:S(2)}) %collective-permute-start.20) | collective-permute-done | bytes 131104 | tf_op jit(solution)/shard_map/ppermute | solution.py:286
  79.3 1.6 %collective-permute-start.17 = (bf16[128,512]{1,0:T(8,128)(2,1)S(1)}, bf16[128,512]{1,0:T(8,128)(2,1)S(1)}, u32[]{:S(2)}, u32[]{:S(2)}) collective-permute-start(bf16[128,512]{1,0:T(8,128)(2,1)S(1)} %get-tuple-element.65), channel_id=1, source_target_pairs={{0,2},{2,4},{4,6},{6,0},{1,3},{3,5},{5,7},{7,1},{8,10},{10,12},{12... | collective-permute-start | bytes 393224 | tf_op jit(solution)/shard_map/ppermute | solution.py:289
  80.9 3.0 %collective-permute-done.21 = bf16[128,512]{1,0:T(8,128)(2,1)S(1)} collective-permute-done((bf16[128,512]{1,0:T(8,128)(2,1)S(1)}, bf16[128,512]{1,0:T(8,128)(2,1)S(1)}, u32[]{:S(2)}, u32[]{:S(2)}) %collective-permute-start.21) | collective-permute-done | bytes 131104 | tf_op jit(solution)/shard_map/ppermute | solution.py:286
  83.9 3.6 %collective-permute-start.16 = (bf16[128,512]{1,0:T(8,128)(2,1)S(1)}, bf16[128,512]{1,0:T(8,128)(2,1)S(1)}, u32[]{:S(2)}, u32[]{:S(2)}) collective-permute-start(bf16[128,512]{1,0:T(8,128)(2,1)S(1)} %get-tuple-element.66), channel_id=1, source_target_pairs={{0,6},{2,0},{4,2},{6,4},{1,7},{3,1},{5,3},{7,5},{8,14},{10,8},{12,... | collective-permute-start | bytes 393224 | tf_op jit(solution)/shard_map/ppermute | solution.py:289
  87.8 3.9 %weight_grads.1 = (bf16[1024,1024]{1,0:T(8,128)(2,1)}, bf16[1024,1024]{1,0:T(8,128)(2,1)}) custom-call(bf16[2,512,2048]{2,1,0:T(8,128)(2,1)S(1)} %get-tuple-element.54.rows, bf16[2,512,1024]{2,1,0:T(8,128)(2,1)S(1)} %get-tuple-element.55.acts, bf16[2,1024,1024]{2,1,0:T(8,128)(2,1)S(1)} %collective-permute-done.24.got), custom_call_target="tpu_custom_call" | custom-call | flops 1000 | bytes 1000 | tf_op jit(solution)/shard_map/weight_grads/pallas_call | solution.py:258
  91.7 4.1 %collective-permute-done.23.refs_3_ = bf16[128,512]{1,0:T(8,128)(2,1)S(1)} collective-permute-done((bf16[128,512]{1,0:T(8,128)(2,1)S(1)}, bf16[128,512]{1,0:T(8,128)(2,1)S(1)}, u32[]{:S(2)}, u32[]{:S(2)}) %collective-permute-start.23) | collective-permute-done | bytes 131104 | tf_op jit(solution)/shard_map/ppermute | solution.py:289
  95.8 1.2 %unplace_rows.1 = bf16[256,512]{1,0:T(8,128)(2,1)} custom-call(s32[1,256]{1,0:T(1,128)S(1)} %bitcast.24, s32[1,256]{1,0:T(1,128)S(1)} %bitcast.27, bf16[128,512]{1,0:T(8,128)(2,1)S(1)} %fusion.1.refs_0_, bf16[128,512]{1,0:T(8,128)(2,1)S(1)} %collective-permute-done.16.refs_1_, bf16[128,512]{1,0:T(8,128)(2,1)S(1)} %collective-permute-done.17.refs_2_, ...), custom_call_target="tpu_custom_call" | custom-call | flops 1000 | bytes 1000 | tf_op jit(solution)/shard_map/unplace_rows/pallas_call | solution.py:230
  (54 shorter events, 7.5 us)
Async XLA Ops:
  0.6 8.2 %copy-start = (bf16[1,1024,1024]{2,1,0:T(8,128)(2,1)S(1)}, bf16[1,1024,1024]{2,1,0:T(8,128)(2,1)}, u32[]{:S(2)}) copy-start(bf16[1,1024,1024]{2,1,0:T(8,128)(2,1)} %param.12) | copy-start | bytes 6291460
  0.6 8.2 %copy-start.6 = (s32[256,1]{0,1:T(1,128)S(1)}, s32[256,1]{0,1:T(1,128)}, u32[]{:S(2)}) copy-start(s32[256,1]{0,1:T(1,128)} %param.11) | copy-start | bytes 3076
  0.7 8.2 %copy-start.5 = (s32[256,1]{0,1:T(1,128)S(1)}, s32[256,1]{0,1:T(1,128)}, u32[]{:S(2)}) copy-start(s32[256,1]{0,1:T(1,128)} %param.10) | copy-start | bytes 3076
  0.7 8.2 %copy-start.7 = (f32[256]{0:T(256)S(1)}, f32[256]{0:T(256)}, u32[]{:S(2)}) copy-start(f32[256]{0:T(256)} %param.9) | copy-start | bytes 3076
  0.7 8.2 %collective-permute-start = (bf16[1024,1024]{1,0:T(8,128)(2,1)}, bf16[1024,1024]{1,0:T(8,128)(2,1)S(1)}, u32[]{:S(2)}, u32[]{:S(2)}) collective-permute-start(bf16[1024,1024]{1,0:T(8,128)(2,1)} %bitcast.14), channel_id=1, source_target_pairs={{0,1},{1,0},{2,3},{3,2},{4,5},{5,4},{6,7},{7,6},{8,9},{9,8},{10,11... | collective-permute-start | bytes 6291464 | tf_op jit(solution)/shard_map/ppermute | solution.py:283
  1.2 7.7 %collective-permute-start.1 = (bf16[1024,1024]{1,0:T(8,128)(2,1)}, bf16[1024,1024]{1,0:T(8,128)(2,1)S(1)}, u32[]{:S(2)}, u32[]{:S(2)}) collective-permute-start(bf16[1024,1024]{1,0:T(8,128)(2,1)} %bitcast.18), channel_id=1, source_target_pairs={{0,1},{1,0},{2,3},{3,2},{4,5},{5,4},{6,7},{7,6},{8,9},{9,8},{10,11... | collective-permute-start | bytes 6291464 | tf_op jit(solution)/shard_map/ppermute | solution.py:283
  3.7 16.3 %collective-permute-start.2 = (bf16[128,1024]{1,0:T(8,128)(2,1)}, bf16[128,1024]{1,0:T(8,128)(2,1)S(1)}, u32[]{:S(2)}, u32[]{:S(2)}) collective-permute-start(bf16[128,1024]{1,0:T(8,128)(2,1)} %get-tuple-element.36), channel_id=1, source_target_pairs={{0,2},{2,4},{4,6},{6,0},{1,3},{3,5},{5,7},{7,1},{8,10},{10,12},{12... | collective-permute-start | bytes 786440 | tf_op jit(solution)/shard_map/ppermute | solution.py:289
  6.8 13.8 %collective-permute-start.3 = (bf16[128,1024]{1,0:T(8,128)(2,1)}, bf16[128,1024]{1,0:T(8,128)(2,1)S(1)}, u32[]{:S(2)}, u32[]{:S(2)}) collective-permute-start(bf16[128,1024]{1,0:T(8,128)(2,1)} %get-tuple-element.38), channel_id=1, source_target_pairs={{0,6},{2,0},{4,2},{6,4},{1,7},{3,1},{5,3},{7,5},{8,14},{10,8},{12,... | collective-permute-start | bytes 786440 | tf_op jit(solution)/shard_map/ppermute | solution.py:289
  8.9 1.6 %copy-start.1 = (bf16[1,1024,1024]{2,1,0:T(8,128)(2,1)S(1)}, bf16[1,1024,1024]{2,1,0:T(8,128)(2,1)}, u32[]{:S(2)}) copy-start(bf16[1,1024,1024]{2,1,0:T(8,128)(2,1)} %param.13) | copy-start | bytes 6291460
  12.9 10.9 %copy-start.8 = (bf16[128,1024]{1,0:T(8,128)(2,1)S(1)}, bf16[128,1024]{1,0:T(8,128)(2,1)}, u32[]{:S(2)}) copy-start(bf16[128,1024]{1,0:T(8,128)(2,1)} %get-tuple-element.40) | copy-start | bytes 786436
  20.0 32.5 %copy-start.2 = (bf16[1,1024,1024]{2,1,0:T(8,128)(2,1)S(1)}, bf16[1,1024,1024]{2,1,0:T(8,128)(2,1)}, u32[]{:S(2)}) copy-start(bf16[1,1024,1024]{2,1,0:T(8,128)(2,1)} %param.13) | copy-start | bytes 6291460
  20.6 14.0 %collective-permute-start.6 = (bf16[256,1024]{1,0:T(8,128)(2,1)S(1)}, bf16[256,1024]{1,0:T(8,128)(2,1)S(1)}, u32[]{:S(2)}, u32[]{:S(2)}) collective-permute-start(bf16[256,1024]{1,0:T(8,128)(2,1)S(1)} %constant_dynamic-update-slice_fusion.refs_0_), channel_id=1, source_target_pairs={{0,8},{8,0},{16,24},{24,16},{1,9},{9,1},{17,25},{25,17},{2,10},{10... | collective-permute-start | bytes 1572872 | tf_op jit(solution)/shard_map/ppermute | solution.py:286
  22.3 14.1 %collective-permute-start.4 = (bf16[256,1024]{1,0:T(8,128)(2,1)S(1)}, bf16[256,1024]{1,0:T(8,128)(2,1)S(1)}, u32[]{:S(2)}, u32[]{:S(2)}) collective-permute-start(bf16[256,1024]{1,0:T(8,128)(2,1)S(1)} %constant_dynamic-update-slice_fusion.refs_0_), channel_id=1, source_target_pairs={{0,16},{8,24},{16,0},{24,8},{1,17},{9,25},{17,1},{25,9},{2,18},{10... | collective-permute-start | bytes 1572872 | tf_op jit(solution)/shard_map/ppermute | solution.py:286
  23.8 14.3 %collective-permute-start.10 = (bf16[128,1024]{1,0:T(8,128)(2,1)S(1)}, bf16[128,1024]{1,0:T(8,128)(2,1)S(1)}, u32[]{:S(2)}, u32[]{:S(2)}) collective-permute-start(bf16[128,1024]{1,0:T(8,128)(2,1)S(1)} %copy-done.8), channel_id=1, source_target_pairs={{0,4},{2,6},{4,0},{6,2},{1,5},{3,7},{5,1},{7,3},{8,12},{10,14},{12... | collective-permute-start | bytes 786440 | tf_op jit(solution)/shard_map/ppermute | solution.py:289
  34.5 9.3 %collective-permute-start.7 = (bf16[256,512]{1,0:T(8,128)(2,1)S(1)}, bf16[256,512]{1,0:T(8,128)(2,1)S(1)}, u32[]{:S(2)}, u32[]{:S(2)}) collective-permute-start(bf16[256,512]{1,0:T(8,128)(2,1)S(1)} %slice.45), channel_id=1, source_target_pairs={{0,16},{8,24},{16,0},{24,8},{1,17},{9,25},{17,1},{25,9},{2,18},{10... | collective-permute-start | bytes 786440 | tf_op jit(solution)/shard_map/ppermute | solution.py:286
  36.4 9.3 %collective-permute-start.5 = (bf16[256,512]{1,0:T(8,128)(2,1)S(1)}, bf16[256,512]{1,0:T(8,128)(2,1)S(1)}, u32[]{:S(2)}, u32[]{:S(2)}) collective-permute-start(bf16[256,512]{1,0:T(8,128)(2,1)S(1)} %slice.44), channel_id=1, source_target_pairs={{0,8},{8,0},{16,24},{24,16},{1,9},{9,1},{17,25},{25,17},{2,10},{10... | collective-permute-start | bytes 786440 | tf_op jit(solution)/shard_map/ppermute | solution.py:286
  38.1 9.6 %collective-permute-start.12 = (bf16[128,1024]{1,0:T(8,128)(2,1)S(1)}, bf16[128,1024]{1,0:T(8,128)(2,1)S(1)}, u32[]{:S(2)}, u32[]{:S(2)}) collective-permute-start(bf16[128,1024]{1,0:T(8,128)(2,1)S(1)} %collective-permute-done.10.refs_0_), channel_id=1, source_target_pairs={{0,16},{8,24},{16,0},{24,8},{1,17},{9,25},{17,1},{25,9},{2,18},{10... | collective-permute-start | bytes 786440 | tf_op jit(solution)/shard_map/ppermute | solution.py:286
  38.6 12.7 %collective-permute-start.11 = (bf16[128,1024]{1,0:T(8,128)(2,1)S(1)}, bf16[128,1024]{1,0:T(8,128)(2,1)S(1)}, u32[]{:S(2)}, u32[]{:S(2)}) collective-permute-start(bf16[128,1024]{1,0:T(8,128)(2,1)S(1)} %collective-permute-done.10.refs_0_), channel_id=1, source_target_pairs={{0,8},{8,0},{16,24},{24,16},{1,9},{9,1},{17,25},{25,17},{2,10},{10... | collective-permute-start | bytes 786440 | tf_op jit(solution)/shard_map/ppermute | solution.py:286
  45.7 16.4 %collective-permute-start.8 = (bf16[2,128,512]{2,1,0:T(8,128)(2,1)S(1)}, bf16[2,128,512]{2,1,0:T(8,128)(2,1)S(1)}, u32[]{:S(2)}, u32[]{:S(2)}) collective-permute-start(bf16[2,128,512]{2,1,0:T(8,128)(2,1)S(1)} %get-tuple-element.39), channel_id=1, source_target_pairs={{0,8},{8,0},{16,24},{24,16},{1,9},{9,1},{17,25},{25,17},{2,10},{10... | collective-permute-start | bytes 786440 | tf_op jit(solution)/shard_map/ppermute | solution.py:286
  47.8 15.4 %collective-permute-start.18 = (bf16[128,512]{1,0:T(8,128)(2,1)S(1)}, bf16[128,512]{1,0:T(8,128)(2,1)S(1)}, u32[]{:S(2)}, u32[]{:S(2)}) collective-permute-start(bf16[128,512]{1,0:T(8,128)(2,1)S(1)} %slice.50), channel_id=1, source_target_pairs={{0,8},{8,0},{16,24},{24,16},{1,9},{9,1},{17,25},{25,17},{2,10},{10... | collective-permute-start | bytes 393224 | tf_op jit(solution)/shard_map/ppermute | solution.py:286
  51.3 11.8 %collective-permute-start.19 = (bf16[128,512]{1,0:T(8,128)(2,1)S(1)}, bf16[128,512]{1,0:T(8,128)(2,1)S(1)}, u32[]{:S(2)}, u32[]{:S(2)}) collective-permute-start(bf16[128,512]{1,0:T(8,128)(2,1)S(1)} %slice.51), channel_id=1, source_target_pairs={{0,16},{8,24},{16,0},{24,8},{1,17},{9,25},{17,1},{25,9},{2,18},{10... | collective-permute-start | bytes 393224 | tf_op jit(solution)/shard_map/ppermute | solution.py:286
  59.6 12.6 %collective-permute-start.13 = (bf16[256,512]{1,0:T(8,128)(2,1)S(1)}, bf16[256,512]{1,0:T(8,128)(2,1)S(1)}, u32[]{:S(2)}, u32[]{:S(2)}) collective-permute-start(bf16[256,512]{1,0:T(8,128)(2,1)S(1)} %get-tuple-element.46), channel_id=1, source_target_pairs={{0,8},{8,0},{16,24},{24,16},{1,9},{9,1},{17,25},{25,17},{2,10},{10... | collective-permute-start | bytes 786440 | tf_op jit(solution)/shard_map/ppermute | solution.py:286
  60.5 11.7 %collective-permute-start.14 = (bf16[256,512]{1,0:T(8,128)(2,1)S(1)}, bf16[256,512]{1,0:T(8,128)(2,1)S(1)}, u32[]{:S(2)}, u32[]{:S(2)}) collective-permute-start(bf16[256,512]{1,0:T(8,128)(2,1)S(1)} %get-tuple-element.47), channel_id=1, source_target_pairs={{0,16},{8,24},{16,0},{24,8},{1,17},{9,25},{17,1},{25,9},{2,18},{10... | collective-permute-start | bytes 786440 | tf_op jit(solution)/shard_map/ppermute | solution.py:286
  62.1 10.1 %collective-permute-start.15 = (bf16[256,512]{1,0:T(8,128)(2,1)S(1)}, bf16[256,512]{1,0:T(8,128)(2,1)S(1)}, u32[]{:S(2)}, u32[]{:S(2)}) collective-permute-start(bf16[256,512]{1,0:T(8,128)(2,1)S(1)} %get-tuple-element.48), channel_id=1, source_target_pairs={{0,24},{8,16},{16,8},{24,0},{1,25},{9,17},{17,9},{25,1},{2,26},{10... | collective-permute-start | bytes 786440 | tf_op jit(solution)/shard_map/ppermute | solution.py:286
  72.2 15.6 %collective-permute-start.24 = (bf16[2,1024,1024]{2,1,0:T(8,128)(2,1)S(1)}, bf16[2,1024,1024]{2,1,0:T(8,128)(2,1)S(1)}, u32[]{:S(2)}, u32[]{:S(2)}) collective-permute-start(bf16[2,1024,1024]{2,1,0:T(8,128)(2,1)S(1)} %convolution_convert_fusion), channel_id=1, source_target_pairs={{0,1},{1,0},{2,3},{3,2},{4,5},{5,4},{6,7},{7,6},{8,9},{9,8},{10,11... | collective-permute-start | bytes 12582920 | tf_op jit(solution)/shard_map/ppermute | solution.py:283
  72.3 15.4 %collective-permute-start.9 = (bf16[128,512]{1,0:T(8,128)(2,1)S(1)}, bf16[128,512]{1,0:T(8,128)(2,1)S(1)}, u32[]{:S(2)}, u32[]{:S(2)}) collective-permute-start(bf16[128,512]{1,0:T(8,128)(2,1)S(1)} %fusion.2), channel_id=1, source_target_pairs={{0,16},{8,24},{16,0},{24,8},{1,17},{9,25},{17,1},{25,9},{2,18},{10... | collective-permute-start | bytes 393224 | tf_op jit(solution)/shard_map/ppermute | solution.py:286
  73.3 6.0 %collective-permute-start.20 = (bf16[128,512]{1,0:T(8,128)(2,1)S(1)}, bf16[128,512]{1,0:T(8,128)(2,1)S(1)}, u32[]{:S(2)}, u32[]{:S(2)}) collective-permute-start(bf16[128,512]{1,0:T(8,128)(2,1)S(1)} %get-tuple-element.56), channel_id=1, source_target_pairs={{0,8},{8,0},{16,24},{24,16},{1,9},{9,1},{17,25},{25,17},{2,10},{10... | collective-permute-start | bytes 393224 | tf_op jit(solution)/shard_map/ppermute | solution.py:286
  74.8 9.1 %collective-permute-start.21 = (bf16[128,512]{1,0:T(8,128)(2,1)S(1)}, bf16[128,512]{1,0:T(8,128)(2,1)S(1)}, u32[]{:S(2)}, u32[]{:S(2)}) collective-permute-start(bf16[128,512]{1,0:T(8,128)(2,1)S(1)} %get-tuple-element.58), channel_id=1, source_target_pairs={{0,16},{8,24},{16,0},{24,8},{1,17},{9,25},{17,1},{25,9},{2,18},{10... | collective-permute-start | bytes 393224 | tf_op jit(solution)/shard_map/ppermute | solution.py:286
  75.3 12.2 %collective-permute-start.22 = (bf16[128,512]{1,0:T(8,128)(2,1)S(1)}, bf16[128,512]{1,0:T(8,128)(2,1)S(1)}, u32[]{:S(2)}, u32[]{:S(2)}) collective-permute-start(bf16[128,512]{1,0:T(8,128)(2,1)S(1)} %get-tuple-element.60), channel_id=1, source_target_pairs={{0,24},{8,16},{16,8},{24,0},{1,25},{9,17},{17,9},{25,1},{2,26},{10... | collective-permute-start | bytes 393224 | tf_op jit(solution)/shard_map/ppermute | solution.py:286
  79.3 16.6 %collective-permute-start.17 = (bf16[128,512]{1,0:T(8,128)(2,1)S(1)}, bf16[128,512]{1,0:T(8,128)(2,1)S(1)}, u32[]{:S(2)}, u32[]{:S(2)}) collective-permute-start(bf16[128,512]{1,0:T(8,128)(2,1)S(1)} %get-tuple-element.65), channel_id=1, source_target_pairs={{0,2},{2,4},{4,6},{6,0},{1,3},{3,5},{5,7},{7,1},{8,10},{10,12},{12... | collective-permute-start | bytes 393224 | tf_op jit(solution)/shard_map/ppermute | solution.py:289
  83.9 11.9 %collective-permute-start.16 = (bf16[128,512]{1,0:T(8,128)(2,1)S(1)}, bf16[128,512]{1,0:T(8,128)(2,1)S(1)}, u32[]{:S(2)}, u32[]{:S(2)}) collective-permute-start(bf16[128,512]{1,0:T(8,128)(2,1)S(1)} %get-tuple-element.66), channel_id=1, source_target_pairs={{0,6},{2,0},{4,2},{6,4},{1,7},{3,1},{5,3},{7,5},{8,14},{10,8},{12,... | collective-permute-start | bytes 393224 | tf_op jit(solution)/shard_map/ppermute | solution.py:289
  87.6 8.2 %collective-permute-start.23 = (bf16[128,512]{1,0:T(8,128)(2,1)S(1)}, bf16[128,512]{1,0:T(8,128)(2,1)S(1)}, u32[]{:S(2)}, u32[]{:S(2)}) collective-permute-start(bf16[128,512]{1,0:T(8,128)(2,1)S(1)} %add_convert_fusion.1), channel_id=1, source_target_pairs={{0,4},{2,6},{4,0},{6,2},{1,5},{3,7},{5,1},{7,3},{8,12},{10,14},{12... | collective-permute-start | bytes 393224 | tf_op jit(solution)/shard_map/ppermute | solution.py:289
  (2 other events, 2.4 us)

commit v10 on v9

--- a/solution.py
+++ b/solution.py
@@ -111,23 +111,23 @@
     return pre * half, half + 0.5 * pre * (1.0 - th * th) * (c + (3 * 0.044715 * c) * square)
 
 
-def expert_kernel(first, base, groups, aliased, *refs):
+def expert_kernel(chunks, base, groups, aliased, *refs):
     refs = list(refs)
     take = lambda n: [refs.pop(0) for _ in range(n)]
-    slots = take(5)
+    slots = take(5) if chunks is None else [take(n) for n in chunks]
     up_halves, down_halves = take(2), take(2)
     take(aliased)
     kept_rows, kept_acts = take(2)
     targets = [take(4 if step is None else 2) for _, step in groups]
     tok, grad, up, down, hidden, slope, back = take(7)
-    if first is None:
+    if chunks is None:
         tok_in, grad_in = take(2)
     copies = Copies(take(1)[0])
     rows, width = tok.shape
     half, share = width // 2, width // 4
     order = lax.axis_index("tensor") ^ (2 * lax.axis_index("dp"))
     arrive = []
-    if first is None:
+    if chunks is None:
         mine = lax.axis_index("dp")
         count = tok_in.shape[0]
         for src, dst in zip(slots[3:], (tok_in, grad_in)):
@@ -135,14 +135,17 @@
                 source = src.at[:, pl.ds(pl.multiple_of(start, half), half)]
                 arrive += copies.rows(source, dst.at[:, pl.ds(i * half, half)], count, 2)
     else:
-        span = pl.ds(first, rows)
-        for j in range(4):
-            columns = pl.ds(pl.multiple_of((order ^ j) * share, share), share)
-            if j < 3:
-                sources = [slots[j].at[span, pl.ds(0, share)], slots[j].at[span, pl.ds(share, share)]]
-            else:
-                sources = [slots[3].at[span, :], slots[4].at[span, :]]
-            arrive += [copies.start(src, dst.at[:, columns]) for src, dst in zip(sources, (tok, grad))]
+        at = 0
+        for chunk in slots:
+            n = chunk[0].shape[0]
+            for j in range(4):
+                columns = pl.ds(pl.multiple_of((order ^ j) * share, share), share)
+                if j == 3 and len(chunk) == 5:
+                    sources = chunk[3:]
+                else:
+                    sources = [chunk[j].at[:, pl.ds(i * share, share)] for i in range(2)]
+                arrive += [copies.start(src, dst.at[pl.ds(at, n), columns]) for src, dst in zip(sources, (tok, grad))]
+            at += n
     hid = hidden.shape[1]
     step = 256
     tiles = []
@@ -152,11 +155,11 @@
         for halves, dst in ((up_halves, up), (down_halves, down)):
             for i in range(2):
                 tiles[-1].append(copies.start(halves[i].at[:, cols], dst.at[pl.ds(i * half, half), cols]))
-    if first is None:
+    if chunks is None:
         hit = hits(places(slots[0], slots[1], rows), expert_first(0, rows), rows)
         hot, scale = hit.astype(BF16), gate_of(hit, slots[2][...])
     wait(arrive)
-    if first is None:
+    if chunks is None:
         tok[...] = dot(hot, tok_in[...]).astype(BF16)
         grad[...] = (dot(hot, grad_in[...]) * scale).astype(BF16)
     mine = pl.ds(base, rows)
@@ -181,7 +184,9 @@
     wait(leave)
 
 
-def expert_rows(slots, first, groups, weights, total_rows, base, kept):
+def expert_rows(own, chunks, groups, weights, total_rows, base, kept):
+    slots = own or sum(chunks, [])
+    counts_in = None if own else [len(c) for c in chunks]
     rows = sum(n for n, _ in groups)
     half, hid = weights[0].shape
     width, share = 2 * half, half // 2
@@ -192,16 +197,16 @@
     quarters = [[shape(n, share)] * 4 if step is None else [shape(2, n, share)] * 2 for n, step in groups]
     counts = [len(q) for q in quarters]
     out = pl.pallas_call(
-        functools.partial(expert_kernel, first, base, groups, len(aliases)),
+        functools.partial(expert_kernel, counts_in, base, groups, len(aliases)),
         out_shape=[shape(2, total_rows, width), shape(2, total_rows, hid)] + sum(quarters, []),
-        in_specs=([VMEM] * 3 if first is None else [ANY] * 3) + [ANY] * (len(operands) - 3),
+        in_specs=([VMEM] * 3 if own else [ANY] * 3) + [ANY] * (len(operands) - 3),
         out_specs=[ANY] * (2 + sum(counts)),
         scratch_shapes=[
             buf(rows, width), buf(rows, width), buf(width, hid), buf(width, hid),
             buf(rows, hid), buf(rows, hid), buf(4, rows, share),
         ]
-        + ([buf(*slots[3].shape)] * 2 if first is None else [])
-        + [pltpu.SemaphoreType.DMA((12 + 4 * (hid // 256) + 4 * len(groups),))],
+        + ([buf(*own[3].shape)] * 2 if own else [])
+        + [pltpu.SemaphoreType.DMA((16 + 4 * (hid // 256) + 4 * len(groups) + 4,))],
         input_output_aliases=aliases,
         compiler_params=pltpu.CompilerParams(vmem_limit_bytes=LIMIT + rows * 2**15),
         cost_estimate=pl.CostEstimate(
@@ -320,25 +325,30 @@
     weights = [up_own, swap(up_own), down_own, swap(down_own)]
 
     if experts == 4:
-        shifts = [1, 3, 2]
+        shifts = [1, 2, 3]
         sends = place([capacity] * 3, shifts, capacity, index, slot, gate, tokens, grad_output)
-        moved = [shift(rows, k) for rows, k in zip(sends, shifts)]
         everything = 4 * capacity
-        own = [index, slot, gate, tokens, grad_output]
+        one = shift(sends[0], 1)
+        two = shift(after(sends[1], one, weights[1], weights[3]), 2)
+        own = [after(index, one), slot, gate, tokens, grad_output]
         kept, (pair,) = expert_rows(own, None, [(capacity, 1)], weights, everything, 0, None)
-        near = spread(jnp.concatenate([after(moved[0], pair[0]), moved[1]], 0))
-        far = spread(after(moved[2], *near[1:3]))
-        near[0] = after(near[0], *far[1:3])
-        back, got_own = collect_pair([pair[0], after(pair[1], *near[3:])], 1)
-        kept, (blocks,) = expert_rows(near, 0, [(2 * capacity, None)], weights, everything, capacity, kept)
+        first = spread(one)
+        three = shift(after(sends[2], two, *first[1:3]), 3)
+        second = spread(after(two, pair[0]))
+        third = after(three, *second[1:3])
+        third = [third] + [across(third, j) for j in (1, 2, 3)]
+        back, got_own = collect_pair([pair[0], after(pair[1], *first[3:])], 1)
+        kept, (blocks,) = expert_rows(
+            None, [first, second], [(2 * capacity, None)], weights, everything, capacity, kept
+        )
         total, got = collect(blocks)
-        backs = [back, shift(total[:capacity], -1), shift(total[capacity:], -3)]
-        slots = [after(far[0], got_own)] + far[1:]
-        kept, (blocks,) = expert_rows(slots, 0, [(capacity, None)], weights, everything, 3 * capacity, kept)
+        backs = [back, shift(total[:capacity], -1), shift(total[capacity:], -2)]
+        third[0] = after(third[0], got_own)
+        kept, (blocks,) = expert_rows(None, [third], [(capacity, None)], weights, everything, 3 * capacity, kept)
         others = other_halves(kept)
         grads = weight_grads(*kept, swap(after(others, *got)))
         total, _ = collect([blocks[0]] + [after(b, got[0], others) for b in blocks[1:]])
-        backs.append(after(shift(total, -2), *grads))
+        backs.append(after(shift(total, -3), *grads))
         shifts = [0] + shifts
     else:
         rows = experts * capacity
@@ -351,7 +361,7 @@
             return moved.reshape(rows, x.shape[1])
 
         (send,) = place([rows], shifts, capacity, index, slot, gate, tokens, grad_output)
-        kept, (blocks,) = expert_rows(spread(exchange(send)), 0, [(rows, None)], weights, rows, 0, None)
+        kept, (blocks,) = expert_rows(None, [spread(exchange(send))], [(rows, None)], weights, rows, 0, None)
         others = other_halves(kept)
         grads = weight_grads(*kept, swap(others))
         total, _ = collect(blocks)

time: 97.2 us -> 101 us (1.039)
  waiting for transfers between devices: 26.7 us -> 32.9 us
  starting transfers between devices: 34.4 us -> 31.5 us
    ppermute x6, waiting for transfers between devices: 4.82 us -> 13.1 us  [shift(): lax.ppermute(x, 'expert', [(i, (i + k) % experts) for i in range(experts)])]
    ppermute x6, starting transfers between devices: 13.1 us -> 9.51 us  [shift(): lax.ppermute(x, 'expert', [(i, (i + k) % experts) for i in range(experts)])]
    ppermute x16 -> x19, waiting for transfers between devices: 21.9 us -> 19.7 us  [across(): return lax.ppermute(x, 'tensor', [(i, i ^ j) for i in range(tensor_size)])]
    ppermute x16 -> x19, starting transfers between devices: 20.6 us -> 21.3 us  [across(): return lax.ppermute(x, 'tensor', [(i, i ^ j) for i in range(tensor_size)])]
    unnamed x19 -> x18, local copies, waits for them, and re-layouts: 4.08 us -> 4.06 us
  transfers between devices with their start and end apart: 25 -> 28, of which waited for: 10 -> 11; matrix products, arithmetic and copies ran while one was open for 3% -> 3% of each run, Pallas kernels for 28% -> 27%
where the time goes in v10:
time: 101 us
  waiting for transfers between devices  32.9 us (33%)
  starting transfers between devices  31.5 us (31%)
  Pallas kernels  28.6 us (28%)
  local copies, waits for them, and re-layouts  4.12 us (4%)
  matrix products  2.39 us (2%)
    ppermute x19, starting transfers between devices, across(): return lax.ppermute(x, 'tensor', [(i, i ^ j) for i in range(tensor_size)])  21.3 us
    pallas_call x3, Pallas kernels, expert_rows(): pl.pallas_call(functools.partial(expert_kernel, counts_in, base, groups,...  21.1 us
    ppermute x19, waiting for transfers between devices, across(): return lax.ppermute(x, 'tensor', [(i, i ^ j) for i in range(tensor_size)])  19.7 us
    ppermute x6, waiting for transfers between devices, shift(): lax.ppermute(x, 'expert', [(i, (i + k) % experts) for i in range(experts)])  13.1 us
    ppermute x6, starting transfers between devices, shift(): lax.ppermute(x, 'expert', [(i, (i + k) % experts) for i in range(experts)])  9.51 us
    unnamed x18, local copies, waits for them, and re-layouts  4.06 us
    pallas_call x1, Pallas kernels, weight_grads(): pl.pallas_call(weight_grad_kernel, out_shape=[jax.ShapeDtypeStruct((half,...  3.87 us
    pallas_call x1, Pallas kernels, place(): pl.pallas_call(functools.partial(place_kernel, spans, shifts, capacity),...  2.41 us
  transfers between devices with their start and end apart: 28, of which 11 were waited for; matrix products, arithmetic and copies ran while one was open for 3% of the time, Pallas kernels for 27%

profile of v10, /device:TPU:0, one launch (start us, length us, event | category | flops | bytes accessed | tf_op | source)
XLA Modules:
  0.0 100.5 jit_solution(18259021893467180221)
XLA Ops:
  1.3 2.4 %place_rows.1 = (bf16[128,1024]{1,0:T(8,128)(2,1)}, bf16[128,1024]{1,0:T(8,128)(2,1)}, bf16[128,1024]{1,0:T(8,128)(2,1)}) custom-call(s32[1,256]{1,0:T(1,128)} %bitcast.22, s32[1,256]{1,0:T(1,128)} %bitcast.25, f32[1,256]{1,0:T(1,128)} %bitcast.28, bf16[256,2048]{1,0:T(8,128)(2,1)} %refs_3_.1, bf16[256,2048]{1,0:T(8,128)(2,1)} %refs_4_.1), custom_call_target="tpu_custom_call" | custom-call | flops 1000 | bytes 1000 | tf_op jit(solution)/shard_map/place_rows/pallas_call | solution.py:90
  3.7 3.1 %collective-permute-start = (bf16[128,1024]{1,0:T(8,128)(2,1)}, bf16[128,1024]{1,0:T(8,128)(2,1)S(1)}, u32[]{:S(2)}, u32[]{:S(2)}) collective-permute-start(bf16[128,1024]{1,0:T(8,128)(2,1)} %get-tuple-element.36), channel_id=1, source_target_pairs={{0,2},{2,4},{4,6},{6,0},{1,3},{3,5},{5,7},{7,1},{8,10},{10,12},{12... | collective-permute-start | bytes 786440 | tf_op jit(solution)/shard_map/ppermute | solution.py:294
  6.8 8.7 %collective-permute-done.refs_0_ = bf16[128,1024]{1,0:T(8,128)(2,1)S(1)} collective-permute-done((bf16[128,1024]{1,0:T(8,128)(2,1)}, bf16[128,1024]{1,0:T(8,128)(2,1)S(1)}, u32[]{:S(2)}, u32[]{:S(2)}) %collective-permute-start) | collective-permute-done | bytes 262176 | tf_op jit(solution)/shard_map/ppermute | solution.py:294
  15.5 1.5 %collective-permute-start.3 = (bf16[128,1024]{1,0:T(8,128)(2,1)S(1)}, bf16[128,1024]{1,0:T(8,128)(2,1)S(1)}, u32[]{:S(2)}, u32[]{:S(2)}) collective-permute-start(bf16[128,1024]{1,0:T(8,128)(2,1)S(1)} %collective-permute-done.refs_0_), channel_id=1, source_target_pairs={{0,16},{8,24},{16,0},{24,8},{1,17},{9,25},{17,1},{25,9},{2,18},{10... | collective-permute-start | bytes 786440 | tf_op jit(solution)/shard_map/ppermute | solution.py:291
  17.0 1.5 %collective-permute-start.5 = (bf16[128,1024]{1,0:T(8,128)(2,1)S(1)}, bf16[128,1024]{1,0:T(8,128)(2,1)S(1)}, u32[]{:S(2)}, u32[]{:S(2)}) collective-permute-start(bf16[128,1024]{1,0:T(8,128)(2,1)S(1)} %collective-permute-done.refs_0_), channel_id=1, source_target_pairs={{0,8},{8,0},{16,24},{24,16},{1,9},{9,1},{17,25},{25,17},{2,10},{10... | collective-permute-start | bytes 786440 | tf_op jit(solution)/shard_map/ppermute | solution.py:291
  19.2 4.0 %collective-permute-done.3.refs_2_ = bf16[128,1024]{1,0:T(8,128)(2,1)S(1)} collective-permute-done((bf16[128,1024]{1,0:T(8,128)(2,1)S(1)}, bf16[128,1024]{1,0:T(8,128)(2,1)S(1)}, u32[]{:S(2)}, u32[]{:S(2)}) %collective-permute-start.3) | collective-permute-done | bytes 262176 | tf_op jit(solution)/shard_map/ppermute | solution.py:291
  24.5 1.6 %collective-permute-start.6 = (bf16[128,512]{1,0:T(8,128)(2,1)S(1)}, bf16[128,512]{1,0:T(8,128)(2,1)S(1)}, u32[]{:S(2)}, u32[]{:S(2)}) collective-permute-start(bf16[128,512]{1,0:T(8,128)(2,1)S(1)} %slice.45), channel_id=1, source_target_pairs={{0,16},{8,24},{16,0},{24,8},{1,17},{9,25},{17,1},{25,9},{2,18},{10... | collective-permute-start | bytes 393224 | tf_op jit(solution)/shard_map/ppermute | solution.py:291
  26.1 1.6 %copy-done.1 = bf16[1,1024,1024]{2,1,0:T(8,128)(2,1)S(1)} copy-done((bf16[1,1024,1024]{2,1,0:T(8,128)(2,1)S(1)}, bf16[1,1024,1024]{2,1,0:T(8,128)(2,1)}, u32[]{:S(2)}) %copy-start.1) | copy-done | bytes 2097176
  30.2 7.1 %expert_rows.3 = (bf16[2,512,2048]{2,1,0:T(8,128)(2,1)S(1)}, bf16[2,512,1024]{2,1,0:T(8,128)(2,1)S(1)}, bf16[2,128,512]{2,1,0:T(8,128)(2,1)S(1)}, bf16[2,128,512]{2,1,0:T(8,128)(2,1)S(1)}) custom-call(s32[1,256]{1,0:T(1,128)S(1)} %bitcast.23, s32[1,256]{1,0:T(1,128)S(1)} %bitcast.26, f32[1,256]{1,0:T(1,128)S(1)} %bitcast.29, ...), custom_call_target="tpu_custom_call" | custom-call | flops 1610612736 | bytes 10485760 | tf_op jit(solution)/shard_map/expert_rows/pallas_call | solution.py:199
  37.9 1.3 %collective-permute-start.10 = (bf16[128,1024]{1,0:T(8,128)(2,1)S(1)}, bf16[128,1024]{1,0:T(8,128)(2,1)S(1)}, u32[]{:S(2)}, u32[]{:S(2)}) collective-permute-start(bf16[128,1024]{1,0:T(8,128)(2,1)S(1)} %collective-permute-done.9.refs_5_), channel_id=1, source_target_pairs={{0,8},{8,0},{16,24},{24,16},{1,9},{9,1},{17,25},{25,17},{2,10},{10... | collective-permute-start | bytes 786440 | tf_op jit(solution)/shard_map/ppermute | solution.py:291
  39.2 1.7 %collective-permute-start.19 = (bf16[128,1024]{1,0:T(8,128)(2,1)S(1)}, bf16[128,1024]{1,0:T(8,128)(2,1)S(1)}, u32[]{:S(2)}, u32[]{:S(2)}) collective-permute-start(bf16[128,1024]{1,0:T(8,128)(2,1)S(1)} %copy-done.8), channel_id=1, source_target_pairs={{0,6},{2,0},{4,2},{6,4},{1,7},{3,1},{5,3},{7,5},{8,14},{10,8},{12,... | collective-permute-start | bytes 786440 | tf_op jit(solution)/shard_map/ppermute | solution.py:294
  41.6 2.5 %collective-permute-done.11.refs_7_ = bf16[128,1024]{1,0:T(8,128)(2,1)S(1)} collective-permute-done((bf16[128,1024]{1,0:T(8,128)(2,1)S(1)}, bf16[128,1024]{1,0:T(8,128)(2,1)S(1)}, u32[]{:S(2)}, u32[]{:S(2)}) %collective-permute-start.11) | collective-permute-done | bytes 262176 | tf_op jit(solution)/shard_map/ppermute | solution.py:291
  44.4 2.8 %collective-permute-done.10.refs_6_ = bf16[128,1024]{1,0:T(8,128)(2,1)S(1)} collective-permute-done((bf16[128,1024]{1,0:T(8,128)(2,1)S(1)}, bf16[128,1024]{1,0:T(8,128)(2,1)S(1)}, u32[]{:S(2)}, u32[]{:S(2)}) %collective-permute-start.10) | collective-permute-done | bytes 262176 | tf_op jit(solution)/shard_map/ppermute | solution.py:291
  47.1 1.6 %collective-permute-start.13 = (bf16[128,512]{1,0:T(8,128)(2,1)S(1)}, bf16[128,512]{1,0:T(8,128)(2,1)S(1)}, u32[]{:S(2)}, u32[]{:S(2)}) collective-permute-start(bf16[128,512]{1,0:T(8,128)(2,1)S(1)} %slice.49), channel_id=1, source_target_pairs={{0,16},{8,24},{16,0},{24,8},{1,17},{9,25},{17,1},{25,9},{2,18},{10... | collective-permute-start | bytes 393224 | tf_op jit(solution)/shard_map/ppermute | solution.py:291
  50.6 2.2 %collective-permute-done.7 = bf16[2,128,512]{2,1,0:T(8,128)(2,1)S(1)} collective-permute-done((bf16[2,128,512]{2,1,0:T(8,128)(2,1)S(1)}, bf16[2,128,512]{2,1,0:T(8,128)(2,1)S(1)}, u32[]{:S(2)}, u32[]{:S(2)}) %collective-permute-start.7) | collective-permute-done | bytes 262176 | tf_op jit(solution)/shard_map/ppermute | solution.py:291
  52.8 1.5 %collective-permute-start.22 = (bf16[128,1024]{1,0:T(8,128)(2,1)S(1)}, bf16[128,1024]{1,0:T(8,128)(2,1)S(1)}, u32[]{:S(2)}, u32[]{:S(2)}) collective-permute-start(bf16[128,1024]{1,0:T(8,128)(2,1)S(1)} %collective-permute-done.19.refs_0_), channel_id=1, source_target_pairs={{0,24},{8,16},{16,8},{24,0},{1,25},{9,17},{17,9},{25,1},{2,26},{10... | collective-permute-start | bytes 786440 | tf_op jit(solution)/shard_map/ppermute | solution.py:291
  54.2 1.3 %collective-permute-done.12.refs_8_ = bf16[128,512]{1,0:T(8,128)(2,1)S(1)} collective-permute-done((bf16[128,512]{1,0:T(8,128)(2,1)S(1)}, bf16[128,512]{1,0:T(8,128)(2,1)S(1)}, u32[]{:S(2)}, u32[]{:S(2)}) %collective-permute-start.12) | collective-permute-done | bytes 131104 | tf_op jit(solution)/shard_map/ppermute | solution.py:291
  55.6 7.3 %expert_rows.4 = (bf16[2,512,2048]{2,1,0:T(8,128)(2,1)S(1)}, bf16[2,512,1024]{2,1,0:T(8,128)(2,1)S(1)}, bf16[256,512]{1,0:T(8,128)(2,1)S(1)}, bf16[256,512]{1,0:...) custom-call(bf16[128,1024]{1,0:T(8,128)(2,1)S(1)} %collective-permut, ...), custom_call_target="tpu_custom_call", output_to_operand_aliasing={{0}: (14, {}), {1}: (15, {})} | custom-call | flops 3221225472 | bytes 12582912 | tf_op jit(solution)/shard_map/expert_rows/pallas_call | solution.py:199
  62.9 1.6 %collective-permute-start.16 = (bf16[256,512]{1,0:T(8,128)(2,1)S(1)}, bf16[256,512]{1,0:T(8,128)(2,1)S(1)}, u32[]{:S(2)}, u32[]{:S(2)}) collective-permute-start(bf16[256,512]{1,0:T(8,128)(2,1)S(1)} %get-tuple-element.49), channel_id=1, source_target_pairs={{0,24},{8,16},{16,8},{24,0},{1,25},{9,17},{17,9},{25,1},{2,26},{10... | collective-permute-start | bytes 786440 | tf_op jit(solution)/shard_map/ppermute | solution.py:291
  64.4 1.3 %collective-permute-start.15 = (bf16[256,512]{1,0:T(8,128)(2,1)S(1)}, bf16[256,512]{1,0:T(8,128)(2,1)S(1)}, u32[]{:S(2)}, u32[]{:S(2)}) collective-permute-start(bf16[256,512]{1,0:T(8,128)(2,1)S(1)} %get-tuple-element.48), channel_id=1, source_target_pairs={{0,16},{8,24},{16,0},{24,8},{1,17},{9,25},{17,1},{25,9},{2,18},{10... | collective-permute-start | bytes 786440 | tf_op jit(solution)/shard_map/ppermute | solution.py:291
  66.4 1.4 %collective-permute-done.22.refs_3_ = bf16[128,1024]{1,0:T(8,128)(2,1)S(1)} collective-permute-done((bf16[128,1024]{1,0:T(8,128)(2,1)S(1)}, bf16[128,1024]{1,0:T(8,128)(2,1)S(1)}, u32[]{:S(2)}, u32[]{:S(2)}) %collective-permute-start.22) | collective-permute-done | bytes 262176 | tf_op jit(solution)/shard_map/ppermute | solution.py:291
  67.8 6.7 %expert_rows.5 = (bf16[2,512,2048]{2,1,0:T(8,128)(2,1)S(1)}, bf16[2,512,1024]{2,1,0:T(8,128)(2,1)S(1)}, bf16[128,512]{1,0:T(8,128)(2,1)S(1)}, bf16[128,512]{1,0:...) custom-call(bf16[128,1024]{1,0:T(8,128)(2,1)S(1)} %collective-permut, ...), custom_call_target="tpu_custom_call", output_to_operand_aliasing={{0}: (8, {}), {1}: (9, {})} | custom-call | flops 1610612736 | bytes 10485760 | tf_op jit(solution)/shard_map/expert_rows/pallas_call | solution.py:199
  74.5 2.4 %convolution_convert_fusion = bf16[2,1024,1024]{2,1,0:T(8,128)(2,1)S(1)} fusion(bf16[2,512,1024]{2,1,0:T(8,128)(2,1)S(1)} %get-tuple-element.59.acts, bf16[2,512,2048]{2,1,0:T(8,128)(2,1)S(1)} %get-tuple-element.58.rows), kind=kOutput, calls=%fused_computation | convolution fusion | flops 2149580800 | bytes 8388608 | tf_op jit(solution)/shard_map/dot_general | solution.py:320
  77.6 1.5 %collective-permute-start.25 = (bf16[128,512]{1,0:T(8,128)(2,1)S(1)}, bf16[128,512]{1,0:T(8,128)(2,1)S(1)}, u32[]{:S(2)}, u32[]{:S(2)}) collective-permute-start(bf16[128,512]{1,0:T(8,128)(2,1)S(1)} %get-tuple-element.64), channel_id=1, source_target_pairs={{0,24},{8,16},{16,8},{24,0},{1,25},{9,17},{17,9},{25,1},{2,26},{10... | collective-permute-start | bytes 393224 | tf_op jit(solution)/shard_map/ppermute | solution.py:291
  79.1 1.3 %collective-permute-start.24 = (bf16[128,512]{1,0:T(8,128)(2,1)S(1)}, bf16[128,512]{1,0:T(8,128)(2,1)S(1)}, u32[]{:S(2)}, u32[]{:S(2)}) collective-permute-start(bf16[128,512]{1,0:T(8,128)(2,1)S(1)} %get-tuple-element.62), channel_id=1, source_target_pairs={{0,16},{8,24},{16,0},{24,8},{1,17},{9,25},{17,1},{25,9},{2,18},{10... | collective-permute-start | bytes 393224 | tf_op jit(solution)/shard_map/ppermute | solution.py:291
  81.3 3.6 %collective-permute-done.25 = bf16[128,512]{1,0:T(8,128)(2,1)S(1)} collective-permute-done((bf16[128,512]{1,0:T(8,128)(2,1)S(1)}, bf16[128,512]{1,0:T(8,128)(2,1)S(1)}, u32[]{:S(2)}, u32[]{:S(2)}) %collective-permute-start.25) | collective-permute-done | bytes 131104 | tf_op jit(solution)/shard_map/ppermute | solution.py:291
  84.9 1.7 %collective-permute-start.17 = (bf16[128,512]{1,0:T(8,128)(2,1)S(1)}, bf16[128,512]{1,0:T(8,128)(2,1)S(1)}, u32[]{:S(2)}, u32[]{:S(2)}) collective-permute-start(bf16[128,512]{1,0:T(8,128)(2,1)S(1)} %get-tuple-element.70), channel_id=1, source_target_pairs={{0,6},{2,0},{4,2},{6,4},{1,7},{3,1},{5,3},{7,5},{8,14},{10,8},{12,... | collective-permute-start | bytes 393224 | tf_op jit(solution)/shard_map/ppermute | solution.py:294
  86.6 2.0 %collective-permute-done.24 = bf16[128,512]{1,0:T(8,128)(2,1)S(1)} collective-permute-done((bf16[128,512]{1,0:T(8,128)(2,1)S(1)}, bf16[128,512]{1,0:T(8,128)(2,1)S(1)}, u32[]{:S(2)}, u32[]{:S(2)}) %collective-permute-start.24) | collective-permute-done | bytes 131104 | tf_op jit(solution)/shard_map/ppermute | solution.py:291
  89.4 1.6 %collective-permute-start.26 = (bf16[128,512]{1,0:T(8,128)(2,1)S(1)}, bf16[128,512]{1,0:T(8,128)(2,1)S(1)}, u32[]{:S(2)}, u32[]{:S(2)}) collective-permute-start(bf16[128,512]{1,0:T(8,128)(2,1)S(1)} %add_convert_fusion.1), channel_id=1, source_target_pairs={{0,2},{2,4},{4,6},{6,0},{1,3},{3,5},{5,7},{7,1},{8,10},{10,12},{12... | collective-permute-start | bytes 393224 | tf_op jit(solution)/shard_map/ppermute | solution.py:294
  91.1 3.9 %weight_grads.1 = (bf16[1024,1024]{1,0:T(8,128)(2,1)}, bf16[1024,1024]{1,0:T(8,128)(2,1)}) custom-call(bf16[2,512,2048]{2,1,0:T(8,128)(2,1)S(1)} %get-tuple-element.58.rows, bf16[2,512,1024]{2,1,0:T(8,128)(2,1)S(1)} %get-tuple-element.59.acts, bf16[2,1024,1024]{2,1,0:T(8,128)(2,1)S(1)} %collective-permute-done.27.got), custom_call_target="tpu_custom_call" | custom-call | flops 1000 | bytes 1000 | tf_op jit(solution)/shard_map/weight_grads/pallas_call | solution.py:263
  95.0 1.7 %collective-permute-done.26.refs_3_ = bf16[128,512]{1,0:T(8,128)(2,1)S(1)} collective-permute-done((bf16[128,512]{1,0:T(8,128)(2,1)S(1)}, bf16[128,512]{1,0:T(8,128)(2,1)S(1)}, u32[]{:S(2)}, u32[]{:S(2)}) %collective-permute-start.26) | collective-permute-done | bytes 131104 | tf_op jit(solution)/shard_map/ppermute | solution.py:294
  96.6 2.7 %collective-permute-done.18.refs_2_ = bf16[128,512]{1,0:T(8,128)(2,1)S(1)} collective-permute-done((bf16[128,512]{1,0:T(8,128)(2,1)S(1)}, bf16[128,512]{1,0:T(8,128)(2,1)S(1)}, u32[]{:S(2)}, u32[]{:S(2)}) %collective-permute-start.18) | collective-permute-done | bytes 131104 | tf_op jit(solution)/shard_map/ppermute | solution.py:294
  (58 shorter events, 12.7 us)
Async XLA Ops:
  0.6 25.5 %copy-start = (bf16[1,1024,1024]{2,1,0:T(8,128)(2,1)S(1)}, bf16[1,1024,1024]{2,1,0:T(8,128)(2,1)}, u32[]{:S(2)}) copy-start(bf16[1,1024,1024]{2,1,0:T(8,128)(2,1)} %param.12) | copy-start | bytes 6291460
  0.6 25.5 %copy-start.5 = (s32[256,1]{0,1:T(1,128)S(1)}, s32[256,1]{0,1:T(1,128)}, u32[]{:S(2)}) copy-start(s32[256,1]{0,1:T(1,128)} %param.10) | copy-start | bytes 3076
  0.7 25.5 %copy-start.6 = (s32[256,1]{0,1:T(1,128)S(1)}, s32[256,1]{0,1:T(1,128)}, u32[]{:S(2)}) copy-start(s32[256,1]{0,1:T(1,128)} %param.11) | copy-start | bytes 3076
  0.7 25.5 %copy-start.7 = (f32[256]{0:T(256)S(1)}, f32[256]{0:T(256)}, u32[]{:S(2)}) copy-start(f32[256]{0:T(256)} %param.9) | copy-start | bytes 3076
  0.7 17.8 %collective-permute-start.1 = (bf16[1024,1024]{1,0:T(8,128)(2,1)}, bf16[1024,1024]{1,0:T(8,128)(2,1)S(1)}, u32[]{:S(2)}, u32[]{:S(2)}) collective-permute-start(bf16[1024,1024]{1,0:T(8,128)(2,1)} %bitcast.14), channel_id=1, source_target_pairs={{0,1},{1,0},{2,3},{3,2},{4,5},{5,4},{6,7},{7,6},{8,9},{9,8},{10,11... | collective-permute-start | bytes 6291464 | tf_op jit(solution)/shard_map/ppermute | solution.py:288
  1.2 17.3 %collective-permute-start.2 = (bf16[1024,1024]{1,0:T(8,128)(2,1)}, bf16[1024,1024]{1,0:T(8,128)(2,1)S(1)}, u32[]{:S(2)}, u32[]{:S(2)}) collective-permute-start(bf16[1024,1024]{1,0:T(8,128)(2,1)} %bitcast.18), channel_id=1, source_target_pairs={{0,1},{1,0},{2,3},{3,2},{4,5},{5,4},{6,7},{7,6},{8,9},{9,8},{10,11... | collective-permute-start | bytes 6291464 | tf_op jit(solution)/shard_map/ppermute | solution.py:288
  3.7 11.8 %collective-permute-start = (bf16[128,1024]{1,0:T(8,128)(2,1)}, bf16[128,1024]{1,0:T(8,128)(2,1)S(1)}, u32[]{:S(2)}, u32[]{:S(2)}) collective-permute-start(bf16[128,1024]{1,0:T(8,128)(2,1)} %get-tuple-element.36), channel_id=1, source_target_pairs={{0,2},{2,4},{4,6},{6,0},{1,3},{3,5},{5,7},{7,1},{8,10},{10,12},{12... | collective-permute-start | bytes 786440 | tf_op jit(solution)/shard_map/ppermute | solution.py:294
  15.5 7.7 %collective-permute-start.3 = (bf16[128,1024]{1,0:T(8,128)(2,1)S(1)}, bf16[128,1024]{1,0:T(8,128)(2,1)S(1)}, u32[]{:S(2)}, u32[]{:S(2)}) collective-permute-start(bf16[128,1024]{1,0:T(8,128)(2,1)S(1)} %collective-permute-done.refs_0_), channel_id=1, source_target_pairs={{0,16},{8,24},{16,0},{24,8},{1,17},{9,25},{17,1},{25,9},{2,18},{10... | collective-permute-start | bytes 786440 | tf_op jit(solution)/shard_map/ppermute | solution.py:291
  17.0 7.5 %collective-permute-start.5 = (bf16[128,1024]{1,0:T(8,128)(2,1)S(1)}, bf16[128,1024]{1,0:T(8,128)(2,1)S(1)}, u32[]{:S(2)}, u32[]{:S(2)}) collective-permute-start(bf16[128,1024]{1,0:T(8,128)(2,1)S(1)} %collective-permute-done.refs_0_), channel_id=1, source_target_pairs={{0,8},{8,0},{16,24},{24,16},{1,9},{9,1},{17,25},{25,17},{2,10},{10... | collective-permute-start | bytes 786440 | tf_op jit(solution)/shard_map/ppermute | solution.py:291
  18.5 18.8 %collective-permute-start.9 = (bf16[128,1024]{1,0:T(8,128)(2,1)}, bf16[128,1024]{1,0:T(8,128)(2,1)S(1)}, u32[]{:S(2)}, u32[]{:S(2)}) collective-permute-start(bf16[128,1024]{1,0:T(8,128)(2,1)} %get-tuple-element.42), channel_id=1, source_target_pairs={{0,4},{2,6},{4,0},{6,2},{1,5},{3,7},{5,1},{7,3},{8,12},{10,14},{12... | collective-permute-start | bytes 786440 | tf_op jit(solution)/shard_map/ppermute | solution.py:294
  23.2 17.8 %collective-permute-start.4 = (bf16[128,512]{1,0:T(8,128)(2,1)S(1)}, bf16[128,512]{1,0:T(8,128)(2,1)S(1)}, u32[]{:S(2)}, u32[]{:S(2)}) collective-permute-start(bf16[128,512]{1,0:T(8,128)(2,1)S(1)} %slice.44), channel_id=1, source_target_pairs={{0,8},{8,0},{16,24},{24,16},{1,9},{9,1},{17,25},{25,17},{2,10},{10... | collective-permute-start | bytes 393224 | tf_op jit(solution)/shard_map/ppermute | solution.py:291
  24.5 16.4 %collective-permute-start.6 = (bf16[128,512]{1,0:T(8,128)(2,1)S(1)}, bf16[128,512]{1,0:T(8,128)(2,1)S(1)}, u32[]{:S(2)}, u32[]{:S(2)}) collective-permute-start(bf16[128,512]{1,0:T(8,128)(2,1)S(1)} %slice.45), channel_id=1, source_target_pairs={{0,16},{8,24},{16,0},{24,8},{1,17},{9,25},{17,1},{25,9},{2,18},{10... | collective-permute-start | bytes 393224 | tf_op jit(solution)/shard_map/ppermute | solution.py:291
  37.3 6.8 %collective-permute-start.11 = (bf16[128,1024]{1,0:T(8,128)(2,1)S(1)}, bf16[128,1024]{1,0:T(8,128)(2,1)S(1)}, u32[]{:S(2)}, u32[]{:S(2)}) collective-permute-start(bf16[128,1024]{1,0:T(8,128)(2,1)S(1)} %collective-permute-done.9.refs_5_), channel_id=1, source_target_pairs={{0,16},{8,24},{16,0},{24,8},{1,17},{9,25},{17,1},{25,9},{2,18},{10... | collective-permute-start | bytes 786440 | tf_op jit(solution)/shard_map/ppermute | solution.py:291
  37.9 9.2 %collective-permute-start.10 = (bf16[128,1024]{1,0:T(8,128)(2,1)S(1)}, bf16[128,1024]{1,0:T(8,128)(2,1)S(1)}, u32[]{:S(2)}, u32[]{:S(2)}) collective-permute-start(bf16[128,1024]{1,0:T(8,128)(2,1)S(1)} %collective-permute-done.9.refs_5_), channel_id=1, source_target_pairs={{0,8},{8,0},{16,24},{24,16},{1,9},{9,1},{17,25},{25,17},{2,10},{10... | collective-permute-start | bytes 786440 | tf_op jit(solution)/shard_map/ppermute | solution.py:291
  39.2 9.5 %collective-permute-start.19 = (bf16[128,1024]{1,0:T(8,128)(2,1)S(1)}, bf16[128,1024]{1,0:T(8,128)(2,1)S(1)}, u32[]{:S(2)}, u32[]{:S(2)}) collective-permute-start(bf16[128,1024]{1,0:T(8,128)(2,1)S(1)} %copy-done.8), channel_id=1, source_target_pairs={{0,6},{2,0},{4,2},{6,4},{1,7},{3,1},{5,3},{7,5},{8,14},{10,8},{12,... | collective-permute-start | bytes 786440 | tf_op jit(solution)/shard_map/ppermute | solution.py:294
  41.0 11.8 %collective-permute-start.7 = (bf16[2,128,512]{2,1,0:T(8,128)(2,1)S(1)}, bf16[2,128,512]{2,1,0:T(8,128)(2,1)S(1)}, u32[]{:S(2)}, u32[]{:S(2)}) collective-permute-start(bf16[2,128,512]{2,1,0:T(8,128)(2,1)S(1)} %get-tuple-element.40), channel_id=1, source_target_pairs={{0,8},{8,0},{16,24},{24,16},{1,9},{9,1},{17,25},{25,17},{2,10},{10... | collective-permute-start | bytes 786440 | tf_op jit(solution)/shard_map/ppermute | solution.py:291
  44.1 11.5 %collective-permute-start.12 = (bf16[128,512]{1,0:T(8,128)(2,1)S(1)}, bf16[128,512]{1,0:T(8,128)(2,1)S(1)}, u32[]{:S(2)}, u32[]{:S(2)}) collective-permute-start(bf16[128,512]{1,0:T(8,128)(2,1)S(1)} %slice.48), channel_id=1, source_target_pairs={{0,8},{8,0},{16,24},{24,16},{1,9},{9,1},{17,25},{25,17},{2,10},{10... | collective-permute-start | bytes 393224 | tf_op jit(solution)/shard_map/ppermute | solution.py:291
  47.1 8.4 %collective-permute-start.13 = (bf16[128,512]{1,0:T(8,128)(2,1)S(1)}, bf16[128,512]{1,0:T(8,128)(2,1)S(1)}, u32[]{:S(2)}, u32[]{:S(2)}) collective-permute-start(bf16[128,512]{1,0:T(8,128)(2,1)S(1)} %slice.49), channel_id=1, source_target_pairs={{0,16},{8,24},{16,0},{24,8},{1,17},{9,25},{17,1},{25,9},{2,18},{10... | collective-permute-start | bytes 393224 | tf_op jit(solution)/shard_map/ppermute | solution.py:291
  48.7 17.0 %collective-permute-start.20 = (bf16[128,1024]{1,0:T(8,128)(2,1)S(1)}, bf16[128,1024]{1,0:T(8,128)(2,1)S(1)}, u32[]{:S(2)}, u32[]{:S(2)}) collective-permute-start(bf16[128,1024]{1,0:T(8,128)(2,1)S(1)} %collective-permute-done.19.refs_0_), channel_id=1, source_target_pairs={{0,8},{8,0},{16,24},{24,16},{1,9},{9,1},{17,25},{25,17},{2,10},{10... | collective-permute-start | bytes 786440 | tf_op jit(solution)/shard_map/ppermute | solution.py:291
  49.3 17.2 %collective-permute-start.21 = (bf16[128,1024]{1,0:T(8,128)(2,1)S(1)}, bf16[128,1024]{1,0:T(8,128)(2,1)S(1)}, u32[]{:S(2)}, u32[]{:S(2)}) collective-permute-start(bf16[128,1024]{1,0:T(8,128)(2,1)S(1)} %collective-permute-done.19.refs_0_), channel_id=1, source_target_pairs={{0,16},{8,24},{16,0},{24,8},{1,17},{9,25},{17,1},{25,9},{2,18},{10... | collective-permute-start | bytes 786440 | tf_op jit(solution)/shard_map/ppermute | solution.py:291
  52.8 15.0 %collective-permute-start.22 = (bf16[128,1024]{1,0:T(8,128)(2,1)S(1)}, bf16[128,1024]{1,0:T(8,128)(2,1)S(1)}, u32[]{:S(2)}, u32[]{:S(2)}) collective-permute-start(bf16[128,1024]{1,0:T(8,128)(2,1)S(1)} %collective-permute-done.19.refs_0_), channel_id=1, source_target_pairs={{0,24},{8,16},{16,8},{24,0},{1,25},{9,17},{17,9},{25,1},{2,26},{10... | collective-permute-start | bytes 786440 | tf_op jit(solution)/shard_map/ppermute | solution.py:291
  62.9 14.0 %collective-permute-start.16 = (bf16[256,512]{1,0:T(8,128)(2,1)S(1)}, bf16[256,512]{1,0:T(8,128)(2,1)S(1)}, u32[]{:S(2)}, u32[]{:S(2)}) collective-permute-start(bf16[256,512]{1,0:T(8,128)(2,1)S(1)} %get-tuple-element.49), channel_id=1, source_target_pairs={{0,24},{8,16},{16,8},{24,0},{1,25},{9,17},{17,9},{25,1},{2,26},{10... | collective-permute-start | bytes 786440 | tf_op jit(solution)/shard_map/ppermute | solution.py:291
  64.4 12.5 %collective-permute-start.15 = (bf16[256,512]{1,0:T(8,128)(2,1)S(1)}, bf16[256,512]{1,0:T(8,128)(2,1)S(1)}, u32[]{:S(2)}, u32[]{:S(2)}) collective-permute-start(bf16[256,512]{1,0:T(8,128)(2,1)S(1)} %get-tuple-element.48), channel_id=1, source_target_pairs={{0,16},{8,24},{16,0},{24,8},{1,17},{9,25},{17,1},{25,9},{2,18},{10... | collective-permute-start | bytes 786440 | tf_op jit(solution)/shard_map/ppermute | solution.py:291
  65.7 11.2 %collective-permute-start.14 = (bf16[256,512]{1,0:T(8,128)(2,1)S(1)}, bf16[256,512]{1,0:T(8,128)(2,1)S(1)}, u32[]{:S(2)}, u32[]{:S(2)}) collective-permute-start(bf16[256,512]{1,0:T(8,128)(2,1)S(1)} %get-tuple-element.47), channel_id=1, source_target_pairs={{0,8},{8,0},{16,24},{24,16},{1,9},{9,1},{17,25},{25,17},{2,10},{10... | collective-permute-start | bytes 786440 | tf_op jit(solution)/shard_map/ppermute | solution.py:291
  76.9 14.1 %collective-permute-start.27 = (bf16[2,1024,1024]{2,1,0:T(8,128)(2,1)S(1)}, bf16[2,1024,1024]{2,1,0:T(8,128)(2,1)S(1)}, u32[]{:S(2)}, u32[]{:S(2)}) collective-permute-start(bf16[2,1024,1024]{2,1,0:T(8,128)(2,1)S(1)} %convolution_convert_fusion), channel_id=1, source_target_pairs={{0,1},{1,0},{2,3},{3,2},{4,5},{5,4},{6,7},{7,6},{8,9},{9,8},{10,11... | collective-permute-start | bytes 12582920 | tf_op jit(solution)/shard_map/ppermute | solution.py:288
  77.1 14.0 %collective-permute-start.8 = (bf16[128,512]{1,0:T(8,128)(2,1)S(1)}, bf16[128,512]{1,0:T(8,128)(2,1)S(1)}, u32[]{:S(2)}, u32[]{:S(2)}) collective-permute-start(bf16[128,512]{1,0:T(8,128)(2,1)S(1)} %fusion.2), channel_id=1, source_target_pairs={{0,16},{8,24},{16,0},{24,8},{1,17},{9,25},{17,1},{25,9},{2,18},{10... | collective-permute-start | bytes 393224 | tf_op jit(solution)/shard_map/ppermute | solution.py:291
  77.6 7.3 %collective-permute-start.25 = (bf16[128,512]{1,0:T(8,128)(2,1)S(1)}, bf16[128,512]{1,0:T(8,128)(2,1)S(1)}, u32[]{:S(2)}, u32[]{:S(2)}) collective-permute-start(bf16[128,512]{1,0:T(8,128)(2,1)S(1)} %get-tuple-element.64), channel_id=1, source_target_pairs={{0,24},{8,16},{16,8},{24,0},{1,25},{9,17},{17,9},{25,1},{2,26},{10... | collective-permute-start | bytes 393224 | tf_op jit(solution)/shard_map/ppermute | solution.py:291
  79.1 9.5 %collective-permute-start.24 = (bf16[128,512]{1,0:T(8,128)(2,1)S(1)}, bf16[128,512]{1,0:T(8,128)(2,1)S(1)}, u32[]{:S(2)}, u32[]{:S(2)}) collective-permute-start(bf16[128,512]{1,0:T(8,128)(2,1)S(1)} %get-tuple-element.62), channel_id=1, source_target_pairs={{0,16},{8,24},{16,0},{24,8},{1,17},{9,25},{17,1},{25,9},{2,18},{10... | collective-permute-start | bytes 393224 | tf_op jit(solution)/shard_map/ppermute | solution.py:291
  80.5 8.9 %collective-permute-start.23 = (bf16[128,512]{1,0:T(8,128)(2,1)S(1)}, bf16[128,512]{1,0:T(8,128)(2,1)S(1)}, u32[]{:S(2)}, u32[]{:S(2)}) collective-permute-start(bf16[128,512]{1,0:T(8,128)(2,1)S(1)} %get-tuple-element.60), channel_id=1, source_target_pairs={{0,8},{8,0},{16,24},{24,16},{1,9},{9,1},{17,25},{25,17},{2,10},{10... | collective-permute-start | bytes 393224 | tf_op jit(solution)/shard_map/ppermute | solution.py:291
  84.9 11.7 %collective-permute-start.17 = (bf16[128,512]{1,0:T(8,128)(2,1)S(1)}, bf16[128,512]{1,0:T(8,128)(2,1)S(1)}, u32[]{:S(2)}, u32[]{:S(2)}) collective-permute-start(bf16[128,512]{1,0:T(8,128)(2,1)S(1)} %get-tuple-element.70), channel_id=1, source_target_pairs={{0,6},{2,0},{4,2},{6,4},{1,7},{3,1},{5,3},{7,5},{8,14},{10,8},{12,... | collective-permute-start | bytes 393224 | tf_op jit(solution)/shard_map/ppermute | solution.py:294
  88.6 10.7 %collective-permute-start.18 = (bf16[128,512]{1,0:T(8,128)(2,1)S(1)}, bf16[128,512]{1,0:T(8,128)(2,1)S(1)}, u32[]{:S(2)}, u32[]{:S(2)}) collective-permute-start(bf16[128,512]{1,0:T(8,128)(2,1)S(1)} %get-tuple-element.69), channel_id=1, source_target_pairs={{0,4},{2,6},{4,0},{6,2},{1,5},{3,7},{5,1},{7,3},{8,12},{10,14},{12... | collective-permute-start | bytes 393224 | tf_op jit(solution)/shard_map/ppermute | solution.py:294
  89.4 7.2 %collective-permute-start.26 = (bf16[128,512]{1,0:T(8,128)(2,1)S(1)}, bf16[128,512]{1,0:T(8,128)(2,1)S(1)}, u32[]{:S(2)}, u32[]{:S(2)}) collective-permute-start(bf16[128,512]{1,0:T(8,128)(2,1)S(1)} %add_convert_fusion.1), channel_id=1, source_target_pairs={{0,2},{2,4},{4,6},{6,0},{1,3},{3,5},{5,7},{7,1},{8,10},{10,12},{12... | collective-permute-start | bytes 393224 | tf_op jit(solution)/shard_map/ppermute | solution.py:294
  (5 other events, 38.5 us)

commit v11 on v10

--- a/solution.py
+++ b/solution.py
@@ -325,30 +325,26 @@
     weights = [up_own, swap(up_own), down_own, swap(down_own)]
 
     if experts == 4:
-        shifts = [1, 2, 3]
+        shifts = [1, 3, 2]
         sends = place([capacity] * 3, shifts, capacity, index, slot, gate, tokens, grad_output)
         everything = 4 * capacity
-        one = shift(sends[0], 1)
-        two = shift(after(sends[1], one, weights[1], weights[3]), 2)
-        own = [after(index, one), slot, gate, tokens, grad_output]
+        moved = [shift(rows, k) for rows, k in zip(sends, shifts)]
+        own = [index, slot, gate, tokens, grad_output]
         kept, (pair,) = expert_rows(own, None, [(capacity, 1)], weights, everything, 0, None)
-        first = spread(one)
-        three = shift(after(sends[2], two, *first[1:3]), 3)
-        second = spread(after(two, pair[0]))
-        third = after(three, *second[1:3])
-        third = [third] + [across(third, j) for j in (1, 2, 3)]
-        back, got_own = collect_pair([pair[0], after(pair[1], *first[3:])], 1)
-        kept, (blocks,) = expert_rows(
-            None, [first, second], [(2 * capacity, None)], weights, everything, capacity, kept
-        )
+        near = spread(jnp.concatenate([after(moved[0], pair[0]), moved[1]], 0))
+        far = after(moved[2], *near[1:3])
+        far = [far] + [across(far, j) for j in (1, 2, 3)]
+        near[0] = after(near[0], far[1])
+        back, got_own = collect_pair([pair[0], after(pair[1], *near[3:])], 1)
+        kept, (blocks,) = expert_rows(None, [near], [(2 * capacity, None)], weights, everything, capacity, kept)
         total, got = collect(blocks)
-        backs = [back, shift(total[:capacity], -1), shift(total[capacity:], -2)]
-        third[0] = after(third[0], got_own)
-        kept, (blocks,) = expert_rows(None, [third], [(capacity, None)], weights, everything, 3 * capacity, kept)
+        backs = [back, shift(total[:capacity], -1), shift(total[capacity:], -3)]
+        far[0] = after(far[0], got_own)
+        kept, (blocks,) = expert_rows(None, [far], [(capacity, None)], weights, everything, 3 * capacity, kept)
         others = other_halves(kept)
         grads = weight_grads(*kept, swap(after(others, *got)))
         total, _ = collect([blocks[0]] + [after(b, got[0], others) for b in blocks[1:]])
-        backs.append(after(shift(total, -3), *grads))
+        backs.append(after(shift(total, -2), *grads))
         shifts = [0] + shifts
     else:
         rows = experts * capacity

time: 101 us -> 97.5 us (0.965)
  waiting for transfers between devices: 32.9 us -> 24.4 us
  starting transfers between devices: 31.5 us -> 36.7 us
    ppermute x6, waiting for transfers between devices: 13.1 us -> 5 us  [shift(): lax.ppermute(x, 'expert', [(i, (i + k) % experts) for i in range(experts)])]
    ppermute x6, starting transfers between devices: 9.51 us -> 14.7 us  [shift(): lax.ppermute(x, 'expert', [(i, (i + k) % experts) for i in range(experts)])]
    ppermute x19 -> x15, waiting for transfers between devices: 19.7 us -> 19.4 us  [across(): return lax.ppermute(x, 'tensor', [(i, i ^ j) for i in range(tensor_size)])]
    ppermute x19 -> x15, starting transfers between devices: 21.3 us -> 21.3 us  [across(): return lax.ppermute(x, 'tensor', [(i, i ^ j) for i in range(tensor_size)])]
    unnamed x18 -> x19, local copies, waits for them, and re-layouts: 4.06 us -> 4.08 us
  transfers between devices with their start and end apart: 28 -> 24, of which waited for: 11 -> 9; matrix products, arithmetic and copies ran while one was open for 3% -> 3% of each run, Pallas kernels for 27% -> 28%
where the time goes in v11:
time: 97.5 us; the launch traced here: 97.2 us
  starting transfers between devices  36.7 us (38%)
  Pallas kernels  28.4 us (29%)
  waiting for transfers between devices  24.4 us (25%)
  local copies, waits for them, and re-layouts  4.15 us (4%)
  matrix products  2.38 us (2%)
    ppermute x15, starting transfers between devices, across(): return lax.ppermute(x, 'tensor', [(i, i ^ j) for i in range(tensor_size)])  21.3 us
    pallas_call x3, Pallas kernels, expert_rows(): pl.pallas_call(functools.partial(expert_kernel, counts_in, base, groups,...  20.9 us
    ppermute x15, waiting for transfers between devices, across(): return lax.ppermute(x, 'tensor', [(i, i ^ j) for i in range(tensor_size)])  19.4 us
    ppermute x6, starting transfers between devices, shift(): lax.ppermute(x, 'expert', [(i, (i + k) % experts) for i in range(experts)])  14.7 us
    ppermute x6, waiting for transfers between devices, shift(): lax.ppermute(x, 'expert', [(i, (i + k) % experts) for i in range(experts)])  5 us
    unnamed x19, local copies, waits for them, and re-layouts  4.08 us
    pallas_call x1, Pallas kernels, weight_grads(): pl.pallas_call(weight_grad_kernel, out_shape=[jax.ShapeDtypeStruct((half,...  3.87 us
    pallas_call x1, Pallas kernels, place(): pl.pallas_call(functools.partial(place_kernel, spans, shifts, capacity),...  2.41 us
  transfers between devices with their start and end apart: 24, of which 9 were waited for; matrix products, arithmetic and copies ran while one was open for 3% of the time, Pallas kernels for 28%

profile of v11, /device:TPU:0, one launch (start us, length us, event | category | flops | bytes accessed | tf_op | source)
XLA Modules:
  0.0 97.2 jit_solution(9520762446484851865)
XLA Ops:
  1.3 2.4 %place_rows.1 = (bf16[128,1024]{1,0:T(8,128)(2,1)}, bf16[128,1024]{1,0:T(8,128)(2,1)}, bf16[128,1024]{1,0:T(8,128)(2,1)}) custom-call(s32[1,256]{1,0:T(1,128)} %bitcast.22, s32[1,256]{1,0:T(1,128)} %bitcast.25, f32[1,256]{1,0:T(1,128)} %bitcast.28, bf16[256,2048]{1,0:T(8,128)(2,1)} %tokens.1, bf16[256,2048]{1,0:T(8,128)(2,1)} %grad_output.1), custom_call_target="tpu_custom_call" | custom-call | flops 1000 | bytes 1000 | tf_op jit(solution)/shard_map/place_rows/pallas_call | solution.py:90
  3.7 3.1 %collective-permute-start.2 = (bf16[128,1024]{1,0:T(8,128)(2,1)}, bf16[128,1024]{1,0:T(8,128)(2,1)S(1)}, u32[]{:S(2)}, u32[]{:S(2)}) collective-permute-start(bf16[128,1024]{1,0:T(8,128)(2,1)} %get-tuple-element.36), channel_id=1, source_target_pairs={{0,2},{2,4},{4,6},{6,0},{1,3},{3,5},{5,7},{7,1},{8,10},{10,12},{12... | collective-permute-start | bytes 786440 | tf_op jit(solution)/shard_map/ppermute | solution.py:294
  6.8 2.1 %collective-permute-start.3 = (bf16[128,1024]{1,0:T(8,128)(2,1)}, bf16[128,1024]{1,0:T(8,128)(2,1)S(1)}, u32[]{:S(2)}, u32[]{:S(2)}) collective-permute-start(bf16[128,1024]{1,0:T(8,128)(2,1)} %get-tuple-element.38), channel_id=1, source_target_pairs={{0,6},{2,0},{4,2},{6,4},{1,7},{3,1},{5,3},{7,5},{8,14},{10,8},{12,... | collective-permute-start | bytes 786440 | tf_op jit(solution)/shard_map/ppermute | solution.py:294
  8.9 1.6 %copy-done.1 = bf16[1,1024,1024]{2,1,0:T(8,128)(2,1)S(1)} copy-done((bf16[1,1024,1024]{2,1,0:T(8,128)(2,1)S(1)}, bf16[1,1024,1024]{2,1,0:T(8,128)(2,1)}, u32[]{:S(2)}) %copy-start.1) | copy-done | bytes 2097176
  10.5 1.2 %copy-done.3 = bf16[256,2048]{1,0:T(8,128)(2,1)S(1)} copy-done((bf16[256,2048]{1,0:T(8,128)(2,1)S(1)}, bf16[256,2048]{1,0:T(8,128)(2,1)}, u32[]{:S(2)}) %copy-start.3) | copy-done | bytes 1048600
  11.7 1.2 %copy-done.4 = bf16[256,2048]{1,0:T(8,128)(2,1)S(1)} copy-done((bf16[256,2048]{1,0:T(8,128)(2,1)S(1)}, bf16[256,2048]{1,0:T(8,128)(2,1)}, u32[]{:S(2)}) %copy-start.4) | copy-done | bytes 1048600
  12.9 7.1 %expert_rows.3 = (bf16[2,512,2048]{2,1,0:T(8,128)(2,1)S(1)}, bf16[2,512,1024]{2,1,0:T(8,128)(2,1)S(1)}, bf16[2,128,512]{2,1,0:T(8,128)(2,1)S(1)}, bf16[2,128,512]{2,1,0:T(8,128)(2,1)S(1)}) custom-call(s32[1,256]{1,0:T(1,128)S(1)} %bitcast.23, s32[1,256]{1,0:T(1,128)S(1)} %bitcast.26, f32[1,256]{1,0:T(1,128)S(1)} %bitcast.29, ...), custom_call_target="tpu_custom_call" | custom-call | flops 1610612736 | bytes 10485760 | tf_op jit(solution)/shard_map/expert_rows/pallas_call | solution.py:199
  20.6 1.9 %collective-permute-start.4 = (bf16[256,1024]{1,0:T(8,128)(2,1)S(1)}, bf16[256,1024]{1,0:T(8,128)(2,1)S(1)}, u32[]{:S(2)}, u32[]{:S(2)}) collective-permute-start(bf16[256,1024]{1,0:T(8,128)(2,1)S(1)} %constant_dynamic-update-slice_fusion.refs_0_), channel_id=1, source_target_pairs={{0,16},{8,24},{16,0},{24,8},{1,17},{9,25},{17,1},{25,9},{2,18},{10... | collective-permute-start | bytes 1572872 | tf_op jit(solution)/shard_map/ppermute | solution.py:291
  22.4 1.5 %collective-permute-start.6 = (bf16[256,1024]{1,0:T(8,128)(2,1)S(1)}, bf16[256,1024]{1,0:T(8,128)(2,1)S(1)}, u32[]{:S(2)}, u32[]{:S(2)}) collective-permute-start(bf16[256,1024]{1,0:T(8,128)(2,1)S(1)} %constant_dynamic-update-slice_fusion.refs_0_), channel_id=1, source_target_pairs={{0,8},{8,0},{16,24},{24,16},{1,9},{9,1},{17,25},{25,17},{2,10},{10... | collective-permute-start | bytes 1572872 | tf_op jit(solution)/shard_map/ppermute | solution.py:291
  23.9 2.6 %collective-permute-start.10 = (bf16[128,1024]{1,0:T(8,128)(2,1)S(1)}, bf16[128,1024]{1,0:T(8,128)(2,1)S(1)}, u32[]{:S(2)}, u32[]{:S(2)}) collective-permute-start(bf16[128,1024]{1,0:T(8,128)(2,1)S(1)} %copy-done.8), channel_id=1, source_target_pairs={{0,4},{2,6},{4,0},{6,2},{1,5},{3,7},{5,1},{7,3},{8,12},{10,14},{12... | collective-permute-start | bytes 786440 | tf_op jit(solution)/shard_map/ppermute | solution.py:294
  26.5 8.1 %collective-permute-done.4.refs_2_ = bf16[256,1024]{1,0:T(8,128)(2,1)S(1)} collective-permute-done((bf16[256,1024]{1,0:T(8,128)(2,1)S(1)}, bf16[256,1024]{1,0:T(8,128)(2,1)S(1)}, u32[]{:S(2)}, u32[]{:S(2)}) %collective-permute-start.4) | collective-permute-done | bytes 524320 | tf_op jit(solution)/shard_map/ppermute | solution.py:291
  34.6 1.8 %collective-permute-start.5 = (bf16[256,512]{1,0:T(8,128)(2,1)S(1)}, bf16[256,512]{1,0:T(8,128)(2,1)S(1)}, u32[]{:S(2)}, u32[]{:S(2)}) collective-permute-start(bf16[256,512]{1,0:T(8,128)(2,1)S(1)} %slice.36), channel_id=1, source_target_pairs={{0,8},{8,0},{16,24},{24,16},{1,9},{9,1},{17,25},{25,17},{2,10},{10... | collective-permute-start | bytes 786440 | tf_op jit(solution)/shard_map/ppermute | solution.py:291
  36.4 1.6 %collective-permute-start.7 = (bf16[256,512]{1,0:T(8,128)(2,1)S(1)}, bf16[256,512]{1,0:T(8,128)(2,1)S(1)}, u32[]{:S(2)}, u32[]{:S(2)}) collective-permute-start(bf16[256,512]{1,0:T(8,128)(2,1)S(1)} %slice.37), channel_id=1, source_target_pairs={{0,16},{8,24},{16,0},{24,8},{1,17},{9,25},{17,1},{25,9},{2,18},{10... | collective-permute-start | bytes 786440 | tf_op jit(solution)/shard_map/ppermute | solution.py:291
  39.7 2.0 %collective-permute-start.18 = (bf16[128,1024]{1,0:T(8,128)(2,1)S(1)}, bf16[128,1024]{1,0:T(8,128)(2,1)S(1)}, u32[]{:S(2)}, u32[]{:S(2)}) collective-permute-start(bf16[128,1024]{1,0:T(8,128)(2,1)S(1)} %collective-permute-done.10.refs_0_), channel_id=1, source_target_pairs={{0,24},{8,16},{16,8},{24,0},{1,25},{9,17},{17,9},{25,1},{2,26},{10... | collective-permute-start | bytes 786440 | tf_op jit(solution)/shard_map/ppermute | solution.py:291
  41.7 2.3 %collective-permute-done.5.refs_3_ = bf16[256,512]{1,0:T(8,128)(2,1)S(1)} collective-permute-done((bf16[256,512]{1,0:T(8,128)(2,1)S(1)}, bf16[256,512]{1,0:T(8,128)(2,1)S(1)}, u32[]{:S(2)}, u32[]{:S(2)}) %collective-permute-start.5) | collective-permute-done | bytes 262176 | tf_op jit(solution)/shard_map/ppermute | solution.py:291
  44.0 1.8 %collective-permute-done.7.refs_4_ = bf16[256,512]{1,0:T(8,128)(2,1)S(1)} collective-permute-done((bf16[256,512]{1,0:T(8,128)(2,1)S(1)}, bf16[256,512]{1,0:T(8,128)(2,1)S(1)}, u32[]{:S(2)}, u32[]{:S(2)}) %collective-permute-start.7) | collective-permute-done | bytes 262176 | tf_op jit(solution)/shard_map/ppermute | solution.py:291
  45.8 1.1 %collective-permute-start.8 = (bf16[2,128,512]{2,1,0:T(8,128)(2,1)S(1)}, bf16[2,128,512]{2,1,0:T(8,128)(2,1)S(1)}, u32[]{:S(2)}, u32[]{:S(2)}) collective-permute-start(bf16[2,128,512]{2,1,0:T(8,128)(2,1)S(1)} %get-tuple-element.39), channel_id=1, source_target_pairs={{0,8},{8,0},{16,24},{24,16},{1,9},{9,1},{17,25},{25,17},{2,10},{10... | collective-permute-start | bytes 786440 | tf_op jit(solution)/shard_map/ppermute | solution.py:291
  46.9 2.7 %collective-permute-done.11.refs_1_ = bf16[128,1024]{1,0:T(8,128)(2,1)S(1)} collective-permute-done((bf16[128,1024]{1,0:T(8,128)(2,1)S(1)}, bf16[128,1024]{1,0:T(8,128)(2,1)S(1)}, u32[]{:S(2)}, u32[]{:S(2)}) %collective-permute-start.11) | collective-permute-done | bytes 262176 | tf_op jit(solution)/shard_map/ppermute | solution.py:291
  49.6 7.1 %expert_rows.4 = (bf16[2,512,2048]{2,1,0:T(8,128)(2,1)S(1)}, bf16[2,512,1024]{2,1,0:T(8,128)(2,1)S(1)}, bf16[256,512]{1,0:T(8,128)(2,1)S(1)}, bf16[256,512]{1,0:...) custom-call(bf16[256,1024]{1,0:T(8,128)(2,1)S(1)} %constant_dynamic-, ...), custom_call_target="tpu_custom_call", output_to_operand_aliasing={{0}: (9, {}), {1}: (10, {})} | custom-call | flops 3221225472 | bytes 12582912 | tf_op jit(solution)/shard_map/expert_rows/pallas_call | solution.py:199
  56.7 2.7 %collective-permute-start.14 = (bf16[256,512]{1,0:T(8,128)(2,1)S(1)}, bf16[256,512]{1,0:T(8,128)(2,1)S(1)}, u32[]{:S(2)}, u32[]{:S(2)}) collective-permute-start(bf16[256,512]{1,0:T(8,128)(2,1)S(1)} %get-tuple-element.48), channel_id=1, source_target_pairs={{0,24},{8,16},{16,8},{24,0},{1,25},{9,17},{17,9},{25,1},{2,26},{10... | collective-permute-start | bytes 786440 | tf_op jit(solution)/shard_map/ppermute | solution.py:291
  60.9 1.7 %collective-permute-start.12 = (bf16[256,512]{1,0:T(8,128)(2,1)S(1)}, bf16[256,512]{1,0:T(8,128)(2,1)S(1)}, u32[]{:S(2)}, u32[]{:S(2)}) collective-permute-start(bf16[256,512]{1,0:T(8,128)(2,1)S(1)} %get-tuple-element.46), channel_id=1, source_target_pairs={{0,8},{8,0},{16,24},{24,16},{1,9},{9,1},{17,25},{25,17},{2,10},{10... | collective-permute-start | bytes 786440 | tf_op jit(solution)/shard_map/ppermute | solution.py:291
  62.6 6.7 %expert_rows.5 = (bf16[2,512,2048]{2,1,0:T(8,128)(2,1)S(1)}, bf16[2,512,1024]{2,1,0:T(8,128)(2,1)S(1)}, bf16[128,512]{1,0:T(8,128)(2,1)S(1)}, bf16[128,512]{1,0:...) custom-call(bf16[128,1024]{1,0:T(8,128)(2,1)S(1)} %collective-permut, ...), custom_call_target="tpu_custom_call", output_to_operand_aliasing={{0}: (8, {}), {1}: (9, {})} | custom-call | flops 1610612736 | bytes 10485760 | tf_op jit(solution)/shard_map/expert_rows/pallas_call | solution.py:199
  69.3 2.4 %convolution_convert_fusion = bf16[2,1024,1024]{2,1,0:T(8,128)(2,1)S(1)} fusion(bf16[2,512,1024]{2,1,0:T(8,128)(2,1)S(1)} %get-tuple-element.55.acts, bf16[2,512,2048]{2,1,0:T(8,128)(2,1)S(1)} %get-tuple-element.54.rows), kind=kOutput, calls=%fused_computation | convolution fusion | flops 2149580800 | bytes 8388608 | tf_op jit(solution)/shard_map/dot_general | solution.py:320
  71.8 1.5 %collective-permute-start.9 = (bf16[128,512]{1,0:T(8,128)(2,1)S(1)}, bf16[128,512]{1,0:T(8,128)(2,1)S(1)}, u32[]{:S(2)}, u32[]{:S(2)}) collective-permute-start(bf16[128,512]{1,0:T(8,128)(2,1)S(1)} %fusion.2), channel_id=1, source_target_pairs={{0,16},{8,24},{16,0},{24,8},{1,17},{9,25},{17,1},{25,9},{2,18},{10... | collective-permute-start | bytes 393224 | tf_op jit(solution)/shard_map/ppermute | solution.py:291
  73.7 1.7 %collective-permute-start.20 = (bf16[128,512]{1,0:T(8,128)(2,1)S(1)}, bf16[128,512]{1,0:T(8,128)(2,1)S(1)}, u32[]{:S(2)}, u32[]{:S(2)}) collective-permute-start(bf16[128,512]{1,0:T(8,128)(2,1)S(1)} %get-tuple-element.58), channel_id=1, source_target_pairs={{0,16},{8,24},{16,0},{24,8},{1,17},{9,25},{17,1},{25,9},{2,18},{10... | collective-permute-start | bytes 393224 | tf_op jit(solution)/shard_map/ppermute | solution.py:291
  75.4 1.4 %collective-permute-start.19 = (bf16[128,512]{1,0:T(8,128)(2,1)S(1)}, bf16[128,512]{1,0:T(8,128)(2,1)S(1)}, u32[]{:S(2)}, u32[]{:S(2)}) collective-permute-start(bf16[128,512]{1,0:T(8,128)(2,1)S(1)} %get-tuple-element.56), channel_id=1, source_target_pairs={{0,8},{8,0},{16,24},{24,16},{1,9},{9,1},{17,25},{25,17},{2,10},{10... | collective-permute-start | bytes 393224 | tf_op jit(solution)/shard_map/ppermute | solution.py:291
  77.0 3.6 %collective-permute-done.21 = bf16[128,512]{1,0:T(8,128)(2,1)S(1)} collective-permute-done((bf16[128,512]{1,0:T(8,128)(2,1)S(1)}, bf16[128,512]{1,0:T(8,128)(2,1)S(1)}, u32[]{:S(2)}, u32[]{:S(2)}) %collective-permute-start.21) | collective-permute-done | bytes 131104 | tf_op jit(solution)/shard_map/ppermute | solution.py:291
  80.6 3.6 %collective-permute-start.15 = (bf16[128,512]{1,0:T(8,128)(2,1)S(1)}, bf16[128,512]{1,0:T(8,128)(2,1)S(1)}, u32[]{:S(2)}, u32[]{:S(2)}) collective-permute-start(bf16[128,512]{1,0:T(8,128)(2,1)S(1)} %get-tuple-element.66), channel_id=1, source_target_pairs={{0,6},{2,0},{4,2},{6,4},{1,7},{3,1},{5,3},{7,5},{8,14},{10,8},{12,... | collective-permute-start | bytes 393224 | tf_op jit(solution)/shard_map/ppermute | solution.py:294
  85.1 2.6 %collective-permute-start.22 = (bf16[128,512]{1,0:T(8,128)(2,1)S(1)}, bf16[128,512]{1,0:T(8,128)(2,1)S(1)}, u32[]{:S(2)}, u32[]{:S(2)}) collective-permute-start(bf16[128,512]{1,0:T(8,128)(2,1)S(1)} %add_convert_fusion.1), channel_id=1, source_target_pairs={{0,4},{2,6},{4,0},{6,2},{1,5},{3,7},{5,1},{7,3},{8,12},{10,14},{12... | collective-permute-start | bytes 393224 | tf_op jit(solution)/shard_map/ppermute | solution.py:294
  87.8 3.9 %weight_grads.1 = (bf16[1024,1024]{1,0:T(8,128)(2,1)}, bf16[1024,1024]{1,0:T(8,128)(2,1)}) custom-call(bf16[2,512,2048]{2,1,0:T(8,128)(2,1)S(1)} %get-tuple-element.54.rows, bf16[2,512,1024]{2,1,0:T(8,128)(2,1)S(1)} %get-tuple-element.55.acts, bf16[2,1024,1024]{2,1,0:T(8,128)(2,1)S(1)} %collective-permute-done.23.got), custom_call_target="tpu_custom_call" | custom-call | flops 1000 | bytes 1000 | tf_op jit(solution)/shard_map/weight_grads/pallas_call | solution.py:263
  91.6 4.4 %collective-permute-done.22.refs_3_ = bf16[128,512]{1,0:T(8,128)(2,1)S(1)} collective-permute-done((bf16[128,512]{1,0:T(8,128)(2,1)S(1)}, bf16[128,512]{1,0:T(8,128)(2,1)S(1)}, u32[]{:S(2)}, u32[]{:S(2)}) %collective-permute-start.22) | collective-permute-done | bytes 131104 | tf_op jit(solution)/shard_map/ppermute | solution.py:294
  96.1 1.2 %unplace_rows.1 = bf16[256,512]{1,0:T(8,128)(2,1)} custom-call(s32[1,256]{1,0:T(1,128)S(1)} %bitcast.24, s32[1,256]{1,0:T(1,128)S(1)} %bitcast.27, bf16[128,512]{1,0:T(8,128)(2,1)S(1)} %fusion.1.refs_0_, bf16[128,512]{1,0:T(8,128)(2,1)S(1)} %collective-permute-done.15.refs_1_, bf16[128,512]{1,0:T(8,128)(2,1)S(1)} %collective-permute-done.16.refs_2_, ...), custom_call_target="tpu_custom_call" | custom-call | flops 1000 | bytes 1000 | tf_op jit(solution)/shard_map/unplace_rows/pallas_call | solution.py:235
  (50 shorter events, 5.6 us)
Async XLA Ops:
  0.6 8.2 %copy-start = (bf16[1,1024,1024]{2,1,0:T(8,128)(2,1)S(1)}, bf16[1,1024,1024]{2,1,0:T(8,128)(2,1)}, u32[]{:S(2)}) copy-start(bf16[1,1024,1024]{2,1,0:T(8,128)(2,1)} %param.12) | copy-start | bytes 6291460
  0.6 8.2 %copy-start.5 = (s32[256,1]{0,1:T(1,128)S(1)}, s32[256,1]{0,1:T(1,128)}, u32[]{:S(2)}) copy-start(s32[256,1]{0,1:T(1,128)} %param.10) | copy-start | bytes 3076
  0.7 8.2 %copy-start.6 = (s32[256,1]{0,1:T(1,128)S(1)}, s32[256,1]{0,1:T(1,128)}, u32[]{:S(2)}) copy-start(s32[256,1]{0,1:T(1,128)} %param.11) | copy-start | bytes 3076
  0.7 8.2 %copy-start.7 = (f32[256]{0:T(256)S(1)}, f32[256]{0:T(256)}, u32[]{:S(2)}) copy-start(f32[256]{0:T(256)} %param.9) | copy-start | bytes 3076
  0.7 8.2 %collective-permute-start = (bf16[1024,1024]{1,0:T(8,128)(2,1)}, bf16[1024,1024]{1,0:T(8,128)(2,1)S(1)}, u32[]{:S(2)}, u32[]{:S(2)}) collective-permute-start(bf16[1024,1024]{1,0:T(8,128)(2,1)} %bitcast.14), channel_id=1, source_target_pairs={{0,1},{1,0},{2,3},{3,2},{4,5},{5,4},{6,7},{7,6},{8,9},{9,8},{10,11... | collective-permute-start | bytes 6291464 | tf_op jit(solution)/shard_map/ppermute | solution.py:288
  1.2 7.7 %collective-permute-start.1 = (bf16[1024,1024]{1,0:T(8,128)(2,1)}, bf16[1024,1024]{1,0:T(8,128)(2,1)S(1)}, u32[]{:S(2)}, u32[]{:S(2)}) collective-permute-start(bf16[1024,1024]{1,0:T(8,128)(2,1)} %bitcast.18), channel_id=1, source_target_pairs={{0,1},{1,0},{2,3},{3,2},{4,5},{5,4},{6,7},{7,6},{8,9},{9,8},{10,11... | collective-permute-start | bytes 6291464 | tf_op jit(solution)/shard_map/ppermute | solution.py:288
  3.7 16.4 %collective-permute-start.2 = (bf16[128,1024]{1,0:T(8,128)(2,1)}, bf16[128,1024]{1,0:T(8,128)(2,1)S(1)}, u32[]{:S(2)}, u32[]{:S(2)}) collective-permute-start(bf16[128,1024]{1,0:T(8,128)(2,1)} %get-tuple-element.36), channel_id=1, source_target_pairs={{0,2},{2,4},{4,6},{6,0},{1,3},{3,5},{5,7},{7,1},{8,10},{10,12},{12... | collective-permute-start | bytes 786440 | tf_op jit(solution)/shard_map/ppermute | solution.py:294
  6.8 13.8 %collective-permute-start.3 = (bf16[128,1024]{1,0:T(8,128)(2,1)}, bf16[128,1024]{1,0:T(8,128)(2,1)S(1)}, u32[]{:S(2)}, u32[]{:S(2)}) collective-permute-start(bf16[128,1024]{1,0:T(8,128)(2,1)} %get-tuple-element.38), channel_id=1, source_target_pairs={{0,6},{2,0},{4,2},{6,4},{1,7},{3,1},{5,3},{7,5},{8,14},{10,8},{12,... | collective-permute-start | bytes 786440 | tf_op jit(solution)/shard_map/ppermute | solution.py:294
  8.9 1.6 %copy-start.1 = (bf16[1,1024,1024]{2,1,0:T(8,128)(2,1)S(1)}, bf16[1,1024,1024]{2,1,0:T(8,128)(2,1)}, u32[]{:S(2)}) copy-start(bf16[1,1024,1024]{2,1,0:T(8,128)(2,1)} %param.13) | copy-start | bytes 6291460
  10.5 1.2 %copy-start.3 = (bf16[256,2048]{1,0:T(8,128)(2,1)S(1)}, bf16[256,2048]{1,0:T(8,128)(2,1)}, u32[]{:S(2)}) copy-start(bf16[256,2048]{1,0:T(8,128)(2,1)} %tokens.1) | copy-start | bytes 3145732
  12.9 11.0 %copy-start.8 = (bf16[128,1024]{1,0:T(8,128)(2,1)S(1)}, bf16[128,1024]{1,0:T(8,128)(2,1)}, u32[]{:S(2)}) copy-start(bf16[128,1024]{1,0:T(8,128)(2,1)} %get-tuple-element.40) | copy-start | bytes 786436
  20.1 29.5 %copy-start.2 = (bf16[1,1024,1024]{2,1,0:T(8,128)(2,1)S(1)}, bf16[1,1024,1024]{2,1,0:T(8,128)(2,1)}, u32[]{:S(2)}) copy-start(bf16[1,1024,1024]{2,1,0:T(8,128)(2,1)} %param.13) | copy-start | bytes 6291460
  20.6 14.1 %collective-permute-start.4 = (bf16[256,1024]{1,0:T(8,128)(2,1)S(1)}, bf16[256,1024]{1,0:T(8,128)(2,1)S(1)}, u32[]{:S(2)}, u32[]{:S(2)}) collective-permute-start(bf16[256,1024]{1,0:T(8,128)(2,1)S(1)} %constant_dynamic-update-slice_fusion.refs_0_), channel_id=1, source_target_pairs={{0,16},{8,24},{16,0},{24,8},{1,17},{9,25},{17,1},{25,9},{2,18},{10... | collective-permute-start | bytes 1572872 | tf_op jit(solution)/shard_map/ppermute | solution.py:291
  22.4 14.0 %collective-permute-start.6 = (bf16[256,1024]{1,0:T(8,128)(2,1)S(1)}, bf16[256,1024]{1,0:T(8,128)(2,1)S(1)}, u32[]{:S(2)}, u32[]{:S(2)}) collective-permute-start(bf16[256,1024]{1,0:T(8,128)(2,1)S(1)} %constant_dynamic-update-slice_fusion.refs_0_), channel_id=1, source_target_pairs={{0,8},{8,0},{16,24},{24,16},{1,9},{9,1},{17,25},{25,17},{2,10},{10... | collective-permute-start | bytes 1572872 | tf_op jit(solution)/shard_map/ppermute | solution.py:291
  23.9 14.3 %collective-permute-start.10 = (bf16[128,1024]{1,0:T(8,128)(2,1)S(1)}, bf16[128,1024]{1,0:T(8,128)(2,1)S(1)}, u32[]{:S(2)}, u32[]{:S(2)}) collective-permute-start(bf16[128,1024]{1,0:T(8,128)(2,1)S(1)} %copy-done.8), channel_id=1, source_target_pairs={{0,4},{2,6},{4,0},{6,2},{1,5},{3,7},{5,1},{7,3},{8,12},{10,14},{12... | collective-permute-start | bytes 786440 | tf_op jit(solution)/shard_map/ppermute | solution.py:294
  34.6 9.3 %collective-permute-start.5 = (bf16[256,512]{1,0:T(8,128)(2,1)S(1)}, bf16[256,512]{1,0:T(8,128)(2,1)S(1)}, u32[]{:S(2)}, u32[]{:S(2)}) collective-permute-start(bf16[256,512]{1,0:T(8,128)(2,1)S(1)} %slice.36), channel_id=1, source_target_pairs={{0,8},{8,0},{16,24},{24,16},{1,9},{9,1},{17,25},{25,17},{2,10},{10... | collective-permute-start | bytes 786440 | tf_op jit(solution)/shard_map/ppermute | solution.py:291
  36.4 9.3 %collective-permute-start.7 = (bf16[256,512]{1,0:T(8,128)(2,1)S(1)}, bf16[256,512]{1,0:T(8,128)(2,1)S(1)}, u32[]{:S(2)}, u32[]{:S(2)}) collective-permute-start(bf16[256,512]{1,0:T(8,128)(2,1)S(1)} %slice.37), channel_id=1, source_target_pairs={{0,16},{8,24},{16,0},{24,8},{1,17},{9,25},{17,1},{25,9},{2,18},{10... | collective-permute-start | bytes 786440 | tf_op jit(solution)/shard_map/ppermute | solution.py:291
  38.2 11.4 %collective-permute-start.11 = (bf16[128,1024]{1,0:T(8,128)(2,1)S(1)}, bf16[128,1024]{1,0:T(8,128)(2,1)S(1)}, u32[]{:S(2)}, u32[]{:S(2)}) collective-permute-start(bf16[128,1024]{1,0:T(8,128)(2,1)S(1)} %collective-permute-done.10.refs_0_), channel_id=1, source_target_pairs={{0,8},{8,0},{16,24},{24,16},{1,9},{9,1},{17,25},{25,17},{2,10},{10... | collective-permute-start | bytes 786440 | tf_op jit(solution)/shard_map/ppermute | solution.py:291
  38.7 23.8 %collective-permute-start.17 = (bf16[128,1024]{1,0:T(8,128)(2,1)S(1)}, bf16[128,1024]{1,0:T(8,128)(2,1)S(1)}, u32[]{:S(2)}, u32[]{:S(2)}) collective-permute-start(bf16[128,1024]{1,0:T(8,128)(2,1)S(1)} %collective-permute-done.10.refs_0_), channel_id=1, source_target_pairs={{0,16},{8,24},{16,0},{24,8},{1,17},{9,25},{17,1},{25,9},{2,18},{10... | collective-permute-start | bytes 786440 | tf_op jit(solution)/shard_map/ppermute | solution.py:291
  39.7 22.9 %collective-permute-start.18 = (bf16[128,1024]{1,0:T(8,128)(2,1)S(1)}, bf16[128,1024]{1,0:T(8,128)(2,1)S(1)}, u32[]{:S(2)}, u32[]{:S(2)}) collective-permute-start(bf16[128,1024]{1,0:T(8,128)(2,1)S(1)} %collective-permute-done.10.refs_0_), channel_id=1, source_target_pairs={{0,24},{8,16},{16,8},{24,0},{1,25},{9,17},{17,9},{25,1},{2,26},{10... | collective-permute-start | bytes 786440 | tf_op jit(solution)/shard_map/ppermute | solution.py:291
  45.8 15.1 %collective-permute-start.8 = (bf16[2,128,512]{2,1,0:T(8,128)(2,1)S(1)}, bf16[2,128,512]{2,1,0:T(8,128)(2,1)S(1)}, u32[]{:S(2)}, u32[]{:S(2)}) collective-permute-start(bf16[2,128,512]{2,1,0:T(8,128)(2,1)S(1)} %get-tuple-element.39), channel_id=1, source_target_pairs={{0,8},{8,0},{16,24},{24,16},{1,9},{9,1},{17,25},{25,17},{2,10},{10... | collective-permute-start | bytes 786440 | tf_op jit(solution)/shard_map/ppermute | solution.py:291
  56.7 15.0 %collective-permute-start.14 = (bf16[256,512]{1,0:T(8,128)(2,1)S(1)}, bf16[256,512]{1,0:T(8,128)(2,1)S(1)}, u32[]{:S(2)}, u32[]{:S(2)}) collective-permute-start(bf16[256,512]{1,0:T(8,128)(2,1)S(1)} %get-tuple-element.48), channel_id=1, source_target_pairs={{0,24},{8,16},{16,8},{24,0},{1,25},{9,17},{17,9},{25,1},{2,26},{10... | collective-permute-start | bytes 786440 | tf_op jit(solution)/shard_map/ppermute | solution.py:291
  59.4 12.2 %collective-permute-start.13 = (bf16[256,512]{1,0:T(8,128)(2,1)S(1)}, bf16[256,512]{1,0:T(8,128)(2,1)S(1)}, u32[]{:S(2)}, u32[]{:S(2)}) collective-permute-start(bf16[256,512]{1,0:T(8,128)(2,1)S(1)} %get-tuple-element.47), channel_id=1, source_target_pairs={{0,16},{8,24},{16,0},{24,8},{1,17},{9,25},{17,1},{25,9},{2,18},{10... | collective-permute-start | bytes 786440 | tf_op jit(solution)/shard_map/ppermute | solution.py:291
  60.9 10.8 %collective-permute-start.12 = (bf16[256,512]{1,0:T(8,128)(2,1)S(1)}, bf16[256,512]{1,0:T(8,128)(2,1)S(1)}, u32[]{:S(2)}, u32[]{:S(2)}) collective-permute-start(bf16[256,512]{1,0:T(8,128)(2,1)S(1)} %get-tuple-element.46), channel_id=1, source_target_pairs={{0,8},{8,0},{16,24},{24,16},{1,9},{9,1},{17,25},{25,17},{2,10},{10... | collective-permute-start | bytes 786440 | tf_op jit(solution)/shard_map/ppermute | solution.py:291
  71.7 16.1 %collective-permute-start.23 = (bf16[2,1024,1024]{2,1,0:T(8,128)(2,1)S(1)}, bf16[2,1024,1024]{2,1,0:T(8,128)(2,1)S(1)}, u32[]{:S(2)}, u32[]{:S(2)}) collective-permute-start(bf16[2,1024,1024]{2,1,0:T(8,128)(2,1)S(1)} %convolution_convert_fusion), channel_id=1, source_target_pairs={{0,1},{1,0},{2,3},{3,2},{4,5},{5,4},{6,7},{7,6},{8,9},{9,8},{10,11... | collective-permute-start | bytes 12582920 | tf_op jit(solution)/shard_map/ppermute | solution.py:288
  71.8 15.9 %collective-permute-start.9 = (bf16[128,512]{1,0:T(8,128)(2,1)S(1)}, bf16[128,512]{1,0:T(8,128)(2,1)S(1)}, u32[]{:S(2)}, u32[]{:S(2)}) collective-permute-start(bf16[128,512]{1,0:T(8,128)(2,1)S(1)} %fusion.2), channel_id=1, source_target_pairs={{0,16},{8,24},{16,0},{24,8},{1,17},{9,25},{17,1},{25,9},{2,18},{10... | collective-permute-start | bytes 393224 | tf_op jit(solution)/shard_map/ppermute | solution.py:291
  73.4 7.3 %collective-permute-start.21 = (bf16[128,512]{1,0:T(8,128)(2,1)S(1)}, bf16[128,512]{1,0:T(8,128)(2,1)S(1)}, u32[]{:S(2)}, u32[]{:S(2)}) collective-permute-start(bf16[128,512]{1,0:T(8,128)(2,1)S(1)} %get-tuple-element.60), channel_id=1, source_target_pairs={{0,24},{8,16},{16,8},{24,0},{1,25},{9,17},{17,9},{25,1},{2,26},{10... | collective-permute-start | bytes 393224 | tf_op jit(solution)/shard_map/ppermute | solution.py:291
  73.7 10.6 %collective-permute-start.20 = (bf16[128,512]{1,0:T(8,128)(2,1)S(1)}, bf16[128,512]{1,0:T(8,128)(2,1)S(1)}, u32[]{:S(2)}, u32[]{:S(2)}) collective-permute-start(bf16[128,512]{1,0:T(8,128)(2,1)S(1)} %get-tuple-element.58), channel_id=1, source_target_pairs={{0,16},{8,24},{16,0},{24,8},{1,17},{9,25},{17,1},{25,9},{2,18},{10... | collective-permute-start | bytes 393224 | tf_op jit(solution)/shard_map/ppermute | solution.py:291
  75.4 9.6 %collective-permute-start.19 = (bf16[128,512]{1,0:T(8,128)(2,1)S(1)}, bf16[128,512]{1,0:T(8,128)(2,1)S(1)}, u32[]{:S(2)}, u32[]{:S(2)}) collective-permute-start(bf16[128,512]{1,0:T(8,128)(2,1)S(1)} %get-tuple-element.56), channel_id=1, source_target_pairs={{0,8},{8,0},{16,24},{24,16},{1,9},{9,1},{17,25},{25,17},{2,10},{10... | collective-permute-start | bytes 393224 | tf_op jit(solution)/shard_map/ppermute | solution.py:291
  80.6 15.4 %collective-permute-start.15 = (bf16[128,512]{1,0:T(8,128)(2,1)S(1)}, bf16[128,512]{1,0:T(8,128)(2,1)S(1)}, u32[]{:S(2)}, u32[]{:S(2)}) collective-permute-start(bf16[128,512]{1,0:T(8,128)(2,1)S(1)} %get-tuple-element.66), channel_id=1, source_target_pairs={{0,6},{2,0},{4,2},{6,4},{1,7},{3,1},{5,3},{7,5},{8,14},{10,8},{12,... | collective-permute-start | bytes 393224 | tf_op jit(solution)/shard_map/ppermute | solution.py:294
  84.3 11.8 %collective-permute-start.16 = (bf16[128,512]{1,0:T(8,128)(2,1)S(1)}, bf16[128,512]{1,0:T(8,128)(2,1)S(1)}, u32[]{:S(2)}, u32[]{:S(2)}) collective-permute-start(bf16[128,512]{1,0:T(8,128)(2,1)S(1)} %get-tuple-element.65), channel_id=1, source_target_pairs={{0,2},{2,4},{4,6},{6,0},{1,3},{3,5},{5,7},{7,1},{8,10},{10,12},{12... | collective-permute-start | bytes 393224 | tf_op jit(solution)/shard_map/ppermute | solution.py:294
  85.1 11.0 %collective-permute-start.22 = (bf16[128,512]{1,0:T(8,128)(2,1)S(1)}, bf16[128,512]{1,0:T(8,128)(2,1)S(1)}, u32[]{:S(2)}, u32[]{:S(2)}) collective-permute-start(bf16[128,512]{1,0:T(8,128)(2,1)S(1)} %add_convert_fusion.1), channel_id=1, source_target_pairs={{0,4},{2,6},{4,0},{6,2},{1,5},{3,7},{5,1},{7,3},{8,12},{10,14},{12... | collective-permute-start | bytes 393224 | tf_op jit(solution)/shard_map/ppermute | solution.py:294
  (1 other events, 1.2 us)

commit v12 on v11

--- a/solution.py
+++ b/solution.py
@@ -111,14 +111,14 @@
     return pre * half, half + 0.5 * pre * (1.0 - th * th) * (c + (3 * 0.044715 * c) * square)
 
 
-def expert_kernel(chunks, base, groups, aliased, *refs):
+def expert_kernel(chunks, base, block_base, aliased, *refs):
     refs = list(refs)
     take = lambda n: [refs.pop(0) for _ in range(n)]
     slots = take(5) if chunks is None else [take(n) for n in chunks]
     up_halves, down_halves = take(2), take(2)
     take(aliased)
-    kept_rows, kept_acts = take(2)
-    targets = [take(4 if step is None else 2) for _, step in groups]
+    kept, mate = take(2)
+    blocks = take(4)
     tok, grad, up, down, hidden, slope, back = take(7)
     if chunks is None:
         tok_in, grad_in = take(2)
@@ -162,8 +162,11 @@
     if chunks is None:
         tok[...] = dot(hot, tok_in[...]).astype(BF16)
         grad[...] = (dot(hot, grad_in[...]) * scale).astype(BF16)
-    mine = pl.ds(base, rows)
-    leave = [copies.start(src, kept_rows.at[i, mine, :]) for i, src in enumerate((tok, grad))]
+    mine, theirs = pl.ds(base, rows), pl.ds(block_base, rows)
+    leave = []
+    for i, src in enumerate((tok, grad)):
+        leave.append(copies.start(src.at[:, pl.ds(0, half)], kept.at[i, mine, :]))
+        leave.append(copies.start(src.at[:, pl.ds(half, half)], mate.at[i, theirs, :]))
     for n, arrived in zip(range(0, hid, step), tiles):
         cols = slice(n, n + step)
         wait(arrived)
@@ -172,41 +175,38 @@
         act, deriv = gelu_parts(pre)
         hidden[:, cols] = act.astype(BF16)
         slope[:, cols] = (hidden_grad * deriv).astype(BF16)
-    leave += [copies.start(src, kept_acts.at[i, mine, :]) for i, src in enumerate((slope, hidden))]
+    for i, src in enumerate((slope, hidden)):
+        leave += [copies.start(src, kept.at[2 + i, mine, :]), copies.start(src, mate.at[2 + i, theirs, :])]
     for j in range(4):
         quarter = pl.ds(pl.multiple_of((order ^ j) * share, share), share)
         back[j] = dot(slope[...], up[quarter, :], 1, 1).astype(BF16)
-        at = 0
-        for (n, step), outs in zip(groups, targets):
-            out = outs[j] if step is None else outs[(j & step) // step].at[(j & (3 - step)) // (3 - step)]
-            leave.append(copies.start(back.at[j, pl.ds(at, n), :], out))
-            at += n
+        leave.append(copies.start(back.at[j], blocks[j].at[theirs, :]))
     wait(leave)
 
 
-def expert_rows(own, chunks, groups, weights, total_rows, base, kept):
+def expert_rows(own, chunks, rows, weights, total_rows, base, block_rows, block_base, kept, sent):
     slots = own or sum(chunks, [])
     counts_in = None if own else [len(c) for c in chunks]
-    rows = sum(n for n, _ in groups)
     half, hid = weights[0].shape
     width, share = 2 * half, half // 2
-    operands = list(slots) + list(weights) + list(kept or [])
-    aliases = {len(slots) + 4 + i: i for i in range(2)} if kept else {}
+    operands = list(slots) + list(weights)
+    aliases = {}
+    for at, previous in ((0, [] if kept is None else [kept]), (1, sent or [])):
+        aliases.update({len(operands) + i: at + i for i in range(len(previous))})
+        operands += previous
     shape = lambda *s: jax.ShapeDtypeStruct(s, BF16)
     buf = lambda *s: pltpu.VMEM(s, BF16)
-    quarters = [[shape(n, share)] * 4 if step is None else [shape(2, n, share)] * 2 for n, step in groups]
-    counts = [len(q) for q in quarters]
     out = pl.pallas_call(
-        functools.partial(expert_kernel, counts_in, base, groups, len(aliases)),
-        out_shape=[shape(2, total_rows, width), shape(2, total_rows, hid)] + sum(quarters, []),
+        functools.partial(expert_kernel, counts_in, base, block_base, len(aliases)),
+        out_shape=[shape(4, total_rows, half), shape(4, block_rows, half)] + [shape(block_rows, share)] * 4,
         in_specs=([VMEM] * 3 if own else [ANY] * 3) + [ANY] * (len(operands) - 3),
-        out_specs=[ANY] * (2 + sum(counts)),
+        out_specs=[ANY] * 6,
         scratch_shapes=[
             buf(rows, width), buf(rows, width), buf(width, hid), buf(width, hid),
             buf(rows, hid), buf(rows, hid), buf(4, rows, share),
         ]
         + ([buf(*own[3].shape)] * 2 if own else [])
-        + [pltpu.SemaphoreType.DMA((16 + 4 * (hid // 256) + 4 * len(groups) + 4,))],
+        + [pltpu.SemaphoreType.DMA((28 + 4 * (hid // 256),))],
         input_output_aliases=aliases,
         compiler_params=pltpu.CompilerParams(vmem_limit_bytes=LIMIT + rows * 2**15),
         cost_estimate=pl.CostEstimate(
@@ -214,8 +214,7 @@
         ),
         name="expert_rows",
     )(*operands)
-    starts = [2 + sum(counts[:i]) for i in range(len(counts))]
-    return list(out[:2]), [list(out[i : i + n]) for i, n in zip(starts, counts)]
+    return out[0], list(out[1:])
 
 
 def unplace_kernel(spans, shifts, capacity, index, slot, *refs):
@@ -243,38 +242,37 @@
     )(index, slot, *backs)
 
 
-def weight_grad_kernel(rows, acts, got, up_out, down_out, total, sem):
+def weight_grad_kernel(kept, *refs):
+    *mates, up_out, down_out, total, sem = refs
     copies = Copies(sem)
     half = total.shape[1]
     step = 128
     leave = []
     for i, out in enumerate((up_out, down_out)):
         for n in range(0, half, step):
-            mine = dot(rows[i, :, n : n + step], acts[i], 0, 0).astype(BF16).astype(F32)
-            total[i, n : n + step, :] = (mine + got[i, n : n + step, :].astype(F32)).astype(BF16)
+            mine = dot(kept[i, :, n : n + step], kept[2 + i], 0, 0)
+            others = sum(dot(mate[i, :, n : n + step], mate[2 + i], 0, 0) for mate in mates)
+            both = mine.astype(BF16).astype(F32) + others.astype(BF16).astype(F32)
+            total[i, n : n + step, :] = both.astype(BF16)
             leave.append(copies.start(total.at[i, pl.ds(n, step), :], out.at[pl.ds(n, step), :]))
     wait(leave)
 
 
-def weight_grads(kept_rows, kept_acts, got):
-    _, count, width = kept_rows.shape
-    hid = kept_acts.shape[2]
-    half = width // 2
+def weight_grads(kept, mates):
+    _, _, half = kept.shape
+    operands = [kept] + mates
+    whole = lambda x: pl.BlockSpec(x.shape, lambda i: (0, 0, 0))
     return pl.pallas_call(
         weight_grad_kernel,
-        out_shape=[jax.ShapeDtypeStruct((half, hid), BF16)] * 2,
+        out_shape=[jax.ShapeDtypeStruct((half, half), BF16)] * 2,
         grid=(1,),
-        in_specs=[
-            pl.BlockSpec((2, count, half), lambda i: (0, 0, 0)),
-            pl.BlockSpec((2, count, hid), lambda i: (0, 0, 0)),
-            pl.BlockSpec((2, half, hid), lambda i: (0, 0, 0)),
-        ],
+        in_specs=[whole(x) for x in operands],
         out_specs=[ANY] * 2,
-        scratch_shapes=[pltpu.VMEM((2, half, hid), BF16), pltpu.SemaphoreType.DMA((2 * (half // 128),))],
+        scratch_shapes=[pltpu.VMEM((2, half, half), BF16), pltpu.SemaphoreType.DMA((2 * (half // 128),))],
         compiler_params=pltpu.CompilerParams(vmem_limit_bytes=40 * 2**20),
         cost_estimate=SMALL,
         name="weight_grads",
-    )(kept_rows, kept_acts, got)
+    )(*operands)
 
 
 def local(tokens, grad_output, gate_prob, expert_index, slot_index, up_weight, down_weight):
@@ -308,17 +306,6 @@
         terms = [b.astype(F32) for b in [blocks[0]] + got]
         return (terms[0] + terms[1] + (terms[2] + terms[3])).astype(BF16), got
 
-    def collect_pair(pair, step):
-        keep, send = pair
-        got = across(send, step)
-        last = across((keep[1].astype(F32) + got[1].astype(F32)).astype(BF16), 3 - step)
-        return (keep[0].astype(F32) + got[0].astype(F32) + last.astype(F32)).astype(BF16), got
-
-    def other_halves(kept):
-        rows, acts = kept
-        dims = (((1,), (1,)), ((0,), (0,)))
-        return lax.dot_general(rows[:, :, width // 2 :], acts, dims, preferred_element_type=F32).astype(BF16)
-
     index, slot = expert_index.reshape(1, tok_count), slot_index.reshape(1, tok_count)
     gate = gate_prob.reshape(1, tok_count)
     up_own, down_own = up_weight[0], down_weight[0]
@@ -330,20 +317,22 @@
         everything = 4 * capacity
         moved = [shift(rows, k) for rows, k in zip(sends, shifts)]
         own = [index, slot, gate, tokens, grad_output]
-        kept, (pair,) = expert_rows(own, None, [(capacity, 1)], weights, everything, 0, None)
-        near = spread(jnp.concatenate([after(moved[0], pair[0]), moved[1]], 0))
+        most = 3 * capacity
+        kept, sent = expert_rows(own, None, capacity, weights, everything, 0, most, 0, None, None)
+        near = spread(jnp.concatenate([after(moved[0], sent[1]), moved[1]], 0))
         far = after(moved[2], *near[1:3])
         far = [far] + [across(far, j) for j in (1, 2, 3)]
-        near[0] = after(near[0], far[1])
-        back, got_own = collect_pair([pair[0], after(pair[1], *near[3:])], 1)
-        kept, (blocks,) = expert_rows(None, [near], [(2 * capacity, None)], weights, everything, capacity, kept)
-        total, got = collect(blocks)
-        backs = [back, shift(total[:capacity], -1), shift(total[capacity:], -3)]
-        far[0] = after(far[0], got_own)
-        kept, (blocks,) = expert_rows(None, [far], [(capacity, None)], weights, everything, 3 * capacity, kept)
-        others = other_halves(kept)
-        grads = weight_grads(*kept, swap(after(others, *got)))
-        total, _ = collect([blocks[0]] + [after(b, got[0], others) for b in blocks[1:]])
+        near[0] = after(near[0], *far[1:])
+        kept, sent = expert_rows(
+            None, [near], 2 * capacity, weights, everything, capacity, most, capacity, kept, sent
+        )
+        total, got = collect(sent[1:])
+        backs = [total[:capacity], shift(total[capacity : 2 * capacity], -1), shift(total[2 * capacity :], -3)]
+        mates = [swap(sent[0])]
+        kept, sent = expert_rows(None, [far], capacity, weights, everything, most, capacity, 0, kept, None)
+        mates.append(swap(sent[0]))
+        total, _ = collect(sent[1:2] + [after(b, got[0]) for b in sent[2:]])
+        grads = weight_grads(kept, mates)
         backs.append(after(shift(total, -2), *grads))
         shifts = [0] + shifts
     else:
@@ -357,10 +346,9 @@
             return moved.reshape(rows, x.shape[1])
 
         (send,) = place([rows], shifts, capacity, index, slot, gate, tokens, grad_output)
-        kept, (blocks,) = expert_rows(None, [spread(exchange(send))], [(rows, None)], weights, rows, 0, None)
-        others = other_halves(kept)
-        grads = weight_grads(*kept, swap(others))
-        total, _ = collect(blocks)
+        kept, sent = expert_rows(None, [spread(exchange(send))], rows, weights, rows, 0, rows, 0, None, None)
+        total, _ = collect(sent[1:])
+        grads = weight_grads(kept, [swap(sent[0])])
         backs = [exchange(total)]
 
     return unplace(shifts, capacity, index, slot, backs), grads[0][None], grads[1][None]

time: 97.5 us -> 110 us (1.13)
  waiting for transfers between devices: 24.4 us -> 40.3 us
  starting transfers between devices: 36.7 us -> 30 us
  Pallas kernels: 28.4 us -> 31.8 us
  matrix products: 2.38 us -> 0 us
  local copies, waits for them, and re-layouts: 4.15 us -> 6.19 us
    ppermute x15 -> x13, waiting for transfers between devices: 19.4 us -> 28.6 us  [across(): return lax.ppermute(x, 'tensor', [(i, i ^ j) for i in range(tensor_size)])]
    ppermute x6, waiting for transfers between devices: 5 us -> 11.7 us  [shift(): lax.ppermute(x, 'expert', [(i, (i + k) % experts) for i in range(experts)])]
    ppermute x15 -> x13, starting transfers between devices: 21.3 us -> 15.6 us  [across(): return lax.ppermute(x, 'tensor', [(i, i ^ j) for i in range(tensor_size)])]
    pallas_call x1, Pallas kernels: 3.87 us -> 6.9 us  [weight_grads(): pl.pallas_call(weight_grad_kernel, out_shape=[jax.ShapeDtypeStruct((half,...]
    dot_general x1 -> x0, matrix products: 2.38 us -> none  [other_halves(): lax.dot_general(rows[:, :, width // 2:], acts, dims, preferred_element_ty...]
    unnamed x19 -> x23, local copies, waits for them, and re-layouts: 4.08 us -> 6.11 us
    ppermute x6, starting transfers between devices: 14.7 us -> 13.6 us  [shift(): lax.ppermute(x, 'expert', [(i, (i + k) % experts) for i in range(experts)])]
  transfers between devices with their start and end apart: 24 -> 23, of which waited for: 9 -> 10; matrix products, arithmetic and copies ran while one was open for 3% -> 0% of each run, Pallas kernels for 28% -> 21%
where the time goes in v12:
time: 110 us; the launch traced here: 109 us
  waiting for transfers between devices  40.3 us (37%)
  Pallas kernels  31.8 us (29%)
  starting transfers between devices  30 us (27%)
  local copies, waits for them, and re-layouts  6.19 us (6%)
    ppermute x13, waiting for transfers between devices, across(): return lax.ppermute(x, 'tensor', [(i, i ^ j) for i in range(tensor_size)])  28.6 us
    pallas_call x3, Pallas kernels, expert_rows(): pl.pallas_call(functools.partial(expert_kernel, counts_in, base, block_ba...  21.3 us
    ppermute x13, starting transfers between devices, across(): return lax.ppermute(x, 'tensor', [(i, i ^ j) for i in range(tensor_size)])  15.6 us
    ppermute x6, starting transfers between devices, shift(): lax.ppermute(x, 'expert', [(i, (i + k) % experts) for i in range(experts)])  13.6 us
    ppermute x6, waiting for transfers between devices, shift(): lax.ppermute(x, 'expert', [(i, (i + k) % experts) for i in range(experts)])  11.7 us
    pallas_call x1, Pallas kernels, weight_grads(): pl.pallas_call(weight_grad_kernel, out_shape=[jax.ShapeDtypeStruct((half,...  6.9 us
    unnamed x23, local copies, waits for them, and re-layouts  6.11 us
    pallas_call x1, Pallas kernels, place(): pl.pallas_call(functools.partial(place_kernel, spans, shifts, capacity),...  2.4 us
  transfers between devices with their start and end apart: 23, of which 10 were waited for; matrix products, arithmetic and copies ran while one was open for 0% of the time, Pallas kernels for 21%

profile of v12, /device:TPU:0, one launch (start us, length us, event | category | flops | bytes accessed | tf_op | source)
XLA Modules:
  0.0 109.4 jit_solution(12897230878538841098)
XLA Ops:
  1.2 2.4 %place_rows.1 = (bf16[128,1024]{1,0:T(8,128)(2,1)}, bf16[128,1024]{1,0:T(8,128)(2,1)}, bf16[128,1024]{1,0:T(8,128)(2,1)}) custom-call(s32[1,256]{1,0:T(1,128)} %bitcast.15, s32[1,256]{1,0:T(1,128)} %bitcast.18, f32[1,256]{1,0:T(1,128)} %bitcast.21, bf16[256,2048]{1,0:T(8,128)(2,1)} %refs_3_.1, bf16[256,2048]{1,0:T(8,128)(2,1)} %refs_4_.1), custom_call_target="tpu_custom_call" | custom-call | flops 1000 | bytes 1000 | tf_op jit(solution)/shard_map/place_rows/pallas_call | solution.py:90
  3.6 3.1 %collective-permute-start = (bf16[128,1024]{1,0:T(8,128)(2,1)}, bf16[128,1024]{1,0:T(8,128)(2,1)S(1)}, u32[]{:S(2)}, u32[]{:S(2)}) collective-permute-start(bf16[128,1024]{1,0:T(8,128)(2,1)} %get-tuple-element.33), channel_id=1, source_target_pairs={{0,2},{2,4},{4,6},{6,0},{1,3},{3,5},{5,7},{7,1},{8,10},{10,12},{12... | collective-permute-start | bytes 786440 | tf_op jit(solution)/shard_map/ppermute | solution.py:292
  6.7 2.1 %collective-permute-start.3 = (bf16[128,1024]{1,0:T(8,128)(2,1)}, bf16[128,1024]{1,0:T(8,128)(2,1)S(1)}, u32[]{:S(2)}, u32[]{:S(2)}) collective-permute-start(bf16[128,1024]{1,0:T(8,128)(2,1)} %get-tuple-element.36), channel_id=1, source_target_pairs={{0,6},{2,0},{4,2},{6,4},{1,7},{3,1},{5,3},{7,5},{8,14},{10,8},{12,... | collective-permute-start | bytes 786440 | tf_op jit(solution)/shard_map/ppermute | solution.py:292
  8.8 1.6 %copy-done.1 = bf16[1,1024,1024]{2,1,0:T(8,128)(2,1)S(1)} copy-done((bf16[1,1024,1024]{2,1,0:T(8,128)(2,1)S(1)}, bf16[1,1024,1024]{2,1,0:T(8,128)(2,1)}, u32[]{:S(2)}) %copy-start.1) | copy-done | bytes 2097176
  10.4 1.2 %copy-done.3 = bf16[256,2048]{1,0:T(8,128)(2,1)S(1)} copy-done((bf16[256,2048]{1,0:T(8,128)(2,1)S(1)}, bf16[256,2048]{1,0:T(8,128)(2,1)}, u32[]{:S(2)}) %copy-start.3) | copy-done | bytes 1048600
  11.6 1.2 %copy-done.4 = bf16[256,2048]{1,0:T(8,128)(2,1)S(1)} copy-done((bf16[256,2048]{1,0:T(8,128)(2,1)S(1)}, bf16[256,2048]{1,0:T(8,128)(2,1)}, u32[]{:S(2)}) %copy-start.4) | copy-done | bytes 1048600
  12.9 0.7 copy-done.5
  13.5 0.7 copy-done.7
  14.9 7.2 %expert_rows.3 = (bf16[4,512,1024]{2,1,0:T(8,128)(2,1)S(1)}, bf16[4,384,1024]{2,1,0:T(8,128)(2,1)S(1)}, bf16[384,512]{1,0:T(8,128)(2,1)S(1)}, bf16[384,512]{1,0:...) custom-call(s32[1,256]{1,0:T(1,128)S(1)} %bitcast.16, s32[1,256]{1,0:T(1,128)S(1)} %bitcast.19, ...), custom_call_target="tpu_custom_call" | custom-call | flops 1610612736 | bytes 10485760 | tf_op jit(solution)/shard_map/expert_rows/pallas_call | solution.py:199
  22.2 2.3 %collective-permute-start.6 = (bf16[256,1024]{1,0:T(8,128)(2,1)S(1)}, bf16[256,1024]{1,0:T(8,128)(2,1)S(1)}, u32[]{:S(2)}, u32[]{:S(2)}) collective-permute-start(bf16[256,1024]{1,0:T(8,128)(2,1)S(1)} %constant_dynamic-update-slice_fusion.refs_0_), channel_id=1, source_target_pairs={{0,16},{8,24},{16,0},{24,8},{1,17},{9,25},{17,1},{25,9},{2,18},{10... | collective-permute-start | bytes 1572872 | tf_op jit(solution)/shard_map/ppermute | solution.py:289
  24.5 1.5 %collective-permute-start.5 = (bf16[256,1024]{1,0:T(8,128)(2,1)S(1)}, bf16[256,1024]{1,0:T(8,128)(2,1)S(1)}, u32[]{:S(2)}, u32[]{:S(2)}) collective-permute-start(bf16[256,1024]{1,0:T(8,128)(2,1)S(1)} %constant_dynamic-update-slice_fusion.refs_0_), channel_id=1, source_target_pairs={{0,8},{8,0},{16,24},{24,16},{1,9},{9,1},{17,25},{25,17},{2,10},{10... | collective-permute-start | bytes 1572872 | tf_op jit(solution)/shard_map/ppermute | solution.py:289
  26.0 2.6 %collective-permute-start.4 = (bf16[128,1024]{1,0:T(8,128)(2,1)S(1)}, bf16[128,1024]{1,0:T(8,128)(2,1)S(1)}, u32[]{:S(2)}, u32[]{:S(2)}) collective-permute-start(bf16[128,1024]{1,0:T(8,128)(2,1)S(1)} %copy-done.10), channel_id=1, source_target_pairs={{0,4},{2,6},{4,0},{6,2},{1,5},{3,7},{5,1},{7,3},{8,12},{10,14},{12... | collective-permute-start | bytes 786440 | tf_op jit(solution)/shard_map/ppermute | solution.py:292
  28.6 11.7 %collective-permute-done.4.refs_0_ = bf16[128,1024]{1,0:T(8,128)(2,1)S(1)} collective-permute-done((bf16[128,1024]{1,0:T(8,128)(2,1)S(1)}, bf16[128,1024]{1,0:T(8,128)(2,1)S(1)}, u32[]{:S(2)}, u32[]{:S(2)}) %collective-permute-start.4) | collective-permute-done | bytes 262176 | tf_op jit(solution)/shard_map/ppermute | solution.py:292
  40.7 1.6 %collective-permute-start.8 = (bf16[128,1024]{1,0:T(8,128)(2,1)S(1)}, bf16[128,1024]{1,0:T(8,128)(2,1)S(1)}, u32[]{:S(2)}, u32[]{:S(2)}) collective-permute-start(bf16[128,1024]{1,0:T(8,128)(2,1)S(1)} %collective-permute-done.4.refs_0_), channel_id=1, source_target_pairs={{0,16},{8,24},{16,0},{24,8},{1,17},{9,25},{17,1},{25,9},{2,18},{10... | collective-permute-start | bytes 786440 | tf_op jit(solution)/shard_map/ppermute | solution.py:289
  42.3 1.5 %collective-permute-start.7 = (bf16[128,1024]{1,0:T(8,128)(2,1)S(1)}, bf16[128,1024]{1,0:T(8,128)(2,1)S(1)}, u32[]{:S(2)}, u32[]{:S(2)}) collective-permute-start(bf16[128,1024]{1,0:T(8,128)(2,1)S(1)} %collective-permute-done.4.refs_0_), channel_id=1, source_target_pairs={{0,8},{8,0},{16,24},{24,16},{1,9},{9,1},{17,25},{25,17},{2,10},{10... | collective-permute-start | bytes 786440 | tf_op jit(solution)/shard_map/ppermute | solution.py:289
  45.0 5.5 %collective-permute-done.9.refs_3_ = bf16[128,1024]{1,0:T(8,128)(2,1)S(1)} collective-permute-done((bf16[128,1024]{1,0:T(8,128)(2,1)S(1)}, bf16[128,1024]{1,0:T(8,128)(2,1)S(1)}, u32[]{:S(2)}, u32[]{:S(2)}) %collective-permute-start.9) | collective-permute-done | bytes 262176 | tf_op jit(solution)/shard_map/ppermute | solution.py:289
  50.5 3.7 %collective-permute-done.8.refs_2_ = bf16[128,1024]{1,0:T(8,128)(2,1)S(1)} collective-permute-done((bf16[128,1024]{1,0:T(8,128)(2,1)S(1)}, bf16[128,1024]{1,0:T(8,128)(2,1)S(1)}, u32[]{:S(2)}, u32[]{:S(2)}) %collective-permute-start.8) | collective-permute-done | bytes 262176 | tf_op jit(solution)/shard_map/ppermute | solution.py:289
  54.1 1.0 collective-permute-done.7.refs_1_
  55.1 3.6 %collective-permute-done.10.refs_3_ = bf16[256,512]{1,0:T(8,128)(2,1)S(1)} collective-permute-done((bf16[256,512]{1,0:T(8,128)(2,1)S(1)}, bf16[256,512]{1,0:T(8,128)(2,1)S(1)}, u32[]{:S(2)}, u32[]{:S(2)}) %collective-permute-start.10) | collective-permute-done | bytes 262176 | tf_op jit(solution)/shard_map/ppermute | solution.py:289
  58.9 7.3 %expert_rows.4 = (bf16[4,512,1024]{2,1,0:T(8,128)(2,1)S(1)}, bf16[4,384,1024]{2,1,0:T(8,128)(2,1)S(1)}, bf16[384,512]{1,0:T(8,128)(2,1)S(1)}, bf16[384,512]{1,0:...) custom-call(bf16[256,1024]{1,0:T(8,128)(2,1)S(1)} %constant_dynamic-, ...), custom_call_target="tpu_custom_call", output_to_operand_aliasing={{0}: (9, {}), {1}: (10, {}), {2}: (11, {}), {3}: (12, {}), ... | custom-call | flops 3221225472 | bytes 12582912 | tf_op jit(solution)/shard_map/expert_rows/pallas_call | solution.py:199
  66.3 1.2 %collective-permute-start.12 = (bf16[384,512]{1,0:T(8,128)(2,1)S(1)}, bf16[384,512]{1,0:T(8,128)(2,1)S(1)}, u32[]{:S(2)}, u32[]{:S(2)}) collective-permute-start(bf16[384,512]{1,0:T(8,128)(2,1)S(1)} %get-tuple-element.46), channel_id=1, source_target_pairs={{0,8},{8,0},{16,24},{24,16},{1,9},{9,1},{17,25},{25,17},{2,10},{10... | collective-permute-start | bytes 1179656 | tf_op jit(solution)/shard_map/ppermute | solution.py:289
  68.2 1.7 %collective-permute-start.14 = (bf16[384,512]{1,0:T(8,128)(2,1)S(1)}, bf16[384,512]{1,0:T(8,128)(2,1)S(1)}, u32[]{:S(2)}, u32[]{:S(2)}) collective-permute-start(bf16[384,512]{1,0:T(8,128)(2,1)S(1)} %get-tuple-element.48), channel_id=1, source_target_pairs={{0,24},{8,16},{16,8},{24,0},{1,25},{9,17},{17,9},{25,1},{2,26},{10... | collective-permute-start | bytes 1179656 | tf_op jit(solution)/shard_map/ppermute | solution.py:289
  69.9 6.8 %expert_rows.5 = (bf16[4,512,1024]{2,1,0:T(8,128)(2,1)S(1)}, bf16[4,128,1024]{2,1,0:T(8,128)(2,1)S(1)}, bf16[128,512]{1,0:T(8,128)(2,1)S(1)}, bf16[128,512]{1,0:...) custom-call(bf16[128,1024]{1,0:T(8,128)(2,1)S(1)} %collective-permut, ...), custom_call_target="tpu_custom_call", output_to_operand_aliasing={{0}: (8, {})} | custom-call | flops 1610612736 | bytes 10485760 | tf_op jit(solution)/shard_map/expert_rows/pallas_call | solution.py:199
  76.8 1.5 %collective-permute-done.12 = bf16[384,512]{1,0:T(8,128)(2,1)S(1)} collective-permute-done((bf16[384,512]{1,0:T(8,128)(2,1)S(1)}, bf16[384,512]{1,0:T(8,128)(2,1)S(1)}, u32[]{:S(2)}, u32[]{:S(2)}) %collective-permute-start.12) | collective-permute-done | bytes 393248 | tf_op jit(solution)/shard_map/ppermute | solution.py:289
  78.3 1.2 %collective-permute-start.19 = (bf16[128,512]{1,0:T(8,128)(2,1)S(1)}, bf16[128,512]{1,0:T(8,128)(2,1)S(1)}, u32[]{:S(2)}, u32[]{:S(2)}) collective-permute-start(bf16[128,512]{1,0:T(8,128)(2,1)S(1)} %get-tuple-element.56), channel_id=1, source_target_pairs={{0,24},{8,16},{16,8},{24,0},{1,25},{9,17},{17,9},{25,1},{2,26},{10... | collective-permute-start | bytes 393224 | tf_op jit(solution)/shard_map/ppermute | solution.py:289
  79.5 10.4 %collective-permute-done.13 = bf16[384,512]{1,0:T(8,128)(2,1)S(1)} collective-permute-done((bf16[384,512]{1,0:T(8,128)(2,1)S(1)}, bf16[384,512]{1,0:T(8,128)(2,1)S(1)}, u32[]{:S(2)}, u32[]{:S(2)}) %collective-permute-start.13) | collective-permute-done | bytes 393248 | tf_op jit(solution)/shard_map/ppermute | solution.py:289
  89.9 2.5 %collective-permute-start.17 = (bf16[128,512]{1,0:T(8,128)(2,1)S(1)}, bf16[128,512]{1,0:T(8,128)(2,1)S(1)}, u32[]{:S(2)}, u32[]{:S(2)}) collective-permute-start(bf16[128,512]{1,0:T(8,128)(2,1)S(1)} %get-tuple-element.52), channel_id=1, source_target_pairs={{0,8},{8,0},{16,24},{24,16},{1,9},{9,1},{17,25},{25,17},{2,10},{10... | collective-permute-start | bytes 393224 | tf_op jit(solution)/shard_map/ppermute | solution.py:289
  92.5 2.3 %collective-permute-done.18 = bf16[128,512]{1,0:T(8,128)(2,1)S(1)} collective-permute-done((bf16[128,512]{1,0:T(8,128)(2,1)S(1)}, bf16[128,512]{1,0:T(8,128)(2,1)S(1)}, u32[]{:S(2)}, u32[]{:S(2)}) %collective-permute-start.18) | collective-permute-done | bytes 131104 | tf_op jit(solution)/shard_map/ppermute | solution.py:289
  95.3 2.0 %collective-permute-start.20 = (bf16[128,512]{1,0:T(8,128)(2,1)S(1)}, bf16[128,512]{1,0:T(8,128)(2,1)S(1)}, u32[]{:S(2)}, u32[]{:S(2)}) collective-permute-start(bf16[128,512]{1,0:T(8,128)(2,1)S(1)} %add_convert_fusion.1), channel_id=1, source_target_pairs={{0,4},{2,6},{4,0},{6,2},{1,5},{3,7},{5,1},{7,3},{8,12},{10,14},{12... | collective-permute-start | bytes 393224 | tf_op jit(solution)/shard_map/ppermute | solution.py:292
  97.3 3.6 %collective-permute-start.16 = (bf16[128,512]{1,0:T(8,128)(2,1)S(1)}, bf16[128,512]{1,0:T(8,128)(2,1)S(1)}, u32[]{:S(2)}, u32[]{:S(2)}) collective-permute-start(bf16[128,512]{1,0:T(8,128)(2,1)S(1)} %get-tuple-element.63), channel_id=1, source_target_pairs={{0,2},{2,4},{4,6},{6,0},{1,3},{3,5},{5,7},{7,1},{8,10},{10,12},{12... | collective-permute-start | bytes 393224 | tf_op jit(solution)/shard_map/ppermute | solution.py:292
  101.3 6.9 %weight_grads.1 = (bf16[1024,1024]{1,0:T(8,128)(2,1)}, bf16[1024,1024]{1,0:T(8,128)(2,1)}) custom-call(bf16[4,512,1024]{2,1,0:T(8,128)(2,1)S(1)} %get-tuple-element.57.kept, bf16[4,384,1024]{2,1,0:T(8,128)(2,1)S(1)} %collective-permute-done.21.refs_0_, bf16[4,128,1024]{2,1,0:T(8,128)(2,1)S(1)} %collective-permute-done.22.refs_1_), custom_call_target="tpu_custom_call" | custom-call | flops 1000 | bytes 1000 | tf_op jit(solution)/shard_map/weight_grads/pallas_call | solution.py:265
  108.2 1.2 %unplace_rows.1 = bf16[256,512]{1,0:T(8,128)(2,1)} custom-call(s32[1,256]{1,0:T(1,128)S(1)} %bitcast.17, s32[1,256]{1,0:T(1,128)S(1)} %bitcast.20, bf16[128,512]{1,0:T(8,128)(2,1)S(1)} %get-tuple-element.65.refs_0_, bf16[128,512]{1,0:T(8,128)(2,1)S(1)} %collective-permute-done.15.refs_1_, bf16[128,512]{1,0:T(8,128)(2,1)S(1)} %collective-permute-done.16.refs_2_, ...), custom_call_target="tpu_custom_call" | custom-call | flops 1000 | bytes 1000 | tf_op jit(solution)/shard_map/unplace_rows/pallas_call | solution.py:234
  (49 shorter events, 5.0 us)
Async XLA Ops:
  0.6 8.2 %copy-start = (bf16[1,1024,1024]{2,1,0:T(8,128)(2,1)S(1)}, bf16[1,1024,1024]{2,1,0:T(8,128)(2,1)}, u32[]{:S(2)}) copy-start(bf16[1,1024,1024]{2,1,0:T(8,128)(2,1)} %param.12) | copy-start | bytes 6291460
  0.6 8.2 %collective-permute-start.1 = (bf16[1024,1024]{1,0:T(8,128)(2,1)}, bf16[1024,1024]{1,0:T(8,128)(2,1)S(1)}, u32[]{:S(2)}, u32[]{:S(2)}) collective-permute-start(bf16[1024,1024]{1,0:T(8,128)(2,1)} %bitcast.7), channel_id=1, source_target_pairs={{0,1},{1,0},{2,3},{3,2},{4,5},{5,4},{6,7},{7,6},{8,9},{9,8},{10,11... | collective-permute-start | bytes 6291464 | tf_op jit(solution)/shard_map/ppermute | solution.py:286
  1.2 7.7 %collective-permute-start.2 = (bf16[1024,1024]{1,0:T(8,128)(2,1)}, bf16[1024,1024]{1,0:T(8,128)(2,1)S(1)}, u32[]{:S(2)}, u32[]{:S(2)}) collective-permute-start(bf16[1024,1024]{1,0:T(8,128)(2,1)} %bitcast.11), channel_id=1, source_target_pairs={{0,1},{1,0},{2,3},{3,2},{4,5},{5,4},{6,7},{7,6},{8,9},{9,8},{10,11... | collective-permute-start | bytes 6291464 | tf_op jit(solution)/shard_map/ppermute | solution.py:286
  3.6 18.5 %collective-permute-start = (bf16[128,1024]{1,0:T(8,128)(2,1)}, bf16[128,1024]{1,0:T(8,128)(2,1)S(1)}, u32[]{:S(2)}, u32[]{:S(2)}) collective-permute-start(bf16[128,1024]{1,0:T(8,128)(2,1)} %get-tuple-element.33), channel_id=1, source_target_pairs={{0,2},{2,4},{4,6},{6,0},{1,3},{3,5},{5,7},{7,1},{8,10},{10,12},{12... | collective-permute-start | bytes 786440 | tf_op jit(solution)/shard_map/ppermute | solution.py:292
  6.7 15.5 %collective-permute-start.3 = (bf16[128,1024]{1,0:T(8,128)(2,1)}, bf16[128,1024]{1,0:T(8,128)(2,1)S(1)}, u32[]{:S(2)}, u32[]{:S(2)}) collective-permute-start(bf16[128,1024]{1,0:T(8,128)(2,1)} %get-tuple-element.36), channel_id=1, source_target_pairs={{0,6},{2,0},{4,2},{6,4},{1,7},{3,1},{5,3},{7,5},{8,14},{10,8},{12,... | collective-permute-start | bytes 786440 | tf_op jit(solution)/shard_map/ppermute | solution.py:292
  8.8 1.6 %copy-start.1 = (bf16[1,1024,1024]{2,1,0:T(8,128)(2,1)S(1)}, bf16[1,1024,1024]{2,1,0:T(8,128)(2,1)}, u32[]{:S(2)}) copy-start(bf16[1,1024,1024]{2,1,0:T(8,128)(2,1)} %param.13) | copy-start | bytes 6291460
  10.4 1.2 %copy-start.3 = (bf16[256,2048]{1,0:T(8,128)(2,1)S(1)}, bf16[256,2048]{1,0:T(8,128)(2,1)}, u32[]{:S(2)}) copy-start(bf16[256,2048]{1,0:T(8,128)(2,1)} %refs_3_.1) | copy-start | bytes 3145732
  11.6 1.2 %copy-start.4 = (bf16[256,2048]{1,0:T(8,128)(2,1)S(1)}, bf16[256,2048]{1,0:T(8,128)(2,1)}, u32[]{:S(2)}) copy-start(bf16[256,2048]{1,0:T(8,128)(2,1)} %refs_4_.1) | copy-start | bytes 3145732
  13.5 0.7 copy-start.7
  14.9 11.1 %copy-start.10 = (bf16[128,1024]{1,0:T(8,128)(2,1)S(1)}, bf16[128,1024]{1,0:T(8,128)(2,1)}, u32[]{:S(2)}) copy-start(bf16[128,1024]{1,0:T(8,128)(2,1)} %get-tuple-element.37) | copy-start | bytes 786436
  22.1 36.8 %copy-start.2 = (bf16[1,1024,1024]{2,1,0:T(8,128)(2,1)S(1)}, bf16[1,1024,1024]{2,1,0:T(8,128)(2,1)}, u32[]{:S(2)}) copy-start(bf16[1,1024,1024]{2,1,0:T(8,128)(2,1)} %param.13) | copy-start | bytes 6291460
  22.2 18.1 %collective-permute-start.6 = (bf16[256,1024]{1,0:T(8,128)(2,1)S(1)}, bf16[256,1024]{1,0:T(8,128)(2,1)S(1)}, u32[]{:S(2)}, u32[]{:S(2)}) collective-permute-start(bf16[256,1024]{1,0:T(8,128)(2,1)S(1)} %constant_dynamic-update-slice_fusion.refs_0_), channel_id=1, source_target_pairs={{0,16},{8,24},{16,0},{24,8},{1,17},{9,25},{17,1},{25,9},{2,18},{10... | collective-permute-start | bytes 1572872 | tf_op jit(solution)/shard_map/ppermute | solution.py:289
  24.5 15.8 %collective-permute-start.5 = (bf16[256,1024]{1,0:T(8,128)(2,1)S(1)}, bf16[256,1024]{1,0:T(8,128)(2,1)S(1)}, u32[]{:S(2)}, u32[]{:S(2)}) collective-permute-start(bf16[256,1024]{1,0:T(8,128)(2,1)S(1)} %constant_dynamic-update-slice_fusion.refs_0_), channel_id=1, source_target_pairs={{0,8},{8,0},{16,24},{24,16},{1,9},{9,1},{17,25},{25,17},{2,10},{10... | collective-permute-start | bytes 1572872 | tf_op jit(solution)/shard_map/ppermute | solution.py:289
  26.0 14.3 %collective-permute-start.4 = (bf16[128,1024]{1,0:T(8,128)(2,1)S(1)}, bf16[128,1024]{1,0:T(8,128)(2,1)S(1)}, u32[]{:S(2)}, u32[]{:S(2)}) collective-permute-start(bf16[128,1024]{1,0:T(8,128)(2,1)S(1)} %copy-done.10), channel_id=1, source_target_pairs={{0,4},{2,6},{4,0},{6,2},{1,5},{3,7},{5,1},{7,3},{8,12},{10,14},{12... | collective-permute-start | bytes 786440 | tf_op jit(solution)/shard_map/ppermute | solution.py:292
  40.3 10.1 %collective-permute-start.9 = (bf16[128,1024]{1,0:T(8,128)(2,1)S(1)}, bf16[128,1024]{1,0:T(8,128)(2,1)S(1)}, u32[]{:S(2)}, u32[]{:S(2)}) collective-permute-start(bf16[128,1024]{1,0:T(8,128)(2,1)S(1)} %collective-permute-done.4.refs_0_), channel_id=1, source_target_pairs={{0,24},{8,16},{16,8},{24,0},{1,25},{9,17},{17,9},{25,1},{2,26},{10... | collective-permute-start | bytes 786440 | tf_op jit(solution)/shard_map/ppermute | solution.py:289
  40.7 13.4 %collective-permute-start.8 = (bf16[128,1024]{1,0:T(8,128)(2,1)S(1)}, bf16[128,1024]{1,0:T(8,128)(2,1)S(1)}, u32[]{:S(2)}, u32[]{:S(2)}) collective-permute-start(bf16[128,1024]{1,0:T(8,128)(2,1)S(1)} %collective-permute-done.4.refs_0_), channel_id=1, source_target_pairs={{0,16},{8,24},{16,0},{24,8},{1,17},{9,25},{17,1},{25,9},{2,18},{10... | collective-permute-start | bytes 786440 | tf_op jit(solution)/shard_map/ppermute | solution.py:289
  42.3 12.8 %collective-permute-start.7 = (bf16[128,1024]{1,0:T(8,128)(2,1)S(1)}, bf16[128,1024]{1,0:T(8,128)(2,1)S(1)}, u32[]{:S(2)}, u32[]{:S(2)}) collective-permute-start(bf16[128,1024]{1,0:T(8,128)(2,1)S(1)} %collective-permute-done.4.refs_0_), channel_id=1, source_target_pairs={{0,8},{8,0},{16,24},{24,16},{1,9},{9,1},{17,25},{25,17},{2,10},{10... | collective-permute-start | bytes 786440 | tf_op jit(solution)/shard_map/ppermute | solution.py:289
  43.8 14.9 %collective-permute-start.10 = (bf16[256,512]{1,0:T(8,128)(2,1)S(1)}, bf16[256,512]{1,0:T(8,128)(2,1)S(1)}, u32[]{:S(2)}, u32[]{:S(2)}) collective-permute-start(bf16[256,512]{1,0:T(8,128)(2,1)S(1)} %slice.20), channel_id=1, source_target_pairs={{0,8},{8,0},{16,24},{24,16},{1,9},{9,1},{17,25},{25,17},{2,10},{10... | collective-permute-start | bytes 786440 | tf_op jit(solution)/shard_map/ppermute | solution.py:289
  44.4 14.5 %collective-permute-start.11 = (bf16[256,512]{1,0:T(8,128)(2,1)S(1)}, bf16[256,512]{1,0:T(8,128)(2,1)S(1)}, u32[]{:S(2)}, u32[]{:S(2)}) collective-permute-start(bf16[256,512]{1,0:T(8,128)(2,1)S(1)} %slice.21), channel_id=1, source_target_pairs={{0,16},{8,24},{16,0},{24,8},{1,17},{9,25},{17,1},{25,9},{2,18},{10... | collective-permute-start | bytes 786440 | tf_op jit(solution)/shard_map/ppermute | solution.py:289
  66.2 35.0 %collective-permute-start.21 = (bf16[4,384,1024]{2,1,0:T(8,128)(2,1)S(1)}, bf16[4,384,1024]{2,1,0:T(8,128)(2,1)S(1)}, u32[]{:S(2)}, u32[]{:S(2)}) collective-permute-start(bf16[4,384,1024]{2,1,0:T(8,128)(2,1)S(1)} %get-tuple-element.58), channel_id=1, source_target_pairs={{0,1},{1,0},{2,3},{3,2},{4,5},{5,4},{6,7},{7,6},{8,9},{9,8},{10,11... | collective-permute-start | bytes 9437192 | tf_op jit(solution)/shard_map/ppermute | solution.py:286
  66.3 12.0 %collective-permute-start.12 = (bf16[384,512]{1,0:T(8,128)(2,1)S(1)}, bf16[384,512]{1,0:T(8,128)(2,1)S(1)}, u32[]{:S(2)}, u32[]{:S(2)}) collective-permute-start(bf16[384,512]{1,0:T(8,128)(2,1)S(1)} %get-tuple-element.46), channel_id=1, source_target_pairs={{0,8},{8,0},{16,24},{24,16},{1,9},{9,1},{17,25},{25,17},{2,10},{10... | collective-permute-start | bytes 1179656 | tf_op jit(solution)/shard_map/ppermute | solution.py:289
  67.6 22.3 %collective-permute-start.13 = (bf16[384,512]{1,0:T(8,128)(2,1)S(1)}, bf16[384,512]{1,0:T(8,128)(2,1)S(1)}, u32[]{:S(2)}, u32[]{:S(2)}) collective-permute-start(bf16[384,512]{1,0:T(8,128)(2,1)S(1)} %get-tuple-element.47), channel_id=1, source_target_pairs={{0,16},{8,24},{16,0},{24,8},{1,17},{9,25},{17,1},{25,9},{2,18},{10... | collective-permute-start | bytes 1179656 | tf_op jit(solution)/shard_map/ppermute | solution.py:289
  68.2 21.7 %collective-permute-start.14 = (bf16[384,512]{1,0:T(8,128)(2,1)S(1)}, bf16[384,512]{1,0:T(8,128)(2,1)S(1)}, u32[]{:S(2)}, u32[]{:S(2)}) collective-permute-start(bf16[384,512]{1,0:T(8,128)(2,1)S(1)} %get-tuple-element.48), channel_id=1, source_target_pairs={{0,24},{8,16},{16,8},{24,0},{1,25},{9,17},{17,9},{25,1},{2,26},{10... | collective-permute-start | bytes 1179656 | tf_op jit(solution)/shard_map/ppermute | solution.py:289
  76.7 24.6 %collective-permute-start.22 = (bf16[4,128,1024]{2,1,0:T(8,128)(2,1)S(1)}, bf16[4,128,1024]{2,1,0:T(8,128)(2,1)S(1)}, u32[]{:S(2)}, u32[]{:S(2)}) collective-permute-start(bf16[4,128,1024]{2,1,0:T(8,128)(2,1)S(1)} %get-tuple-element.59), channel_id=1, source_target_pairs={{0,1},{1,0},{2,3},{3,2},{4,5},{5,4},{6,7},{7,6},{8,9},{9,8},{10,11... | collective-permute-start | bytes 3145736 | tf_op jit(solution)/shard_map/ppermute | solution.py:286
  78.3 14.2 %collective-permute-start.19 = (bf16[128,512]{1,0:T(8,128)(2,1)S(1)}, bf16[128,512]{1,0:T(8,128)(2,1)S(1)}, u32[]{:S(2)}, u32[]{:S(2)}) collective-permute-start(bf16[128,512]{1,0:T(8,128)(2,1)S(1)} %get-tuple-element.56), channel_id=1, source_target_pairs={{0,24},{8,16},{16,8},{24,0},{1,25},{9,17},{17,9},{25,1},{2,26},{10... | collective-permute-start | bytes 393224 | tf_op jit(solution)/shard_map/ppermute | solution.py:289
  89.9 5.0 %collective-permute-start.18 = (bf16[128,512]{1,0:T(8,128)(2,1)S(1)}, bf16[128,512]{1,0:T(8,128)(2,1)S(1)}, u32[]{:S(2)}, u32[]{:S(2)}) collective-permute-start(bf16[128,512]{1,0:T(8,128)(2,1)S(1)} %get-tuple-element.54), channel_id=1, source_target_pairs={{0,16},{8,24},{16,0},{24,8},{1,17},{9,25},{17,1},{25,9},{2,18},{10... | collective-permute-start | bytes 393224 | tf_op jit(solution)/shard_map/ppermute | solution.py:289
  89.9 5.4 %collective-permute-start.17 = (bf16[128,512]{1,0:T(8,128)(2,1)S(1)}, bf16[128,512]{1,0:T(8,128)(2,1)S(1)}, u32[]{:S(2)}, u32[]{:S(2)}) collective-permute-start(bf16[128,512]{1,0:T(8,128)(2,1)S(1)} %get-tuple-element.52), channel_id=1, source_target_pairs={{0,8},{8,0},{16,24},{24,16},{1,9},{9,1},{17,25},{25,17},{2,10},{10... | collective-permute-start | bytes 393224 | tf_op jit(solution)/shard_map/ppermute | solution.py:289
  95.3 12.8 %collective-permute-start.20 = (bf16[128,512]{1,0:T(8,128)(2,1)S(1)}, bf16[128,512]{1,0:T(8,128)(2,1)S(1)}, u32[]{:S(2)}, u32[]{:S(2)}) collective-permute-start(bf16[128,512]{1,0:T(8,128)(2,1)S(1)} %add_convert_fusion.1), channel_id=1, source_target_pairs={{0,4},{2,6},{4,0},{6,2},{1,5},{3,7},{5,1},{7,3},{8,12},{10,14},{12... | collective-permute-start | bytes 393224 | tf_op jit(solution)/shard_map/ppermute | solution.py:292
  97.3 10.8 %collective-permute-start.16 = (bf16[128,512]{1,0:T(8,128)(2,1)S(1)}, bf16[128,512]{1,0:T(8,128)(2,1)S(1)}, u32[]{:S(2)}, u32[]{:S(2)}) collective-permute-start(bf16[128,512]{1,0:T(8,128)(2,1)S(1)} %get-tuple-element.63), channel_id=1, source_target_pairs={{0,2},{2,4},{4,6},{6,0},{1,3},{3,5},{5,7},{7,1},{8,10},{10,12},{12... | collective-permute-start | bytes 393224 | tf_op jit(solution)/shard_map/ppermute | solution.py:292
  101.0 7.2 %collective-permute-start.15 = (bf16[128,512]{1,0:T(8,128)(2,1)S(1)}, bf16[128,512]{1,0:T(8,128)(2,1)S(1)}, u32[]{:S(2)}, u32[]{:S(2)}) collective-permute-start(bf16[128,512]{1,0:T(8,128)(2,1)S(1)} %get-tuple-element.64), channel_id=1, source_target_pairs={{0,6},{2,0},{4,2},{6,4},{1,7},{3,1},{5,3},{7,5},{8,14},{10,8},{12,... | collective-permute-start | bytes 393224 | tf_op jit(solution)/shard_map/ppermute | solution.py:292
  101.2 7.0 %copy-start.6 = (s32[256,1]{0,1:T(1,128)S(1)}, s32[256,1]{0,1:T(1,128)}, u32[]{:S(2)}) copy-start(s32[256,1]{0,1:T(1,128)} %param.10) | copy-start | bytes 3076
  101.2 7.0 %copy-start.8 = (s32[256,1]{0,1:T(1,128)S(1)}, s32[256,1]{0,1:T(1,128)}, u32[]{:S(2)}) copy-start(s32[256,1]{0,1:T(1,128)} %param.11) | copy-start | bytes 3076
  (2 other events, 1.4 us)

commit v13 on v9

--- a/solution.py
+++ b/solution.py
@@ -327,10 +327,9 @@
         own = [index, slot, gate, tokens, grad_output]
         kept, (pair,) = expert_rows(own, None, [(capacity, 1)], weights, everything, 0, None)
         near = spread(jnp.concatenate([after(moved[0], pair[0]), moved[1]], 0))
-        far = spread(after(moved[2], *near[1:3]))
-        near[0] = after(near[0], *far[1:3])
         back, got_own = collect_pair([pair[0], after(pair[1], *near[3:])], 1)
         kept, (blocks,) = expert_rows(near, 0, [(2 * capacity, None)], weights, everything, capacity, kept)
+        far = spread(after(moved[2], *near[1:3]), blocks[0])
         total, got = collect(blocks)
         backs = [back, shift(total[:capacity], -1), shift(total[capacity:], -3)]
         slots = [after(far[0], got_own)] + far[1:]

time: 97.2 us -> 97.6 us (level)
  starting transfers between devices: 34.4 us -> 35.7 us
    ppermute x6, starting transfers between devices: 13.1 us -> 15.2 us  [shift(): lax.ppermute(x, 'expert', [(i, (i + k) % experts) for i in range(experts)])]
    ppermute x16, waiting for transfers between devices: 21.9 us -> 20.8 us  [across(): return lax.ppermute(x, 'tensor', [(i, i ^ j) for i in range(tensor_size)])]
  transfers between devices with their start and end apart: 25 -> 25, of which waited for: 10 -> 9; matrix products, arithmetic and copies ran while one was open for 3% -> 3% of each run, Pallas kernels for 28% -> 28%
where the time goes in v13:
time: 97.6 us; the launch traced here: 97.4 us
  starting transfers between devices  35.7 us (37%)
  Pallas kernels  28.2 us (29%)
  waiting for transfers between devices  25.8 us (26%)
  local copies, waits for them, and re-layouts  4.17 us (4%)
  matrix products  2.39 us (2%)
    ppermute x16, waiting for transfers between devices, across(): return lax.ppermute(x, 'tensor', [(i, i ^ j) for i in range(tensor_size)])  20.8 us
    pallas_call x3, Pallas kernels, expert_rows(): pl.pallas_call(functools.partial(expert_kernel, first, base, groups, len(...  20.7 us
    ppermute x16, starting transfers between devices, across(): return lax.ppermute(x, 'tensor', [(i, i ^ j) for i in range(tensor_size)])  19.9 us
    ppermute x6, starting transfers between devices, shift(): lax.ppermute(x, 'expert', [(i, (i + k) % experts) for i in range(experts)])  15.2 us
    ppermute x6, waiting for transfers between devices, shift(): lax.ppermute(x, 'expert', [(i, (i + k) % experts) for i in range(experts)])  5.01 us
    unnamed x19, local copies, waits for them, and re-layouts  4.08 us
    pallas_call x1, Pallas kernels, weight_grads(): pl.pallas_call(weight_grad_kernel, out_shape=[jax.ShapeDtypeStruct((half,...  3.86 us
    pallas_call x1, Pallas kernels, place(): pl.pallas_call(functools.partial(place_kernel, spans, shifts, capacity),...  2.41 us
  transfers between devices with their start and end apart: 25, of which 9 were waited for; matrix products, arithmetic and copies ran while one was open for 3% of the time, Pallas kernels for 28%

profile of v13, /device:TPU:0, one launch (start us, length us, event | category | flops | bytes accessed | tf_op | source)
XLA Modules:
  0.0 97.4 jit_solution(18175144412038673681)
XLA Ops:
  1.3 2.4 %place_rows.1 = (bf16[128,1024]{1,0:T(8,128)(2,1)}, bf16[128,1024]{1,0:T(8,128)(2,1)}, bf16[128,1024]{1,0:T(8,128)(2,1)}) custom-call(s32[1,256]{1,0:T(1,128)} %bitcast.22, s32[1,256]{1,0:T(1,128)} %bitcast.25, f32[1,256]{1,0:T(1,128)} %bitcast.28, bf16[256,2048]{1,0:T(8,128)(2,1)} %tokens.1, bf16[256,2048]{1,0:T(8,128)(2,1)} %grad_output.1), custom_call_target="tpu_custom_call" | custom-call | flops 1000 | bytes 1000 | tf_op jit(solution)/shard_map/place_rows/pallas_call | solution.py:90
  3.7 3.1 %collective-permute-start.2 = (bf16[128,1024]{1,0:T(8,128)(2,1)}, bf16[128,1024]{1,0:T(8,128)(2,1)S(1)}, u32[]{:S(2)}, u32[]{:S(2)}) collective-permute-start(bf16[128,1024]{1,0:T(8,128)(2,1)} %get-tuple-element.37), channel_id=1, source_target_pairs={{0,2},{2,4},{4,6},{6,0},{1,3},{3,5},{5,7},{7,1},{8,10},{10,12},{12... | collective-permute-start | bytes 786440 | tf_op jit(solution)/shard_map/ppermute | solution.py:289
  6.8 2.1 %collective-permute-start.3 = (bf16[128,1024]{1,0:T(8,128)(2,1)}, bf16[128,1024]{1,0:T(8,128)(2,1)S(1)}, u32[]{:S(2)}, u32[]{:S(2)}) collective-permute-start(bf16[128,1024]{1,0:T(8,128)(2,1)} %get-tuple-element.39), channel_id=1, source_target_pairs={{0,6},{2,0},{4,2},{6,4},{1,7},{3,1},{5,3},{7,5},{8,14},{10,8},{12,... | collective-permute-start | bytes 786440 | tf_op jit(solution)/shard_map/ppermute | solution.py:289
  8.9 1.6 %copy-done.1 = bf16[1,1024,1024]{2,1,0:T(8,128)(2,1)S(1)} copy-done((bf16[1,1024,1024]{2,1,0:T(8,128)(2,1)S(1)}, bf16[1,1024,1024]{2,1,0:T(8,128)(2,1)}, u32[]{:S(2)}) %copy-start.1) | copy-done | bytes 2097176
  10.5 1.2 %copy-done.3 = bf16[256,2048]{1,0:T(8,128)(2,1)S(1)} copy-done((bf16[256,2048]{1,0:T(8,128)(2,1)S(1)}, bf16[256,2048]{1,0:T(8,128)(2,1)}, u32[]{:S(2)}) %copy-start.3) | copy-done | bytes 1048600
  11.7 1.2 %copy-done.4 = bf16[256,2048]{1,0:T(8,128)(2,1)S(1)} copy-done((bf16[256,2048]{1,0:T(8,128)(2,1)S(1)}, bf16[256,2048]{1,0:T(8,128)(2,1)}, u32[]{:S(2)}) %copy-start.4) | copy-done | bytes 1048600
  12.9 7.0 %expert_rows.3 = (bf16[2,512,2048]{2,1,0:T(8,128)(2,1)S(1)}, bf16[2,512,1024]{2,1,0:T(8,128)(2,1)S(1)}, bf16[2,128,512]{2,1,0:T(8,128)(2,1)S(1)}, bf16[2,128,512]{2,1,0:T(8,128)(2,1)S(1)}) custom-call(s32[1,256]{1,0:T(1,128)S(1)} %bitcast.23, s32[1,256]{1,0:T(1,128)S(1)} %bitcast.26, f32[1,256]{1,0:T(1,128)S(1)} %bitcast.29, ...), custom_call_target="tpu_custom_call" | custom-call | flops 1610612736 | bytes 10485760 | tf_op jit(solution)/shard_map/expert_rows/pallas_call | solution.py:194
  20.6 1.8 %collective-permute-start.4 = (bf16[256,1024]{1,0:T(8,128)(2,1)S(1)}, bf16[256,1024]{1,0:T(8,128)(2,1)S(1)}, u32[]{:S(2)}, u32[]{:S(2)}) collective-permute-start(bf16[256,1024]{1,0:T(8,128)(2,1)S(1)} %constant_dynamic-update-slice_fusion.refs_0_), channel_id=1, source_target_pairs={{0,16},{8,24},{16,0},{24,8},{1,17},{9,25},{17,1},{25,9},{2,18},{10... | collective-permute-start | bytes 1572872 | tf_op jit(solution)/shard_map/ppermute | solution.py:286
  22.3 1.5 %collective-permute-start.6 = (bf16[256,1024]{1,0:T(8,128)(2,1)S(1)}, bf16[256,1024]{1,0:T(8,128)(2,1)S(1)}, u32[]{:S(2)}, u32[]{:S(2)}) collective-permute-start(bf16[256,1024]{1,0:T(8,128)(2,1)S(1)} %constant_dynamic-update-slice_fusion.refs_0_), channel_id=1, source_target_pairs={{0,8},{8,0},{16,24},{24,16},{1,9},{9,1},{17,25},{25,17},{2,10},{10... | collective-permute-start | bytes 1572872 | tf_op jit(solution)/shard_map/ppermute | solution.py:286
  23.8 2.6 %collective-permute-start.15 = (bf16[128,1024]{1,0:T(8,128)(2,1)S(1)}, bf16[128,1024]{1,0:T(8,128)(2,1)S(1)}, u32[]{:S(2)}, u32[]{:S(2)}) collective-permute-start(bf16[128,1024]{1,0:T(8,128)(2,1)S(1)} %copy-done.8), channel_id=1, source_target_pairs={{0,4},{2,6},{4,0},{6,2},{1,5},{3,7},{5,1},{7,3},{8,12},{10,14},{12... | collective-permute-start | bytes 786440 | tf_op jit(solution)/shard_map/ppermute | solution.py:289
  26.4 8.1 %collective-permute-done.4.refs_2_ = bf16[256,1024]{1,0:T(8,128)(2,1)S(1)} collective-permute-done((bf16[256,1024]{1,0:T(8,128)(2,1)S(1)}, bf16[256,1024]{1,0:T(8,128)(2,1)S(1)}, u32[]{:S(2)}, u32[]{:S(2)}) %collective-permute-start.4) | collective-permute-done | bytes 524320 | tf_op jit(solution)/shard_map/ppermute | solution.py:286
  34.6 1.8 %collective-permute-start.5 = (bf16[256,512]{1,0:T(8,128)(2,1)S(1)}, bf16[256,512]{1,0:T(8,128)(2,1)S(1)}, u32[]{:S(2)}, u32[]{:S(2)}) collective-permute-start(bf16[256,512]{1,0:T(8,128)(2,1)S(1)} %slice.44), channel_id=1, source_target_pairs={{0,8},{8,0},{16,24},{24,16},{1,9},{9,1},{17,25},{25,17},{2,10},{10... | collective-permute-start | bytes 786440 | tf_op jit(solution)/shard_map/ppermute | solution.py:286
  36.4 1.6 %collective-permute-start.7 = (bf16[256,512]{1,0:T(8,128)(2,1)S(1)}, bf16[256,512]{1,0:T(8,128)(2,1)S(1)}, u32[]{:S(2)}, u32[]{:S(2)}) collective-permute-start(bf16[256,512]{1,0:T(8,128)(2,1)S(1)} %slice.45), channel_id=1, source_target_pairs={{0,16},{8,24},{16,0},{24,8},{1,17},{9,25},{17,1},{25,9},{2,18},{10... | collective-permute-start | bytes 786440 | tf_op jit(solution)/shard_map/ppermute | solution.py:286
  39.6 4.3 %collective-permute-done.5.refs_3_ = bf16[256,512]{1,0:T(8,128)(2,1)S(1)} collective-permute-done((bf16[256,512]{1,0:T(8,128)(2,1)S(1)}, bf16[256,512]{1,0:T(8,128)(2,1)S(1)}, u32[]{:S(2)}, u32[]{:S(2)}) %collective-permute-start.5) | collective-permute-done | bytes 262176 | tf_op jit(solution)/shard_map/ppermute | solution.py:286
  43.9 1.8 %collective-permute-done.7.refs_4_ = bf16[256,512]{1,0:T(8,128)(2,1)S(1)} collective-permute-done((bf16[256,512]{1,0:T(8,128)(2,1)S(1)}, bf16[256,512]{1,0:T(8,128)(2,1)S(1)}, u32[]{:S(2)}, u32[]{:S(2)}) %collective-permute-start.7) | collective-permute-done | bytes 262176 | tf_op jit(solution)/shard_map/ppermute | solution.py:286
  45.7 1.1 %collective-permute-start.8 = (bf16[2,128,512]{2,1,0:T(8,128)(2,1)S(1)}, bf16[2,128,512]{2,1,0:T(8,128)(2,1)S(1)}, u32[]{:S(2)}, u32[]{:S(2)}) collective-permute-start(bf16[2,128,512]{2,1,0:T(8,128)(2,1)S(1)} %get-tuple-element.40), channel_id=1, source_target_pairs={{0,8},{8,0},{16,24},{24,16},{1,9},{9,1},{17,25},{25,17},{2,10},{10... | collective-permute-start | bytes 786440 | tf_op jit(solution)/shard_map/ppermute | solution.py:286
  46.8 7.1 %expert_rows.4 = (bf16[2,512,2048]{2,1,0:T(8,128)(2,1)S(1)}, bf16[2,512,1024]{2,1,0:T(8,128)(2,1)S(1)}, bf16[256,512]{1,0:T(8,128)(2,1)S(1)}, bf16[256,512]{1,0:...) custom-call(bf16[256,1024]{1,0:T(8,128)(2,1)S(1)} %constant_dynamic-, ...), custom_call_target="tpu_custom_call", output_to_operand_aliasing={{0}: (9, {}), {1}: (10, {})} | custom-call | flops 3221225472 | bytes 12582912 | tf_op jit(solution)/shard_map/expert_rows/pallas_call | solution.py:194
  54.9 1.6 %collective-permute-start.19 = (bf16[128,512]{1,0:T(8,128)(2,1)S(1)}, bf16[128,512]{1,0:T(8,128)(2,1)S(1)}, u32[]{:S(2)}, u32[]{:S(2)}) collective-permute-start(bf16[128,512]{1,0:T(8,128)(2,1)S(1)} %slice.51), channel_id=1, source_target_pairs={{0,16},{8,24},{16,0},{24,8},{1,17},{9,25},{17,1},{25,9},{2,18},{10... | collective-permute-start | bytes 393224 | tf_op jit(solution)/shard_map/ppermute | solution.py:286
  58.5 1.5 %collective-permute-start.10 = (bf16[256,512]{1,0:T(8,128)(2,1)S(1)}, bf16[256,512]{1,0:T(8,128)(2,1)S(1)}, u32[]{:S(2)}, u32[]{:S(2)}) collective-permute-start(bf16[256,512]{1,0:T(8,128)(2,1)S(1)} %get-tuple-element.44), channel_id=1, source_target_pairs={{0,8},{8,0},{16,24},{24,16},{1,9},{9,1},{17,25},{25,17},{2,10},{10... | collective-permute-start | bytes 786440 | tf_op jit(solution)/shard_map/ppermute | solution.py:286
  60.4 2.4 %collective-permute-done.19.refs_4_ = bf16[128,512]{1,0:T(8,128)(2,1)S(1)} collective-permute-done((bf16[128,512]{1,0:T(8,128)(2,1)S(1)}, bf16[128,512]{1,0:T(8,128)(2,1)S(1)}, u32[]{:S(2)}, u32[]{:S(2)}) %collective-permute-start.19) | collective-permute-done | bytes 131104 | tf_op jit(solution)/shard_map/ppermute | solution.py:286
  62.9 6.6 %expert_rows.5 = (bf16[2,512,2048]{2,1,0:T(8,128)(2,1)S(1)}, bf16[2,512,1024]{2,1,0:T(8,128)(2,1)S(1)}, bf16[128,512]{1,0:T(8,128)(2,1)S(1)}, bf16[128,512]{1,0:...) custom-call(bf16[128,1024]{1,0:T(8,128)(2,1)S(1)} %collective-permut, ...), custom_call_target="tpu_custom_call", output_to_operand_aliasing={{0}: (9, {}), {1}: (10, {})} | custom-call | flops 1610612736 | bytes 10485760 | tf_op jit(solution)/shard_map/expert_rows/pallas_call | solution.py:194
  69.5 2.4 %convolution_convert_fusion = bf16[2,1024,1024]{2,1,0:T(8,128)(2,1)S(1)} fusion(bf16[2,512,1024]{2,1,0:T(8,128)(2,1)S(1)} %get-tuple-element.57.acts, bf16[2,512,2048]{2,1,0:T(8,128)(2,1)S(1)} %get-tuple-element.56.rows), kind=kOutput, calls=%fused_computation | convolution fusion | flops 2149580800 | bytes 8388608 | tf_op jit(solution)/shard_map/dot_general | solution.py:315
  72.0 1.1 %collective-permute-start.9 = (bf16[128,512]{1,0:T(8,128)(2,1)S(1)}, bf16[128,512]{1,0:T(8,128)(2,1)S(1)}, u32[]{:S(2)}, u32[]{:S(2)}) collective-permute-start(bf16[128,512]{1,0:T(8,128)(2,1)S(1)} %fusion.2), channel_id=1, source_target_pairs={{0,16},{8,24},{16,0},{24,8},{1,17},{9,25},{17,1},{25,9},{2,18},{10... | collective-permute-start | bytes 393224 | tf_op jit(solution)/shard_map/ppermute | solution.py:286
  73.1 1.3 %collective-permute-start.22 = (bf16[128,512]{1,0:T(8,128)(2,1)S(1)}, bf16[128,512]{1,0:T(8,128)(2,1)S(1)}, u32[]{:S(2)}, u32[]{:S(2)}) collective-permute-start(bf16[128,512]{1,0:T(8,128)(2,1)S(1)} %get-tuple-element.62), channel_id=1, source_target_pairs={{0,24},{8,16},{16,8},{24,0},{1,25},{9,17},{17,9},{25,1},{2,26},{10... | collective-permute-start | bytes 393224 | tf_op jit(solution)/shard_map/ppermute | solution.py:286
  74.4 1.4 %collective-permute-start.21 = (bf16[128,512]{1,0:T(8,128)(2,1)S(1)}, bf16[128,512]{1,0:T(8,128)(2,1)S(1)}, u32[]{:S(2)}, u32[]{:S(2)}) collective-permute-start(bf16[128,512]{1,0:T(8,128)(2,1)S(1)} %get-tuple-element.60), channel_id=1, source_target_pairs={{0,16},{8,24},{16,0},{24,8},{1,17},{9,25},{17,1},{25,9},{2,18},{10... | collective-permute-start | bytes 393224 | tf_op jit(solution)/shard_map/ppermute | solution.py:286
  76.8 3.6 %collective-permute-done.22 = bf16[128,512]{1,0:T(8,128)(2,1)S(1)} collective-permute-done((bf16[128,512]{1,0:T(8,128)(2,1)S(1)}, bf16[128,512]{1,0:T(8,128)(2,1)S(1)}, u32[]{:S(2)}, u32[]{:S(2)}) %collective-permute-start.22) | collective-permute-done | bytes 131104 | tf_op jit(solution)/shard_map/ppermute | solution.py:286
  80.4 3.6 %collective-permute-start.13 = (bf16[128,512]{1,0:T(8,128)(2,1)S(1)}, bf16[128,512]{1,0:T(8,128)(2,1)S(1)}, u32[]{:S(2)}, u32[]{:S(2)}) collective-permute-start(bf16[128,512]{1,0:T(8,128)(2,1)S(1)} %get-tuple-element.68), channel_id=1, source_target_pairs={{0,6},{2,0},{4,2},{6,4},{1,7},{3,1},{5,3},{7,5},{8,14},{10,8},{12,... | collective-permute-start | bytes 393224 | tf_op jit(solution)/shard_map/ppermute | solution.py:289
  84.1 1.2 %collective-permute-start.14 = (bf16[128,512]{1,0:T(8,128)(2,1)S(1)}, bf16[128,512]{1,0:T(8,128)(2,1)S(1)}, u32[]{:S(2)}, u32[]{:S(2)}) collective-permute-start(bf16[128,512]{1,0:T(8,128)(2,1)S(1)} %get-tuple-element.67), channel_id=1, source_target_pairs={{0,2},{2,4},{4,6},{6,0},{1,3},{3,5},{5,7},{7,1},{8,10},{10,12},{12... | collective-permute-start | bytes 393224 | tf_op jit(solution)/shard_map/ppermute | solution.py:289
  85.3 2.6 %collective-permute-start.23 = (bf16[128,512]{1,0:T(8,128)(2,1)S(1)}, bf16[128,512]{1,0:T(8,128)(2,1)S(1)}, u32[]{:S(2)}, u32[]{:S(2)}) collective-permute-start(bf16[128,512]{1,0:T(8,128)(2,1)S(1)} %add_convert_fusion.1), channel_id=1, source_target_pairs={{0,4},{2,6},{4,0},{6,2},{1,5},{3,7},{5,1},{7,3},{8,12},{10,14},{12... | collective-permute-start | bytes 393224 | tf_op jit(solution)/shard_map/ppermute | solution.py:289
  88.0 3.9 %weight_grads.1 = (bf16[1024,1024]{1,0:T(8,128)(2,1)}, bf16[1024,1024]{1,0:T(8,128)(2,1)}) custom-call(bf16[2,512,2048]{2,1,0:T(8,128)(2,1)S(1)} %get-tuple-element.56.rows, bf16[2,512,1024]{2,1,0:T(8,128)(2,1)S(1)} %get-tuple-element.57.acts, bf16[2,1024,1024]{2,1,0:T(8,128)(2,1)S(1)} %collective-permute-done.24.got), custom_call_target="tpu_custom_call" | custom-call | flops 1000 | bytes 1000 | tf_op jit(solution)/shard_map/weight_grads/pallas_call | solution.py:258
  91.8 4.3 %collective-permute-done.23.refs_3_ = bf16[128,512]{1,0:T(8,128)(2,1)S(1)} collective-permute-done((bf16[128,512]{1,0:T(8,128)(2,1)S(1)}, bf16[128,512]{1,0:T(8,128)(2,1)S(1)}, u32[]{:S(2)}, u32[]{:S(2)}) %collective-permute-start.23) | collective-permute-done | bytes 131104 | tf_op jit(solution)/shard_map/ppermute | solution.py:289
  96.2 1.2 %unplace_rows.1 = bf16[256,512]{1,0:T(8,128)(2,1)} custom-call(s32[1,256]{1,0:T(1,128)S(1)} %bitcast.24, s32[1,256]{1,0:T(1,128)S(1)} %bitcast.27, bf16[128,512]{1,0:T(8,128)(2,1)S(1)} %fusion.1.refs_0_, bf16[128,512]{1,0:T(8,128)(2,1)S(1)} %collective-permute-done.13.refs_1_, bf16[128,512]{1,0:T(8,128)(2,1)S(1)} %collective-permute-done.14.refs_2_, ...), custom_call_target="tpu_custom_call" | custom-call | flops 1000 | bytes 1000 | tf_op jit(solution)/shard_map/unplace_rows/pallas_call | solution.py:230
  (54 shorter events, 7.5 us)
Async XLA Ops:
  0.6 8.2 %copy-start = (bf16[1,1024,1024]{2,1,0:T(8,128)(2,1)S(1)}, bf16[1,1024,1024]{2,1,0:T(8,128)(2,1)}, u32[]{:S(2)}) copy-start(bf16[1,1024,1024]{2,1,0:T(8,128)(2,1)} %param.12) | copy-start | bytes 6291460
  0.6 8.2 %copy-start.5 = (s32[256,1]{0,1:T(1,128)S(1)}, s32[256,1]{0,1:T(1,128)}, u32[]{:S(2)}) copy-start(s32[256,1]{0,1:T(1,128)} %param.10) | copy-start | bytes 3076
  0.7 8.2 %copy-start.6 = (s32[256,1]{0,1:T(1,128)S(1)}, s32[256,1]{0,1:T(1,128)}, u32[]{:S(2)}) copy-start(s32[256,1]{0,1:T(1,128)} %param.11) | copy-start | bytes 3076
  0.7 8.2 %copy-start.7 = (f32[256]{0:T(256)S(1)}, f32[256]{0:T(256)}, u32[]{:S(2)}) copy-start(f32[256]{0:T(256)} %param.9) | copy-start | bytes 3076
  0.7 8.2 %collective-permute-start = (bf16[1024,1024]{1,0:T(8,128)(2,1)}, bf16[1024,1024]{1,0:T(8,128)(2,1)S(1)}, u32[]{:S(2)}, u32[]{:S(2)}) collective-permute-start(bf16[1024,1024]{1,0:T(8,128)(2,1)} %bitcast.14), channel_id=1, source_target_pairs={{0,1},{1,0},{2,3},{3,2},{4,5},{5,4},{6,7},{7,6},{8,9},{9,8},{10,11... | collective-permute-start | bytes 6291464 | tf_op jit(solution)/shard_map/ppermute | solution.py:283
  1.2 7.7 %collective-permute-start.1 = (bf16[1024,1024]{1,0:T(8,128)(2,1)}, bf16[1024,1024]{1,0:T(8,128)(2,1)S(1)}, u32[]{:S(2)}, u32[]{:S(2)}) collective-permute-start(bf16[1024,1024]{1,0:T(8,128)(2,1)} %bitcast.18), channel_id=1, source_target_pairs={{0,1},{1,0},{2,3},{3,2},{4,5},{5,4},{6,7},{7,6},{8,9},{9,8},{10,11... | collective-permute-start | bytes 6291464 | tf_op jit(solution)/shard_map/ppermute | solution.py:283
  3.7 16.3 %collective-permute-start.2 = (bf16[128,1024]{1,0:T(8,128)(2,1)}, bf16[128,1024]{1,0:T(8,128)(2,1)S(1)}, u32[]{:S(2)}, u32[]{:S(2)}) collective-permute-start(bf16[128,1024]{1,0:T(8,128)(2,1)} %get-tuple-element.37), channel_id=1, source_target_pairs={{0,2},{2,4},{4,6},{6,0},{1,3},{3,5},{5,7},{7,1},{8,10},{10,12},{12... | collective-permute-start | bytes 786440 | tf_op jit(solution)/shard_map/ppermute | solution.py:289
  6.8 13.8 %collective-permute-start.3 = (bf16[128,1024]{1,0:T(8,128)(2,1)}, bf16[128,1024]{1,0:T(8,128)(2,1)S(1)}, u32[]{:S(2)}, u32[]{:S(2)}) collective-permute-start(bf16[128,1024]{1,0:T(8,128)(2,1)} %get-tuple-element.39), channel_id=1, source_target_pairs={{0,6},{2,0},{4,2},{6,4},{1,7},{3,1},{5,3},{7,5},{8,14},{10,8},{12,... | collective-permute-start | bytes 786440 | tf_op jit(solution)/shard_map/ppermute | solution.py:289
  8.9 1.6 %copy-start.1 = (bf16[1,1024,1024]{2,1,0:T(8,128)(2,1)S(1)}, bf16[1,1024,1024]{2,1,0:T(8,128)(2,1)}, u32[]{:S(2)}) copy-start(bf16[1,1024,1024]{2,1,0:T(8,128)(2,1)} %param.13) | copy-start | bytes 6291460
  12.9 10.9 %copy-start.8 = (bf16[128,1024]{1,0:T(8,128)(2,1)S(1)}, bf16[128,1024]{1,0:T(8,128)(2,1)}, u32[]{:S(2)}) copy-start(bf16[128,1024]{1,0:T(8,128)(2,1)} %get-tuple-element.47) | copy-start | bytes 786436
  20.0 26.8 %copy-start.2 = (bf16[1,1024,1024]{2,1,0:T(8,128)(2,1)S(1)}, bf16[1,1024,1024]{2,1,0:T(8,128)(2,1)}, u32[]{:S(2)}) copy-start(bf16[1,1024,1024]{2,1,0:T(8,128)(2,1)} %param.13) | copy-start | bytes 6291460
  20.6 14.0 %collective-permute-start.4 = (bf16[256,1024]{1,0:T(8,128)(2,1)S(1)}, bf16[256,1024]{1,0:T(8,128)(2,1)S(1)}, u32[]{:S(2)}, u32[]{:S(2)}) collective-permute-start(bf16[256,1024]{1,0:T(8,128)(2,1)S(1)} %constant_dynamic-update-slice_fusion.refs_0_), channel_id=1, source_target_pairs={{0,16},{8,24},{16,0},{24,8},{1,17},{9,25},{17,1},{25,9},{2,18},{10... | collective-permute-start | bytes 1572872 | tf_op jit(solution)/shard_map/ppermute | solution.py:286
  22.3 14.0 %collective-permute-start.6 = (bf16[256,1024]{1,0:T(8,128)(2,1)S(1)}, bf16[256,1024]{1,0:T(8,128)(2,1)S(1)}, u32[]{:S(2)}, u32[]{:S(2)}) collective-permute-start(bf16[256,1024]{1,0:T(8,128)(2,1)S(1)} %constant_dynamic-update-slice_fusion.refs_0_), channel_id=1, source_target_pairs={{0,8},{8,0},{16,24},{24,16},{1,9},{9,1},{17,25},{25,17},{2,10},{10... | collective-permute-start | bytes 1572872 | tf_op jit(solution)/shard_map/ppermute | solution.py:286
  23.8 14.3 %collective-permute-start.15 = (bf16[128,1024]{1,0:T(8,128)(2,1)S(1)}, bf16[128,1024]{1,0:T(8,128)(2,1)S(1)}, u32[]{:S(2)}, u32[]{:S(2)}) collective-permute-start(bf16[128,1024]{1,0:T(8,128)(2,1)S(1)} %copy-done.8), channel_id=1, source_target_pairs={{0,4},{2,6},{4,0},{6,2},{1,5},{3,7},{5,1},{7,3},{8,12},{10,14},{12... | collective-permute-start | bytes 786440 | tf_op jit(solution)/shard_map/ppermute | solution.py:289
  34.6 9.3 %collective-permute-start.5 = (bf16[256,512]{1,0:T(8,128)(2,1)S(1)}, bf16[256,512]{1,0:T(8,128)(2,1)S(1)}, u32[]{:S(2)}, u32[]{:S(2)}) collective-permute-start(bf16[256,512]{1,0:T(8,128)(2,1)S(1)} %slice.44), channel_id=1, source_target_pairs={{0,8},{8,0},{16,24},{24,16},{1,9},{9,1},{17,25},{25,17},{2,10},{10... | collective-permute-start | bytes 786440 | tf_op jit(solution)/shard_map/ppermute | solution.py:286
  36.4 9.3 %collective-permute-start.7 = (bf16[256,512]{1,0:T(8,128)(2,1)S(1)}, bf16[256,512]{1,0:T(8,128)(2,1)S(1)}, u32[]{:S(2)}, u32[]{:S(2)}) collective-permute-start(bf16[256,512]{1,0:T(8,128)(2,1)S(1)} %slice.45), channel_id=1, source_target_pairs={{0,16},{8,24},{16,0},{24,8},{1,17},{9,25},{17,1},{25,9},{2,18},{10... | collective-permute-start | bytes 786440 | tf_op jit(solution)/shard_map/ppermute | solution.py:286
  38.1 16.8 %collective-permute-start.16 = (bf16[128,1024]{1,0:T(8,128)(2,1)S(1)}, bf16[128,1024]{1,0:T(8,128)(2,1)S(1)}, u32[]{:S(2)}, u32[]{:S(2)}) collective-permute-start(bf16[128,1024]{1,0:T(8,128)(2,1)S(1)} %collective-permute-done.15.refs_0_), channel_id=1, source_target_pairs={{0,8},{8,0},{16,24},{24,16},{1,9},{9,1},{17,25},{25,17},{2,10},{10... | collective-permute-start | bytes 786440 | tf_op jit(solution)/shard_map/ppermute | solution.py:286
  38.7 15.3 %collective-permute-start.17 = (bf16[128,1024]{1,0:T(8,128)(2,1)S(1)}, bf16[128,1024]{1,0:T(8,128)(2,1)S(1)}, u32[]{:S(2)}, u32[]{:S(2)}) collective-permute-start(bf16[128,1024]{1,0:T(8,128)(2,1)S(1)} %collective-permute-done.15.refs_0_), channel_id=1, source_target_pairs={{0,16},{8,24},{16,0},{24,8},{1,17},{9,25},{17,1},{25,9},{2,18},{10... | collective-permute-start | bytes 786440 | tf_op jit(solution)/shard_map/ppermute | solution.py:286
  45.7 12.8 %collective-permute-start.8 = (bf16[2,128,512]{2,1,0:T(8,128)(2,1)S(1)}, bf16[2,128,512]{2,1,0:T(8,128)(2,1)S(1)}, u32[]{:S(2)}, u32[]{:S(2)}) collective-permute-start(bf16[2,128,512]{2,1,0:T(8,128)(2,1)S(1)} %get-tuple-element.40), channel_id=1, source_target_pairs={{0,8},{8,0},{16,24},{24,16},{1,9},{9,1},{17,25},{25,17},{2,10},{10... | collective-permute-start | bytes 786440 | tf_op jit(solution)/shard_map/ppermute | solution.py:286
  53.9 6.5 %collective-permute-start.18 = (bf16[128,512]{1,0:T(8,128)(2,1)S(1)}, bf16[128,512]{1,0:T(8,128)(2,1)S(1)}, u32[]{:S(2)}, u32[]{:S(2)}) collective-permute-start(bf16[128,512]{1,0:T(8,128)(2,1)S(1)} %slice.50), channel_id=1, source_target_pairs={{0,8},{8,0},{16,24},{24,16},{1,9},{9,1},{17,25},{25,17},{2,10},{10... | collective-permute-start | bytes 393224 | tf_op jit(solution)/shard_map/ppermute | solution.py:286
  54.9 8.0 %collective-permute-start.19 = (bf16[128,512]{1,0:T(8,128)(2,1)S(1)}, bf16[128,512]{1,0:T(8,128)(2,1)S(1)}, u32[]{:S(2)}, u32[]{:S(2)}) collective-permute-start(bf16[128,512]{1,0:T(8,128)(2,1)S(1)} %slice.51), channel_id=1, source_target_pairs={{0,16},{8,24},{16,0},{24,8},{1,17},{9,25},{17,1},{25,9},{2,18},{10... | collective-permute-start | bytes 393224 | tf_op jit(solution)/shard_map/ppermute | solution.py:286
  56.5 15.4 %collective-permute-start.12 = (bf16[256,512]{1,0:T(8,128)(2,1)S(1)}, bf16[256,512]{1,0:T(8,128)(2,1)S(1)}, u32[]{:S(2)}, u32[]{:S(2)}) collective-permute-start(bf16[256,512]{1,0:T(8,128)(2,1)S(1)} %get-tuple-element.46), channel_id=1, source_target_pairs={{0,24},{8,16},{16,8},{24,0},{1,25},{9,17},{17,9},{25,1},{2,26},{10... | collective-permute-start | bytes 786440 | tf_op jit(solution)/shard_map/ppermute | solution.py:286
  57.6 14.3 %collective-permute-start.11 = (bf16[256,512]{1,0:T(8,128)(2,1)S(1)}, bf16[256,512]{1,0:T(8,128)(2,1)S(1)}, u32[]{:S(2)}, u32[]{:S(2)}) collective-permute-start(bf16[256,512]{1,0:T(8,128)(2,1)S(1)} %get-tuple-element.45), channel_id=1, source_target_pairs={{0,16},{8,24},{16,0},{24,8},{1,17},{9,25},{17,1},{25,9},{2,18},{10... | collective-permute-start | bytes 786440 | tf_op jit(solution)/shard_map/ppermute | solution.py:286
  58.5 13.4 %collective-permute-start.10 = (bf16[256,512]{1,0:T(8,128)(2,1)S(1)}, bf16[256,512]{1,0:T(8,128)(2,1)S(1)}, u32[]{:S(2)}, u32[]{:S(2)}) collective-permute-start(bf16[256,512]{1,0:T(8,128)(2,1)S(1)} %get-tuple-element.44), channel_id=1, source_target_pairs={{0,8},{8,0},{16,24},{24,16},{1,9},{9,1},{17,25},{25,17},{2,10},{10... | collective-permute-start | bytes 786440 | tf_op jit(solution)/shard_map/ppermute | solution.py:286
  71.9 16.0 %collective-permute-start.24 = (bf16[2,1024,1024]{2,1,0:T(8,128)(2,1)S(1)}, bf16[2,1024,1024]{2,1,0:T(8,128)(2,1)S(1)}, u32[]{:S(2)}, u32[]{:S(2)}) collective-permute-start(bf16[2,1024,1024]{2,1,0:T(8,128)(2,1)S(1)} %convolution_convert_fusion), channel_id=1, source_target_pairs={{0,1},{1,0},{2,3},{3,2},{4,5},{5,4},{6,7},{7,6},{8,9},{9,8},{10,11... | collective-permute-start | bytes 12582920 | tf_op jit(solution)/shard_map/ppermute | solution.py:283
  72.0 15.9 %collective-permute-start.9 = (bf16[128,512]{1,0:T(8,128)(2,1)S(1)}, bf16[128,512]{1,0:T(8,128)(2,1)S(1)}, u32[]{:S(2)}, u32[]{:S(2)}) collective-permute-start(bf16[128,512]{1,0:T(8,128)(2,1)S(1)} %fusion.2), channel_id=1, source_target_pairs={{0,16},{8,24},{16,0},{24,8},{1,17},{9,25},{17,1},{25,9},{2,18},{10... | collective-permute-start | bytes 393224 | tf_op jit(solution)/shard_map/ppermute | solution.py:286
  73.1 7.3 %collective-permute-start.22 = (bf16[128,512]{1,0:T(8,128)(2,1)S(1)}, bf16[128,512]{1,0:T(8,128)(2,1)S(1)}, u32[]{:S(2)}, u32[]{:S(2)}) collective-permute-start(bf16[128,512]{1,0:T(8,128)(2,1)S(1)} %get-tuple-element.62), channel_id=1, source_target_pairs={{0,24},{8,16},{16,8},{24,0},{1,25},{9,17},{17,9},{25,1},{2,26},{10... | collective-permute-start | bytes 393224 | tf_op jit(solution)/shard_map/ppermute | solution.py:286
  74.4 9.6 %collective-permute-start.21 = (bf16[128,512]{1,0:T(8,128)(2,1)S(1)}, bf16[128,512]{1,0:T(8,128)(2,1)S(1)}, u32[]{:S(2)}, u32[]{:S(2)}) collective-permute-start(bf16[128,512]{1,0:T(8,128)(2,1)S(1)} %get-tuple-element.60), channel_id=1, source_target_pairs={{0,16},{8,24},{16,0},{24,8},{1,17},{9,25},{17,1},{25,9},{2,18},{10... | collective-permute-start | bytes 393224 | tf_op jit(solution)/shard_map/ppermute | solution.py:286
  75.9 9.4 %collective-permute-start.20 = (bf16[128,512]{1,0:T(8,128)(2,1)S(1)}, bf16[128,512]{1,0:T(8,128)(2,1)S(1)}, u32[]{:S(2)}, u32[]{:S(2)}) collective-permute-start(bf16[128,512]{1,0:T(8,128)(2,1)S(1)} %get-tuple-element.58), channel_id=1, source_target_pairs={{0,8},{8,0},{16,24},{24,16},{1,9},{9,1},{17,25},{25,17},{2,10},{10... | collective-permute-start | bytes 393224 | tf_op jit(solution)/shard_map/ppermute | solution.py:286
  80.4 15.8 %collective-permute-start.13 = (bf16[128,512]{1,0:T(8,128)(2,1)S(1)}, bf16[128,512]{1,0:T(8,128)(2,1)S(1)}, u32[]{:S(2)}, u32[]{:S(2)}) collective-permute-start(bf16[128,512]{1,0:T(8,128)(2,1)S(1)} %get-tuple-element.68), channel_id=1, source_target_pairs={{0,6},{2,0},{4,2},{6,4},{1,7},{3,1},{5,3},{7,5},{8,14},{10,8},{12,... | collective-permute-start | bytes 393224 | tf_op jit(solution)/shard_map/ppermute | solution.py:289
  84.1 12.1 %collective-permute-start.14 = (bf16[128,512]{1,0:T(8,128)(2,1)S(1)}, bf16[128,512]{1,0:T(8,128)(2,1)S(1)}, u32[]{:S(2)}, u32[]{:S(2)}) collective-permute-start(bf16[128,512]{1,0:T(8,128)(2,1)S(1)} %get-tuple-element.67), channel_id=1, source_target_pairs={{0,2},{2,4},{4,6},{6,0},{1,3},{3,5},{5,7},{7,1},{8,10},{10,12},{12... | collective-permute-start | bytes 393224 | tf_op jit(solution)/shard_map/ppermute | solution.py:289
  85.3 10.9 %collective-permute-start.23 = (bf16[128,512]{1,0:T(8,128)(2,1)S(1)}, bf16[128,512]{1,0:T(8,128)(2,1)S(1)}, u32[]{:S(2)}, u32[]{:S(2)}) collective-permute-start(bf16[128,512]{1,0:T(8,128)(2,1)S(1)} %add_convert_fusion.1), channel_id=1, source_target_pairs={{0,4},{2,6},{4,0},{6,2},{1,5},{3,7},{5,1},{7,3},{8,12},{10,14},{12... | collective-permute-start | bytes 393224 | tf_op jit(solution)/shard_map/ppermute | solution.py:289
  (2 other events, 2.4 us)

commit v14 on v11

--- a/solution.py
+++ b/solution.py
@@ -334,7 +334,6 @@
         near = spread(jnp.concatenate([after(moved[0], pair[0]), moved[1]], 0))
         far = after(moved[2], *near[1:3])
         far = [far] + [across(far, j) for j in (1, 2, 3)]
-        near[0] = after(near[0], far[1])
         back, got_own = collect_pair([pair[0], after(pair[1], *near[3:])], 1)
         kept, (blocks,) = expert_rows(None, [near], [(2 * capacity, None)], weights, everything, capacity, kept)
         total, got = collect(blocks)

time: 97.5 us -> 98.9 us (1.014)
  waiting for transfers between devices: 24.4 us -> 25.8 us
    ppermute x15, waiting for transfers between devices: 19.4 us -> 20.8 us  [across(): return lax.ppermute(x, 'tensor', [(i, i ^ j) for i in range(tensor_size)])]
where the time goes in v14:
time: 98.9 us; the launch traced here: 98.7 us
  starting transfers between devices  36.8 us (37%)
  Pallas kernels  28.4 us (29%)
  waiting for transfers between devices  25.8 us (26%)
  local copies, waits for them, and re-layouts  4.15 us (4%)
  matrix products  2.38 us (2%)
    pallas_call x3, Pallas kernels, expert_rows(): pl.pallas_call(functools.partial(expert_kernel, counts_in, base, groups,...  20.9 us
    ppermute x15, waiting for transfers between devices, across(): return lax.ppermute(x, 'tensor', [(i, i ^ j) for i in range(tensor_size)])  20.8 us
    ppermute x15, starting transfers between devices, across(): return lax.ppermute(x, 'tensor', [(i, i ^ j) for i in range(tensor_size)])  20.5 us
    ppermute x6, starting transfers between devices, shift(): lax.ppermute(x, 'expert', [(i, (i + k) % experts) for i in range(experts)])  15.6 us
    ppermute x6, waiting for transfers between devices, shift(): lax.ppermute(x, 'expert', [(i, (i + k) % experts) for i in range(experts)])  4.94 us
    unnamed x19, local copies, waits for them, and re-layouts  4.08 us
    pallas_call x1, Pallas kernels, weight_grads(): pl.pallas_call(weight_grad_kernel, out_shape=[jax.ShapeDtypeStruct((half,...  3.87 us
    pallas_call x1, Pallas kernels, place(): pl.pallas_call(functools.partial(place_kernel, spans, shifts, capacity),...  2.41 us
  transfers between devices with their start and end apart: 24, of which 9 were waited for; matrix products, arithmetic and copies ran while one was open for 3% of the time, Pallas kernels for 28%

profile of v14, /device:TPU:0, one launch (start us, length us, event | category | flops | bytes accessed | tf_op | source)
XLA Modules:
  0.0 98.7 jit_solution(2250898223433865059)
XLA Ops:
  1.3 2.4 %place_rows.1 = (bf16[128,1024]{1,0:T(8,128)(2,1)}, bf16[128,1024]{1,0:T(8,128)(2,1)}, bf16[128,1024]{1,0:T(8,128)(2,1)}) custom-call(s32[1,256]{1,0:T(1,128)} %bitcast.22, s32[1,256]{1,0:T(1,128)} %bitcast.25, f32[1,256]{1,0:T(1,128)} %bitcast.28, bf16[256,2048]{1,0:T(8,128)(2,1)} %tokens.1, bf16[256,2048]{1,0:T(8,128)(2,1)} %grad_output.1), custom_call_target="tpu_custom_call" | custom-call | flops 1000 | bytes 1000 | tf_op jit(solution)/shard_map/place_rows/pallas_call | solution.py:90
  3.7 3.1 %collective-permute-start.2 = (bf16[128,1024]{1,0:T(8,128)(2,1)}, bf16[128,1024]{1,0:T(8,128)(2,1)S(1)}, u32[]{:S(2)}, u32[]{:S(2)}) collective-permute-start(bf16[128,1024]{1,0:T(8,128)(2,1)} %get-tuple-element.35), channel_id=1, source_target_pairs={{0,2},{2,4},{4,6},{6,0},{1,3},{3,5},{5,7},{7,1},{8,10},{10,12},{12... | collective-permute-start | bytes 786440 | tf_op jit(solution)/shard_map/ppermute | solution.py:294
  6.8 2.1 %collective-permute-start.3 = (bf16[128,1024]{1,0:T(8,128)(2,1)}, bf16[128,1024]{1,0:T(8,128)(2,1)S(1)}, u32[]{:S(2)}, u32[]{:S(2)}) collective-permute-start(bf16[128,1024]{1,0:T(8,128)(2,1)} %get-tuple-element.37), channel_id=1, source_target_pairs={{0,6},{2,0},{4,2},{6,4},{1,7},{3,1},{5,3},{7,5},{8,14},{10,8},{12,... | collective-permute-start | bytes 786440 | tf_op jit(solution)/shard_map/ppermute | solution.py:294
  8.9 1.6 %copy-done.1 = bf16[1,1024,1024]{2,1,0:T(8,128)(2,1)S(1)} copy-done((bf16[1,1024,1024]{2,1,0:T(8,128)(2,1)S(1)}, bf16[1,1024,1024]{2,1,0:T(8,128)(2,1)}, u32[]{:S(2)}) %copy-start.1) | copy-done | bytes 2097176
  10.5 1.2 %copy-done.3 = bf16[256,2048]{1,0:T(8,128)(2,1)S(1)} copy-done((bf16[256,2048]{1,0:T(8,128)(2,1)S(1)}, bf16[256,2048]{1,0:T(8,128)(2,1)}, u32[]{:S(2)}) %copy-start.3) | copy-done | bytes 1048600
  11.7 1.2 %copy-done.4 = bf16[256,2048]{1,0:T(8,128)(2,1)S(1)} copy-done((bf16[256,2048]{1,0:T(8,128)(2,1)S(1)}, bf16[256,2048]{1,0:T(8,128)(2,1)}, u32[]{:S(2)}) %copy-start.4) | copy-done | bytes 1048600
  12.9 7.1 %expert_rows.3 = (bf16[2,512,2048]{2,1,0:T(8,128)(2,1)S(1)}, bf16[2,512,1024]{2,1,0:T(8,128)(2,1)S(1)}, bf16[2,128,512]{2,1,0:T(8,128)(2,1)S(1)}, bf16[2,128,512]{2,1,0:T(8,128)(2,1)S(1)}) custom-call(s32[1,256]{1,0:T(1,128)S(1)} %bitcast.23, s32[1,256]{1,0:T(1,128)S(1)} %bitcast.26, f32[1,256]{1,0:T(1,128)S(1)} %bitcast.29, ...), custom_call_target="tpu_custom_call" | custom-call | flops 1610612736 | bytes 10485760 | tf_op jit(solution)/shard_map/expert_rows/pallas_call | solution.py:199
  20.6 1.9 %collective-permute-start.4 = (bf16[256,1024]{1,0:T(8,128)(2,1)S(1)}, bf16[256,1024]{1,0:T(8,128)(2,1)S(1)}, u32[]{:S(2)}, u32[]{:S(2)}) collective-permute-start(bf16[256,1024]{1,0:T(8,128)(2,1)S(1)} %constant_dynamic-update-slice_fusion.refs_0_), channel_id=1, source_target_pairs={{0,16},{8,24},{16,0},{24,8},{1,17},{9,25},{17,1},{25,9},{2,18},{10... | collective-permute-start | bytes 1572872 | tf_op jit(solution)/shard_map/ppermute | solution.py:291
  22.4 1.5 %collective-permute-start.6 = (bf16[256,1024]{1,0:T(8,128)(2,1)S(1)}, bf16[256,1024]{1,0:T(8,128)(2,1)S(1)}, u32[]{:S(2)}, u32[]{:S(2)}) collective-permute-start(bf16[256,1024]{1,0:T(8,128)(2,1)S(1)} %constant_dynamic-update-slice_fusion.refs_0_), channel_id=1, source_target_pairs={{0,8},{8,0},{16,24},{24,16},{1,9},{9,1},{17,25},{25,17},{2,10},{10... | collective-permute-start | bytes 1572872 | tf_op jit(solution)/shard_map/ppermute | solution.py:291
  23.9 2.6 %collective-permute-start.15 = (bf16[128,1024]{1,0:T(8,128)(2,1)S(1)}, bf16[128,1024]{1,0:T(8,128)(2,1)S(1)}, u32[]{:S(2)}, u32[]{:S(2)}) collective-permute-start(bf16[128,1024]{1,0:T(8,128)(2,1)S(1)} %copy-done.8), channel_id=1, source_target_pairs={{0,4},{2,6},{4,0},{6,2},{1,5},{3,7},{5,1},{7,3},{8,12},{10,14},{12... | collective-permute-start | bytes 786440 | tf_op jit(solution)/shard_map/ppermute | solution.py:294
  26.5 8.1 %collective-permute-done.4.refs_2_ = bf16[256,1024]{1,0:T(8,128)(2,1)S(1)} collective-permute-done((bf16[256,1024]{1,0:T(8,128)(2,1)S(1)}, bf16[256,1024]{1,0:T(8,128)(2,1)S(1)}, u32[]{:S(2)}, u32[]{:S(2)}) %collective-permute-start.4) | collective-permute-done | bytes 524320 | tf_op jit(solution)/shard_map/ppermute | solution.py:291
  34.6 1.8 %collective-permute-start.5 = (bf16[256,512]{1,0:T(8,128)(2,1)S(1)}, bf16[256,512]{1,0:T(8,128)(2,1)S(1)}, u32[]{:S(2)}, u32[]{:S(2)}) collective-permute-start(bf16[256,512]{1,0:T(8,128)(2,1)S(1)} %slice.36), channel_id=1, source_target_pairs={{0,8},{8,0},{16,24},{24,16},{1,9},{9,1},{17,25},{25,17},{2,10},{10... | collective-permute-start | bytes 786440 | tf_op jit(solution)/shard_map/ppermute | solution.py:291
  36.4 1.6 %collective-permute-start.7 = (bf16[256,512]{1,0:T(8,128)(2,1)S(1)}, bf16[256,512]{1,0:T(8,128)(2,1)S(1)}, u32[]{:S(2)}, u32[]{:S(2)}) collective-permute-start(bf16[256,512]{1,0:T(8,128)(2,1)S(1)} %slice.37), channel_id=1, source_target_pairs={{0,16},{8,24},{16,0},{24,8},{1,17},{9,25},{17,1},{25,9},{2,18},{10... | collective-permute-start | bytes 786440 | tf_op jit(solution)/shard_map/ppermute | solution.py:291
  39.7 2.0 %collective-permute-start.18 = (bf16[128,1024]{1,0:T(8,128)(2,1)S(1)}, bf16[128,1024]{1,0:T(8,128)(2,1)S(1)}, u32[]{:S(2)}, u32[]{:S(2)}) collective-permute-start(bf16[128,1024]{1,0:T(8,128)(2,1)S(1)} %collective-permute-done.15.refs_0_), channel_id=1, source_target_pairs={{0,24},{8,16},{16,8},{24,0},{1,25},{9,17},{17,9},{25,1},{2,26},{10... | collective-permute-start | bytes 786440 | tf_op jit(solution)/shard_map/ppermute | solution.py:291
  41.7 2.3 %collective-permute-done.5.refs_3_ = bf16[256,512]{1,0:T(8,128)(2,1)S(1)} collective-permute-done((bf16[256,512]{1,0:T(8,128)(2,1)S(1)}, bf16[256,512]{1,0:T(8,128)(2,1)S(1)}, u32[]{:S(2)}, u32[]{:S(2)}) %collective-permute-start.5) | collective-permute-done | bytes 262176 | tf_op jit(solution)/shard_map/ppermute | solution.py:291
  44.0 1.8 %collective-permute-done.7.refs_4_ = bf16[256,512]{1,0:T(8,128)(2,1)S(1)} collective-permute-done((bf16[256,512]{1,0:T(8,128)(2,1)S(1)}, bf16[256,512]{1,0:T(8,128)(2,1)S(1)}, u32[]{:S(2)}, u32[]{:S(2)}) %collective-permute-start.7) | collective-permute-done | bytes 262176 | tf_op jit(solution)/shard_map/ppermute | solution.py:291
  46.9 7.1 %expert_rows.4 = (bf16[2,512,2048]{2,1,0:T(8,128)(2,1)S(1)}, bf16[2,512,1024]{2,1,0:T(8,128)(2,1)S(1)}, bf16[256,512]{1,0:T(8,128)(2,1)S(1)}, bf16[256,512]{1,0:...) custom-call(bf16[256,1024]{1,0:T(8,128)(2,1)S(1)} %constant_dynamic-, ...), custom_call_target="tpu_custom_call", output_to_operand_aliasing={{0}: (9, {}), {1}: (10, {})} | custom-call | flops 3221225472 | bytes 12582912 | tf_op jit(solution)/shard_map/expert_rows/pallas_call | solution.py:199
  54.1 1.9 %collective-permute-start.12 = (bf16[256,512]{1,0:T(8,128)(2,1)S(1)}, bf16[256,512]{1,0:T(8,128)(2,1)S(1)}, u32[]{:S(2)}, u32[]{:S(2)}) collective-permute-start(bf16[256,512]{1,0:T(8,128)(2,1)S(1)} %get-tuple-element.44), channel_id=1, source_target_pairs={{0,24},{8,16},{16,8},{24,0},{1,25},{9,17},{17,9},{25,1},{2,26},{10... | collective-permute-start | bytes 786440 | tf_op jit(solution)/shard_map/ppermute | solution.py:291
  56.0 4.9 %collective-permute-done.8 = bf16[2,128,512]{2,1,0:T(8,128)(2,1)S(1)} collective-permute-done((bf16[2,128,512]{2,1,0:T(8,128)(2,1)S(1)}, bf16[2,128,512]{2,1,0:T(8,128)(2,1)S(1)}, u32[]{:S(2)}, u32[]{:S(2)}) %collective-permute-start.8) | collective-permute-done | bytes 262176 | tf_op jit(solution)/shard_map/ppermute | solution.py:291
  60.9 1.7 %collective-permute-start.11 = (bf16[256,512]{1,0:T(8,128)(2,1)S(1)}, bf16[256,512]{1,0:T(8,128)(2,1)S(1)}, u32[]{:S(2)}, u32[]{:S(2)}) collective-permute-start(bf16[256,512]{1,0:T(8,128)(2,1)S(1)} %get-tuple-element.43), channel_id=1, source_target_pairs={{0,16},{8,24},{16,0},{24,8},{1,17},{9,25},{17,1},{25,9},{2,18},{10... | collective-permute-start | bytes 786440 | tf_op jit(solution)/shard_map/ppermute | solution.py:291
  62.6 1.4 %collective-permute-start.10 = (bf16[256,512]{1,0:T(8,128)(2,1)S(1)}, bf16[256,512]{1,0:T(8,128)(2,1)S(1)}, u32[]{:S(2)}, u32[]{:S(2)}) collective-permute-start(bf16[256,512]{1,0:T(8,128)(2,1)S(1)} %get-tuple-element.42), channel_id=1, source_target_pairs={{0,8},{8,0},{16,24},{24,16},{1,9},{9,1},{17,25},{25,17},{2,10},{10... | collective-permute-start | bytes 786440 | tf_op jit(solution)/shard_map/ppermute | solution.py:291
  64.0 6.7 %expert_rows.5 = (bf16[2,512,2048]{2,1,0:T(8,128)(2,1)S(1)}, bf16[2,512,1024]{2,1,0:T(8,128)(2,1)S(1)}, bf16[128,512]{1,0:T(8,128)(2,1)S(1)}, bf16[128,512]{1,0:...) custom-call(bf16[128,1024]{1,0:T(8,128)(2,1)S(1)} %collective-permut, ...), custom_call_target="tpu_custom_call", output_to_operand_aliasing={{0}: (8, {}), {1}: (9, {})} | custom-call | flops 1610612736 | bytes 10485760 | tf_op jit(solution)/shard_map/expert_rows/pallas_call | solution.py:199
  70.8 2.4 %convolution_convert_fusion = bf16[2,1024,1024]{2,1,0:T(8,128)(2,1)S(1)} fusion(bf16[2,512,1024]{2,1,0:T(8,128)(2,1)S(1)} %get-tuple-element.53.acts, bf16[2,512,2048]{2,1,0:T(8,128)(2,1)S(1)} %get-tuple-element.52.rows), kind=kOutput, calls=%fused_computation | convolution fusion | flops 2149580800 | bytes 8388608 | tf_op jit(solution)/shard_map/dot_general | solution.py:320
  73.9 1.5 %collective-permute-start.21 = (bf16[128,512]{1,0:T(8,128)(2,1)S(1)}, bf16[128,512]{1,0:T(8,128)(2,1)S(1)}, u32[]{:S(2)}, u32[]{:S(2)}) collective-permute-start(bf16[128,512]{1,0:T(8,128)(2,1)S(1)} %get-tuple-element.58), channel_id=1, source_target_pairs={{0,24},{8,16},{16,8},{24,0},{1,25},{9,17},{17,9},{25,1},{2,26},{10... | collective-permute-start | bytes 393224 | tf_op jit(solution)/shard_map/ppermute | solution.py:291
  75.7 1.7 %collective-permute-start.19 = (bf16[128,512]{1,0:T(8,128)(2,1)S(1)}, bf16[128,512]{1,0:T(8,128)(2,1)S(1)}, u32[]{:S(2)}, u32[]{:S(2)}) collective-permute-start(bf16[128,512]{1,0:T(8,128)(2,1)S(1)} %get-tuple-element.54), channel_id=1, source_target_pairs={{0,8},{8,0},{16,24},{24,16},{1,9},{9,1},{17,25},{25,17},{2,10},{10... | collective-permute-start | bytes 393224 | tf_op jit(solution)/shard_map/ppermute | solution.py:291
  77.6 3.6 %collective-permute-done.21 = bf16[128,512]{1,0:T(8,128)(2,1)S(1)} collective-permute-done((bf16[128,512]{1,0:T(8,128)(2,1)S(1)}, bf16[128,512]{1,0:T(8,128)(2,1)S(1)}, u32[]{:S(2)}, u32[]{:S(2)}) %collective-permute-start.21) | collective-permute-done | bytes 131104 | tf_op jit(solution)/shard_map/ppermute | solution.py:291
  81.2 3.6 %collective-permute-start.13 = (bf16[128,512]{1,0:T(8,128)(2,1)S(1)}, bf16[128,512]{1,0:T(8,128)(2,1)S(1)}, u32[]{:S(2)}, u32[]{:S(2)}) collective-permute-start(bf16[128,512]{1,0:T(8,128)(2,1)S(1)} %get-tuple-element.64), channel_id=1, source_target_pairs={{0,6},{2,0},{4,2},{6,4},{1,7},{3,1},{5,3},{7,5},{8,14},{10,8},{12,... | collective-permute-start | bytes 393224 | tf_op jit(solution)/shard_map/ppermute | solution.py:294
  84.9 1.6 %collective-permute-start.14 = (bf16[128,512]{1,0:T(8,128)(2,1)S(1)}, bf16[128,512]{1,0:T(8,128)(2,1)S(1)}, u32[]{:S(2)}, u32[]{:S(2)}) collective-permute-start(bf16[128,512]{1,0:T(8,128)(2,1)S(1)} %get-tuple-element.63), channel_id=1, source_target_pairs={{0,2},{2,4},{4,6},{6,0},{1,3},{3,5},{5,7},{7,1},{8,10},{10,12},{12... | collective-permute-start | bytes 393224 | tf_op jit(solution)/shard_map/ppermute | solution.py:294
  86.5 2.7 %collective-permute-start.22 = (bf16[128,512]{1,0:T(8,128)(2,1)S(1)}, bf16[128,512]{1,0:T(8,128)(2,1)S(1)}, u32[]{:S(2)}, u32[]{:S(2)}) collective-permute-start(bf16[128,512]{1,0:T(8,128)(2,1)S(1)} %add_convert_fusion.1), channel_id=1, source_target_pairs={{0,4},{2,6},{4,0},{6,2},{1,5},{3,7},{5,1},{7,3},{8,12},{10,14},{12... | collective-permute-start | bytes 393224 | tf_op jit(solution)/shard_map/ppermute | solution.py:294
  89.3 3.9 %weight_grads.1 = (bf16[1024,1024]{1,0:T(8,128)(2,1)}, bf16[1024,1024]{1,0:T(8,128)(2,1)}) custom-call(bf16[2,512,2048]{2,1,0:T(8,128)(2,1)S(1)} %get-tuple-element.52.rows, bf16[2,512,1024]{2,1,0:T(8,128)(2,1)S(1)} %get-tuple-element.53.acts, bf16[2,1024,1024]{2,1,0:T(8,128)(2,1)S(1)} %collective-permute-done.23.got), custom_call_target="tpu_custom_call" | custom-call | flops 1000 | bytes 1000 | tf_op jit(solution)/shard_map/weight_grads/pallas_call | solution.py:263
  93.1 4.3 %collective-permute-done.22.refs_3_ = bf16[128,512]{1,0:T(8,128)(2,1)S(1)} collective-permute-done((bf16[128,512]{1,0:T(8,128)(2,1)S(1)}, bf16[128,512]{1,0:T(8,128)(2,1)S(1)}, u32[]{:S(2)}, u32[]{:S(2)}) %collective-permute-start.22) | collective-permute-done | bytes 131104 | tf_op jit(solution)/shard_map/ppermute | solution.py:294
  97.5 1.2 %unplace_rows.1 = bf16[256,512]{1,0:T(8,128)(2,1)} custom-call(s32[1,256]{1,0:T(1,128)S(1)} %bitcast.24, s32[1,256]{1,0:T(1,128)S(1)} %bitcast.27, bf16[128,512]{1,0:T(8,128)(2,1)S(1)} %fusion.1.refs_0_, bf16[128,512]{1,0:T(8,128)(2,1)S(1)} %collective-permute-done.13.refs_1_, bf16[128,512]{1,0:T(8,128)(2,1)S(1)} %collective-permute-done.14.refs_2_, ...), custom_call_target="tpu_custom_call" | custom-call | flops 1000 | bytes 1000 | tf_op jit(solution)/shard_map/unplace_rows/pallas_call | solution.py:235
  (50 shorter events, 5.3 us)
Async XLA Ops:
  0.6 8.2 %copy-start = (bf16[1,1024,1024]{2,1,0:T(8,128)(2,1)S(1)}, bf16[1,1024,1024]{2,1,0:T(8,128)(2,1)}, u32[]{:S(2)}) copy-start(bf16[1,1024,1024]{2,1,0:T(8,128)(2,1)} %param.12) | copy-start | bytes 6291460
  0.6 8.2 %copy-start.5 = (s32[256,1]{0,1:T(1,128)S(1)}, s32[256,1]{0,1:T(1,128)}, u32[]{:S(2)}) copy-start(s32[256,1]{0,1:T(1,128)} %param.10) | copy-start | bytes 3076
  0.7 8.2 %copy-start.6 = (s32[256,1]{0,1:T(1,128)S(1)}, s32[256,1]{0,1:T(1,128)}, u32[]{:S(2)}) copy-start(s32[256,1]{0,1:T(1,128)} %param.11) | copy-start | bytes 3076
  0.7 8.2 %copy-start.7 = (f32[256]{0:T(256)S(1)}, f32[256]{0:T(256)}, u32[]{:S(2)}) copy-start(f32[256]{0:T(256)} %param.9) | copy-start | bytes 3076
  0.7 8.2 %collective-permute-start = (bf16[1024,1024]{1,0:T(8,128)(2,1)}, bf16[1024,1024]{1,0:T(8,128)(2,1)S(1)}, u32[]{:S(2)}, u32[]{:S(2)}) collective-permute-start(bf16[1024,1024]{1,0:T(8,128)(2,1)} %bitcast.14), channel_id=1, source_target_pairs={{0,1},{1,0},{2,3},{3,2},{4,5},{5,4},{6,7},{7,6},{8,9},{9,8},{10,11... | collective-permute-start | bytes 6291464 | tf_op jit(solution)/shard_map/ppermute | solution.py:288
  1.2 7.7 %collective-permute-start.1 = (bf16[1024,1024]{1,0:T(8,128)(2,1)}, bf16[1024,1024]{1,0:T(8,128)(2,1)S(1)}, u32[]{:S(2)}, u32[]{:S(2)}) collective-permute-start(bf16[1024,1024]{1,0:T(8,128)(2,1)} %bitcast.18), channel_id=1, source_target_pairs={{0,1},{1,0},{2,3},{3,2},{4,5},{5,4},{6,7},{7,6},{8,9},{9,8},{10,11... | collective-permute-start | bytes 6291464 | tf_op jit(solution)/shard_map/ppermute | solution.py:288
  3.7 16.4 %collective-permute-start.2 = (bf16[128,1024]{1,0:T(8,128)(2,1)}, bf16[128,1024]{1,0:T(8,128)(2,1)S(1)}, u32[]{:S(2)}, u32[]{:S(2)}) collective-permute-start(bf16[128,1024]{1,0:T(8,128)(2,1)} %get-tuple-element.35), channel_id=1, source_target_pairs={{0,2},{2,4},{4,6},{6,0},{1,3},{3,5},{5,7},{7,1},{8,10},{10,12},{12... | collective-permute-start | bytes 786440 | tf_op jit(solution)/shard_map/ppermute | solution.py:294
  6.8 13.8 %collective-permute-start.3 = (bf16[128,1024]{1,0:T(8,128)(2,1)}, bf16[128,1024]{1,0:T(8,128)(2,1)S(1)}, u32[]{:S(2)}, u32[]{:S(2)}) collective-permute-start(bf16[128,1024]{1,0:T(8,128)(2,1)} %get-tuple-element.37), channel_id=1, source_target_pairs={{0,6},{2,0},{4,2},{6,4},{1,7},{3,1},{5,3},{7,5},{8,14},{10,8},{12,... | collective-permute-start | bytes 786440 | tf_op jit(solution)/shard_map/ppermute | solution.py:294
  8.9 1.6 %copy-start.1 = (bf16[1,1024,1024]{2,1,0:T(8,128)(2,1)S(1)}, bf16[1,1024,1024]{2,1,0:T(8,128)(2,1)}, u32[]{:S(2)}) copy-start(bf16[1,1024,1024]{2,1,0:T(8,128)(2,1)} %param.13) | copy-start | bytes 6291460
  10.5 1.2 %copy-start.3 = (bf16[256,2048]{1,0:T(8,128)(2,1)S(1)}, bf16[256,2048]{1,0:T(8,128)(2,1)}, u32[]{:S(2)}) copy-start(bf16[256,2048]{1,0:T(8,128)(2,1)} %tokens.1) | copy-start | bytes 3145732
  12.9 11.0 %copy-start.8 = (bf16[128,1024]{1,0:T(8,128)(2,1)S(1)}, bf16[128,1024]{1,0:T(8,128)(2,1)}, u32[]{:S(2)}) copy-start(bf16[128,1024]{1,0:T(8,128)(2,1)} %get-tuple-element.45) | copy-start | bytes 786436
  20.1 26.8 %copy-start.2 = (bf16[1,1024,1024]{2,1,0:T(8,128)(2,1)S(1)}, bf16[1,1024,1024]{2,1,0:T(8,128)(2,1)}, u32[]{:S(2)}) copy-start(bf16[1,1024,1024]{2,1,0:T(8,128)(2,1)} %param.13) | copy-start | bytes 6291460
  20.6 14.1 %collective-permute-start.4 = (bf16[256,1024]{1,0:T(8,128)(2,1)S(1)}, bf16[256,1024]{1,0:T(8,128)(2,1)S(1)}, u32[]{:S(2)}, u32[]{:S(2)}) collective-permute-start(bf16[256,1024]{1,0:T(8,128)(2,1)S(1)} %constant_dynamic-update-slice_fusion.refs_0_), channel_id=1, source_target_pairs={{0,16},{8,24},{16,0},{24,8},{1,17},{9,25},{17,1},{25,9},{2,18},{10... | collective-permute-start | bytes 1572872 | tf_op jit(solution)/shard_map/ppermute | solution.py:291
  22.4 14.0 %collective-permute-start.6 = (bf16[256,1024]{1,0:T(8,128)(2,1)S(1)}, bf16[256,1024]{1,0:T(8,128)(2,1)S(1)}, u32[]{:S(2)}, u32[]{:S(2)}) collective-permute-start(bf16[256,1024]{1,0:T(8,128)(2,1)S(1)} %constant_dynamic-update-slice_fusion.refs_0_), channel_id=1, source_target_pairs={{0,8},{8,0},{16,24},{24,16},{1,9},{9,1},{17,25},{25,17},{2,10},{10... | collective-permute-start | bytes 1572872 | tf_op jit(solution)/shard_map/ppermute | solution.py:291
  23.9 14.3 %collective-permute-start.15 = (bf16[128,1024]{1,0:T(8,128)(2,1)S(1)}, bf16[128,1024]{1,0:T(8,128)(2,1)S(1)}, u32[]{:S(2)}, u32[]{:S(2)}) collective-permute-start(bf16[128,1024]{1,0:T(8,128)(2,1)S(1)} %copy-done.8), channel_id=1, source_target_pairs={{0,4},{2,6},{4,0},{6,2},{1,5},{3,7},{5,1},{7,3},{8,12},{10,14},{12... | collective-permute-start | bytes 786440 | tf_op jit(solution)/shard_map/ppermute | solution.py:294
  34.6 9.3 %collective-permute-start.5 = (bf16[256,512]{1,0:T(8,128)(2,1)S(1)}, bf16[256,512]{1,0:T(8,128)(2,1)S(1)}, u32[]{:S(2)}, u32[]{:S(2)}) collective-permute-start(bf16[256,512]{1,0:T(8,128)(2,1)S(1)} %slice.36), channel_id=1, source_target_pairs={{0,8},{8,0},{16,24},{24,16},{1,9},{9,1},{17,25},{25,17},{2,10},{10... | collective-permute-start | bytes 786440 | tf_op jit(solution)/shard_map/ppermute | solution.py:291
  36.4 9.3 %collective-permute-start.7 = (bf16[256,512]{1,0:T(8,128)(2,1)S(1)}, bf16[256,512]{1,0:T(8,128)(2,1)S(1)}, u32[]{:S(2)}, u32[]{:S(2)}) collective-permute-start(bf16[256,512]{1,0:T(8,128)(2,1)S(1)} %slice.37), channel_id=1, source_target_pairs={{0,16},{8,24},{16,0},{24,8},{1,17},{9,25},{17,1},{25,9},{2,18},{10... | collective-permute-start | bytes 786440 | tf_op jit(solution)/shard_map/ppermute | solution.py:291
  38.2 24.4 %collective-permute-start.16 = (bf16[128,1024]{1,0:T(8,128)(2,1)S(1)}, bf16[128,1024]{1,0:T(8,128)(2,1)S(1)}, u32[]{:S(2)}, u32[]{:S(2)}) collective-permute-start(bf16[128,1024]{1,0:T(8,128)(2,1)S(1)} %collective-permute-done.15.refs_0_), channel_id=1, source_target_pairs={{0,8},{8,0},{16,24},{24,16},{1,9},{9,1},{17,25},{25,17},{2,10},{10... | collective-permute-start | bytes 786440 | tf_op jit(solution)/shard_map/ppermute | solution.py:291
  38.7 25.3 %collective-permute-start.17 = (bf16[128,1024]{1,0:T(8,128)(2,1)S(1)}, bf16[128,1024]{1,0:T(8,128)(2,1)S(1)}, u32[]{:S(2)}, u32[]{:S(2)}) collective-permute-start(bf16[128,1024]{1,0:T(8,128)(2,1)S(1)} %collective-permute-done.15.refs_0_), channel_id=1, source_target_pairs={{0,16},{8,24},{16,0},{24,8},{1,17},{9,25},{17,1},{25,9},{2,18},{10... | collective-permute-start | bytes 786440 | tf_op jit(solution)/shard_map/ppermute | solution.py:291
  39.7 24.4 %collective-permute-start.18 = (bf16[128,1024]{1,0:T(8,128)(2,1)S(1)}, bf16[128,1024]{1,0:T(8,128)(2,1)S(1)}, u32[]{:S(2)}, u32[]{:S(2)}) collective-permute-start(bf16[128,1024]{1,0:T(8,128)(2,1)S(1)} %collective-permute-done.15.refs_0_), channel_id=1, source_target_pairs={{0,24},{8,16},{16,8},{24,0},{1,25},{9,17},{17,9},{25,1},{2,26},{10... | collective-permute-start | bytes 786440 | tf_op jit(solution)/shard_map/ppermute | solution.py:291
  45.8 15.1 %collective-permute-start.8 = (bf16[2,128,512]{2,1,0:T(8,128)(2,1)S(1)}, bf16[2,128,512]{2,1,0:T(8,128)(2,1)S(1)}, u32[]{:S(2)}, u32[]{:S(2)}) collective-permute-start(bf16[2,128,512]{2,1,0:T(8,128)(2,1)S(1)} %get-tuple-element.38), channel_id=1, source_target_pairs={{0,8},{8,0},{16,24},{24,16},{1,9},{9,1},{17,25},{25,17},{2,10},{10... | collective-permute-start | bytes 786440 | tf_op jit(solution)/shard_map/ppermute | solution.py:291
  54.1 19.1 %collective-permute-start.12 = (bf16[256,512]{1,0:T(8,128)(2,1)S(1)}, bf16[256,512]{1,0:T(8,128)(2,1)S(1)}, u32[]{:S(2)}, u32[]{:S(2)}) collective-permute-start(bf16[256,512]{1,0:T(8,128)(2,1)S(1)} %get-tuple-element.44), channel_id=1, source_target_pairs={{0,24},{8,16},{16,8},{24,0},{1,25},{9,17},{17,9},{25,1},{2,26},{10... | collective-permute-start | bytes 786440 | tf_op jit(solution)/shard_map/ppermute | solution.py:291
  60.9 12.3 %collective-permute-start.11 = (bf16[256,512]{1,0:T(8,128)(2,1)S(1)}, bf16[256,512]{1,0:T(8,128)(2,1)S(1)}, u32[]{:S(2)}, u32[]{:S(2)}) collective-permute-start(bf16[256,512]{1,0:T(8,128)(2,1)S(1)} %get-tuple-element.43), channel_id=1, source_target_pairs={{0,16},{8,24},{16,0},{24,8},{1,17},{9,25},{17,1},{25,9},{2,18},{10... | collective-permute-start | bytes 786440 | tf_op jit(solution)/shard_map/ppermute | solution.py:291
  62.6 10.6 %collective-permute-start.10 = (bf16[256,512]{1,0:T(8,128)(2,1)S(1)}, bf16[256,512]{1,0:T(8,128)(2,1)S(1)}, u32[]{:S(2)}, u32[]{:S(2)}) collective-permute-start(bf16[256,512]{1,0:T(8,128)(2,1)S(1)} %get-tuple-element.42), channel_id=1, source_target_pairs={{0,8},{8,0},{16,24},{24,16},{1,9},{9,1},{17,25},{25,17},{2,10},{10... | collective-permute-start | bytes 786440 | tf_op jit(solution)/shard_map/ppermute | solution.py:291
  73.2 16.1 %collective-permute-start.23 = (bf16[2,1024,1024]{2,1,0:T(8,128)(2,1)S(1)}, bf16[2,1024,1024]{2,1,0:T(8,128)(2,1)S(1)}, u32[]{:S(2)}, u32[]{:S(2)}) collective-permute-start(bf16[2,1024,1024]{2,1,0:T(8,128)(2,1)S(1)} %convolution_convert_fusion), channel_id=1, source_target_pairs={{0,1},{1,0},{2,3},{3,2},{4,5},{5,4},{6,7},{7,6},{8,9},{9,8},{10,11... | collective-permute-start | bytes 12582920 | tf_op jit(solution)/shard_map/ppermute | solution.py:288
  73.3 15.9 %collective-permute-start.9 = (bf16[128,512]{1,0:T(8,128)(2,1)S(1)}, bf16[128,512]{1,0:T(8,128)(2,1)S(1)}, u32[]{:S(2)}, u32[]{:S(2)}) collective-permute-start(bf16[128,512]{1,0:T(8,128)(2,1)S(1)} %fusion.2), channel_id=1, source_target_pairs={{0,16},{8,24},{16,0},{24,8},{1,17},{9,25},{17,1},{25,9},{2,18},{10... | collective-permute-start | bytes 393224 | tf_op jit(solution)/shard_map/ppermute | solution.py:291
  73.9 7.3 %collective-permute-start.21 = (bf16[128,512]{1,0:T(8,128)(2,1)S(1)}, bf16[128,512]{1,0:T(8,128)(2,1)S(1)}, u32[]{:S(2)}, u32[]{:S(2)}) collective-permute-start(bf16[128,512]{1,0:T(8,128)(2,1)S(1)} %get-tuple-element.58), channel_id=1, source_target_pairs={{0,24},{8,16},{16,8},{24,0},{1,25},{9,17},{17,9},{25,1},{2,26},{10... | collective-permute-start | bytes 393224 | tf_op jit(solution)/shard_map/ppermute | solution.py:291
  75.4 9.4 %collective-permute-start.20 = (bf16[128,512]{1,0:T(8,128)(2,1)S(1)}, bf16[128,512]{1,0:T(8,128)(2,1)S(1)}, u32[]{:S(2)}, u32[]{:S(2)}) collective-permute-start(bf16[128,512]{1,0:T(8,128)(2,1)S(1)} %get-tuple-element.56), channel_id=1, source_target_pairs={{0,16},{8,24},{16,0},{24,8},{1,17},{9,25},{17,1},{25,9},{2,18},{10... | collective-permute-start | bytes 393224 | tf_op jit(solution)/shard_map/ppermute | solution.py:291
  75.7 10.8 %collective-permute-start.19 = (bf16[128,512]{1,0:T(8,128)(2,1)S(1)}, bf16[128,512]{1,0:T(8,128)(2,1)S(1)}, u32[]{:S(2)}, u32[]{:S(2)}) collective-permute-start(bf16[128,512]{1,0:T(8,128)(2,1)S(1)} %get-tuple-element.54), channel_id=1, source_target_pairs={{0,8},{8,0},{16,24},{24,16},{1,9},{9,1},{17,25},{25,17},{2,10},{10... | collective-permute-start | bytes 393224 | tf_op jit(solution)/shard_map/ppermute | solution.py:291
  81.2 16.3 %collective-permute-start.13 = (bf16[128,512]{1,0:T(8,128)(2,1)S(1)}, bf16[128,512]{1,0:T(8,128)(2,1)S(1)}, u32[]{:S(2)}, u32[]{:S(2)}) collective-permute-start(bf16[128,512]{1,0:T(8,128)(2,1)S(1)} %get-tuple-element.64), channel_id=1, source_target_pairs={{0,6},{2,0},{4,2},{6,4},{1,7},{3,1},{5,3},{7,5},{8,14},{10,8},{12,... | collective-permute-start | bytes 393224 | tf_op jit(solution)/shard_map/ppermute | solution.py:294
  84.9 12.6 %collective-permute-start.14 = (bf16[128,512]{1,0:T(8,128)(2,1)S(1)}, bf16[128,512]{1,0:T(8,128)(2,1)S(1)}, u32[]{:S(2)}, u32[]{:S(2)}) collective-permute-start(bf16[128,512]{1,0:T(8,128)(2,1)S(1)} %get-tuple-element.63), channel_id=1, source_target_pairs={{0,2},{2,4},{4,6},{6,0},{1,3},{3,5},{5,7},{7,1},{8,10},{10,12},{12... | collective-permute-start | bytes 393224 | tf_op jit(solution)/shard_map/ppermute | solution.py:294
  86.5 11.0 %collective-permute-start.22 = (bf16[128,512]{1,0:T(8,128)(2,1)S(1)}, bf16[128,512]{1,0:T(8,128)(2,1)S(1)}, u32[]{:S(2)}, u32[]{:S(2)}) collective-permute-start(bf16[128,512]{1,0:T(8,128)(2,1)S(1)} %add_convert_fusion.1), channel_id=1, source_target_pairs={{0,4},{2,6},{4,0},{6,2},{1,5},{3,7},{5,1},{7,3},{8,12},{10,14},{12... | collective-permute-start | bytes 393224 | tf_op jit(solution)/shard_map/ppermute | solution.py:294
  (1 other events, 1.2 us)

commit v15 on v14

--- a/solution.py
+++ b/solution.py
@@ -334,16 +334,15 @@
         near = spread(jnp.concatenate([after(moved[0], pair[0]), moved[1]], 0))
         far = after(moved[2], *near[1:3])
         far = [far] + [across(far, j) for j in (1, 2, 3)]
-        back, got_own = collect_pair([pair[0], after(pair[1], *near[3:])], 1)
         kept, (blocks,) = expert_rows(None, [near], [(2 * capacity, None)], weights, everything, capacity, kept)
         total, got = collect(blocks)
-        backs = [back, shift(total[:capacity], -1), shift(total[capacity:], -3)]
-        far[0] = after(far[0], got_own)
+        backs = [shift(total[:capacity], -1), shift(total[capacity:], -3)]
         kept, (blocks,) = expert_rows(None, [far], [(capacity, None)], weights, everything, 3 * capacity, kept)
         others = other_halves(kept)
         grads = weight_grads(*kept, swap(after(others, *got)))
-        total, _ = collect([blocks[0]] + [after(b, got[0], others) for b in blocks[1:]])
-        backs.append(after(shift(total, -2), *grads))
+        total, last = collect([blocks[0]] + [after(b, got[0], others) for b in blocks[1:]])
+        back, _ = collect_pair([pair[0], after(pair[1], others)], 1)
+        backs = [back] + backs + [after(shift(total, -2), *grads)]
         shifts = [0] + shifts
     else:
         rows = experts * capacity

time: 98.9 us -> 97.2 us (0.983)
  starting transfers between devices: 36.8 us -> 35.4 us
    ppermute x6, waiting for transfers between devices: 4.94 us -> 0.98 us  [shift(): lax.ppermute(x, 'expert', [(i, (i + k) % experts) for i in range(experts)])]
    ppermute x15, waiting for transfers between devices: 20.8 us -> 24.4 us  [across(): return lax.ppermute(x, 'tensor', [(i, i ^ j) for i in range(tensor_size)])]
    ppermute x6, starting transfers between devices: 15.6 us -> 13.9 us  [shift(): lax.ppermute(x, 'expert', [(i, (i + k) % experts) for i in range(experts)])]
where the time goes in v15:
time: 97.2 us; the launch traced here: 96.9 us
  starting transfers between devices  35.4 us (36%)
  Pallas kernels  28.4 us (29%)
  waiting for transfers between devices  25.4 us (26%)
  local copies, waits for them, and re-layouts  4.15 us (4%)
  matrix products  2.38 us (2%)
    ppermute x15, waiting for transfers between devices, across(): return lax.ppermute(x, 'tensor', [(i, i ^ j) for i in range(tensor_size)])  24.4 us
    pallas_call x3, Pallas kernels, expert_rows(): pl.pallas_call(functools.partial(expert_kernel, counts_in, base, groups,...  20.9 us
    ppermute x15, starting transfers between devices, across(): return lax.ppermute(x, 'tensor', [(i, i ^ j) for i in range(tensor_size)])  20.8 us
    ppermute x6, starting transfers between devices, shift(): lax.ppermute(x, 'expert', [(i, (i + k) % experts) for i in range(experts)])  13.9 us
    unnamed x19, local copies, waits for them, and re-layouts  4.08 us
    pallas_call x1, Pallas kernels, weight_grads(): pl.pallas_call(weight_grad_kernel, out_shape=[jax.ShapeDtypeStruct((half,...  3.87 us
    pallas_call x1, Pallas kernels, place(): pl.pallas_call(functools.partial(place_kernel, spans, shifts, capacity),...  2.41 us
    dot_general x1, matrix products, other_halves(): lax.dot_general(rows[:, :, width // 2:], acts, dims, preferred_element_ty...  2.38 us
  transfers between devices with their start and end apart: 24, of which 9 were waited for; matrix products, arithmetic and copies ran while one was open for 3% of the time, Pallas kernels for 28%

profile of v15, /device:TPU:0, one launch (start us, length us, event | category | flops | bytes accessed | tf_op | source)
XLA Modules:
  0.0 96.9 jit_solution(12498555237199788487)
XLA Ops:
  1.3 2.4 %place_rows.1 = (bf16[128,1024]{1,0:T(8,128)(2,1)}, bf16[128,1024]{1,0:T(8,128)(2,1)}, bf16[128,1024]{1,0:T(8,128)(2,1)}) custom-call(s32[1,256]{1,0:T(1,128)} %bitcast.22, s32[1,256]{1,0:T(1,128)} %bitcast.25, f32[1,256]{1,0:T(1,128)} %bitcast.28, bf16[256,2048]{1,0:T(8,128)(2,1)} %tokens.1, bf16[256,2048]{1,0:T(8,128)(2,1)} %grad_output.1), custom_call_target="tpu_custom_call" | custom-call | flops 1000 | bytes 1000 | tf_op jit(solution)/shard_map/place_rows/pallas_call | solution.py:90
  3.7 3.1 %collective-permute-start.3 = (bf16[128,1024]{1,0:T(8,128)(2,1)}, bf16[128,1024]{1,0:T(8,128)(2,1)S(1)}, u32[]{:S(2)}, u32[]{:S(2)}) collective-permute-start(bf16[128,1024]{1,0:T(8,128)(2,1)} %get-tuple-element.35), channel_id=1, source_target_pairs={{0,2},{2,4},{4,6},{6,0},{1,3},{3,5},{5,7},{7,1},{8,10},{10,12},{12... | collective-permute-start | bytes 786440 | tf_op jit(solution)/shard_map/ppermute | solution.py:294
  6.8 2.1 %collective-permute-start.4 = (bf16[128,1024]{1,0:T(8,128)(2,1)}, bf16[128,1024]{1,0:T(8,128)(2,1)S(1)}, u32[]{:S(2)}, u32[]{:S(2)}) collective-permute-start(bf16[128,1024]{1,0:T(8,128)(2,1)} %get-tuple-element.37), channel_id=1, source_target_pairs={{0,6},{2,0},{4,2},{6,4},{1,7},{3,1},{5,3},{7,5},{8,14},{10,8},{12,... | collective-permute-start | bytes 786440 | tf_op jit(solution)/shard_map/ppermute | solution.py:294
  8.9 1.6 %copy-done.1 = bf16[1,1024,1024]{2,1,0:T(8,128)(2,1)S(1)} copy-done((bf16[1,1024,1024]{2,1,0:T(8,128)(2,1)S(1)}, bf16[1,1024,1024]{2,1,0:T(8,128)(2,1)}, u32[]{:S(2)}) %copy-start.1) | copy-done | bytes 2097176
  10.5 1.2 %copy-done.3 = bf16[256,2048]{1,0:T(8,128)(2,1)S(1)} copy-done((bf16[256,2048]{1,0:T(8,128)(2,1)S(1)}, bf16[256,2048]{1,0:T(8,128)(2,1)}, u32[]{:S(2)}) %copy-start.3) | copy-done | bytes 1048600
  11.7 1.2 %copy-done.4 = bf16[256,2048]{1,0:T(8,128)(2,1)S(1)} copy-done((bf16[256,2048]{1,0:T(8,128)(2,1)S(1)}, bf16[256,2048]{1,0:T(8,128)(2,1)}, u32[]{:S(2)}) %copy-start.4) | copy-done | bytes 1048600
  12.9 7.1 %expert_rows.3 = (bf16[2,512,2048]{2,1,0:T(8,128)(2,1)S(1)}, bf16[2,512,1024]{2,1,0:T(8,128)(2,1)S(1)}, bf16[2,128,512]{2,1,0:T(8,128)(2,1)S(1)}, bf16[2,128,512]{2,1,0:T(8,128)(2,1)S(1)}) custom-call(s32[1,256]{1,0:T(1,128)S(1)} %bitcast.23, s32[1,256]{1,0:T(1,128)S(1)} %bitcast.26, f32[1,256]{1,0:T(1,128)S(1)} %bitcast.29, ...), custom_call_target="tpu_custom_call" | custom-call | flops 1610612736 | bytes 10485760 | tf_op jit(solution)/shard_map/expert_rows/pallas_call | solution.py:199
  20.6 1.9 %collective-permute-start.6 = (bf16[256,1024]{1,0:T(8,128)(2,1)S(1)}, bf16[256,1024]{1,0:T(8,128)(2,1)S(1)}, u32[]{:S(2)}, u32[]{:S(2)}) collective-permute-start(bf16[256,1024]{1,0:T(8,128)(2,1)S(1)} %constant_dynamic-update-slice_fusion.refs_0_), channel_id=1, source_target_pairs={{0,16},{8,24},{16,0},{24,8},{1,17},{9,25},{17,1},{25,9},{2,18},{10... | collective-permute-start | bytes 1572872 | tf_op jit(solution)/shard_map/ppermute | solution.py:291
  22.4 1.5 %collective-permute-start.5 = (bf16[256,1024]{1,0:T(8,128)(2,1)S(1)}, bf16[256,1024]{1,0:T(8,128)(2,1)S(1)}, u32[]{:S(2)}, u32[]{:S(2)}) collective-permute-start(bf16[256,1024]{1,0:T(8,128)(2,1)S(1)} %constant_dynamic-update-slice_fusion.refs_0_), channel_id=1, source_target_pairs={{0,8},{8,0},{16,24},{24,16},{1,9},{9,1},{17,25},{25,17},{2,10},{10... | collective-permute-start | bytes 1572872 | tf_op jit(solution)/shard_map/ppermute | solution.py:291
  23.9 2.6 %collective-permute-start.2 = (bf16[128,1024]{1,0:T(8,128)(2,1)S(1)}, bf16[128,1024]{1,0:T(8,128)(2,1)S(1)}, u32[]{:S(2)}, u32[]{:S(2)}) collective-permute-start(bf16[128,1024]{1,0:T(8,128)(2,1)S(1)} %copy-done.8), channel_id=1, source_target_pairs={{0,4},{2,6},{4,0},{6,2},{1,5},{3,7},{5,1},{7,3},{8,12},{10,14},{12... | collective-permute-start | bytes 786440 | tf_op jit(solution)/shard_map/ppermute | solution.py:294
  26.5 8.1 %collective-permute-done.6.refs_2_ = bf16[256,1024]{1,0:T(8,128)(2,1)S(1)} collective-permute-done((bf16[256,1024]{1,0:T(8,128)(2,1)S(1)}, bf16[256,1024]{1,0:T(8,128)(2,1)S(1)}, u32[]{:S(2)}, u32[]{:S(2)}) %collective-permute-start.6) | collective-permute-done | bytes 524320 | tf_op jit(solution)/shard_map/ppermute | solution.py:291
  34.6 1.8 %collective-permute-start.10 = (bf16[256,512]{1,0:T(8,128)(2,1)S(1)}, bf16[256,512]{1,0:T(8,128)(2,1)S(1)}, u32[]{:S(2)}, u32[]{:S(2)}) collective-permute-start(bf16[256,512]{1,0:T(8,128)(2,1)S(1)} %slice.36), channel_id=1, source_target_pairs={{0,8},{8,0},{16,24},{24,16},{1,9},{9,1},{17,25},{25,17},{2,10},{10... | collective-permute-start | bytes 786440 | tf_op jit(solution)/shard_map/ppermute | solution.py:291
  36.4 1.6 %collective-permute-start.11 = (bf16[256,512]{1,0:T(8,128)(2,1)S(1)}, bf16[256,512]{1,0:T(8,128)(2,1)S(1)}, u32[]{:S(2)}, u32[]{:S(2)}) collective-permute-start(bf16[256,512]{1,0:T(8,128)(2,1)S(1)} %slice.37), channel_id=1, source_target_pairs={{0,16},{8,24},{16,0},{24,8},{1,17},{9,25},{17,1},{25,9},{2,18},{10... | collective-permute-start | bytes 786440 | tf_op jit(solution)/shard_map/ppermute | solution.py:291
  39.1 1.1 %collective-permute-start.8 = (bf16[128,1024]{1,0:T(8,128)(2,1)S(1)}, bf16[128,1024]{1,0:T(8,128)(2,1)S(1)}, u32[]{:S(2)}, u32[]{:S(2)}) collective-permute-start(bf16[128,1024]{1,0:T(8,128)(2,1)S(1)} %collective-permute-done.2.refs_0_), channel_id=1, source_target_pairs={{0,16},{8,24},{16,0},{24,8},{1,17},{9,25},{17,1},{25,9},{2,18},{10... | collective-permute-start | bytes 786440 | tf_op jit(solution)/shard_map/ppermute | solution.py:291
  40.2 1.5 %collective-permute-start.7 = (bf16[128,1024]{1,0:T(8,128)(2,1)S(1)}, bf16[128,1024]{1,0:T(8,128)(2,1)S(1)}, u32[]{:S(2)}, u32[]{:S(2)}) collective-permute-start(bf16[128,1024]{1,0:T(8,128)(2,1)S(1)} %collective-permute-done.2.refs_0_), channel_id=1, source_target_pairs={{0,8},{8,0},{16,24},{24,16},{1,9},{9,1},{17,25},{25,17},{2,10},{10... | collective-permute-start | bytes 786440 | tf_op jit(solution)/shard_map/ppermute | solution.py:291
  41.7 2.3 %collective-permute-done.10.refs_3_ = bf16[256,512]{1,0:T(8,128)(2,1)S(1)} collective-permute-done((bf16[256,512]{1,0:T(8,128)(2,1)S(1)}, bf16[256,512]{1,0:T(8,128)(2,1)S(1)}, u32[]{:S(2)}, u32[]{:S(2)}) %collective-permute-start.10) | collective-permute-done | bytes 262176 | tf_op jit(solution)/shard_map/ppermute | solution.py:291
  44.0 7.4 %collective-permute-done.11.refs_4_ = bf16[256,512]{1,0:T(8,128)(2,1)S(1)} collective-permute-done((bf16[256,512]{1,0:T(8,128)(2,1)S(1)}, bf16[256,512]{1,0:T(8,128)(2,1)S(1)}, u32[]{:S(2)}, u32[]{:S(2)}) %collective-permute-start.11) | collective-permute-done | bytes 262176 | tf_op jit(solution)/shard_map/ppermute | solution.py:291
  51.4 7.1 %expert_rows.4 = (bf16[2,512,2048]{2,1,0:T(8,128)(2,1)S(1)}, bf16[2,512,1024]{2,1,0:T(8,128)(2,1)S(1)}, bf16[256,512]{1,0:T(8,128)(2,1)S(1)}, bf16[256,512]{1,0:...) custom-call(bf16[256,1024]{1,0:T(8,128)(2,1)S(1)} %constant_dynamic-, ...), custom_call_target="tpu_custom_call", output_to_operand_aliasing={{0}: (9, {}), {1}: (10, {})} | custom-call | flops 3221225472 | bytes 12582912 | tf_op jit(solution)/shard_map/expert_rows/pallas_call | solution.py:199
  58.5 1.2 %collective-permute-start.14 = (bf16[256,512]{1,0:T(8,128)(2,1)S(1)}, bf16[256,512]{1,0:T(8,128)(2,1)S(1)}, u32[]{:S(2)}, u32[]{:S(2)}) collective-permute-start(bf16[256,512]{1,0:T(8,128)(2,1)S(1)} %get-tuple-element.47), channel_id=1, source_target_pairs={{0,8},{8,0},{16,24},{24,16},{1,9},{9,1},{17,25},{25,17},{2,10},{10... | collective-permute-start | bytes 786440 | tf_op jit(solution)/shard_map/ppermute | solution.py:291
  60.6 1.4 %collective-permute-start.16 = (bf16[256,512]{1,0:T(8,128)(2,1)S(1)}, bf16[256,512]{1,0:T(8,128)(2,1)S(1)}, u32[]{:S(2)}, u32[]{:S(2)}) collective-permute-start(bf16[256,512]{1,0:T(8,128)(2,1)S(1)} %get-tuple-element.49), channel_id=1, source_target_pairs={{0,24},{8,16},{16,8},{24,0},{1,25},{9,17},{17,9},{25,1},{2,26},{10... | collective-permute-start | bytes 786440 | tf_op jit(solution)/shard_map/ppermute | solution.py:291
  62.1 6.7 %expert_rows.5 = (bf16[2,512,2048]{2,1,0:T(8,128)(2,1)S(1)}, bf16[2,512,1024]{2,1,0:T(8,128)(2,1)S(1)}, bf16[128,512]{1,0:T(8,128)(2,1)S(1)}, bf16[128,512]{1,0:...) custom-call(bf16[128,1024]{1,0:T(8,128)(2,1)S(1)} %collective-permut, ...), custom_call_target="tpu_custom_call", output_to_operand_aliasing={{0}: (8, {}), {1}: (9, {})} | custom-call | flops 1610612736 | bytes 10485760 | tf_op jit(solution)/shard_map/expert_rows/pallas_call | solution.py:199
  68.8 2.4 %convolution_convert_fusion = bf16[2,1024,1024]{2,1,0:T(8,128)(2,1)S(1)} fusion(bf16[2,512,1024]{2,1,0:T(8,128)(2,1)S(1)} %get-tuple-element.44.acts, bf16[2,512,2048]{2,1,0:T(8,128)(2,1)S(1)} %get-tuple-element.43.rows), kind=kOutput, calls=%fused_computation | convolution fusion | flops 2149580800 | bytes 8388608 | tf_op jit(solution)/shard_map/dot_general | solution.py:320
  71.3 1.2 %collective-permute-start.12 = (bf16[2,128,512]{2,1,0:T(8,128)(2,1)S(1)}, bf16[2,128,512]{2,1,0:T(8,128)(2,1)S(1)}, u32[]{:S(2)}, u32[]{:S(2)}) collective-permute-start(bf16[2,128,512]{2,1,0:T(8,128)(2,1)S(1)} %get-tuple-element.45), channel_id=1, source_target_pairs={{0,8},{8,0},{16,24},{24,16},{1,9},{9,1},{17,25},{25,17},{2,10},{10... | collective-permute-start | bytes 786440 | tf_op jit(solution)/shard_map/ppermute | solution.py:291
  72.7 1.6 %collective-permute-start.18 = (bf16[128,512]{1,0:T(8,128)(2,1)S(1)}, bf16[128,512]{1,0:T(8,128)(2,1)S(1)}, u32[]{:S(2)}, u32[]{:S(2)}) collective-permute-start(bf16[128,512]{1,0:T(8,128)(2,1)S(1)} %get-tuple-element.61), channel_id=1, source_target_pairs={{0,2},{2,4},{4,6},{6,0},{1,3},{3,5},{5,7},{7,1},{8,10},{10,12},{12... | collective-permute-start | bytes 393224 | tf_op jit(solution)/shard_map/ppermute | solution.py:294
  75.2 1.5 %collective-permute-start.20 = (bf16[128,512]{1,0:T(8,128)(2,1)S(1)}, bf16[128,512]{1,0:T(8,128)(2,1)S(1)}, u32[]{:S(2)}, u32[]{:S(2)}) collective-permute-start(bf16[128,512]{1,0:T(8,128)(2,1)S(1)} %get-tuple-element.54), channel_id=1, source_target_pairs={{0,16},{8,24},{16,0},{24,8},{1,17},{9,25},{17,1},{25,9},{2,18},{10... | collective-permute-start | bytes 393224 | tf_op jit(solution)/shard_map/ppermute | solution.py:291
  76.7 3.8 %collective-permute-done.12 = bf16[2,128,512]{2,1,0:T(8,128)(2,1)S(1)} collective-permute-done((bf16[2,128,512]{2,1,0:T(8,128)(2,1)S(1)}, bf16[2,128,512]{2,1,0:T(8,128)(2,1)S(1)}, u32[]{:S(2)}, u32[]{:S(2)}) %collective-permute-start.12) | collective-permute-done | bytes 262176 | tf_op jit(solution)/shard_map/ppermute | solution.py:291
  80.5 1.5 %collective-permute-start.21 = (bf16[128,512]{1,0:T(8,128)(2,1)S(1)}, bf16[128,512]{1,0:T(8,128)(2,1)S(1)}, u32[]{:S(2)}, u32[]{:S(2)}) collective-permute-start(bf16[128,512]{1,0:T(8,128)(2,1)S(1)} %get-tuple-element.56), channel_id=1, source_target_pairs={{0,24},{8,16},{16,8},{24,0},{1,25},{9,17},{17,9},{25,1},{2,26},{10... | collective-permute-start | bytes 393224 | tf_op jit(solution)/shard_map/ppermute | solution.py:291
  82.8 3.6 %collective-permute-start.17 = (bf16[128,512]{1,0:T(8,128)(2,1)S(1)}, bf16[128,512]{1,0:T(8,128)(2,1)S(1)}, u32[]{:S(2)}, u32[]{:S(2)}) collective-permute-start(bf16[128,512]{1,0:T(8,128)(2,1)S(1)} %get-tuple-element.62), channel_id=1, source_target_pairs={{0,6},{2,0},{4,2},{6,4},{1,7},{3,1},{5,3},{7,5},{8,14},{10,8},{12,... | collective-permute-start | bytes 393224 | tf_op jit(solution)/shard_map/ppermute | solution.py:294
  86.4 2.0 %collective-permute-start.13 = (bf16[128,512]{1,0:T(8,128)(2,1)S(1)}, bf16[128,512]{1,0:T(8,128)(2,1)S(1)}, u32[]{:S(2)}, u32[]{:S(2)}) collective-permute-start(bf16[128,512]{1,0:T(8,128)(2,1)S(1)} %fusion.2), channel_id=1, source_target_pairs={{0,16},{8,24},{16,0},{24,8},{1,17},{9,25},{17,1},{25,9},{2,18},{10... | collective-permute-start | bytes 393224 | tf_op jit(solution)/shard_map/ppermute | solution.py:291
  89.4 2.0 %collective-permute-done.13 = bf16[128,512]{1,0:T(8,128)(2,1)S(1)} collective-permute-done((bf16[128,512]{1,0:T(8,128)(2,1)S(1)}, bf16[128,512]{1,0:T(8,128)(2,1)S(1)}, u32[]{:S(2)}, u32[]{:S(2)}) %collective-permute-start.13) | collective-permute-done | bytes 131104 | tf_op jit(solution)/shard_map/ppermute | solution.py:291
  91.4 3.9 %weight_grads.1 = (bf16[1024,1024]{1,0:T(8,128)(2,1)}, bf16[1024,1024]{1,0:T(8,128)(2,1)}) custom-call(bf16[2,512,2048]{2,1,0:T(8,128)(2,1)S(1)} %get-tuple-element.43.rows, bf16[2,512,1024]{2,1,0:T(8,128)(2,1)S(1)} %get-tuple-element.44.acts, bf16[2,1024,1024]{2,1,0:T(8,128)(2,1)S(1)} %collective-permute-done.23.got), custom_call_target="tpu_custom_call" | custom-call | flops 1000 | bytes 1000 | tf_op jit(solution)/shard_map/weight_grads/pallas_call | solution.py:263
  95.7 1.2 %unplace_rows.1 = bf16[256,512]{1,0:T(8,128)(2,1)} custom-call(s32[1,256]{1,0:T(1,128)S(1)} %bitcast.24, s32[1,256]{1,0:T(1,128)S(1)} %bitcast.27, bf16[128,512]{1,0:T(8,128)(2,1)S(1)} %fusion.1.refs_0_, bf16[128,512]{1,0:T(8,128)(2,1)S(1)} %collective-permute-done.17.refs_1_, bf16[128,512]{1,0:T(8,128)(2,1)S(1)} %collective-permute-done.18.refs_2_, ...), custom_call_target="tpu_custom_call" | custom-call | flops 1000 | bytes 1000 | tf_op jit(solution)/shard_map/unplace_rows/pallas_call | solution.py:235
  (50 shorter events, 6.5 us)
Async XLA Ops:
  0.6 8.2 %copy-start = (bf16[1,1024,1024]{2,1,0:T(8,128)(2,1)S(1)}, bf16[1,1024,1024]{2,1,0:T(8,128)(2,1)}, u32[]{:S(2)}) copy-start(bf16[1,1024,1024]{2,1,0:T(8,128)(2,1)} %param.12) | copy-start | bytes 6291460
  0.6 8.2 %copy-start.6 = (s32[256,1]{0,1:T(1,128)S(1)}, s32[256,1]{0,1:T(1,128)}, u32[]{:S(2)}) copy-start(s32[256,1]{0,1:T(1,128)} %param.11) | copy-start | bytes 3076
  0.7 8.2 %copy-start.5 = (s32[256,1]{0,1:T(1,128)S(1)}, s32[256,1]{0,1:T(1,128)}, u32[]{:S(2)}) copy-start(s32[256,1]{0,1:T(1,128)} %param.10) | copy-start | bytes 3076
  0.7 8.2 %copy-start.7 = (f32[256]{0:T(256)S(1)}, f32[256]{0:T(256)}, u32[]{:S(2)}) copy-start(f32[256]{0:T(256)} %param.9) | copy-start | bytes 3076
  0.7 8.2 %collective-permute-start = (bf16[1024,1024]{1,0:T(8,128)(2,1)}, bf16[1024,1024]{1,0:T(8,128)(2,1)S(1)}, u32[]{:S(2)}, u32[]{:S(2)}) collective-permute-start(bf16[1024,1024]{1,0:T(8,128)(2,1)} %bitcast.14), channel_id=1, source_target_pairs={{0,1},{1,0},{2,3},{3,2},{4,5},{5,4},{6,7},{7,6},{8,9},{9,8},{10,11... | collective-permute-start | bytes 6291464 | tf_op jit(solution)/shard_map/ppermute | solution.py:288
  1.2 7.7 %collective-permute-start.1 = (bf16[1024,1024]{1,0:T(8,128)(2,1)}, bf16[1024,1024]{1,0:T(8,128)(2,1)S(1)}, u32[]{:S(2)}, u32[]{:S(2)}) collective-permute-start(bf16[1024,1024]{1,0:T(8,128)(2,1)} %bitcast.18), channel_id=1, source_target_pairs={{0,1},{1,0},{2,3},{3,2},{4,5},{5,4},{6,7},{7,6},{8,9},{9,8},{10,11... | collective-permute-start | bytes 6291464 | tf_op jit(solution)/shard_map/ppermute | solution.py:288
  3.7 16.4 %collective-permute-start.3 = (bf16[128,1024]{1,0:T(8,128)(2,1)}, bf16[128,1024]{1,0:T(8,128)(2,1)S(1)}, u32[]{:S(2)}, u32[]{:S(2)}) collective-permute-start(bf16[128,1024]{1,0:T(8,128)(2,1)} %get-tuple-element.35), channel_id=1, source_target_pairs={{0,2},{2,4},{4,6},{6,0},{1,3},{3,5},{5,7},{7,1},{8,10},{10,12},{12... | collective-permute-start | bytes 786440 | tf_op jit(solution)/shard_map/ppermute | solution.py:294
  6.8 13.8 %collective-permute-start.4 = (bf16[128,1024]{1,0:T(8,128)(2,1)}, bf16[128,1024]{1,0:T(8,128)(2,1)S(1)}, u32[]{:S(2)}, u32[]{:S(2)}) collective-permute-start(bf16[128,1024]{1,0:T(8,128)(2,1)} %get-tuple-element.37), channel_id=1, source_target_pairs={{0,6},{2,0},{4,2},{6,4},{1,7},{3,1},{5,3},{7,5},{8,14},{10,8},{12,... | collective-permute-start | bytes 786440 | tf_op jit(solution)/shard_map/ppermute | solution.py:294
  8.9 1.6 %copy-start.1 = (bf16[1,1024,1024]{2,1,0:T(8,128)(2,1)S(1)}, bf16[1,1024,1024]{2,1,0:T(8,128)(2,1)}, u32[]{:S(2)}) copy-start(bf16[1,1024,1024]{2,1,0:T(8,128)(2,1)} %param.13) | copy-start | bytes 6291460
  10.5 1.2 %copy-start.3 = (bf16[256,2048]{1,0:T(8,128)(2,1)S(1)}, bf16[256,2048]{1,0:T(8,128)(2,1)}, u32[]{:S(2)}) copy-start(bf16[256,2048]{1,0:T(8,128)(2,1)} %tokens.1) | copy-start | bytes 3145732
  12.9 11.0 %copy-start.8 = (bf16[128,1024]{1,0:T(8,128)(2,1)S(1)}, bf16[128,1024]{1,0:T(8,128)(2,1)}, u32[]{:S(2)}) copy-start(bf16[128,1024]{1,0:T(8,128)(2,1)} %get-tuple-element.34) | copy-start | bytes 786436
  20.1 31.3 %copy-start.2 = (bf16[1,1024,1024]{2,1,0:T(8,128)(2,1)S(1)}, bf16[1,1024,1024]{2,1,0:T(8,128)(2,1)}, u32[]{:S(2)}) copy-start(bf16[1,1024,1024]{2,1,0:T(8,128)(2,1)} %param.13) | copy-start | bytes 6291460
  20.6 14.1 %collective-permute-start.6 = (bf16[256,1024]{1,0:T(8,128)(2,1)S(1)}, bf16[256,1024]{1,0:T(8,128)(2,1)S(1)}, u32[]{:S(2)}, u32[]{:S(2)}) collective-permute-start(bf16[256,1024]{1,0:T(8,128)(2,1)S(1)} %constant_dynamic-update-slice_fusion.refs_0_), channel_id=1, source_target_pairs={{0,16},{8,24},{16,0},{24,8},{1,17},{9,25},{17,1},{25,9},{2,18},{10... | collective-permute-start | bytes 1572872 | tf_op jit(solution)/shard_map/ppermute | solution.py:291
  22.4 14.0 %collective-permute-start.5 = (bf16[256,1024]{1,0:T(8,128)(2,1)S(1)}, bf16[256,1024]{1,0:T(8,128)(2,1)S(1)}, u32[]{:S(2)}, u32[]{:S(2)}) collective-permute-start(bf16[256,1024]{1,0:T(8,128)(2,1)S(1)} %constant_dynamic-update-slice_fusion.refs_0_), channel_id=1, source_target_pairs={{0,8},{8,0},{16,24},{24,16},{1,9},{9,1},{17,25},{25,17},{2,10},{10... | collective-permute-start | bytes 1572872 | tf_op jit(solution)/shard_map/ppermute | solution.py:291
  23.9 14.3 %collective-permute-start.2 = (bf16[128,1024]{1,0:T(8,128)(2,1)S(1)}, bf16[128,1024]{1,0:T(8,128)(2,1)S(1)}, u32[]{:S(2)}, u32[]{:S(2)}) collective-permute-start(bf16[128,1024]{1,0:T(8,128)(2,1)S(1)} %copy-done.8), channel_id=1, source_target_pairs={{0,4},{2,6},{4,0},{6,2},{1,5},{3,7},{5,1},{7,3},{8,12},{10,14},{12... | collective-permute-start | bytes 786440 | tf_op jit(solution)/shard_map/ppermute | solution.py:294
  34.6 9.3 %collective-permute-start.10 = (bf16[256,512]{1,0:T(8,128)(2,1)S(1)}, bf16[256,512]{1,0:T(8,128)(2,1)S(1)}, u32[]{:S(2)}, u32[]{:S(2)}) collective-permute-start(bf16[256,512]{1,0:T(8,128)(2,1)S(1)} %slice.36), channel_id=1, source_target_pairs={{0,8},{8,0},{16,24},{24,16},{1,9},{9,1},{17,25},{25,17},{2,10},{10... | collective-permute-start | bytes 786440 | tf_op jit(solution)/shard_map/ppermute | solution.py:291
  36.4 14.9 %collective-permute-start.11 = (bf16[256,512]{1,0:T(8,128)(2,1)S(1)}, bf16[256,512]{1,0:T(8,128)(2,1)S(1)}, u32[]{:S(2)}, u32[]{:S(2)}) collective-permute-start(bf16[256,512]{1,0:T(8,128)(2,1)S(1)} %slice.37), channel_id=1, source_target_pairs={{0,16},{8,24},{16,0},{24,8},{1,17},{9,25},{17,1},{25,9},{2,18},{10... | collective-permute-start | bytes 786440 | tf_op jit(solution)/shard_map/ppermute | solution.py:291
  38.2 22.4 %collective-permute-start.9 = (bf16[128,1024]{1,0:T(8,128)(2,1)S(1)}, bf16[128,1024]{1,0:T(8,128)(2,1)S(1)}, u32[]{:S(2)}, u32[]{:S(2)}) collective-permute-start(bf16[128,1024]{1,0:T(8,128)(2,1)S(1)} %collective-permute-done.2.refs_0_), channel_id=1, source_target_pairs={{0,24},{8,16},{16,8},{24,0},{1,25},{9,17},{17,9},{25,1},{2,26},{10... | collective-permute-start | bytes 786440 | tf_op jit(solution)/shard_map/ppermute | solution.py:291
  39.1 22.9 %collective-permute-start.8 = (bf16[128,1024]{1,0:T(8,128)(2,1)S(1)}, bf16[128,1024]{1,0:T(8,128)(2,1)S(1)}, u32[]{:S(2)}, u32[]{:S(2)}) collective-permute-start(bf16[128,1024]{1,0:T(8,128)(2,1)S(1)} %collective-permute-done.2.refs_0_), channel_id=1, source_target_pairs={{0,16},{8,24},{16,0},{24,8},{1,17},{9,25},{17,1},{25,9},{2,18},{10... | collective-permute-start | bytes 786440 | tf_op jit(solution)/shard_map/ppermute | solution.py:291
  40.2 21.9 %collective-permute-start.7 = (bf16[128,1024]{1,0:T(8,128)(2,1)S(1)}, bf16[128,1024]{1,0:T(8,128)(2,1)S(1)}, u32[]{:S(2)}, u32[]{:S(2)}) collective-permute-start(bf16[128,1024]{1,0:T(8,128)(2,1)S(1)} %collective-permute-done.2.refs_0_), channel_id=1, source_target_pairs={{0,8},{8,0},{16,24},{24,16},{1,9},{9,1},{17,25},{25,17},{2,10},{10... | collective-permute-start | bytes 786440 | tf_op jit(solution)/shard_map/ppermute | solution.py:291
  58.5 12.7 %collective-permute-start.14 = (bf16[256,512]{1,0:T(8,128)(2,1)S(1)}, bf16[256,512]{1,0:T(8,128)(2,1)S(1)}, u32[]{:S(2)}, u32[]{:S(2)}) collective-permute-start(bf16[256,512]{1,0:T(8,128)(2,1)S(1)} %get-tuple-element.47), channel_id=1, source_target_pairs={{0,8},{8,0},{16,24},{24,16},{1,9},{9,1},{17,25},{25,17},{2,10},{10... | collective-permute-start | bytes 786440 | tf_op jit(solution)/shard_map/ppermute | solution.py:291
  59.7 11.5 %collective-permute-start.15 = (bf16[256,512]{1,0:T(8,128)(2,1)S(1)}, bf16[256,512]{1,0:T(8,128)(2,1)S(1)}, u32[]{:S(2)}, u32[]{:S(2)}) collective-permute-start(bf16[256,512]{1,0:T(8,128)(2,1)S(1)} %get-tuple-element.48), channel_id=1, source_target_pairs={{0,16},{8,24},{16,0},{24,8},{1,17},{9,25},{17,1},{25,9},{2,18},{10... | collective-permute-start | bytes 786440 | tf_op jit(solution)/shard_map/ppermute | solution.py:291
  60.6 10.6 %collective-permute-start.16 = (bf16[256,512]{1,0:T(8,128)(2,1)S(1)}, bf16[256,512]{1,0:T(8,128)(2,1)S(1)}, u32[]{:S(2)}, u32[]{:S(2)}) collective-permute-start(bf16[256,512]{1,0:T(8,128)(2,1)S(1)} %get-tuple-element.49), channel_id=1, source_target_pairs={{0,24},{8,16},{16,8},{24,0},{1,25},{9,17},{17,9},{25,1},{2,26},{10... | collective-permute-start | bytes 786440 | tf_op jit(solution)/shard_map/ppermute | solution.py:291
  71.2 20.2 %collective-permute-start.23 = (bf16[2,1024,1024]{2,1,0:T(8,128)(2,1)S(1)}, bf16[2,1024,1024]{2,1,0:T(8,128)(2,1)S(1)}, u32[]{:S(2)}, u32[]{:S(2)}) collective-permute-start(bf16[2,1024,1024]{2,1,0:T(8,128)(2,1)S(1)} %convolution_convert_fusion), channel_id=1, source_target_pairs={{0,1},{1,0},{2,3},{3,2},{4,5},{5,4},{6,7},{7,6},{8,9},{9,8},{10,11... | collective-permute-start | bytes 12582920 | tf_op jit(solution)/shard_map/ppermute | solution.py:288
  71.3 9.2 %collective-permute-start.12 = (bf16[2,128,512]{2,1,0:T(8,128)(2,1)S(1)}, bf16[2,128,512]{2,1,0:T(8,128)(2,1)S(1)}, u32[]{:S(2)}, u32[]{:S(2)}) collective-permute-start(bf16[2,128,512]{2,1,0:T(8,128)(2,1)S(1)} %get-tuple-element.45), channel_id=1, source_target_pairs={{0,8},{8,0},{16,24},{24,16},{1,9},{9,1},{17,25},{25,17},{2,10},{10... | collective-permute-start | bytes 786440 | tf_op jit(solution)/shard_map/ppermute | solution.py:291
  72.7 23.0 %collective-permute-start.18 = (bf16[128,512]{1,0:T(8,128)(2,1)S(1)}, bf16[128,512]{1,0:T(8,128)(2,1)S(1)}, u32[]{:S(2)}, u32[]{:S(2)}) collective-permute-start(bf16[128,512]{1,0:T(8,128)(2,1)S(1)} %get-tuple-element.61), channel_id=1, source_target_pairs={{0,2},{2,4},{4,6},{6,0},{1,3},{3,5},{5,7},{7,1},{8,10},{10,12},{12... | collective-permute-start | bytes 393224 | tf_op jit(solution)/shard_map/ppermute | solution.py:294
  74.3 8.5 %collective-permute-start.19 = (bf16[128,512]{1,0:T(8,128)(2,1)S(1)}, bf16[128,512]{1,0:T(8,128)(2,1)S(1)}, u32[]{:S(2)}, u32[]{:S(2)}) collective-permute-start(bf16[128,512]{1,0:T(8,128)(2,1)S(1)} %get-tuple-element.52), channel_id=1, source_target_pairs={{0,8},{8,0},{16,24},{24,16},{1,9},{9,1},{17,25},{25,17},{2,10},{10... | collective-permute-start | bytes 393224 | tf_op jit(solution)/shard_map/ppermute | solution.py:291
  75.2 11.2 %collective-permute-start.20 = (bf16[128,512]{1,0:T(8,128)(2,1)S(1)}, bf16[128,512]{1,0:T(8,128)(2,1)S(1)}, u32[]{:S(2)}, u32[]{:S(2)}) collective-permute-start(bf16[128,512]{1,0:T(8,128)(2,1)S(1)} %get-tuple-element.54), channel_id=1, source_target_pairs={{0,16},{8,24},{16,0},{24,8},{1,17},{9,25},{17,1},{25,9},{2,18},{10... | collective-permute-start | bytes 393224 | tf_op jit(solution)/shard_map/ppermute | solution.py:291
  80.5 7.9 %collective-permute-start.21 = (bf16[128,512]{1,0:T(8,128)(2,1)S(1)}, bf16[128,512]{1,0:T(8,128)(2,1)S(1)}, u32[]{:S(2)}, u32[]{:S(2)}) collective-permute-start(bf16[128,512]{1,0:T(8,128)(2,1)S(1)} %get-tuple-element.56), channel_id=1, source_target_pairs={{0,24},{8,16},{16,8},{24,0},{1,25},{9,17},{17,9},{25,1},{2,26},{10... | collective-permute-start | bytes 393224 | tf_op jit(solution)/shard_map/ppermute | solution.py:291
  82.8 12.9 %collective-permute-start.17 = (bf16[128,512]{1,0:T(8,128)(2,1)S(1)}, bf16[128,512]{1,0:T(8,128)(2,1)S(1)}, u32[]{:S(2)}, u32[]{:S(2)}) collective-permute-start(bf16[128,512]{1,0:T(8,128)(2,1)S(1)} %get-tuple-element.62), channel_id=1, source_target_pairs={{0,6},{2,0},{4,2},{6,4},{1,7},{3,1},{5,3},{7,5},{8,14},{10,8},{12,... | collective-permute-start | bytes 393224 | tf_op jit(solution)/shard_map/ppermute | solution.py:294
  86.4 5.0 %collective-permute-start.13 = (bf16[128,512]{1,0:T(8,128)(2,1)S(1)}, bf16[128,512]{1,0:T(8,128)(2,1)S(1)}, u32[]{:S(2)}, u32[]{:S(2)}) collective-permute-start(bf16[128,512]{1,0:T(8,128)(2,1)S(1)} %fusion.2), channel_id=1, source_target_pairs={{0,16},{8,24},{16,0},{24,8},{1,17},{9,25},{17,1},{25,9},{2,18},{10... | collective-permute-start | bytes 393224 | tf_op jit(solution)/shard_map/ppermute | solution.py:291
  88.5 7.2 %collective-permute-start.22 = (bf16[128,512]{1,0:T(8,128)(2,1)S(1)}, bf16[128,512]{1,0:T(8,128)(2,1)S(1)}, u32[]{:S(2)}, u32[]{:S(2)}) collective-permute-start(bf16[128,512]{1,0:T(8,128)(2,1)S(1)} %add_convert_fusion.1), channel_id=1, source_target_pairs={{0,4},{2,6},{4,0},{6,2},{1,5},{3,7},{5,1},{7,3},{8,12},{10,14},{12... | collective-permute-start | bytes 393224 | tf_op jit(solution)/shard_map/ppermute | solution.py:294
  (1 other events, 1.2 us)

commit v16 on v15

--- a/solution.py
+++ b/solution.py
@@ -333,7 +333,7 @@
         kept, (pair,) = expert_rows(own, None, [(capacity, 1)], weights, everything, 0, None)
         near = spread(jnp.concatenate([after(moved[0], pair[0]), moved[1]], 0))
         far = after(moved[2], *near[1:3])
-        far = [far] + [across(far, j) for j in (1, 2, 3)]
+        far = [far, across(far, 1), across(far, 2), across(after(far, *near[3:]), 3)]
         kept, (blocks,) = expert_rows(None, [near], [(2 * capacity, None)], weights, everything, capacity, kept)
         total, got = collect(blocks)
         backs = [shift(total[:capacity], -1), shift(total[capacity:], -3)]

time: 97.2 us -> 92.7 us (0.954)
  waiting for transfers between devices: 25.4 us -> 22.1 us
  starting transfers between devices: 35.4 us -> 34.2 us
    ppermute x15, waiting for transfers between devices: 24.4 us -> 21.5 us  [across(): return lax.ppermute(x, 'tensor', [(i, i ^ j) for i in range(tensor_size)])]
    ppermute x15, starting transfers between devices: 20.8 us -> 19.2 us  [across(): return lax.ppermute(x, 'tensor', [(i, i ^ j) for i in range(tensor_size)])]
  transfers between devices with their start and end apart: 24 -> 24, of which waited for: 9 -> 9; matrix products, arithmetic and copies ran while one was open for 3% -> 3% of each run, Pallas kernels for 28% -> 29%
where the time goes in v16:
time: 92.7 us; the launch traced here: 92.5 us
  starting transfers between devices  34.2 us (37%)
  Pallas kernels  28.4 us (31%)
  waiting for transfers between devices  22.1 us (24%)
  local copies, waits for them, and re-layouts  4.15 us (4%)
  matrix products  2.38 us (3%)
    ppermute x15, waiting for transfers between devices, across(): return lax.ppermute(x, 'tensor', [(i, i ^ j) for i in range(tensor_size)])  21.5 us
    pallas_call x3, Pallas kernels, expert_rows(): pl.pallas_call(functools.partial(expert_kernel, counts_in, base, groups,...  21 us
    ppermute x15, starting transfers between devices, across(): return lax.ppermute(x, 'tensor', [(i, i ^ j) for i in range(tensor_size)])  19.2 us
    ppermute x6, starting transfers between devices, shift(): lax.ppermute(x, 'expert', [(i, (i + k) % experts) for i in range(experts)])  14.3 us
    unnamed x19, local copies, waits for them, and re-layouts  4.08 us
    pallas_call x1, Pallas kernels, weight_grads(): pl.pallas_call(weight_grad_kernel, out_shape=[jax.ShapeDtypeStruct((half,...  3.86 us
    pallas_call x1, Pallas kernels, place(): pl.pallas_call(functools.partial(place_kernel, spans, shifts, capacity),...  2.41 us
    dot_general x1, matrix products, other_halves(): lax.dot_general(rows[:, :, width // 2:], acts, dims, preferred_element_ty...  2.38 us
  transfers between devices with their start and end apart: 24, of which 9 were waited for; matrix products, arithmetic and copies ran while one was open for 3% of the time, Pallas kernels for 29%

profile of v16, /device:TPU:0, one launch (start us, length us, event | category | flops | bytes accessed | tf_op | source)
XLA Modules:
  0.0 92.5 jit_solution(17979661525559387323)
XLA Ops:
  1.3 2.4 %place_rows.1 = (bf16[128,1024]{1,0:T(8,128)(2,1)}, bf16[128,1024]{1,0:T(8,128)(2,1)}, bf16[128,1024]{1,0:T(8,128)(2,1)}) custom-call(s32[1,256]{1,0:T(1,128)} %bitcast.22, s32[1,256]{1,0:T(1,128)} %bitcast.25, f32[1,256]{1,0:T(1,128)} %bitcast.28, bf16[256,2048]{1,0:T(8,128)(2,1)} %tokens.1, bf16[256,2048]{1,0:T(8,128)(2,1)} %grad_output.1), custom_call_target="tpu_custom_call" | custom-call | flops 1000 | bytes 1000 | tf_op jit(solution)/shard_map/place_rows/pallas_call | solution.py:90
  3.7 3.1 %collective-permute-start.3 = (bf16[128,1024]{1,0:T(8,128)(2,1)}, bf16[128,1024]{1,0:T(8,128)(2,1)S(1)}, u32[]{:S(2)}, u32[]{:S(2)}) collective-permute-start(bf16[128,1024]{1,0:T(8,128)(2,1)} %get-tuple-element.36), channel_id=1, source_target_pairs={{0,2},{2,4},{4,6},{6,0},{1,3},{3,5},{5,7},{7,1},{8,10},{10,12},{12... | collective-permute-start | bytes 786440 | tf_op jit(solution)/shard_map/ppermute | solution.py:294
  6.8 2.1 %collective-permute-start.4 = (bf16[128,1024]{1,0:T(8,128)(2,1)}, bf16[128,1024]{1,0:T(8,128)(2,1)S(1)}, u32[]{:S(2)}, u32[]{:S(2)}) collective-permute-start(bf16[128,1024]{1,0:T(8,128)(2,1)} %get-tuple-element.38), channel_id=1, source_target_pairs={{0,6},{2,0},{4,2},{6,4},{1,7},{3,1},{5,3},{7,5},{8,14},{10,8},{12,... | collective-permute-start | bytes 786440 | tf_op jit(solution)/shard_map/ppermute | solution.py:294
  8.9 1.6 %copy-done.1 = bf16[1,1024,1024]{2,1,0:T(8,128)(2,1)S(1)} copy-done((bf16[1,1024,1024]{2,1,0:T(8,128)(2,1)S(1)}, bf16[1,1024,1024]{2,1,0:T(8,128)(2,1)}, u32[]{:S(2)}) %copy-start.1) | copy-done | bytes 2097176
  10.5 1.2 %copy-done.3 = bf16[256,2048]{1,0:T(8,128)(2,1)S(1)} copy-done((bf16[256,2048]{1,0:T(8,128)(2,1)S(1)}, bf16[256,2048]{1,0:T(8,128)(2,1)}, u32[]{:S(2)}) %copy-start.3) | copy-done | bytes 1048600
  11.7 1.2 %copy-done.4 = bf16[256,2048]{1,0:T(8,128)(2,1)S(1)} copy-done((bf16[256,2048]{1,0:T(8,128)(2,1)S(1)}, bf16[256,2048]{1,0:T(8,128)(2,1)}, u32[]{:S(2)}) %copy-start.4) | copy-done | bytes 1048600
  12.9 7.1 %expert_rows.3 = (bf16[2,512,2048]{2,1,0:T(8,128)(2,1)S(1)}, bf16[2,512,1024]{2,1,0:T(8,128)(2,1)S(1)}, bf16[2,128,512]{2,1,0:T(8,128)(2,1)S(1)}, bf16[2,128,512]{2,1,0:T(8,128)(2,1)S(1)}) custom-call(s32[1,256]{1,0:T(1,128)S(1)} %bitcast.23, s32[1,256]{1,0:T(1,128)S(1)} %bitcast.26, f32[1,256]{1,0:T(1,128)S(1)} %bitcast.29, ...), custom_call_target="tpu_custom_call" | custom-call | flops 1610612736 | bytes 10485760 | tf_op jit(solution)/shard_map/expert_rows/pallas_call | solution.py:199
  20.6 1.9 %collective-permute-start.6 = (bf16[256,1024]{1,0:T(8,128)(2,1)S(1)}, bf16[256,1024]{1,0:T(8,128)(2,1)S(1)}, u32[]{:S(2)}, u32[]{:S(2)}) collective-permute-start(bf16[256,1024]{1,0:T(8,128)(2,1)S(1)} %constant_dynamic-update-slice_fusion.refs_0_), channel_id=1, source_target_pairs={{0,16},{8,24},{16,0},{24,8},{1,17},{9,25},{17,1},{25,9},{2,18},{10... | collective-permute-start | bytes 1572872 | tf_op jit(solution)/shard_map/ppermute | solution.py:291
  22.4 1.5 %collective-permute-start.5 = (bf16[256,1024]{1,0:T(8,128)(2,1)S(1)}, bf16[256,1024]{1,0:T(8,128)(2,1)S(1)}, u32[]{:S(2)}, u32[]{:S(2)}) collective-permute-start(bf16[256,1024]{1,0:T(8,128)(2,1)S(1)} %constant_dynamic-update-slice_fusion.refs_0_), channel_id=1, source_target_pairs={{0,8},{8,0},{16,24},{24,16},{1,9},{9,1},{17,25},{25,17},{2,10},{10... | collective-permute-start | bytes 1572872 | tf_op jit(solution)/shard_map/ppermute | solution.py:291
  23.9 2.6 %collective-permute-start.2 = (bf16[128,1024]{1,0:T(8,128)(2,1)S(1)}, bf16[128,1024]{1,0:T(8,128)(2,1)S(1)}, u32[]{:S(2)}, u32[]{:S(2)}) collective-permute-start(bf16[128,1024]{1,0:T(8,128)(2,1)S(1)} %copy-done.8), channel_id=1, source_target_pairs={{0,4},{2,6},{4,0},{6,2},{1,5},{3,7},{5,1},{7,3},{8,12},{10,14},{12... | collective-permute-start | bytes 786440 | tf_op jit(solution)/shard_map/ppermute | solution.py:294
  26.5 8.1 %collective-permute-done.6.refs_2_ = bf16[256,1024]{1,0:T(8,128)(2,1)S(1)} collective-permute-done((bf16[256,1024]{1,0:T(8,128)(2,1)S(1)}, bf16[256,1024]{1,0:T(8,128)(2,1)S(1)}, u32[]{:S(2)}, u32[]{:S(2)}) %collective-permute-start.6) | collective-permute-done | bytes 524320 | tf_op jit(solution)/shard_map/ppermute | solution.py:291
  34.6 1.8 %collective-permute-start.9 = (bf16[256,512]{1,0:T(8,128)(2,1)S(1)}, bf16[256,512]{1,0:T(8,128)(2,1)S(1)}, u32[]{:S(2)}, u32[]{:S(2)}) collective-permute-start(bf16[256,512]{1,0:T(8,128)(2,1)S(1)} %slice.36), channel_id=1, source_target_pairs={{0,8},{8,0},{16,24},{24,16},{1,9},{9,1},{17,25},{25,17},{2,10},{10... | collective-permute-start | bytes 786440 | tf_op jit(solution)/shard_map/ppermute | solution.py:291
  36.4 1.6 %collective-permute-start.10 = (bf16[256,512]{1,0:T(8,128)(2,1)S(1)}, bf16[256,512]{1,0:T(8,128)(2,1)S(1)}, u32[]{:S(2)}, u32[]{:S(2)}) collective-permute-start(bf16[256,512]{1,0:T(8,128)(2,1)S(1)} %slice.37), channel_id=1, source_target_pairs={{0,16},{8,24},{16,0},{24,8},{1,17},{9,25},{17,1},{25,9},{2,18},{10... | collective-permute-start | bytes 786440 | tf_op jit(solution)/shard_map/ppermute | solution.py:291
  39.7 4.3 %collective-permute-done.9.refs_3_ = bf16[256,512]{1,0:T(8,128)(2,1)S(1)} collective-permute-done((bf16[256,512]{1,0:T(8,128)(2,1)S(1)}, bf16[256,512]{1,0:T(8,128)(2,1)S(1)}, u32[]{:S(2)}, u32[]{:S(2)}) %collective-permute-start.9) | collective-permute-done | bytes 262176 | tf_op jit(solution)/shard_map/ppermute | solution.py:291
  44.0 1.8 %collective-permute-done.10.refs_4_ = bf16[256,512]{1,0:T(8,128)(2,1)S(1)} collective-permute-done((bf16[256,512]{1,0:T(8,128)(2,1)S(1)}, bf16[256,512]{1,0:T(8,128)(2,1)S(1)}, u32[]{:S(2)}, u32[]{:S(2)}) %collective-permute-start.10) | collective-permute-done | bytes 262176 | tf_op jit(solution)/shard_map/ppermute | solution.py:291
  45.8 1.5 %collective-permute-start.11 = (bf16[128,1024]{1,0:T(8,128)(2,1)S(1)}, bf16[128,1024]{1,0:T(8,128)(2,1)S(1)}, u32[]{:S(2)}, u32[]{:S(2)}) collective-permute-start(bf16[128,1024]{1,0:T(8,128)(2,1)S(1)} %collective-permute-done.2.refs_0_), channel_id=1, source_target_pairs={{0,24},{8,16},{16,8},{24,0},{1,25},{9,17},{17,9},{25,1},{2,26},{10... | collective-permute-start | bytes 786440 | tf_op jit(solution)/shard_map/ppermute | solution.py:291
  47.3 7.1 %expert_rows.4 = (bf16[2,512,2048]{2,1,0:T(8,128)(2,1)S(1)}, bf16[2,512,1024]{2,1,0:T(8,128)(2,1)S(1)}, bf16[256,512]{1,0:T(8,128)(2,1)S(1)}, bf16[256,512]{1,0:...) custom-call(bf16[256,1024]{1,0:T(8,128)(2,1)S(1)} %constant_dynamic-, ...), custom_call_target="tpu_custom_call", output_to_operand_aliasing={{0}: (9, {}), {1}: (10, {})} | custom-call | flops 3221225472 | bytes 12582912 | tf_op jit(solution)/shard_map/expert_rows/pallas_call | solution.py:199
  54.4 1.6 %collective-permute-start.14 = (bf16[256,512]{1,0:T(8,128)(2,1)S(1)}, bf16[256,512]{1,0:T(8,128)(2,1)S(1)}, u32[]{:S(2)}, u32[]{:S(2)}) collective-permute-start(bf16[256,512]{1,0:T(8,128)(2,1)S(1)} %get-tuple-element.49), channel_id=1, source_target_pairs={{0,8},{8,0},{16,24},{24,16},{1,9},{9,1},{17,25},{25,17},{2,10},{10... | collective-permute-start | bytes 786440 | tf_op jit(solution)/shard_map/ppermute | solution.py:291
  56.5 1.5 %collective-permute-start.16 = (bf16[256,512]{1,0:T(8,128)(2,1)S(1)}, bf16[256,512]{1,0:T(8,128)(2,1)S(1)}, u32[]{:S(2)}, u32[]{:S(2)}) collective-permute-start(bf16[256,512]{1,0:T(8,128)(2,1)S(1)} %get-tuple-element.51), channel_id=1, source_target_pairs={{0,24},{8,16},{16,8},{24,0},{1,25},{9,17},{17,9},{25,1},{2,26},{10... | collective-permute-start | bytes 786440 | tf_op jit(solution)/shard_map/ppermute | solution.py:291
  58.0 6.7 %expert_rows.5 = (bf16[2,512,2048]{2,1,0:T(8,128)(2,1)S(1)}, bf16[2,512,1024]{2,1,0:T(8,128)(2,1)S(1)}, bf16[128,512]{1,0:T(8,128)(2,1)S(1)}, bf16[128,512]{1,0:...) custom-call(bf16[128,1024]{1,0:T(8,128)(2,1)S(1)} %collective-permut, ...), custom_call_target="tpu_custom_call", output_to_operand_aliasing={{0}: (8, {}), {1}: (9, {})} | custom-call | flops 1610612736 | bytes 10485760 | tf_op jit(solution)/shard_map/expert_rows/pallas_call | solution.py:199
  64.7 2.4 %convolution_convert_fusion = bf16[2,1024,1024]{2,1,0:T(8,128)(2,1)S(1)} fusion(bf16[2,512,1024]{2,1,0:T(8,128)(2,1)S(1)} %get-tuple-element.46.acts, bf16[2,512,2048]{2,1,0:T(8,128)(2,1)S(1)} %get-tuple-element.45.rows), kind=kOutput, calls=%fused_computation | convolution fusion | flops 2149580800 | bytes 8388608 | tf_op jit(solution)/shard_map/dot_general | solution.py:320
  67.2 1.5 %collective-permute-start.12 = (bf16[2,128,512]{2,1,0:T(8,128)(2,1)S(1)}, bf16[2,128,512]{2,1,0:T(8,128)(2,1)S(1)}, u32[]{:S(2)}, u32[]{:S(2)}) collective-permute-start(bf16[2,128,512]{2,1,0:T(8,128)(2,1)S(1)} %get-tuple-element.47), channel_id=1, source_target_pairs={{0,8},{8,0},{16,24},{24,16},{1,9},{9,1},{17,25},{25,17},{2,10},{10... | collective-permute-start | bytes 786440 | tf_op jit(solution)/shard_map/ppermute | solution.py:291
  68.9 1.6 %collective-permute-start.18 = (bf16[128,512]{1,0:T(8,128)(2,1)S(1)}, bf16[128,512]{1,0:T(8,128)(2,1)S(1)}, u32[]{:S(2)}, u32[]{:S(2)}) collective-permute-start(bf16[128,512]{1,0:T(8,128)(2,1)S(1)} %get-tuple-element.63), channel_id=1, source_target_pairs={{0,2},{2,4},{4,6},{6,0},{1,3},{3,5},{5,7},{7,1},{8,10},{10,12},{12... | collective-permute-start | bytes 393224 | tf_op jit(solution)/shard_map/ppermute | solution.py:294
  71.1 1.1 %collective-permute-start.20 = (bf16[128,512]{1,0:T(8,128)(2,1)S(1)}, bf16[128,512]{1,0:T(8,128)(2,1)S(1)}, u32[]{:S(2)}, u32[]{:S(2)}) collective-permute-start(bf16[128,512]{1,0:T(8,128)(2,1)S(1)} %get-tuple-element.56), channel_id=1, source_target_pairs={{0,16},{8,24},{16,0},{24,8},{1,17},{9,25},{17,1},{25,9},{2,18},{10... | collective-permute-start | bytes 393224 | tf_op jit(solution)/shard_map/ppermute | solution.py:291
  72.2 4.2 %collective-permute-done.12 = bf16[2,128,512]{2,1,0:T(8,128)(2,1)S(1)} collective-permute-done((bf16[2,128,512]{2,1,0:T(8,128)(2,1)S(1)}, bf16[2,128,512]{2,1,0:T(8,128)(2,1)S(1)}, u32[]{:S(2)}, u32[]{:S(2)}) %collective-permute-start.12) | collective-permute-done | bytes 262176 | tf_op jit(solution)/shard_map/ppermute | solution.py:291
  76.3 1.4 %collective-permute-start.21 = (bf16[128,512]{1,0:T(8,128)(2,1)S(1)}, bf16[128,512]{1,0:T(8,128)(2,1)S(1)}, u32[]{:S(2)}, u32[]{:S(2)}) collective-permute-start(bf16[128,512]{1,0:T(8,128)(2,1)S(1)} %get-tuple-element.58), channel_id=1, source_target_pairs={{0,24},{8,16},{16,8},{24,0},{1,25},{9,17},{17,9},{25,1},{2,26},{10... | collective-permute-start | bytes 393224 | tf_op jit(solution)/shard_map/ppermute | solution.py:291
  78.7 3.6 %collective-permute-start.17 = (bf16[128,512]{1,0:T(8,128)(2,1)S(1)}, bf16[128,512]{1,0:T(8,128)(2,1)S(1)}, u32[]{:S(2)}, u32[]{:S(2)}) collective-permute-start(bf16[128,512]{1,0:T(8,128)(2,1)S(1)} %get-tuple-element.64), channel_id=1, source_target_pairs={{0,6},{2,0},{4,2},{6,4},{1,7},{3,1},{5,3},{7,5},{8,14},{10,8},{12,... | collective-permute-start | bytes 393224 | tf_op jit(solution)/shard_map/ppermute | solution.py:294
  82.3 1.3 %collective-permute-start.13 = (bf16[128,512]{1,0:T(8,128)(2,1)S(1)}, bf16[128,512]{1,0:T(8,128)(2,1)S(1)}, u32[]{:S(2)}, u32[]{:S(2)}) collective-permute-start(bf16[128,512]{1,0:T(8,128)(2,1)S(1)} %fusion.2), channel_id=1, source_target_pairs={{0,16},{8,24},{16,0},{24,8},{1,17},{9,25},{17,1},{25,9},{2,18},{10... | collective-permute-start | bytes 393224 | tf_op jit(solution)/shard_map/ppermute | solution.py:291
  83.7 1.4 %collective-permute-start.22 = (bf16[128,512]{1,0:T(8,128)(2,1)S(1)}, bf16[128,512]{1,0:T(8,128)(2,1)S(1)}, u32[]{:S(2)}, u32[]{:S(2)}) collective-permute-start(bf16[128,512]{1,0:T(8,128)(2,1)S(1)} %add_convert_fusion.1), channel_id=1, source_target_pairs={{0,4},{2,6},{4,0},{6,2},{1,5},{3,7},{5,1},{7,3},{8,12},{10,14},{12... | collective-permute-start | bytes 393224 | tf_op jit(solution)/shard_map/ppermute | solution.py:294
  85.1 2.2 %collective-permute-done.13 = bf16[128,512]{1,0:T(8,128)(2,1)S(1)} collective-permute-done((bf16[128,512]{1,0:T(8,128)(2,1)S(1)}, bf16[128,512]{1,0:T(8,128)(2,1)S(1)}, u32[]{:S(2)}, u32[]{:S(2)}) %collective-permute-start.13) | collective-permute-done | bytes 131104 | tf_op jit(solution)/shard_map/ppermute | solution.py:291
  87.3 3.9 %weight_grads.1 = (bf16[1024,1024]{1,0:T(8,128)(2,1)}, bf16[1024,1024]{1,0:T(8,128)(2,1)}) custom-call(bf16[2,512,2048]{2,1,0:T(8,128)(2,1)S(1)} %get-tuple-element.45.rows, bf16[2,512,1024]{2,1,0:T(8,128)(2,1)S(1)} %get-tuple-element.46.acts, bf16[2,1024,1024]{2,1,0:T(8,128)(2,1)S(1)} %collective-permute-done.23.got), custom_call_target="tpu_custom_call" | custom-call | flops 1000 | bytes 1000 | tf_op jit(solution)/shard_map/weight_grads/pallas_call | solution.py:263
  91.3 1.2 %unplace_rows.1 = bf16[256,512]{1,0:T(8,128)(2,1)} custom-call(s32[1,256]{1,0:T(1,128)S(1)} %bitcast.24, s32[1,256]{1,0:T(1,128)S(1)} %bitcast.27, bf16[128,512]{1,0:T(8,128)(2,1)S(1)} %fusion.1.refs_0_, bf16[128,512]{1,0:T(8,128)(2,1)S(1)} %collective-permute-done.17.refs_1_, bf16[128,512]{1,0:T(8,128)(2,1)S(1)} %collective-permute-done.18.refs_2_, ...), custom_call_target="tpu_custom_call" | custom-call | flops 1000 | bytes 1000 | tf_op jit(solution)/shard_map/unplace_rows/pallas_call | solution.py:235
  (50 shorter events, 5.2 us)
Async XLA Ops:
  0.6 8.2 %copy-start = (bf16[1,1024,1024]{2,1,0:T(8,128)(2,1)S(1)}, bf16[1,1024,1024]{2,1,0:T(8,128)(2,1)}, u32[]{:S(2)}) copy-start(bf16[1,1024,1024]{2,1,0:T(8,128)(2,1)} %param.12) | copy-start | bytes 6291460
  0.6 8.2 %copy-start.6 = (s32[256,1]{0,1:T(1,128)S(1)}, s32[256,1]{0,1:T(1,128)}, u32[]{:S(2)}) copy-start(s32[256,1]{0,1:T(1,128)} %param.11) | copy-start | bytes 3076
  0.7 8.2 %copy-start.5 = (s32[256,1]{0,1:T(1,128)S(1)}, s32[256,1]{0,1:T(1,128)}, u32[]{:S(2)}) copy-start(s32[256,1]{0,1:T(1,128)} %param.10) | copy-start | bytes 3076
  0.7 8.2 %copy-start.7 = (f32[256]{0:T(256)S(1)}, f32[256]{0:T(256)}, u32[]{:S(2)}) copy-start(f32[256]{0:T(256)} %param.9) | copy-start | bytes 3076
  0.7 8.2 %collective-permute-start = (bf16[1024,1024]{1,0:T(8,128)(2,1)}, bf16[1024,1024]{1,0:T(8,128)(2,1)S(1)}, u32[]{:S(2)}, u32[]{:S(2)}) collective-permute-start(bf16[1024,1024]{1,0:T(8,128)(2,1)} %bitcast.14), channel_id=1, source_target_pairs={{0,1},{1,0},{2,3},{3,2},{4,5},{5,4},{6,7},{7,6},{8,9},{9,8},{10,11... | collective-permute-start | bytes 6291464 | tf_op jit(solution)/shard_map/ppermute | solution.py:288
  1.2 7.7 %collective-permute-start.1 = (bf16[1024,1024]{1,0:T(8,128)(2,1)}, bf16[1024,1024]{1,0:T(8,128)(2,1)S(1)}, u32[]{:S(2)}, u32[]{:S(2)}) collective-permute-start(bf16[1024,1024]{1,0:T(8,128)(2,1)} %bitcast.18), channel_id=1, source_target_pairs={{0,1},{1,0},{2,3},{3,2},{4,5},{5,4},{6,7},{7,6},{8,9},{9,8},{10,11... | collective-permute-start | bytes 6291464 | tf_op jit(solution)/shard_map/ppermute | solution.py:288
  3.7 16.4 %collective-permute-start.3 = (bf16[128,1024]{1,0:T(8,128)(2,1)}, bf16[128,1024]{1,0:T(8,128)(2,1)S(1)}, u32[]{:S(2)}, u32[]{:S(2)}) collective-permute-start(bf16[128,1024]{1,0:T(8,128)(2,1)} %get-tuple-element.36), channel_id=1, source_target_pairs={{0,2},{2,4},{4,6},{6,0},{1,3},{3,5},{5,7},{7,1},{8,10},{10,12},{12... | collective-permute-start | bytes 786440 | tf_op jit(solution)/shard_map/ppermute | solution.py:294
  6.8 13.8 %collective-permute-start.4 = (bf16[128,1024]{1,0:T(8,128)(2,1)}, bf16[128,1024]{1,0:T(8,128)(2,1)S(1)}, u32[]{:S(2)}, u32[]{:S(2)}) collective-permute-start(bf16[128,1024]{1,0:T(8,128)(2,1)} %get-tuple-element.38), channel_id=1, source_target_pairs={{0,6},{2,0},{4,2},{6,4},{1,7},{3,1},{5,3},{7,5},{8,14},{10,8},{12,... | collective-permute-start | bytes 786440 | tf_op jit(solution)/shard_map/ppermute | solution.py:294
  8.9 1.6 %copy-start.1 = (bf16[1,1024,1024]{2,1,0:T(8,128)(2,1)S(1)}, bf16[1,1024,1024]{2,1,0:T(8,128)(2,1)}, u32[]{:S(2)}) copy-start(bf16[1,1024,1024]{2,1,0:T(8,128)(2,1)} %param.13) | copy-start | bytes 6291460
  10.5 1.2 %copy-start.3 = (bf16[256,2048]{1,0:T(8,128)(2,1)S(1)}, bf16[256,2048]{1,0:T(8,128)(2,1)}, u32[]{:S(2)}) copy-start(bf16[256,2048]{1,0:T(8,128)(2,1)} %tokens.1) | copy-start | bytes 3145732
  12.9 11.0 %copy-start.8 = (bf16[128,1024]{1,0:T(8,128)(2,1)S(1)}, bf16[128,1024]{1,0:T(8,128)(2,1)}, u32[]{:S(2)}) copy-start(bf16[128,1024]{1,0:T(8,128)(2,1)} %get-tuple-element.35) | copy-start | bytes 786436
  20.1 27.2 %copy-start.2 = (bf16[1,1024,1024]{2,1,0:T(8,128)(2,1)S(1)}, bf16[1,1024,1024]{2,1,0:T(8,128)(2,1)}, u32[]{:S(2)}) copy-start(bf16[1,1024,1024]{2,1,0:T(8,128)(2,1)} %param.13) | copy-start | bytes 6291460
  20.6 14.1 %collective-permute-start.6 = (bf16[256,1024]{1,0:T(8,128)(2,1)S(1)}, bf16[256,1024]{1,0:T(8,128)(2,1)S(1)}, u32[]{:S(2)}, u32[]{:S(2)}) collective-permute-start(bf16[256,1024]{1,0:T(8,128)(2,1)S(1)} %constant_dynamic-update-slice_fusion.refs_0_), channel_id=1, source_target_pairs={{0,16},{8,24},{16,0},{24,8},{1,17},{9,25},{17,1},{25,9},{2,18},{10... | collective-permute-start | bytes 1572872 | tf_op jit(solution)/shard_map/ppermute | solution.py:291
  22.4 14.0 %collective-permute-start.5 = (bf16[256,1024]{1,0:T(8,128)(2,1)S(1)}, bf16[256,1024]{1,0:T(8,128)(2,1)S(1)}, u32[]{:S(2)}, u32[]{:S(2)}) collective-permute-start(bf16[256,1024]{1,0:T(8,128)(2,1)S(1)} %constant_dynamic-update-slice_fusion.refs_0_), channel_id=1, source_target_pairs={{0,8},{8,0},{16,24},{24,16},{1,9},{9,1},{17,25},{25,17},{2,10},{10... | collective-permute-start | bytes 1572872 | tf_op jit(solution)/shard_map/ppermute | solution.py:291
  23.9 14.3 %collective-permute-start.2 = (bf16[128,1024]{1,0:T(8,128)(2,1)S(1)}, bf16[128,1024]{1,0:T(8,128)(2,1)S(1)}, u32[]{:S(2)}, u32[]{:S(2)}) collective-permute-start(bf16[128,1024]{1,0:T(8,128)(2,1)S(1)} %copy-done.8), channel_id=1, source_target_pairs={{0,4},{2,6},{4,0},{6,2},{1,5},{3,7},{5,1},{7,3},{8,12},{10,14},{12... | collective-permute-start | bytes 786440 | tf_op jit(solution)/shard_map/ppermute | solution.py:294
  34.6 9.3 %collective-permute-start.9 = (bf16[256,512]{1,0:T(8,128)(2,1)S(1)}, bf16[256,512]{1,0:T(8,128)(2,1)S(1)}, u32[]{:S(2)}, u32[]{:S(2)}) collective-permute-start(bf16[256,512]{1,0:T(8,128)(2,1)S(1)} %slice.36), channel_id=1, source_target_pairs={{0,8},{8,0},{16,24},{24,16},{1,9},{9,1},{17,25},{25,17},{2,10},{10... | collective-permute-start | bytes 786440 | tf_op jit(solution)/shard_map/ppermute | solution.py:291
  36.4 9.3 %collective-permute-start.10 = (bf16[256,512]{1,0:T(8,128)(2,1)S(1)}, bf16[256,512]{1,0:T(8,128)(2,1)S(1)}, u32[]{:S(2)}, u32[]{:S(2)}) collective-permute-start(bf16[256,512]{1,0:T(8,128)(2,1)S(1)} %slice.37), channel_id=1, source_target_pairs={{0,16},{8,24},{16,0},{24,8},{1,17},{9,25},{17,1},{25,9},{2,18},{10... | collective-permute-start | bytes 786440 | tf_op jit(solution)/shard_map/ppermute | solution.py:291
  38.2 18.3 %collective-permute-start.8 = (bf16[128,1024]{1,0:T(8,128)(2,1)S(1)}, bf16[128,1024]{1,0:T(8,128)(2,1)S(1)}, u32[]{:S(2)}, u32[]{:S(2)}) collective-permute-start(bf16[128,1024]{1,0:T(8,128)(2,1)S(1)} %collective-permute-done.2.refs_0_), channel_id=1, source_target_pairs={{0,16},{8,24},{16,0},{24,8},{1,17},{9,25},{17,1},{25,9},{2,18},{10... | collective-permute-start | bytes 786440 | tf_op jit(solution)/shard_map/ppermute | solution.py:291
  38.7 19.2 %collective-permute-start.7 = (bf16[128,1024]{1,0:T(8,128)(2,1)S(1)}, bf16[128,1024]{1,0:T(8,128)(2,1)S(1)}, u32[]{:S(2)}, u32[]{:S(2)}) collective-permute-start(bf16[128,1024]{1,0:T(8,128)(2,1)S(1)} %collective-permute-done.2.refs_0_), channel_id=1, source_target_pairs={{0,8},{8,0},{16,24},{24,16},{1,9},{9,1},{17,25},{25,17},{2,10},{10... | collective-permute-start | bytes 786440 | tf_op jit(solution)/shard_map/ppermute | solution.py:291
  45.8 12.2 %collective-permute-start.11 = (bf16[128,1024]{1,0:T(8,128)(2,1)S(1)}, bf16[128,1024]{1,0:T(8,128)(2,1)S(1)}, u32[]{:S(2)}, u32[]{:S(2)}) collective-permute-start(bf16[128,1024]{1,0:T(8,128)(2,1)S(1)} %collective-permute-done.2.refs_0_), channel_id=1, source_target_pairs={{0,24},{8,16},{16,8},{24,0},{1,25},{9,17},{17,9},{25,1},{2,26},{10... | collective-permute-start | bytes 786440 | tf_op jit(solution)/shard_map/ppermute | solution.py:291
  54.4 12.7 %collective-permute-start.14 = (bf16[256,512]{1,0:T(8,128)(2,1)S(1)}, bf16[256,512]{1,0:T(8,128)(2,1)S(1)}, u32[]{:S(2)}, u32[]{:S(2)}) collective-permute-start(bf16[256,512]{1,0:T(8,128)(2,1)S(1)} %get-tuple-element.49), channel_id=1, source_target_pairs={{0,8},{8,0},{16,24},{24,16},{1,9},{9,1},{17,25},{25,17},{2,10},{10... | collective-permute-start | bytes 786440 | tf_op jit(solution)/shard_map/ppermute | solution.py:291
  56.0 11.1 %collective-permute-start.15 = (bf16[256,512]{1,0:T(8,128)(2,1)S(1)}, bf16[256,512]{1,0:T(8,128)(2,1)S(1)}, u32[]{:S(2)}, u32[]{:S(2)}) collective-permute-start(bf16[256,512]{1,0:T(8,128)(2,1)S(1)} %get-tuple-element.50), channel_id=1, source_target_pairs={{0,16},{8,24},{16,0},{24,8},{1,17},{9,25},{17,1},{25,9},{2,18},{10... | collective-permute-start | bytes 786440 | tf_op jit(solution)/shard_map/ppermute | solution.py:291
  56.5 10.6 %collective-permute-start.16 = (bf16[256,512]{1,0:T(8,128)(2,1)S(1)}, bf16[256,512]{1,0:T(8,128)(2,1)S(1)}, u32[]{:S(2)}, u32[]{:S(2)}) collective-permute-start(bf16[256,512]{1,0:T(8,128)(2,1)S(1)} %get-tuple-element.51), channel_id=1, source_target_pairs={{0,24},{8,16},{16,8},{24,0},{1,25},{9,17},{17,9},{25,1},{2,26},{10... | collective-permute-start | bytes 786440 | tf_op jit(solution)/shard_map/ppermute | solution.py:291
  67.1 20.2 %collective-permute-start.23 = (bf16[2,1024,1024]{2,1,0:T(8,128)(2,1)S(1)}, bf16[2,1024,1024]{2,1,0:T(8,128)(2,1)S(1)}, u32[]{:S(2)}, u32[]{:S(2)}) collective-permute-start(bf16[2,1024,1024]{2,1,0:T(8,128)(2,1)S(1)} %convolution_convert_fusion), channel_id=1, source_target_pairs={{0,1},{1,0},{2,3},{3,2},{4,5},{5,4},{6,7},{7,6},{8,9},{9,8},{10,11... | collective-permute-start | bytes 12582920 | tf_op jit(solution)/shard_map/ppermute | solution.py:288
  67.2 9.2 %collective-permute-start.12 = (bf16[2,128,512]{2,1,0:T(8,128)(2,1)S(1)}, bf16[2,128,512]{2,1,0:T(8,128)(2,1)S(1)}, u32[]{:S(2)}, u32[]{:S(2)}) collective-permute-start(bf16[2,128,512]{2,1,0:T(8,128)(2,1)S(1)} %get-tuple-element.47), channel_id=1, source_target_pairs={{0,8},{8,0},{16,24},{24,16},{1,9},{9,1},{17,25},{25,17},{2,10},{10... | collective-permute-start | bytes 786440 | tf_op jit(solution)/shard_map/ppermute | solution.py:291
  68.9 22.4 %collective-permute-start.18 = (bf16[128,512]{1,0:T(8,128)(2,1)S(1)}, bf16[128,512]{1,0:T(8,128)(2,1)S(1)}, u32[]{:S(2)}, u32[]{:S(2)}) collective-permute-start(bf16[128,512]{1,0:T(8,128)(2,1)S(1)} %get-tuple-element.63), channel_id=1, source_target_pairs={{0,2},{2,4},{4,6},{6,0},{1,3},{3,5},{5,7},{7,1},{8,10},{10,12},{12... | collective-permute-start | bytes 393224 | tf_op jit(solution)/shard_map/ppermute | solution.py:294
  70.5 8.2 %collective-permute-start.19 = (bf16[128,512]{1,0:T(8,128)(2,1)S(1)}, bf16[128,512]{1,0:T(8,128)(2,1)S(1)}, u32[]{:S(2)}, u32[]{:S(2)}) collective-permute-start(bf16[128,512]{1,0:T(8,128)(2,1)S(1)} %get-tuple-element.54), channel_id=1, source_target_pairs={{0,8},{8,0},{16,24},{24,16},{1,9},{9,1},{17,25},{25,17},{2,10},{10... | collective-permute-start | bytes 393224 | tf_op jit(solution)/shard_map/ppermute | solution.py:291
  71.1 11.2 %collective-permute-start.20 = (bf16[128,512]{1,0:T(8,128)(2,1)S(1)}, bf16[128,512]{1,0:T(8,128)(2,1)S(1)}, u32[]{:S(2)}, u32[]{:S(2)}) collective-permute-start(bf16[128,512]{1,0:T(8,128)(2,1)S(1)} %get-tuple-element.56), channel_id=1, source_target_pairs={{0,16},{8,24},{16,0},{24,8},{1,17},{9,25},{17,1},{25,9},{2,18},{10... | collective-permute-start | bytes 393224 | tf_op jit(solution)/shard_map/ppermute | solution.py:291
  76.3 7.3 %collective-permute-start.21 = (bf16[128,512]{1,0:T(8,128)(2,1)S(1)}, bf16[128,512]{1,0:T(8,128)(2,1)S(1)}, u32[]{:S(2)}, u32[]{:S(2)}) collective-permute-start(bf16[128,512]{1,0:T(8,128)(2,1)S(1)} %get-tuple-element.58), channel_id=1, source_target_pairs={{0,24},{8,16},{16,8},{24,0},{1,25},{9,17},{17,9},{25,1},{2,26},{10... | collective-permute-start | bytes 393224 | tf_op jit(solution)/shard_map/ppermute | solution.py:291
  78.7 12.6 %collective-permute-start.17 = (bf16[128,512]{1,0:T(8,128)(2,1)S(1)}, bf16[128,512]{1,0:T(8,128)(2,1)S(1)}, u32[]{:S(2)}, u32[]{:S(2)}) collective-permute-start(bf16[128,512]{1,0:T(8,128)(2,1)S(1)} %get-tuple-element.64), channel_id=1, source_target_pairs={{0,6},{2,0},{4,2},{6,4},{1,7},{3,1},{5,3},{7,5},{8,14},{10,8},{12,... | collective-permute-start | bytes 393224 | tf_op jit(solution)/shard_map/ppermute | solution.py:294
  82.3 5.0 %collective-permute-start.13 = (bf16[128,512]{1,0:T(8,128)(2,1)S(1)}, bf16[128,512]{1,0:T(8,128)(2,1)S(1)}, u32[]{:S(2)}, u32[]{:S(2)}) collective-permute-start(bf16[128,512]{1,0:T(8,128)(2,1)S(1)} %fusion.2), channel_id=1, source_target_pairs={{0,16},{8,24},{16,0},{24,8},{1,17},{9,25},{17,1},{25,9},{2,18},{10... | collective-permute-start | bytes 393224 | tf_op jit(solution)/shard_map/ppermute | solution.py:291
  83.7 7.6 %collective-permute-start.22 = (bf16[128,512]{1,0:T(8,128)(2,1)S(1)}, bf16[128,512]{1,0:T(8,128)(2,1)S(1)}, u32[]{:S(2)}, u32[]{:S(2)}) collective-permute-start(bf16[128,512]{1,0:T(8,128)(2,1)S(1)} %add_convert_fusion.1), channel_id=1, source_target_pairs={{0,4},{2,6},{4,0},{6,2},{1,5},{3,7},{5,1},{7,3},{8,12},{10,14},{12... | collective-permute-start | bytes 393224 | tf_op jit(solution)/shard_map/ppermute | solution.py:294
  (1 other events, 1.2 us)

commit v17 on v16

--- a/solution.py
+++ b/solution.py
@@ -246,7 +246,7 @@
 def weight_grad_kernel(rows, acts, got, up_out, down_out, total, sem):
     copies = Copies(sem)
     half = total.shape[1]
-    step = 128
+    step = 256
     leave = []
     for i, out in enumerate((up_out, down_out)):
         for n in range(0, half, step):

time: 92.7 us -> 92.7 us (level)
  no operation moved by 1% of the time
where the time goes in v17:
time: 92.7 us; the launch traced here: 92.5 us
  starting transfers between devices  34.2 us (37%)
  Pallas kernels  28 us (30%)
  waiting for transfers between devices  22.5 us (24%)
  local copies, waits for them, and re-layouts  4.15 us (4%)
  matrix products  2.38 us (3%)
    ppermute x15, waiting for transfers between devices, across(): return lax.ppermute(x, 'tensor', [(i, i ^ j) for i in range(tensor_size)])  21.5 us
    pallas_call x3, Pallas kernels, expert_rows(): pl.pallas_call(functools.partial(expert_kernel, counts_in, base, groups,...  21 us
    ppermute x15, starting transfers between devices, across(): return lax.ppermute(x, 'tensor', [(i, i ^ j) for i in range(tensor_size)])  19.2 us
    ppermute x6, starting transfers between devices, shift(): lax.ppermute(x, 'expert', [(i, (i + k) % experts) for i in range(experts)])  14.3 us
    unnamed x19, local copies, waits for them, and re-layouts  4.08 us
    pallas_call x1, Pallas kernels, weight_grads(): pl.pallas_call(weight_grad_kernel, out_shape=[jax.ShapeDtypeStruct((half,...  3.46 us
    pallas_call x1, Pallas kernels, place(): pl.pallas_call(functools.partial(place_kernel, spans, shifts, capacity),...  2.41 us
    dot_general x1, matrix products, other_halves(): lax.dot_general(rows[:, :, width // 2:], acts, dims, preferred_element_ty...  2.38 us
  transfers between devices with their start and end apart: 24, of which 9 were waited for; matrix products, arithmetic and copies ran while one was open for 3% of the time, Pallas kernels for 29%

profile of v17, /device:TPU:0, one launch (start us, length us, event | category | flops | bytes accessed | tf_op | source)
XLA Modules:
  0.0 92.5 jit_solution(5500018725044538826)
XLA Ops:
  1.3 2.4 %place_rows.1 = (bf16[128,1024]{1,0:T(8,128)(2,1)}, bf16[128,1024]{1,0:T(8,128)(2,1)}, bf16[128,1024]{1,0:T(8,128)(2,1)}) custom-call(s32[1,256]{1,0:T(1,128)} %bitcast.22, s32[1,256]{1,0:T(1,128)} %bitcast.25, f32[1,256]{1,0:T(1,128)} %bitcast.28, bf16[256,2048]{1,0:T(8,128)(2,1)} %tokens.1, bf16[256,2048]{1,0:T(8,128)(2,1)} %grad_output.1), custom_call_target="tpu_custom_call" | custom-call | flops 1000 | bytes 1000 | tf_op jit(solution)/shard_map/place_rows/pallas_call | solution.py:90
  3.7 3.1 %collective-permute-start.3 = (bf16[128,1024]{1,0:T(8,128)(2,1)}, bf16[128,1024]{1,0:T(8,128)(2,1)S(1)}, u32[]{:S(2)}, u32[]{:S(2)}) collective-permute-start(bf16[128,1024]{1,0:T(8,128)(2,1)} %get-tuple-element.36), channel_id=1, source_target_pairs={{0,2},{2,4},{4,6},{6,0},{1,3},{3,5},{5,7},{7,1},{8,10},{10,12},{12... | collective-permute-start | bytes 786440 | tf_op jit(solution)/shard_map/ppermute | solution.py:294
  6.8 2.1 %collective-permute-start.4 = (bf16[128,1024]{1,0:T(8,128)(2,1)}, bf16[128,1024]{1,0:T(8,128)(2,1)S(1)}, u32[]{:S(2)}, u32[]{:S(2)}) collective-permute-start(bf16[128,1024]{1,0:T(8,128)(2,1)} %get-tuple-element.38), channel_id=1, source_target_pairs={{0,6},{2,0},{4,2},{6,4},{1,7},{3,1},{5,3},{7,5},{8,14},{10,8},{12,... | collective-permute-start | bytes 786440 | tf_op jit(solution)/shard_map/ppermute | solution.py:294
  8.9 1.6 %copy-done.1 = bf16[1,1024,1024]{2,1,0:T(8,128)(2,1)S(1)} copy-done((bf16[1,1024,1024]{2,1,0:T(8,128)(2,1)S(1)}, bf16[1,1024,1024]{2,1,0:T(8,128)(2,1)}, u32[]{:S(2)}) %copy-start.1) | copy-done | bytes 2097176
  10.5 1.2 %copy-done.3 = bf16[256,2048]{1,0:T(8,128)(2,1)S(1)} copy-done((bf16[256,2048]{1,0:T(8,128)(2,1)S(1)}, bf16[256,2048]{1,0:T(8,128)(2,1)}, u32[]{:S(2)}) %copy-start.3) | copy-done | bytes 1048600
  11.7 1.2 %copy-done.4 = bf16[256,2048]{1,0:T(8,128)(2,1)S(1)} copy-done((bf16[256,2048]{1,0:T(8,128)(2,1)S(1)}, bf16[256,2048]{1,0:T(8,128)(2,1)}, u32[]{:S(2)}) %copy-start.4) | copy-done | bytes 1048600
  12.9 7.1 %expert_rows.3 = (bf16[2,512,2048]{2,1,0:T(8,128)(2,1)S(1)}, bf16[2,512,1024]{2,1,0:T(8,128)(2,1)S(1)}, bf16[2,128,512]{2,1,0:T(8,128)(2,1)S(1)}, bf16[2,128,512]{2,1,0:T(8,128)(2,1)S(1)}) custom-call(s32[1,256]{1,0:T(1,128)S(1)} %bitcast.23, s32[1,256]{1,0:T(1,128)S(1)} %bitcast.26, f32[1,256]{1,0:T(1,128)S(1)} %bitcast.29, ...), custom_call_target="tpu_custom_call" | custom-call | flops 1610612736 | bytes 10485760 | tf_op jit(solution)/shard_map/expert_rows/pallas_call | solution.py:199
  20.6 1.9 %collective-permute-start.6 = (bf16[256,1024]{1,0:T(8,128)(2,1)S(1)}, bf16[256,1024]{1,0:T(8,128)(2,1)S(1)}, u32[]{:S(2)}, u32[]{:S(2)}) collective-permute-start(bf16[256,1024]{1,0:T(8,128)(2,1)S(1)} %constant_dynamic-update-slice_fusion.refs_0_), channel_id=1, source_target_pairs={{0,16},{8,24},{16,0},{24,8},{1,17},{9,25},{17,1},{25,9},{2,18},{10... | collective-permute-start | bytes 1572872 | tf_op jit(solution)/shard_map/ppermute | solution.py:291
  22.4 1.5 %collective-permute-start.5 = (bf16[256,1024]{1,0:T(8,128)(2,1)S(1)}, bf16[256,1024]{1,0:T(8,128)(2,1)S(1)}, u32[]{:S(2)}, u32[]{:S(2)}) collective-permute-start(bf16[256,1024]{1,0:T(8,128)(2,1)S(1)} %constant_dynamic-update-slice_fusion.refs_0_), channel_id=1, source_target_pairs={{0,8},{8,0},{16,24},{24,16},{1,9},{9,1},{17,25},{25,17},{2,10},{10... | collective-permute-start | bytes 1572872 | tf_op jit(solution)/shard_map/ppermute | solution.py:291
  23.9 2.6 %collective-permute-start.2 = (bf16[128,1024]{1,0:T(8,128)(2,1)S(1)}, bf16[128,1024]{1,0:T(8,128)(2,1)S(1)}, u32[]{:S(2)}, u32[]{:S(2)}) collective-permute-start(bf16[128,1024]{1,0:T(8,128)(2,1)S(1)} %copy-done.8), channel_id=1, source_target_pairs={{0,4},{2,6},{4,0},{6,2},{1,5},{3,7},{5,1},{7,3},{8,12},{10,14},{12... | collective-permute-start | bytes 786440 | tf_op jit(solution)/shard_map/ppermute | solution.py:294
  26.5 8.1 %collective-permute-done.6.refs_2_ = bf16[256,1024]{1,0:T(8,128)(2,1)S(1)} collective-permute-done((bf16[256,1024]{1,0:T(8,128)(2,1)S(1)}, bf16[256,1024]{1,0:T(8,128)(2,1)S(1)}, u32[]{:S(2)}, u32[]{:S(2)}) %collective-permute-start.6) | collective-permute-done | bytes 524320 | tf_op jit(solution)/shard_map/ppermute | solution.py:291
  34.6 1.8 %collective-permute-start.9 = (bf16[256,512]{1,0:T(8,128)(2,1)S(1)}, bf16[256,512]{1,0:T(8,128)(2,1)S(1)}, u32[]{:S(2)}, u32[]{:S(2)}) collective-permute-start(bf16[256,512]{1,0:T(8,128)(2,1)S(1)} %slice.36), channel_id=1, source_target_pairs={{0,8},{8,0},{16,24},{24,16},{1,9},{9,1},{17,25},{25,17},{2,10},{10... | collective-permute-start | bytes 786440 | tf_op jit(solution)/shard_map/ppermute | solution.py:291
  36.4 1.6 %collective-permute-start.10 = (bf16[256,512]{1,0:T(8,128)(2,1)S(1)}, bf16[256,512]{1,0:T(8,128)(2,1)S(1)}, u32[]{:S(2)}, u32[]{:S(2)}) collective-permute-start(bf16[256,512]{1,0:T(8,128)(2,1)S(1)} %slice.37), channel_id=1, source_target_pairs={{0,16},{8,24},{16,0},{24,8},{1,17},{9,25},{17,1},{25,9},{2,18},{10... | collective-permute-start | bytes 786440 | tf_op jit(solution)/shard_map/ppermute | solution.py:291
  39.7 4.3 %collective-permute-done.9.refs_3_ = bf16[256,512]{1,0:T(8,128)(2,1)S(1)} collective-permute-done((bf16[256,512]{1,0:T(8,128)(2,1)S(1)}, bf16[256,512]{1,0:T(8,128)(2,1)S(1)}, u32[]{:S(2)}, u32[]{:S(2)}) %collective-permute-start.9) | collective-permute-done | bytes 262176 | tf_op jit(solution)/shard_map/ppermute | solution.py:291
  44.0 1.8 %collective-permute-done.10.refs_4_ = bf16[256,512]{1,0:T(8,128)(2,1)S(1)} collective-permute-done((bf16[256,512]{1,0:T(8,128)(2,1)S(1)}, bf16[256,512]{1,0:T(8,128)(2,1)S(1)}, u32[]{:S(2)}, u32[]{:S(2)}) %collective-permute-start.10) | collective-permute-done | bytes 262176 | tf_op jit(solution)/shard_map/ppermute | solution.py:291
  45.8 1.5 %collective-permute-start.11 = (bf16[128,1024]{1,0:T(8,128)(2,1)S(1)}, bf16[128,1024]{1,0:T(8,128)(2,1)S(1)}, u32[]{:S(2)}, u32[]{:S(2)}) collective-permute-start(bf16[128,1024]{1,0:T(8,128)(2,1)S(1)} %collective-permute-done.2.refs_0_), channel_id=1, source_target_pairs={{0,24},{8,16},{16,8},{24,0},{1,25},{9,17},{17,9},{25,1},{2,26},{10... | collective-permute-start | bytes 786440 | tf_op jit(solution)/shard_map/ppermute | solution.py:291
  47.3 7.1 %expert_rows.4 = (bf16[2,512,2048]{2,1,0:T(8,128)(2,1)S(1)}, bf16[2,512,1024]{2,1,0:T(8,128)(2,1)S(1)}, bf16[256,512]{1,0:T(8,128)(2,1)S(1)}, bf16[256,512]{1,0:...) custom-call(bf16[256,1024]{1,0:T(8,128)(2,1)S(1)} %constant_dynamic-, ...), custom_call_target="tpu_custom_call", output_to_operand_aliasing={{0}: (9, {}), {1}: (10, {})} | custom-call | flops 3221225472 | bytes 12582912 | tf_op jit(solution)/shard_map/expert_rows/pallas_call | solution.py:199
  54.4 1.6 %collective-permute-start.14 = (bf16[256,512]{1,0:T(8,128)(2,1)S(1)}, bf16[256,512]{1,0:T(8,128)(2,1)S(1)}, u32[]{:S(2)}, u32[]{:S(2)}) collective-permute-start(bf16[256,512]{1,0:T(8,128)(2,1)S(1)} %get-tuple-element.49), channel_id=1, source_target_pairs={{0,8},{8,0},{16,24},{24,16},{1,9},{9,1},{17,25},{25,17},{2,10},{10... | collective-permute-start | bytes 786440 | tf_op jit(solution)/shard_map/ppermute | solution.py:291
  56.5 1.5 %collective-permute-start.16 = (bf16[256,512]{1,0:T(8,128)(2,1)S(1)}, bf16[256,512]{1,0:T(8,128)(2,1)S(1)}, u32[]{:S(2)}, u32[]{:S(2)}) collective-permute-start(bf16[256,512]{1,0:T(8,128)(2,1)S(1)} %get-tuple-element.51), channel_id=1, source_target_pairs={{0,24},{8,16},{16,8},{24,0},{1,25},{9,17},{17,9},{25,1},{2,26},{10... | collective-permute-start | bytes 786440 | tf_op jit(solution)/shard_map/ppermute | solution.py:291
  58.0 6.7 %expert_rows.5 = (bf16[2,512,2048]{2,1,0:T(8,128)(2,1)S(1)}, bf16[2,512,1024]{2,1,0:T(8,128)(2,1)S(1)}, bf16[128,512]{1,0:T(8,128)(2,1)S(1)}, bf16[128,512]{1,0:...) custom-call(bf16[128,1024]{1,0:T(8,128)(2,1)S(1)} %collective-permut, ...), custom_call_target="tpu_custom_call", output_to_operand_aliasing={{0}: (8, {}), {1}: (9, {})} | custom-call | flops 1610612736 | bytes 10485760 | tf_op jit(solution)/shard_map/expert_rows/pallas_call | solution.py:199
  64.7 2.4 %convolution_convert_fusion = bf16[2,1024,1024]{2,1,0:T(8,128)(2,1)S(1)} fusion(bf16[2,512,1024]{2,1,0:T(8,128)(2,1)S(1)} %get-tuple-element.46.acts, bf16[2,512,2048]{2,1,0:T(8,128)(2,1)S(1)} %get-tuple-element.45.rows), kind=kOutput, calls=%fused_computation | convolution fusion | flops 2149580800 | bytes 8388608 | tf_op jit(solution)/shard_map/dot_general | solution.py:320
  67.2 1.5 %collective-permute-start.12 = (bf16[2,128,512]{2,1,0:T(8,128)(2,1)S(1)}, bf16[2,128,512]{2,1,0:T(8,128)(2,1)S(1)}, u32[]{:S(2)}, u32[]{:S(2)}) collective-permute-start(bf16[2,128,512]{2,1,0:T(8,128)(2,1)S(1)} %get-tuple-element.47), channel_id=1, source_target_pairs={{0,8},{8,0},{16,24},{24,16},{1,9},{9,1},{17,25},{25,17},{2,10},{10... | collective-permute-start | bytes 786440 | tf_op jit(solution)/shard_map/ppermute | solution.py:291
  68.9 1.6 %collective-permute-start.18 = (bf16[128,512]{1,0:T(8,128)(2,1)S(1)}, bf16[128,512]{1,0:T(8,128)(2,1)S(1)}, u32[]{:S(2)}, u32[]{:S(2)}) collective-permute-start(bf16[128,512]{1,0:T(8,128)(2,1)S(1)} %get-tuple-element.63), channel_id=1, source_target_pairs={{0,2},{2,4},{4,6},{6,0},{1,3},{3,5},{5,7},{7,1},{8,10},{10,12},{12... | collective-permute-start | bytes 393224 | tf_op jit(solution)/shard_map/ppermute | solution.py:294
  71.1 1.1 %collective-permute-start.20 = (bf16[128,512]{1,0:T(8,128)(2,1)S(1)}, bf16[128,512]{1,0:T(8,128)(2,1)S(1)}, u32[]{:S(2)}, u32[]{:S(2)}) collective-permute-start(bf16[128,512]{1,0:T(8,128)(2,1)S(1)} %get-tuple-element.56), channel_id=1, source_target_pairs={{0,16},{8,24},{16,0},{24,8},{1,17},{9,25},{17,1},{25,9},{2,18},{10... | collective-permute-start | bytes 393224 | tf_op jit(solution)/shard_map/ppermute | solution.py:291
  72.2 4.2 %collective-permute-done.12 = bf16[2,128,512]{2,1,0:T(8,128)(2,1)S(1)} collective-permute-done((bf16[2,128,512]{2,1,0:T(8,128)(2,1)S(1)}, bf16[2,128,512]{2,1,0:T(8,128)(2,1)S(1)}, u32[]{:S(2)}, u32[]{:S(2)}) %collective-permute-start.12) | collective-permute-done | bytes 262176 | tf_op jit(solution)/shard_map/ppermute | solution.py:291
  76.3 1.4 %collective-permute-start.21 = (bf16[128,512]{1,0:T(8,128)(2,1)S(1)}, bf16[128,512]{1,0:T(8,128)(2,1)S(1)}, u32[]{:S(2)}, u32[]{:S(2)}) collective-permute-start(bf16[128,512]{1,0:T(8,128)(2,1)S(1)} %get-tuple-element.58), channel_id=1, source_target_pairs={{0,24},{8,16},{16,8},{24,0},{1,25},{9,17},{17,9},{25,1},{2,26},{10... | collective-permute-start | bytes 393224 | tf_op jit(solution)/shard_map/ppermute | solution.py:291
  78.7 3.6 %collective-permute-start.17 = (bf16[128,512]{1,0:T(8,128)(2,1)S(1)}, bf16[128,512]{1,0:T(8,128)(2,1)S(1)}, u32[]{:S(2)}, u32[]{:S(2)}) collective-permute-start(bf16[128,512]{1,0:T(8,128)(2,1)S(1)} %get-tuple-element.64), channel_id=1, source_target_pairs={{0,6},{2,0},{4,2},{6,4},{1,7},{3,1},{5,3},{7,5},{8,14},{10,8},{12,... | collective-permute-start | bytes 393224 | tf_op jit(solution)/shard_map/ppermute | solution.py:294
  82.3 1.3 %collective-permute-start.13 = (bf16[128,512]{1,0:T(8,128)(2,1)S(1)}, bf16[128,512]{1,0:T(8,128)(2,1)S(1)}, u32[]{:S(2)}, u32[]{:S(2)}) collective-permute-start(bf16[128,512]{1,0:T(8,128)(2,1)S(1)} %fusion.2), channel_id=1, source_target_pairs={{0,16},{8,24},{16,0},{24,8},{1,17},{9,25},{17,1},{25,9},{2,18},{10... | collective-permute-start | bytes 393224 | tf_op jit(solution)/shard_map/ppermute | solution.py:291
  83.7 1.4 %collective-permute-start.22 = (bf16[128,512]{1,0:T(8,128)(2,1)S(1)}, bf16[128,512]{1,0:T(8,128)(2,1)S(1)}, u32[]{:S(2)}, u32[]{:S(2)}) collective-permute-start(bf16[128,512]{1,0:T(8,128)(2,1)S(1)} %add_convert_fusion.1), channel_id=1, source_target_pairs={{0,4},{2,6},{4,0},{6,2},{1,5},{3,7},{5,1},{7,3},{8,12},{10,14},{12... | collective-permute-start | bytes 393224 | tf_op jit(solution)/shard_map/ppermute | solution.py:294
  85.1 2.2 %collective-permute-done.13 = bf16[128,512]{1,0:T(8,128)(2,1)S(1)} collective-permute-done((bf16[128,512]{1,0:T(8,128)(2,1)S(1)}, bf16[128,512]{1,0:T(8,128)(2,1)S(1)}, u32[]{:S(2)}, u32[]{:S(2)}) %collective-permute-start.13) | collective-permute-done | bytes 131104 | tf_op jit(solution)/shard_map/ppermute | solution.py:291
  87.3 3.5 %weight_grads.1 = (bf16[1024,1024]{1,0:T(8,128)(2,1)}, bf16[1024,1024]{1,0:T(8,128)(2,1)}) custom-call(bf16[2,512,2048]{2,1,0:T(8,128)(2,1)S(1)} %get-tuple-element.45.rows, bf16[2,512,1024]{2,1,0:T(8,128)(2,1)S(1)} %get-tuple-element.46.acts, bf16[2,1024,1024]{2,1,0:T(8,128)(2,1)S(1)} %collective-permute-done.23.got), custom_call_target="tpu_custom_call" | custom-call | flops 1000 | bytes 1000 | tf_op jit(solution)/shard_map/weight_grads/pallas_call | solution.py:263
  91.3 1.2 %unplace_rows.1 = bf16[256,512]{1,0:T(8,128)(2,1)} custom-call(s32[1,256]{1,0:T(1,128)S(1)} %bitcast.24, s32[1,256]{1,0:T(1,128)S(1)} %bitcast.27, bf16[128,512]{1,0:T(8,128)(2,1)S(1)} %fusion.1.refs_0_, bf16[128,512]{1,0:T(8,128)(2,1)S(1)} %collective-permute-done.17.refs_1_, bf16[128,512]{1,0:T(8,128)(2,1)S(1)} %collective-permute-done.18.refs_2_, ...), custom_call_target="tpu_custom_call" | custom-call | flops 1000 | bytes 1000 | tf_op jit(solution)/shard_map/unplace_rows/pallas_call | solution.py:235
  (50 shorter events, 5.6 us)
Async XLA Ops:
  0.6 8.2 %copy-start = (bf16[1,1024,1024]{2,1,0:T(8,128)(2,1)S(1)}, bf16[1,1024,1024]{2,1,0:T(8,128)(2,1)}, u32[]{:S(2)}) copy-start(bf16[1,1024,1024]{2,1,0:T(8,128)(2,1)} %param.12) | copy-start | bytes 6291460
  0.6 8.2 %copy-start.6 = (s32[256,1]{0,1:T(1,128)S(1)}, s32[256,1]{0,1:T(1,128)}, u32[]{:S(2)}) copy-start(s32[256,1]{0,1:T(1,128)} %param.11) | copy-start | bytes 3076
  0.7 8.2 %copy-start.5 = (s32[256,1]{0,1:T(1,128)S(1)}, s32[256,1]{0,1:T(1,128)}, u32[]{:S(2)}) copy-start(s32[256,1]{0,1:T(1,128)} %param.10) | copy-start | bytes 3076
  0.7 8.2 %copy-start.7 = (f32[256]{0:T(256)S(1)}, f32[256]{0:T(256)}, u32[]{:S(2)}) copy-start(f32[256]{0:T(256)} %param.9) | copy-start | bytes 3076
  0.7 8.2 %collective-permute-start = (bf16[1024,1024]{1,0:T(8,128)(2,1)}, bf16[1024,1024]{1,0:T(8,128)(2,1)S(1)}, u32[]{:S(2)}, u32[]{:S(2)}) collective-permute-start(bf16[1024,1024]{1,0:T(8,128)(2,1)} %bitcast.14), channel_id=1, source_target_pairs={{0,1},{1,0},{2,3},{3,2},{4,5},{5,4},{6,7},{7,6},{8,9},{9,8},{10,11... | collective-permute-start | bytes 6291464 | tf_op jit(solution)/shard_map/ppermute | solution.py:288
  1.2 7.7 %collective-permute-start.1 = (bf16[1024,1024]{1,0:T(8,128)(2,1)}, bf16[1024,1024]{1,0:T(8,128)(2,1)S(1)}, u32[]{:S(2)}, u32[]{:S(2)}) collective-permute-start(bf16[1024,1024]{1,0:T(8,128)(2,1)} %bitcast.18), channel_id=1, source_target_pairs={{0,1},{1,0},{2,3},{3,2},{4,5},{5,4},{6,7},{7,6},{8,9},{9,8},{10,11... | collective-permute-start | bytes 6291464 | tf_op jit(solution)/shard_map/ppermute | solution.py:288
  3.7 16.4 %collective-permute-start.3 = (bf16[128,1024]{1,0:T(8,128)(2,1)}, bf16[128,1024]{1,0:T(8,128)(2,1)S(1)}, u32[]{:S(2)}, u32[]{:S(2)}) collective-permute-start(bf16[128,1024]{1,0:T(8,128)(2,1)} %get-tuple-element.36), channel_id=1, source_target_pairs={{0,2},{2,4},{4,6},{6,0},{1,3},{3,5},{5,7},{7,1},{8,10},{10,12},{12... | collective-permute-start | bytes 786440 | tf_op jit(solution)/shard_map/ppermute | solution.py:294
  6.8 13.8 %collective-permute-start.4 = (bf16[128,1024]{1,0:T(8,128)(2,1)}, bf16[128,1024]{1,0:T(8,128)(2,1)S(1)}, u32[]{:S(2)}, u32[]{:S(2)}) collective-permute-start(bf16[128,1024]{1,0:T(8,128)(2,1)} %get-tuple-element.38), channel_id=1, source_target_pairs={{0,6},{2,0},{4,2},{6,4},{1,7},{3,1},{5,3},{7,5},{8,14},{10,8},{12,... | collective-permute-start | bytes 786440 | tf_op jit(solution)/shard_map/ppermute | solution.py:294
  8.9 1.6 %copy-start.1 = (bf16[1,1024,1024]{2,1,0:T(8,128)(2,1)S(1)}, bf16[1,1024,1024]{2,1,0:T(8,128)(2,1)}, u32[]{:S(2)}) copy-start(bf16[1,1024,1024]{2,1,0:T(8,128)(2,1)} %param.13) | copy-start | bytes 6291460
  10.5 1.2 %copy-start.3 = (bf16[256,2048]{1,0:T(8,128)(2,1)S(1)}, bf16[256,2048]{1,0:T(8,128)(2,1)}, u32[]{:S(2)}) copy-start(bf16[256,2048]{1,0:T(8,128)(2,1)} %tokens.1) | copy-start | bytes 3145732
  12.9 11.0 %copy-start.8 = (bf16[128,1024]{1,0:T(8,128)(2,1)S(1)}, bf16[128,1024]{1,0:T(8,128)(2,1)}, u32[]{:S(2)}) copy-start(bf16[128,1024]{1,0:T(8,128)(2,1)} %get-tuple-element.35) | copy-start | bytes 786436
  20.1 27.2 %copy-start.2 = (bf16[1,1024,1024]{2,1,0:T(8,128)(2,1)S(1)}, bf16[1,1024,1024]{2,1,0:T(8,128)(2,1)}, u32[]{:S(2)}) copy-start(bf16[1,1024,1024]{2,1,0:T(8,128)(2,1)} %param.13) | copy-start | bytes 6291460
  20.6 14.1 %collective-permute-start.6 = (bf16[256,1024]{1,0:T(8,128)(2,1)S(1)}, bf16[256,1024]{1,0:T(8,128)(2,1)S(1)}, u32[]{:S(2)}, u32[]{:S(2)}) collective-permute-start(bf16[256,1024]{1,0:T(8,128)(2,1)S(1)} %constant_dynamic-update-slice_fusion.refs_0_), channel_id=1, source_target_pairs={{0,16},{8,24},{16,0},{24,8},{1,17},{9,25},{17,1},{25,9},{2,18},{10... | collective-permute-start | bytes 1572872 | tf_op jit(solution)/shard_map/ppermute | solution.py:291
  22.4 14.0 %collective-permute-start.5 = (bf16[256,1024]{1,0:T(8,128)(2,1)S(1)}, bf16[256,1024]{1,0:T(8,128)(2,1)S(1)}, u32[]{:S(2)}, u32[]{:S(2)}) collective-permute-start(bf16[256,1024]{1,0:T(8,128)(2,1)S(1)} %constant_dynamic-update-slice_fusion.refs_0_), channel_id=1, source_target_pairs={{0,8},{8,0},{16,24},{24,16},{1,9},{9,1},{17,25},{25,17},{2,10},{10... | collective-permute-start | bytes 1572872 | tf_op jit(solution)/shard_map/ppermute | solution.py:291
  23.9 14.3 %collective-permute-start.2 = (bf16[128,1024]{1,0:T(8,128)(2,1)S(1)}, bf16[128,1024]{1,0:T(8,128)(2,1)S(1)}, u32[]{:S(2)}, u32[]{:S(2)}) collective-permute-start(bf16[128,1024]{1,0:T(8,128)(2,1)S(1)} %copy-done.8), channel_id=1, source_target_pairs={{0,4},{2,6},{4,0},{6,2},{1,5},{3,7},{5,1},{7,3},{8,12},{10,14},{12... | collective-permute-start | bytes 786440 | tf_op jit(solution)/shard_map/ppermute | solution.py:294
  34.6 9.3 %collective-permute-start.9 = (bf16[256,512]{1,0:T(8,128)(2,1)S(1)}, bf16[256,512]{1,0:T(8,128)(2,1)S(1)}, u32[]{:S(2)}, u32[]{:S(2)}) collective-permute-start(bf16[256,512]{1,0:T(8,128)(2,1)S(1)} %slice.36), channel_id=1, source_target_pairs={{0,8},{8,0},{16,24},{24,16},{1,9},{9,1},{17,25},{25,17},{2,10},{10... | collective-permute-start | bytes 786440 | tf_op jit(solution)/shard_map/ppermute | solution.py:291
  36.4 9.3 %collective-permute-start.10 = (bf16[256,512]{1,0:T(8,128)(2,1)S(1)}, bf16[256,512]{1,0:T(8,128)(2,1)S(1)}, u32[]{:S(2)}, u32[]{:S(2)}) collective-permute-start(bf16[256,512]{1,0:T(8,128)(2,1)S(1)} %slice.37), channel_id=1, source_target_pairs={{0,16},{8,24},{16,0},{24,8},{1,17},{9,25},{17,1},{25,9},{2,18},{10... | collective-permute-start | bytes 786440 | tf_op jit(solution)/shard_map/ppermute | solution.py:291
  38.2 18.3 %collective-permute-start.8 = (bf16[128,1024]{1,0:T(8,128)(2,1)S(1)}, bf16[128,1024]{1,0:T(8,128)(2,1)S(1)}, u32[]{:S(2)}, u32[]{:S(2)}) collective-permute-start(bf16[128,1024]{1,0:T(8,128)(2,1)S(1)} %collective-permute-done.2.refs_0_), channel_id=1, source_target_pairs={{0,16},{8,24},{16,0},{24,8},{1,17},{9,25},{17,1},{25,9},{2,18},{10... | collective-permute-start | bytes 786440 | tf_op jit(solution)/shard_map/ppermute | solution.py:291
  38.7 19.2 %collective-permute-start.7 = (bf16[128,1024]{1,0:T(8,128)(2,1)S(1)}, bf16[128,1024]{1,0:T(8,128)(2,1)S(1)}, u32[]{:S(2)}, u32[]{:S(2)}) collective-permute-start(bf16[128,1024]{1,0:T(8,128)(2,1)S(1)} %collective-permute-done.2.refs_0_), channel_id=1, source_target_pairs={{0,8},{8,0},{16,24},{24,16},{1,9},{9,1},{17,25},{25,17},{2,10},{10... | collective-permute-start | bytes 786440 | tf_op jit(solution)/shard_map/ppermute | solution.py:291
  45.8 12.2 %collective-permute-start.11 = (bf16[128,1024]{1,0:T(8,128)(2,1)S(1)}, bf16[128,1024]{1,0:T(8,128)(2,1)S(1)}, u32[]{:S(2)}, u32[]{:S(2)}) collective-permute-start(bf16[128,1024]{1,0:T(8,128)(2,1)S(1)} %collective-permute-done.2.refs_0_), channel_id=1, source_target_pairs={{0,24},{8,16},{16,8},{24,0},{1,25},{9,17},{17,9},{25,1},{2,26},{10... | collective-permute-start | bytes 786440 | tf_op jit(solution)/shard_map/ppermute | solution.py:291
  54.4 12.7 %collective-permute-start.14 = (bf16[256,512]{1,0:T(8,128)(2,1)S(1)}, bf16[256,512]{1,0:T(8,128)(2,1)S(1)}, u32[]{:S(2)}, u32[]{:S(2)}) collective-permute-start(bf16[256,512]{1,0:T(8,128)(2,1)S(1)} %get-tuple-element.49), channel_id=1, source_target_pairs={{0,8},{8,0},{16,24},{24,16},{1,9},{9,1},{17,25},{25,17},{2,10},{10... | collective-permute-start | bytes 786440 | tf_op jit(solution)/shard_map/ppermute | solution.py:291
  56.0 11.1 %collective-permute-start.15 = (bf16[256,512]{1,0:T(8,128)(2,1)S(1)}, bf16[256,512]{1,0:T(8,128)(2,1)S(1)}, u32[]{:S(2)}, u32[]{:S(2)}) collective-permute-start(bf16[256,512]{1,0:T(8,128)(2,1)S(1)} %get-tuple-element.50), channel_id=1, source_target_pairs={{0,16},{8,24},{16,0},{24,8},{1,17},{9,25},{17,1},{25,9},{2,18},{10... | collective-permute-start | bytes 786440 | tf_op jit(solution)/shard_map/ppermute | solution.py:291
  56.5 10.6 %collective-permute-start.16 = (bf16[256,512]{1,0:T(8,128)(2,1)S(1)}, bf16[256,512]{1,0:T(8,128)(2,1)S(1)}, u32[]{:S(2)}, u32[]{:S(2)}) collective-permute-start(bf16[256,512]{1,0:T(8,128)(2,1)S(1)} %get-tuple-element.51), channel_id=1, source_target_pairs={{0,24},{8,16},{16,8},{24,0},{1,25},{9,17},{17,9},{25,1},{2,26},{10... | collective-permute-start | bytes 786440 | tf_op jit(solution)/shard_map/ppermute | solution.py:291
  67.1 20.2 %collective-permute-start.23 = (bf16[2,1024,1024]{2,1,0:T(8,128)(2,1)S(1)}, bf16[2,1024,1024]{2,1,0:T(8,128)(2,1)S(1)}, u32[]{:S(2)}, u32[]{:S(2)}) collective-permute-start(bf16[2,1024,1024]{2,1,0:T(8,128)(2,1)S(1)} %convolution_convert_fusion), channel_id=1, source_target_pairs={{0,1},{1,0},{2,3},{3,2},{4,5},{5,4},{6,7},{7,6},{8,9},{9,8},{10,11... | collective-permute-start | bytes 12582920 | tf_op jit(solution)/shard_map/ppermute | solution.py:288
  67.2 9.2 %collective-permute-start.12 = (bf16[2,128,512]{2,1,0:T(8,128)(2,1)S(1)}, bf16[2,128,512]{2,1,0:T(8,128)(2,1)S(1)}, u32[]{:S(2)}, u32[]{:S(2)}) collective-permute-start(bf16[2,128,512]{2,1,0:T(8,128)(2,1)S(1)} %get-tuple-element.47), channel_id=1, source_target_pairs={{0,8},{8,0},{16,24},{24,16},{1,9},{9,1},{17,25},{25,17},{2,10},{10... | collective-permute-start | bytes 786440 | tf_op jit(solution)/shard_map/ppermute | solution.py:291
  68.9 22.4 %collective-permute-start.18 = (bf16[128,512]{1,0:T(8,128)(2,1)S(1)}, bf16[128,512]{1,0:T(8,128)(2,1)S(1)}, u32[]{:S(2)}, u32[]{:S(2)}) collective-permute-start(bf16[128,512]{1,0:T(8,128)(2,1)S(1)} %get-tuple-element.63), channel_id=1, source_target_pairs={{0,2},{2,4},{4,6},{6,0},{1,3},{3,5},{5,7},{7,1},{8,10},{10,12},{12... | collective-permute-start | bytes 393224 | tf_op jit(solution)/shard_map/ppermute | solution.py:294
  70.5 8.2 %collective-permute-start.19 = (bf16[128,512]{1,0:T(8,128)(2,1)S(1)}, bf16[128,512]{1,0:T(8,128)(2,1)S(1)}, u32[]{:S(2)}, u32[]{:S(2)}) collective-permute-start(bf16[128,512]{1,0:T(8,128)(2,1)S(1)} %get-tuple-element.54), channel_id=1, source_target_pairs={{0,8},{8,0},{16,24},{24,16},{1,9},{9,1},{17,25},{25,17},{2,10},{10... | collective-permute-start | bytes 393224 | tf_op jit(solution)/shard_map/ppermute | solution.py:291
  71.1 11.2 %collective-permute-start.20 = (bf16[128,512]{1,0:T(8,128)(2,1)S(1)}, bf16[128,512]{1,0:T(8,128)(2,1)S(1)}, u32[]{:S(2)}, u32[]{:S(2)}) collective-permute-start(bf16[128,512]{1,0:T(8,128)(2,1)S(1)} %get-tuple-element.56), channel_id=1, source_target_pairs={{0,16},{8,24},{16,0},{24,8},{1,17},{9,25},{17,1},{25,9},{2,18},{10... | collective-permute-start | bytes 393224 | tf_op jit(solution)/shard_map/ppermute | solution.py:291
  76.3 7.3 %collective-permute-start.21 = (bf16[128,512]{1,0:T(8,128)(2,1)S(1)}, bf16[128,512]{1,0:T(8,128)(2,1)S(1)}, u32[]{:S(2)}, u32[]{:S(2)}) collective-permute-start(bf16[128,512]{1,0:T(8,128)(2,1)S(1)} %get-tuple-element.58), channel_id=1, source_target_pairs={{0,24},{8,16},{16,8},{24,0},{1,25},{9,17},{17,9},{25,1},{2,26},{10... | collective-permute-start | bytes 393224 | tf_op jit(solution)/shard_map/ppermute | solution.py:291
  78.7 12.6 %collective-permute-start.17 = (bf16[128,512]{1,0:T(8,128)(2,1)S(1)}, bf16[128,512]{1,0:T(8,128)(2,1)S(1)}, u32[]{:S(2)}, u32[]{:S(2)}) collective-permute-start(bf16[128,512]{1,0:T(8,128)(2,1)S(1)} %get-tuple-element.64), channel_id=1, source_target_pairs={{0,6},{2,0},{4,2},{6,4},{1,7},{3,1},{5,3},{7,5},{8,14},{10,8},{12,... | collective-permute-start | bytes 393224 | tf_op jit(solution)/shard_map/ppermute | solution.py:294
  82.3 5.0 %collective-permute-start.13 = (bf16[128,512]{1,0:T(8,128)(2,1)S(1)}, bf16[128,512]{1,0:T(8,128)(2,1)S(1)}, u32[]{:S(2)}, u32[]{:S(2)}) collective-permute-start(bf16[128,512]{1,0:T(8,128)(2,1)S(1)} %fusion.2), channel_id=1, source_target_pairs={{0,16},{8,24},{16,0},{24,8},{1,17},{9,25},{17,1},{25,9},{2,18},{10... | collective-permute-start | bytes 393224 | tf_op jit(solution)/shard_map/ppermute | solution.py:291
  83.7 7.6 %collective-permute-start.22 = (bf16[128,512]{1,0:T(8,128)(2,1)S(1)}, bf16[128,512]{1,0:T(8,128)(2,1)S(1)}, u32[]{:S(2)}, u32[]{:S(2)}) collective-permute-start(bf16[128,512]{1,0:T(8,128)(2,1)S(1)} %add_convert_fusion.1), channel_id=1, source_target_pairs={{0,4},{2,6},{4,0},{6,2},{1,5},{3,7},{5,1},{7,3},{8,12},{10,14},{12... | collective-permute-start | bytes 393224 | tf_op jit(solution)/shard_map/ppermute | solution.py:294
  (1 other events, 1.2 us)
